TPU v7x, 32 devices: a whole 2x2x4 slice. The times are simulated.
32 devices in a mesh: tm: 16 (over z, y, x), space: 2 (over core).
Axes of the slice: x: 2, y: 2, z: 4, core: 2. Of those that a mesh axis runs over, the one named last changes fastest.
Arguments:
- feats: bfloat16 [64, 8, 96, 256], P('tm', 'space'), may hold values from -120 to 120
- clip_ids: int32 [16], replicated, may hold values from 0 to 3, never falling along the last dimension, each value on 1 to 8 neighbouring positions
- gain_one: float32 [256], replicated, may hold values from 0.25 to 1.75
- shift_one: float32 [256], replicated, may hold values from -3 to 3
- kernel_one: bfloat16 [3, 3, 3, 256, 256], replicated, may hold values from -0.078125 to 0.078125
- gain_two: float32 [256], replicated, may hold values from 0.25 to 1.75
- shift_two: float32 [256], replicated, may hold values from -3 to 3
- kernel_two: bfloat16 [3, 3, 3, 256, 256], replicated, may hold values from -0.078125 to 0.078125
Outputs:
- block_out: float32 [64, 8, 96, 256], P('tm', 'space')
Inputs may be any that keep to these rules, and one draw needn't show every extreme that they name: `clip_ids`: clip numbers of the slabs in order, never falling; every clip covers 1 to 8 consecutive slabs, at least one exactly 8.
All inputs are finite; a program needn't handle non-finite values.
Results may differ from a plain program's by a relative error of at most 0.0015.
Values may be sent and summed in bfloat16 or wider, within the bound.
No kernel may reach another device: no remote copies, remote signals or barrier semaphores. Data moves between devices by JAX's collectives and lax.ppermute only.
A program may use at most 128 MiB of HBM per device.

v0:
```python
import jax
import jax.numpy as jnp
from jax import lax
from jax.sharding import PartitionSpec as P

GROUPS = 32


def padded_2(value, sides, width):
    for axis, dim in sides:
        peers, length = (lax.axis_size(axis), value.shape[dim])
        up = [(i, (i + 1) % peers) for i in range(peers - 1)]
        down = [(j, i) for i, j in up]
        last = lax.slice_in_dim(value, length - width, length, axis=dim)
        leading = lax.slice_in_dim(value, 0, width, axis=dim)
        before = lax.ppermute(last, axis, up)
        after = lax.ppermute(leading, axis, down)
        value = jnp.concatenate([before, value, after], axis=dim)
    return value


def passed_along(block, axis, distance):
    devices = range(lax.axis_size(axis))
    route = [(i - distance, i) for i in devices if i - distance in devices]
    return lax.ppermute(block, axis, route)


def clip_stats(values, clip_ids):
    width = values.shape[3]
    grouped = values.reshape(-1, GROUPS, width // GROUPS)
    local_sum = jnp.sum(grouped, axis=(0, 2))
    local_square = jnp.sum(grouped * grouped, axis=(0, 2))
    slab_count = lax.axis_size("tm")
    own_slab = lax.axis_index("tm")
    own_clip = lax.dynamic_index_in_dim(clip_ids, own_slab, keepdims=False)
    own_row = (jnp.arange(slab_count, dtype=jnp.int32) == own_clip).astype(jnp.float32)[:, None]
    table_sum, table_square = lax.psum(
        (own_row * local_sum[None, :], own_row * local_square[None, :]), ("tm", "space")
    )
    clip_sum = jnp.sum(table_sum * own_row, axis=0)
    clip_square = jnp.sum(table_square * own_row, axis=0)
    slabs_in = jnp.sum((clip_ids == own_clip).astype(jnp.float32))
    count = slabs_in * (
        values.shape[0]
        * values.shape[1]
        * lax.axis_size("space")
        * values.shape[2]
        * (width // GROUPS)
    )
    mean = clip_sum / count
    variance = clip_square / count - mean * mean
    return (mean, lax.rsqrt(variance + 1e-06))


def apply_norm(values, mean, scale, gain, shift):
    width = values.shape[3]
    grouped = values.reshape(values.shape[:3] + (GROUPS, width // GROUPS))
    normed = (grouped - mean[:, None]) * scale[:, None]
    normed = normed.reshape(values.shape) * gain + shift
    return jax.nn.silu(normed).astype(jnp.bfloat16)


def edge_rows(extended, margin):
    place = lax.axis_index("space")
    last = lax.axis_size("space") - 1
    rows = extended.shape[1]
    row_pos = jnp.arange(rows, dtype=jnp.int32)
    top_row = extended[:, margin : margin + 1]
    bottom_row = extended[:, rows - margin - 1 : rows - margin]
    upper = jnp.logical_and(place == 0, row_pos < margin)[None, :, None, None]
    lower = jnp.logical_and(place == last, row_pos >= rows - margin)[None, :, None, None]
    extended = jnp.where(upper, top_row, extended)
    return jnp.where(lower, bottom_row, extended)


def with_rims(frames):
    return edge_rows(padded_2(frames, (("space", 1),), 1), 1)


def causal_conv(extended, kernel):
    frames = extended.shape[0] - 2
    rows = extended.shape[1] - 2
    cols = extended.shape[2]
    width = extended.shape[3]
    padded = jnp.pad(extended, ((0, 0), (0, 0), (1, 1), (0, 0)), mode="edge")
    total = jnp.zeros((frames * rows * cols, kernel.shape[4]), jnp.float32)
    for tap_time in range(3):
        for tap_row in range(3):
            window = padded[tap_time : tap_time + frames, tap_row : tap_row + rows]
            stacked = jnp.concatenate(
                [window[:, :, offset : offset + cols] for offset in range(3)], axis=3
            )
            stacked = stacked.reshape(-1, 3 * width)
            total = total + jnp.dot(
                stacked,
                kernel[tap_time, tap_row].reshape(3 * width, -1),
                preferred_element_type=jnp.float32,
            )
    return total.reshape(frames, rows, cols, -1)


def repeat_first(act, count):
    return jnp.broadcast_to(act[0:1], (count,) + act.shape[1:])


def temporal_front(act, starting):
    earlier = passed_along(act[-2:], "tm", 1)
    front = jnp.where(starting, repeat_first(act, 2), earlier)
    return jnp.concatenate([front, act], axis=0)


def on_device(feats, clip_ids, gain_one, shift_one, kernel_one, gain_two, shift_two, kernel_two):
    own_slab = lax.axis_index("tm")
    own_clip = lax.dynamic_index_in_dim(clip_ids, own_slab, keepdims=False)
    before_clip = lax.dynamic_index_in_dim(clip_ids, jnp.maximum(own_slab - 1, 0), keepdims=False)
    starting = jnp.logical_or(own_slab == 0, own_clip != before_clip)
    inputs = feats.astype(jnp.float32)
    mean_one, scale_one = clip_stats(inputs, clip_ids)
    first = apply_norm(inputs, mean_one, scale_one, gain_one, shift_one)
    front_first = temporal_front(first, starting)
    hidden = causal_conv(with_rims(front_first), kernel_one).astype(jnp.bfloat16)
    hidden_float = hidden.astype(jnp.float32)
    mean_two, scale_two = clip_stats(hidden_float, clip_ids)
    second = apply_norm(hidden_float, mean_two, scale_two, gain_two, shift_two)
    extended = with_rims(temporal_front(second, starting))
    return inputs + causal_conv(extended, kernel_two)


def solution(mesh):
    return jax.shard_map(
        on_device,
        mesh=mesh,
        in_specs=(P("tm", "space", None, None), P(), P(), P(), P(), P(), P(), P()),
        out_specs=P("tm", "space", None, None),
        check_vma=False,
    )
```

profile of v0, /device:TPU:0, one launch (start us, length us, event | category | flops | bytes accessed | tf_op | source)
XLA Modules:
  0.0 165.4 jit_solution(14084040062750256918)
XLA Ops:
  0.0 1.4 fusion.57
  1.4 0.7 compare_convert_fusion.1
  2.1 1.9 %fusion.50 = f32[]{:T(128)} fusion(s32[16]{0:T(128)} %param.9, s32[]{:T(128)} %bitcast), kind=kLoop, calls=%fused_computation.180 | loop fusion | flops 47 | bytes 72 | tf_op jit(solution)/shard_map/reduce_sum | solution.py:42
  4.0 1.4 fusion.17
  5.9 42.1 %all-reduce.1 = (f32[16,32]{1,0:T(8,128)S(1)}, f32[16,32]{1,0:T(8,128)S(1)}) all-reduce(f32[16,32]{1,0:T(8,128)S(1)} %get-tuple-element.102, f32[16,32]{1,0:T(8,128)S(1)} %get-tuple-element.101), channel_id=1, replica_groups=mesh['tm'=16,'space'=2] {'tm','space'}, use_global_device_ids=true, to_apply=%region_7.8 | all-reduce | flops 1024 | bytes 8192 | tf_op jit(solution)/shard_map/psum | solution.py:37
  49.0 1.7 %fusion.16 = bf16[4,4,96,256]{3,2,1,0:T(8,128)(2,1)S(1)} fusion(bf16[4,4,96,256]{3,2,1,0:T(8,128)(2,1)} %param.8, f32[256]{0:T(256)} %param.11, f32[256]{0:T(256)} %param.10, f32[256]{0:T(256)S(1)} %mul.156, f32[256]{0:T(256)S(1)} %sub.45), kind=kLoop, calls=%fused_computation.90 | loop fusion | flops 3932160 | bytes 1576960 | tf_op jit(solution)/shard_map/convert_element_type | solution.py:60
  50.8 4.2 %collective-permute-start = (bf16[2,4,96,256]{3,2,1,0:T(8,128)(2,1)S(1)}, bf16[2,4,96,256]{3,2,1,0:T(8,128)(2,1)S(1)}, u32[]{:S(2)}, u32[]{:S(2)}) collective-permute-start(bf16[2,4,96,256]{3,2,1,0:T(8,128)(2,1)S(1)} %slice.469), channel_id=1, source_target_pairs={{0,2},{2,4},{4,6},{6,8},{8,10},{10,12},{12,14},{14,16},{16,18},{18... | collective-permute-start | bytes 1179656 | tf_op jit(solution)/shard_map/ppermute | solution.py:25
  56.4 5.2 %collective-permute-done = bf16[2,4,96,256]{3,2,1,0:T(8,128)(2,1)S(1)} collective-permute-done((bf16[2,4,96,256]{3,2,1,0:T(8,128)(2,1)S(1)}, bf16[2,4,96,256]{3,2,1,0:T(8,128)(2,1)S(1)}, u32[]{:S(2)}, u32[]{:S(2)}) %collective-permute-start) | collective-permute-done | bytes 393248 | tf_op jit(solution)/shard_map/ppermute | solution.py:25
  61.7 1.3 collective-permute-start.1
  63.0 1.3 collective-permute-start.2
  64.3 2.3 %fusion.52 = (bf16[1,1,3,256,256]{4,3,2,1,0:T(8,128)(2,1)S(1)}, bf16[1,1,3,256,256]{4,3,2,1,0:T(8,128)(2,1)S(1)}, bf16[1,1,3,256,256]{4,3,2,1,0:T(8,128)(2,1)S(1...) fusion(bf16[3,3,3,256,256]{4,3,2,1,0:T(8,128)(2,1)} %param.12), kind=kLoop, calls=%fused_computation.186 | loop fusion | bytes 7077888 | tf_op jit(solution)/shard_map/slice | solution.py:96
  66.6 0.4 fusion.6
  67.1 0.9 fusion.55
  68.0 3.9 %fusion.42 = (bf16[4,4,96,256]{3,2,1,0:T(8,128)(2,1)S(1)}, bf16[4,4,96,256]{3,2,1,0:T(8,128)(2,1)S(1)}, bf16[4,4,96,256]{3,2,1,0:T(8,128)(2,1)S(1)}, bf16[4,4,96...) fusion(bf16[6,6,96,256]{3,2,1,0:T(8,128)(2,1)S(1)} %fusion.6, ...), kind=kLoop, calls=%fused_computation.150 | loop fusion | flops 12582912 | bytes 8079360 | tf_op jit(solution)/shard_map/jit(_pad)/concatenate | solution.py:85
  71.8 3.5 %fusion.34 = (bf16[4,4,96,256]{3,2,1,0:T(8,128)(2,1)S(1)}, bf16[4,4,96,256]{3,2,1,0:T(8,128)(2,1)S(1)}, bf16[4,4,96,256]{3,2,1,0:T(8,128)(2,1)S(1)}, bf16[4,4,96...) fusion(bf16[6,6,96,256]{3,2,1,0:T(8,128)(2,1)S(1)} %fusion.6, ...), kind=kLoop, calls=%fused_computation.142 | loop fusion | flops 12582912 | bytes 8079360 | tf_op jit(solution)/shard_map/jit(_pad)/concatenate | solution.py:85
  75.3 0.9 fusion.4
  76.2 0.2 pad_maximum_fusion.4
  76.4 0.8 fusion.58
  77.2 0.2 pad_maximum_fusion.7
  77.4 0.2 pad_maximum_fusion.6
  77.5 0.2 pad_maximum_fusion.5
  77.7 0.8 convolution_add_fusion.15
  78.5 0.8 convolution_add_fusion.14
  79.4 0.8 convolution_add_fusion.13
  80.2 0.2 pad_maximum_fusion.8
  80.4 0.8 convolution_add_fusion.12
  81.1 0.2 pad_maximum_fusion.9
  81.3 0.8 convolution_add_fusion.11
  82.1 0.2 pad_maximum_fusion.10
  82.3 0.8 convolution_add_fusion.10
  83.1 0.2 pad_maximum_fusion.11
  83.2 0.8 convolution_add_fusion.9
  84.1 0.8 multiply_reduce_fusion
  85.4 42.3 %all-reduce = (f32[16,32]{1,0:T(8,128)S(1)}, f32[16,32]{1,0:T(8,128)S(1)}) all-reduce(f32[16,32]{1,0:T(8,128)S(1)} %get-tuple-element.98, f32[16,32]{1,0:T(8,128)S(1)} %get-tuple-element.97), channel_id=1, replica_groups=mesh['tm'=16,'space'=2] {'tm','space'}, use_global_device_ids=true, to_apply=%region_15.16 | all-reduce | flops 1024 | bytes 8192 | tf_op jit(solution)/shard_map/psum | solution.py:37
  128.2 0.5 multiply_convert_fusion
  128.7 4.5 %collective-permute-start.3 = (bf16[2,4,96,256]{3,2,1,0:T(8,128)(2,1)S(1)}, bf16[2,4,96,256]{3,2,1,0:T(8,128)(2,1)S(1)}, u32[]{:S(2)}, u32[]{:S(2)}) collective-permute-start(bf16[2,4,96,256]{3,2,1,0:T(8,128)(2,1)S(1)} %slice.514), channel_id=1, source_target_pairs={{0,2},{2,4},{4,6},{6,8},{8,10},{10,12},{12,14},{14,16},{16,18},{18... | collective-permute-start | bytes 1179656 | tf_op jit(solution)/shard_map/ppermute | solution.py:25
  133.2 7.2 %collective-permute-done.3 = bf16[2,4,96,256]{3,2,1,0:T(8,128)(2,1)S(1)} collective-permute-done((bf16[2,4,96,256]{3,2,1,0:T(8,128)(2,1)S(1)}, bf16[2,4,96,256]{3,2,1,0:T(8,128)(2,1)S(1)}, u32[]{:S(2)}, u32[]{:S(2)}) %collective-permute-start.3) | collective-permute-done | bytes 393248 | tf_op jit(solution)/shard_map/ppermute | solution.py:25
  140.5 1.3 collective-permute-start.4
  141.8 1.3 collective-permute-start.5
  143.1 0.3 fusion.51
  143.5 1.8 %collective-permute-done.5 = bf16[6,1,96,256]{3,2,1,0:T(8,128)(2,1)S(1)} collective-permute-done((bf16[6,1,96,256]{3,2,1,0:T(8,128)(2,1)S(1)}, bf16[6,1,96,256]{3,2,1,0:T(8,128)(2,1)S(1)}, u32[]{:S(2)}, u32[]{:S(2)}) %collective-permute-start.5) | collective-permute-done | bytes 294944 | tf_op jit(solution)/shard_map/ppermute | solution.py:17
  145.3 0.4 fusion.7
  145.6 0.9 fusion.53
  146.6 4.1 %fusion.26 = (bf16[4,4,96,256]{3,2,1,0:T(8,128)(2,1)S(1)}, bf16[4,4,96,256]{3,2,1,0:T(8,128)(2,1)S(1)}, bf16[4,4,96,256]{3,2,1,0:T(8,128)(2,1)S(1)}, bf16[4,4,96...) fusion(bf16[6,6,96,256]{3,2,1,0:T(8,128)(2,1)S(1)} %fusion.7, ...), kind=kLoop, calls=%fused_computation.134 | loop fusion | flops 12582912 | bytes 8079360 | tf_op jit(solution)/shard_map/jit(_pad)/concatenate | solution.py:85
  150.7 3.5 %fusion.18 = (bf16[4,4,96,256]{3,2,1,0:T(8,128)(2,1)S(1)}, bf16[4,4,96,256]{3,2,1,0:T(8,128)(2,1)S(1)}, bf16[4,4,96,256]{3,2,1,0:T(8,128)(2,1)S(1)}, bf16[4,4,96...) fusion(bf16[6,6,96,256]{3,2,1,0:T(8,128)(2,1)S(1)} %fusion.7, ...), kind=kLoop, calls=%fused_computation.126 | loop fusion | flops 12582912 | bytes 8079360 | tf_op jit(solution)/shard_map/jit(_pad)/concatenate | solution.py:85
  154.2 0.7 fusion.2
  154.9 0.2 pad_maximum_fusion.12
  155.1 0.8 fusion.59
  155.9 0.2 pad_maximum_fusion.19
  156.0 0.2 pad_maximum_fusion.18
  156.2 0.2 pad_maximum_fusion.17
  156.4 0.2 pad_maximum_fusion.16
  156.6 0.2 pad_maximum_fusion.15
  156.7 0.2 pad_maximum_fusion.14
  157.1 0.8 convolution_add_fusion.7
  157.9 0.8 convolution_add_fusion.6
  158.7 0.8 convolution_add_fusion.5
  159.6 0.8 convolution_add_fusion.4
  160.4 0.8 convolution_add_fusion.3
  161.2 0.8 convolution_add_fusion.2
  162.1 0.8 convolution_add_fusion.1
  162.9 0.8 convolution_add_fusion
  163.8 0.3 copy-done
  164.1 1.3 convert_add_fusion
  (44 shorter events, 2.4 us)
Async XLA Ops:
  50.8 10.8 %collective-permute-start = (bf16[2,4,96,256]{3,2,1,0:T(8,128)(2,1)S(1)}, bf16[2,4,96,256]{3,2,1,0:T(8,128)(2,1)S(1)}, u32[]{:S(2)}, u32[]{:S(2)}) collective-permute-start(bf16[2,4,96,256]{3,2,1,0:T(8,128)(2,1)S(1)} %slice.469), channel_id=1, source_target_pairs={{0,2},{2,4},{4,6},{6,8},{8,10},{10,12},{12,14},{14,16},{16,18},{18... | collective-permute-start | bytes 1179656 | tf_op jit(solution)/shard_map/ppermute | solution.py:25
  61.7 4.9 %collective-permute-start.1 = (bf16[6,1,96,256]{3,2,1,0:T(8,128)(2,1)S(1)}, bf16[6,1,96,256]{3,2,1,0:T(8,128)(2,1)S(1)}, u32[]{:S(2)}, u32[]{:S(2)}) collective-permute-start(bf16[6,1,96,256]{3,2,1,0:T(8,128)(2,1)S(1)} %get-tuple-element.95), channel_id=1, source_target_pairs={{0,1},{2,3},{4,5},{6,7},{8,9},{10,11},{12,13},{14,15},{16,17},{18,... | collective-permute-start | bytes 884744 | tf_op jit(solution)/shard_map/ppermute | solution.py:16
  63.0 3.6 %collective-permute-start.2 = (bf16[6,1,96,256]{3,2,1,0:T(8,128)(2,1)S(1)}, bf16[6,1,96,256]{3,2,1,0:T(8,128)(2,1)S(1)}, u32[]{:S(2)}, u32[]{:S(2)}) collective-permute-start(bf16[6,1,96,256]{3,2,1,0:T(8,128)(2,1)S(1)} %get-tuple-element.96), channel_id=1, source_target_pairs={{1,0},{3,2},{5,4},{7,6},{9,8},{11,10},{13,12},{15,14},{17,16},{19,... | collective-permute-start | bytes 884744 | tf_op jit(solution)/shard_map/ppermute | solution.py:17
  84.0 44.1 %copy-start.2 = (f32[256]{0:T(256)S(1)}, f32[256]{0:T(256)}, u32[]{:S(2)}) copy-start(f32[256]{0:T(256)} %param.14) | copy-start | bytes 3076
  84.1 44.1 %copy-start.3 = (f32[256]{0:T(256)S(1)}, f32[256]{0:T(256)}, u32[]{:S(2)}) copy-start(f32[256]{0:T(256)} %param.13) | copy-start | bytes 3076
  128.7 14.4 %copy-start.1 = (bf16[3,3,3,256,256]{4,3,2,1,0:T(8,128)(2,1)S(1)}, bf16[3,3,3,256,256]{4,3,2,1,0:T(8,128)(2,1)}, u32[]{:S(2)}) copy-start(bf16[3,3,3,256,256]{4,3,2,1,0:T(8,128)(2,1)} %param.15) | copy-start | bytes 10616836
  128.7 11.7 %collective-permute-start.3 = (bf16[2,4,96,256]{3,2,1,0:T(8,128)(2,1)S(1)}, bf16[2,4,96,256]{3,2,1,0:T(8,128)(2,1)S(1)}, u32[]{:S(2)}, u32[]{:S(2)}) collective-permute-start(bf16[2,4,96,256]{3,2,1,0:T(8,128)(2,1)S(1)} %slice.514), channel_id=1, source_target_pairs={{0,2},{2,4},{4,6},{6,8},{8,10},{10,12},{12,14},{14,16},{16,18},{18... | collective-permute-start | bytes 1179656 | tf_op jit(solution)/shard_map/ppermute | solution.py:25
  140.5 3.0 %collective-permute-start.4 = (bf16[6,1,96,256]{3,2,1,0:T(8,128)(2,1)S(1)}, bf16[6,1,96,256]{3,2,1,0:T(8,128)(2,1)S(1)}, u32[]{:S(2)}, u32[]{:S(2)}) collective-permute-start(bf16[6,1,96,256]{3,2,1,0:T(8,128)(2,1)S(1)} %get-tuple-element.93), channel_id=1, source_target_pairs={{0,1},{2,3},{4,5},{6,7},{8,9},{10,11},{12,13},{14,15},{16,17},{18,... | collective-permute-start | bytes 884744 | tf_op jit(solution)/shard_map/ppermute | solution.py:16
  141.8 3.5 %collective-permute-start.5 = (bf16[6,1,96,256]{3,2,1,0:T(8,128)(2,1)S(1)}, bf16[6,1,96,256]{3,2,1,0:T(8,128)(2,1)S(1)}, u32[]{:S(2)}, u32[]{:S(2)}) collective-permute-start(bf16[6,1,96,256]{3,2,1,0:T(8,128)(2,1)S(1)} %get-tuple-element.94), channel_id=1, source_target_pairs={{1,0},{3,2},{5,4},{7,6},{9,8},{11,10},{13,12},{15,14},{17,16},{19,... | collective-permute-start | bytes 884744 | tf_op jit(solution)/shard_map/ppermute | solution.py:17
  162.9 1.1 copy-start
where the time goes:
time: 167 us; the launch traced here: 165 us
  blocking collectives  84.4 us (51%)
  other arithmetic  28.4 us (17%)
  matrix products  14.7 us (9%)
  waiting for transfers between devices  14.2 us (9%)
  starting transfers between devices  13.9 us (8%)
  local copies, waits for them, and re-layouts  7.32 us (4%)
  between operations  2.52 us (2%)
    psum x2, blocking collectives, clip_stats(): lax.psum((own_row * local_sum[None, :], own_row * local_square[None, :]),...  84.4 us
    concatenate x4, other arithmetic, causal_conv(): padded = jnp.pad(extended, ((0, 0), (0, 0), (1, 1), (0, 0)), mode='edge')  14.9 us
    dot_general x18, matrix products, causal_conv(): jnp.dot(stacked, kernel[tap_time, tap_row].reshape(3 * width, -1), prefer...  14.7 us
    ppermute x2, waiting for transfers between devices, passed_along(): return lax.ppermute(block, axis, route)  12.4 us
    ppermute x2, starting transfers between devices, passed_along(): return lax.ppermute(block, axis, route)  8.67 us
    concatenate x18, other arithmetic, causal_conv(): jnp.concatenate([window[:, :, offset:offset + cols] for offset in range(3...  4.19 us
  transfers between devices with their start and end apart: 6, of which 3 were waited for; matrix products, arithmetic and copies ran while one was open for 2% of the time, Pallas kernels for 0%

commit v1 on v0

--- a/solution.py
+++ b/solution.py
@@ -25,6 +25,17 @@
     return lax.ppermute(block, axis, route)
 
 
+def summed_over(table, axes):
+    peers = lax.axis_size(axes)
+    if peers & (peers - 1):
+        return lax.psum(table, axes)
+    step = 1
+    while step < peers:
+        table = table + lax.ppermute(table, axes, [(i, i ^ step) for i in range(peers)])
+        step *= 2
+    return table
+
+
 def clip_stats(values, clip_ids):
     width = values.shape[3]
     grouped = values.reshape(-1, GROUPS, width // GROUPS)
@@ -34,9 +45,9 @@
     own_slab = lax.axis_index("tm")
     own_clip = lax.dynamic_index_in_dim(clip_ids, own_slab, keepdims=False)
     own_row = (jnp.arange(slab_count, dtype=jnp.int32) == own_clip).astype(jnp.float32)[:, None]
-    table_sum, table_square = lax.psum(
-        (own_row * local_sum[None, :], own_row * local_square[None, :]), ("tm", "space")
-    )
+    table = jnp.concatenate([own_row * local_sum[None, :], own_row * local_square[None, :]], axis=1)
+    table = summed_over(table, ("tm", "space"))
+    table_sum, table_square = (table[:, :GROUPS], table[:, GROUPS:])
     clip_sum = jnp.sum(table_sum * own_row, axis=0)
     clip_square = jnp.sum(table_square * own_row, axis=0)
     slabs_in = jnp.sum((clip_ids == own_clip).astype(jnp.float32))

time: 167 us -> 115 us (0.69)
  the two profiles are of different devices: /device:TPU:0 before, /device:TPU:9 now
where the time goes in v1:
time: 115 us; the launch traced here: 114 us
  waiting for transfers between devices  31 us (27%)
  starting transfers between devices  30.4 us (26%)
  other arithmetic  28.6 us (25%)
  matrix products  14.7 us (13%)
  local copies, waits for them, and re-layouts  7.28 us (6%)
  between operations  2.54 us (2%)
    ppermute x10, waiting for transfers between devices, summed_over(): lax.ppermute(table, axes, [(i, i ^ step) for i in range(peers)])  15.9 us
    ppermute x2, starting transfers between devices, padded_2(): after = lax.ppermute(leading, axis, down)  15 us
    concatenate x4, other arithmetic, causal_conv(): padded = jnp.pad(extended, ((0, 0), (0, 0), (1, 1), (0, 0)), mode='edge')  14.9 us
    dot_general x18, matrix products, causal_conv(): jnp.dot(stacked, kernel[tap_time, tap_row].reshape(3 * width, -1), prefer...  14.7 us
    ppermute x2, waiting for transfers between devices, passed_along(): return lax.ppermute(block, axis, route)  14.3 us
    ppermute x10, starting transfers between devices, summed_over(): lax.ppermute(table, axes, [(i, i ^ step) for i in range(peers)])  7.57 us
    ppermute x2, starting transfers between devices, passed_along(): return lax.ppermute(block, axis, route)  5.3 us
    concatenate x18, other arithmetic, causal_conv(): jnp.concatenate([window[:, :, offset:offset + cols] for offset in range(3...  4.19 us
  transfers between devices with their start and end apart: 16, of which 12 were waited for; matrix products, arithmetic and copies ran while one was open for 4% of the time, Pallas kernels for 0%

profile of v1, /device:TPU:9, one launch (start us, length us, event | category | flops | bytes accessed | tf_op | source)
XLA Modules:
  0.0 114.5 jit_solution(8703114356517355878)
XLA Ops:
  0.0 1.3 %fusion.62 = (s32[1]{0:T(128)}, s32[1]{0:T(128)}) fusion(s32[16]{0:T(128)} %param.9, s32[]{:T(128)S(6)} %max.3, s32[]{:T(128)S(6)} %select_n.32), kind=kLoop, calls=%fused_computation.198 | loop fusion | bytes 24 | tf_op jit(solution)/shard_map/jit(dynamic_index_in_dim)/dynamic_slice | solution.py:126
  1.3 0.6 compare_convert_fusion.1
  2.0 1.4 %convert_reduce_fusion = (f32[256]{0:T(256)S(1)}, f32[256]{0:T(256)S(1)}) fusion(bf16[4,4,96,256]{3,2,1,0:T(8,128)(2,1)} %param.8), kind=kLoop, calls=%fused_computation.51 | loop fusion | flops 1572352 | bytes 788480 | tf_op jit(solution)/shard_map/reduce_sum | solution.py:42
  3.9 0.7 collective-permute-start
  4.6 0.8 collective-permute-done
  5.5 1.2 %collective-permute-start.1 = (f32[16,64]{1,0:T(8,128)S(1)}, f32[16,64]{1,0:T(8,128)S(1)}, u32[]{:S(2)}, u32[]{:S(2)}) collective-permute-start(f32[16,64]{1,0:T(8,128)S(1)} %fusion.102), channel_id=1, source_target_pairs={{0,2},{1,3},{2,0},{3,1},{4,6},{5,7},{6,4},{7,5},{8,10},{9,11},{10,... | collective-permute-start | bytes 12296 | tf_op jit(solution)/shard_map/ppermute | solution.py:34
  6.7 1.3 %collective-permute-done.1 = f32[16,64]{1,0:T(8,128)S(1)} collective-permute-done((f32[16,64]{1,0:T(8,128)S(1)}, f32[16,64]{1,0:T(8,128)S(1)}, u32[]{:S(2)}, u32[]{:S(2)}) %collective-permute-start.1) | collective-permute-done | bytes 4128 | tf_op jit(solution)/shard_map/ppermute | solution.py:34
  8.0 1.2 %collective-permute-start.2 = (f32[16,64]{1,0:T(8,128)S(1)}, f32[16,64]{1,0:T(8,128)S(1)}, u32[]{:S(2)}, u32[]{:S(2)}) collective-permute-start(f32[16,64]{1,0:T(8,128)S(1)} %add.128), channel_id=1, source_target_pairs={{0,4},{1,5},{2,6},{3,7},{4,0},{5,1},{6,2},{7,3},{8,12},{9,13},{10,... | collective-permute-start | bytes 12296 | tf_op jit(solution)/shard_map/ppermute | solution.py:34
  9.3 1.3 %collective-permute-done.2 = f32[16,64]{1,0:T(8,128)S(1)} collective-permute-done((f32[16,64]{1,0:T(8,128)S(1)}, f32[16,64]{1,0:T(8,128)S(1)}, u32[]{:S(2)}, u32[]{:S(2)}) %collective-permute-start.2) | collective-permute-done | bytes 4128 | tf_op jit(solution)/shard_map/ppermute | solution.py:34
  10.5 2.5 %collective-permute-done.3 = f32[16,64]{1,0:T(8,128)S(1)} collective-permute-done((f32[16,64]{1,0:T(8,128)S(1)}, f32[16,64]{1,0:T(8,128)S(1)}, u32[]{:S(2)}, u32[]{:S(2)}) %collective-permute-start.3) | collective-permute-done | bytes 4128 | tf_op jit(solution)/shard_map/ppermute | solution.py:34
  13.0 2.3 %collective-permute-start.4 = (f32[16,64]{1,0:T(8,128)S(1)}, f32[16,64]{1,0:T(8,128)S(1)}, u32[]{:S(2)}, u32[]{:S(2)}) collective-permute-start(f32[16,64]{1,0:T(8,128)S(1)} %add.130), channel_id=1, source_target_pairs={{0,16},{1,17},{2,18},{3,19},{4,20},{5,21},{6,22},{7,23},{8,24},{9,... | collective-permute-start | bytes 12296 | tf_op jit(solution)/shard_map/ppermute | solution.py:34
  15.3 1.9 %fusion.54 = f32[]{:T(128)} fusion(s32[16]{0:T(128)} %param.9, s32[]{:T(128)} %bitcast), kind=kLoop, calls=%fused_computation.186 | loop fusion | flops 47 | bytes 72 | tf_op jit(solution)/shard_map/reduce_sum | solution.py:53
  18.3 1.7 %fusion.17 = bf16[4,4,96,256]{3,2,1,0:T(8,128)(2,1)S(1)} fusion(bf16[4,4,96,256]{3,2,1,0:T(8,128)(2,1)} %param.8, f32[256]{0:T(256)} %param.11, f32[256]{0:T(256)} %param.10, f32[256]{0:T(256)S(1)} %mul.156, f32[256]{0:T(256)S(1)} %sub.45), kind=kLoop, calls=%fused_computation.91 | loop fusion | flops 3932160 | bytes 1576960 | tf_op jit(solution)/shard_map/convert_element_type | solution.py:71
  20.0 3.1 %collective-permute-start.5 = (bf16[2,4,96,256]{3,2,1,0:T(8,128)(2,1)S(1)}, bf16[2,4,96,256]{3,2,1,0:T(8,128)(2,1)S(1)}, u32[]{:S(2)}, u32[]{:S(2)}) collective-permute-start(bf16[2,4,96,256]{3,2,1,0:T(8,128)(2,1)S(1)} %slice.487), channel_id=1, source_target_pairs={{0,2},{2,4},{4,6},{6,8},{8,10},{10,12},{12,14},{14,16},{16,18},{18... | collective-permute-start | bytes 1179656 | tf_op jit(solution)/shard_map/ppermute | solution.py:25
  24.5 5.9 %collective-permute-done.5 = bf16[2,4,96,256]{3,2,1,0:T(8,128)(2,1)S(1)} collective-permute-done((bf16[2,4,96,256]{3,2,1,0:T(8,128)(2,1)S(1)}, bf16[2,4,96,256]{3,2,1,0:T(8,128)(2,1)S(1)}, u32[]{:S(2)}, u32[]{:S(2)}) %collective-permute-start.5) | collective-permute-done | bytes 393248 | tf_op jit(solution)/shard_map/ppermute | solution.py:25
  30.5 1.3 %collective-permute-start.6 = (bf16[6,1,96,256]{3,2,1,0:T(8,128)(2,1)S(1)}, bf16[6,1,96,256]{3,2,1,0:T(8,128)(2,1)S(1)}, u32[]{:S(2)}, u32[]{:S(2)}) collective-permute-start(bf16[6,1,96,256]{3,2,1,0:T(8,128)(2,1)S(1)} %get-tuple-element.91), channel_id=1, source_target_pairs={{0,1},{2,3},{4,5},{6,7},{8,9},{10,11},{12,13},{14,15},{16,17},{18,... | collective-permute-start | bytes 884744 | tf_op jit(solution)/shard_map/ppermute | solution.py:16
  31.8 7.2 %collective-permute-start.7 = (bf16[6,1,96,256]{3,2,1,0:T(8,128)(2,1)S(1)}, bf16[6,1,96,256]{3,2,1,0:T(8,128)(2,1)S(1)}, u32[]{:S(2)}, u32[]{:S(2)}) collective-permute-start(bf16[6,1,96,256]{3,2,1,0:T(8,128)(2,1)S(1)} %get-tuple-element.92), channel_id=1, source_target_pairs={{1,0},{3,2},{5,4},{7,6},{9,8},{11,10},{13,12},{15,14},{17,16},{19,... | collective-permute-start | bytes 884744 | tf_op jit(solution)/shard_map/ppermute | solution.py:17
  38.9 2.3 %fusion.57 = (bf16[1,1,3,256,256]{4,3,2,1,0:T(8,128)(2,1)S(1)}, bf16[1,1,3,256,256]{4,3,2,1,0:T(8,128)(2,1)S(1)}, bf16[1,1,3,256,256]{4,3,2,1,0:T(8,128)(2,1)S(1...) fusion(bf16[3,3,3,256,256]{4,3,2,1,0:T(8,128)(2,1)} %param.12), kind=kLoop, calls=%fused_computation.193 | loop fusion | bytes 7077888 | tf_op jit(solution)/shard_map/slice | solution.py:107
  41.3 0.4 fusion.6
  41.7 0.9 fusion.60
  42.6 3.9 %fusion.42 = (bf16[4,4,96,256]{3,2,1,0:T(8,128)(2,1)S(1)}, bf16[4,4,96,256]{3,2,1,0:T(8,128)(2,1)S(1)}, bf16[4,4,96,256]{3,2,1,0:T(8,128)(2,1)S(1)}, bf16[4,4,96...) fusion(bf16[6,6,96,256]{3,2,1,0:T(8,128)(2,1)S(1)} %fusion.6, ...), kind=kLoop, calls=%fused_computation.150 | loop fusion | flops 12582912 | bytes 8079360 | tf_op jit(solution)/shard_map/jit(_pad)/concatenate | solution.py:96
  46.5 3.5 %fusion.34 = (bf16[4,4,96,256]{3,2,1,0:T(8,128)(2,1)S(1)}, bf16[4,4,96,256]{3,2,1,0:T(8,128)(2,1)S(1)}, bf16[4,4,96,256]{3,2,1,0:T(8,128)(2,1)S(1)}, bf16[4,4,96...) fusion(bf16[6,6,96,256]{3,2,1,0:T(8,128)(2,1)S(1)} %fusion.6, ...), kind=kLoop, calls=%fused_computation.142 | loop fusion | flops 12582912 | bytes 8079360 | tf_op jit(solution)/shard_map/jit(_pad)/concatenate | solution.py:96
  50.0 0.9 fusion.4
  51.0 0.8 fusion.63
  52.3 0.8 convolution_add_fusion.15
  53.1 0.8 convolution_add_fusion.14
  54.0 0.8 convolution_add_fusion.13
  54.8 0.2 pad_maximum_fusion.8
  55.0 0.8 convolution_add_fusion.12
  55.9 0.8 convolution_add_fusion.11
  56.9 0.8 convolution_add_fusion.10
  57.9 0.8 convolution_add_fusion.9
  58.7 0.8 fusion.55
  60.1 1.2 %collective-permute-done.8 = f32[16,64]{1,0:T(8,128)S(1)} collective-permute-done((f32[16,64]{1,0:T(8,128)S(1)}, f32[16,64]{1,0:T(8,128)S(1)}, u32[]{:S(2)}, u32[]{:S(2)}) %collective-permute-start.8) | collective-permute-done | bytes 4128 | tf_op jit(solution)/shard_map/ppermute | solution.py:34
  61.4 2.5 %collective-permute-done.9 = f32[16,64]{1,0:T(8,128)S(1)} collective-permute-done((f32[16,64]{1,0:T(8,128)S(1)}, f32[16,64]{1,0:T(8,128)S(1)}, u32[]{:S(2)}, u32[]{:S(2)}) %collective-permute-start.9) | collective-permute-done | bytes 4128 | tf_op jit(solution)/shard_map/ppermute | solution.py:34
  63.9 0.3 collective-permute-start.10
  64.2 2.2 %collective-permute-done.10 = f32[16,64]{1,0:T(8,128)S(1)} collective-permute-done((f32[16,64]{1,0:T(8,128)S(1)}, f32[16,64]{1,0:T(8,128)S(1)}, u32[]{:S(2)}, u32[]{:S(2)}) %collective-permute-start.10) | collective-permute-done | bytes 4128 | tf_op jit(solution)/shard_map/ppermute | solution.py:34
  66.4 2.5 %collective-permute-done.11 = f32[16,64]{1,0:T(8,128)S(1)} collective-permute-done((f32[16,64]{1,0:T(8,128)S(1)}, f32[16,64]{1,0:T(8,128)S(1)}, u32[]{:S(2)}, u32[]{:S(2)}) %collective-permute-start.11) | collective-permute-done | bytes 4128 | tf_op jit(solution)/shard_map/ppermute | solution.py:34
  68.9 1.8 %collective-permute-start.12 = (f32[16,64]{1,0:T(8,128)S(1)}, f32[16,64]{1,0:T(8,128)S(1)}, u32[]{:S(2)}, u32[]{:S(2)}) collective-permute-start(f32[16,64]{1,0:T(8,128)S(1)} %add.147), channel_id=1, source_target_pairs={{0,16},{1,17},{2,18},{3,19},{4,20},{5,21},{6,22},{7,23},{8,24},{9,... | collective-permute-start | bytes 12296 | tf_op jit(solution)/shard_map/ppermute | solution.py:34
  70.6 1.7 %collective-permute-done.12 = f32[16,64]{1,0:T(8,128)S(1)} collective-permute-done((f32[16,64]{1,0:T(8,128)S(1)}, f32[16,64]{1,0:T(8,128)S(1)}, u32[]{:S(2)}, u32[]{:S(2)}) %collective-permute-start.12) | collective-permute-done | bytes 4128 | tf_op jit(solution)/shard_map/ppermute | solution.py:34
  72.8 0.5 multiply_convert_fusion
  73.4 2.2 %collective-permute-start.13 = (bf16[2,4,96,256]{3,2,1,0:T(8,128)(2,1)S(1)}, bf16[2,4,96,256]{3,2,1,0:T(8,128)(2,1)S(1)}, u32[]{:S(2)}, u32[]{:S(2)}) collective-permute-start(bf16[2,4,96,256]{3,2,1,0:T(8,128)(2,1)S(1)} %slice.534), channel_id=1, source_target_pairs={{0,2},{2,4},{4,6},{6,8},{8,10},{10,12},{12,14},{14,16},{16,18},{18... | collective-permute-start | bytes 1179656 | tf_op jit(solution)/shard_map/ppermute | solution.py:25
  75.6 8.4 %collective-permute-done.13 = bf16[2,4,96,256]{3,2,1,0:T(8,128)(2,1)S(1)} collective-permute-done((bf16[2,4,96,256]{3,2,1,0:T(8,128)(2,1)S(1)}, bf16[2,4,96,256]{3,2,1,0:T(8,128)(2,1)S(1)}, u32[]{:S(2)}, u32[]{:S(2)}) %collective-permute-start.13) | collective-permute-done | bytes 393248 | tf_op jit(solution)/shard_map/ppermute | solution.py:25
  84.1 1.3 %collective-permute-start.14 = (bf16[6,1,96,256]{3,2,1,0:T(8,128)(2,1)S(1)}, bf16[6,1,96,256]{3,2,1,0:T(8,128)(2,1)S(1)}, u32[]{:S(2)}, u32[]{:S(2)}) collective-permute-start(bf16[6,1,96,256]{3,2,1,0:T(8,128)(2,1)S(1)} %get-tuple-element.89), channel_id=1, source_target_pairs={{0,1},{2,3},{4,5},{6,7},{8,9},{10,11},{12,13},{14,15},{16,17},{18,... | collective-permute-start | bytes 884744 | tf_op jit(solution)/shard_map/ppermute | solution.py:16
  85.4 7.8 %collective-permute-start.15 = (bf16[6,1,96,256]{3,2,1,0:T(8,128)(2,1)S(1)}, bf16[6,1,96,256]{3,2,1,0:T(8,128)(2,1)S(1)}, u32[]{:S(2)}, u32[]{:S(2)}) collective-permute-start(bf16[6,1,96,256]{3,2,1,0:T(8,128)(2,1)S(1)} %get-tuple-element.90), channel_id=1, source_target_pairs={{1,0},{3,2},{5,4},{7,6},{9,8},{11,10},{13,12},{15,14},{17,16},{19,... | collective-permute-start | bytes 884744 | tf_op jit(solution)/shard_map/ppermute | solution.py:17
  93.2 0.3 fusion.56
  93.6 0.8 collective-permute-done.15
  94.4 0.4 fusion.7
  94.7 0.9 fusion.58
  95.7 4.1 %fusion.26 = (bf16[4,4,96,256]{3,2,1,0:T(8,128)(2,1)S(1)}, bf16[4,4,96,256]{3,2,1,0:T(8,128)(2,1)S(1)}, bf16[4,4,96,256]{3,2,1,0:T(8,128)(2,1)S(1)}, bf16[4,4,96...) fusion(bf16[6,6,96,256]{3,2,1,0:T(8,128)(2,1)S(1)} %fusion.7, ...), kind=kLoop, calls=%fused_computation.134 | loop fusion | flops 12582912 | bytes 8079360 | tf_op jit(solution)/shard_map/jit(_pad)/concatenate | solution.py:96
  99.8 3.5 %fusion.18 = (bf16[4,4,96,256]{3,2,1,0:T(8,128)(2,1)S(1)}, bf16[4,4,96,256]{3,2,1,0:T(8,128)(2,1)S(1)}, bf16[4,4,96,256]{3,2,1,0:T(8,128)(2,1)S(1)}, bf16[4,4,96...) fusion(bf16[6,6,96,256]{3,2,1,0:T(8,128)(2,1)S(1)} %fusion.7, ...), kind=kLoop, calls=%fused_computation.126 | loop fusion | flops 12582912 | bytes 8079360 | tf_op jit(solution)/shard_map/jit(_pad)/concatenate | solution.py:96
  103.3 0.7 fusion.2
  104.2 0.8 fusion.64
  105.0 0.2 pad_maximum_fusion.19
  106.2 0.8 convolution_add_fusion.7
  107.0 0.8 convolution_add_fusion.6
  107.8 0.8 convolution_add_fusion.5
  108.7 0.8 convolution_add_fusion.4
  109.5 0.8 convolution_add_fusion.3
  110.3 0.8 convolution_add_fusion.2
  111.2 0.8 convolution_add_fusion.1
  112.0 0.8 convolution_add_fusion
  112.9 0.3 copy-done
  113.2 1.3 %convert_add_fusion = f32[4,4,96,256]{3,2,1,0:T(8,128)} fusion(f32[4,4,96,256]{3,2,1,0:T(8,128)S(1)} %bitcast.102, bf16[4,4,96,256]{3,2,1,0:T(8,128)(2,1)S(1)} %copy-done), kind=kLoop, calls=%fused_computation.48 | loop fusion | flops 786432 | bytes 3932160 | tf_op jit(solution)/shard_map/add | solution.py:137
  (74 shorter events, 4.9 us)
Async XLA Ops:
  3.9 1.5 %collective-permute-start = (f32[16,64]{1,0:T(8,128)S(1)}, f32[16,64]{1,0:T(8,128)S(1)}, u32[]{:S(2)}, u32[]{:S(2)}) collective-permute-start(f32[16,64]{1,0:T(8,128)S(1)} %pad_maximum_fusion.24), channel_id=1, source_target_pairs={{0,1},{1,0},{2,3},{3,2},{4,5},{5,4},{6,7},{7,6},{8,9},{9,8},{10,11... | collective-permute-start | bytes 12296 | tf_op jit(solution)/shard_map/ppermute | solution.py:34
  5.5 2.5 %collective-permute-start.1 = (f32[16,64]{1,0:T(8,128)S(1)}, f32[16,64]{1,0:T(8,128)S(1)}, u32[]{:S(2)}, u32[]{:S(2)}) collective-permute-start(f32[16,64]{1,0:T(8,128)S(1)} %fusion.102), channel_id=1, source_target_pairs={{0,2},{1,3},{2,0},{3,1},{4,6},{5,7},{6,4},{7,5},{8,10},{9,11},{10,... | collective-permute-start | bytes 12296 | tf_op jit(solution)/shard_map/ppermute | solution.py:34
  8.0 2.5 %collective-permute-start.2 = (f32[16,64]{1,0:T(8,128)S(1)}, f32[16,64]{1,0:T(8,128)S(1)}, u32[]{:S(2)}, u32[]{:S(2)}) collective-permute-start(f32[16,64]{1,0:T(8,128)S(1)} %add.128), channel_id=1, source_target_pairs={{0,4},{1,5},{2,6},{3,7},{4,0},{5,1},{6,2},{7,3},{8,12},{9,13},{10,... | collective-permute-start | bytes 12296 | tf_op jit(solution)/shard_map/ppermute | solution.py:34
  10.5 2.5 %collective-permute-start.3 = (f32[16,64]{1,0:T(8,128)S(1)}, f32[16,64]{1,0:T(8,128)S(1)}, u32[]{:S(2)}, u32[]{:S(2)}) collective-permute-start(f32[16,64]{1,0:T(8,128)S(1)} %add.129), channel_id=1, source_target_pairs={{0,8},{1,9},{2,10},{3,11},{4,12},{5,13},{6,14},{7,15},{8,0},{9,1},... | collective-permute-start | bytes 12296 | tf_op jit(solution)/shard_map/ppermute | solution.py:34
  13.0 4.8 %collective-permute-start.4 = (f32[16,64]{1,0:T(8,128)S(1)}, f32[16,64]{1,0:T(8,128)S(1)}, u32[]{:S(2)}, u32[]{:S(2)}) collective-permute-start(f32[16,64]{1,0:T(8,128)S(1)} %add.130), channel_id=1, source_target_pairs={{0,16},{1,17},{2,18},{3,19},{4,20},{5,21},{6,22},{7,23},{8,24},{9,... | collective-permute-start | bytes 12296 | tf_op jit(solution)/shard_map/ppermute | solution.py:34
  20.0 10.3 %collective-permute-start.5 = (bf16[2,4,96,256]{3,2,1,0:T(8,128)(2,1)S(1)}, bf16[2,4,96,256]{3,2,1,0:T(8,128)(2,1)S(1)}, u32[]{:S(2)}, u32[]{:S(2)}) collective-permute-start(bf16[2,4,96,256]{3,2,1,0:T(8,128)(2,1)S(1)} %slice.487), channel_id=1, source_target_pairs={{0,2},{2,4},{4,6},{6,8},{8,10},{10,12},{12,14},{14,16},{16,18},{18... | collective-permute-start | bytes 1179656 | tf_op jit(solution)/shard_map/ppermute | solution.py:25
  30.5 10.8 %collective-permute-start.6 = (bf16[6,1,96,256]{3,2,1,0:T(8,128)(2,1)S(1)}, bf16[6,1,96,256]{3,2,1,0:T(8,128)(2,1)S(1)}, u32[]{:S(2)}, u32[]{:S(2)}) collective-permute-start(bf16[6,1,96,256]{3,2,1,0:T(8,128)(2,1)S(1)} %get-tuple-element.91), channel_id=1, source_target_pairs={{0,1},{2,3},{4,5},{6,7},{8,9},{10,11},{12,13},{14,15},{16,17},{18,... | collective-permute-start | bytes 884744 | tf_op jit(solution)/shard_map/ppermute | solution.py:16
  31.8 9.5 %collective-permute-start.7 = (bf16[6,1,96,256]{3,2,1,0:T(8,128)(2,1)S(1)}, bf16[6,1,96,256]{3,2,1,0:T(8,128)(2,1)S(1)}, u32[]{:S(2)}, u32[]{:S(2)}) collective-permute-start(bf16[6,1,96,256]{3,2,1,0:T(8,128)(2,1)S(1)} %get-tuple-element.92), channel_id=1, source_target_pairs={{1,0},{3,2},{5,4},{7,6},{9,8},{11,10},{13,12},{15,14},{17,16},{19,... | collective-permute-start | bytes 884744 | tf_op jit(solution)/shard_map/ppermute | solution.py:17
  58.7 14.1 %copy-start.2 = (f32[256]{0:T(256)S(1)}, f32[256]{0:T(256)}, u32[]{:S(2)}) copy-start(f32[256]{0:T(256)} %param.14) | copy-start | bytes 3076
  58.7 14.1 %copy-start.3 = (f32[256]{0:T(256)S(1)}, f32[256]{0:T(256)}, u32[]{:S(2)}) copy-start(f32[256]{0:T(256)} %param.13) | copy-start | bytes 3076
  60.1 1.2 %collective-permute-start.8 = (f32[16,64]{1,0:T(8,128)S(1)}, f32[16,64]{1,0:T(8,128)S(1)}, u32[]{:S(2)}, u32[]{:S(2)}) collective-permute-start(f32[16,64]{1,0:T(8,128)S(1)} %pad_maximum_fusion.25), channel_id=1, source_target_pairs={{0,1},{1,0},{2,3},{3,2},{4,5},{5,4},{6,7},{7,6},{8,9},{9,8},{10,11... | collective-permute-start | bytes 12296 | tf_op jit(solution)/shard_map/ppermute | solution.py:34
  61.4 2.5 %collective-permute-start.9 = (f32[16,64]{1,0:T(8,128)S(1)}, f32[16,64]{1,0:T(8,128)S(1)}, u32[]{:S(2)}, u32[]{:S(2)}) collective-permute-start(f32[16,64]{1,0:T(8,128)S(1)} %fusion.101), channel_id=1, source_target_pairs={{0,2},{1,3},{2,0},{3,1},{4,6},{5,7},{6,4},{7,5},{8,10},{9,11},{10,... | collective-permute-start | bytes 12296 | tf_op jit(solution)/shard_map/ppermute | solution.py:34
  63.9 2.5 %collective-permute-start.10 = (f32[16,64]{1,0:T(8,128)S(1)}, f32[16,64]{1,0:T(8,128)S(1)}, u32[]{:S(2)}, u32[]{:S(2)}) collective-permute-start(f32[16,64]{1,0:T(8,128)S(1)} %add.145), channel_id=1, source_target_pairs={{0,4},{1,5},{2,6},{3,7},{4,0},{5,1},{6,2},{7,3},{8,12},{9,13},{10,... | collective-permute-start | bytes 12296 | tf_op jit(solution)/shard_map/ppermute | solution.py:34
  66.4 2.5 %collective-permute-start.11 = (f32[16,64]{1,0:T(8,128)S(1)}, f32[16,64]{1,0:T(8,128)S(1)}, u32[]{:S(2)}, u32[]{:S(2)}) collective-permute-start(f32[16,64]{1,0:T(8,128)S(1)} %add.146), channel_id=1, source_target_pairs={{0,8},{1,9},{2,10},{3,11},{4,12},{5,13},{6,14},{7,15},{8,0},{9,1},... | collective-permute-start | bytes 12296 | tf_op jit(solution)/shard_map/ppermute | solution.py:34
  68.9 3.5 %collective-permute-start.12 = (f32[16,64]{1,0:T(8,128)S(1)}, f32[16,64]{1,0:T(8,128)S(1)}, u32[]{:S(2)}, u32[]{:S(2)}) collective-permute-start(f32[16,64]{1,0:T(8,128)S(1)} %add.147), channel_id=1, source_target_pairs={{0,16},{1,17},{2,18},{3,19},{4,20},{5,21},{6,22},{7,23},{8,24},{9,... | collective-permute-start | bytes 12296 | tf_op jit(solution)/shard_map/ppermute | solution.py:34
  73.3 19.9 %copy-start.1 = (bf16[3,3,3,256,256]{4,3,2,1,0:T(8,128)(2,1)S(1)}, bf16[3,3,3,256,256]{4,3,2,1,0:T(8,128)(2,1)}, u32[]{:S(2)}) copy-start(bf16[3,3,3,256,256]{4,3,2,1,0:T(8,128)(2,1)} %param.15) | copy-start | bytes 10616836
  73.4 10.6 %collective-permute-start.13 = (bf16[2,4,96,256]{3,2,1,0:T(8,128)(2,1)S(1)}, bf16[2,4,96,256]{3,2,1,0:T(8,128)(2,1)S(1)}, u32[]{:S(2)}, u32[]{:S(2)}) collective-permute-start(bf16[2,4,96,256]{3,2,1,0:T(8,128)(2,1)S(1)} %slice.534), channel_id=1, source_target_pairs={{0,2},{2,4},{4,6},{6,8},{8,10},{10,12},{12,14},{14,16},{16,18},{18... | collective-permute-start | bytes 1179656 | tf_op jit(solution)/shard_map/ppermute | solution.py:25
  84.1 9.5 %collective-permute-start.14 = (bf16[6,1,96,256]{3,2,1,0:T(8,128)(2,1)S(1)}, bf16[6,1,96,256]{3,2,1,0:T(8,128)(2,1)S(1)}, u32[]{:S(2)}, u32[]{:S(2)}) collective-permute-start(bf16[6,1,96,256]{3,2,1,0:T(8,128)(2,1)S(1)} %get-tuple-element.89), channel_id=1, source_target_pairs={{0,1},{2,3},{4,5},{6,7},{8,9},{10,11},{12,13},{14,15},{16,17},{18,... | collective-permute-start | bytes 884744 | tf_op jit(solution)/shard_map/ppermute | solution.py:16
  85.4 9.0 %collective-permute-start.15 = (bf16[6,1,96,256]{3,2,1,0:T(8,128)(2,1)S(1)}, bf16[6,1,96,256]{3,2,1,0:T(8,128)(2,1)S(1)}, u32[]{:S(2)}, u32[]{:S(2)}) collective-permute-start(bf16[6,1,96,256]{3,2,1,0:T(8,128)(2,1)S(1)} %get-tuple-element.90), channel_id=1, source_target_pairs={{1,0},{3,2},{5,4},{7,6},{9,8},{11,10},{13,12},{15,14},{17,16},{19,... | collective-permute-start | bytes 884744 | tf_op jit(solution)/shard_map/ppermute | solution.py:17
  112.0 1.1 copy-start

commit v2 on v0

--- a/solution.py
+++ b/solution.py
@@ -33,12 +33,11 @@
     slab_count = lax.axis_size("tm")
     own_slab = lax.axis_index("tm")
     own_clip = lax.dynamic_index_in_dim(clip_ids, own_slab, keepdims=False)
-    own_row = (jnp.arange(slab_count, dtype=jnp.int32) == own_clip).astype(jnp.float32)[:, None]
-    table_sum, table_square = lax.psum(
-        (own_row * local_sum[None, :], own_row * local_square[None, :]), ("tm", "space")
-    )
-    clip_sum = jnp.sum(table_sum * own_row, axis=0)
-    clip_square = jnp.sum(table_square * own_row, axis=0)
+    stats = jnp.concatenate([local_sum, local_square])
+    parts = lax.all_to_all(jnp.broadcast_to(stats, (slab_count * lax.axis_size("space"), 2 * GROUPS)), ("tm", "space"), 0, 0)
+    same_clip = (clip_ids == own_clip).astype(jnp.float32)
+    totals = jnp.sum(parts.reshape(slab_count, -1, 2 * GROUPS) * same_clip[:, None, None], axis=(0, 1))
+    clip_sum, clip_square = (totals[:GROUPS], totals[GROUPS:])
     slabs_in = jnp.sum((clip_ids == own_clip).astype(jnp.float32))
     count = slabs_in * (
         values.shape[0]

time: 167 us -> 106 us (0.63)
  blocking collectives: 84.4 us -> 12.8 us
  waiting for transfers between devices: 14.2 us -> 20.3 us
  starting transfers between devices: 13.9 us -> 17.7 us
    psum x2 -> x0, blocking collectives: 84.4 us -> none  [clip_stats(): lax.psum((own_row * local_sum[None, :], own_row * local_square[None, :]),...]
    all_to_all x0 -> x1, blocking collectives: none -> 12.8 us  [clip_stats(): lax.all_to_all(jnp.broadcast_to(stats, (slab_count * lax.axis_size('space...]
    all_to_all x0 -> x1, starting transfers between devices: none -> 7.3 us  [clip_stats(): lax.all_to_all(jnp.broadcast_to(stats, (slab_count * lax.axis_size('space...]
    ppermute x2, starting transfers between devices: 8.67 us -> 5.18 us  [passed_along(): return lax.ppermute(block, axis, route)]
    ppermute x2, waiting for transfers between devices: 12.4 us -> 15.4 us  [passed_along(): return lax.ppermute(block, axis, route)]
    all_to_all x0 -> x1, waiting for transfers between devices: none -> 3.01 us  [clip_stats(): lax.all_to_all(jnp.broadcast_to(stats, (slab_count * lax.axis_size('space...]
  transfers between devices with their start and end apart: 6 -> 7, of which waited for: 3 -> 4; matrix products, arithmetic and copies ran while one was open for 2% -> 6% of each run, Pallas kernels for 0% -> 0%
where the time goes in v2:
time: 106 us; the launch traced here: 104 us
  other arithmetic  27.7 us (26%)
  waiting for transfers between devices  20.3 us (19%)
  starting transfers between devices  17.7 us (17%)
  matrix products  14.7 us (14%)
  blocking collectives  12.8 us (12%)
  local copies, waits for them, and re-layouts  8.13 us (8%)
  between operations  2.53 us (2%)
    ppermute x2, waiting for transfers between devices, passed_along(): return lax.ppermute(block, axis, route)  15.4 us
    concatenate x4, other arithmetic, causal_conv(): padded = jnp.pad(extended, ((0, 0), (0, 0), (1, 1), (0, 0)), mode='edge')  14.9 us
    dot_general x18, matrix products, causal_conv(): jnp.dot(stacked, kernel[tap_time, tap_row].reshape(3 * width, -1), prefer...  14.7 us
    all_to_all x1, blocking collectives, clip_stats(): lax.all_to_all(jnp.broadcast_to(stats, (slab_count * lax.axis_size('space...  12.8 us
    all_to_all x1, starting transfers between devices, clip_stats(): lax.all_to_all(jnp.broadcast_to(stats, (slab_count * lax.axis_size('space...  7.3 us
    ppermute x2, starting transfers between devices, passed_along(): return lax.ppermute(block, axis, route)  5.18 us
    concatenate x18, other arithmetic, causal_conv(): jnp.concatenate([window[:, :, offset:offset + cols] for offset in range(3...  4.19 us
    all_to_all x1, waiting for transfers between devices, clip_stats(): lax.all_to_all(jnp.broadcast_to(stats, (slab_count * lax.axis_size('space...  3.01 us
  transfers between devices with their start and end apart: 7, of which 4 were waited for; matrix products, arithmetic and copies ran while one was open for 6% of the time, Pallas kernels for 0%

profile of v2, /device:TPU:0, one launch (start us, length us, event | category | flops | bytes accessed | tf_op | source)
XLA Modules:
  0.0 103.7 jit_solution(9871064983491989138)
XLA Ops:
  0.0 1.4 %convert_reduce_fusion = (f32[256]{0:T(256)S(1)}, f32[256]{0:T(256)S(1)}) fusion(bf16[4,4,96,256]{3,2,1,0:T(8,128)(2,1)} %param.8), kind=kLoop, calls=%fused_computation.51 | loop fusion | flops 1572352 | bytes 788480 | tf_op jit(solution)/shard_map/reduce_sum | solution.py:31
  1.9 0.6 broadcast_in_dim.81
  2.5 7.3 %all-to-all-start = ((f32[32,1,64]{2,1,0:T(1,128)}), f32[32,1,64]{2,1,0:T(1,128)S(1)}, u32[]{:S(2)}, u32[]{:S(2)}) async-start(f32[32,1,64]{2,1,0:T(1,128)} %broadcast_in_dim.81), calls=%async_computation | async-start | bytes 32768 | tf_op jit(solution)/shard_map/all_to_all | solution.py:37
  9.8 1.4 %fusion.58 = (s32[1]{0:T(128)}, s32[1]{0:T(128)}) fusion(s32[16]{0:T(128)} %param.9, s32[]{:T(128)S(6)} %max.3, s32[]{:T(128)S(6)} %select_n.32), kind=kLoop, calls=%fused_computation.187 | loop fusion | bytes 24 | tf_op jit(solution)/shard_map/jit(dynamic_index_in_dim)/dynamic_slice | solution.py:114
  11.2 1.8 %fusion.51 = (f32[]{:T(128)}, f32[16]{0:T(128)S(1)}) fusion(s32[16]{0:T(128)} %param.9, s32[]{:T(128)} %bitcast), kind=kLoop, calls=%fused_computation.180 | loop fusion | flops 47 | bytes 136 | tf_op jit(solution)/shard_map/reduce_sum | solution.py:41
  13.9 3.0 %all-to-all-done = f32[32,1,64]{2,1,0:T(1,128)S(1)} async-done(((f32[32,1,64]{2,1,0:T(1,128)}), f32[32,1,64]{2,1,0:T(1,128)S(1)}, u32[]{:S(2)}, u32[]{:S(2)}) %all-to-all-start) | async-done | bytes 8224 | tf_op jit(solution)/shard_map/all_to_all | solution.py:37
  17.4 1.7 %fusion.17 = bf16[4,4,96,256]{3,2,1,0:T(8,128)(2,1)S(1)} fusion(bf16[4,4,96,256]{3,2,1,0:T(8,128)(2,1)} %param.8, f32[256]{0:T(256)} %param.11, f32[256]{0:T(256)} %param.10, f32[256]{0:T(256)S(1)} %mul.95, f32[256]{0:T(256)S(1)} %sub.37), kind=kLoop, calls=%fused_computation.91 | loop fusion | flops 3932160 | bytes 1576960 | tf_op jit(solution)/shard_map/convert_element_type | solution.py:59
  19.1 2.5 %collective-permute-start = (bf16[2,4,96,256]{3,2,1,0:T(8,128)(2,1)S(1)}, bf16[2,4,96,256]{3,2,1,0:T(8,128)(2,1)S(1)}, u32[]{:S(2)}, u32[]{:S(2)}) collective-permute-start(bf16[2,4,96,256]{3,2,1,0:T(8,128)(2,1)S(1)} %slice.485), channel_id=1, source_target_pairs={{0,2},{2,4},{4,6},{6,8},{8,10},{10,12},{12,14},{14,16},{16,18},{18... | collective-permute-start | bytes 1179656 | tf_op jit(solution)/shard_map/ppermute | solution.py:25
  22.9 7.1 %collective-permute-done = bf16[2,4,96,256]{3,2,1,0:T(8,128)(2,1)S(1)} collective-permute-done((bf16[2,4,96,256]{3,2,1,0:T(8,128)(2,1)S(1)}, bf16[2,4,96,256]{3,2,1,0:T(8,128)(2,1)S(1)}, u32[]{:S(2)}, u32[]{:S(2)}) %collective-permute-start) | collective-permute-done | bytes 393248 | tf_op jit(solution)/shard_map/ppermute | solution.py:25
  30.1 1.3 %collective-permute-start.1 = (bf16[6,1,96,256]{3,2,1,0:T(8,128)(2,1)S(1)}, bf16[6,1,96,256]{3,2,1,0:T(8,128)(2,1)S(1)}, u32[]{:S(2)}, u32[]{:S(2)}) collective-permute-start(bf16[6,1,96,256]{3,2,1,0:T(8,128)(2,1)S(1)} %get-tuple-element.89), channel_id=1, source_target_pairs={{0,1},{2,3},{4,5},{6,7},{8,9},{10,11},{12,13},{14,15},{16,17},{18,... | collective-permute-start | bytes 884744 | tf_op jit(solution)/shard_map/ppermute | solution.py:16
  31.4 1.3 %collective-permute-start.2 = (bf16[6,1,96,256]{3,2,1,0:T(8,128)(2,1)S(1)}, bf16[6,1,96,256]{3,2,1,0:T(8,128)(2,1)S(1)}, u32[]{:S(2)}, u32[]{:S(2)}) collective-permute-start(bf16[6,1,96,256]{3,2,1,0:T(8,128)(2,1)S(1)} %get-tuple-element.90), channel_id=1, source_target_pairs={{1,0},{3,2},{5,4},{7,6},{9,8},{11,10},{13,12},{15,14},{17,16},{19,... | collective-permute-start | bytes 884744 | tf_op jit(solution)/shard_map/ppermute | solution.py:17
  32.7 2.3 %fusion.53 = (bf16[1,1,3,256,256]{4,3,2,1,0:T(8,128)(2,1)S(1)}, bf16[1,1,3,256,256]{4,3,2,1,0:T(8,128)(2,1)S(1)}, bf16[1,1,3,256,256]{4,3,2,1,0:T(8,128)(2,1)S(1...) fusion(bf16[3,3,3,256,256]{4,3,2,1,0:T(8,128)(2,1)} %param.12), kind=kLoop, calls=%fused_computation.182 | loop fusion | bytes 7077888 | tf_op jit(solution)/shard_map/slice | solution.py:95
  35.0 0.4 fusion.6
  35.5 0.9 fusion.56
  36.3 3.9 %fusion.42 = (bf16[4,4,96,256]{3,2,1,0:T(8,128)(2,1)S(1)}, bf16[4,4,96,256]{3,2,1,0:T(8,128)(2,1)S(1)}, bf16[4,4,96,256]{3,2,1,0:T(8,128)(2,1)S(1)}, bf16[4,4,96...) fusion(bf16[6,6,96,256]{3,2,1,0:T(8,128)(2,1)S(1)} %fusion.6, ...), kind=kLoop, calls=%fused_computation.150 | loop fusion | flops 12582912 | bytes 8079360 | tf_op jit(solution)/shard_map/jit(_pad)/concatenate | solution.py:84
  40.2 3.5 %fusion.34 = (bf16[4,4,96,256]{3,2,1,0:T(8,128)(2,1)S(1)}, bf16[4,4,96,256]{3,2,1,0:T(8,128)(2,1)S(1)}, bf16[4,4,96,256]{3,2,1,0:T(8,128)(2,1)S(1)}, bf16[4,4,96...) fusion(bf16[6,6,96,256]{3,2,1,0:T(8,128)(2,1)S(1)} %fusion.6, ...), kind=kLoop, calls=%fused_computation.142 | loop fusion | flops 12582912 | bytes 8079360 | tf_op jit(solution)/shard_map/jit(_pad)/concatenate | solution.py:84
  43.7 0.9 fusion.4
  44.6 0.2 pad_maximum_fusion.4
  44.8 0.8 fusion.59
  45.6 0.2 pad_maximum_fusion.7
  45.7 0.2 pad_maximum_fusion.6
  45.9 0.2 pad_maximum_fusion.5
  46.1 0.8 convolution_add_fusion.15
  46.9 0.8 convolution_add_fusion.14
  47.7 0.8 convolution_add_fusion.13
  48.6 0.2 pad_maximum_fusion.8
  48.7 0.8 convolution_add_fusion.12
  49.5 0.2 pad_maximum_fusion.9
  49.7 0.8 convolution_add_fusion.11
  50.6 0.8 convolution_add_fusion.10
  51.4 0.2 pad_maximum_fusion.11
  51.6 0.8 convolution_add_fusion.9
  52.4 0.8 fusion.50
  53.8 12.8 %all_to_all.18 = f32[32,1,64]{2,1,0:T(1,128)S(1)} all-to-all(f32[32,1,64]{2,1,0:T(1,128)S(1)} %broadcast_in_dim.89), channel_id=1, replica_groups=mesh['tm'=16,'space'=2] {'tm','space'}, dimensions={0} | all-to-all | bytes 16384 | tf_op jit(solution)/shard_map/all_to_all | solution.py:37
  67.1 0.5 multiply_convert_fusion
  67.6 2.7 %collective-permute-start.3 = (bf16[2,4,96,256]{3,2,1,0:T(8,128)(2,1)S(1)}, bf16[2,4,96,256]{3,2,1,0:T(8,128)(2,1)S(1)}, u32[]{:S(2)}, u32[]{:S(2)}) collective-permute-start(bf16[2,4,96,256]{3,2,1,0:T(8,128)(2,1)S(1)} %slice.530), channel_id=1, source_target_pairs={{0,2},{2,4},{4,6},{6,8},{8,10},{10,12},{12,14},{14,16},{16,18},{18... | collective-permute-start | bytes 1179656 | tf_op jit(solution)/shard_map/ppermute | solution.py:25
  70.4 8.3 %collective-permute-done.3 = bf16[2,4,96,256]{3,2,1,0:T(8,128)(2,1)S(1)} collective-permute-done((bf16[2,4,96,256]{3,2,1,0:T(8,128)(2,1)S(1)}, bf16[2,4,96,256]{3,2,1,0:T(8,128)(2,1)S(1)}, u32[]{:S(2)}, u32[]{:S(2)}) %collective-permute-start.3) | collective-permute-done | bytes 393248 | tf_op jit(solution)/shard_map/ppermute | solution.py:25
  78.8 1.3 %collective-permute-start.4 = (bf16[6,1,96,256]{3,2,1,0:T(8,128)(2,1)S(1)}, bf16[6,1,96,256]{3,2,1,0:T(8,128)(2,1)S(1)}, u32[]{:S(2)}, u32[]{:S(2)}) collective-permute-start(bf16[6,1,96,256]{3,2,1,0:T(8,128)(2,1)S(1)} %get-tuple-element.87), channel_id=1, source_target_pairs={{0,1},{2,3},{4,5},{6,7},{8,9},{10,11},{12,13},{14,15},{16,17},{18,... | collective-permute-start | bytes 884744 | tf_op jit(solution)/shard_map/ppermute | solution.py:16
  80.2 1.3 %collective-permute-start.5 = (bf16[6,1,96,256]{3,2,1,0:T(8,128)(2,1)S(1)}, bf16[6,1,96,256]{3,2,1,0:T(8,128)(2,1)S(1)}, u32[]{:S(2)}, u32[]{:S(2)}) collective-permute-start(bf16[6,1,96,256]{3,2,1,0:T(8,128)(2,1)S(1)} %get-tuple-element.88), channel_id=1, source_target_pairs={{1,0},{3,2},{5,4},{7,6},{9,8},{11,10},{13,12},{15,14},{17,16},{19,... | collective-permute-start | bytes 884744 | tf_op jit(solution)/shard_map/ppermute | solution.py:17
  81.5 0.3 fusion.52
  81.8 1.8 %collective-permute-done.5 = bf16[6,1,96,256]{3,2,1,0:T(8,128)(2,1)S(1)} collective-permute-done((bf16[6,1,96,256]{3,2,1,0:T(8,128)(2,1)S(1)}, bf16[6,1,96,256]{3,2,1,0:T(8,128)(2,1)S(1)}, u32[]{:S(2)}, u32[]{:S(2)}) %collective-permute-start.5) | collective-permute-done | bytes 294944 | tf_op jit(solution)/shard_map/ppermute | solution.py:17
  83.6 0.4 fusion.7
  84.0 0.9 fusion.54
  85.0 4.1 %fusion.26 = (bf16[4,4,96,256]{3,2,1,0:T(8,128)(2,1)S(1)}, bf16[4,4,96,256]{3,2,1,0:T(8,128)(2,1)S(1)}, bf16[4,4,96,256]{3,2,1,0:T(8,128)(2,1)S(1)}, bf16[4,4,96...) fusion(bf16[6,6,96,256]{3,2,1,0:T(8,128)(2,1)S(1)} %fusion.7, ...), kind=kLoop, calls=%fused_computation.134 | loop fusion | flops 12582912 | bytes 8079360 | tf_op jit(solution)/shard_map/jit(_pad)/concatenate | solution.py:84
  89.1 3.5 %fusion.18 = (bf16[4,4,96,256]{3,2,1,0:T(8,128)(2,1)S(1)}, bf16[4,4,96,256]{3,2,1,0:T(8,128)(2,1)S(1)}, bf16[4,4,96,256]{3,2,1,0:T(8,128)(2,1)S(1)}, bf16[4,4,96...) fusion(bf16[6,6,96,256]{3,2,1,0:T(8,128)(2,1)S(1)} %fusion.7, ...), kind=kLoop, calls=%fused_computation.126 | loop fusion | flops 12582912 | bytes 8079360 | tf_op jit(solution)/shard_map/jit(_pad)/concatenate | solution.py:84
  92.6 0.7 fusion.2
  93.4 0.8 fusion.60
  94.2 0.2 pad_maximum_fusion.19
  94.4 0.2 pad_maximum_fusion.18
  94.6 0.2 pad_maximum_fusion.17
  94.7 0.2 pad_maximum_fusion.16
  94.9 0.2 pad_maximum_fusion.15
  95.1 0.2 pad_maximum_fusion.14
  95.2 0.2 pad_maximum_fusion.13
  95.4 0.8 convolution_add_fusion.7
  96.2 0.8 convolution_add_fusion.6
  97.1 0.8 convolution_add_fusion.5
  97.9 0.8 convolution_add_fusion.4
  98.8 0.8 convolution_add_fusion.3
  99.6 0.8 convolution_add_fusion.2
  100.4 0.8 convolution_add_fusion.1
  101.3 0.8 convolution_add_fusion
  102.1 0.3 copy-done
  102.4 1.3 %convert_add_fusion = f32[4,4,96,256]{3,2,1,0:T(8,128)} fusion(f32[4,4,96,256]{3,2,1,0:T(8,128)S(1)} %bitcast.104, bf16[4,4,96,256]{3,2,1,0:T(8,128)(2,1)S(1)} %copy-done), kind=kLoop, calls=%fused_computation.48 | loop fusion | flops 786432 | bytes 3932160 | tf_op jit(solution)/shard_map/add | solution.py:125
  (48 shorter events, 2.9 us)
Async XLA Ops:
  2.5 14.4 %all-to-all-start = ((f32[32,1,64]{2,1,0:T(1,128)}), f32[32,1,64]{2,1,0:T(1,128)S(1)}, u32[]{:S(2)}, u32[]{:S(2)}) async-start(f32[32,1,64]{2,1,0:T(1,128)} %broadcast_in_dim.81), calls=%async_computation | async-start | bytes 32768 | tf_op jit(solution)/shard_map/all_to_all | solution.py:37
  19.1 10.8 %collective-permute-start = (bf16[2,4,96,256]{3,2,1,0:T(8,128)(2,1)S(1)}, bf16[2,4,96,256]{3,2,1,0:T(8,128)(2,1)S(1)}, u32[]{:S(2)}, u32[]{:S(2)}) collective-permute-start(bf16[2,4,96,256]{3,2,1,0:T(8,128)(2,1)S(1)} %slice.485), channel_id=1, source_target_pairs={{0,2},{2,4},{4,6},{6,8},{8,10},{10,12},{12,14},{14,16},{16,18},{18... | collective-permute-start | bytes 1179656 | tf_op jit(solution)/shard_map/ppermute | solution.py:25
  30.1 4.9 %collective-permute-start.1 = (bf16[6,1,96,256]{3,2,1,0:T(8,128)(2,1)S(1)}, bf16[6,1,96,256]{3,2,1,0:T(8,128)(2,1)S(1)}, u32[]{:S(2)}, u32[]{:S(2)}) collective-permute-start(bf16[6,1,96,256]{3,2,1,0:T(8,128)(2,1)S(1)} %get-tuple-element.89), channel_id=1, source_target_pairs={{0,1},{2,3},{4,5},{6,7},{8,9},{10,11},{12,13},{14,15},{16,17},{18,... | collective-permute-start | bytes 884744 | tf_op jit(solution)/shard_map/ppermute | solution.py:16
  31.4 3.6 %collective-permute-start.2 = (bf16[6,1,96,256]{3,2,1,0:T(8,128)(2,1)S(1)}, bf16[6,1,96,256]{3,2,1,0:T(8,128)(2,1)S(1)}, u32[]{:S(2)}, u32[]{:S(2)}) collective-permute-start(bf16[6,1,96,256]{3,2,1,0:T(8,128)(2,1)S(1)} %get-tuple-element.90), channel_id=1, source_target_pairs={{1,0},{3,2},{5,4},{7,6},{9,8},{11,10},{13,12},{15,14},{17,16},{19,... | collective-permute-start | bytes 884744 | tf_op jit(solution)/shard_map/ppermute | solution.py:17
  52.4 14.7 %copy-start.2 = (f32[256]{0:T(256)S(1)}, f32[256]{0:T(256)}, u32[]{:S(2)}) copy-start(f32[256]{0:T(256)} %param.14) | copy-start | bytes 3076
  52.4 14.6 %copy-start.3 = (f32[256]{0:T(256)S(1)}, f32[256]{0:T(256)}, u32[]{:S(2)}) copy-start(f32[256]{0:T(256)} %param.13) | copy-start | bytes 3076
  67.6 13.9 %copy-start.1 = (bf16[3,3,3,256,256]{4,3,2,1,0:T(8,128)(2,1)S(1)}, bf16[3,3,3,256,256]{4,3,2,1,0:T(8,128)(2,1)}, u32[]{:S(2)}) copy-start(bf16[3,3,3,256,256]{4,3,2,1,0:T(8,128)(2,1)} %param.15) | copy-start | bytes 10616836
  67.6 11.1 %collective-permute-start.3 = (bf16[2,4,96,256]{3,2,1,0:T(8,128)(2,1)S(1)}, bf16[2,4,96,256]{3,2,1,0:T(8,128)(2,1)S(1)}, u32[]{:S(2)}, u32[]{:S(2)}) collective-permute-start(bf16[2,4,96,256]{3,2,1,0:T(8,128)(2,1)S(1)} %slice.530), channel_id=1, source_target_pairs={{0,2},{2,4},{4,6},{6,8},{8,10},{10,12},{12,14},{14,16},{16,18},{18... | collective-permute-start | bytes 1179656 | tf_op jit(solution)/shard_map/ppermute | solution.py:25
  78.8 3.0 %collective-permute-start.4 = (bf16[6,1,96,256]{3,2,1,0:T(8,128)(2,1)S(1)}, bf16[6,1,96,256]{3,2,1,0:T(8,128)(2,1)S(1)}, u32[]{:S(2)}, u32[]{:S(2)}) collective-permute-start(bf16[6,1,96,256]{3,2,1,0:T(8,128)(2,1)S(1)} %get-tuple-element.87), channel_id=1, source_target_pairs={{0,1},{2,3},{4,5},{6,7},{8,9},{10,11},{12,13},{14,15},{16,17},{18,... | collective-permute-start | bytes 884744 | tf_op jit(solution)/shard_map/ppermute | solution.py:16
  80.2 3.5 %collective-permute-start.5 = (bf16[6,1,96,256]{3,2,1,0:T(8,128)(2,1)S(1)}, bf16[6,1,96,256]{3,2,1,0:T(8,128)(2,1)S(1)}, u32[]{:S(2)}, u32[]{:S(2)}) collective-permute-start(bf16[6,1,96,256]{3,2,1,0:T(8,128)(2,1)S(1)} %get-tuple-element.88), channel_id=1, source_target_pairs={{1,0},{3,2},{5,4},{7,6},{9,8},{11,10},{13,12},{15,14},{17,16},{19,... | collective-permute-start | bytes 884744 | tf_op jit(solution)/shard_map/ppermute | solution.py:17
  101.3 1.1 %copy-start = (bf16[4,4,96,256]{3,2,1,0:T(8,128)(2,1)S(1)}, bf16[4,4,96,256]{3,2,1,0:T(8,128)(2,1)}, u32[]{:S(2)}) copy-start(bf16[4,4,96,256]{3,2,1,0:T(8,128)(2,1)} %param.8) | copy-start | bytes 2359300

commit v3 on v2

--- a/solution.py
+++ b/solution.py
@@ -34,7 +34,7 @@
     own_slab = lax.axis_index("tm")
     own_clip = lax.dynamic_index_in_dim(clip_ids, own_slab, keepdims=False)
     stats = jnp.concatenate([local_sum, local_square])
-    parts = lax.all_to_all(jnp.broadcast_to(stats, (slab_count * lax.axis_size("space"), 2 * GROUPS)), ("tm", "space"), 0, 0)
+    parts = lax.all_gather(stats, ("tm", "space"))
     same_clip = (clip_ids == own_clip).astype(jnp.float32)
     totals = jnp.sum(parts.reshape(slab_count, -1, 2 * GROUPS) * same_clip[:, None, None], axis=(0, 1))
     clip_sum, clip_square = (totals[:GROUPS], totals[GROUPS:])

time: 106 us -> 166 us (1.57)
  blocking collectives: 12.8 us -> 84.2 us
  waiting for transfers between devices: 20.3 us -> 14.2 us
  starting transfers between devices: 17.7 us -> 13.9 us
    unnamed x0 -> x2, blocking collectives: none -> 84.2 us
    all_to_all x1 -> x0, blocking collectives: 12.8 us -> none  [clip_stats(): lax.all_to_all(jnp.broadcast_to(stats, (slab_count * lax.axis_size('space...]
    all_to_all x1 -> x0, starting transfers between devices: 7.3 us -> none  [clip_stats(): lax.all_to_all(jnp.broadcast_to(stats, (slab_count * lax.axis_size('space...]
    ppermute x2, starting transfers between devices: 5.18 us -> 8.67 us  [passed_along(): return lax.ppermute(block, axis, route)]
    ppermute x2, waiting for transfers between devices: 15.4 us -> 12.4 us  [passed_along(): return lax.ppermute(block, axis, route)]
    all_to_all x1 -> x0, waiting for transfers between devices: 3.01 us -> none  [clip_stats(): lax.all_to_all(jnp.broadcast_to(stats, (slab_count * lax.axis_size('space...]
  transfers between devices with their start and end apart: 7 -> 6, of which waited for: 4 -> 3; matrix products, arithmetic and copies ran while one was open for 6% -> 2% of each run, Pallas kernels for 0% -> 0%
where the time goes in v3:
time: 166 us; the launch traced here: 165 us
  blocking collectives  84.2 us (51%)
  other arithmetic  28 us (17%)
  matrix products  14.7 us (9%)
  waiting for transfers between devices  14.2 us (9%)
  starting transfers between devices  13.9 us (8%)
  local copies, waits for them, and re-layouts  7.63 us (5%)
  between operations  2.54 us (2%)
    unnamed x2, blocking collectives  84.2 us
    concatenate x4, other arithmetic, causal_conv(): padded = jnp.pad(extended, ((0, 0), (0, 0), (1, 1), (0, 0)), mode='edge')  14.9 us
    dot_general x18, matrix products, causal_conv(): jnp.dot(stacked, kernel[tap_time, tap_row].reshape(3 * width, -1), prefer...  14.7 us
    ppermute x2, waiting for transfers between devices, passed_along(): return lax.ppermute(block, axis, route)  12.4 us
    ppermute x2, starting transfers between devices, passed_along(): return lax.ppermute(block, axis, route)  8.67 us
    concatenate x18, other arithmetic, causal_conv(): jnp.concatenate([window[:, :, offset:offset + cols] for offset in range(3...  4.19 us
  transfers between devices with their start and end apart: 6, of which 3 were waited for; matrix products, arithmetic and copies ran while one was open for 2% of the time, Pallas kernels for 0%

profile of v3, /device:TPU:0, one launch (start us, length us, event | category | flops | bytes accessed | tf_op | source)
XLA Modules:
  0.0 165.1 jit_solution(13083530898730552727)
XLA Ops:
  0.0 1.4 fusion.58
  1.4 1.9 %fusion.51 = (f32[]{:T(128)}, f32[16]{0:T(128)S(1)}) fusion(s32[16]{0:T(128)} %param.9, s32[]{:T(128)} %bitcast), kind=kLoop, calls=%fused_computation.180 | loop fusion | flops 47 | bytes 136 | tf_op jit(solution)/shard_map/reduce_sum | solution.py:41
  3.5 1.4 convert_reduce_fusion
  5.3 0.2 maximum_dynamic-update-slice_fusion
  5.5 42.0 %all-reduce = f32[2048]{0:T(1024)S(1)} all-reduce(f32[2048]{0:T(1024)S(1)} %maximum_dynamic-update-slice_fusion), channel_id=2, replica_groups=mesh['tm'=16,'space'=2] {'tm','space'}, use_global_device_ids=true, to_apply=%add | all-reduce | flops 2048 | bytes 16384
  48.7 1.7 %fusion.17 = bf16[4,4,96,256]{3,2,1,0:T(8,128)(2,1)S(1)} fusion(bf16[4,4,96,256]{3,2,1,0:T(8,128)(2,1)} %param.8, f32[256]{0:T(256)} %param.11, f32[256]{0:T(256)} %param.10, f32[256]{0:T(256)S(1)} %mul.95, f32[256]{0:T(256)S(1)} %sub.37), kind=kLoop, calls=%fused_computation.91 | loop fusion | flops 3932160 | bytes 1576960 | tf_op jit(solution)/shard_map/convert_element_type | solution.py:59
  50.4 4.2 %collective-permute-start = (bf16[2,4,96,256]{3,2,1,0:T(8,128)(2,1)S(1)}, bf16[2,4,96,256]{3,2,1,0:T(8,128)(2,1)S(1)}, u32[]{:S(2)}, u32[]{:S(2)}) collective-permute-start(bf16[2,4,96,256]{3,2,1,0:T(8,128)(2,1)S(1)} %slice.485), channel_id=1, source_target_pairs={{0,2},{2,4},{4,6},{6,8},{8,10},{10,12},{12,14},{14,16},{16,18},{18... | collective-permute-start | bytes 1179656 | tf_op jit(solution)/shard_map/ppermute | solution.py:25
  56.0 5.2 %collective-permute-done = bf16[2,4,96,256]{3,2,1,0:T(8,128)(2,1)S(1)} collective-permute-done((bf16[2,4,96,256]{3,2,1,0:T(8,128)(2,1)S(1)}, bf16[2,4,96,256]{3,2,1,0:T(8,128)(2,1)S(1)}, u32[]{:S(2)}, u32[]{:S(2)}) %collective-permute-start) | collective-permute-done | bytes 393248 | tf_op jit(solution)/shard_map/ppermute | solution.py:25
  61.3 1.3 collective-permute-start.1
  62.6 1.3 collective-permute-start.2
  63.9 2.3 %fusion.53 = (bf16[1,1,3,256,256]{4,3,2,1,0:T(8,128)(2,1)S(1)}, bf16[1,1,3,256,256]{4,3,2,1,0:T(8,128)(2,1)S(1)}, bf16[1,1,3,256,256]{4,3,2,1,0:T(8,128)(2,1)S(1...) fusion(bf16[3,3,3,256,256]{4,3,2,1,0:T(8,128)(2,1)} %param.12), kind=kLoop, calls=%fused_computation.182 | loop fusion | bytes 7077888 | tf_op jit(solution)/shard_map/slice | solution.py:95
  66.3 0.4 fusion.6
  66.7 0.9 fusion.56
  67.6 3.9 %fusion.42 = (bf16[4,4,96,256]{3,2,1,0:T(8,128)(2,1)S(1)}, bf16[4,4,96,256]{3,2,1,0:T(8,128)(2,1)S(1)}, bf16[4,4,96,256]{3,2,1,0:T(8,128)(2,1)S(1)}, bf16[4,4,96...) fusion(bf16[6,6,96,256]{3,2,1,0:T(8,128)(2,1)S(1)} %fusion.6, ...), kind=kLoop, calls=%fused_computation.150 | loop fusion | flops 12582912 | bytes 8079360 | tf_op jit(solution)/shard_map/jit(_pad)/concatenate | solution.py:84
  71.5 3.5 %fusion.34 = (bf16[4,4,96,256]{3,2,1,0:T(8,128)(2,1)S(1)}, bf16[4,4,96,256]{3,2,1,0:T(8,128)(2,1)S(1)}, bf16[4,4,96,256]{3,2,1,0:T(8,128)(2,1)S(1)}, bf16[4,4,96...) fusion(bf16[6,6,96,256]{3,2,1,0:T(8,128)(2,1)S(1)} %fusion.6, ...), kind=kLoop, calls=%fused_computation.142 | loop fusion | flops 12582912 | bytes 8079360 | tf_op jit(solution)/shard_map/jit(_pad)/concatenate | solution.py:84
  75.0 0.9 fusion.4
  75.9 0.2 pad_maximum_fusion.4
  76.0 0.8 fusion.59
  76.8 0.2 pad_maximum_fusion.7
  77.0 0.2 pad_maximum_fusion.6
  77.2 0.2 pad_maximum_fusion.5
  77.3 0.8 convolution_add_fusion.15
  78.1 0.8 convolution_add_fusion.14
  79.0 0.8 convolution_add_fusion.13
  79.8 0.2 pad_maximum_fusion.8
  80.0 0.8 convolution_add_fusion.12
  80.8 0.2 pad_maximum_fusion.9
  80.9 0.8 convolution_add_fusion.11
  81.7 0.2 pad_maximum_fusion.10
  81.9 0.8 convolution_add_fusion.10
  82.7 0.2 pad_maximum_fusion.11
  82.8 0.8 convolution_add_fusion.9
  83.7 0.8 fusion.50
  85.0 0.2 maximum_dynamic-update-slice_fusion.1
  85.1 42.2 %all-reduce.1 = f32[2048]{0:T(1024)S(1)} all-reduce(f32[2048]{0:T(1024)S(1)} %maximum_dynamic-update-slice_fusion.1), channel_id=3, replica_groups=mesh['tm'=16,'space'=2] {'tm','space'}, use_global_device_ids=true, to_apply=%add.1 | all-reduce | flops 2048 | bytes 16384
  127.9 0.5 multiply_convert_fusion
  128.5 4.5 %collective-permute-start.3 = (bf16[2,4,96,256]{3,2,1,0:T(8,128)(2,1)S(1)}, bf16[2,4,96,256]{3,2,1,0:T(8,128)(2,1)S(1)}, u32[]{:S(2)}, u32[]{:S(2)}) collective-permute-start(bf16[2,4,96,256]{3,2,1,0:T(8,128)(2,1)S(1)} %slice.530), channel_id=1, source_target_pairs={{0,2},{2,4},{4,6},{6,8},{8,10},{10,12},{12,14},{14,16},{16,18},{18... | collective-permute-start | bytes 1179656 | tf_op jit(solution)/shard_map/ppermute | solution.py:25
  133.0 7.2 %collective-permute-done.3 = bf16[2,4,96,256]{3,2,1,0:T(8,128)(2,1)S(1)} collective-permute-done((bf16[2,4,96,256]{3,2,1,0:T(8,128)(2,1)S(1)}, bf16[2,4,96,256]{3,2,1,0:T(8,128)(2,1)S(1)}, u32[]{:S(2)}, u32[]{:S(2)}) %collective-permute-start.3) | collective-permute-done | bytes 393248 | tf_op jit(solution)/shard_map/ppermute | solution.py:25
  140.2 1.3 collective-permute-start.4
  141.6 1.3 collective-permute-start.5
  142.9 0.3 fusion.52
  143.2 1.8 %collective-permute-done.5 = bf16[6,1,96,256]{3,2,1,0:T(8,128)(2,1)S(1)} collective-permute-done((bf16[6,1,96,256]{3,2,1,0:T(8,128)(2,1)S(1)}, bf16[6,1,96,256]{3,2,1,0:T(8,128)(2,1)S(1)}, u32[]{:S(2)}, u32[]{:S(2)}) %collective-permute-start.5) | collective-permute-done | bytes 294944 | tf_op jit(solution)/shard_map/ppermute | solution.py:17
  145.0 0.4 fusion.7
  145.4 0.9 fusion.54
  146.4 4.1 %fusion.26 = (bf16[4,4,96,256]{3,2,1,0:T(8,128)(2,1)S(1)}, bf16[4,4,96,256]{3,2,1,0:T(8,128)(2,1)S(1)}, bf16[4,4,96,256]{3,2,1,0:T(8,128)(2,1)S(1)}, bf16[4,4,96...) fusion(bf16[6,6,96,256]{3,2,1,0:T(8,128)(2,1)S(1)} %fusion.7, ...), kind=kLoop, calls=%fused_computation.134 | loop fusion | flops 12582912 | bytes 8079360 | tf_op jit(solution)/shard_map/jit(_pad)/concatenate | solution.py:84
  150.4 3.5 %fusion.18 = (bf16[4,4,96,256]{3,2,1,0:T(8,128)(2,1)S(1)}, bf16[4,4,96,256]{3,2,1,0:T(8,128)(2,1)S(1)}, bf16[4,4,96,256]{3,2,1,0:T(8,128)(2,1)S(1)}, bf16[4,4,96...) fusion(bf16[6,6,96,256]{3,2,1,0:T(8,128)(2,1)S(1)} %fusion.7, ...), kind=kLoop, calls=%fused_computation.126 | loop fusion | flops 12582912 | bytes 8079360 | tf_op jit(solution)/shard_map/jit(_pad)/concatenate | solution.py:84
  153.9 0.7 fusion.2
  154.7 0.2 pad_maximum_fusion.12
  154.8 0.8 fusion.60
  155.6 0.2 pad_maximum_fusion.19
  155.8 0.2 pad_maximum_fusion.18
  156.0 0.2 pad_maximum_fusion.17
  156.1 0.2 pad_maximum_fusion.16
  156.3 0.2 pad_maximum_fusion.15
  156.8 0.8 convolution_add_fusion.7
  157.6 0.8 convolution_add_fusion.6
  158.5 0.8 convolution_add_fusion.5
  159.3 0.8 convolution_add_fusion.4
  160.1 0.8 convolution_add_fusion.3
  161.0 0.8 convolution_add_fusion.2
  161.8 0.8 convolution_add_fusion.1
  162.7 0.8 convolution_add_fusion
  163.5 0.3 copy-done
  163.8 1.3 convert_add_fusion
  (49 shorter events, 2.9 us)
Async XLA Ops:
  50.4 10.8 %collective-permute-start = (bf16[2,4,96,256]{3,2,1,0:T(8,128)(2,1)S(1)}, bf16[2,4,96,256]{3,2,1,0:T(8,128)(2,1)S(1)}, u32[]{:S(2)}, u32[]{:S(2)}) collective-permute-start(bf16[2,4,96,256]{3,2,1,0:T(8,128)(2,1)S(1)} %slice.485), channel_id=1, source_target_pairs={{0,2},{2,4},{4,6},{6,8},{8,10},{10,12},{12,14},{14,16},{16,18},{18... | collective-permute-start | bytes 1179656 | tf_op jit(solution)/shard_map/ppermute | solution.py:25
  61.3 4.9 %collective-permute-start.1 = (bf16[6,1,96,256]{3,2,1,0:T(8,128)(2,1)S(1)}, bf16[6,1,96,256]{3,2,1,0:T(8,128)(2,1)S(1)}, u32[]{:S(2)}, u32[]{:S(2)}) collective-permute-start(bf16[6,1,96,256]{3,2,1,0:T(8,128)(2,1)S(1)} %get-tuple-element.89), channel_id=1, source_target_pairs={{0,1},{2,3},{4,5},{6,7},{8,9},{10,11},{12,13},{14,15},{16,17},{18,... | collective-permute-start | bytes 884744 | tf_op jit(solution)/shard_map/ppermute | solution.py:16
  62.6 3.6 %collective-permute-start.2 = (bf16[6,1,96,256]{3,2,1,0:T(8,128)(2,1)S(1)}, bf16[6,1,96,256]{3,2,1,0:T(8,128)(2,1)S(1)}, u32[]{:S(2)}, u32[]{:S(2)}) collective-permute-start(bf16[6,1,96,256]{3,2,1,0:T(8,128)(2,1)S(1)} %get-tuple-element.90), channel_id=1, source_target_pairs={{1,0},{3,2},{5,4},{7,6},{9,8},{11,10},{13,12},{15,14},{17,16},{19,... | collective-permute-start | bytes 884744 | tf_op jit(solution)/shard_map/ppermute | solution.py:17
  83.7 44.2 %copy-start.2 = (f32[256]{0:T(256)S(1)}, f32[256]{0:T(256)}, u32[]{:S(2)}) copy-start(f32[256]{0:T(256)} %param.14) | copy-start | bytes 3076
  83.7 44.2 %copy-start.3 = (f32[256]{0:T(256)S(1)}, f32[256]{0:T(256)}, u32[]{:S(2)}) copy-start(f32[256]{0:T(256)} %param.13) | copy-start | bytes 3076
  128.4 14.4 %copy-start.1 = (bf16[3,3,3,256,256]{4,3,2,1,0:T(8,128)(2,1)S(1)}, bf16[3,3,3,256,256]{4,3,2,1,0:T(8,128)(2,1)}, u32[]{:S(2)}) copy-start(bf16[3,3,3,256,256]{4,3,2,1,0:T(8,128)(2,1)} %param.15) | copy-start | bytes 10616836
  128.5 11.7 %collective-permute-start.3 = (bf16[2,4,96,256]{3,2,1,0:T(8,128)(2,1)S(1)}, bf16[2,4,96,256]{3,2,1,0:T(8,128)(2,1)S(1)}, u32[]{:S(2)}, u32[]{:S(2)}) collective-permute-start(bf16[2,4,96,256]{3,2,1,0:T(8,128)(2,1)S(1)} %slice.530), channel_id=1, source_target_pairs={{0,2},{2,4},{4,6},{6,8},{8,10},{10,12},{12,14},{14,16},{16,18},{18... | collective-permute-start | bytes 1179656 | tf_op jit(solution)/shard_map/ppermute | solution.py:25
  140.2 3.0 %collective-permute-start.4 = (bf16[6,1,96,256]{3,2,1,0:T(8,128)(2,1)S(1)}, bf16[6,1,96,256]{3,2,1,0:T(8,128)(2,1)S(1)}, u32[]{:S(2)}, u32[]{:S(2)}) collective-permute-start(bf16[6,1,96,256]{3,2,1,0:T(8,128)(2,1)S(1)} %get-tuple-element.87), channel_id=1, source_target_pairs={{0,1},{2,3},{4,5},{6,7},{8,9},{10,11},{12,13},{14,15},{16,17},{18,... | collective-permute-start | bytes 884744 | tf_op jit(solution)/shard_map/ppermute | solution.py:16
  141.6 3.5 %collective-permute-start.5 = (bf16[6,1,96,256]{3,2,1,0:T(8,128)(2,1)S(1)}, bf16[6,1,96,256]{3,2,1,0:T(8,128)(2,1)S(1)}, u32[]{:S(2)}, u32[]{:S(2)}) collective-permute-start(bf16[6,1,96,256]{3,2,1,0:T(8,128)(2,1)S(1)} %get-tuple-element.88), channel_id=1, source_target_pairs={{1,0},{3,2},{5,4},{7,6},{9,8},{11,10},{13,12},{15,14},{17,16},{19,... | collective-permute-start | bytes 884744 | tf_op jit(solution)/shard_map/ppermute | solution.py:17
  162.7 1.1 copy-start

commit v4 on v3

v4 whole, which is shorter than its diff:
```python
import functools

import jax
import jax.numpy as jnp
from jax import lax
from jax.experimental import pallas as pl
from jax.experimental.pallas import tpu as pltpu
from jax.sharding import PartitionSpec as P

GROUPS = 32
AXES = ("tm", "space")


def is_power(number):
    return number & (number - 1) == 0


def traded(value, axis, mask):
    return lax.ppermute(value, axis, [(i, i ^ mask) for i in range(lax.axis_size(axis))])


def space_total(stats):
    peers = lax.axis_size("space")
    if not is_power(peers):
        return lax.psum(stats, "space")
    step = 1
    while step < peers:
        stats = stats + traded(stats, "space", step)
        step *= 2
    return stats


def slab_tables(stats):
    peers = lax.axis_size("tm")
    total = space_total(stats)[None]
    if not is_power(peers):
        return [lax.all_gather(total, "tm", tiled=True)]
    held = [total]
    step = 1
    while step < peers:
        ways = min(4, peers // step)
        block = held[0] if len(held) == 1 else jnp.concatenate(held, axis=0)
        held = [block] + [traded(block, "tm", step * way) for way in range(1, ways)]
        step *= ways
    return held


def slab_weights(clip_ids):
    slabs = jnp.arange(lax.axis_size("tm"), dtype=jnp.int32)
    own_slab = lax.axis_index("tm")
    own_clip = lax.dynamic_index_in_dim(clip_ids, own_slab, keepdims=False)
    order = slabs ^ own_slab if is_power(lax.axis_size("tm")) else slabs
    return (jnp.take(clip_ids, order) == own_clip).astype(jnp.float32)


def next_slab(value):
    peers = lax.axis_size("tm")
    return lax.ppermute(value, "tm", [(i, (i + 1) % peers) for i in range(peers)])


def halos(frames, edges):
    slabs, places = lax.axis_size("tm"), lax.axis_size("space")
    top, bottom = edges
    if places == 2:
        outer = jnp.where(lax.axis_index("space") == 0, bottom, top)
        rows = traded(outer, "space", 1)
        before = next_slab(frames[-2:])
        cross = [(t * 2 + s, (t + 1) % slabs * 2 + 1 - s) for t in range(slabs) for s in range(2)]
        corner = lax.ppermute(outer[-2:], AXES, cross)
        return [rows], before, [corner]
    above = lax.ppermute(bottom, "space", [(i, (i + 1) % places) for i in range(places)])
    below = lax.ppermute(top, "space", [(i, (i - 1) % places) for i in range(places)])
    before = next_slab(frames[-2:])
    return [above, below], before, [next_slab(above[-2:]), next_slab(below[-2:])]


def group_total(values):
    width = values.shape[-1]
    lane = lax.broadcasted_iota(jnp.int32, values.shape, 1)
    step = 1
    while step < width // GROUPS:
        upper = pltpu.roll(values, step, 1)
        lower = pltpu.roll(values, width - step, 1)
        values = values + jnp.where((lane & step) != 0, upper, lower)
        step *= 2
    return values


def conv_kernel(n_tables, n_sides, first, *refs):
    flags, weights = refs[:2]
    tables = refs[2 : 2 + n_tables]
    gain, shift, frames = refs[2 + n_tables : 5 + n_tables]
    rest = refs[5 + n_tables :]
    rows_halo, before, corners = rest[:n_sides], rest[n_sides], rest[n_sides + 1 : 2 * n_sides + 1]
    rest = rest[2 * n_sides + 1 :]
    if first:
        kernel_hbm, hidden, stats, act, taps, sems = rest
    else:
        kernel_hbm, feats, out, act, taps, sems = rest
    n_frames, n_rows, cols, width = frames.shape
    copies = [pltpu.make_async_copy(kernel_hbm.at[i], taps.at[i], sems.at[i]) for i in range(3)]
    for copy in copies:
        copy.start()

    total = jnp.zeros((2, width), jnp.float32)
    entry = 0
    slabs_in = 0.0
    for table in tables:
        for i in range(table.shape[0]):
            total = total + table[i] * weights[entry]
            slabs_in = slabs_in + weights[entry]
            entry += 1
    grouped = group_total(total)
    count = slabs_in * weights[entry]
    mean = grouped[0:1] / count
    variance = grouped[1:2] / count - mean * mean
    scale = lax.rsqrt(variance + 1e-06) * gain[...]
    half_scale = 0.5 * scale
    half_shift = 0.5 * (shift[...] - mean * scale)

    starting = flags[0] != 0
    edge = (flags[1] != 0, flags[2] != 0)

    def put(frame, row, raw):
        half = raw.astype(jnp.float32) * half_scale + half_shift
        act[frame, row] = (half * jnp.tanh(half) + half).astype(jnp.bfloat16)

    def normed(frame):
        for row in range(n_rows + 2):
            side = 0 if row == 0 else n_sides - 1
            inner = min(max(row - 1, 0), n_rows - 1)
            outside = row in (0, n_rows + 1)
            if frame < 2:
                raw = before[frame, inner]
                own = frames[0, inner]
                if outside:
                    at_edge = edge[0 if row == 0 else 1]
                    raw = jnp.where(at_edge, raw, corners[side][frame, 0])
                    own = jnp.where(at_edge, own, rows_halo[side][0, 0])
                raw = jnp.where(starting, own, raw)
            else:
                raw = frames[frame - 2, inner]
                if outside:
                    raw = jnp.where(edge[0 if row == 0 else 1], raw, rows_halo[side][frame - 2, 0])
            put(frame, row, raw)

    column = lax.broadcasted_iota(jnp.int32, (cols, width), 0)

    def conv(frame):
        lhs = jnp.concatenate(
            [
                act[frame + i, j : j + n_rows].reshape(n_rows * cols, width)
                for i in range(3)
                for j in range(3)
            ],
            axis=1,
        )
        sums = []
        for l in range(3):
            rhs = jnp.concatenate([taps[i, j, l] for i in range(3) for j in range(3)], axis=0)
            sums.append(jnp.dot(lhs, rhs, preferred_element_type=jnp.float32))
        done = []
        for row in range(n_rows):
            left, mid, right = (s[row * cols : (row + 1) * cols] for s in sums)
            left = jnp.where(column == 0, left, pltpu.roll(left, 1, 0))
            right = jnp.where(column == cols - 1, right, pltpu.roll(right, cols - 1, 0))
            done.append(left + mid + right)
        return done

    for frame in range(3):
        normed(frame)
    for copy in copies:
        copy.wait()
    if first:
        part_sum = jnp.zeros((8, width), jnp.float32)
        part_square = jnp.zeros((8, width), jnp.float32)
    for frame in range(n_frames):
        for row, value in enumerate(conv(frame)):
            if first:
                rounded = value.astype(jnp.bfloat16)
                hidden[frame, row] = rounded
                again = rounded.astype(jnp.float32)
                part_sum = part_sum + jnp.sum(again.reshape(-1, 8, width), axis=0)
                part_square = part_square + jnp.sum((again * again).reshape(-1, 8, width), axis=0)
            else:
                out[frame, row] = feats[frame, row].astype(jnp.float32) + value
        if frame + 3 < n_frames + 2:
            normed(frame + 3)
    if first:
        stats[0:1] = jnp.sum(part_sum, axis=0, keepdims=True)
        stats[1:2] = jnp.sum(part_square, axis=0, keepdims=True)


def conv_call(first, flags, weights, tables, gain, shift, frames, halo, kernel, feats=None):
    rows_halo, before, corners = halo
    n_frames, n_rows, cols, width = frames.shape
    smem, vmem, anywhere = (pl.BlockSpec(memory_space=m) for m in (pltpu.SMEM, pltpu.VMEM, pl.ANY))
    operands = [*tables, gain[None], shift[None], frames, *rows_halo, before, *corners]
    in_specs = [smem, smem] + [vmem] * len(operands) + [anywhere]
    operands = [flags, weights, *operands, kernel]
    if first:
        out_shape = (
            jax.ShapeDtypeStruct(frames.shape, jnp.bfloat16),
            jax.ShapeDtypeStruct((2, width), jnp.float32),
        )
        out_specs = (vmem, vmem)
    else:
        operands.append(feats)
        in_specs.append(vmem)
        out_shape = jax.ShapeDtypeStruct(frames.shape, jnp.float32)
        out_specs = vmem
    return pl.pallas_call(
        functools.partial(conv_kernel, len(tables), len(rows_halo), first),
        out_shape=out_shape,
        in_specs=in_specs,
        out_specs=out_specs,
        scratch_shapes=[
            pltpu.VMEM((n_frames + 2, n_rows + 2, cols, width), jnp.bfloat16),
            pltpu.VMEM(kernel.shape, jnp.bfloat16),
            pltpu.SemaphoreType.DMA((3,)),
        ],
        compiler_params=pltpu.CompilerParams(vmem_limit_bytes=40 << 20),
        cost_estimate=pl.CostEstimate(
            flops=2 * frames.size * width * 27, bytes_accessed=kernel.size * 2 + frames.size * 8, transcendentals=frames.size * 2
        ),
    )(*operands)


def edge_rows(frames):
    return frames[:, :1], frames[:, -1:]


def on_device(feats, clip_ids, gain_one, shift_one, kernel_one, gain_two, shift_two, kernel_two):
    own_slab = lax.axis_index("tm")
    place, places = lax.axis_index("space"), lax.axis_size("space")
    own_clip = lax.dynamic_index_in_dim(clip_ids, own_slab, keepdims=False)
    before_clip = lax.dynamic_index_in_dim(clip_ids, jnp.maximum(own_slab - 1, 0), keepdims=False)
    starting = jnp.logical_or(own_slab == 0, own_clip != before_clip)
    flags = jnp.stack([starting, place == 0, place == places - 1]).astype(jnp.int32)
    per_slab = feats.size // GROUPS * places
    weights = jnp.concatenate([slab_weights(clip_ids), jnp.full((1,), per_slab, jnp.float32)])

    halo = halos(feats, edge_rows(feats))
    inputs = feats.astype(jnp.float32)
    stats = jnp.stack([jnp.sum(inputs, axis=(0, 1, 2)), jnp.sum(inputs * inputs, axis=(0, 1, 2))])
    hidden, stats = conv_call(True, flags, weights, slab_tables(stats), gain_one, shift_one, feats, halo, kernel_one)
    halo = halos(hidden, edge_rows(hidden))
    return conv_call(False, flags, weights, slab_tables(stats), gain_two, shift_two, hidden, halo, kernel_two, feats)


def solution(mesh):
    return jax.shard_map(
        on_device,
        mesh=mesh,
        in_specs=(P("tm", "space", None, None), P(), P(), P(), P(), P(), P(), P()),
        out_specs=P("tm", "space", None, None),
        check_vma=False,
    )
```

time: 166 us -> 67 us (0.40)
  blocking collectives: 84.2 us -> 0 us
  other arithmetic: 28 us -> 3.4 us
  Pallas kernels: 0 us -> 16.4 us
  matrix products: 14.7 us -> 0 us
  starting transfers between devices: 13.9 us -> 23.5 us
  waiting for transfers between devices: 14.2 us -> 18.6 us
  local copies, waits for them, and re-layouts: 7.63 us -> 3.41 us
    unnamed x2 -> x0, blocking collectives: 84.2 us -> none
    concatenate x22 -> x3, other arithmetic: 19.1 us -> 0.09 us  [the longest x1 0.07 us: on_device(): jnp.concatenate([slab_weights(clip_ids), jnp.full((1,), per_slab, jnp.flo...]
    pallas_call x0 -> x2, Pallas kernels: none -> 16.4 us  [conv_call(): pl.pallas_call(functools.partial(conv_kernel, len(tables), len(rows_halo)...]
    dot_general x18 -> x0, matrix products: 14.7 us -> none  [causal_conv(): jnp.dot(stacked, kernel[tap_time, tap_row].reshape(3 * width, -1), prefer...]
    ppermute x6 -> x20, starting transfers between devices: 13.9 us -> 23.5 us  [the longest x16 15.4 us: traded(): lax.ppermute(value, axis, [(i, i ^ mask) for i in range(lax.axis_size(axi...]
    slice x8 -> x4, local copies, waits for them, and re-layouts: 4.61 us -> 0.07 us  [the longest x2 0.05 us: halos(): before = next_slab(frames[-2:])]
    ppermute x6 -> x20, waiting for transfers between devices: 14.2 us -> 18.6 us  [the longest x16 18.6 us: traded(): lax.ppermute(value, axis, [(i, i ^ mask) for i in range(lax.axis_size(axi...]
    reduce_sum x8 -> x1, other arithmetic: 3.99 us -> 1.46 us  [on_device(): jnp.sum(inputs, axis=(0, 1, 2))]
  transfers between devices with their start and end apart: 6 -> 20, of which waited for: 3 -> 9; matrix products, arithmetic and copies ran while one was open for 2% -> 5% of each run, Pallas kernels for 0% -> 0%
where the time goes in v4:
time: 67 us; the launch traced here: 66.8 us
  starting transfers between devices  23.5 us (35%)
  waiting for transfers between devices  18.6 us (28%)
  Pallas kernels  16.4 us (24%)
  local copies, waits for them, and re-layouts  3.41 us (5%)
  other arithmetic  3.4 us (5%)
  between operations  1.42 us (2%)
    ppermute x16, waiting for transfers between devices, traded(): lax.ppermute(value, axis, [(i, i ^ mask) for i in range(lax.axis_size(axi...  18.6 us
    pallas_call x2, Pallas kernels, conv_call(): pl.pallas_call(functools.partial(conv_kernel, len(tables), len(rows_halo)...  16.4 us
    ppermute x16, starting transfers between devices, traded(): lax.ppermute(value, axis, [(i, i ^ mask) for i in range(lax.axis_size(axi...  15.4 us
    ppermute x2, starting transfers between devices, next_slab(): lax.ppermute(value, 'tm', [(i, (i + 1) % peers) for i in range(peers)])  4.68 us
    ppermute x2, starting transfers between devices, halos(): corner = lax.ppermute(outer[-2:], AXES, cross)  3.48 us
    unnamed x16, local copies, waits for them, and re-layouts  2.03 us
    reduce_sum x1, other arithmetic, on_device(): jnp.sum(inputs, axis=(0, 1, 2))  1.46 us
  transfers between devices with their start and end apart: 20, of which 9 were waited for; matrix products, arithmetic and copies ran while one was open for 5% of the time, Pallas kernels for 0%

profile of v4, /device:TPU:0, one launch (start us, length us, event | category | flops | bytes accessed | tf_op | source)
XLA Modules:
  0.0 66.8 jit_solution(11098130951714245501)
XLA Ops:
  0.0 0.0 copy-start
  0.0 0.0 copy-start.7
  0.0 0.0 copy-start.4
  0.0 0.0 copy-start.3
  0.0 1.5 %convert_reduce_fusion = (f32[256]{0:T(256)S(1)}, f32[256]{0:T(256)S(1)}) fusion(bf16[4,4,96,256]{3,2,1,0:T(8,128)(2,1)} %refs_13_.1), kind=kLoop, calls=%fused_computation.2 | loop fusion | flops 1572352 | bytes 788480 | tf_op jit(solution)/shard_map/reduce_sum | solution.py:245
  1.5 0.5 collective-permute-start
  2.0 1.0 %slice_select_fusion.1 = bf16[4,1,96,256]{3,2,1,0:T(8,128)(2,1)S(1)} fusion(bf16[4,4,96,256]{3,2,1,0:T(8,128)(2,1)} %refs_13_.1, pred[]{:T(512)} %eq.18), kind=kLoop, calls=%fused_computation.5 | loop fusion | flops 98304 | bytes 589825 | tf_op jit(solution)/shard_map/jit(_where)/select_n | solution.py:65
  3.1 0.1 collective-permute-start.7
  3.2 0.0 copy-done
  3.2 3.0 %collective-permute-start.8 = (bf16[2,4,96,256]{3,2,1,0:T(8,128)(2,1)S(1)}, bf16[2,4,96,256]{3,2,1,0:T(8,128)(2,1)S(1)}, u32[]{:S(2)}, u32[]{:S(2)}) collective-permute-start(bf16[2,4,96,256]{3,2,1,0:T(8,128)(2,1)S(1)} %slice.26), channel_id=1, source_target_pairs={{0,2},{2,4},{4,6},{6,8},{8,10},{10,12},{12,14},{14,16},{16,18},{18... | collective-permute-start | bytes 1179656 | tf_op jit(solution)/shard_map/ppermute | solution.py:58
  6.2 0.0 copy-done.7
  6.2 0.7 gather_fusion
  6.9 0.7 fusion.2
  7.6 0.0 collective-permute-done
  7.6 2.5 %collective-permute-start.3 = (f32[1,2,256]{2,1,0:T(2,128)S(1)}, f32[1,2,256]{2,1,0:T(2,128)S(1)}, u32[]{:S(2)}, u32[]{:S(2)}) collective-permute-start(f32[1,2,256]{2,1,0:T(2,128)S(1)} %add_bitcast_fusion.1), channel_id=1, source_target_pairs={{0,6},{2,4},{4,2},{6,0},{8,14},{10,12},{12,10},{14,8},{16,22},{18,... | collective-permute-start | bytes 6152 | tf_op jit(solution)/shard_map/ppermute | solution.py:19
  10.1 0.5 collective-permute-start.2
  10.6 0.5 collective-permute-start.1
  11.1 0.7 %compare_convert_fusion = f32[16]{0:T(128)S(1)} fusion(s32[16]{0:T(128)S(1)} %gather_fusion, s32[]{:T(128)} %bitcast, s32[]{:T(128)S(6)} %axis_index.15), kind=kLoop, calls=%fused_computation.15 | loop fusion | flops 160 | bytes 136 | tf_op jit(solution)/shard_map/convert_element_type | solution.py:53
  11.8 3.0 %collective-permute-done.3 = f32[1,2,256]{2,1,0:T(2,128)S(1)} collective-permute-done((f32[1,2,256]{2,1,0:T(2,128)S(1)}, f32[1,2,256]{2,1,0:T(2,128)S(1)}, u32[]{:S(2)}, u32[]{:S(2)}) %collective-permute-start.3) | collective-permute-done | bytes 2080 | tf_op jit(solution)/shard_map/ppermute | solution.py:19
  14.8 1.9 %collective-permute-start.9 = (bf16[2,1,96,256]{3,2,1,0:T(8,128)(2,1)S(1)}, bf16[2,1,96,256]{3,2,1,0:T(8,128)(2,1)S(1)}, u32[]{:S(2)}, u32[]{:S(2)}) collective-permute-start(bf16[2,1,96,256]{3,2,1,0:T(8,128)(2,1)S(1)} %slice.34), channel_id=1, source_target_pairs={{0,3},{1,2},{2,5},{3,4},{4,7},{5,6},{6,9},{7,8},{8,11},{9,10},{10,... | collective-permute-start | bytes 294920 | tf_op jit(solution)/shard_map/ppermute | solution.py:69
  16.7 0.0 collective-permute-done.2
  16.7 0.1 collective-permute-done.1
  16.8 3.6 %collective-permute-start.6 = (f32[4,2,256]{2,1,0:T(2,128)S(1)}, f32[4,2,256]{2,1,0:T(2,128)S(1)}, u32[]{:S(2)}, u32[]{:S(2)}) collective-permute-start(f32[4,2,256]{2,1,0:T(2,128)S(1)} %pad_maximum_fusion.refs_2_), channel_id=1, source_target_pairs={{0,24},{2,26},{4,28},{6,30},{8,16},{10,18},{12,20},{14,22},{16,8},... | collective-permute-start | bytes 24584 | tf_op jit(solution)/shard_map/ppermute | solution.py:19
  20.4 0.1 pad_maximum_fusion.3.refs_1_
  21.8 0.1 collective-permute-start.5
  21.9 0.4 collective-permute-done.6.refs_5_
  22.3 0.3 collective-permute-start.4
  22.6 0.1 add_convert_fusion.refs_0_
  22.7 3.7 %collective-permute-done.5.refs_4_ = f32[4,2,256]{2,1,0:T(2,128)S(1)} collective-permute-done((f32[4,2,256]{2,1,0:T(2,128)S(1)}, f32[4,2,256]{2,1,0:T(2,128)S(1)}, u32[]{:S(2)}, u32[]{:S(2)}) %collective-permute-start.5) | collective-permute-done | bytes 8224 | tf_op jit(solution)/shard_map/ppermute | solution.py:19
  26.4 0.0 collective-permute-done.4.refs_3_
  26.4 0.0 collective-permute-done.9.refs_11_
  26.4 0.0 collective-permute-done.7.refs_9_
  26.4 0.0 collective-permute-done.8.refs_10_
  26.4 0.0 copy-done.4
  26.4 0.0 copy-done.3
  26.4 0.0 copy-start.1
  26.4 2.0 %copy-done.1 = bf16[3,3,3,256,256]{4,3,2,1,0:T(8,128)(2,1)S(1)} copy-done((bf16[3,3,3,256,256]{4,3,2,1,0:T(8,128)(2,1)S(1)}, bf16[3,3,3,256,256]{4,3,2,1,0:T(8,128)(2,1)}, u32[]{:S(2)}) %copy-start.1) | copy-done | bytes 3538968
  28.4 7.7 %shard_map.82 = (bf16[4,4,96,256]{3,2,1,0:T(8,128)(2,1)S(1)}, f32[2,256]{1,0:T(2,128)S(1)}) custom-call(s32[3]{0:T(128)S(1)} %add_convert_fusion.refs_0_, f32[17]{0:T(128)S(1)} %pad_maximum_fusion.3.refs_1_, f32[4,2,256]{2,1,0:T(2,128)S(1)} %pad_maximum_fusion.refs_2_, f32[4,2,256]{2,1,0:T(2,128)S(1)} %collective-permute-done.4.refs_3_, ...), custom_call_target="tpu_custom_call" | custom-call | flops 5435817984 | bytes 6684672 | tf_op jit(solution)/shard_map/pallas_call | solution.py:212
  36.1 0.0 copy-start.5
  36.1 0.0 copy-start.6
  36.1 0.3 collective-permute-start.10
  36.4 1.7 %collective-permute-start.18 = (bf16[2,4,96,256]{3,2,1,0:T(8,128)(2,1)S(1)}, bf16[2,4,96,256]{3,2,1,0:T(8,128)(2,1)S(1)}, u32[]{:S(2)}, u32[]{:S(2)}) collective-permute-start(bf16[2,4,96,256]{3,2,1,0:T(8,128)(2,1)S(1)} %slice.30), channel_id=1, source_target_pairs={{0,2},{2,4},{4,6},{6,8},{8,10},{10,12},{12,14},{14,16},{16,18},{18... | collective-permute-start | bytes 1179656 | tf_op jit(solution)/shard_map/ppermute | solution.py:58
  38.1 0.2 collective-permute-start.17
  38.4 0.0 collective-permute-done.10
  38.4 0.8 %collective-permute-start.13 = (f32[1,2,256]{2,1,0:T(2,128)S(1)}, f32[1,2,256]{2,1,0:T(2,128)S(1)}, u32[]{:S(2)}, u32[]{:S(2)}) collective-permute-start(f32[1,2,256]{2,1,0:T(2,128)S(1)} %add_bitcast_fusion), channel_id=1, source_target_pairs={{0,6},{2,4},{4,2},{6,0},{8,14},{10,12},{12,10},{14,8},{16,22},{18,... | collective-permute-start | bytes 6152 | tf_op jit(solution)/shard_map/ppermute | solution.py:19
  39.2 1.8 %collective-permute-start.12 = (f32[1,2,256]{2,1,0:T(2,128)S(1)}, f32[1,2,256]{2,1,0:T(2,128)S(1)}, u32[]{:S(2)}, u32[]{:S(2)}) collective-permute-start(f32[1,2,256]{2,1,0:T(2,128)S(1)} %add_bitcast_fusion), channel_id=1, source_target_pairs={{0,4},{2,6},{4,0},{6,2},{8,12},{10,14},{12,8},{14,10},{16,20},{18,... | collective-permute-start | bytes 6152 | tf_op jit(solution)/shard_map/ppermute | solution.py:19
  41.1 0.8 %collective-permute-start.11 = (f32[1,2,256]{2,1,0:T(2,128)S(1)}, f32[1,2,256]{2,1,0:T(2,128)S(1)}, u32[]{:S(2)}, u32[]{:S(2)}) collective-permute-start(f32[1,2,256]{2,1,0:T(2,128)S(1)} %add_bitcast_fusion), channel_id=1, source_target_pairs={{0,2},{2,0},{4,6},{6,4},{8,10},{10,8},{12,14},{14,12},{16,18},{18,... | collective-permute-start | bytes 6152 | tf_op jit(solution)/shard_map/ppermute | solution.py:19
  41.9 5.3 %collective-permute-done.13 = f32[1,2,256]{2,1,0:T(2,128)S(1)} collective-permute-done((f32[1,2,256]{2,1,0:T(2,128)S(1)}, f32[1,2,256]{2,1,0:T(2,128)S(1)}, u32[]{:S(2)}, u32[]{:S(2)}) %collective-permute-start.13) | collective-permute-done | bytes 2080 | tf_op jit(solution)/shard_map/ppermute | solution.py:19
  47.2 1.6 %collective-permute-start.19 = (bf16[2,1,96,256]{3,2,1,0:T(8,128)(2,1)S(1)}, bf16[2,1,96,256]{3,2,1,0:T(8,128)(2,1)S(1)}, u32[]{:S(2)}, u32[]{:S(2)}) collective-permute-start(bf16[2,1,96,256]{3,2,1,0:T(8,128)(2,1)S(1)} %slice.35), channel_id=1, source_target_pairs={{0,3},{1,2},{2,5},{3,4},{4,7},{5,6},{6,9},{7,8},{8,11},{9,10},{10,... | collective-permute-start | bytes 294920 | tf_op jit(solution)/shard_map/ppermute | solution.py:69
  48.7 0.0 collective-permute-done.12
  48.7 0.1 collective-permute-done.11
  48.9 3.2 %collective-permute-start.16 = (f32[4,2,256]{2,1,0:T(2,128)S(1)}, f32[4,2,256]{2,1,0:T(2,128)S(1)}, u32[]{:S(2)}, u32[]{:S(2)}) collective-permute-start(f32[4,2,256]{2,1,0:T(2,128)S(1)} %pad_maximum_fusion.1.refs_2_), channel_id=1, source_target_pairs={{0,24},{2,26},{4,28},{6,30},{8,16},{10,18},{12,20},{14,22},{16,8},... | collective-permute-start | bytes 24584 | tf_op jit(solution)/shard_map/ppermute | solution.py:19
  52.0 0.0 collective-permute-start.15
  52.0 2.3 %collective-permute-done.16.refs_5_ = f32[4,2,256]{2,1,0:T(2,128)S(1)} collective-permute-done((f32[4,2,256]{2,1,0:T(2,128)S(1)}, f32[4,2,256]{2,1,0:T(2,128)S(1)}, u32[]{:S(2)}, u32[]{:S(2)}) %collective-permute-start.16) | collective-permute-done | bytes 8224 | tf_op jit(solution)/shard_map/ppermute | solution.py:19
  54.3 0.0 collective-permute-start.14
  54.3 2.2 %collective-permute-done.15.refs_4_ = f32[4,2,256]{2,1,0:T(2,128)S(1)} collective-permute-done((f32[4,2,256]{2,1,0:T(2,128)S(1)}, f32[4,2,256]{2,1,0:T(2,128)S(1)}, u32[]{:S(2)}, u32[]{:S(2)}) %collective-permute-start.15) | collective-permute-done | bytes 8224 | tf_op jit(solution)/shard_map/ppermute | solution.py:19
  56.6 1.4 %collective-permute-done.14.refs_3_ = f32[4,2,256]{2,1,0:T(2,128)S(1)} collective-permute-done((f32[4,2,256]{2,1,0:T(2,128)S(1)}, f32[4,2,256]{2,1,0:T(2,128)S(1)}, u32[]{:S(2)}, u32[]{:S(2)}) %collective-permute-start.14) | collective-permute-done | bytes 8224 | tf_op jit(solution)/shard_map/ppermute | solution.py:19
  58.0 0.0 collective-permute-done.19.refs_11_
  58.0 0.0 collective-permute-done.17.refs_9_
  58.0 0.0 collective-permute-done.18.refs_10_
  58.0 0.0 copy-done.2
  58.0 0.0 copy-done.5
  58.0 0.0 copy-done.6
  58.0 8.8 %shard_map.83 = f32[4,4,96,256]{3,2,1,0:T(8,128)} custom-call(s32[3]{0:T(128)S(1)} %add_convert_fusion.refs_0_, f32[17]{0:T(128)S(1)} %pad_maximum_fusion.3.refs_1_, f32[4,2,256]{2,1,0:T(2,128)S(1)} %pad_maximum_fusion.1.refs_2_, f32[4,2,256]{2,1,0:T(2,128)S(1)} %collective-permute-done.14.refs_3_, f32[4,2,256]{2,1,0:T(2,128)S(1)} %collective-permute-done.15.refs_4_, ...), custom_call_target="tpu_custom_call" | custom-call | flops 5435817984 | bytes 6684672 | tf_op jit(solution)/shard_map/pallas_call | solution.py:212
  (13 shorter events, 0.1 us)
Async XLA Ops:
  0.0 3.2 %copy-start = (bf16[4,4,96,256]{3,2,1,0:T(8,128)(2,1)S(1)}, bf16[4,4,96,256]{3,2,1,0:T(8,128)(2,1)}, u32[]{:S(2)}) copy-start(bf16[4,4,96,256]{3,2,1,0:T(8,128)(2,1)} %refs_13_.1) | copy-start | bytes 2359300
  0.0 6.2 %copy-start.7 = (s32[16]{0:T(128)S(1)}, s32[16]{0:T(128)}, u32[]{:S(2)}) copy-start(s32[16]{0:T(128)} %param.9) | copy-start | bytes 196
  0.0 26.4 %copy-start.4 = (f32[256]{0:T(256)S(1)}, f32[256]{0:T(256)}, u32[]{:S(2)}) copy-start(f32[256]{0:T(256)} %param.11) | copy-start | bytes 3076
  0.0 26.4 %copy-start.3 = (f32[256]{0:T(256)S(1)}, f32[256]{0:T(256)}, u32[]{:S(2)}) copy-start(f32[256]{0:T(256)} %param.10) | copy-start | bytes 3076
  1.5 6.1 %collective-permute-start = (f32[2,256]{1,0:T(2,128)S(1)}, f32[2,256]{1,0:T(2,128)S(1)}, u32[]{:S(2)}, u32[]{:S(2)}) collective-permute-start(f32[2,256]{1,0:T(2,128)S(1)} %pad_maximum_fusion.2), channel_id=1, source_target_pairs={{0,1},{1,0},{2,3},{3,2},{4,5},{5,4},{6,7},{7,6},{8,9},{9,8},{10,11... | collective-permute-start | bytes 6152 | tf_op jit(solution)/shard_map/ppermute | solution.py:19
  3.1 23.3 %collective-permute-start.7 = (bf16[4,1,96,256]{3,2,1,0:T(8,128)(2,1)S(1)}, bf16[4,1,96,256]{3,2,1,0:T(8,128)(2,1)S(1)}, u32[]{:S(2)}, u32[]{:S(2)}) collective-permute-start(bf16[4,1,96,256]{3,2,1,0:T(8,128)(2,1)S(1)} %slice_select_fusion.1), channel_id=1, source_target_pairs={{0,1},{1,0},{2,3},{3,2},{4,5},{5,4},{6,7},{7,6},{8,9},{9,8},{10,11... | collective-permute-start | bytes 589832 | tf_op jit(solution)/shard_map/ppermute | solution.py:19
  3.2 23.2 %collective-permute-start.8 = (bf16[2,4,96,256]{3,2,1,0:T(8,128)(2,1)S(1)}, bf16[2,4,96,256]{3,2,1,0:T(8,128)(2,1)S(1)}, u32[]{:S(2)}, u32[]{:S(2)}) collective-permute-start(bf16[2,4,96,256]{3,2,1,0:T(8,128)(2,1)S(1)} %slice.26), channel_id=1, source_target_pairs={{0,2},{2,4},{4,6},{6,8},{8,10},{10,12},{12,14},{14,16},{16,18},{18... | collective-permute-start | bytes 1179656 | tf_op jit(solution)/shard_map/ppermute | solution.py:58
  7.6 7.3 %collective-permute-start.3 = (f32[1,2,256]{2,1,0:T(2,128)S(1)}, f32[1,2,256]{2,1,0:T(2,128)S(1)}, u32[]{:S(2)}, u32[]{:S(2)}) collective-permute-start(f32[1,2,256]{2,1,0:T(2,128)S(1)} %add_bitcast_fusion.1), channel_id=1, source_target_pairs={{0,6},{2,4},{4,2},{6,0},{8,14},{10,12},{12,10},{14,8},{16,22},{18,... | collective-permute-start | bytes 6152 | tf_op jit(solution)/shard_map/ppermute | solution.py:19
  10.1 6.7 %collective-permute-start.2 = (f32[1,2,256]{2,1,0:T(2,128)S(1)}, f32[1,2,256]{2,1,0:T(2,128)S(1)}, u32[]{:S(2)}, u32[]{:S(2)}) collective-permute-start(f32[1,2,256]{2,1,0:T(2,128)S(1)} %add_bitcast_fusion.1), channel_id=1, source_target_pairs={{0,4},{2,6},{4,0},{6,2},{8,12},{10,14},{12,8},{14,10},{16,20},{18,... | collective-permute-start | bytes 6152 | tf_op jit(solution)/shard_map/ppermute | solution.py:19
  10.6 6.2 %collective-permute-start.1 = (f32[1,2,256]{2,1,0:T(2,128)S(1)}, f32[1,2,256]{2,1,0:T(2,128)S(1)}, u32[]{:S(2)}, u32[]{:S(2)}) collective-permute-start(f32[1,2,256]{2,1,0:T(2,128)S(1)} %add_bitcast_fusion.1), channel_id=1, source_target_pairs={{0,2},{2,0},{4,6},{6,4},{8,10},{10,8},{12,14},{14,12},{16,18},{18,... | collective-permute-start | bytes 6152 | tf_op jit(solution)/shard_map/ppermute | solution.py:19
  14.8 11.6 %collective-permute-start.9 = (bf16[2,1,96,256]{3,2,1,0:T(8,128)(2,1)S(1)}, bf16[2,1,96,256]{3,2,1,0:T(8,128)(2,1)S(1)}, u32[]{:S(2)}, u32[]{:S(2)}) collective-permute-start(bf16[2,1,96,256]{3,2,1,0:T(8,128)(2,1)S(1)} %slice.34), channel_id=1, source_target_pairs={{0,3},{1,2},{2,5},{3,4},{4,7},{5,6},{6,9},{7,8},{8,11},{9,10},{10,... | collective-permute-start | bytes 294920 | tf_op jit(solution)/shard_map/ppermute | solution.py:69
  16.8 5.5 %collective-permute-start.6 = (f32[4,2,256]{2,1,0:T(2,128)S(1)}, f32[4,2,256]{2,1,0:T(2,128)S(1)}, u32[]{:S(2)}, u32[]{:S(2)}) collective-permute-start(f32[4,2,256]{2,1,0:T(2,128)S(1)} %pad_maximum_fusion.refs_2_), channel_id=1, source_target_pairs={{0,24},{2,26},{4,28},{6,30},{8,16},{10,18},{12,20},{14,22},{16,8},... | collective-permute-start | bytes 24584 | tf_op jit(solution)/shard_map/ppermute | solution.py:19
  21.8 4.6 %collective-permute-start.5 = (f32[4,2,256]{2,1,0:T(2,128)S(1)}, f32[4,2,256]{2,1,0:T(2,128)S(1)}, u32[]{:S(2)}, u32[]{:S(2)}) collective-permute-start(f32[4,2,256]{2,1,0:T(2,128)S(1)} %pad_maximum_fusion.refs_2_), channel_id=1, source_target_pairs={{0,16},{2,18},{4,20},{6,22},{8,24},{10,26},{12,28},{14,30},{16,0},... | collective-permute-start | bytes 24584 | tf_op jit(solution)/shard_map/ppermute | solution.py:19
  22.3 4.1 %collective-permute-start.4 = (f32[4,2,256]{2,1,0:T(2,128)S(1)}, f32[4,2,256]{2,1,0:T(2,128)S(1)}, u32[]{:S(2)}, u32[]{:S(2)}) collective-permute-start(f32[4,2,256]{2,1,0:T(2,128)S(1)} %pad_maximum_fusion.refs_2_), channel_id=1, source_target_pairs={{0,8},{2,10},{4,12},{6,14},{8,0},{10,2},{12,4},{14,6},{16,24},{18,... | collective-permute-start | bytes 24584 | tf_op jit(solution)/shard_map/ppermute | solution.py:19
  26.4 2.0 %copy-start.1 = (bf16[3,3,3,256,256]{4,3,2,1,0:T(8,128)(2,1)S(1)}, bf16[3,3,3,256,256]{4,3,2,1,0:T(8,128)(2,1)}, u32[]{:S(2)}) copy-start(bf16[3,3,3,256,256]{4,3,2,1,0:T(8,128)(2,1)} %refs_12_.2) | copy-start | bytes 10616836
  28.4 29.5 %copy-start.2 = (bf16[3,3,3,256,256]{4,3,2,1,0:T(8,128)(2,1)S(1)}, bf16[3,3,3,256,256]{4,3,2,1,0:T(8,128)(2,1)}, u32[]{:S(2)}) copy-start(bf16[3,3,3,256,256]{4,3,2,1,0:T(8,128)(2,1)} %refs_12_.3) | copy-start | bytes 10616836
  36.1 21.9 %copy-start.5 = (f32[256]{0:T(256)S(1)}, f32[256]{0:T(256)}, u32[]{:S(2)}) copy-start(f32[256]{0:T(256)} %param.13) | copy-start | bytes 3076
  36.1 21.9 %copy-start.6 = (f32[256]{0:T(256)S(1)}, f32[256]{0:T(256)}, u32[]{:S(2)}) copy-start(f32[256]{0:T(256)} %param.14) | copy-start | bytes 3076
  36.1 2.2 %collective-permute-start.10 = (f32[2,256]{1,0:T(2,128)S(1)}, f32[2,256]{1,0:T(2,128)S(1)}, u32[]{:S(2)}, u32[]{:S(2)}) collective-permute-start(f32[2,256]{1,0:T(2,128)S(1)} %get-tuple-element.7), channel_id=1, source_target_pairs={{0,1},{1,0},{2,3},{3,2},{4,5},{5,4},{6,7},{7,6},{8,9},{9,8},{10,11... | collective-permute-start | bytes 6152 | tf_op jit(solution)/shard_map/ppermute | solution.py:19
  36.4 21.5 %collective-permute-start.18 = (bf16[2,4,96,256]{3,2,1,0:T(8,128)(2,1)S(1)}, bf16[2,4,96,256]{3,2,1,0:T(8,128)(2,1)S(1)}, u32[]{:S(2)}, u32[]{:S(2)}) collective-permute-start(bf16[2,4,96,256]{3,2,1,0:T(8,128)(2,1)S(1)} %slice.30), channel_id=1, source_target_pairs={{0,2},{2,4},{4,6},{6,8},{8,10},{10,12},{12,14},{14,16},{16,18},{18... | collective-permute-start | bytes 1179656 | tf_op jit(solution)/shard_map/ppermute | solution.py:58
  38.1 19.8 %collective-permute-start.17 = (bf16[4,1,96,256]{3,2,1,0:T(8,128)(2,1)S(1)}, bf16[4,1,96,256]{3,2,1,0:T(8,128)(2,1)S(1)}, u32[]{:S(2)}, u32[]{:S(2)}) collective-permute-start(bf16[4,1,96,256]{3,2,1,0:T(8,128)(2,1)S(1)} %slice_select_fusion), channel_id=1, source_target_pairs={{0,1},{1,0},{2,3},{3,2},{4,5},{5,4},{6,7},{7,6},{8,9},{9,8},{10,11... | collective-permute-start | bytes 589832 | tf_op jit(solution)/shard_map/ppermute | solution.py:19
  38.4 8.8 %collective-permute-start.13 = (f32[1,2,256]{2,1,0:T(2,128)S(1)}, f32[1,2,256]{2,1,0:T(2,128)S(1)}, u32[]{:S(2)}, u32[]{:S(2)}) collective-permute-start(f32[1,2,256]{2,1,0:T(2,128)S(1)} %add_bitcast_fusion), channel_id=1, source_target_pairs={{0,6},{2,4},{4,2},{6,0},{8,14},{10,12},{12,10},{14,8},{16,22},{18,... | collective-permute-start | bytes 6152 | tf_op jit(solution)/shard_map/ppermute | solution.py:19
  39.2 9.5 %collective-permute-start.12 = (f32[1,2,256]{2,1,0:T(2,128)S(1)}, f32[1,2,256]{2,1,0:T(2,128)S(1)}, u32[]{:S(2)}, u32[]{:S(2)}) collective-permute-start(f32[1,2,256]{2,1,0:T(2,128)S(1)} %add_bitcast_fusion), channel_id=1, source_target_pairs={{0,4},{2,6},{4,0},{6,2},{8,12},{10,14},{12,8},{14,10},{16,20},{18,... | collective-permute-start | bytes 6152 | tf_op jit(solution)/shard_map/ppermute | solution.py:19
  41.1 7.8 %collective-permute-start.11 = (f32[1,2,256]{2,1,0:T(2,128)S(1)}, f32[1,2,256]{2,1,0:T(2,128)S(1)}, u32[]{:S(2)}, u32[]{:S(2)}) collective-permute-start(f32[1,2,256]{2,1,0:T(2,128)S(1)} %add_bitcast_fusion), channel_id=1, source_target_pairs={{0,2},{2,0},{4,6},{6,4},{8,10},{10,8},{12,14},{14,12},{16,18},{18,... | collective-permute-start | bytes 6152 | tf_op jit(solution)/shard_map/ppermute | solution.py:19
  47.2 10.8 %collective-permute-start.19 = (bf16[2,1,96,256]{3,2,1,0:T(8,128)(2,1)S(1)}, bf16[2,1,96,256]{3,2,1,0:T(8,128)(2,1)S(1)}, u32[]{:S(2)}, u32[]{:S(2)}) collective-permute-start(bf16[2,1,96,256]{3,2,1,0:T(8,128)(2,1)S(1)} %slice.35), channel_id=1, source_target_pairs={{0,3},{1,2},{2,5},{3,4},{4,7},{5,6},{6,9},{7,8},{8,11},{9,10},{10,... | collective-permute-start | bytes 294920 | tf_op jit(solution)/shard_map/ppermute | solution.py:69
  48.9 5.5 %collective-permute-start.16 = (f32[4,2,256]{2,1,0:T(2,128)S(1)}, f32[4,2,256]{2,1,0:T(2,128)S(1)}, u32[]{:S(2)}, u32[]{:S(2)}) collective-permute-start(f32[4,2,256]{2,1,0:T(2,128)S(1)} %pad_maximum_fusion.1.refs_2_), channel_id=1, source_target_pairs={{0,24},{2,26},{4,28},{6,30},{8,16},{10,18},{12,20},{14,22},{16,8},... | collective-permute-start | bytes 24584 | tf_op jit(solution)/shard_map/ppermute | solution.py:19
  52.0 4.5 %collective-permute-start.15 = (f32[4,2,256]{2,1,0:T(2,128)S(1)}, f32[4,2,256]{2,1,0:T(2,128)S(1)}, u32[]{:S(2)}, u32[]{:S(2)}) collective-permute-start(f32[4,2,256]{2,1,0:T(2,128)S(1)} %pad_maximum_fusion.1.refs_2_), channel_id=1, source_target_pairs={{0,16},{2,18},{4,20},{6,22},{8,24},{10,26},{12,28},{14,30},{16,0},... | collective-permute-start | bytes 24584 | tf_op jit(solution)/shard_map/ppermute | solution.py:19
  54.3 3.7 %collective-permute-start.14 = (f32[4,2,256]{2,1,0:T(2,128)S(1)}, f32[4,2,256]{2,1,0:T(2,128)S(1)}, u32[]{:S(2)}, u32[]{:S(2)}) collective-permute-start(f32[4,2,256]{2,1,0:T(2,128)S(1)} %pad_maximum_fusion.1.refs_2_), channel_id=1, source_target_pairs={{0,8},{2,10},{4,12},{6,14},{8,0},{10,2},{12,4},{14,6},{16,24},{18,... | collective-permute-start | bytes 24584 | tf_op jit(solution)/shard_map/ppermute | solution.py:19

commit v5 on v4

--- a/solution.py
+++ b/solution.py
@@ -34,23 +34,16 @@
     peers = lax.axis_size("tm")
     total = space_total(stats)[None]
     if not is_power(peers):
-        return [lax.all_gather(total, "tm", tiled=True)]
-    held = [total]
-    step = 1
-    while step < peers:
-        ways = min(4, peers // step)
+        return [lax.all_gather(total, "tm", tiled=True)], None
+    held, offsets = [total], [0]
+    left = peers
+    while left > 1:
+        ways = min(4, left)
+        left //= ways
         block = held[0] if len(held) == 1 else jnp.concatenate(held, axis=0)
-        held = [block] + [traded(block, "tm", step * way) for way in range(1, ways)]
-        step *= ways
-    return held
-
-
-def slab_weights(clip_ids):
-    slabs = jnp.arange(lax.axis_size("tm"), dtype=jnp.int32)
-    own_slab = lax.axis_index("tm")
-    own_clip = lax.dynamic_index_in_dim(clip_ids, own_slab, keepdims=False)
-    order = slabs ^ own_slab if is_power(lax.axis_size("tm")) else slabs
-    return (jnp.take(clip_ids, order) == own_clip).astype(jnp.float32)
+        held = [block] + [traded(block, "tm", left * way) for way in range(1, ways)]
+        offsets = [(left * way) ^ offset for way in range(ways) for offset in offsets]
+    return held, tuple(offsets)
 
 
 def next_slab(value):
@@ -60,14 +53,14 @@
 
 def halos(frames, edges):
     slabs, places = lax.axis_size("tm"), lax.axis_size("space")
-    top, bottom = edges
     if places == 2:
-        outer = jnp.where(lax.axis_index("space") == 0, bottom, top)
+        (outer,) = edges
+        before = next_slab(frames[-2:])
         rows = traded(outer, "space", 1)
-        before = next_slab(frames[-2:])
         cross = [(t * 2 + s, (t + 1) % slabs * 2 + 1 - s) for t in range(slabs) for s in range(2)]
         corner = lax.ppermute(outer[-2:], AXES, cross)
         return [rows], before, [corner]
+    top, bottom = edges
     above = lax.ppermute(bottom, "space", [(i, (i + 1) % places) for i in range(places)])
     below = lax.ppermute(top, "space", [(i, (i - 1) % places) for i in range(places)])
     before = next_slab(frames[-2:])
@@ -86,15 +79,66 @@
     return values
 
 
-def conv_kernel(n_tables, n_sides, first, *refs):
-    flags, weights = refs[:2]
-    tables = refs[2 : 2 + n_tables]
-    gain, shift, frames = refs[2 + n_tables : 5 + n_tables]
-    rest = refs[5 + n_tables :]
+def sent_rows(frames, frame, places, edges):
+    n_rows = frames.shape[1]
+    if places == 2:
+        low = lax.axis_index("space") == 0
+        edges[0][frame, 0] = jnp.where(low, frames[frame, n_rows - 1], frames[frame, 0])
+    else:
+        edges[0][frame, 0] = frames[frame, 0]
+        edges[1][frame, 0] = frames[frame, n_rows - 1]
+
+
+def stats_kernel(places, frames_hbm, stats, *rest):
+    edges, (frames, sems) = rest[:-2], rest[-2:]
+    n_frames, n_rows, _, width = frames.shape
+    copies = [pltpu.make_async_copy(frames_hbm.at[f], frames.at[f], sems.at[f]) for f in range(n_frames)]
+    for copy in copies:
+        copy.start()
+    part_sum = jnp.zeros((8, width), jnp.float32)
+    part_square = jnp.zeros((8, width), jnp.float32)
+    for frame in range(n_frames):
+        copies[frame].wait()
+        for row in range(n_rows):
+            values = frames[frame, row].astype(jnp.float32)
+            part_sum = part_sum + jnp.sum(values.reshape(-1, 8, width), axis=0)
+            part_square = part_square + jnp.sum((values * values).reshape(-1, 8, width), axis=0)
+        sent_rows(frames, frame, places, edges)
+    stats[0:1] = jnp.sum(part_sum, axis=0, keepdims=True)
+    stats[1:2] = jnp.sum(part_square, axis=0, keepdims=True)
+
+
+def edge_shapes(frames, places):
+    shape = (frames.shape[0], 1) + frames.shape[2:]
+    return (jax.ShapeDtypeStruct(shape, jnp.bfloat16),) * (1 if places == 2 else 2)
+
+
+def stats_call(frames):
+    places = lax.axis_size("space")
+    edges = edge_shapes(frames, places)
+    vmem = pl.BlockSpec(memory_space=pltpu.VMEM)
+    stats, *edges = pl.pallas_call(
+        functools.partial(stats_kernel, places),
+        out_shape=(jax.ShapeDtypeStruct((2, frames.shape[3]), jnp.float32),) + edges,
+        in_specs=[pl.BlockSpec(memory_space=pl.ANY)],
+        out_specs=(vmem,) * (1 + len(edges)),
+        scratch_shapes=[pltpu.VMEM(frames.shape, jnp.bfloat16), pltpu.SemaphoreType.DMA((frames.shape[0],))],
+        compiler_params=pltpu.CompilerParams(vmem_limit_bytes=8 << 20),
+        cost_estimate=pl.CostEstimate(flops=4 * frames.size, bytes_accessed=2 * frames.size, transcendentals=0),
+    )(frames)
+    return stats, edges
+
+
+def conv_kernel(n_tables, n_sides, offsets, first, *refs):
+    clip_ids = refs[0]
+    tables = refs[1 : 1 + n_tables]
+    gain, shift, frames = refs[1 + n_tables : 4 + n_tables]
+    rest = refs[4 + n_tables :]
     rows_halo, before, corners = rest[:n_sides], rest[n_sides], rest[n_sides + 1 : 2 * n_sides + 1]
     rest = rest[2 * n_sides + 1 :]
     if first:
-        kernel_hbm, hidden, stats, act, taps, sems = rest
+        kernel_hbm, hidden, stats = rest[:3]
+        edges, (act, taps, sems) = rest[3:-3], rest[-3:]
     else:
         kernel_hbm, feats, out, act, taps, sems = rest
     n_frames, n_rows, cols, width = frames.shape
@@ -102,24 +146,27 @@
     for copy in copies:
         copy.start()
 
+    own_slab = lax.axis_index("tm")
+    place, places = lax.axis_index("space"), lax.axis_size("space")
+    own_clip = clip_ids[own_slab]
+    entries = [(table, i) for table in tables for i in range(table.shape[0])]
     total = jnp.zeros((2, width), jnp.float32)
-    entry = 0
-    slabs_in = 0.0
-    for table in tables:
-        for i in range(table.shape[0]):
-            total = total + table[i] * weights[entry]
-            slabs_in = slabs_in + weights[entry]
-            entry += 1
+    slabs_in = jnp.int32(0)
+    for entry, (table, i) in enumerate(entries):
+        slab = entry if offsets is None else own_slab ^ offsets[entry]
+        same = clip_ids[slab] == own_clip
+        total = jnp.where(same, total + table[i], total)
+        slabs_in = slabs_in + same.astype(jnp.int32)
     grouped = group_total(total)
-    count = slabs_in * weights[entry]
+    count = slabs_in.astype(jnp.float32) * float(n_frames * n_rows * cols * width // GROUPS * places)
     mean = grouped[0:1] / count
     variance = grouped[1:2] / count - mean * mean
     scale = lax.rsqrt(variance + 1e-06) * gain[...]
     half_scale = 0.5 * scale
     half_shift = 0.5 * (shift[...] - mean * scale)
 
-    starting = flags[0] != 0
-    edge = (flags[1] != 0, flags[2] != 0)
+    starting = jnp.logical_or(own_slab == 0, clip_ids[jnp.maximum(own_slab - 1, 0)] != own_clip)
+    edge = (place == 0, place == places - 1)
 
     def put(frame, row, raw):
         half = raw.astype(jnp.float32) * half_scale + half_shift
@@ -184,6 +231,8 @@
                 part_square = part_square + jnp.sum((again * again).reshape(-1, 8, width), axis=0)
             else:
                 out[frame, row] = feats[frame, row].astype(jnp.float32) + value
+        if first:
+            sent_rows(hidden, frame, places, edges)
         if frame + 3 < n_frames + 2:
             normed(frame + 3)
     if first:
@@ -191,26 +240,28 @@
         stats[1:2] = jnp.sum(part_square, axis=0, keepdims=True)
 
 
-def conv_call(first, flags, weights, tables, gain, shift, frames, halo, kernel, feats=None):
+def conv_call(first, clip_ids, tables, gain, shift, frames, halo, kernel, feats=None):
+    tables, offsets = tables
     rows_halo, before, corners = halo
     n_frames, n_rows, cols, width = frames.shape
-    smem, vmem, anywhere = (pl.BlockSpec(memory_space=m) for m in (pltpu.SMEM, pltpu.VMEM, pl.ANY))
+    smem, vmem, hbm = (pl.BlockSpec(memory_space=m) for m in (pltpu.SMEM, pltpu.VMEM, pltpu.HBM))
     operands = [*tables, gain[None], shift[None], frames, *rows_halo, before, *corners]
-    in_specs = [smem, smem] + [vmem] * len(operands) + [anywhere]
-    operands = [flags, weights, *operands, kernel]
-    if first:
+    in_specs = [smem] + [vmem] * len(operands) + [hbm]
+    operands = [clip_ids, *operands, kernel]
+    if first:
+        edges = edge_shapes(frames, lax.axis_size("space"))
         out_shape = (
             jax.ShapeDtypeStruct(frames.shape, jnp.bfloat16),
             jax.ShapeDtypeStruct((2, width), jnp.float32),
-        )
-        out_specs = (vmem, vmem)
+        ) + edges
+        out_specs = (vmem,) * len(out_shape)
     else:
         operands.append(feats)
         in_specs.append(vmem)
         out_shape = jax.ShapeDtypeStruct(frames.shape, jnp.float32)
         out_specs = vmem
     return pl.pallas_call(
-        functools.partial(conv_kernel, len(tables), len(rows_halo), first),
+        functools.partial(conv_kernel, len(tables), len(rows_halo), offsets, first),
         out_shape=out_shape,
         in_specs=in_specs,
         out_specs=out_specs,
@@ -226,26 +277,12 @@
     )(*operands)
 
 
-def edge_rows(frames):
-    return frames[:, :1], frames[:, -1:]
-
-
 def on_device(feats, clip_ids, gain_one, shift_one, kernel_one, gain_two, shift_two, kernel_two):
-    own_slab = lax.axis_index("tm")
-    place, places = lax.axis_index("space"), lax.axis_size("space")
-    own_clip = lax.dynamic_index_in_dim(clip_ids, own_slab, keepdims=False)
-    before_clip = lax.dynamic_index_in_dim(clip_ids, jnp.maximum(own_slab - 1, 0), keepdims=False)
-    starting = jnp.logical_or(own_slab == 0, own_clip != before_clip)
-    flags = jnp.stack([starting, place == 0, place == places - 1]).astype(jnp.int32)
-    per_slab = feats.size // GROUPS * places
-    weights = jnp.concatenate([slab_weights(clip_ids), jnp.full((1,), per_slab, jnp.float32)])
-
-    halo = halos(feats, edge_rows(feats))
-    inputs = feats.astype(jnp.float32)
-    stats = jnp.stack([jnp.sum(inputs, axis=(0, 1, 2)), jnp.sum(inputs * inputs, axis=(0, 1, 2))])
-    hidden, stats = conv_call(True, flags, weights, slab_tables(stats), gain_one, shift_one, feats, halo, kernel_one)
-    halo = halos(hidden, edge_rows(hidden))
-    return conv_call(False, flags, weights, slab_tables(stats), gain_two, shift_two, hidden, halo, kernel_two, feats)
+    stats, edges = stats_call(feats)
+    halo = halos(feats, edges)
+    hidden, stats, *edges = conv_call(True, clip_ids, slab_tables(stats), gain_one, shift_one, feats, halo, kernel_one)
+    halo = halos(hidden, edges)
+    return conv_call(False, clip_ids, slab_tables(stats), gain_two, shift_two, hidden, halo, kernel_two, feats)
 
 
 def solution(mesh):

time: 67 us -> 66.6 us (level)
  local copies, waits for them, and re-layouts: 3.41 us -> 7.35 us
  other arithmetic: 3.4 us -> 0.02 us
  between operations: 1.42 us -> 0.11 us
  Pallas kernels: 16.4 us -> 17.6 us
    unnamed x16 -> x18, local copies, waits for them, and re-layouts: 2.03 us -> 6.28 us
    ppermute x16, starting transfers between devices: 15.4 us -> 19.2 us  [traded(): lax.ppermute(value, axis, [(i, i ^ mask) for i in range(lax.axis_size(axi...]
    ppermute x2, starting transfers between devices: 3.48 us -> 0.23 us  [halos(): corner = lax.ppermute(outer[-2:], AXES, cross)]
    reduce_sum x1 -> x0, other arithmetic: 1.46 us -> none  [on_device(): jnp.sum(inputs, axis=(0, 1, 2))]
    pallas_call x0 -> x1, Pallas kernels: none -> 1.19 us  [stats_call(): pl.pallas_call(functools.partial(stats_kernel, places), out_shape=(jax.Sh...]
    select_n x3 -> x0, other arithmetic: 1.07 us -> none  [the longest x2 1.07 us: halos(): outer = jnp.where(lax.axis_index('space') == 0, bottom, top)]
    slice x2, local copies, waits for them, and re-layouts: 0.05 us -> 1.05 us  [halos(): before = next_slab(frames[-2:])]
    ppermute x2, starting transfers between devices: 4.68 us -> 3.71 us  [next_slab(): lax.ppermute(value, 'tm', [(i, (i + 1) % peers) for i in range(peers)])]
  transfers between devices with their start and end apart: 20 -> 20, of which waited for: 9 -> 12; matrix products, arithmetic and copies ran while one was open for 5% -> 0% of each run, Pallas kernels for 0% -> 2%
where the time goes in v5:
time: 66.6 us; the launch traced here: 66.3 us
  starting transfers between devices  23.1 us (35%)
  waiting for transfers between devices  18 us (27%)
  Pallas kernels  17.6 us (26%)
  local copies, waits for them, and re-layouts  7.35 us (11%)
    ppermute x16, starting transfers between devices, traded(): lax.ppermute(value, axis, [(i, i ^ mask) for i in range(lax.axis_size(axi...  19.2 us
    ppermute x16, waiting for transfers between devices, traded(): lax.ppermute(value, axis, [(i, i ^ mask) for i in range(lax.axis_size(axi...  18 us
    pallas_call x2, Pallas kernels, conv_call(): pl.pallas_call(functools.partial(conv_kernel, len(tables), len(rows_halo)...  16.5 us
    unnamed x18, local copies, waits for them, and re-layouts  6.28 us
    ppermute x2, starting transfers between devices, next_slab(): lax.ppermute(value, 'tm', [(i, (i + 1) % peers) for i in range(peers)])  3.71 us
  transfers between devices with their start and end apart: 20, of which 12 were waited for; matrix products, arithmetic and copies ran while one was open for 0% of the time, Pallas kernels for 2%

profile of v5, /device:TPU:0, one launch (start us, length us, event | category | flops | bytes accessed | tf_op | source)
XLA Modules:
  0.0 66.3 jit_solution(11724757931829545951)
XLA Ops:
  0.0 1.0 %slice.12 = bf16[2,4,96,256]{3,2,1,0:T(8,128)(2,1)S(1)} slice(bf16[4,4,96,256]{3,2,1,0:T(8,128)(2,1)} %refs_12_.1), slice={[2:4], [0:4], [0:96], [0:256]} | slice | bytes 786432 | tf_op jit(solution)/shard_map/slice | solution.py:58
  1.0 3.0 %collective-permute-start.8 = (bf16[2,4,96,256]{3,2,1,0:T(8,128)(2,1)S(1)}, bf16[2,4,96,256]{3,2,1,0:T(8,128)(2,1)S(1)}, u32[]{:S(2)}, u32[]{:S(2)}) collective-permute-start(bf16[2,4,96,256]{3,2,1,0:T(8,128)(2,1)S(1)} %slice.12), channel_id=1, source_target_pairs={{0,2},{2,4},{4,6},{6,8},{8,10},{10,12},{12,14},{14,16},{16,18},{18... | collective-permute-start | bytes 1179656 | tf_op jit(solution)/shard_map/ppermute | solution.py:51
  4.0 0.0 copy-start
  4.0 1.1 %copy-done = bf16[4,4,96,256]{3,2,1,0:T(8,128)(2,1)S(1)} copy-done((bf16[4,4,96,256]{3,2,1,0:T(8,128)(2,1)S(1)}, bf16[4,4,96,256]{3,2,1,0:T(8,128)(2,1)}, u32[]{:S(2)}) %copy-start) | copy-done | bytes 786456
  5.2 1.2 %shard_map.82 = (f32[2,256]{1,0:T(2,128)S(1)}, bf16[4,1,96,256]{3,2,1,0:T(8,128)(2,1)S(1)}) custom-call(bf16[4,4,96,256]{3,2,1,0:T(8,128)(2,1)S(1)} %copy-done), custom_call_target="tpu_custom_call" | custom-call | flops 1572864 | bytes 786432 | tf_op jit(solution)/shard_map/pallas_call | solution.py:120
  6.3 0.1 collective-permute-start
  6.4 0.5 collective-permute-start.7
  6.9 0.6 collective-permute-done
  7.6 3.6 %collective-permute-start.3 = (f32[1,2,256]{2,1,0:T(2,128)S(1)}, f32[1,2,256]{2,1,0:T(2,128)S(1)}, u32[]{:S(2)}, u32[]{:S(2)}) collective-permute-start(f32[1,2,256]{2,1,0:T(2,128)S(1)} %add_bitcast_fusion.1), channel_id=1, source_target_pairs={{0,24},{2,26},{4,28},{6,30},{8,16},{10,18},{12,20},{14,22},{16,8},... | collective-permute-start | bytes 6152 | tf_op jit(solution)/shard_map/ppermute | solution.py:19
  11.2 0.0 collective-permute-start.2
  11.2 0.8 %collective-permute-start.1 = (f32[1,2,256]{2,1,0:T(2,128)S(1)}, f32[1,2,256]{2,1,0:T(2,128)S(1)}, u32[]{:S(2)}, u32[]{:S(2)}) collective-permute-start(f32[1,2,256]{2,1,0:T(2,128)S(1)} %add_bitcast_fusion.1), channel_id=1, source_target_pairs={{0,8},{2,10},{4,12},{6,14},{8,0},{10,2},{12,4},{14,6},{16,24},{18,... | collective-permute-start | bytes 6152 | tf_op jit(solution)/shard_map/ppermute | solution.py:19
  12.0 1.0 %collective-permute-done.3 = f32[1,2,256]{2,1,0:T(2,128)S(1)} collective-permute-done((f32[1,2,256]{2,1,0:T(2,128)S(1)}, f32[1,2,256]{2,1,0:T(2,128)S(1)}, u32[]{:S(2)}, u32[]{:S(2)}) %collective-permute-start.3) | collective-permute-done | bytes 2080 | tf_op jit(solution)/shard_map/ppermute | solution.py:19
  13.0 0.2 collective-permute-start.9
  13.1 2.5 %collective-permute-done.2 = f32[1,2,256]{2,1,0:T(2,128)S(1)} collective-permute-done((f32[1,2,256]{2,1,0:T(2,128)S(1)}, f32[1,2,256]{2,1,0:T(2,128)S(1)}, u32[]{:S(2)}, u32[]{:S(2)}) %collective-permute-start.2) | collective-permute-done | bytes 2080 | tf_op jit(solution)/shard_map/ppermute | solution.py:19
  15.7 0.0 collective-permute-done.1
  15.7 2.3 %collective-permute-start.6 = (f32[4,2,256]{2,1,0:T(2,128)S(1)}, f32[4,2,256]{2,1,0:T(2,128)S(1)}, u32[]{:S(2)}, u32[]{:S(2)}) collective-permute-start(f32[4,2,256]{2,1,0:T(2,128)S(1)} %pad_maximum_fusion.refs_1_), channel_id=1, source_target_pairs={{0,6},{2,4},{4,2},{6,0},{8,14},{10,12},{12,10},{14,8},{16,22},{18,... | collective-permute-start | bytes 24584 | tf_op jit(solution)/shard_map/ppermute | solution.py:19
  18.0 0.7 %collective-permute-start.5 = (f32[4,2,256]{2,1,0:T(2,128)S(1)}, f32[4,2,256]{2,1,0:T(2,128)S(1)}, u32[]{:S(2)}, u32[]{:S(2)}) collective-permute-start(f32[4,2,256]{2,1,0:T(2,128)S(1)} %pad_maximum_fusion.refs_1_), channel_id=1, source_target_pairs={{0,4},{2,6},{4,0},{6,2},{8,12},{10,14},{12,8},{14,10},{16,20},{18,... | collective-permute-start | bytes 24584 | tf_op jit(solution)/shard_map/ppermute | solution.py:19
  18.7 2.5 %collective-permute-done.6.refs_4_ = f32[4,2,256]{2,1,0:T(2,128)S(1)} collective-permute-done((f32[4,2,256]{2,1,0:T(2,128)S(1)}, f32[4,2,256]{2,1,0:T(2,128)S(1)}, u32[]{:S(2)}, u32[]{:S(2)}) %collective-permute-start.6) | collective-permute-done | bytes 8224 | tf_op jit(solution)/shard_map/ppermute | solution.py:19
  21.2 0.7 %collective-permute-start.4 = (f32[4,2,256]{2,1,0:T(2,128)S(1)}, f32[4,2,256]{2,1,0:T(2,128)S(1)}, u32[]{:S(2)}, u32[]{:S(2)}) collective-permute-start(f32[4,2,256]{2,1,0:T(2,128)S(1)} %pad_maximum_fusion.refs_1_), channel_id=1, source_target_pairs={{0,2},{2,0},{4,6},{6,4},{8,10},{10,8},{12,14},{14,12},{16,18},{18,... | collective-permute-start | bytes 24584 | tf_op jit(solution)/shard_map/ppermute | solution.py:19
  21.8 0.1 collective-permute-done.5.refs_3_
  21.9 2.9 %collective-permute-done.4.refs_2_ = f32[4,2,256]{2,1,0:T(2,128)S(1)} collective-permute-done((f32[4,2,256]{2,1,0:T(2,128)S(1)}, f32[4,2,256]{2,1,0:T(2,128)S(1)}, u32[]{:S(2)}, u32[]{:S(2)}) %collective-permute-start.4) | collective-permute-done | bytes 8224 | tf_op jit(solution)/shard_map/ppermute | solution.py:19
  24.8 0.0 collective-permute-done.9.refs_10_
  24.8 0.0 collective-permute-done.7.refs_8_
  24.8 0.0 collective-permute-done.8.refs_9_
  24.8 0.0 copy-start.1
  24.9 1.1 %copy-done.1 = bf16[4,4,96,256]{3,2,1,0:T(8,128)(2,1)S(1)} copy-done((bf16[4,4,96,256]{3,2,1,0:T(8,128)(2,1)S(1)}, bf16[4,4,96,256]{3,2,1,0:T(8,128)(2,1)}, u32[]{:S(2)}) %copy-start.1) | copy-done | bytes 786456
  26.0 0.0 copy-start.2
  26.0 2.0 %copy-done.2 = bf16[3,3,3,256,256]{4,3,2,1,0:T(8,128)(2,1)S(1)} copy-done((bf16[3,3,3,256,256]{4,3,2,1,0:T(8,128)(2,1)S(1)}, bf16[3,3,3,256,256]{4,3,2,1,0:T(8,128)(2,1)}, u32[]{:S(2)}) %copy-start.2) | copy-done | bytes 3538968
  28.0 0.0 copy-start.4
  28.0 0.7 %copy-done.4 = f32[256]{0:T(256)S(1)} copy-done((f32[256]{0:T(256)S(1)}, f32[256]{0:T(256)}, u32[]{:S(2)}) %copy-start.4) | copy-done | bytes 1048
  28.7 0.0 copy-start.5
  28.7 0.7 %copy-done.5 = f32[256]{0:T(256)S(1)} copy-done((f32[256]{0:T(256)S(1)}, f32[256]{0:T(256)}, u32[]{:S(2)}) %copy-start.5) | copy-done | bytes 1048
  29.3 0.0 copy-start.8
  29.3 0.7 copy-done.8
  30.0 0.0 copy-start.3
  30.0 0.0 copy-start.6
  30.0 0.0 copy-start.7
  30.0 7.7 %shard_map.83 = (bf16[4,4,96,256]{3,2,1,0:T(8,128)(2,1)S(1)}, f32[2,256]{1,0:T(2,128)S(1)}, bf16[4,1,96,256]{3,2,1,0:T(8,128)(2,1)S(1)}) custom-call(s32[16]{0:T(128)S(1)} %copy-done.8, f32[4,2,256]{2,1,0:T(2,128)S(1)} %pad_maximum_fusion.refs_1_, f32[4,2,256]{2,1,0:T(2,128)S(1)} %collective-permute-done.4.refs_2_, ...), custom_call_target="tpu_custom_call" | custom-call | flops 5435817984 | bytes 6684672 | tf_op jit(solution)/shard_map/pallas_call | solution.py:263
  37.7 0.7 %collective-permute-start.18 = (bf16[2,4,96,256]{3,2,1,0:T(8,128)(2,1)S(1)}, bf16[2,4,96,256]{3,2,1,0:T(8,128)(2,1)S(1)}, u32[]{:S(2)}, u32[]{:S(2)}) collective-permute-start(bf16[2,4,96,256]{3,2,1,0:T(8,128)(2,1)S(1)} %slice.14), channel_id=1, source_target_pairs={{0,2},{2,4},{4,6},{6,8},{8,10},{10,12},{12,14},{14,16},{16,18},{18... | collective-permute-start | bytes 1179656 | tf_op jit(solution)/shard_map/ppermute | solution.py:51
  38.5 0.0 collective-permute-start.10
  38.5 0.5 collective-permute-start.17
  39.0 0.6 collective-permute-done.10
  39.6 1.5 %collective-permute-start.13 = (f32[1,2,256]{2,1,0:T(2,128)S(1)}, f32[1,2,256]{2,1,0:T(2,128)S(1)}, u32[]{:S(2)}, u32[]{:S(2)}) collective-permute-start(f32[1,2,256]{2,1,0:T(2,128)S(1)} %add_bitcast_fusion), channel_id=1, source_target_pairs={{0,24},{2,26},{4,28},{6,30},{8,16},{10,18},{12,20},{14,22},{16,8},... | collective-permute-start | bytes 6152 | tf_op jit(solution)/shard_map/ppermute | solution.py:19
  41.1 0.4 collective-permute-start.12
  41.5 2.5 %collective-permute-start.11 = (f32[1,2,256]{2,1,0:T(2,128)S(1)}, f32[1,2,256]{2,1,0:T(2,128)S(1)}, u32[]{:S(2)}, u32[]{:S(2)}) collective-permute-start(f32[1,2,256]{2,1,0:T(2,128)S(1)} %add_bitcast_fusion), channel_id=1, source_target_pairs={{0,8},{2,10},{4,12},{6,14},{8,0},{10,2},{12,4},{14,6},{16,24},{18,... | collective-permute-start | bytes 6152 | tf_op jit(solution)/shard_map/ppermute | solution.py:19
  44.0 1.0 %collective-permute-done.13 = f32[1,2,256]{2,1,0:T(2,128)S(1)} collective-permute-done((f32[1,2,256]{2,1,0:T(2,128)S(1)}, f32[1,2,256]{2,1,0:T(2,128)S(1)}, u32[]{:S(2)}, u32[]{:S(2)}) %collective-permute-start.13) | collective-permute-done | bytes 2080 | tf_op jit(solution)/shard_map/ppermute | solution.py:19
  45.0 0.1 collective-permute-start.19
  45.1 0.6 collective-permute-done.12
  45.6 0.0 collective-permute-done.11
  45.6 5.6 %collective-permute-start.16 = (f32[4,2,256]{2,1,0:T(2,128)S(1)}, f32[4,2,256]{2,1,0:T(2,128)S(1)}, u32[]{:S(2)}, u32[]{:S(2)}) collective-permute-start(f32[4,2,256]{2,1,0:T(2,128)S(1)} %pad_maximum_fusion.1.refs_1_), channel_id=1, source_target_pairs={{0,6},{2,4},{4,2},{6,0},{8,14},{10,12},{12,10},{14,8},{16,22},{18,... | collective-permute-start | bytes 24584 | tf_op jit(solution)/shard_map/ppermute | solution.py:19
  51.3 0.0 collective-permute-start.15
  51.3 2.5 %collective-permute-done.16.refs_4_ = f32[4,2,256]{2,1,0:T(2,128)S(1)} collective-permute-done((f32[4,2,256]{2,1,0:T(2,128)S(1)}, f32[4,2,256]{2,1,0:T(2,128)S(1)}, u32[]{:S(2)}, u32[]{:S(2)}) %collective-permute-start.16) | collective-permute-done | bytes 8224 | tf_op jit(solution)/shard_map/ppermute | solution.py:19
  53.8 0.0 collective-permute-start.14
  53.8 1.1 %collective-permute-done.15.refs_3_ = f32[4,2,256]{2,1,0:T(2,128)S(1)} collective-permute-done((f32[4,2,256]{2,1,0:T(2,128)S(1)}, f32[4,2,256]{2,1,0:T(2,128)S(1)}, u32[]{:S(2)}, u32[]{:S(2)}) %collective-permute-start.15) | collective-permute-done | bytes 8224 | tf_op jit(solution)/shard_map/ppermute | solution.py:19
  54.9 2.5 %collective-permute-done.14.refs_2_ = f32[4,2,256]{2,1,0:T(2,128)S(1)} collective-permute-done((f32[4,2,256]{2,1,0:T(2,128)S(1)}, f32[4,2,256]{2,1,0:T(2,128)S(1)}, u32[]{:S(2)}, u32[]{:S(2)}) %collective-permute-start.14) | collective-permute-done | bytes 8224 | tf_op jit(solution)/shard_map/ppermute | solution.py:19
  57.5 0.0 collective-permute-done.19.refs_10_
  57.5 0.0 collective-permute-done.17.refs_8_
  57.5 0.0 collective-permute-done.18.refs_9_
  57.5 0.0 copy-done.3
  57.5 0.0 copy-done.6
  57.5 0.0 copy-done.7
  57.5 8.8 %shard_map.84 = f32[4,4,96,256]{3,2,1,0:T(8,128)} custom-call(s32[16]{0:T(128)S(1)} %copy-done.8, f32[4,2,256]{2,1,0:T(2,128)S(1)} %pad_maximum_fusion.1.refs_1_, f32[4,2,256]{2,1,0:T(2,128)S(1)} %collective-permute-done.14.refs_2_, f32[4,2,256]{2,1,0:T(2,128)S(1)} %collective-permute-done.15.refs_3_, f32[4,2,256]{2,1,0:T(2,128)S(1)} %collective-permute-done.16.refs_4_, ...), custom_call_target="tpu_custom_call" | custom-call | flops 5435817984 | bytes 6684672 | tf_op jit(solution)/shard_map/pallas_call | solution.py:263
  (7 shorter events, 0.1 us)
Async XLA Ops:
  1.0 23.8 %collective-permute-start.8 = (bf16[2,4,96,256]{3,2,1,0:T(8,128)(2,1)S(1)}, bf16[2,4,96,256]{3,2,1,0:T(8,128)(2,1)S(1)}, u32[]{:S(2)}, u32[]{:S(2)}) collective-permute-start(bf16[2,4,96,256]{3,2,1,0:T(8,128)(2,1)S(1)} %slice.12), channel_id=1, source_target_pairs={{0,2},{2,4},{4,6},{6,8},{8,10},{10,12},{12,14},{14,16},{16,18},{18... | collective-permute-start | bytes 1179656 | tf_op jit(solution)/shard_map/ppermute | solution.py:51
  4.0 1.1 %copy-start = (bf16[4,4,96,256]{3,2,1,0:T(8,128)(2,1)S(1)}, bf16[4,4,96,256]{3,2,1,0:T(8,128)(2,1)}, u32[]{:S(2)}) copy-start(bf16[4,4,96,256]{3,2,1,0:T(8,128)(2,1)} %refs_12_.1) | copy-start | bytes 2359300
  6.3 1.2 %collective-permute-start = (f32[2,256]{1,0:T(2,128)S(1)}, f32[2,256]{1,0:T(2,128)S(1)}, u32[]{:S(2)}, u32[]{:S(2)}) collective-permute-start(f32[2,256]{1,0:T(2,128)S(1)} %get-tuple-element.10), channel_id=1, source_target_pairs={{0,1},{1,0},{2,3},{3,2},{4,5},{5,4},{6,7},{7,6},{8,9},{9,8},{10,11... | collective-permute-start | bytes 6152 | tf_op jit(solution)/shard_map/ppermute | solution.py:19
  6.4 18.4 %collective-permute-start.7 = (bf16[4,1,96,256]{3,2,1,0:T(8,128)(2,1)S(1)}, bf16[4,1,96,256]{3,2,1,0:T(8,128)(2,1)S(1)}, u32[]{:S(2)}, u32[]{:S(2)}) collective-permute-start(bf16[4,1,96,256]{3,2,1,0:T(8,128)(2,1)S(1)} %get-tuple-element.11), channel_id=1, source_target_pairs={{0,1},{1,0},{2,3},{3,2},{4,5},{5,4},{6,7},{7,6},{8,9},{9,8},{10,11... | collective-permute-start | bytes 589832 | tf_op jit(solution)/shard_map/ppermute | solution.py:19
  7.6 5.4 %collective-permute-start.3 = (f32[1,2,256]{2,1,0:T(2,128)S(1)}, f32[1,2,256]{2,1,0:T(2,128)S(1)}, u32[]{:S(2)}, u32[]{:S(2)}) collective-permute-start(f32[1,2,256]{2,1,0:T(2,128)S(1)} %add_bitcast_fusion.1), channel_id=1, source_target_pairs={{0,24},{2,26},{4,28},{6,30},{8,16},{10,18},{12,20},{14,22},{16,8},... | collective-permute-start | bytes 6152 | tf_op jit(solution)/shard_map/ppermute | solution.py:19
  11.2 4.5 %collective-permute-start.2 = (f32[1,2,256]{2,1,0:T(2,128)S(1)}, f32[1,2,256]{2,1,0:T(2,128)S(1)}, u32[]{:S(2)}, u32[]{:S(2)}) collective-permute-start(f32[1,2,256]{2,1,0:T(2,128)S(1)} %add_bitcast_fusion.1), channel_id=1, source_target_pairs={{0,16},{2,18},{4,20},{6,22},{8,24},{10,26},{12,28},{14,30},{16,0},... | collective-permute-start | bytes 6152 | tf_op jit(solution)/shard_map/ppermute | solution.py:19
  11.2 4.5 %collective-permute-start.1 = (f32[1,2,256]{2,1,0:T(2,128)S(1)}, f32[1,2,256]{2,1,0:T(2,128)S(1)}, u32[]{:S(2)}, u32[]{:S(2)}) collective-permute-start(f32[1,2,256]{2,1,0:T(2,128)S(1)} %add_bitcast_fusion.1), channel_id=1, source_target_pairs={{0,8},{2,10},{4,12},{6,14},{8,0},{10,2},{12,4},{14,6},{16,24},{18,... | collective-permute-start | bytes 6152 | tf_op jit(solution)/shard_map/ppermute | solution.py:19
  13.0 11.9 %collective-permute-start.9 = (bf16[2,1,96,256]{3,2,1,0:T(8,128)(2,1)S(1)}, bf16[2,1,96,256]{3,2,1,0:T(8,128)(2,1)S(1)}, u32[]{:S(2)}, u32[]{:S(2)}) collective-permute-start(bf16[2,1,96,256]{3,2,1,0:T(8,128)(2,1)S(1)} %slice.13), channel_id=1, source_target_pairs={{0,3},{1,2},{2,5},{3,4},{4,7},{5,6},{6,9},{7,8},{8,11},{9,10},{10,... | collective-permute-start | bytes 294920 | tf_op jit(solution)/shard_map/ppermute | solution.py:61
  15.7 5.5 %collective-permute-start.6 = (f32[4,2,256]{2,1,0:T(2,128)S(1)}, f32[4,2,256]{2,1,0:T(2,128)S(1)}, u32[]{:S(2)}, u32[]{:S(2)}) collective-permute-start(f32[4,2,256]{2,1,0:T(2,128)S(1)} %pad_maximum_fusion.refs_1_), channel_id=1, source_target_pairs={{0,6},{2,4},{4,2},{6,0},{8,14},{10,12},{12,10},{14,8},{16,22},{18,... | collective-permute-start | bytes 24584 | tf_op jit(solution)/shard_map/ppermute | solution.py:19
  18.0 4.0 %collective-permute-start.5 = (f32[4,2,256]{2,1,0:T(2,128)S(1)}, f32[4,2,256]{2,1,0:T(2,128)S(1)}, u32[]{:S(2)}, u32[]{:S(2)}) collective-permute-start(f32[4,2,256]{2,1,0:T(2,128)S(1)} %pad_maximum_fusion.refs_1_), channel_id=1, source_target_pairs={{0,4},{2,6},{4,0},{6,2},{8,12},{10,14},{12,8},{14,10},{16,20},{18,... | collective-permute-start | bytes 24584 | tf_op jit(solution)/shard_map/ppermute | solution.py:19
  21.2 3.7 %collective-permute-start.4 = (f32[4,2,256]{2,1,0:T(2,128)S(1)}, f32[4,2,256]{2,1,0:T(2,128)S(1)}, u32[]{:S(2)}, u32[]{:S(2)}) collective-permute-start(f32[4,2,256]{2,1,0:T(2,128)S(1)} %pad_maximum_fusion.refs_1_), channel_id=1, source_target_pairs={{0,2},{2,0},{4,6},{6,4},{8,10},{10,8},{12,14},{14,12},{16,18},{18,... | collective-permute-start | bytes 24584 | tf_op jit(solution)/shard_map/ppermute | solution.py:19
  24.8 1.1 %copy-start.1 = (bf16[4,4,96,256]{3,2,1,0:T(8,128)(2,1)S(1)}, bf16[4,4,96,256]{3,2,1,0:T(8,128)(2,1)}, u32[]{:S(2)}) copy-start(bf16[4,4,96,256]{3,2,1,0:T(8,128)(2,1)} %refs_12_.1) | copy-start | bytes 2359300
  26.0 2.0 %copy-start.2 = (bf16[3,3,3,256,256]{4,3,2,1,0:T(8,128)(2,1)S(1)}, bf16[3,3,3,256,256]{4,3,2,1,0:T(8,128)(2,1)}, u32[]{:S(2)}) copy-start(bf16[3,3,3,256,256]{4,3,2,1,0:T(8,128)(2,1)} %refs_11_.2) | copy-start | bytes 10616836
  28.0 0.7 %copy-start.4 = (f32[256]{0:T(256)S(1)}, f32[256]{0:T(256)}, u32[]{:S(2)}) copy-start(f32[256]{0:T(256)} %param.10) | copy-start | bytes 3076
  28.7 0.7 %copy-start.5 = (f32[256]{0:T(256)S(1)}, f32[256]{0:T(256)}, u32[]{:S(2)}) copy-start(f32[256]{0:T(256)} %param.11) | copy-start | bytes 3076
  29.3 0.7 copy-start.8
  30.0 27.5 %copy-start.3 = (bf16[3,3,3,256,256]{4,3,2,1,0:T(8,128)(2,1)S(1)}, bf16[3,3,3,256,256]{4,3,2,1,0:T(8,128)(2,1)}, u32[]{:S(2)}) copy-start(bf16[3,3,3,256,256]{4,3,2,1,0:T(8,128)(2,1)} %refs_11_.3) | copy-start | bytes 10616836
  30.0 27.5 %copy-start.6 = (f32[256]{0:T(256)S(1)}, f32[256]{0:T(256)}, u32[]{:S(2)}) copy-start(f32[256]{0:T(256)} %param.13) | copy-start | bytes 3076
  30.0 27.5 %copy-start.7 = (f32[256]{0:T(256)S(1)}, f32[256]{0:T(256)}, u32[]{:S(2)}) copy-start(f32[256]{0:T(256)} %param.14) | copy-start | bytes 3076
  37.7 19.7 %collective-permute-start.18 = (bf16[2,4,96,256]{3,2,1,0:T(8,128)(2,1)S(1)}, bf16[2,4,96,256]{3,2,1,0:T(8,128)(2,1)S(1)}, u32[]{:S(2)}, u32[]{:S(2)}) collective-permute-start(bf16[2,4,96,256]{3,2,1,0:T(8,128)(2,1)S(1)} %slice.14), channel_id=1, source_target_pairs={{0,2},{2,4},{4,6},{6,8},{8,10},{10,12},{12,14},{14,16},{16,18},{18... | collective-permute-start | bytes 1179656 | tf_op jit(solution)/shard_map/ppermute | solution.py:51
  38.5 1.2 %collective-permute-start.10 = (f32[2,256]{1,0:T(2,128)S(1)}, f32[2,256]{1,0:T(2,128)S(1)}, u32[]{:S(2)}, u32[]{:S(2)}) collective-permute-start(f32[2,256]{1,0:T(2,128)S(1)} %get-tuple-element.12), channel_id=1, source_target_pairs={{0,1},{1,0},{2,3},{3,2},{4,5},{5,4},{6,7},{7,6},{8,9},{9,8},{10,11... | collective-permute-start | bytes 6152 | tf_op jit(solution)/shard_map/ppermute | solution.py:19
  38.5 19.0 %collective-permute-start.17 = (bf16[4,1,96,256]{3,2,1,0:T(8,128)(2,1)S(1)}, bf16[4,1,96,256]{3,2,1,0:T(8,128)(2,1)S(1)}, u32[]{:S(2)}, u32[]{:S(2)}) collective-permute-start(bf16[4,1,96,256]{3,2,1,0:T(8,128)(2,1)S(1)} %get-tuple-element.14), channel_id=1, source_target_pairs={{0,1},{1,0},{2,3},{3,2},{4,5},{5,4},{6,7},{7,6},{8,9},{9,8},{10,11... | collective-permute-start | bytes 589832 | tf_op jit(solution)/shard_map/ppermute | solution.py:19
  39.6 5.4 %collective-permute-start.13 = (f32[1,2,256]{2,1,0:T(2,128)S(1)}, f32[1,2,256]{2,1,0:T(2,128)S(1)}, u32[]{:S(2)}, u32[]{:S(2)}) collective-permute-start(f32[1,2,256]{2,1,0:T(2,128)S(1)} %add_bitcast_fusion), channel_id=1, source_target_pairs={{0,24},{2,26},{4,28},{6,30},{8,16},{10,18},{12,20},{14,22},{16,8},... | collective-permute-start | bytes 6152 | tf_op jit(solution)/shard_map/ppermute | solution.py:19
  41.1 4.5 %collective-permute-start.12 = (f32[1,2,256]{2,1,0:T(2,128)S(1)}, f32[1,2,256]{2,1,0:T(2,128)S(1)}, u32[]{:S(2)}, u32[]{:S(2)}) collective-permute-start(f32[1,2,256]{2,1,0:T(2,128)S(1)} %add_bitcast_fusion), channel_id=1, source_target_pairs={{0,16},{2,18},{4,20},{6,22},{8,24},{10,26},{12,28},{14,30},{16,0},... | collective-permute-start | bytes 6152 | tf_op jit(solution)/shard_map/ppermute | solution.py:19
  41.5 4.1 %collective-permute-start.11 = (f32[1,2,256]{2,1,0:T(2,128)S(1)}, f32[1,2,256]{2,1,0:T(2,128)S(1)}, u32[]{:S(2)}, u32[]{:S(2)}) collective-permute-start(f32[1,2,256]{2,1,0:T(2,128)S(1)} %add_bitcast_fusion), channel_id=1, source_target_pairs={{0,8},{2,10},{4,12},{6,14},{8,0},{10,2},{12,4},{14,6},{16,24},{18,... | collective-permute-start | bytes 6152 | tf_op jit(solution)/shard_map/ppermute | solution.py:19
  45.0 12.5 %collective-permute-start.19 = (bf16[2,1,96,256]{3,2,1,0:T(8,128)(2,1)S(1)}, bf16[2,1,96,256]{3,2,1,0:T(8,128)(2,1)S(1)}, u32[]{:S(2)}, u32[]{:S(2)}) collective-permute-start(bf16[2,1,96,256]{3,2,1,0:T(8,128)(2,1)S(1)} %slice.15), channel_id=1, source_target_pairs={{0,3},{1,2},{2,5},{3,4},{4,7},{5,6},{6,9},{7,8},{8,11},{9,10},{10,... | collective-permute-start | bytes 294920 | tf_op jit(solution)/shard_map/ppermute | solution.py:61
  45.6 8.2 %collective-permute-start.16 = (f32[4,2,256]{2,1,0:T(2,128)S(1)}, f32[4,2,256]{2,1,0:T(2,128)S(1)}, u32[]{:S(2)}, u32[]{:S(2)}) collective-permute-start(f32[4,2,256]{2,1,0:T(2,128)S(1)} %pad_maximum_fusion.1.refs_1_), channel_id=1, source_target_pairs={{0,6},{2,4},{4,2},{6,0},{8,14},{10,12},{12,10},{14,8},{16,22},{18,... | collective-permute-start | bytes 24584 | tf_op jit(solution)/shard_map/ppermute | solution.py:19
  51.3 3.7 %collective-permute-start.15 = (f32[4,2,256]{2,1,0:T(2,128)S(1)}, f32[4,2,256]{2,1,0:T(2,128)S(1)}, u32[]{:S(2)}, u32[]{:S(2)}) collective-permute-start(f32[4,2,256]{2,1,0:T(2,128)S(1)} %pad_maximum_fusion.1.refs_1_), channel_id=1, source_target_pairs={{0,4},{2,6},{4,0},{6,2},{8,12},{10,14},{12,8},{14,10},{16,20},{18,... | collective-permute-start | bytes 24584 | tf_op jit(solution)/shard_map/ppermute | solution.py:19
  53.8 3.7 %collective-permute-start.14 = (f32[4,2,256]{2,1,0:T(2,128)S(1)}, f32[4,2,256]{2,1,0:T(2,128)S(1)}, u32[]{:S(2)}, u32[]{:S(2)}) collective-permute-start(f32[4,2,256]{2,1,0:T(2,128)S(1)} %pad_maximum_fusion.1.refs_1_), channel_id=1, source_target_pairs={{0,2},{2,0},{4,6},{6,4},{8,10},{10,8},{12,14},{14,12},{16,18},{18,... | collective-permute-start | bytes 24584 | tf_op jit(solution)/shard_map/ppermute | solution.py:19

commit v6 on v3

v6 whole, which is shorter than its diff:
```python
import functools

import jax
import jax.numpy as jnp
from jax import lax
from jax.experimental import pallas as pl
from jax.experimental.pallas import tpu as pltpu
from jax.sharding import PartitionSpec as P

GROUPS = 32
TAIL = 2
F32, BF16 = jnp.float32, jnp.bfloat16


def vmem_params():
    return pltpu.CompilerParams(vmem_limit_bytes=32 << 20)


def shaped(shape, dtype=BF16):
    return jax.ShapeDtypeStruct(tuple(shape), dtype)


def in_hbm(value):
    return pltpu.with_memory_space_constraint(value, pltpu.HBM)


VMEM = pl.BlockSpec(memory_space=pltpu.VMEM)
ANYWHERE = pl.BlockSpec(memory_space=pl.ANY)


def traded(value, axis, mask):
    return lax.ppermute(value, axis, [(i, i ^ mask) for i in range(lax.axis_size(axis))])


def shifted(value, axis, step):
    peers = lax.axis_size(axis)
    return lax.ppermute(value, axis, [(i, (i + step) % peers) for i in range(peers)])


def slab_table(stats):
    slabs, places = lax.axis_size("tm"), lax.axis_size("space")
    total = stats + traded(stats, "space", 1) if places == 2 else lax.psum(stats, "space")
    copies = jnp.broadcast_to(total, (slabs, total.shape[1]))
    return total, lax.all_to_all(copies, "tm", 0, 0, tiled=True)


def row_halo(edges):
    if lax.axis_size("space") == 2:
        return [traded(edges[0], "space", 1)]
    top, bottom = edges
    return [shifted(bottom, "space", 1), shifted(top, "space", -1)]


def edges_of(frames):
    rows = frames.shape[1]
    if lax.axis_size("space") == 2:
        return [lax.dynamic_slice_in_dim(frames, (rows - 1) * (1 - lax.axis_index("space")), 1, axis=1)]
    return [frames[:, :1], frames[:, rows - 1 :]]


def slab_halo(tail, after=None):
    before = shifted(tail, "tm", 1)
    if after is not None:
        before, after = lax.optimization_barrier((before, after))
    return before, row_halo(edges_of(before)), after


def edge_shapes(frames, count):
    shape = (count, 1) + frames.shape[2:]
    return [shaped(shape)] * (1 if lax.axis_size("space") == 2 else 2)


def send_rows(source, frame, edges):
    rows = source.shape[1]
    if len(edges) == 1:
        edges[0][frame, 0] = jnp.where(lax.axis_index("space") == 0, source[frame, rows - 1], source[frame, 0])
    else:
        edges[0][frame, 0] = source[frame, 0]
        edges[1][frame, 0] = source[frame, rows - 1]


def add_stats(sums, values):
    width = values.shape[1]
    return (
        sums[0] + jnp.sum(values.reshape(-1, 8, width), axis=0),
        sums[1] + jnp.sum((values * values).reshape(-1, 8, width), axis=0),
    )


def no_stats(width):
    return jnp.zeros((8, width), F32), jnp.zeros((8, width), F32)


def store_stats(stats, sums, base=None):
    width = sums[0].shape[1]
    for k in range(2):
        part = jnp.sum(sums[k], axis=0, keepdims=True)
        stats[:, k * width : (k + 1) * width] = part if base is None else part + base[:, k * width : (k + 1) * width]


def entry_kernel(slabs, *refs):
    feats_hbm, clips_hbm = refs[:2]
    params_hbm = refs[2:6]
    frames, tail, stats, aux = refs[6:10]
    edges = refs[10:-4]
    params, clips, sems, frame_sems = refs[-4:]
    n_frames, n_rows, cols, width = frames.shape
    loads = [pltpu.make_async_copy(feats_hbm.at[f], frames.at[f], frame_sems.at[f]) for f in range(n_frames)]
    clip_load = pltpu.make_async_copy(clips_hbm, clips, sems.at[0])
    tail_load = pltpu.make_async_copy(feats_hbm.at[pl.ds(n_frames - TAIL, TAIL)], tail, sems.at[1])
    param_loads = [pltpu.make_async_copy(p, params.at[k], sems.at[2 + k]) for k, p in enumerate(params_hbm)]
    for copy in [*loads, clip_load, tail_load, *param_loads]:
        copy.start()
    sums = no_stats(width)
    for frame in range(n_frames):
        loads[frame].wait()
        for row in range(n_rows):
            sums = add_stats(sums, frames[frame, row].astype(F32))
        send_rows(frames, frame, edges)
    store_stats(stats, sums)
    clip_load.wait()
    own = lax.axis_index("tm")
    own_clip = clips[own]
    slabs_in = jnp.int32(0)
    for slab in range(slabs):
        same = (clips[slab] == own_clip).astype(jnp.int32)
        slabs_in = slabs_in + same
        aux[slab : slab + 1] = jnp.full((1, width), same.astype(F32), F32)
    starting = jnp.logical_or(own == 0, clips[jnp.maximum(own - 1, 0)] != own_clip)
    aux[slabs : slabs + 1] = jnp.full((1, width), starting.astype(F32), F32)
    per_slab = n_frames * n_rows * cols * width // GROUPS * lax.axis_size("space")
    aux[slabs + 1 : slabs + 2] = jnp.full((1, width), slabs_in.astype(F32) * float(per_slab), F32)
    for k, copy in enumerate(param_loads):
        copy.wait()
        aux[slabs + 2 + k : slabs + 3 + k] = params[k]
    tail_load.wait()


def entry_call(feats, clip_ids, params):
    slabs = lax.axis_size("tm")
    n_frames, width = feats.shape[0], feats.shape[3]
    outs = [shaped(feats.shape), shaped((TAIL,) + feats.shape[1:]), shaped((1, 2 * width), F32), shaped((slabs + 8, width), F32)]
    outs += edge_shapes(feats, n_frames)
    frames, tail, stats, aux, *edges = pl.pallas_call(
        functools.partial(entry_kernel, slabs),
        out_shape=outs,
        in_specs=[ANYWHERE] * 6,
        out_specs=[VMEM] * len(outs),
        scratch_shapes=[
            pltpu.VMEM((4, 1, width), F32),
            pltpu.SMEM(clip_ids.shape, jnp.int32),
            pltpu.SemaphoreType.DMA((6,)),
            pltpu.SemaphoreType.DMA((n_frames,)),
        ],
        compiler_params=vmem_params(),
        cost_estimate=pl.CostEstimate(flops=4 * feats.size, bytes_accessed=4 * feats.size, transcendentals=0),
    )(*[in_hbm(x) for x in (feats, clip_ids, *[p[None] for p in params])])
    return frames, tail, stats, aux, edges


def load_kernel(kernel_hbm, after, taps, sem):
    copy = pltpu.make_async_copy(kernel_hbm, taps, sem)
    copy.start()
    copy.wait()


def load_call(kernel, after):
    return pl.pallas_call(
        load_kernel,
        out_shape=shaped(kernel.shape),
        in_specs=[ANYWHERE, ANYWHERE],
        out_specs=VMEM,
        scratch_shapes=[pltpu.SemaphoreType.DMA],
        compiler_params=vmem_params(),
        cost_estimate=pl.CostEstimate(flops=0, bytes_accessed=4 * kernel.size, transcendentals=0),
    )(in_hbm(kernel), after)


def group_total(values):
    width = values.shape[-1]
    lane = lax.broadcasted_iota(jnp.int32, values.shape, 1)
    step = 1
    while step < width // GROUPS:
        upper = pltpu.roll(values, step, 1)
        lower = pltpu.roll(values, width - step, 1)
        values = values + jnp.where((lane & step) != 0, upper, lower)
        step *= 2
    return values


def half_affine(table, aux, which):
    slabs = table.shape[0]
    width = aux.shape[1]
    mask = aux[:slabs]
    sums = [jnp.sum(table[:, k * width : (k + 1) * width] * mask, axis=0, keepdims=True) for k in range(2)]
    grouped = group_total(jnp.concatenate(sums, axis=0))
    count = aux[slabs + 1 : slabs + 2]
    gain = aux[slabs + 2 + 2 * which : slabs + 3 + 2 * which]
    shift = aux[slabs + 3 + 2 * which : slabs + 4 + 2 * which]
    mean = grouped[0:1] / count
    variance = grouped[1:2] / count - mean * mean
    scale = lax.rsqrt(variance + 1e-06) * gain
    return 0.5 * scale, 0.5 * (shift - mean * scale)


def normed(raw, affine):
    half = raw.astype(F32) * affine[0] + affine[1]
    return (half * jnp.tanh(half) + half).astype(BF16)


def extended_row(frames, sides, frame, row):
    n_rows = frames.shape[1]
    inner = frames[frame, min(max(row - 1, 0), n_rows - 1)]
    if 0 < row <= n_rows:
        return inner
    place, places = lax.axis_index("space"), lax.axis_size("space")
    side = sides[0 if row == 0 else -1]
    return jnp.where(place == (0 if row == 0 else places - 1), inner, side[frame, 0])


def conv_rows(planes, taps):
    ref, index = planes[0]
    n_rows, cols, width = ref.shape[1] - 2, ref.shape[2], ref.shape[3]
    lhs = jnp.concatenate(
        [ref[index, j : j + n_rows].reshape(n_rows * cols, width) for ref, index in planes for j in range(3)], axis=1
    )
    column = lax.broadcasted_iota(jnp.int32, (cols, width), 0)
    sums = []
    for l in range(3):
        rhs = jnp.concatenate([taps[i, j, l] for i in range(3) for j in range(3)], axis=0)
        sums.append(jnp.dot(lhs, rhs, preferred_element_type=F32))
    for row in range(n_rows):
        left, mid, right = (s[row * cols : (row + 1) * cols] for s in sums)
        left = jnp.where(column == 0, left, pltpu.roll(left, 1, 0))
        right = jnp.where(column == cols - 1, right, pltpu.roll(right, cols - 1, 0))
        yield row, left + mid + right


def put_hidden(hidden, frame, row, value, sums):
    rounded = value.astype(BF16)
    hidden[frame, row] = rounded
    return add_stats(sums, rounded.astype(F32))


def late_kernel(n_sides, aux, table, frames, *refs):
    sides, taps = refs[:n_sides], refs[n_sides]
    hidden, act_low, stats, affine_out, *edges, act_high = refs[n_sides + 1 :]
    n_frames = frames.shape[0]
    low = act_low.shape[0]
    affine = half_affine(table, aux, 0)
    for k in range(2):
        affine_out[k : k + 1] = affine[k]
    planes = [(act_low, f) for f in range(low)] + [(act_high, f) for f in range(n_frames - low)]
    for frame, (act, index) in enumerate(planes):
        for row in range(frames.shape[1] + 2):
            act[index, row] = normed(extended_row(frames, sides, frame, row), affine)
    sums = no_stats(frames.shape[3])
    for frame in range(n_frames - 2):
        for row, value in conv_rows(planes[frame : frame + 3], taps):
            sums = put_hidden(hidden, frame, row, value, sums)
        send_rows(hidden, frame, edges)
    store_stats(stats, sums)


def early_kernel(n_sides, aux, before, *refs):
    corners, (act_low, affine_in, stats_in, taps) = refs[:n_sides], refs[n_sides : n_sides + 4]
    hidden, stats, *edges, act_before = refs[n_sides + 4 :]
    slabs = aux.shape[0] - 8
    starting = aux[slabs : slabs + 1] != 0.0
    affine = affine_in[0:1], affine_in[1:2]
    for frame in range(2):
        for row in range(before.shape[1] + 2):
            value = normed(extended_row(before, corners, frame, row), affine).astype(F32)
            act_before[frame, row] = jnp.where(starting, act_low[0, row].astype(F32), value).astype(BF16)
    planes = [(act_before, 0), (act_before, 1)] + [(act_low, f) for f in range(act_low.shape[0])]
    sums = no_stats(before.shape[3])
    for frame in range(2):
        for row, value in conv_rows(planes[frame : frame + 3], taps):
            sums = put_hidden(hidden, frame, row, value, sums)
        send_rows(hidden, frame, edges)
    store_stats(stats, sums, stats_in)


def last_kernel(n_sides, aux, table, early, late, *refs):
    sides_early, sides_late = refs[:n_sides], refs[n_sides : 2 * n_sides]
    before, *corners = refs[2 * n_sides : 3 * n_sides + 1]
    taps, feats, out, act = refs[3 * n_sides + 1 :]
    slabs = aux.shape[0] - 8
    starting = aux[slabs : slabs + 1] != 0.0
    affine = half_affine(table, aux, 1)
    n_frames, n_rows = out.shape[:2]

    def fill(frame):
        for row in range(n_rows + 2):
            if frame < 2:
                value = normed(extended_row(before, corners, frame, row), affine).astype(F32)
                act[frame, row] = jnp.where(starting, act[2, row].astype(F32), value).astype(BF16)
            elif frame < 4:
                act[frame, row] = normed(extended_row(early, sides_early, frame - 2, row), affine)
            else:
                act[frame, row] = normed(extended_row(late, sides_late, frame - 4, row), affine)

    for frame in range(2, n_frames + 2):
        fill(frame)
    for frame in list(range(2, n_frames)) + [0, 1]:
        if frame < 2:
            fill(frame)
        if frame == 0:
            fill(1)
        for row, value in conv_rows([(act, frame + i) for i in range(3)], taps):
            out[frame, row] = feats[frame, row].astype(F32) + value


def call(kernel, outs, scratch, frames, *operands):
    return pl.pallas_call(
        kernel,
        out_shape=outs,
        in_specs=[VMEM] * len(operands),
        out_specs=[VMEM] * len(outs) if isinstance(outs, list) else VMEM,
        scratch_shapes=scratch,
        compiler_params=vmem_params(),
        cost_estimate=pl.CostEstimate(flops=54 * frames * 384 * 65536, bytes_accessed=1 << 20, transcendentals=1 << 20),
    )(*operands)


def on_device(feats, clip_ids, gain_one, shift_one, kernel_one, gain_two, shift_two, kernel_two):
    n_frames, n_rows, cols, width = feats.shape
    frames, tail, stats, aux, edges = entry_call(feats, clip_ids, (gain_one, shift_one, gain_two, shift_two))
    before, corners, _ = slab_halo(tail)
    total, table = slab_table(stats)
    sides = row_halo(edges)
    taps = load_call(kernel_one, total)
    n_sides = len(sides)
    plane = (n_rows + 2, cols, width)
    late = n_frames - 2
    hidden_late, act_low, stats, affine, *edges = call(
        functools.partial(late_kernel, n_sides),
        [shaped((late, n_rows, cols, width)), shaped((2,) + plane), shaped((1, 2 * width), F32), shaped((2, width), F32)]
        + edge_shapes(feats, late),
        [pltpu.VMEM((late,) + plane, BF16)],
        late, aux, table, frames, *sides, taps,
    )
    sides_late = row_halo(edges)
    hidden_early, stats, *edges = call(
        functools.partial(early_kernel, n_sides),
        [shaped((2, n_rows, cols, width)), shaped((1, 2 * width), F32)] + edge_shapes(feats, 2),
        [pltpu.VMEM((2,) + plane, BF16)],
        2, aux, before, *corners, act_low, affine, stats, taps,
    )
    sides_early = row_halo(edges)
    total, table = slab_table(stats)
    before, corners, table = slab_halo(hidden_late[late - 2 :], table)
    taps = load_call(kernel_two, total)
    return call(
        functools.partial(last_kernel, n_sides),
        shaped(feats.shape, F32),
        [pltpu.VMEM((n_frames + 2,) + plane, BF16)],
        n_frames, aux, table, hidden_early, hidden_late, *sides_early, *sides_late, before, *corners, taps, frames,
    )


def solution(mesh):
    return jax.shard_map(
        on_device,
        mesh=mesh,
        in_specs=(P("tm", "space", None, None), P(), P(), P(), P(), P(), P(), P()),
        out_specs=P("tm", "space", None, None),
        check_vma=False,
    )
```

time: 166 us -> 64.3 us (0.39)
  blocking collectives: 84.2 us -> 0 us
  other arithmetic: 28 us -> 0.01 us
  Pallas kernels: 0 us -> 23.6 us
  matrix products: 14.7 us -> 0 us
  starting transfers between devices: 13.9 us -> 17.3 us
  between operations: 2.54 us -> 0.19 us
    unnamed x2 -> x0, blocking collectives: 84.2 us -> none
    pallas_call x0 -> x6, Pallas kernels: none -> 23.6 us  [the longest x3 17.2 us: call(): pl.pallas_call(kernel, out_shape=outs, in_specs=[VMEM] * len(operands), o...]
    concatenate x22 -> x0, other arithmetic: 19.1 us -> none  [the longest x4 14.9 us: causal_conv(): padded = jnp.pad(extended, ((0, 0), (0, 0), (1, 1), (0, 0)), mode='edge')]
    dot_general x18 -> x0, matrix products: 14.7 us -> none  [causal_conv(): jnp.dot(stacked, kernel[tap_time, tap_row].reshape(3 * width, -1), prefer...]
    ppermute x6 -> x9, waiting for transfers between devices: 14.2 us -> 1.78 us  [the longest x7 1.77 us: traded(): lax.ppermute(value, axis, [(i, i ^ mask) for i in range(lax.axis_size(axi...]
    all_to_all x0 -> x2, starting transfers between devices: none -> 12.3 us  [slab_table(): return (total, lax.all_to_all(copies, 'tm', 0, 0, tiled=True))]
    all_to_all x0 -> x2, waiting for transfers between devices: none -> 12.3 us  [slab_table(): return (total, lax.all_to_all(copies, 'tm', 0, 0, tiled=True))]
    ppermute x6 -> x9, starting transfers between devices: 13.9 us -> 5 us  [the longest x2 3.63 us: shifted(): lax.ppermute(value, axis, [(i, (i + step) % peers) for i in range(peers)])]
  transfers between devices with their start and end apart: 6 -> 11, of which waited for: 3 -> 4; matrix products, arithmetic and copies ran while one was open for 2% -> 6% of each run, Pallas kernels for 0% -> 20%
where the time goes in v6:
time: 64.3 us; the launch traced here: 63.7 us
  Pallas kernels  23.6 us (37%)
  starting transfers between devices  17.3 us (27%)
  waiting for transfers between devices  14 us (22%)
  local copies, waits for them, and re-layouts  8.58 us (13%)
    pallas_call x3, Pallas kernels, call(): pl.pallas_call(kernel, out_shape=outs, in_specs=[VMEM] * len(operands), o...  17.2 us
    all_to_all x2, starting transfers between devices, slab_table(): return (total, lax.all_to_all(copies, 'tm', 0, 0, tiled=True))  12.3 us
    all_to_all x2, waiting for transfers between devices, slab_table(): return (total, lax.all_to_all(copies, 'tm', 0, 0, tiled=True))  12.3 us
    unnamed x22, local copies, waits for them, and re-layouts  5.53 us
    pallas_call x2, Pallas kernels, load_call(): pl.pallas_call(load_kernel, out_shape=shaped(kernel.shape), in_specs=[ANY...  4.1 us
    ppermute x2, starting transfers between devices, shifted(): lax.ppermute(value, axis, [(i, (i + step) % peers) for i in range(peers)])  3.63 us
    pallas_call x1, Pallas kernels, entry_call(): pl.pallas_call(functools.partial(entry_kernel, slabs), out_shape=outs, in...  2.32 us
    dynamic_slice x2, local copies, waits for them, and re-layouts, edges_of(): lax.dynamic_slice_in_dim(frames, (rows - 1) * (1 - lax.axis_index('space'...  1.8 us
  transfers between devices with their start and end apart: 11, of which 4 were waited for; matrix products, arithmetic and copies ran while one was open for 6% of the time, Pallas kernels for 20%

profile of v6, /device:TPU:0, one launch (start us, length us, event | category | flops | bytes accessed | tf_op | source)
XLA Modules:
  0.0 63.7 jit_solution(3341301554293867741)
XLA Ops:
  0.0 2.3 %shard_map.82 = (bf16[4,4,96,256]{3,2,1,0:T(8,128)(2,1)S(1)}, bf16[2,4,96,256]{3,2,1,0:T(8,128)(2,1)}, f32[1,512]{1,0:T(1,128)S(1)}, f32[24,256]{1,0:T(8,128)S(1)}, bf16[4,1,96,256]{3,2,1,0:T(8,128)(2,1)}) custom-call(bf16[4,4,96,256]{3,2,1,0:T(8,128)(2,1)} %refs_0_.1, s32[16]{0:T(128)} %refs_1_.1, f32[1,256]{1,0:T(1,128)} %bitcast.16, f32[1,256]{1,0:T(1,128)} %bitcast.17, ...), custom_call_target="tpu_custom_call" | custom-call | flops 1572864 | bytes 1572864 | tf_op jit(solution)/shard_map/pallas_call | solution.py:144
  2.3 0.0 copy-start
  2.3 0.9 %copy-done = bf16[4,4,96,256]{3,2,1,0:T(8,128)(2,1)} copy-done((bf16[4,4,96,256]{3,2,1,0:T(8,128)(2,1)}, bf16[4,4,96,256]{3,2,1,0:T(8,128)(2,1)S(1)}, u32[]{:S(2)}) %copy-start) | copy-done | bytes 786456
  3.2 0.0 copy-start.5
  3.2 0.6 copy-done.5
  3.8 2.9 %collective-permute-start.3 = (bf16[2,4,96,256]{3,2,1,0:T(8,128)(2,1)}, bf16[2,4,96,256]{3,2,1,0:T(8,128)(2,1)}, u32[]{:S(2)}, u32[]{:S(2)}) collective-permute-start(bf16[2,4,96,256]{3,2,1,0:T(8,128)(2,1)} %get-tuple-element.25), channel_id=1, source_target_pairs={{0,2},{2,4},{4,6},{6,8},{8,10},{10,12},{12,14},{14,16},{16,18},{18... | collective-permute-start | bytes 1179656 | tf_op jit(solution)/shard_map/ppermute | solution.py:37
  6.7 0.0 collective-permute-start.1
  6.8 0.5 collective-permute-start
  7.3 0.8 %collective-permute-done = f32[1,512]{1,0:T(1,128)S(1)} collective-permute-done((f32[1,512]{1,0:T(1,128)S(1)}, f32[1,512]{1,0:T(1,128)S(1)}, u32[]{:S(2)}, u32[]{:S(2)}) %collective-permute-start) | collective-permute-done | bytes 2080 | tf_op jit(solution)/shard_map/ppermute | solution.py:32
  8.1 0.6 broadcast_in_dim.26
  8.7 6.0 %all-to-all-start = ((f32[16,1,512]{2,1,0:T(1,128)}), f32[16,1,512]{2,1,0:T(1,128)}, u32[]{:S(2)}, u32[]{:S(2)}) async-start(f32[16,1,512]{2,1,0:T(1,128)} %broadcast_in_dim.26), calls=%async_computation | async-start | bytes 65536 | tf_op jit(solution)/shard_map/all_to_all | solution.py:44
  14.7 2.0 %shard_map.83.refs_1_.refs_4_ = bf16[3,3,3,256,256]{4,3,2,1,0:T(8,128)(2,1)S(1)} custom-call(bf16[3,3,3,256,256]{4,3,2,1,0:T(8,128)(2,1)} %kernel_hbm.2, f32[1,512]{1,0:T(1,128)S(1)} %add.14.after), custom_call_target="tpu_custom_call" | custom-call | bytes 7077888 | tf_op jit(solution)/shard_map/pallas_call | solution.py:168
  16.7 5.4 %all-to-all-done = f32[16,1,512]{2,1,0:T(1,128)} async-done(((f32[16,1,512]{2,1,0:T(1,128)}), f32[16,1,512]{2,1,0:T(1,128)}, u32[]{:S(2)}, u32[]{:S(2)}) %all-to-all-start) | async-done | bytes 32800 | tf_op jit(solution)/shard_map/all_to_all | solution.py:44
  22.2 0.8 %copy.14 = f32[16,1,512]{2,0,1:T(8,128)S(1)} copy(f32[16,1,512]{2,1,0:T(1,128)} %all-to-all-done) | data formatting | bytes 65536
  22.9 0.0 collective-permute-done.3.before
  22.9 0.9 %constant_dynamic-slice_fusion.1 = bf16[2,1,96,256]{3,2,1,0:T(8,128)(2,1)S(1)} fusion(bf16[2,4,96,256]{3,2,1,0:T(8,128)(2,1)} %collective-permute-done.3.before, s32[]{:T(128)S(6)} %select_n.4), kind=kLoop, calls=%fused_computation.3 | loop fusion | bytes 196612 | tf_op jit(solution)/shard_map/dynamic_slice | solution.py:57
  23.8 0.0 collective-permute-start.4
  23.8 0.0 collective-permute-done.1.refs_0_
  23.8 0.0 copy-start.1
  23.9 1.1 %copy-done.1 = bf16[4,4,96,256]{3,2,1,0:T(8,128)(2,1)S(1)} copy-done((bf16[4,4,96,256]{3,2,1,0:T(8,128)(2,1)S(1)}, bf16[4,4,96,256]{3,2,1,0:T(8,128)(2,1)}, u32[]{:S(2)}) %copy-start.1) | copy-done | bytes 786456
  25.0 0.0 copy-start.6
  25.0 0.7 %copy-done.6 = f32[24,256]{1,0:T(8,128)S(1)} copy-done((f32[24,256]{1,0:T(8,128)S(1)}, f32[24,256]{1,0:T(8,128)}, u32[]{:S(2)}) %copy-start.6) | copy-done | bytes 24600
  25.7 4.9 %shard_map.84 = (bf16[2,4,96,256]{3,2,1,0:T(8,128)(2,1)}, bf16[2,6,96,256]{3,2,1,0:T(8,128)(2,1)S(1)}, f32[1,512]{1,0:T(1,128)S(1)}, f32[2,256]{1,0:T(2,128)S(1)}, bf16[2,1,96,256]{3,2,1,0:T(8,128)(2,1)S(1)}) custom-call(f32[24,256]{1,0:T(8,128)S(1)} %copy-done.6, f32[16,512]{1,0:T(8,128)S(1)} %bitcast.13, bf16[4,4,96,256]{3,2,1,0:T(8,128)(2,1)S(1)} %copy-done.1, ...), custom_call_target="tpu_custom_call" | custom-call | flops 2717908992 | bytes 1048576 | tf_op jit(solution)/shard_map/pallas_call | solution.py:315
  30.6 0.0 copy-start.3
  30.6 0.7 %collective-permute-start.2 = (bf16[2,4,96,256]{3,2,1,0:T(8,128)(2,1)}, bf16[2,4,96,256]{3,2,1,0:T(8,128)(2,1)}, u32[]{:S(2)}, u32[]{:S(2)}) collective-permute-start(bf16[2,4,96,256]{3,2,1,0:T(8,128)(2,1)} %get-tuple-element.24.late), channel_id=1, source_target_pairs={{0,2},{2,4},{4,6},{6,8},{8,10},{10,12},{12,14},{14,16},{16,18},{18... | collective-permute-start | bytes 1179656 | tf_op jit(solution)/shard_map/ppermute | solution.py:37
  31.3 0.0 collective-permute-done.4.refs_0_
  31.3 4.0 %shard_map.85 = (bf16[2,4,96,256]{3,2,1,0:T(8,128)(2,1)S(1)}, f32[1,512]{1,0:T(1,128)S(1)}, bf16[2,1,96,256]{3,2,1,0:T(8,128)(2,1)S(1)}) custom-call(f32[24,256]{1,0:T(8,128)S(1)} %copy-done.6, bf16[2,4,96,256]{3,2,1,0:T(8,128)(2,1)} %collective-permute-done.3.before, bf16[2,1,96,256]{3,2,1,0:T(8,128)(2,1)S(1)} %collective-permute-done.4.refs_0_, ...), custom_call_target="tpu_custom_call" | custom-call | flops 2717908992 | bytes 1048576 | tf_op jit(solution)/shard_map/pallas_call | solution.py:315
  35.3 0.0 copy-done.3
  35.3 0.0 copy-start.4
  35.3 0.6 copy-done.4
  36.0 0.0 copy-start.8
  36.0 0.7 %copy-done.8 = bf16[2,4,96,256]{3,2,1,0:T(8,128)(2,1)} copy-done((bf16[2,4,96,256]{3,2,1,0:T(8,128)(2,1)}, bf16[2,4,96,256]{3,2,1,0:T(8,128)(2,1)S(1)}, u32[]{:S(2)}) %copy-start.8) | copy-done | bytes 393240
  36.7 0.2 collective-permute-start.5
  36.9 0.9 %collective-permute-done.5 = f32[1,512]{1,0:T(1,128)S(1)} collective-permute-done((f32[1,512]{1,0:T(1,128)S(1)}, f32[1,512]{1,0:T(1,128)S(1)}, u32[]{:S(2)}, u32[]{:S(2)}) %collective-permute-start.5) | collective-permute-done | bytes 2080 | tf_op jit(solution)/shard_map/ppermute | solution.py:32
  37.8 0.6 broadcast_in_dim.27
  38.5 6.3 %all-to-all-start.1 = ((f32[16,1,512]{2,1,0:T(1,128)}), f32[16,1,512]{2,1,0:T(1,128)S(1)}, u32[]{:S(2)}, u32[]{:S(2)}) async-start(f32[16,1,512]{2,1,0:T(1,128)} %broadcast_in_dim.27), calls=%async_computation.1 | async-start | bytes 65536 | tf_op jit(solution)/shard_map/all_to_all | solution.py:44
  44.8 0.1 collective-permute-start.7
  44.9 0.5 collective-permute-start.6
  45.4 6.8 %all-to-all-done.1 = f32[16,1,512]{2,1,0:T(1,128)S(1)} async-done(((f32[16,1,512]{2,1,0:T(1,128)}), f32[16,1,512]{2,1,0:T(1,128)S(1)}, u32[]{:S(2)}, u32[]{:S(2)}) %all-to-all-start.1) | async-done | bytes 32800 | tf_op jit(solution)/shard_map/all_to_all | solution.py:44
  52.2 0.0 collective-permute-done.2.refs_2_
  52.2 0.9 %constant_dynamic-slice_fusion = bf16[2,1,96,256]{3,2,1,0:T(8,128)(2,1)S(1)} fusion(bf16[2,4,96,256]{3,2,1,0:T(8,128)(2,1)} %collective-permute-done.2.refs_2_, s32[]{:T(128)S(6)} %select_n.4), kind=kLoop, calls=%fused_computation.2 | loop fusion | bytes 196612 | tf_op jit(solution)/shard_map/dynamic_slice | solution.py:57
  53.1 0.0 copy-start.2
  53.1 0.0 copy-start.7
  53.1 0.0 copy-start.9
  53.1 0.1 collective-permute-start.8
  53.2 2.1 %shard_map.86.refs_4_ = bf16[3,3,3,256,256]{4,3,2,1,0:T(8,128)(2,1)S(1)} custom-call(bf16[3,3,3,256,256]{4,3,2,1,0:T(8,128)(2,1)} %kernel_hbm.3, f32[1,512]{1,0:T(1,128)S(1)} %add.17.after), custom_call_target="tpu_custom_call" | custom-call | bytes 7077888 | tf_op jit(solution)/shard_map/pallas_call | solution.py:168
  55.3 0.0 collective-permute-done.7.refs_1_
  55.3 0.0 collective-permute-done.6.refs_0_
  55.3 0.0 collective-permute-done.8.refs_3_
  55.3 0.0 copy-done.2
  55.3 0.0 copy-done.7
  55.4 0.1 copy-done.9
  55.4 8.3 %shard_map.87 = f32[4,4,96,256]{3,2,1,0:T(8,128)} custom-call(f32[24,256]{1,0:T(8,128)S(1)} %copy-done.7, f32[16,512]{1,0:T(8,128)S(1)} %bitcast.12, bf16[2,4,96,256]{3,2,1,0:T(8,128)(2,1)S(1)} %copy-done.9, bf16[2,4,96,256]{3,2,1,0:T(8,128)(2,1)} %get-tuple-element.24.late, bf16[2,1,96,256]{3,2,1,0:T(8,128)(2,1)S(1)} %collective-permute-done.6.refs_0_, ...), custom_call_target="tpu_custom_call" | custom-call | flops 5435817984 | bytes 1048576 | tf_op jit(solution)/shard_map/pallas_call | solution.py:315
  (3 shorter events, 0.0 us)
Async XLA Ops:
  2.3 0.9 %copy-start = (bf16[4,4,96,256]{3,2,1,0:T(8,128)(2,1)}, bf16[4,4,96,256]{3,2,1,0:T(8,128)(2,1)S(1)}, u32[]{:S(2)}) copy-start(bf16[4,4,96,256]{3,2,1,0:T(8,128)(2,1)S(1)} %get-tuple-element.22.frames.refs_5_) | copy-start | bytes 2359300
  3.2 0.6 copy-start.5
  3.8 19.1 %collective-permute-start.3 = (bf16[2,4,96,256]{3,2,1,0:T(8,128)(2,1)}, bf16[2,4,96,256]{3,2,1,0:T(8,128)(2,1)}, u32[]{:S(2)}, u32[]{:S(2)}) collective-permute-start(bf16[2,4,96,256]{3,2,1,0:T(8,128)(2,1)} %get-tuple-element.25), channel_id=1, source_target_pairs={{0,2},{2,4},{4,6},{6,8},{8,10},{10,12},{12,14},{14,16},{16,18},{18... | collective-permute-start | bytes 1179656 | tf_op jit(solution)/shard_map/ppermute | solution.py:37
  6.7 17.1 %collective-permute-start.1 = (bf16[4,1,96,256]{3,2,1,0:T(8,128)(2,1)}, bf16[4,1,96,256]{3,2,1,0:T(8,128)(2,1)}, u32[]{:S(2)}, u32[]{:S(2)}) collective-permute-start(bf16[4,1,96,256]{3,2,1,0:T(8,128)(2,1)} %get-tuple-element.23), channel_id=1, source_target_pairs={{0,1},{1,0},{2,3},{3,2},{4,5},{5,4},{6,7},{7,6},{8,9},{9,8},{10,11... | collective-permute-start | bytes 589832 | tf_op jit(solution)/shard_map/ppermute | solution.py:32
  6.8 1.3 %collective-permute-start = (f32[1,512]{1,0:T(1,128)S(1)}, f32[1,512]{1,0:T(1,128)S(1)}, u32[]{:S(2)}, u32[]{:S(2)}) collective-permute-start(f32[1,512]{1,0:T(1,128)S(1)} %get-tuple-element.21), channel_id=1, source_target_pairs={{0,1},{1,0},{2,3},{3,2},{4,5},{5,4},{6,7},{7,6},{8,9},{9,8},{10,11... | collective-permute-start | bytes 6152 | tf_op jit(solution)/shard_map/ppermute | solution.py:32
  8.7 13.5 %all-to-all-start = ((f32[16,1,512]{2,1,0:T(1,128)}), f32[16,1,512]{2,1,0:T(1,128)}, u32[]{:S(2)}, u32[]{:S(2)}) async-start(f32[16,1,512]{2,1,0:T(1,128)} %broadcast_in_dim.26), calls=%async_computation | async-start | bytes 65536 | tf_op jit(solution)/shard_map/all_to_all | solution.py:44
  23.8 7.5 %collective-permute-start.4 = (bf16[2,1,96,256]{3,2,1,0:T(8,128)(2,1)S(1)}, bf16[2,1,96,256]{3,2,1,0:T(8,128)(2,1)S(1)}, u32[]{:S(2)}, u32[]{:S(2)}) collective-permute-start(bf16[2,1,96,256]{3,2,1,0:T(8,128)(2,1)S(1)} %constant_dynamic-slice_fusion.1), channel_id=1, source_target_pairs={{0,1},{1,0},{2,3},{3,2},{4,5},{5,4},{6,7},{7,6},{8,9},{9,8},{10,11... | collective-permute-start | bytes 294920 | tf_op jit(solution)/shard_map/ppermute | solution.py:32
  23.8 1.1 %copy-start.1 = (bf16[4,4,96,256]{3,2,1,0:T(8,128)(2,1)S(1)}, bf16[4,4,96,256]{3,2,1,0:T(8,128)(2,1)}, u32[]{:S(2)}) copy-start(bf16[4,4,96,256]{3,2,1,0:T(8,128)(2,1)} %copy-done) | copy-start | bytes 2359300
  25.0 0.7 %copy-start.6 = (f32[24,256]{1,0:T(8,128)S(1)}, f32[24,256]{1,0:T(8,128)}, u32[]{:S(2)}) copy-start(f32[24,256]{1,0:T(8,128)} %copy-done.5) | copy-start | bytes 73732
  30.6 4.7 %copy-start.3 = (bf16[2,1,96,256]{3,2,1,0:T(8,128)(2,1)}, bf16[2,1,96,256]{3,2,1,0:T(8,128)(2,1)S(1)}, u32[]{:S(2)}) copy-start(bf16[2,1,96,256]{3,2,1,0:T(8,128)(2,1)S(1)} %get-tuple-element.33) | copy-start | bytes 294916
  30.6 21.6 %collective-permute-start.2 = (bf16[2,4,96,256]{3,2,1,0:T(8,128)(2,1)}, bf16[2,4,96,256]{3,2,1,0:T(8,128)(2,1)}, u32[]{:S(2)}, u32[]{:S(2)}) collective-permute-start(bf16[2,4,96,256]{3,2,1,0:T(8,128)(2,1)} %get-tuple-element.24.late), channel_id=1, source_target_pairs={{0,2},{2,4},{4,6},{6,8},{8,10},{10,12},{12,14},{14,16},{16,18},{18... | collective-permute-start | bytes 1179656 | tf_op jit(solution)/shard_map/ppermute | solution.py:37
  35.3 0.6 copy-start.4
  36.0 0.7 %copy-start.8 = (bf16[2,4,96,256]{3,2,1,0:T(8,128)(2,1)}, bf16[2,4,96,256]{3,2,1,0:T(8,128)(2,1)S(1)}, u32[]{:S(2)}) copy-start(bf16[2,4,96,256]{3,2,1,0:T(8,128)(2,1)S(1)} %get-tuple-element.31.early) | copy-start | bytes 1179652
  36.7 1.2 %collective-permute-start.5 = (f32[1,512]{1,0:T(1,128)S(1)}, f32[1,512]{1,0:T(1,128)S(1)}, u32[]{:S(2)}, u32[]{:S(2)}) collective-permute-start(f32[1,512]{1,0:T(1,128)S(1)} %get-tuple-element.29), channel_id=1, source_target_pairs={{0,1},{1,0},{2,3},{3,2},{4,5},{5,4},{6,7},{7,6},{8,9},{9,8},{10,11... | collective-permute-start | bytes 6152 | tf_op jit(solution)/shard_map/ppermute | solution.py:32
  38.5 13.7 %all-to-all-start.1 = ((f32[16,1,512]{2,1,0:T(1,128)}), f32[16,1,512]{2,1,0:T(1,128)S(1)}, u32[]{:S(2)}, u32[]{:S(2)}) async-start(f32[16,1,512]{2,1,0:T(1,128)} %broadcast_in_dim.27), calls=%async_computation.1 | async-start | bytes 65536 | tf_op jit(solution)/shard_map/all_to_all | solution.py:44
  44.8 10.5 %collective-permute-start.7 = (bf16[2,1,96,256]{3,2,1,0:T(8,128)(2,1)}, bf16[2,1,96,256]{3,2,1,0:T(8,128)(2,1)S(1)}, u32[]{:S(2)}, u32[]{:S(2)}) collective-permute-start(bf16[2,1,96,256]{3,2,1,0:T(8,128)(2,1)} %copy-done.3), channel_id=1, source_target_pairs={{0,1},{1,0},{2,3},{3,2},{4,5},{5,4},{6,7},{7,6},{8,9},{9,8},{10,11... | collective-permute-start | bytes 294920 | tf_op jit(solution)/shard_map/ppermute | solution.py:32
  44.9 10.4 %collective-permute-start.6 = (bf16[2,1,96,256]{3,2,1,0:T(8,128)(2,1)}, bf16[2,1,96,256]{3,2,1,0:T(8,128)(2,1)S(1)}, u32[]{:S(2)}, u32[]{:S(2)}) collective-permute-start(bf16[2,1,96,256]{3,2,1,0:T(8,128)(2,1)} %copy-done.4), channel_id=1, source_target_pairs={{0,1},{1,0},{2,3},{3,2},{4,5},{5,4},{6,7},{7,6},{8,9},{9,8},{10,11... | collective-permute-start | bytes 294920 | tf_op jit(solution)/shard_map/ppermute | solution.py:32
  53.1 2.2 %copy-start.2 = (bf16[4,4,96,256]{3,2,1,0:T(8,128)(2,1)S(1)}, bf16[4,4,96,256]{3,2,1,0:T(8,128)(2,1)}, u32[]{:S(2)}) copy-start(bf16[4,4,96,256]{3,2,1,0:T(8,128)(2,1)} %copy-done) | copy-start | bytes 2359300
  53.1 2.2 %copy-start.7 = (f32[24,256]{1,0:T(8,128)S(1)}, f32[24,256]{1,0:T(8,128)}, u32[]{:S(2)}) copy-start(f32[24,256]{1,0:T(8,128)} %copy-done.5) | copy-start | bytes 73732
  53.1 2.3 %copy-start.9 = (bf16[2,4,96,256]{3,2,1,0:T(8,128)(2,1)S(1)}, bf16[2,4,96,256]{3,2,1,0:T(8,128)(2,1)}, u32[]{:S(2)}) copy-start(bf16[2,4,96,256]{3,2,1,0:T(8,128)(2,1)} %copy-done.8) | copy-start | bytes 1179652
  53.1 2.2 %collective-permute-start.8 = (bf16[2,1,96,256]{3,2,1,0:T(8,128)(2,1)S(1)}, bf16[2,1,96,256]{3,2,1,0:T(8,128)(2,1)S(1)}, u32[]{:S(2)}, u32[]{:S(2)}) collective-permute-start(bf16[2,1,96,256]{3,2,1,0:T(8,128)(2,1)S(1)} %constant_dynamic-slice_fusion), channel_id=1, source_target_pairs={{0,1},{1,0},{2,3},{3,2},{4,5},{5,4},{6,7},{7,6},{8,9},{9,8},{10,11... | collective-permute-start | bytes 294920 | tf_op jit(solution)/shard_map/ppermute | solution.py:32

commit v7 on v6

--- a/solution.py
+++ b/solution.py
@@ -37,11 +37,31 @@
     return lax.ppermute(value, axis, [(i, (i + step) % peers) for i in range(peers)])
 
 
-def slab_table(stats):
-    slabs, places = lax.axis_size("tm"), lax.axis_size("space")
-    total = stats + traded(stats, "space", 1) if places == 2 else lax.psum(stats, "space")
-    copies = jnp.broadcast_to(total, (slabs, total.shape[1]))
-    return total, lax.all_to_all(copies, "tm", 0, 0, tiled=True)
+def group_sizes(peers):
+    sizes = []
+    while peers > 1:
+        sizes.append(min(4, peers))
+        peers //= sizes[-1]
+    return sizes
+
+
+def slab_offsets(peers):
+    offsets, left = [0], peers
+    for ways in group_sizes(peers):
+        left //= ways
+        offsets = [(left * way) ^ offset for way in range(ways) for offset in offsets]
+    return offsets
+
+
+def slab_tables(stats):
+    peers = lax.axis_size("tm")
+    total = stats + traded(stats, "space", 1) if lax.axis_size("space") == 2 else lax.psum(stats, "space")
+    held, left = [total], peers
+    for ways in group_sizes(peers):
+        left //= ways
+        block = held[0] if len(held) == 1 else jnp.concatenate(held, axis=0)
+        held = [block] + [traded(block, "tm", left * way) for way in range(1, ways)]
+    return total, held
 
 
 def row_halo(edges):
@@ -98,64 +118,80 @@
         stats[:, k * width : (k + 1) * width] = part if base is None else part + base[:, k * width : (k + 1) * width]
 
 
-def entry_kernel(slabs, *refs):
-    feats_hbm, clips_hbm = refs[:2]
-    params_hbm = refs[2:6]
-    frames, tail, stats, aux = refs[6:10]
-    edges = refs[10:-4]
-    params, clips, sems, frame_sems = refs[-4:]
-    n_frames, n_rows, cols, width = frames.shape
-    loads = [pltpu.make_async_copy(feats_hbm.at[f], frames.at[f], frame_sems.at[f]) for f in range(n_frames)]
-    clip_load = pltpu.make_async_copy(clips_hbm, clips, sems.at[0])
-    tail_load = pltpu.make_async_copy(feats_hbm.at[pl.ds(n_frames - TAIL, TAIL)], tail, sems.at[1])
-    param_loads = [pltpu.make_async_copy(p, params.at[k], sems.at[2 + k]) for k, p in enumerate(params_hbm)]
-    for copy in [*loads, clip_load, tail_load, *param_loads]:
+def entry_kernel(feats_hbm, frames, tail, stats, *rest):
+    *edges, sems = rest
+    n_frames, n_rows, _, width = frames.shape
+    loads = [pltpu.make_async_copy(feats_hbm.at[f], frames.at[f], sems.at[f]) for f in range(n_frames)]
+    for copy in loads:
         copy.start()
     sums = no_stats(width)
     for frame in range(n_frames):
         loads[frame].wait()
         for row in range(n_rows):
+            if frame >= n_frames - TAIL:
+                tail[frame - n_frames + TAIL, row] = frames[frame, row]
             sums = add_stats(sums, frames[frame, row].astype(F32))
         send_rows(frames, frame, edges)
     store_stats(stats, sums)
+
+
+def entry_call(feats):
+    n_frames, width = feats.shape[0], feats.shape[3]
+    outs = [shaped(feats.shape), shaped((TAIL,) + feats.shape[1:]), shaped((1, 2 * width), F32)]
+    outs += edge_shapes(feats, n_frames)
+    frames, tail, stats, *edges = pl.pallas_call(
+        entry_kernel,
+        out_shape=outs,
+        in_specs=[ANYWHERE],
+        out_specs=[VMEM] * len(outs),
+        scratch_shapes=[pltpu.SemaphoreType.DMA((n_frames,))],
+        compiler_params=vmem_params(),
+        cost_estimate=pl.CostEstimate(flops=4 * feats.size, bytes_accessed=4 * feats.size, transcendentals=0),
+    )(in_hbm(feats))
+    return frames, tail, stats, edges
+
+
+def setup_kernel(slabs, per_slab, kernel_hbm, clips_hbm, *refs):
+    params_hbm, (_, taps, aux, params, clips, sems) = refs[:4], refs[4:]
+    width = aux.shape[1]
+    taps_load = pltpu.make_async_copy(kernel_hbm, taps, sems.at[0])
+    clip_load = pltpu.make_async_copy(clips_hbm, clips, sems.at[1])
+    param_loads = [pltpu.make_async_copy(p, params.at[k], sems.at[2 + k]) for k, p in enumerate(params_hbm)]
+    for copy in [clip_load, *param_loads, taps_load]:
+        copy.start()
     clip_load.wait()
     own = lax.axis_index("tm")
     own_clip = clips[own]
     slabs_in = jnp.int32(0)
-    for slab in range(slabs):
-        same = (clips[slab] == own_clip).astype(jnp.int32)
+    for entry, offset in enumerate(slab_offsets(slabs)):
+        same = (clips[own ^ offset] == own_clip).astype(jnp.int32)
         slabs_in = slabs_in + same
-        aux[slab : slab + 1] = jnp.full((1, width), same.astype(F32), F32)
+        aux[entry : entry + 1] = jnp.full((1, width), same.astype(F32), F32)
     starting = jnp.logical_or(own == 0, clips[jnp.maximum(own - 1, 0)] != own_clip)
     aux[slabs : slabs + 1] = jnp.full((1, width), starting.astype(F32), F32)
-    per_slab = n_frames * n_rows * cols * width // GROUPS * lax.axis_size("space")
     aux[slabs + 1 : slabs + 2] = jnp.full((1, width), slabs_in.astype(F32) * float(per_slab), F32)
     for k, copy in enumerate(param_loads):
         copy.wait()
         aux[slabs + 2 + k : slabs + 3 + k] = params[k]
-    tail_load.wait()
-
-
-def entry_call(feats, clip_ids, params):
-    slabs = lax.axis_size("tm")
-    n_frames, width = feats.shape[0], feats.shape[3]
-    outs = [shaped(feats.shape), shaped((TAIL,) + feats.shape[1:]), shaped((1, 2 * width), F32), shaped((slabs + 8, width), F32)]
-    outs += edge_shapes(feats, n_frames)
-    frames, tail, stats, aux, *edges = pl.pallas_call(
-        functools.partial(entry_kernel, slabs),
-        out_shape=outs,
-        in_specs=[ANYWHERE] * 6,
-        out_specs=[VMEM] * len(outs),
+    aux[slabs + 6 : slabs + 8] = jnp.zeros((2, width), F32)
+    taps_load.wait()
+
+
+def setup_call(kernel, clip_ids, params, per_slab, after):
+    slabs, width = lax.axis_size("tm"), kernel.shape[4]
+    return pl.pallas_call(
+        functools.partial(setup_kernel, slabs, per_slab),
+        out_shape=[shaped(kernel.shape), shaped((slabs + 8, width), F32)],
+        in_specs=[ANYWHERE] * 7,
+        out_specs=[VMEM, VMEM],
         scratch_shapes=[
             pltpu.VMEM((4, 1, width), F32),
             pltpu.SMEM(clip_ids.shape, jnp.int32),
             pltpu.SemaphoreType.DMA((6,)),
-            pltpu.SemaphoreType.DMA((n_frames,)),
         ],
         compiler_params=vmem_params(),
-        cost_estimate=pl.CostEstimate(flops=4 * feats.size, bytes_accessed=4 * feats.size, transcendentals=0),
-    )(*[in_hbm(x) for x in (feats, clip_ids, *[p[None] for p in params])])
-    return frames, tail, stats, aux, edges
+        cost_estimate=pl.CostEstimate(flops=0, bytes_accessed=4 * kernel.size, transcendentals=0),
+    )(*[in_hbm(x) for x in (kernel, clip_ids, *[p[None] for p in params])], after)
 
 
 def load_kernel(kernel_hbm, after, taps, sem):
@@ -188,11 +224,17 @@
     return values
 
 
-def half_affine(table, aux, which):
-    slabs = table.shape[0]
+def half_affine(tables, aux, which):
     width = aux.shape[1]
-    mask = aux[:slabs]
-    sums = [jnp.sum(table[:, k * width : (k + 1) * width] * mask, axis=0, keepdims=True) for k in range(2)]
+    slabs = aux.shape[0] - 8
+    sums = [jnp.zeros((1, width), F32)] * 2
+    entry = 0
+    for table in tables:
+        mask = aux[entry : entry + table.shape[0]]
+        entry += table.shape[0]
+        sums = [
+            total + jnp.sum(table[:, k * width : (k + 1) * width] * mask, axis=0, keepdims=True) for k, total in enumerate(sums)
+        ]
     grouped = group_total(jnp.concatenate(sums, axis=0))
     count = aux[slabs + 1 : slabs + 2]
     gain = aux[slabs + 2 + 2 * which : slabs + 3 + 2 * which]
@@ -242,12 +284,13 @@
     return add_stats(sums, rounded.astype(F32))
 
 
-def late_kernel(n_sides, aux, table, frames, *refs):
+def late_kernel(n_tables, n_sides, aux, *refs):
+    tables, frames, refs = refs[:n_tables], refs[n_tables], refs[n_tables + 1 :]
     sides, taps = refs[:n_sides], refs[n_sides]
     hidden, act_low, stats, affine_out, *edges, act_high = refs[n_sides + 1 :]
     n_frames = frames.shape[0]
     low = act_low.shape[0]
-    affine = half_affine(table, aux, 0)
+    affine = half_affine(tables, aux, 0)
     for k in range(2):
         affine_out[k : k + 1] = affine[k]
     planes = [(act_low, f) for f in range(low)] + [(act_high, f) for f in range(n_frames - low)]
@@ -281,13 +324,14 @@
     store_stats(stats, sums, stats_in)
 
 
-def last_kernel(n_sides, aux, table, early, late, *refs):
+def last_kernel(n_tables, n_sides, aux, *refs):
+    tables, early, late, refs = refs[:n_tables], refs[n_tables], refs[n_tables + 1], refs[n_tables + 2 :]
     sides_early, sides_late = refs[:n_sides], refs[n_sides : 2 * n_sides]
     before, *corners = refs[2 * n_sides : 3 * n_sides + 1]
     taps, feats, out, act = refs[3 * n_sides + 1 :]
     slabs = aux.shape[0] - 8
     starting = aux[slabs : slabs + 1] != 0.0
-    affine = half_affine(table, aux, 1)
+    affine = half_affine(tables, aux, 1)
     n_frames, n_rows = out.shape[:2]
 
     def fill(frame):
@@ -325,20 +369,22 @@
 
 def on_device(feats, clip_ids, gain_one, shift_one, kernel_one, gain_two, shift_two, kernel_two):
     n_frames, n_rows, cols, width = feats.shape
-    frames, tail, stats, aux, edges = entry_call(feats, clip_ids, (gain_one, shift_one, gain_two, shift_two))
+    params = (gain_one, shift_one, gain_two, shift_two)
+    frames, tail, stats, edges = entry_call(feats)
     before, corners, _ = slab_halo(tail)
-    total, table = slab_table(stats)
+    total, tables = slab_tables(stats)
     sides = row_halo(edges)
-    taps = load_call(kernel_one, total)
+    per_slab = feats.size // GROUPS * lax.axis_size("space")
+    taps, aux = setup_call(kernel_one, clip_ids, params, per_slab, total)
     n_sides = len(sides)
     plane = (n_rows + 2, cols, width)
     late = n_frames - 2
     hidden_late, act_low, stats, affine, *edges = call(
-        functools.partial(late_kernel, n_sides),
+        functools.partial(late_kernel, len(tables), n_sides),
         [shaped((late, n_rows, cols, width)), shaped((2,) + plane), shaped((1, 2 * width), F32), shaped((2, width), F32)]
         + edge_shapes(feats, late),
         [pltpu.VMEM((late,) + plane, BF16)],
-        late, aux, table, frames, *sides, taps,
+        late, aux, *tables, frames, *sides, taps,
     )
     sides_late = row_halo(edges)
     hidden_early, stats, *edges = call(
@@ -348,14 +394,14 @@
         2, aux, before, *corners, act_low, affine, stats, taps,
     )
     sides_early = row_halo(edges)
-    total, table = slab_table(stats)
-    before, corners, table = slab_halo(hidden_late[late - 2 :], table)
+    total, tables = slab_tables(stats)
+    before, corners, tables[0] = slab_halo(hidden_late[late - 2 :], tables[0])
     taps = load_call(kernel_two, total)
     return call(
-        functools.partial(last_kernel, n_sides),
+        functools.partial(last_kernel, len(tables), n_sides),
         shaped(feats.shape, F32),
         [pltpu.VMEM((n_frames + 2,) + plane, BF16)],
-        n_frames, aux, table, hidden_early, hidden_late, *sides_early, *sides_late, before, *corners, taps, frames,
+        n_frames, aux, *tables, hidden_early, hidden_late, *sides_early, *sides_late, before, *corners, taps, frames,
     )
 
 

time: 64.3 us -> 51.8 us (0.81)
  local copies, waits for them, and re-layouts: 8.58 us -> 0.01 us
  Pallas kernels: 23.6 us -> 19 us
  starting transfers between devices: 17.3 us -> 21.5 us
  waiting for transfers between devices: 14 us -> 11 us
    ppermute x7 -> x19, starting transfers between devices: 1.37 us -> 17.9 us  [traded(): lax.ppermute(value, axis, [(i, i ^ mask) for i in range(lax.axis_size(axi...]
    all_to_all x2 -> x0, starting transfers between devices: 12.3 us -> none  [slab_table(): return (total, lax.all_to_all(copies, 'tm', 0, 0, tiled=True))]
    all_to_all x2 -> x0, waiting for transfers between devices: 12.3 us -> none  [slab_table(): return (total, lax.all_to_all(copies, 'tm', 0, 0, tiled=True))]
    ppermute x7 -> x19, waiting for transfers between devices: 1.77 us -> 9.41 us  [traded(): lax.ppermute(value, axis, [(i, i ^ mask) for i in range(lax.axis_size(axi...]
    unnamed x22 -> x0, local copies, waits for them, and re-layouts: 5.53 us -> none
    pallas_call x3, Pallas kernels: 17.2 us -> 13.5 us  [call(): pl.pallas_call(kernel, out_shape=outs, in_specs=[VMEM] * len(operands), o...]
    pallas_call x2 -> x1, Pallas kernels: 4.1 us -> 2.01 us  [load_call(): pl.pallas_call(load_kernel, out_shape=shaped(kernel.shape), in_specs=[ANY...]
    dynamic_slice x2, local copies, waits for them, and re-layouts: 1.8 us -> 0.01 us  [edges_of(): lax.dynamic_slice_in_dim(frames, (rows - 1) * (1 - lax.axis_index('space'...]
  transfers between devices with their start and end apart: 11 -> 21, of which waited for: 4 -> 10; matrix products, arithmetic and copies ran while one was open for 6% -> 0% of each run, Pallas kernels for 20% -> 20%
where the time goes in v7:
time: 51.8 us; the launch traced here: 51.6 us
  starting transfers between devices  21.5 us (42%)
  Pallas kernels  19 us (37%)
  waiting for transfers between devices  11 us (21%)
    ppermute x19, starting transfers between devices, traded(): lax.ppermute(value, axis, [(i, i ^ mask) for i in range(lax.axis_size(axi...  17.9 us
    pallas_call x3, Pallas kernels, call(): pl.pallas_call(kernel, out_shape=outs, in_specs=[VMEM] * len(operands), o...  13.5 us
    ppermute x19, waiting for transfers between devices, traded(): lax.ppermute(value, axis, [(i, i ^ mask) for i in range(lax.axis_size(axi...  9.41 us
    ppermute x2, starting transfers between devices, shifted(): lax.ppermute(value, axis, [(i, (i + step) % peers) for i in range(peers)])  3.68 us
    pallas_call x1, Pallas kernels, setup_call(): pl.pallas_call(functools.partial(setup_kernel, slabs, per_slab), out_shap...  2.12 us
    pallas_call x1, Pallas kernels, load_call(): pl.pallas_call(load_kernel, out_shape=shaped(kernel.shape), in_specs=[ANY...  2.01 us
    ppermute x2, waiting for transfers between devices, shifted(): lax.ppermute(value, axis, [(i, (i + step) % peers) for i in range(peers)])  1.54 us
    pallas_call x1, Pallas kernels, entry_call(): pl.pallas_call(entry_kernel, out_shape=outs, in_specs=[ANYWHERE], out_spe...  1.3 us
  transfers between devices with their start and end apart: 21, of which 10 were waited for; matrix products, arithmetic and copies ran while one was open for 0% of the time, Pallas kernels for 20%

profile of v7, /device:TPU:0, one launch (start us, length us, event | category | flops | bytes accessed | tf_op | source)
XLA Modules:
  0.0 51.6 jit_solution(4469546318882178572)
XLA Ops:
  0.0 1.3 %shard_map.82 = (bf16[4,4,96,256]{3,2,1,0:T(8,128)(2,1)S(1)}, bf16[2,4,96,256]{3,2,1,0:T(8,128)(2,1)S(1)}, f32[1,512]{1,0:T(1,128)S(1)}, bf16[4,1,96,256]{3,2,1,0:T(8,128)(2,1)S(1)}) custom-call(bf16[4,4,96,256]{3,2,1,0:T(8,128)(2,1)} %feats_hbm.1), custom_call_target="tpu_custom_call" | custom-call | flops 1572864 | bytes 1572864 | tf_op jit(solution)/shard_map/pallas_call | solution.py:142
  1.3 3.0 %collective-permute-start.9 = (bf16[2,4,96,256]{3,2,1,0:T(8,128)(2,1)S(1)}, bf16[2,4,96,256]{3,2,1,0:T(8,128)(2,1)S(1)}, u32[]{:S(2)}, u32[]{:S(2)}) collective-permute-start(bf16[2,4,96,256]{3,2,1,0:T(8,128)(2,1)S(1)} %get-tuple-element.27), channel_id=1, source_target_pairs={{0,2},{2,4},{4,6},{6,8},{8,10},{10,12},{12,14},{14,16},{16,18},{18... | collective-permute-start | bytes 1179656 | tf_op jit(solution)/shard_map/ppermute | solution.py:37
  4.3 0.0 collective-permute-start
  4.3 1.2 %collective-permute-done = f32[1,512]{1,0:T(1,128)S(1)} collective-permute-done((f32[1,512]{1,0:T(1,128)S(1)}, f32[1,512]{1,0:T(1,128)S(1)}, u32[]{:S(2)}, u32[]{:S(2)}) %collective-permute-start) | collective-permute-done | bytes 2080 | tf_op jit(solution)/shard_map/ppermute | solution.py:32
  5.5 3.6 %collective-permute-start.3 = (f32[1,512]{1,0:T(1,128)S(1)}, f32[1,512]{1,0:T(1,128)S(1)}, u32[]{:S(2)}, u32[]{:S(2)}) collective-permute-start(f32[1,512]{1,0:T(1,128)S(1)} %add.10.refs_4_), channel_id=1, source_target_pairs={{0,24},{2,26},{4,28},{6,30},{8,16},{10,18},{12,20},{14,22},{16,8},... | collective-permute-start | bytes 6152 | tf_op jit(solution)/shard_map/ppermute | solution.py:32
  9.1 0.0 collective-permute-start.2
  9.1 0.8 %collective-permute-start.1 = (f32[1,512]{1,0:T(1,128)S(1)}, f32[1,512]{1,0:T(1,128)S(1)}, u32[]{:S(2)}, u32[]{:S(2)}) collective-permute-start(f32[1,512]{1,0:T(1,128)S(1)} %add.10.refs_4_), channel_id=1, source_target_pairs={{0,8},{2,10},{4,12},{6,14},{8,0},{10,2},{12,4},{14,6},{16,24},{18,... | collective-permute-start | bytes 6152 | tf_op jit(solution)/shard_map/ppermute | solution.py:32
  9.9 0.0 collective-permute-start.7
  9.9 2.1 %shard_map.83 = (bf16[3,3,3,256,256]{4,3,2,1,0:T(8,128)(2,1)S(1)}, f32[24,256]{1,0:T(8,128)S(1)}) custom-call(bf16[3,3,3,256,256]{4,3,2,1,0:T(8,128)(2,1)} %kernel_hbm.2, s32[16]{0:T(128)} %clips_hbm.1, f32[1,256]{1,0:T(1,128)} %bitcast.4, f32[1,256]{1,0:T(1,128)} %bitcast.5, f32[1,256]{1,0:T(1,128)} %bitcast.6, f32[1,256]{1,0:T(1,128)} %bitcast.7, ...), custom_call_target="tpu_custom_call" | custom-call | bytes 7077888 | tf_op jit(solution)/shard_map/pallas_call | solution.py:182
  12.0 0.0 collective-permute-done.3
  12.0 1.6 %collective-permute-done.2 = f32[1,512]{1,0:T(1,128)S(1)} collective-permute-done((f32[1,512]{1,0:T(1,128)S(1)}, f32[1,512]{1,0:T(1,128)S(1)}, u32[]{:S(2)}, u32[]{:S(2)}) %collective-permute-start.2) | collective-permute-done | bytes 2080 | tf_op jit(solution)/shard_map/ppermute | solution.py:32
  13.6 0.0 collective-permute-done.1
  13.6 4.7 %collective-permute-start.6 = (f32[4,512]{1,0:T(4,128)S(1)}, f32[4,512]{1,0:T(4,128)S(1)}, u32[]{:S(2)}, u32[]{:S(2)}) collective-permute-start(f32[4,512]{1,0:T(4,128)S(1)} %pad_maximum_fusion.refs_0_), channel_id=1, source_target_pairs={{0,6},{2,4},{4,2},{6,0},{8,14},{10,12},{12,10},{14,8},{16,22},{18,... | collective-permute-start | bytes 24584 | tf_op jit(solution)/shard_map/ppermute | solution.py:32
  18.2 0.0 collective-permute-start.5
  18.2 0.6 %collective-permute-start.4 = (f32[4,512]{1,0:T(4,128)S(1)}, f32[4,512]{1,0:T(4,128)S(1)}, u32[]{:S(2)}, u32[]{:S(2)}) collective-permute-start(f32[4,512]{1,0:T(4,128)S(1)} %pad_maximum_fusion.refs_0_), channel_id=1, source_target_pairs={{0,2},{2,0},{4,6},{6,4},{8,10},{10,8},{12,14},{14,12},{16,18},{18,... | collective-permute-start | bytes 24584 | tf_op jit(solution)/shard_map/ppermute | solution.py:32
  18.9 0.0 collective-permute-done.9.before
  18.9 0.1 collective-permute-start.10
  19.0 0.9 %collective-permute-done.6.refs_3_ = f32[4,512]{1,0:T(4,128)S(1)} collective-permute-done((f32[4,512]{1,0:T(4,128)S(1)}, f32[4,512]{1,0:T(4,128)S(1)}, u32[]{:S(2)}, u32[]{:S(2)}) %collective-permute-start.6) | collective-permute-done | bytes 8224 | tf_op jit(solution)/shard_map/ppermute | solution.py:32
  19.9 2.0 %collective-permute-done.5.refs_2_ = f32[4,512]{1,0:T(4,128)S(1)} collective-permute-done((f32[4,512]{1,0:T(4,128)S(1)}, f32[4,512]{1,0:T(4,128)S(1)}, u32[]{:S(2)}, u32[]{:S(2)}) %collective-permute-start.5) | collective-permute-done | bytes 8224 | tf_op jit(solution)/shard_map/ppermute | solution.py:32
  21.9 0.0 collective-permute-done.4.refs_1_
  21.9 0.0 collective-permute-done.7.refs_5_
  21.9 3.3 %shard_map.84 = (bf16[2,4,96,256]{3,2,1,0:T(8,128)(2,1)S(1)}, bf16[2,6,96,256]{3,2,1,0:T(8,128)(2,1)S(1)}, f32[1,512]{1,0:T(1,128)S(1)}, f32[2,256]{1,0:T(2,128)S(1)}, bf16[2,1,96,256]{3,2,1,0:T(8,128)(2,1)S(1)}) custom-call(f32[24,256]{1,0:T(8,128)S(1)} %get-tuple-element.22.aux, f32[4,512]{1,0:T(4,128)S(1)} %pad_maximum_fusion.refs_0_, ...), custom_call_target="tpu_custom_call" | custom-call | flops 2717908992 | bytes 1048576 | tf_op jit(solution)/shard_map/pallas_call | solution.py:359
  25.2 0.7 %collective-permute-start.8 = (bf16[2,4,96,256]{3,2,1,0:T(8,128)(2,1)S(1)}, bf16[2,4,96,256]{3,2,1,0:T(8,128)(2,1)S(1)}, u32[]{:S(2)}, u32[]{:S(2)}) collective-permute-start(bf16[2,4,96,256]{3,2,1,0:T(8,128)(2,1)S(1)} %get-tuple-element.26.refs_5_), channel_id=1, source_target_pairs={{0,2},{2,4},{4,6},{6,8},{8,10},{10,12},{12,14},{14,16},{16,18},{18... | collective-permute-start | bytes 1179656 | tf_op jit(solution)/shard_map/ppermute | solution.py:37
  25.9 0.0 collective-permute-done.10.refs_0_
  25.9 3.1 %shard_map.85 = (bf16[2,4,96,256]{3,2,1,0:T(8,128)(2,1)S(1)}, f32[1,512]{1,0:T(1,128)S(1)}, bf16[2,1,96,256]{3,2,1,0:T(8,128)(2,1)S(1)}) custom-call(f32[24,256]{1,0:T(8,128)S(1)} %get-tuple-element.22.aux, bf16[2,4,96,256]{3,2,1,0:T(8,128)(2,1)S(1)} %collective-permute-done.9.before, bf16[2,1,96,256]{3,2,1,0:T(8,128)(2,1)S(1)} %collective-permute-done.10.refs_0_, ...), custom_call_target="tpu_custom_call" | custom-call | flops 2717908992 | bytes 1048576 | tf_op jit(solution)/shard_map/pallas_call | solution.py:359
  28.9 0.1 collective-permute-start.11
  29.0 1.1 %collective-permute-done.11 = f32[1,512]{1,0:T(1,128)S(1)} collective-permute-done((f32[1,512]{1,0:T(1,128)S(1)}, f32[1,512]{1,0:T(1,128)S(1)}, u32[]{:S(2)}, u32[]{:S(2)}) %collective-permute-start.11) | collective-permute-done | bytes 2080 | tf_op jit(solution)/shard_map/ppermute | solution.py:32
  30.2 1.6 %collective-permute-start.14 = (f32[1,512]{1,0:T(1,128)S(1)}, f32[1,512]{1,0:T(1,128)S(1)}, u32[]{:S(2)}, u32[]{:S(2)}) collective-permute-start(f32[1,512]{1,0:T(1,128)S(1)} %add.12.after), channel_id=1, source_target_pairs={{0,24},{2,26},{4,28},{6,30},{8,16},{10,18},{12,20},{14,22},{16,8},... | collective-permute-start | bytes 6152 | tf_op jit(solution)/shard_map/ppermute | solution.py:32
  31.8 0.4 collective-permute-start.13
  32.2 2.4 %collective-permute-start.12 = (f32[1,512]{1,0:T(1,128)S(1)}, f32[1,512]{1,0:T(1,128)S(1)}, u32[]{:S(2)}, u32[]{:S(2)}) collective-permute-start(f32[1,512]{1,0:T(1,128)S(1)} %add.12.after), channel_id=1, source_target_pairs={{0,8},{2,10},{4,12},{6,14},{8,0},{10,2},{12,4},{14,6},{16,24},{18,... | collective-permute-start | bytes 6152 | tf_op jit(solution)/shard_map/ppermute | solution.py:32
  34.5 0.0 collective-permute-start.19
  34.5 1.0 %collective-permute-done.14 = f32[1,512]{1,0:T(1,128)S(1)} collective-permute-done((f32[1,512]{1,0:T(1,128)S(1)}, f32[1,512]{1,0:T(1,128)S(1)}, u32[]{:S(2)}, u32[]{:S(2)}) %collective-permute-start.14) | collective-permute-done | bytes 2080 | tf_op jit(solution)/shard_map/ppermute | solution.py:32
  35.5 0.0 collective-permute-start.18
  35.5 0.7 %collective-permute-done.13 = f32[1,512]{1,0:T(1,128)S(1)} collective-permute-done((f32[1,512]{1,0:T(1,128)S(1)}, f32[1,512]{1,0:T(1,128)S(1)}, u32[]{:S(2)}, u32[]{:S(2)}) %collective-permute-start.13) | collective-permute-done | bytes 2080 | tf_op jit(solution)/shard_map/ppermute | solution.py:32
  36.2 0.0 collective-permute-done.12
  36.3 1.5 %collective-permute-done.8.refs_8_ = bf16[2,4,96,256]{3,2,1,0:T(8,128)(2,1)S(1)} collective-permute-done((bf16[2,4,96,256]{3,2,1,0:T(8,128)(2,1)S(1)}, bf16[2,4,96,256]{3,2,1,0:T(8,128)(2,1)S(1)}, u32[]{:S(2)}, u32[]{:S(2)}) %collective-permute-start.8) | collective-permute-done | bytes 393248 | tf_op jit(solution)/shard_map/ppermute | solution.py:37
  37.8 0.1 collective-permute-start.20
  37.9 2.5 %collective-permute-start.17 = (f32[4,512]{1,0:T(4,128)S(1)}, f32[4,512]{1,0:T(4,128)S(1)}, u32[]{:S(2)}, u32[]{:S(2)}) collective-permute-start(f32[4,512]{1,0:T(4,128)S(1)} %pad_maximum_fusion.1.refs_0_), channel_id=1, source_target_pairs={{0,6},{2,4},{4,2},{6,0},{8,14},{10,12},{12,10},{14,8},{16,22},{18,... | collective-permute-start | bytes 24584 | tf_op jit(solution)/shard_map/ppermute | solution.py:32
  40.4 0.4 collective-permute-start.16
  40.7 0.0 collective-permute-done.19.refs_7_
  40.7 0.7 %collective-permute-start.15 = (f32[4,512]{1,0:T(4,128)S(1)}, f32[4,512]{1,0:T(4,128)S(1)}, u32[]{:S(2)}, u32[]{:S(2)}) collective-permute-start(f32[4,512]{1,0:T(4,128)S(1)} %pad_maximum_fusion.1.refs_0_), channel_id=1, source_target_pairs={{0,2},{2,0},{4,6},{6,4},{8,10},{10,8},{12,14},{14,12},{16,18},{18,... | collective-permute-start | bytes 24584 | tf_op jit(solution)/shard_map/ppermute | solution.py:32
  41.4 2.0 %shard_map.86.refs_10_ = bf16[3,3,3,256,256]{4,3,2,1,0:T(8,128)(2,1)S(1)} custom-call(bf16[3,3,3,256,256]{4,3,2,1,0:T(8,128)(2,1)} %kernel_hbm.3, f32[1,512]{1,0:T(1,128)S(1)} %add.12.after), custom_call_target="tpu_custom_call" | custom-call | bytes 7077888 | tf_op jit(solution)/shard_map/pallas_call | solution.py:204
  43.5 0.0 collective-permute-done.17.refs_3_
  43.5 0.6 %collective-permute-done.16.refs_2_ = f32[4,512]{1,0:T(4,128)S(1)} collective-permute-done((f32[4,512]{1,0:T(4,128)S(1)}, f32[4,512]{1,0:T(4,128)S(1)}, u32[]{:S(2)}, u32[]{:S(2)}) %collective-permute-start.16) | collective-permute-done | bytes 8224 | tf_op jit(solution)/shard_map/ppermute | solution.py:32
  44.0 0.4 collective-permute-done.15.refs_1_
  44.4 0.0 collective-permute-done.18.refs_6_
  44.4 0.0 collective-permute-done.20.refs_9_
  44.4 7.2 %shard_map.87 = f32[4,4,96,256]{3,2,1,0:T(8,128)} custom-call(f32[24,256]{1,0:T(8,128)S(1)} %get-tuple-element.22.aux, f32[4,512]{1,0:T(4,128)S(1)} %pad_maximum_fusion.1.refs_0_, f32[4,512]{1,0:T(4,128)S(1)} %collective-permute-done.15.refs_1_, f32[4,512]{1,0:T(4,128)S(1)} %collective-permute-done.16.refs_2_, f32[4,512]{1,0:T(4,128)S(1)} %collective-permute-done.17.refs_3_, ...), custom_call_target="tpu_custom_call" | custom-call | flops 5435817984 | bytes 1048576 | tf_op jit(solution)/shard_map/pallas_call | solution.py:359
  (6 shorter events, 0.1 us)
Async XLA Ops:
  1.3 17.6 %collective-permute-start.9 = (bf16[2,4,96,256]{3,2,1,0:T(8,128)(2,1)S(1)}, bf16[2,4,96,256]{3,2,1,0:T(8,128)(2,1)S(1)}, u32[]{:S(2)}, u32[]{:S(2)}) collective-permute-start(bf16[2,4,96,256]{3,2,1,0:T(8,128)(2,1)S(1)} %get-tuple-element.27), channel_id=1, source_target_pairs={{0,2},{2,4},{4,6},{6,8},{8,10},{10,12},{12,14},{14,16},{16,18},{18... | collective-permute-start | bytes 1179656 | tf_op jit(solution)/shard_map/ppermute | solution.py:37
  4.3 1.2 %collective-permute-start = (f32[1,512]{1,0:T(1,128)S(1)}, f32[1,512]{1,0:T(1,128)S(1)}, u32[]{:S(2)}, u32[]{:S(2)}) collective-permute-start(f32[1,512]{1,0:T(1,128)S(1)} %get-tuple-element.21), channel_id=1, source_target_pairs={{0,1},{1,0},{2,3},{3,2},{4,5},{5,4},{6,7},{7,6},{8,9},{9,8},{10,11... | collective-permute-start | bytes 6152 | tf_op jit(solution)/shard_map/ppermute | solution.py:32
  5.5 6.5 %collective-permute-start.3 = (f32[1,512]{1,0:T(1,128)S(1)}, f32[1,512]{1,0:T(1,128)S(1)}, u32[]{:S(2)}, u32[]{:S(2)}) collective-permute-start(f32[1,512]{1,0:T(1,128)S(1)} %add.10.refs_4_), channel_id=1, source_target_pairs={{0,24},{2,26},{4,28},{6,30},{8,16},{10,18},{12,20},{14,22},{16,8},... | collective-permute-start | bytes 6152 | tf_op jit(solution)/shard_map/ppermute | solution.py:32
  9.1 4.5 %collective-permute-start.2 = (f32[1,512]{1,0:T(1,128)S(1)}, f32[1,512]{1,0:T(1,128)S(1)}, u32[]{:S(2)}, u32[]{:S(2)}) collective-permute-start(f32[1,512]{1,0:T(1,128)S(1)} %add.10.refs_4_), channel_id=1, source_target_pairs={{0,16},{2,18},{4,20},{6,22},{8,24},{10,26},{12,28},{14,30},{16,0},... | collective-permute-start | bytes 6152 | tf_op jit(solution)/shard_map/ppermute | solution.py:32
  9.1 4.5 %collective-permute-start.1 = (f32[1,512]{1,0:T(1,128)S(1)}, f32[1,512]{1,0:T(1,128)S(1)}, u32[]{:S(2)}, u32[]{:S(2)}) collective-permute-start(f32[1,512]{1,0:T(1,128)S(1)} %add.10.refs_4_), channel_id=1, source_target_pairs={{0,8},{2,10},{4,12},{6,14},{8,0},{10,2},{12,4},{14,6},{16,24},{18,... | collective-permute-start | bytes 6152 | tf_op jit(solution)/shard_map/ppermute | solution.py:32
  9.9 12.0 %collective-permute-start.7 = (bf16[4,1,96,256]{3,2,1,0:T(8,128)(2,1)S(1)}, bf16[4,1,96,256]{3,2,1,0:T(8,128)(2,1)S(1)}, u32[]{:S(2)}, u32[]{:S(2)}) collective-permute-start(bf16[4,1,96,256]{3,2,1,0:T(8,128)(2,1)S(1)} %get-tuple-element.24), channel_id=1, source_target_pairs={{0,1},{1,0},{2,3},{3,2},{4,5},{5,4},{6,7},{7,6},{8,9},{9,8},{10,11... | collective-permute-start | bytes 589832 | tf_op jit(solution)/shard_map/ppermute | solution.py:32
  13.6 6.3 %collective-permute-start.6 = (f32[4,512]{1,0:T(4,128)S(1)}, f32[4,512]{1,0:T(4,128)S(1)}, u32[]{:S(2)}, u32[]{:S(2)}) collective-permute-start(f32[4,512]{1,0:T(4,128)S(1)} %pad_maximum_fusion.refs_0_), channel_id=1, source_target_pairs={{0,6},{2,4},{4,2},{6,0},{8,14},{10,12},{12,10},{14,8},{16,22},{18,... | collective-permute-start | bytes 24584 | tf_op jit(solution)/shard_map/ppermute | solution.py:32
  18.2 3.7 %collective-permute-start.5 = (f32[4,512]{1,0:T(4,128)S(1)}, f32[4,512]{1,0:T(4,128)S(1)}, u32[]{:S(2)}, u32[]{:S(2)}) collective-permute-start(f32[4,512]{1,0:T(4,128)S(1)} %pad_maximum_fusion.refs_0_), channel_id=1, source_target_pairs={{0,4},{2,6},{4,0},{6,2},{8,12},{10,14},{12,8},{14,10},{16,20},{18,... | collective-permute-start | bytes 24584 | tf_op jit(solution)/shard_map/ppermute | solution.py:32
  18.2 3.7 %collective-permute-start.4 = (f32[4,512]{1,0:T(4,128)S(1)}, f32[4,512]{1,0:T(4,128)S(1)}, u32[]{:S(2)}, u32[]{:S(2)}) collective-permute-start(f32[4,512]{1,0:T(4,128)S(1)} %pad_maximum_fusion.refs_0_), channel_id=1, source_target_pairs={{0,2},{2,0},{4,6},{6,4},{8,10},{10,8},{12,14},{14,12},{16,18},{18,... | collective-permute-start | bytes 24584 | tf_op jit(solution)/shard_map/ppermute | solution.py:32
  18.9 7.0 %collective-permute-start.10 = (bf16[2,1,96,256]{3,2,1,0:T(8,128)(2,1)S(1)}, bf16[2,1,96,256]{3,2,1,0:T(8,128)(2,1)S(1)}, u32[]{:S(2)}, u32[]{:S(2)}) collective-permute-start(bf16[2,1,96,256]{3,2,1,0:T(8,128)(2,1)S(1)} %constant_dynamic-slice_fusion.1), channel_id=1, source_target_pairs={{0,1},{1,0},{2,3},{3,2},{4,5},{5,4},{6,7},{7,6},{8,9},{9,8},{10,11... | collective-permute-start | bytes 294920 | tf_op jit(solution)/shard_map/ppermute | solution.py:32
  25.2 12.6 %collective-permute-start.8 = (bf16[2,4,96,256]{3,2,1,0:T(8,128)(2,1)S(1)}, bf16[2,4,96,256]{3,2,1,0:T(8,128)(2,1)S(1)}, u32[]{:S(2)}, u32[]{:S(2)}) collective-permute-start(bf16[2,4,96,256]{3,2,1,0:T(8,128)(2,1)S(1)} %get-tuple-element.26.refs_5_), channel_id=1, source_target_pairs={{0,2},{2,4},{4,6},{6,8},{8,10},{10,12},{12,14},{14,16},{16,18},{18... | collective-permute-start | bytes 1179656 | tf_op jit(solution)/shard_map/ppermute | solution.py:37
  28.9 1.2 %collective-permute-start.11 = (f32[1,512]{1,0:T(1,128)S(1)}, f32[1,512]{1,0:T(1,128)S(1)}, u32[]{:S(2)}, u32[]{:S(2)}) collective-permute-start(f32[1,512]{1,0:T(1,128)S(1)} %get-tuple-element.31), channel_id=1, source_target_pairs={{0,1},{1,0},{2,3},{3,2},{4,5},{5,4},{6,7},{7,6},{8,9},{9,8},{10,11... | collective-permute-start | bytes 6152 | tf_op jit(solution)/shard_map/ppermute | solution.py:32
  30.2 5.4 %collective-permute-start.14 = (f32[1,512]{1,0:T(1,128)S(1)}, f32[1,512]{1,0:T(1,128)S(1)}, u32[]{:S(2)}, u32[]{:S(2)}) collective-permute-start(f32[1,512]{1,0:T(1,128)S(1)} %add.12.after), channel_id=1, source_target_pairs={{0,24},{2,26},{4,28},{6,30},{8,16},{10,18},{12,20},{14,22},{16,8},... | collective-permute-start | bytes 6152 | tf_op jit(solution)/shard_map/ppermute | solution.py:32
  31.8 4.5 %collective-permute-start.13 = (f32[1,512]{1,0:T(1,128)S(1)}, f32[1,512]{1,0:T(1,128)S(1)}, u32[]{:S(2)}, u32[]{:S(2)}) collective-permute-start(f32[1,512]{1,0:T(1,128)S(1)} %add.12.after), channel_id=1, source_target_pairs={{0,16},{2,18},{4,20},{6,22},{8,24},{10,26},{12,28},{14,30},{16,0},... | collective-permute-start | bytes 6152 | tf_op jit(solution)/shard_map/ppermute | solution.py:32
  32.2 4.1 %collective-permute-start.12 = (f32[1,512]{1,0:T(1,128)S(1)}, f32[1,512]{1,0:T(1,128)S(1)}, u32[]{:S(2)}, u32[]{:S(2)}) collective-permute-start(f32[1,512]{1,0:T(1,128)S(1)} %add.12.after), channel_id=1, source_target_pairs={{0,8},{2,10},{4,12},{6,14},{8,0},{10,2},{12,4},{14,6},{16,24},{18,... | collective-permute-start | bytes 6152 | tf_op jit(solution)/shard_map/ppermute | solution.py:32
  34.5 6.2 %collective-permute-start.19 = (bf16[2,1,96,256]{3,2,1,0:T(8,128)(2,1)S(1)}, bf16[2,1,96,256]{3,2,1,0:T(8,128)(2,1)S(1)}, u32[]{:S(2)}, u32[]{:S(2)}) collective-permute-start(bf16[2,1,96,256]{3,2,1,0:T(8,128)(2,1)S(1)} %get-tuple-element.35), channel_id=1, source_target_pairs={{0,1},{1,0},{2,3},{3,2},{4,5},{5,4},{6,7},{7,6},{8,9},{9,8},{10,11... | collective-permute-start | bytes 294920 | tf_op jit(solution)/shard_map/ppermute | solution.py:32
  35.5 8.9 %collective-permute-start.18 = (bf16[2,1,96,256]{3,2,1,0:T(8,128)(2,1)S(1)}, bf16[2,1,96,256]{3,2,1,0:T(8,128)(2,1)S(1)}, u32[]{:S(2)}, u32[]{:S(2)}) collective-permute-start(bf16[2,1,96,256]{3,2,1,0:T(8,128)(2,1)S(1)} %get-tuple-element.34), channel_id=1, source_target_pairs={{0,1},{1,0},{2,3},{3,2},{4,5},{5,4},{6,7},{7,6},{8,9},{9,8},{10,11... | collective-permute-start | bytes 294920 | tf_op jit(solution)/shard_map/ppermute | solution.py:32
  37.8 6.6 %collective-permute-start.20 = (bf16[2,1,96,256]{3,2,1,0:T(8,128)(2,1)S(1)}, bf16[2,1,96,256]{3,2,1,0:T(8,128)(2,1)S(1)}, u32[]{:S(2)}, u32[]{:S(2)}) collective-permute-start(bf16[2,1,96,256]{3,2,1,0:T(8,128)(2,1)S(1)} %constant_dynamic-slice_fusion), channel_id=1, source_target_pairs={{0,1},{1,0},{2,3},{3,2},{4,5},{5,4},{6,7},{7,6},{8,9},{9,8},{10,11... | collective-permute-start | bytes 294920 | tf_op jit(solution)/shard_map/ppermute | solution.py:32
  37.9 5.6 %collective-permute-start.17 = (f32[4,512]{1,0:T(4,128)S(1)}, f32[4,512]{1,0:T(4,128)S(1)}, u32[]{:S(2)}, u32[]{:S(2)}) collective-permute-start(f32[4,512]{1,0:T(4,128)S(1)} %pad_maximum_fusion.1.refs_0_), channel_id=1, source_target_pairs={{0,6},{2,4},{4,2},{6,0},{8,14},{10,12},{12,10},{14,8},{16,22},{18,... | collective-permute-start | bytes 24584 | tf_op jit(solution)/shard_map/ppermute | solution.py:32
  40.4 3.7 %collective-permute-start.16 = (f32[4,512]{1,0:T(4,128)S(1)}, f32[4,512]{1,0:T(4,128)S(1)}, u32[]{:S(2)}, u32[]{:S(2)}) collective-permute-start(f32[4,512]{1,0:T(4,128)S(1)} %pad_maximum_fusion.1.refs_0_), channel_id=1, source_target_pairs={{0,4},{2,6},{4,0},{6,2},{8,12},{10,14},{12,8},{14,10},{16,20},{18,... | collective-permute-start | bytes 24584 | tf_op jit(solution)/shard_map/ppermute | solution.py:32
  40.7 3.7 %collective-permute-start.15 = (f32[4,512]{1,0:T(4,128)S(1)}, f32[4,512]{1,0:T(4,128)S(1)}, u32[]{:S(2)}, u32[]{:S(2)}) collective-permute-start(f32[4,512]{1,0:T(4,128)S(1)} %pad_maximum_fusion.1.refs_0_), channel_id=1, source_target_pairs={{0,2},{2,0},{4,6},{6,4},{8,10},{10,8},{12,14},{14,12},{16,18},{18,... | collective-permute-start | bytes 24584 | tf_op jit(solution)/shard_map/ppermute | solution.py:32

commit v8 on v7

--- a/solution.py
+++ b/solution.py
@@ -146,18 +146,17 @@
         out_specs=[VMEM] * len(outs),
         scratch_shapes=[pltpu.SemaphoreType.DMA((n_frames,))],
         compiler_params=vmem_params(),
-        cost_estimate=pl.CostEstimate(flops=4 * feats.size, bytes_accessed=4 * feats.size, transcendentals=0),
+        cost_estimate=pl.CostEstimate(flops=1 << 33, bytes_accessed=4 * feats.size, transcendentals=0),
     )(in_hbm(feats))
     return frames, tail, stats, edges
 
 
-def setup_kernel(slabs, per_slab, kernel_hbm, clips_hbm, *refs):
-    params_hbm, (_, taps, aux, params, clips, sems) = refs[:4], refs[4:]
+def setup_kernel(slabs, per_slab, clips_hbm, *refs):
+    params_hbm, (_, aux, params, clips, sems) = refs[:4], refs[4:]
     width = aux.shape[1]
-    taps_load = pltpu.make_async_copy(kernel_hbm, taps, sems.at[0])
-    clip_load = pltpu.make_async_copy(clips_hbm, clips, sems.at[1])
-    param_loads = [pltpu.make_async_copy(p, params.at[k], sems.at[2 + k]) for k, p in enumerate(params_hbm)]
-    for copy in [clip_load, *param_loads, taps_load]:
+    clip_load = pltpu.make_async_copy(clips_hbm, clips, sems.at[0])
+    param_loads = [pltpu.make_async_copy(p, params.at[k], sems.at[1 + k]) for k, p in enumerate(params_hbm)]
+    for copy in [clip_load, *param_loads]:
         copy.start()
     clip_load.wait()
     own = lax.axis_index("tm")
@@ -174,42 +173,23 @@
         copy.wait()
         aux[slabs + 2 + k : slabs + 3 + k] = params[k]
     aux[slabs + 6 : slabs + 8] = jnp.zeros((2, width), F32)
-    taps_load.wait()
-
-
-def setup_call(kernel, clip_ids, params, per_slab, after):
-    slabs, width = lax.axis_size("tm"), kernel.shape[4]
+
+
+def setup_call(clip_ids, params, per_slab, after):
+    slabs, width = lax.axis_size("tm"), params[0].shape[0]
     return pl.pallas_call(
         functools.partial(setup_kernel, slabs, per_slab),
-        out_shape=[shaped(kernel.shape), shaped((slabs + 8, width), F32)],
-        in_specs=[ANYWHERE] * 7,
-        out_specs=[VMEM, VMEM],
+        out_shape=shaped((slabs + 8, width), F32),
+        in_specs=[ANYWHERE] * 6,
+        out_specs=VMEM,
         scratch_shapes=[
             pltpu.VMEM((4, 1, width), F32),
             pltpu.SMEM(clip_ids.shape, jnp.int32),
-            pltpu.SemaphoreType.DMA((6,)),
+            pltpu.SemaphoreType.DMA((5,)),
         ],
         compiler_params=vmem_params(),
-        cost_estimate=pl.CostEstimate(flops=0, bytes_accessed=4 * kernel.size, transcendentals=0),
-    )(*[in_hbm(x) for x in (kernel, clip_ids, *[p[None] for p in params])], after)
-
-
-def load_kernel(kernel_hbm, after, taps, sem):
-    copy = pltpu.make_async_copy(kernel_hbm, taps, sem)
-    copy.start()
-    copy.wait()
-
-
-def load_call(kernel, after):
-    return pl.pallas_call(
-        load_kernel,
-        out_shape=shaped(kernel.shape),
-        in_specs=[ANYWHERE, ANYWHERE],
-        out_specs=VMEM,
-        scratch_shapes=[pltpu.SemaphoreType.DMA],
-        compiler_params=vmem_params(),
-        cost_estimate=pl.CostEstimate(flops=0, bytes_accessed=4 * kernel.size, transcendentals=0),
-    )(in_hbm(kernel), after)
+        cost_estimate=pl.CostEstimate(flops=0, bytes_accessed=1 << 16, transcendentals=0),
+    )(*[in_hbm(x) for x in (clip_ids, *[p[None] for p in params])], after)
 
 
 def group_total(values):
@@ -328,7 +308,8 @@
     tables, early, late, refs = refs[:n_tables], refs[n_tables], refs[n_tables + 1], refs[n_tables + 2 :]
     sides_early, sides_late = refs[:n_sides], refs[n_sides : 2 * n_sides]
     before, *corners = refs[2 * n_sides : 3 * n_sides + 1]
-    taps, feats, out, act = refs[3 * n_sides + 1 :]
+    taps, feats, out_hbm, act, out, sems = refs[3 * n_sides + 1 :]
+    stores = [pltpu.make_async_copy(out.at[f], out_hbm.at[f], sems.at[f]) for f in range(out.shape[0])]
     slabs = aux.shape[0] - 8
     starting = aux[slabs : slabs + 1] != 0.0
     affine = half_affine(tables, aux, 1)
@@ -347,12 +328,14 @@
     for frame in range(2, n_frames + 2):
         fill(frame)
     for frame in list(range(2, n_frames)) + [0, 1]:
-        if frame < 2:
-            fill(frame)
         if frame == 0:
+            fill(0)
             fill(1)
         for row, value in conv_rows([(act, frame + i) for i in range(3)], taps):
             out[frame, row] = feats[frame, row].astype(F32) + value
+        stores[frame].start()
+    for store in stores:
+        store.wait()
 
 
 def call(kernel, outs, scratch, frames, *operands):
@@ -360,7 +343,7 @@
         kernel,
         out_shape=outs,
         in_specs=[VMEM] * len(operands),
-        out_specs=[VMEM] * len(outs) if isinstance(outs, list) else VMEM,
+        out_specs=[VMEM] * len(outs) if isinstance(outs, list) else ANYWHERE,
         scratch_shapes=scratch,
         compiler_params=vmem_params(),
         cost_estimate=pl.CostEstimate(flops=54 * frames * 384 * 65536, bytes_accessed=1 << 20, transcendentals=1 << 20),
@@ -375,7 +358,7 @@
     total, tables = slab_tables(stats)
     sides = row_halo(edges)
     per_slab = feats.size // GROUPS * lax.axis_size("space")
-    taps, aux = setup_call(kernel_one, clip_ids, params, per_slab, total)
+    aux = setup_call(clip_ids, params, per_slab, total)
     n_sides = len(sides)
     plane = (n_rows + 2, cols, width)
     late = n_frames - 2
@@ -384,24 +367,23 @@
         [shaped((late, n_rows, cols, width)), shaped((2,) + plane), shaped((1, 2 * width), F32), shaped((2, width), F32)]
         + edge_shapes(feats, late),
         [pltpu.VMEM((late,) + plane, BF16)],
-        late, aux, *tables, frames, *sides, taps,
+        late, aux, *tables, frames, *sides, kernel_one,
     )
     sides_late = row_halo(edges)
     hidden_early, stats, *edges = call(
         functools.partial(early_kernel, n_sides),
         [shaped((2, n_rows, cols, width)), shaped((1, 2 * width), F32)] + edge_shapes(feats, 2),
         [pltpu.VMEM((2,) + plane, BF16)],
-        2, aux, before, *corners, act_low, affine, stats, taps,
+        2, aux, before, *corners, act_low, affine, stats, kernel_one,
     )
     sides_early = row_halo(edges)
     total, tables = slab_tables(stats)
     before, corners, tables[0] = slab_halo(hidden_late[late - 2 :], tables[0])
-    taps = load_call(kernel_two, total)
     return call(
         functools.partial(last_kernel, len(tables), n_sides),
         shaped(feats.shape, F32),
-        [pltpu.VMEM((n_frames + 2,) + plane, BF16)],
-        n_frames, aux, *tables, hidden_early, hidden_late, *sides_early, *sides_late, before, *corners, taps, frames,
+        [pltpu.VMEM((n_frames + 2,) + plane, BF16), pltpu.VMEM(feats.shape, F32), pltpu.SemaphoreType.DMA((n_frames,))],
+        n_frames, aux, *tables, hidden_early, hidden_late, *sides_early, *sides_late, before, *corners, kernel_two, frames,
     )
 
 

time: 51.8 us -> 53.3 us (1.029)
  Pallas kernels: 19 us -> 15 us
  waiting for transfers between devices: 11 us -> 14.3 us
  local copies, waits for them, and re-layouts: 0.01 us -> 2.02 us
    ppermute x19, waiting for transfers between devices: 9.41 us -> 12.7 us  [traded(): lax.ppermute(value, axis, [(i, i ^ mask) for i in range(lax.axis_size(axi...]
    pallas_call x1 -> x0, Pallas kernels: 2.01 us -> none  [load_call(): pl.pallas_call(load_kernel, out_shape=shaped(kernel.shape), in_specs=[ANY...]
    unnamed x0 -> x6, local copies, waits for them, and re-layouts: none -> 2.01 us
    pallas_call x1, Pallas kernels: 2.12 us -> 0.77 us  [setup_call(): pl.pallas_call(functools.partial(setup_kernel, slabs, per_slab), out_shap...]
    pallas_call x3, Pallas kernels: 13.5 us -> 13 us  [call(): pl.pallas_call(kernel, out_shape=outs, in_specs=[VMEM] * len(operands), o...]
  transfers between devices with their start and end apart: 21 -> 21, of which waited for: 10 -> 12; matrix products, arithmetic and copies ran while one was open for 0% -> 0% of each run, Pallas kernels for 20% -> 13%
where the time goes in v8:
time: 53.3 us; the launch traced here: 53.1 us
  starting transfers between devices  21.5 us (40%)
  Pallas kernels  15 us (28%)
  waiting for transfers between devices  14.3 us (27%)
  local copies, waits for them, and re-layouts  2.02 us (4%)
    ppermute x19, starting transfers between devices, traded(): lax.ppermute(value, axis, [(i, i ^ mask) for i in range(lax.axis_size(axi...  17.9 us
    pallas_call x3, Pallas kernels, call(): pl.pallas_call(kernel, out_shape=outs, in_specs=[VMEM] * len(operands), o...  13 us
    ppermute x19, waiting for transfers between devices, traded(): lax.ppermute(value, axis, [(i, i ^ mask) for i in range(lax.axis_size(axi...  12.7 us
    ppermute x2, starting transfers between devices, shifted(): lax.ppermute(value, axis, [(i, (i + step) % peers) for i in range(peers)])  3.68 us
    unnamed x6, local copies, waits for them, and re-layouts  2.01 us
    ppermute x2, waiting for transfers between devices, shifted(): lax.ppermute(value, axis, [(i, (i + step) % peers) for i in range(peers)])  1.6 us
    pallas_call x1, Pallas kernels, entry_call(): pl.pallas_call(entry_kernel, out_shape=outs, in_specs=[ANYWHERE], out_spe...  1.3 us
  transfers between devices with their start and end apart: 21, of which 12 were waited for; matrix products, arithmetic and copies ran while one was open for 0% of the time, Pallas kernels for 13%

profile of v8, /device:TPU:0, one launch (start us, length us, event | category | flops | bytes accessed | tf_op | source)
XLA Modules:
  0.0 53.1 jit_solution(8596192820043024621)
XLA Ops:
  0.0 1.3 %shard_map.82 = (bf16[4,4,96,256]{3,2,1,0:T(8,128)(2,1)S(1)}, bf16[2,4,96,256]{3,2,1,0:T(8,128)(2,1)S(1)}, f32[1,512]{1,0:T(1,128)S(1)}, bf16[4,1,96,256]{3,2,1,0:T(8,128)(2,1)S(1)}) custom-call(bf16[4,4,96,256]{3,2,1,0:T(8,128)(2,1)} %feats_hbm.1), custom_call_target="tpu_custom_call" | custom-call | flops 8589934592 | bytes 1572864 | tf_op jit(solution)/shard_map/pallas_call | solution.py:142
  1.3 3.0 %collective-permute-start.9 = (bf16[2,4,96,256]{3,2,1,0:T(8,128)(2,1)S(1)}, bf16[2,4,96,256]{3,2,1,0:T(8,128)(2,1)S(1)}, u32[]{:S(2)}, u32[]{:S(2)}) collective-permute-start(bf16[2,4,96,256]{3,2,1,0:T(8,128)(2,1)S(1)} %get-tuple-element.23), channel_id=1, source_target_pairs={{0,2},{2,4},{4,6},{6,8},{8,10},{10,12},{12,14},{14,16},{16,18},{18... | collective-permute-start | bytes 1179656 | tf_op jit(solution)/shard_map/ppermute | solution.py:37
  4.3 0.0 collective-permute-start
  4.3 1.2 %collective-permute-done = f32[1,512]{1,0:T(1,128)S(1)} collective-permute-done((f32[1,512]{1,0:T(1,128)S(1)}, f32[1,512]{1,0:T(1,128)S(1)}, u32[]{:S(2)}, u32[]{:S(2)}) %collective-permute-start) | collective-permute-done | bytes 2080 | tf_op jit(solution)/shard_map/ppermute | solution.py:32
  5.5 3.6 %collective-permute-start.3 = (f32[1,512]{1,0:T(1,128)S(1)}, f32[1,512]{1,0:T(1,128)S(1)}, u32[]{:S(2)}, u32[]{:S(2)}) collective-permute-start(f32[1,512]{1,0:T(1,128)S(1)} %add.10.refs_4_), channel_id=1, source_target_pairs={{0,24},{2,26},{4,28},{6,30},{8,16},{10,18},{12,20},{14,22},{16,8},... | collective-permute-start | bytes 6152 | tf_op jit(solution)/shard_map/ppermute | solution.py:32
  9.1 0.0 collective-permute-start.2
  9.1 0.8 %collective-permute-start.1 = (f32[1,512]{1,0:T(1,128)S(1)}, f32[1,512]{1,0:T(1,128)S(1)}, u32[]{:S(2)}, u32[]{:S(2)}) collective-permute-start(f32[1,512]{1,0:T(1,128)S(1)} %add.10.refs_4_), channel_id=1, source_target_pairs={{0,8},{2,10},{4,12},{6,14},{8,0},{10,2},{12,4},{14,6},{16,24},{18,... | collective-permute-start | bytes 6152 | tf_op jit(solution)/shard_map/ppermute | solution.py:32
  9.9 0.0 collective-permute-start.7
  9.9 0.8 %shard_map.83.aux = f32[24,256]{1,0:T(8,128)S(1)} custom-call(s32[16]{0:T(128)} %clips_hbm.1, f32[1,256]{1,0:T(1,128)} %bitcast.4, f32[1,256]{1,0:T(1,128)} %bitcast.5, f32[1,256]{1,0:T(1,128)} %bitcast.6, f32[1,256]{1,0:T(1,128)} %bitcast.7, f32[1,512]{1,0:T(1,128)S(1)} %add.10.refs_4_), custom_call_target="tpu_custom_call" | custom-call | bytes 65536 | tf_op jit(solution)/shard_map/pallas_call | solution.py:180
  10.6 0.2 collective-permute-done.3
  10.8 2.7 %collective-permute-done.2 = f32[1,512]{1,0:T(1,128)S(1)} collective-permute-done((f32[1,512]{1,0:T(1,128)S(1)}, f32[1,512]{1,0:T(1,128)S(1)}, u32[]{:S(2)}, u32[]{:S(2)}) %collective-permute-start.2) | collective-permute-done | bytes 2080 | tf_op jit(solution)/shard_map/ppermute | solution.py:32
  13.6 0.0 collective-permute-done.1
  13.6 4.7 %collective-permute-start.6 = (f32[4,512]{1,0:T(4,128)S(1)}, f32[4,512]{1,0:T(4,128)S(1)}, u32[]{:S(2)}, u32[]{:S(2)}) collective-permute-start(f32[4,512]{1,0:T(4,128)S(1)} %pad_maximum_fusion.refs_0_), channel_id=1, source_target_pairs={{0,6},{2,4},{4,2},{6,0},{8,14},{10,12},{12,10},{14,8},{16,22},{18,... | collective-permute-start | bytes 24584 | tf_op jit(solution)/shard_map/ppermute | solution.py:32
  18.2 0.0 collective-permute-start.5
  18.2 0.6 %collective-permute-start.4 = (f32[4,512]{1,0:T(4,128)S(1)}, f32[4,512]{1,0:T(4,128)S(1)}, u32[]{:S(2)}, u32[]{:S(2)}) collective-permute-start(f32[4,512]{1,0:T(4,128)S(1)} %pad_maximum_fusion.refs_0_), channel_id=1, source_target_pairs={{0,2},{2,0},{4,6},{6,4},{8,10},{10,8},{12,14},{14,12},{16,18},{18,... | collective-permute-start | bytes 24584 | tf_op jit(solution)/shard_map/ppermute | solution.py:32
  18.9 0.0 collective-permute-done.9.before
  18.9 0.1 collective-permute-start.10
  19.0 0.9 %collective-permute-done.6.refs_3_ = f32[4,512]{1,0:T(4,128)S(1)} collective-permute-done((f32[4,512]{1,0:T(4,128)S(1)}, f32[4,512]{1,0:T(4,128)S(1)}, u32[]{:S(2)}, u32[]{:S(2)}) %collective-permute-start.6) | collective-permute-done | bytes 8224 | tf_op jit(solution)/shard_map/ppermute | solution.py:32
  19.9 2.0 %collective-permute-done.5.refs_2_ = f32[4,512]{1,0:T(4,128)S(1)} collective-permute-done((f32[4,512]{1,0:T(4,128)S(1)}, f32[4,512]{1,0:T(4,128)S(1)}, u32[]{:S(2)}, u32[]{:S(2)}) %collective-permute-start.5) | collective-permute-done | bytes 8224 | tf_op jit(solution)/shard_map/ppermute | solution.py:32
  21.9 0.0 collective-permute-done.4.refs_1_
  21.9 0.0 collective-permute-done.7.refs_5_
  21.9 0.0 copy-start
  21.9 2.0 %copy-done = bf16[3,3,3,256,256]{4,3,2,1,0:T(8,128)(2,1)S(1)} copy-done((bf16[3,3,3,256,256]{4,3,2,1,0:T(8,128)(2,1)S(1)}, bf16[3,3,3,256,256]{4,3,2,1,0:T(8,128)(2,1)}, u32[]{:S(2)}) %copy-start) | copy-done | bytes 3538968
  23.9 0.0 copy-start.1
  23.9 3.3 %shard_map.84 = (bf16[2,4,96,256]{3,2,1,0:T(8,128)(2,1)S(1)}, bf16[2,6,96,256]{3,2,1,0:T(8,128)(2,1)S(1)}, f32[1,512]{1,0:T(1,128)S(1)}, f32[2,256]{1,0:T(2,128)S(1)}, bf16[2,1,96,256]{3,2,1,0:T(8,128)(2,1)S(1)}) custom-call(f32[24,256]{1,0:T(8,128)S(1)} %shard_map.83.aux, f32[4,512]{1,0:T(4,128)S(1)} %pad_maximum_fusion.refs_0_, ...), custom_call_target="tpu_custom_call" | custom-call | flops 2717908992 | bytes 1048576 | tf_op jit(solution)/shard_map/pallas_call | solution.py:342
  27.2 0.7 %collective-permute-start.8 = (bf16[2,4,96,256]{3,2,1,0:T(8,128)(2,1)S(1)}, bf16[2,4,96,256]{3,2,1,0:T(8,128)(2,1)S(1)}, u32[]{:S(2)}, u32[]{:S(2)}) collective-permute-start(bf16[2,4,96,256]{3,2,1,0:T(8,128)(2,1)S(1)} %get-tuple-element.22.refs_5_), channel_id=1, source_target_pairs={{0,2},{2,4},{4,6},{6,8},{8,10},{10,12},{12,14},{14,16},{16,18},{18... | collective-permute-start | bytes 1179656 | tf_op jit(solution)/shard_map/ppermute | solution.py:37
  27.9 0.0 collective-permute-done.10.refs_0_
  27.9 0.0 copy-done.1
  27.9 0.0 copy-start.2
  27.9 3.0 %shard_map.85 = (bf16[2,4,96,256]{3,2,1,0:T(8,128)(2,1)S(1)}, f32[1,512]{1,0:T(1,128)S(1)}, bf16[2,1,96,256]{3,2,1,0:T(8,128)(2,1)S(1)}) custom-call(f32[24,256]{1,0:T(8,128)S(1)} %shard_map.83.aux, bf16[2,4,96,256]{3,2,1,0:T(8,128)(2,1)S(1)} %collective-permute-done.9.before, bf16[2,1,96,256]{3,2,1,0:T(8,128)(2,1)S(1)} %collective-permute-done.10.refs_0_, ...), custom_call_target="tpu_custom_call" | custom-call | flops 2717908992 | bytes 1048576 | tf_op jit(solution)/shard_map/pallas_call | solution.py:342
  30.9 0.1 collective-permute-start.11
  30.9 1.1 %collective-permute-done.11 = f32[1,512]{1,0:T(1,128)S(1)} collective-permute-done((f32[1,512]{1,0:T(1,128)S(1)}, f32[1,512]{1,0:T(1,128)S(1)}, u32[]{:S(2)}, u32[]{:S(2)}) %collective-permute-start.11) | collective-permute-done | bytes 2080 | tf_op jit(solution)/shard_map/ppermute | solution.py:32
  32.1 1.6 %collective-permute-start.14 = (f32[1,512]{1,0:T(1,128)S(1)}, f32[1,512]{1,0:T(1,128)S(1)}, u32[]{:S(2)}, u32[]{:S(2)}) collective-permute-start(f32[1,512]{1,0:T(1,128)S(1)} %add.12), channel_id=1, source_target_pairs={{0,24},{2,26},{4,28},{6,30},{8,16},{10,18},{12,20},{14,22},{16,8},... | collective-permute-start | bytes 6152 | tf_op jit(solution)/shard_map/ppermute | solution.py:32
  33.7 0.4 collective-permute-start.13
  34.1 2.4 %collective-permute-start.12 = (f32[1,512]{1,0:T(1,128)S(1)}, f32[1,512]{1,0:T(1,128)S(1)}, u32[]{:S(2)}, u32[]{:S(2)}) collective-permute-start(f32[1,512]{1,0:T(1,128)S(1)} %add.12), channel_id=1, source_target_pairs={{0,8},{2,10},{4,12},{6,14},{8,0},{10,2},{12,4},{14,6},{16,24},{18,... | collective-permute-start | bytes 6152 | tf_op jit(solution)/shard_map/ppermute | solution.py:32
  36.5 0.0 collective-permute-start.19
  36.5 1.0 %collective-permute-done.14 = f32[1,512]{1,0:T(1,128)S(1)} collective-permute-done((f32[1,512]{1,0:T(1,128)S(1)}, f32[1,512]{1,0:T(1,128)S(1)}, u32[]{:S(2)}, u32[]{:S(2)}) %collective-permute-start.14) | collective-permute-done | bytes 2080 | tf_op jit(solution)/shard_map/ppermute | solution.py:32
  37.5 0.0 collective-permute-start.18
  37.5 0.7 %collective-permute-done.13 = f32[1,512]{1,0:T(1,128)S(1)} collective-permute-done((f32[1,512]{1,0:T(1,128)S(1)}, f32[1,512]{1,0:T(1,128)S(1)}, u32[]{:S(2)}, u32[]{:S(2)}) %collective-permute-start.13) | collective-permute-done | bytes 2080 | tf_op jit(solution)/shard_map/ppermute | solution.py:32
  38.2 0.0 collective-permute-done.12
  38.2 1.6 %collective-permute-done.8.refs_8_ = bf16[2,4,96,256]{3,2,1,0:T(8,128)(2,1)S(1)} collective-permute-done((bf16[2,4,96,256]{3,2,1,0:T(8,128)(2,1)S(1)}, bf16[2,4,96,256]{3,2,1,0:T(8,128)(2,1)S(1)}, u32[]{:S(2)}, u32[]{:S(2)}) %collective-permute-start.8) | collective-permute-done | bytes 393248 | tf_op jit(solution)/shard_map/ppermute | solution.py:37
  39.8 0.1 collective-permute-start.20
  39.9 2.4 %collective-permute-start.17 = (f32[4,512]{1,0:T(4,128)S(1)}, f32[4,512]{1,0:T(4,128)S(1)}, u32[]{:S(2)}, u32[]{:S(2)}) collective-permute-start(f32[4,512]{1,0:T(4,128)S(1)} %pad_maximum_fusion.1.refs_0_), channel_id=1, source_target_pairs={{0,6},{2,4},{4,2},{6,0},{8,14},{10,12},{12,10},{14,8},{16,22},{18,... | collective-permute-start | bytes 24584 | tf_op jit(solution)/shard_map/ppermute | solution.py:32
  42.3 0.4 collective-permute-start.16
  42.7 0.0 collective-permute-done.19.refs_7_
  42.7 0.8 %collective-permute-start.15 = (f32[4,512]{1,0:T(4,128)S(1)}, f32[4,512]{1,0:T(4,128)S(1)}, u32[]{:S(2)}, u32[]{:S(2)}) collective-permute-start(f32[4,512]{1,0:T(4,128)S(1)} %pad_maximum_fusion.1.refs_0_), channel_id=1, source_target_pairs={{0,2},{2,0},{4,6},{6,4},{8,10},{10,8},{12,14},{14,12},{16,18},{18,... | collective-permute-start | bytes 24584 | tf_op jit(solution)/shard_map/ppermute | solution.py:32
  43.5 1.1 %collective-permute-done.17.refs_3_ = f32[4,512]{1,0:T(4,128)S(1)} collective-permute-done((f32[4,512]{1,0:T(4,128)S(1)}, f32[4,512]{1,0:T(4,128)S(1)}, u32[]{:S(2)}, u32[]{:S(2)}) %collective-permute-start.17) | collective-permute-done | bytes 8224 | tf_op jit(solution)/shard_map/ppermute | solution.py:32
  44.5 1.5 %collective-permute-done.16.refs_2_ = f32[4,512]{1,0:T(4,128)S(1)} collective-permute-done((f32[4,512]{1,0:T(4,128)S(1)}, f32[4,512]{1,0:T(4,128)S(1)}, u32[]{:S(2)}, u32[]{:S(2)}) %collective-permute-start.16) | collective-permute-done | bytes 8224 | tf_op jit(solution)/shard_map/ppermute | solution.py:32
  46.0 0.4 collective-permute-done.15.refs_1_
  46.4 0.0 collective-permute-done.18.refs_6_
  46.4 0.0 collective-permute-done.20.refs_9_
  46.4 0.0 copy-done.2
  46.4 6.7 %shard_map.86 = f32[4,4,96,256]{3,2,1,0:T(8,128)} custom-call(f32[24,256]{1,0:T(8,128)S(1)} %shard_map.83.aux, f32[4,512]{1,0:T(4,128)S(1)} %pad_maximum_fusion.1.refs_0_, f32[4,512]{1,0:T(4,128)S(1)} %collective-permute-done.15.refs_1_, f32[4,512]{1,0:T(4,128)S(1)} %collective-permute-done.16.refs_2_, f32[4,512]{1,0:T(4,128)S(1)} %collective-permute-done.17.refs_3_, ...), custom_call_target="tpu_custom_call" | custom-call | flops 5435817984 | bytes 1048576 | tf_op jit(solution)/shard_map/pallas_call | solution.py:342
  (6 shorter events, 0.1 us)
Async XLA Ops:
  1.3 17.6 %collective-permute-start.9 = (bf16[2,4,96,256]{3,2,1,0:T(8,128)(2,1)S(1)}, bf16[2,4,96,256]{3,2,1,0:T(8,128)(2,1)S(1)}, u32[]{:S(2)}, u32[]{:S(2)}) collective-permute-start(bf16[2,4,96,256]{3,2,1,0:T(8,128)(2,1)S(1)} %get-tuple-element.23), channel_id=1, source_target_pairs={{0,2},{2,4},{4,6},{6,8},{8,10},{10,12},{12,14},{14,16},{16,18},{18... | collective-permute-start | bytes 1179656 | tf_op jit(solution)/shard_map/ppermute | solution.py:37
  4.3 1.2 %collective-permute-start = (f32[1,512]{1,0:T(1,128)S(1)}, f32[1,512]{1,0:T(1,128)S(1)}, u32[]{:S(2)}, u32[]{:S(2)}) collective-permute-start(f32[1,512]{1,0:T(1,128)S(1)} %get-tuple-element.19), channel_id=1, source_target_pairs={{0,1},{1,0},{2,3},{3,2},{4,5},{5,4},{6,7},{7,6},{8,9},{9,8},{10,11... | collective-permute-start | bytes 6152 | tf_op jit(solution)/shard_map/ppermute | solution.py:32
  5.5 5.4 %collective-permute-start.3 = (f32[1,512]{1,0:T(1,128)S(1)}, f32[1,512]{1,0:T(1,128)S(1)}, u32[]{:S(2)}, u32[]{:S(2)}) collective-permute-start(f32[1,512]{1,0:T(1,128)S(1)} %add.10.refs_4_), channel_id=1, source_target_pairs={{0,24},{2,26},{4,28},{6,30},{8,16},{10,18},{12,20},{14,22},{16,8},... | collective-permute-start | bytes 6152 | tf_op jit(solution)/shard_map/ppermute | solution.py:32
  9.1 4.5 %collective-permute-start.2 = (f32[1,512]{1,0:T(1,128)S(1)}, f32[1,512]{1,0:T(1,128)S(1)}, u32[]{:S(2)}, u32[]{:S(2)}) collective-permute-start(f32[1,512]{1,0:T(1,128)S(1)} %add.10.refs_4_), channel_id=1, source_target_pairs={{0,16},{2,18},{4,20},{6,22},{8,24},{10,26},{12,28},{14,30},{16,0},... | collective-permute-start | bytes 6152 | tf_op jit(solution)/shard_map/ppermute | solution.py:32
  9.1 4.5 %collective-permute-start.1 = (f32[1,512]{1,0:T(1,128)S(1)}, f32[1,512]{1,0:T(1,128)S(1)}, u32[]{:S(2)}, u32[]{:S(2)}) collective-permute-start(f32[1,512]{1,0:T(1,128)S(1)} %add.10.refs_4_), channel_id=1, source_target_pairs={{0,8},{2,10},{4,12},{6,14},{8,0},{10,2},{12,4},{14,6},{16,24},{18,... | collective-permute-start | bytes 6152 | tf_op jit(solution)/shard_map/ppermute | solution.py:32
  9.9 12.0 %collective-permute-start.7 = (bf16[4,1,96,256]{3,2,1,0:T(8,128)(2,1)S(1)}, bf16[4,1,96,256]{3,2,1,0:T(8,128)(2,1)S(1)}, u32[]{:S(2)}, u32[]{:S(2)}) collective-permute-start(bf16[4,1,96,256]{3,2,1,0:T(8,128)(2,1)S(1)} %get-tuple-element.21), channel_id=1, source_target_pairs={{0,1},{1,0},{2,3},{3,2},{4,5},{5,4},{6,7},{7,6},{8,9},{9,8},{10,11... | collective-permute-start | bytes 589832 | tf_op jit(solution)/shard_map/ppermute | solution.py:32
  13.6 6.3 %collective-permute-start.6 = (f32[4,512]{1,0:T(4,128)S(1)}, f32[4,512]{1,0:T(4,128)S(1)}, u32[]{:S(2)}, u32[]{:S(2)}) collective-permute-start(f32[4,512]{1,0:T(4,128)S(1)} %pad_maximum_fusion.refs_0_), channel_id=1, source_target_pairs={{0,6},{2,4},{4,2},{6,0},{8,14},{10,12},{12,10},{14,8},{16,22},{18,... | collective-permute-start | bytes 24584 | tf_op jit(solution)/shard_map/ppermute | solution.py:32
  18.2 3.7 %collective-permute-start.5 = (f32[4,512]{1,0:T(4,128)S(1)}, f32[4,512]{1,0:T(4,128)S(1)}, u32[]{:S(2)}, u32[]{:S(2)}) collective-permute-start(f32[4,512]{1,0:T(4,128)S(1)} %pad_maximum_fusion.refs_0_), channel_id=1, source_target_pairs={{0,4},{2,6},{4,0},{6,2},{8,12},{10,14},{12,8},{14,10},{16,20},{18,... | collective-permute-start | bytes 24584 | tf_op jit(solution)/shard_map/ppermute | solution.py:32
  18.2 3.7 %collective-permute-start.4 = (f32[4,512]{1,0:T(4,128)S(1)}, f32[4,512]{1,0:T(4,128)S(1)}, u32[]{:S(2)}, u32[]{:S(2)}) collective-permute-start(f32[4,512]{1,0:T(4,128)S(1)} %pad_maximum_fusion.refs_0_), channel_id=1, source_target_pairs={{0,2},{2,0},{4,6},{6,4},{8,10},{10,8},{12,14},{14,12},{16,18},{18,... | collective-permute-start | bytes 24584 | tf_op jit(solution)/shard_map/ppermute | solution.py:32
  18.9 9.0 %collective-permute-start.10 = (bf16[2,1,96,256]{3,2,1,0:T(8,128)(2,1)S(1)}, bf16[2,1,96,256]{3,2,1,0:T(8,128)(2,1)S(1)}, u32[]{:S(2)}, u32[]{:S(2)}) collective-permute-start(bf16[2,1,96,256]{3,2,1,0:T(8,128)(2,1)S(1)} %constant_dynamic-slice_fusion.1), channel_id=1, source_target_pairs={{0,1},{1,0},{2,3},{3,2},{4,5},{5,4},{6,7},{7,6},{8,9},{9,8},{10,11... | collective-permute-start | bytes 294920 | tf_op jit(solution)/shard_map/ppermute | solution.py:32
  21.9 2.0 %copy-start = (bf16[3,3,3,256,256]{4,3,2,1,0:T(8,128)(2,1)S(1)}, bf16[3,3,3,256,256]{4,3,2,1,0:T(8,128)(2,1)}, u32[]{:S(2)}) copy-start(bf16[3,3,3,256,256]{4,3,2,1,0:T(8,128)(2,1)} %refs_4_.1) | copy-start | bytes 10616836
  23.9 4.0 %copy-start.1 = (bf16[3,3,3,256,256]{4,3,2,1,0:T(8,128)(2,1)S(1)}, bf16[3,3,3,256,256]{4,3,2,1,0:T(8,128)(2,1)}, u32[]{:S(2)}) copy-start(bf16[3,3,3,256,256]{4,3,2,1,0:T(8,128)(2,1)} %refs_4_.1) | copy-start | bytes 10616836
  27.2 12.6 %collective-permute-start.8 = (bf16[2,4,96,256]{3,2,1,0:T(8,128)(2,1)S(1)}, bf16[2,4,96,256]{3,2,1,0:T(8,128)(2,1)S(1)}, u32[]{:S(2)}, u32[]{:S(2)}) collective-permute-start(bf16[2,4,96,256]{3,2,1,0:T(8,128)(2,1)S(1)} %get-tuple-element.22.refs_5_), channel_id=1, source_target_pairs={{0,2},{2,4},{4,6},{6,8},{8,10},{10,12},{12,14},{14,16},{16,18},{18... | collective-permute-start | bytes 1179656 | tf_op jit(solution)/shard_map/ppermute | solution.py:37
  27.9 18.5 %copy-start.2 = (bf16[3,3,3,256,256]{4,3,2,1,0:T(8,128)(2,1)S(1)}, bf16[3,3,3,256,256]{4,3,2,1,0:T(8,128)(2,1)}, u32[]{:S(2)}) copy-start(bf16[3,3,3,256,256]{4,3,2,1,0:T(8,128)(2,1)} %refs_10_.1) | copy-start | bytes 10616836
  30.9 1.2 %collective-permute-start.11 = (f32[1,512]{1,0:T(1,128)S(1)}, f32[1,512]{1,0:T(1,128)S(1)}, u32[]{:S(2)}, u32[]{:S(2)}) collective-permute-start(f32[1,512]{1,0:T(1,128)S(1)} %get-tuple-element.27), channel_id=1, source_target_pairs={{0,1},{1,0},{2,3},{3,2},{4,5},{5,4},{6,7},{7,6},{8,9},{9,8},{10,11... | collective-permute-start | bytes 6152 | tf_op jit(solution)/shard_map/ppermute | solution.py:32
  32.1 5.4 %collective-permute-start.14 = (f32[1,512]{1,0:T(1,128)S(1)}, f32[1,512]{1,0:T(1,128)S(1)}, u32[]{:S(2)}, u32[]{:S(2)}) collective-permute-start(f32[1,512]{1,0:T(1,128)S(1)} %add.12), channel_id=1, source_target_pairs={{0,24},{2,26},{4,28},{6,30},{8,16},{10,18},{12,20},{14,22},{16,8},... | collective-permute-start | bytes 6152 | tf_op jit(solution)/shard_map/ppermute | solution.py:32
  33.7 4.5 %collective-permute-start.13 = (f32[1,512]{1,0:T(1,128)S(1)}, f32[1,512]{1,0:T(1,128)S(1)}, u32[]{:S(2)}, u32[]{:S(2)}) collective-permute-start(f32[1,512]{1,0:T(1,128)S(1)} %add.12), channel_id=1, source_target_pairs={{0,16},{2,18},{4,20},{6,22},{8,24},{10,26},{12,28},{14,30},{16,0},... | collective-permute-start | bytes 6152 | tf_op jit(solution)/shard_map/ppermute | solution.py:32
  34.1 4.1 %collective-permute-start.12 = (f32[1,512]{1,0:T(1,128)S(1)}, f32[1,512]{1,0:T(1,128)S(1)}, u32[]{:S(2)}, u32[]{:S(2)}) collective-permute-start(f32[1,512]{1,0:T(1,128)S(1)} %add.12), channel_id=1, source_target_pairs={{0,8},{2,10},{4,12},{6,14},{8,0},{10,2},{12,4},{14,6},{16,24},{18,... | collective-permute-start | bytes 6152 | tf_op jit(solution)/shard_map/ppermute | solution.py:32
  36.5 6.2 %collective-permute-start.19 = (bf16[2,1,96,256]{3,2,1,0:T(8,128)(2,1)S(1)}, bf16[2,1,96,256]{3,2,1,0:T(8,128)(2,1)S(1)}, u32[]{:S(2)}, u32[]{:S(2)}) collective-permute-start(bf16[2,1,96,256]{3,2,1,0:T(8,128)(2,1)S(1)} %get-tuple-element.31), channel_id=1, source_target_pairs={{0,1},{1,0},{2,3},{3,2},{4,5},{5,4},{6,7},{7,6},{8,9},{9,8},{10,11... | collective-permute-start | bytes 294920 | tf_op jit(solution)/shard_map/ppermute | solution.py:32
  37.5 8.9 %collective-permute-start.18 = (bf16[2,1,96,256]{3,2,1,0:T(8,128)(2,1)S(1)}, bf16[2,1,96,256]{3,2,1,0:T(8,128)(2,1)S(1)}, u32[]{:S(2)}, u32[]{:S(2)}) collective-permute-start(bf16[2,1,96,256]{3,2,1,0:T(8,128)(2,1)S(1)} %get-tuple-element.30), channel_id=1, source_target_pairs={{0,1},{1,0},{2,3},{3,2},{4,5},{5,4},{6,7},{7,6},{8,9},{9,8},{10,11... | collective-permute-start | bytes 294920 | tf_op jit(solution)/shard_map/ppermute | solution.py:32
  39.8 6.5 %collective-permute-start.20 = (bf16[2,1,96,256]{3,2,1,0:T(8,128)(2,1)S(1)}, bf16[2,1,96,256]{3,2,1,0:T(8,128)(2,1)S(1)}, u32[]{:S(2)}, u32[]{:S(2)}) collective-permute-start(bf16[2,1,96,256]{3,2,1,0:T(8,128)(2,1)S(1)} %constant_dynamic-slice_fusion), channel_id=1, source_target_pairs={{0,1},{1,0},{2,3},{3,2},{4,5},{5,4},{6,7},{7,6},{8,9},{9,8},{10,11... | collective-permute-start | bytes 294920 | tf_op jit(solution)/shard_map/ppermute | solution.py:32
  39.9 4.6 %collective-permute-start.17 = (f32[4,512]{1,0:T(4,128)S(1)}, f32[4,512]{1,0:T(4,128)S(1)}, u32[]{:S(2)}, u32[]{:S(2)}) collective-permute-start(f32[4,512]{1,0:T(4,128)S(1)} %pad_maximum_fusion.1.refs_0_), channel_id=1, source_target_pairs={{0,6},{2,4},{4,2},{6,0},{8,14},{10,12},{12,10},{14,8},{16,22},{18,... | collective-permute-start | bytes 24584 | tf_op jit(solution)/shard_map/ppermute | solution.py:32
  42.3 3.7 %collective-permute-start.16 = (f32[4,512]{1,0:T(4,128)S(1)}, f32[4,512]{1,0:T(4,128)S(1)}, u32[]{:S(2)}, u32[]{:S(2)}) collective-permute-start(f32[4,512]{1,0:T(4,128)S(1)} %pad_maximum_fusion.1.refs_0_), channel_id=1, source_target_pairs={{0,4},{2,6},{4,0},{6,2},{8,12},{10,14},{12,8},{14,10},{16,20},{18,... | collective-permute-start | bytes 24584 | tf_op jit(solution)/shard_map/ppermute | solution.py:32
  42.7 3.7 %collective-permute-start.15 = (f32[4,512]{1,0:T(4,128)S(1)}, f32[4,512]{1,0:T(4,128)S(1)}, u32[]{:S(2)}, u32[]{:S(2)}) collective-permute-start(f32[4,512]{1,0:T(4,128)S(1)} %pad_maximum_fusion.1.refs_0_), channel_id=1, source_target_pairs={{0,2},{2,0},{4,6},{6,4},{8,10},{10,8},{12,14},{14,12},{16,18},{18,... | collective-permute-start | bytes 24584 | tf_op jit(solution)/shard_map/ppermute | solution.py:32

commit v9 on v7

--- a/solution.py
+++ b/solution.py
@@ -53,15 +53,17 @@
     return offsets
 
 
-def slab_tables(stats):
+def slab_tables(stats, beside=None):
     peers = lax.axis_size("tm")
     total = stats + traded(stats, "space", 1) if lax.axis_size("space") == 2 else lax.psum(stats, "space")
     held, left = [total], peers
     for ways in group_sizes(peers):
         left //= ways
         block = held[0] if len(held) == 1 else jnp.concatenate(held, axis=0)
+        if left == 1 and beside is not None:
+            block, beside = lax.optimization_barrier((block, beside))
         held = [block] + [traded(block, "tm", left * way) for way in range(1, ways)]
-    return total, held
+    return total, held, beside
 
 
 def row_halo(edges):
@@ -76,13 +78,6 @@
     if lax.axis_size("space") == 2:
         return [lax.dynamic_slice_in_dim(frames, (rows - 1) * (1 - lax.axis_index("space")), 1, axis=1)]
     return [frames[:, :1], frames[:, rows - 1 :]]
-
-
-def slab_halo(tail, after=None):
-    before = shifted(tail, "tm", 1)
-    if after is not None:
-        before, after = lax.optimization_barrier((before, after))
-    return before, row_halo(edges_of(before)), after
 
 
 def edge_shapes(frames, count):
@@ -154,9 +149,9 @@
 def setup_kernel(slabs, per_slab, kernel_hbm, clips_hbm, *refs):
     params_hbm, (_, taps, aux, params, clips, sems) = refs[:4], refs[4:]
     width = aux.shape[1]
-    taps_load = pltpu.make_async_copy(kernel_hbm, taps, sems.at[0])
-    clip_load = pltpu.make_async_copy(clips_hbm, clips, sems.at[1])
-    param_loads = [pltpu.make_async_copy(p, params.at[k], sems.at[2 + k]) for k, p in enumerate(params_hbm)]
+    clip_load = pltpu.make_async_copy(clips_hbm, clips, sems.at[0])
+    param_loads = [pltpu.make_async_copy(p, params.at[k], sems.at[1 + k]) for k, p in enumerate(params_hbm)]
+    taps_load = pltpu.make_async_copy(kernel_hbm, taps, sems.at[5])
     for copy in [clip_load, *param_loads, taps_load]:
         copy.start()
     clip_load.wait()
@@ -178,7 +173,7 @@
 
 
 def setup_call(kernel, clip_ids, params, per_slab, after):
-    slabs, width = lax.axis_size("tm"), kernel.shape[4]
+    slabs, width = lax.axis_size("tm"), params[0].shape[0]
     return pl.pallas_call(
         functools.partial(setup_kernel, slabs, per_slab),
         out_shape=[shaped(kernel.shape), shaped((slabs + 8, width), F32)],
@@ -192,24 +187,6 @@
         compiler_params=vmem_params(),
         cost_estimate=pl.CostEstimate(flops=0, bytes_accessed=4 * kernel.size, transcendentals=0),
     )(*[in_hbm(x) for x in (kernel, clip_ids, *[p[None] for p in params])], after)
-
-
-def load_kernel(kernel_hbm, after, taps, sem):
-    copy = pltpu.make_async_copy(kernel_hbm, taps, sem)
-    copy.start()
-    copy.wait()
-
-
-def load_call(kernel, after):
-    return pl.pallas_call(
-        load_kernel,
-        out_shape=shaped(kernel.shape),
-        in_specs=[ANYWHERE, ANYWHERE],
-        out_specs=VMEM,
-        scratch_shapes=[pltpu.SemaphoreType.DMA],
-        compiler_params=vmem_params(),
-        cost_estimate=pl.CostEstimate(flops=0, bytes_accessed=4 * kernel.size, transcendentals=0),
-    )(in_hbm(kernel), after)
 
 
 def group_total(values):
@@ -284,84 +261,92 @@
     return add_stats(sums, rounded.astype(F32))
 
 
-def late_kernel(n_tables, n_sides, aux, *refs):
+def late_kernel(n_tables, n_sides, which, aux, *refs):
     tables, frames, refs = refs[:n_tables], refs[n_tables], refs[n_tables + 1 :]
-    sides, taps = refs[:n_sides], refs[n_sides]
-    hidden, act_low, stats, affine_out, *edges, act_high = refs[n_sides + 1 :]
-    n_frames = frames.shape[0]
-    low = act_low.shape[0]
-    affine = half_affine(tables, aux, 0)
+    early_sides, late_sides, taps = refs[:n_sides], refs[n_sides : 2 * n_sides], refs[2 * n_sides]
+    if which == 0:
+        act_low, affine_out, hidden, stats, *edges, act_high = refs[2 * n_sides + 1 :]
+        early = late = frames
+        late_first = 0
+    else:
+        late, feats, act_low, affine_out, out_hbm, act_high, out, sems = refs[2 * n_sides + 1 :]
+        early, late_first = frames, frames.shape[0]
+    n_rows, width = frames.shape[1], frames.shape[3]
+    low, high = act_low.shape[0], act_high.shape[0]
+    affine = half_affine(tables, aux, which)
     for k in range(2):
         affine_out[k : k + 1] = affine[k]
-    planes = [(act_low, f) for f in range(low)] + [(act_high, f) for f in range(n_frames - low)]
+    planes = [(act_low, f) for f in range(low)] + [(act_high, f) for f in range(high)]
     for frame, (act, index) in enumerate(planes):
-        for row in range(frames.shape[1] + 2):
-            act[index, row] = normed(extended_row(frames, sides, frame, row), affine)
-    sums = no_stats(frames.shape[3])
-    for frame in range(n_frames - 2):
+        for row in range(n_rows + 2):
+            if which == 0 or frame < 2:
+                value = extended_row(early, early_sides, frame, row)
+            else:
+                value = extended_row(late, late_sides, frame - late_first, row)
+            act[index, row] = normed(value, affine)
+    sums = no_stats(width)
+    stores = []
+    for frame in range(high):
         for row, value in conv_rows(planes[frame : frame + 3], taps):
-            sums = put_hidden(hidden, frame, row, value, sums)
-        send_rows(hidden, frame, edges)
-    store_stats(stats, sums)
-
-
-def early_kernel(n_sides, aux, before, *refs):
-    corners, (act_low, affine_in, stats_in, taps) = refs[:n_sides], refs[n_sides : n_sides + 4]
-    hidden, stats, *edges, act_before = refs[n_sides + 4 :]
+            if which == 0:
+                sums = put_hidden(hidden, frame, row, value, sums)
+            else:
+                out[frame, row] = feats[low + frame, row].astype(F32) + value
+        if which == 0:
+            send_rows(hidden, frame, edges)
+        else:
+            stores.append(pltpu.make_async_copy(out.at[frame], out_hbm.at[low + frame], sems.at[frame]))
+            stores[-1].start()
+    if which == 0:
+        store_stats(stats, sums)
+    for store in stores:
+        store.wait()
+
+
+def early_kernel(n_sides, n_before, which, aux, *refs):
+    before = [(ref, f) for ref in refs[:n_before] for f in range(ref.shape[0])]
+    corners = [refs[n_before + k * n_sides : n_before + (k + 1) * n_sides] for k in range(n_before)]
+    corners = [corners[k] for k in range(n_before) for _ in range(refs[k].shape[0])]
+    act_low, affine_in, taps, *refs = refs[n_before * (n_sides + 1) :]
+    if which == 0:
+        stats_in, hidden, stats, *edges, act_before = refs
+    else:
+        feats, _, out_hbm, act_before, out, sems = refs
     slabs = aux.shape[0] - 8
     starting = aux[slabs : slabs + 1] != 0.0
     affine = affine_in[0:1], affine_in[1:2]
-    for frame in range(2):
-        for row in range(before.shape[1] + 2):
-            value = normed(extended_row(before, corners, frame, row), affine).astype(F32)
+    for frame, (ref, index) in enumerate(before):
+        for row in range(ref.shape[1] + 2):
+            value = normed(extended_row(ref, corners[frame], index, row), affine).astype(F32)
             act_before[frame, row] = jnp.where(starting, act_low[0, row].astype(F32), value).astype(BF16)
     planes = [(act_before, 0), (act_before, 1)] + [(act_low, f) for f in range(act_low.shape[0])]
-    sums = no_stats(before.shape[3])
+    sums = no_stats(act_low.shape[3])
+    stores = []
     for frame in range(2):
         for row, value in conv_rows(planes[frame : frame + 3], taps):
-            sums = put_hidden(hidden, frame, row, value, sums)
-        send_rows(hidden, frame, edges)
-    store_stats(stats, sums, stats_in)
-
-
-def last_kernel(n_tables, n_sides, aux, *refs):
-    tables, early, late, refs = refs[:n_tables], refs[n_tables], refs[n_tables + 1], refs[n_tables + 2 :]
-    sides_early, sides_late = refs[:n_sides], refs[n_sides : 2 * n_sides]
-    before, *corners = refs[2 * n_sides : 3 * n_sides + 1]
-    taps, feats, out, act = refs[3 * n_sides + 1 :]
-    slabs = aux.shape[0] - 8
-    starting = aux[slabs : slabs + 1] != 0.0
-    affine = half_affine(tables, aux, 1)
-    n_frames, n_rows = out.shape[:2]
-
-    def fill(frame):
-        for row in range(n_rows + 2):
-            if frame < 2:
-                value = normed(extended_row(before, corners, frame, row), affine).astype(F32)
-                act[frame, row] = jnp.where(starting, act[2, row].astype(F32), value).astype(BF16)
-            elif frame < 4:
-                act[frame, row] = normed(extended_row(early, sides_early, frame - 2, row), affine)
+            if which == 0:
+                sums = put_hidden(hidden, frame, row, value, sums)
             else:
-                act[frame, row] = normed(extended_row(late, sides_late, frame - 4, row), affine)
-
-    for frame in range(2, n_frames + 2):
-        fill(frame)
-    for frame in list(range(2, n_frames)) + [0, 1]:
-        if frame < 2:
-            fill(frame)
-        if frame == 0:
-            fill(1)
-        for row, value in conv_rows([(act, frame + i) for i in range(3)], taps):
-            out[frame, row] = feats[frame, row].astype(F32) + value
-
-
-def call(kernel, outs, scratch, frames, *operands):
+                out[frame, row] = feats[frame, row].astype(F32) + value
+        if which == 0:
+            send_rows(hidden, frame, edges)
+        else:
+            stores.append(pltpu.make_async_copy(out.at[frame], out_hbm.at[frame], sems.at[frame]))
+            stores[-1].start()
+    if which == 0:
+        store_stats(stats, sums, stats_in)
+    for store in stores:
+        store.wait()
+
+
+def call(kernel, outs, scratch, frames, operands, out_specs=None, aliases=None):
     return pl.pallas_call(
         kernel,
         out_shape=outs,
-        in_specs=[VMEM] * len(operands),
-        out_specs=[VMEM] * len(outs) if isinstance(outs, list) else VMEM,
+        in_specs=[VMEM if aliases is None or k not in aliases else ANYWHERE for k in range(len(operands))],
+        out_specs=[VMEM] * len(outs) if out_specs is None else out_specs,
         scratch_shapes=scratch,
+        input_output_aliases=aliases or {},
         compiler_params=vmem_params(),
         cost_estimate=pl.CostEstimate(flops=54 * frames * 384 * 65536, bytes_accessed=1 << 20, transcendentals=1 << 20),
     )(*operands)
@@ -370,38 +355,61 @@
 def on_device(feats, clip_ids, gain_one, shift_one, kernel_one, gain_two, shift_two, kernel_two):
     n_frames, n_rows, cols, width = feats.shape
     params = (gain_one, shift_one, gain_two, shift_two)
+    per_slab = feats.size // GROUPS * lax.axis_size("space")
+    late = n_frames - 2
+    plane = (n_rows + 2, cols, width)
+    act = pltpu.VMEM((2,) + plane, BF16)
+    act_late = pltpu.VMEM((late,) + plane, BF16)
+    act_shapes = [shaped((2,) + plane), shaped((2, width), F32)]
+    stats_shape = shaped((1, 2 * width), F32)
+
     frames, tail, stats, edges = entry_call(feats)
-    before, corners, _ = slab_halo(tail)
-    total, tables = slab_tables(stats)
+    total, tables, first_part = slab_tables(stats, shifted(tail[:1], "tm", 1))
     sides = row_halo(edges)
-    per_slab = feats.size // GROUPS * lax.axis_size("space")
+    second, _ = lax.optimization_barrier((tail[1:], total))
+    before = [first_part, shifted(second, "tm", 1)]
+    corners = [corner for part in before for corner in row_halo(edges_of(part))]
     taps, aux = setup_call(kernel_one, clip_ids, params, per_slab, total)
     n_sides = len(sides)
-    plane = (n_rows + 2, cols, width)
-    late = n_frames - 2
-    hidden_late, act_low, stats, affine, *edges = call(
-        functools.partial(late_kernel, len(tables), n_sides),
-        [shaped((late, n_rows, cols, width)), shaped((2,) + plane), shaped((1, 2 * width), F32), shaped((2, width), F32)]
-        + edge_shapes(feats, late),
-        [pltpu.VMEM((late,) + plane, BF16)],
-        late, aux, *tables, frames, *sides, taps,
-    )
+    act_low, affine, hidden_late, stats, *edges = call(
+        functools.partial(late_kernel, len(tables), n_sides, 0),
+        act_shapes + [shaped((late, n_rows, cols, width)), stats_shape] + edge_shapes(feats, late),
+        [act_late],
+        late,
+        [aux, *tables, frames, *sides, *sides, taps],
+    )
+    tail = hidden_late[late - 2 :]
+    before_two = shifted(tail, "tm", 1)
     sides_late = row_halo(edges)
     hidden_early, stats, *edges = call(
-        functools.partial(early_kernel, n_sides),
-        [shaped((2, n_rows, cols, width)), shaped((1, 2 * width), F32)] + edge_shapes(feats, 2),
-        [pltpu.VMEM((2,) + plane, BF16)],
-        2, aux, before, *corners, act_low, affine, stats, taps,
-    )
+        functools.partial(early_kernel, n_sides, len(before), 0),
+        [shaped((2, n_rows, cols, width)), stats_shape] + edge_shapes(feats, 2),
+        [act],
+        2,
+        [aux, *before, *corners, act_low, affine, taps, stats],
+    )
+
     sides_early = row_halo(edges)
-    total, tables = slab_tables(stats)
-    before, corners, tables[0] = slab_halo(hidden_late[late - 2 :], tables[0])
-    taps = load_call(kernel_two, total)
+    _, tables, _ = slab_tables(stats)
+    before_two, *tables = lax.optimization_barrier((before_two, *tables))
+    corners = row_halo(edges_of(before_two))
+    act_low, affine, out = call(
+        functools.partial(late_kernel, len(tables), n_sides, 1),
+        act_shapes + [shaped(feats.shape, F32)],
+        [act_late, pltpu.VMEM((late, n_rows, cols, width), F32), pltpu.SemaphoreType.DMA((late,))],
+        late,
+        [aux, *tables, hidden_early, *sides_early, *sides_late, kernel_two, hidden_late, frames],
+        out_specs=[VMEM, VMEM, ANYWHERE],
+    )
+    operands = [aux, before_two, *corners, act_low, affine, kernel_two, frames, out]
     return call(
-        functools.partial(last_kernel, len(tables), n_sides),
+        functools.partial(early_kernel, n_sides, 1, 1),
         shaped(feats.shape, F32),
-        [pltpu.VMEM((n_frames + 2,) + plane, BF16)],
-        n_frames, aux, *tables, hidden_early, hidden_late, *sides_early, *sides_late, before, *corners, taps, frames,
+        [act, pltpu.VMEM((2, n_rows, cols, width), F32), pltpu.SemaphoreType.DMA((2,))],
+        2,
+        operands,
+        out_specs=ANYWHERE,
+        aliases={len(operands) - 1: 0},
     )
 
 

time: 51.8 us -> 54.2 us (1.046)
  waiting for transfers between devices: 11 us -> 13.2 us
  Pallas kernels: 19 us -> 17.4 us
  starting transfers between devices: 21.5 us -> 23.1 us
    ppermute x2 -> x3, waiting for transfers between devices: 1.54 us -> 5.92 us  [shifted(): lax.ppermute(value, axis, [(i, (i + step) % peers) for i in range(peers)])]
    ppermute x19 -> x20, waiting for transfers between devices: 9.41 us -> 7.32 us  [traded(): lax.ppermute(value, axis, [(i, i ^ mask) for i in range(lax.axis_size(axi...]
    pallas_call x4, Pallas kernels: 15.5 us -> 14 us  [call(): pl.pallas_call(kernel, out_shape=outs, in_specs=[VMEM if aliases is None...]
    ppermute x2 -> x3, starting transfers between devices: 3.68 us -> 4.59 us  [shifted(): lax.ppermute(value, axis, [(i, (i + step) % peers) for i in range(peers)])]
    ppermute x19 -> x20, starting transfers between devices: 17.9 us -> 18.5 us  [traded(): lax.ppermute(value, axis, [(i, i ^ mask) for i in range(lax.axis_size(axi...]
  transfers between devices with their start and end apart: 21 -> 23, of which waited for: 10 -> 7; matrix products, arithmetic and copies ran while one was open for 0% -> 0% of each run, Pallas kernels for 20% -> 23%
where the time goes in v9:
time: 54.2 us; the launch traced here: 54 us
  starting transfers between devices  23.1 us (43%)
  Pallas kernels  17.4 us (32%)
  waiting for transfers between devices  13.2 us (24%)
    ppermute x20, starting transfers between devices, traded(): lax.ppermute(value, axis, [(i, i ^ mask) for i in range(lax.axis_size(axi...  18.5 us
    pallas_call x4, Pallas kernels, call(): pl.pallas_call(kernel, out_shape=outs, in_specs=[VMEM if aliases is None...  14 us
    ppermute x20, waiting for transfers between devices, traded(): lax.ppermute(value, axis, [(i, i ^ mask) for i in range(lax.axis_size(axi...  7.32 us
    ppermute x3, waiting for transfers between devices, shifted(): lax.ppermute(value, axis, [(i, (i + step) % peers) for i in range(peers)])  5.92 us
    ppermute x3, starting transfers between devices, shifted(): lax.ppermute(value, axis, [(i, (i + step) % peers) for i in range(peers)])  4.59 us
    pallas_call x1, Pallas kernels, setup_call(): pl.pallas_call(functools.partial(setup_kernel, slabs, per_slab), out_shap...  2.12 us
    pallas_call x1, Pallas kernels, entry_call(): pl.pallas_call(entry_kernel, out_shape=outs, in_specs=[ANYWHERE], out_spe...  1.3 us
  transfers between devices with their start and end apart: 23, of which 7 were waited for; matrix products, arithmetic and copies ran while one was open for 0% of the time, Pallas kernels for 23%

profile of v9, /device:TPU:0, one launch (start us, length us, event | category | flops | bytes accessed | tf_op | source)
XLA Modules:
  0.0 54.0 jit_solution(10698365529585089522)
XLA Ops:
  0.0 1.3 %shard_map.82 = (bf16[4,4,96,256]{3,2,1,0:T(8,128)(2,1)S(1)}, bf16[2,4,96,256]{3,2,1,0:T(8,128)(2,1)S(1)}, f32[1,512]{1,0:T(1,128)S(1)}, bf16[4,1,96,256]{3,2,1,0:T(8,128)(2,1)S(1)}) custom-call(bf16[4,4,96,256]{3,2,1,0:T(8,128)(2,1)} %feats_hbm.1), custom_call_target="tpu_custom_call" | custom-call | flops 1572864 | bytes 1572864 | tf_op jit(solution)/shard_map/pallas_call | solution.py:137
  1.3 3.0 %collective-permute-start.4 = (bf16[1,4,96,256]{3,2,1,0:T(8,128)(2,1)S(1)}, bf16[1,4,96,256]{3,2,1,0:T(8,128)(2,1)S(1)}, u32[]{:S(2)}, u32[]{:S(2)}) collective-permute-start(bf16[1,4,96,256]{3,2,1,0:T(8,128)(2,1)S(1)} %get-tuple-element.56), channel_id=1, source_target_pairs={{0,2},{2,4},{4,6},{6,8},{8,10},{10,12},{12,14},{14,16},{16,18},{18... | collective-permute-start | bytes 589832 | tf_op jit(solution)/shard_map/ppermute | solution.py:37
  4.3 0.0 collective-permute-start
  4.3 1.2 %collective-permute-done = f32[1,512]{1,0:T(1,128)S(1)} collective-permute-done((f32[1,512]{1,0:T(1,128)S(1)}, f32[1,512]{1,0:T(1,128)S(1)}, u32[]{:S(2)}, u32[]{:S(2)}) %collective-permute-start) | collective-permute-done | bytes 2080 | tf_op jit(solution)/shard_map/ppermute | solution.py:32
  5.5 3.6 %collective-permute-start.3 = (f32[1,512]{1,0:T(1,128)S(1)}, f32[1,512]{1,0:T(1,128)S(1)}, u32[]{:S(2)}, u32[]{:S(2)}) collective-permute-start(f32[1,512]{1,0:T(1,128)S(1)} %add.11.refs_4_), channel_id=1, source_target_pairs={{0,24},{2,26},{4,28},{6,30},{8,16},{10,18},{12,20},{14,22},{16,8},... | collective-permute-start | bytes 6152 | tf_op jit(solution)/shard_map/ppermute | solution.py:32
  9.1 0.0 collective-permute-start.2
  9.1 0.8 %collective-permute-start.1 = (f32[1,512]{1,0:T(1,128)S(1)}, f32[1,512]{1,0:T(1,128)S(1)}, u32[]{:S(2)}, u32[]{:S(2)}) collective-permute-start(f32[1,512]{1,0:T(1,128)S(1)} %add.11.refs_4_), channel_id=1, source_target_pairs={{0,8},{2,10},{4,12},{6,14},{8,0},{10,2},{12,4},{14,6},{16,24},{18,... | collective-permute-start | bytes 6152 | tf_op jit(solution)/shard_map/ppermute | solution.py:32
  9.9 0.0 collective-permute-start.8
  9.9 2.1 %shard_map.83 = (bf16[3,3,3,256,256]{4,3,2,1,0:T(8,128)(2,1)S(1)}, f32[24,256]{1,0:T(8,128)S(1)}) custom-call(bf16[3,3,3,256,256]{4,3,2,1,0:T(8,128)(2,1)} %kernel_hbm.1, s32[16]{0:T(128)} %clips_hbm.1, f32[1,256]{1,0:T(1,128)} %bitcast.4, f32[1,256]{1,0:T(1,128)} %bitcast.5, f32[1,256]{1,0:T(1,128)} %bitcast.6, f32[1,256]{1,0:T(1,128)} %bitcast.7, ...), custom_call_target="tpu_custom_call" | custom-call | bytes 7077888 | tf_op jit(solution)/shard_map/pallas_call | solution.py:177
  12.0 0.0 collective-permute-done.3
  12.0 1.5 %collective-permute-start.10 = (bf16[1,4,96,256]{3,2,1,0:T(8,128)(2,1)S(1)}, bf16[1,4,96,256]{3,2,1,0:T(8,128)(2,1)S(1)}, u32[]{:S(2)}, u32[]{:S(2)}) collective-permute-start(bf16[1,4,96,256]{3,2,1,0:T(8,128)(2,1)S(1)} %get-tuple-element.39), channel_id=1, source_target_pairs={{0,2},{2,4},{4,6},{6,8},{8,10},{10,12},{12,14},{14,16},{16,18},{18... | collective-permute-start | bytes 589832 | tf_op jit(solution)/shard_map/ppermute | solution.py:37
  13.6 0.0 collective-permute-done.2
  13.6 0.0 collective-permute-done.1
  13.6 0.0 collective-permute-done.4.refs_0_
  13.6 2.2 %collective-permute-start.7 = (f32[4,512]{1,0:T(4,128)S(1)}, f32[4,512]{1,0:T(4,128)S(1)}, u32[]{:S(2)}, u32[]{:S(2)}) collective-permute-start(f32[4,512]{1,0:T(4,128)S(1)} %pad_maximum_fusion.refs_0_), channel_id=1, source_target_pairs={{0,6},{2,4},{4,2},{6,0},{8,14},{10,12},{12,10},{14,8},{16,22},{18,... | collective-permute-start | bytes 24584 | tf_op jit(solution)/shard_map/ppermute | solution.py:32
  15.8 0.9 %collective-permute-start.6 = (f32[4,512]{1,0:T(4,128)S(1)}, f32[4,512]{1,0:T(4,128)S(1)}, u32[]{:S(2)}, u32[]{:S(2)}) collective-permute-start(f32[4,512]{1,0:T(4,128)S(1)} %pad_maximum_fusion.refs_0_), channel_id=1, source_target_pairs={{0,4},{2,6},{4,0},{6,2},{8,12},{10,14},{12,8},{14,10},{16,20},{18,... | collective-permute-start | bytes 24584 | tf_op jit(solution)/shard_map/ppermute | solution.py:32
  16.6 0.5 collective-permute-start.5
  17.2 5.9 %collective-permute-done.10.refs_1_ = bf16[1,4,96,256]{3,2,1,0:T(8,128)(2,1)S(1)} collective-permute-done((bf16[1,4,96,256]{3,2,1,0:T(8,128)(2,1)S(1)}, bf16[1,4,96,256]{3,2,1,0:T(8,128)(2,1)S(1)}, u32[]{:S(2)}, u32[]{:S(2)}) %collective-permute-start.10) | collective-permute-done | bytes 196640 | tf_op jit(solution)/shard_map/ppermute | solution.py:37
  23.1 0.0 collective-permute-start.11
  23.1 0.0 collective-permute-done.8.refs_5_.refs_6_
  23.1 0.6 %collective-permute-start.12 = (bf16[1,1,96,256]{3,2,1,0:T(8,128)(2,1)S(1)}, bf16[1,1,96,256]{3,2,1,0:T(8,128)(2,1)S(1)}, u32[]{:S(2)}, u32[]{:S(2)}) collective-permute-start(bf16[1,1,96,256]{3,2,1,0:T(8,128)(2,1)S(1)} %constant_dynamic-slice_fusion.1), channel_id=1, source_target_pairs={{0,1},{1,0},{2,3},{3,2},{4,5},{5,4},{6,7},{7,6},{8,9},{9,8},{10,11... | collective-permute-start | bytes 147464 | tf_op jit(solution)/shard_map/ppermute | solution.py:32
  23.7 0.0 collective-permute-done.7.refs_3_
  23.7 0.0 collective-permute-done.6.refs_2_
  23.7 0.0 collective-permute-done.5.refs_1_
  23.7 3.2 %shard_map.84 = (bf16[2,6,96,256]{3,2,1,0:T(8,128)(2,1)S(1)}, f32[2,256]{1,0:T(2,128)S(1)}, bf16[2,4,96,256]{3,2,1,0:T(8,128)(2,1)S(1)}, f32[1,512]{1,0:T(1,128)S(1)}, bf16[2,1,96,256]{3,2,1,0:T(8,128)(2,1)S(1)}) custom-call(f32[24,256]{1,0:T(8,128)S(1)} %get-tuple-element.31.aux, f32[4,512]{1,0:T(4,128)S(1)} %pad_maximum_fusion.refs_0_, ...), custom_call_target="tpu_custom_call" | custom-call | flops 2717908992 | bytes 1048576 | tf_op jit(solution)/shard_map/pallas_call | solution.py:343
  26.9 0.1 collective-permute-start.9
  27.0 0.0 collective-permute-done.11.refs_2_
  27.0 0.0 collective-permute-done.12.refs_3_
  27.0 0.0 copy-start
  27.0 3.0 %shard_map.85 = (bf16[2,4,96,256]{3,2,1,0:T(8,128)(2,1)S(1)}, f32[1,512]{1,0:T(1,128)S(1)}, bf16[2,1,96,256]{3,2,1,0:T(8,128)(2,1)S(1)}) custom-call(f32[24,256]{1,0:T(8,128)S(1)} %get-tuple-element.31.aux, bf16[1,4,96,256]{3,2,1,0:T(8,128)(2,1)S(1)} %collective-permute-done.4.refs_0_, bf16[1,4,96,256]{3,2,1,0:T(8,128)(2,1)S(1)} %collective-permute-done.10.refs_1_, ...), custom_call_target="tpu_custom_call" | custom-call | flops 2717908992 | bytes 1048576 | tf_op jit(solution)/shard_map/pallas_call | solution.py:343
  30.1 0.1 collective-permute-start.13
  30.2 1.1 %collective-permute-done.13 = f32[1,512]{1,0:T(1,128)S(1)} collective-permute-done((f32[1,512]{1,0:T(1,128)S(1)}, f32[1,512]{1,0:T(1,128)S(1)}, u32[]{:S(2)}, u32[]{:S(2)}) %collective-permute-start.13) | collective-permute-done | bytes 2080 | tf_op jit(solution)/shard_map/ppermute | solution.py:32
  31.3 1.9 %collective-permute-start.16 = (f32[1,512]{1,0:T(1,128)S(1)}, f32[1,512]{1,0:T(1,128)S(1)}, u32[]{:S(2)}, u32[]{:S(2)}) collective-permute-start(f32[1,512]{1,0:T(1,128)S(1)} %add.13), channel_id=1, source_target_pairs={{0,24},{2,26},{4,28},{6,30},{8,16},{10,18},{12,20},{14,22},{16,8},... | collective-permute-start | bytes 6152 | tf_op jit(solution)/shard_map/ppermute | solution.py:32
  33.2 0.0 collective-permute-start.15
  33.2 2.5 %collective-permute-start.14 = (f32[1,512]{1,0:T(1,128)S(1)}, f32[1,512]{1,0:T(1,128)S(1)}, u32[]{:S(2)}, u32[]{:S(2)}) collective-permute-start(f32[1,512]{1,0:T(1,128)S(1)} %add.13), channel_id=1, source_target_pairs={{0,8},{2,10},{4,12},{6,14},{8,0},{10,2},{12,4},{14,6},{16,24},{18,... | collective-permute-start | bytes 6152 | tf_op jit(solution)/shard_map/ppermute | solution.py:32
  35.7 1.0 %collective-permute-done.16 = f32[1,512]{1,0:T(1,128)S(1)} collective-permute-done((f32[1,512]{1,0:T(1,128)S(1)}, f32[1,512]{1,0:T(1,128)S(1)}, u32[]{:S(2)}, u32[]{:S(2)}) %collective-permute-start.16) | collective-permute-done | bytes 2080 | tf_op jit(solution)/shard_map/ppermute | solution.py:32
  36.7 1.0 %collective-permute-done.15 = f32[1,512]{1,0:T(1,128)S(1)} collective-permute-done((f32[1,512]{1,0:T(1,128)S(1)}, f32[1,512]{1,0:T(1,128)S(1)}, u32[]{:S(2)}, u32[]{:S(2)}) %collective-permute-start.15) | collective-permute-done | bytes 2080 | tf_op jit(solution)/shard_map/ppermute | solution.py:32
  37.7 0.0 collective-permute-done.14
  37.7 4.8 %collective-permute-start.19 = (f32[4,512]{1,0:T(4,128)S(1)}, f32[4,512]{1,0:T(4,128)S(1)}, u32[]{:S(2)}, u32[]{:S(2)}) collective-permute-start(f32[4,512]{1,0:T(4,128)S(1)} %pad_maximum_fusion.1.refs_0_), channel_id=1, source_target_pairs={{0,6},{2,4},{4,2},{6,0},{8,14},{10,12},{12,10},{14,8},{16,22},{18,... | collective-permute-start | bytes 24584 | tf_op jit(solution)/shard_map/ppermute | solution.py:32
  42.5 0.0 collective-permute-start.18
  42.5 0.6 %collective-permute-start.17 = (f32[4,512]{1,0:T(4,128)S(1)}, f32[4,512]{1,0:T(4,128)S(1)}, u32[]{:S(2)}, u32[]{:S(2)}) collective-permute-start(f32[4,512]{1,0:T(4,128)S(1)} %pad_maximum_fusion.1.refs_0_), channel_id=1, source_target_pairs={{0,2},{2,0},{4,6},{6,4},{8,10},{10,8},{12,14},{14,12},{16,18},{18,... | collective-permute-start | bytes 24584 | tf_op jit(solution)/shard_map/ppermute | solution.py:32
  43.1 0.0 collective-permute-start.22
  43.1 1.0 %collective-permute-done.19.refs_3_ = f32[4,512]{1,0:T(4,128)S(1)} collective-permute-done((f32[4,512]{1,0:T(4,128)S(1)}, f32[4,512]{1,0:T(4,128)S(1)}, u32[]{:S(2)}, u32[]{:S(2)}) %collective-permute-start.19) | collective-permute-done | bytes 8224 | tf_op jit(solution)/shard_map/ppermute | solution.py:32
  44.1 0.0 collective-permute-start.21
  44.1 2.0 %collective-permute-done.18.refs_2_ = f32[4,512]{1,0:T(4,128)S(1)} collective-permute-done((f32[4,512]{1,0:T(4,128)S(1)}, f32[4,512]{1,0:T(4,128)S(1)}, u32[]{:S(2)}, u32[]{:S(2)}) %collective-permute-start.18) | collective-permute-done | bytes 8224 | tf_op jit(solution)/shard_map/ppermute | solution.py:32
  46.1 0.0 collective-permute-done.17.refs_1_
  46.1 0.0 collective-permute-done.9.refs_0_
  46.1 0.1 collective-permute-start.20
  46.2 0.0 collective-permute-done.22.refs_6_
  46.2 0.0 collective-permute-done.21.refs_5_
  46.2 0.0 copy-done
  46.2 4.0 %shard_map.86 = (bf16[2,6,96,256]{3,2,1,0:T(8,128)(2,1)S(1)}, f32[2,256]{1,0:T(2,128)S(1)}, f32[4,4,96,256]{3,2,1,0:T(8,128)}) custom-call(f32[24,256]{1,0:T(8,128)S(1)} %get-tuple-element.31.aux, f32[4,512]{1,0:T(4,128)S(1)} %pad_maximum_fusion.1.refs_0_, f32[4,512]{1,0:T(4,128)S(1)} %collective-permute-done.17.refs_1_, ...), custom_call_target="tpu_custom_call" | custom-call | flops 2717908992 | bytes 1048576 | tf_op jit(solution)/shard_map/pallas_call | solution.py:343
  50.2 0.0 collective-permute-done.20.refs_1_
  50.2 3.7 %shard_map.87 = f32[4,4,96,256]{3,2,1,0:T(8,128)} custom-call(f32[24,256]{1,0:T(8,128)S(1)} %get-tuple-element.31.aux, bf16[2,4,96,256]{3,2,1,0:T(8,128)(2,1)S(1)} %collective-permute-done.9.refs_0_, bf16[2,1,96,256]{3,2,1,0:T(8,128)(2,1)S(1)} %collective-permute-done.20.refs_1_, ...), custom_call_target="tpu_custom_call", output_to_operand_aliasing={{}: (7, {})} | custom-call | flops 2717908992 | bytes 1048576 | tf_op jit(solution)/shard_map/pallas_call | solution.py:343
  (8 shorter events, 0.1 us)
Async XLA Ops:
  1.3 12.3 %collective-permute-start.4 = (bf16[1,4,96,256]{3,2,1,0:T(8,128)(2,1)S(1)}, bf16[1,4,96,256]{3,2,1,0:T(8,128)(2,1)S(1)}, u32[]{:S(2)}, u32[]{:S(2)}) collective-permute-start(bf16[1,4,96,256]{3,2,1,0:T(8,128)(2,1)S(1)} %get-tuple-element.56), channel_id=1, source_target_pairs={{0,2},{2,4},{4,6},{6,8},{8,10},{10,12},{12,14},{14,16},{16,18},{18... | collective-permute-start | bytes 589832 | tf_op jit(solution)/shard_map/ppermute | solution.py:37
  4.3 1.2 %collective-permute-start = (f32[1,512]{1,0:T(1,128)S(1)}, f32[1,512]{1,0:T(1,128)S(1)}, u32[]{:S(2)}, u32[]{:S(2)}) collective-permute-start(f32[1,512]{1,0:T(1,128)S(1)} %get-tuple-element.30), channel_id=1, source_target_pairs={{0,1},{1,0},{2,3},{3,2},{4,5},{5,4},{6,7},{7,6},{8,9},{9,8},{10,11... | collective-permute-start | bytes 6152 | tf_op jit(solution)/shard_map/ppermute | solution.py:32
  5.5 6.5 %collective-permute-start.3 = (f32[1,512]{1,0:T(1,128)S(1)}, f32[1,512]{1,0:T(1,128)S(1)}, u32[]{:S(2)}, u32[]{:S(2)}) collective-permute-start(f32[1,512]{1,0:T(1,128)S(1)} %add.11.refs_4_), channel_id=1, source_target_pairs={{0,24},{2,26},{4,28},{6,30},{8,16},{10,18},{12,20},{14,22},{16,8},... | collective-permute-start | bytes 6152 | tf_op jit(solution)/shard_map/ppermute | solution.py:32
  9.1 4.5 %collective-permute-start.2 = (f32[1,512]{1,0:T(1,128)S(1)}, f32[1,512]{1,0:T(1,128)S(1)}, u32[]{:S(2)}, u32[]{:S(2)}) collective-permute-start(f32[1,512]{1,0:T(1,128)S(1)} %add.11.refs_4_), channel_id=1, source_target_pairs={{0,16},{2,18},{4,20},{6,22},{8,24},{10,26},{12,28},{14,30},{16,0},... | collective-permute-start | bytes 6152 | tf_op jit(solution)/shard_map/ppermute | solution.py:32
  9.1 4.5 %collective-permute-start.1 = (f32[1,512]{1,0:T(1,128)S(1)}, f32[1,512]{1,0:T(1,128)S(1)}, u32[]{:S(2)}, u32[]{:S(2)}) collective-permute-start(f32[1,512]{1,0:T(1,128)S(1)} %add.11.refs_4_), channel_id=1, source_target_pairs={{0,8},{2,10},{4,12},{6,14},{8,0},{10,2},{12,4},{14,6},{16,24},{18,... | collective-permute-start | bytes 6152 | tf_op jit(solution)/shard_map/ppermute | solution.py:32
  9.9 13.2 %collective-permute-start.8 = (bf16[4,1,96,256]{3,2,1,0:T(8,128)(2,1)S(1)}, bf16[4,1,96,256]{3,2,1,0:T(8,128)(2,1)S(1)}, u32[]{:S(2)}, u32[]{:S(2)}) collective-permute-start(bf16[4,1,96,256]{3,2,1,0:T(8,128)(2,1)S(1)} %get-tuple-element.35), channel_id=1, source_target_pairs={{0,1},{1,0},{2,3},{3,2},{4,5},{5,4},{6,7},{7,6},{8,9},{9,8},{10,11... | collective-permute-start | bytes 589832 | tf_op jit(solution)/shard_map/ppermute | solution.py:32
  12.0 11.1 %collective-permute-start.10 = (bf16[1,4,96,256]{3,2,1,0:T(8,128)(2,1)S(1)}, bf16[1,4,96,256]{3,2,1,0:T(8,128)(2,1)S(1)}, u32[]{:S(2)}, u32[]{:S(2)}) collective-permute-start(bf16[1,4,96,256]{3,2,1,0:T(8,128)(2,1)S(1)} %get-tuple-element.39), channel_id=1, source_target_pairs={{0,2},{2,4},{4,6},{6,8},{8,10},{10,12},{12,14},{14,16},{16,18},{18... | collective-permute-start | bytes 589832 | tf_op jit(solution)/shard_map/ppermute | solution.py:37
  13.6 10.1 %collective-permute-start.7 = (f32[4,512]{1,0:T(4,128)S(1)}, f32[4,512]{1,0:T(4,128)S(1)}, u32[]{:S(2)}, u32[]{:S(2)}) collective-permute-start(f32[4,512]{1,0:T(4,128)S(1)} %pad_maximum_fusion.refs_0_), channel_id=1, source_target_pairs={{0,6},{2,4},{4,2},{6,0},{8,14},{10,12},{12,10},{14,8},{16,22},{18,... | collective-permute-start | bytes 24584 | tf_op jit(solution)/shard_map/ppermute | solution.py:32
  15.8 7.9 %collective-permute-start.6 = (f32[4,512]{1,0:T(4,128)S(1)}, f32[4,512]{1,0:T(4,128)S(1)}, u32[]{:S(2)}, u32[]{:S(2)}) collective-permute-start(f32[4,512]{1,0:T(4,128)S(1)} %pad_maximum_fusion.refs_0_), channel_id=1, source_target_pairs={{0,4},{2,6},{4,0},{6,2},{8,12},{10,14},{12,8},{14,10},{16,20},{18,... | collective-permute-start | bytes 24584 | tf_op jit(solution)/shard_map/ppermute | solution.py:32
  16.6 7.0 %collective-permute-start.5 = (f32[4,512]{1,0:T(4,128)S(1)}, f32[4,512]{1,0:T(4,128)S(1)}, u32[]{:S(2)}, u32[]{:S(2)}) collective-permute-start(f32[4,512]{1,0:T(4,128)S(1)} %pad_maximum_fusion.refs_0_), channel_id=1, source_target_pairs={{0,2},{2,0},{4,6},{6,4},{8,10},{10,8},{12,14},{14,12},{16,18},{18,... | collective-permute-start | bytes 24584 | tf_op jit(solution)/shard_map/ppermute | solution.py:32
  23.1 3.9 %collective-permute-start.11 = (bf16[1,1,96,256]{3,2,1,0:T(8,128)(2,1)S(1)}, bf16[1,1,96,256]{3,2,1,0:T(8,128)(2,1)S(1)}, u32[]{:S(2)}, u32[]{:S(2)}) collective-permute-start(bf16[1,1,96,256]{3,2,1,0:T(8,128)(2,1)S(1)} %constant_dynamic-slice_fusion.2), channel_id=1, source_target_pairs={{0,1},{1,0},{2,3},{3,2},{4,5},{5,4},{6,7},{7,6},{8,9},{9,8},{10,11... | collective-permute-start | bytes 147464 | tf_op jit(solution)/shard_map/ppermute | solution.py:32
  23.1 3.9 %collective-permute-start.12 = (bf16[1,1,96,256]{3,2,1,0:T(8,128)(2,1)S(1)}, bf16[1,1,96,256]{3,2,1,0:T(8,128)(2,1)S(1)}, u32[]{:S(2)}, u32[]{:S(2)}) collective-permute-start(bf16[1,1,96,256]{3,2,1,0:T(8,128)(2,1)S(1)} %constant_dynamic-slice_fusion.1), channel_id=1, source_target_pairs={{0,1},{1,0},{2,3},{3,2},{4,5},{5,4},{6,7},{7,6},{8,9},{9,8},{10,11... | collective-permute-start | bytes 147464 | tf_op jit(solution)/shard_map/ppermute | solution.py:32
  26.9 19.2 %collective-permute-start.9 = (bf16[2,4,96,256]{3,2,1,0:T(8,128)(2,1)S(1)}, bf16[2,4,96,256]{3,2,1,0:T(8,128)(2,1)S(1)}, u32[]{:S(2)}, u32[]{:S(2)}) collective-permute-start(bf16[2,4,96,256]{3,2,1,0:T(8,128)(2,1)S(1)} %get-tuple-element.37.refs_8_), channel_id=1, source_target_pairs={{0,2},{2,4},{4,6},{6,8},{8,10},{10,12},{12,14},{14,16},{16,18},{18... | collective-permute-start | bytes 1179656 | tf_op jit(solution)/shard_map/ppermute | solution.py:37
  27.0 19.2 %copy-start = (bf16[3,3,3,256,256]{4,3,2,1,0:T(8,128)(2,1)S(1)}, bf16[3,3,3,256,256]{4,3,2,1,0:T(8,128)(2,1)}, u32[]{:S(2)}) copy-start(bf16[3,3,3,256,256]{4,3,2,1,0:T(8,128)(2,1)} %refs_4_.1) | copy-start | bytes 10616836
  30.1 1.2 %collective-permute-start.13 = (f32[1,512]{1,0:T(1,128)S(1)}, f32[1,512]{1,0:T(1,128)S(1)}, u32[]{:S(2)}, u32[]{:S(2)}) collective-permute-start(f32[1,512]{1,0:T(1,128)S(1)} %get-tuple-element.43), channel_id=1, source_target_pairs={{0,1},{1,0},{2,3},{3,2},{4,5},{5,4},{6,7},{7,6},{8,9},{9,8},{10,11... | collective-permute-start | bytes 6152 | tf_op jit(solution)/shard_map/ppermute | solution.py:32
  31.3 5.4 %collective-permute-start.16 = (f32[1,512]{1,0:T(1,128)S(1)}, f32[1,512]{1,0:T(1,128)S(1)}, u32[]{:S(2)}, u32[]{:S(2)}) collective-permute-start(f32[1,512]{1,0:T(1,128)S(1)} %add.13), channel_id=1, source_target_pairs={{0,24},{2,26},{4,28},{6,30},{8,16},{10,18},{12,20},{14,22},{16,8},... | collective-permute-start | bytes 6152 | tf_op jit(solution)/shard_map/ppermute | solution.py:32
  33.2 4.5 %collective-permute-start.15 = (f32[1,512]{1,0:T(1,128)S(1)}, f32[1,512]{1,0:T(1,128)S(1)}, u32[]{:S(2)}, u32[]{:S(2)}) collective-permute-start(f32[1,512]{1,0:T(1,128)S(1)} %add.13), channel_id=1, source_target_pairs={{0,16},{2,18},{4,20},{6,22},{8,24},{10,26},{12,28},{14,30},{16,0},... | collective-permute-start | bytes 6152 | tf_op jit(solution)/shard_map/ppermute | solution.py:32
  33.2 4.5 %collective-permute-start.14 = (f32[1,512]{1,0:T(1,128)S(1)}, f32[1,512]{1,0:T(1,128)S(1)}, u32[]{:S(2)}, u32[]{:S(2)}) collective-permute-start(f32[1,512]{1,0:T(1,128)S(1)} %add.13), channel_id=1, source_target_pairs={{0,8},{2,10},{4,12},{6,14},{8,0},{10,2},{12,4},{14,6},{16,24},{18,... | collective-permute-start | bytes 6152 | tf_op jit(solution)/shard_map/ppermute | solution.py:32
  37.7 6.4 %collective-permute-start.19 = (f32[4,512]{1,0:T(4,128)S(1)}, f32[4,512]{1,0:T(4,128)S(1)}, u32[]{:S(2)}, u32[]{:S(2)}) collective-permute-start(f32[4,512]{1,0:T(4,128)S(1)} %pad_maximum_fusion.1.refs_0_), channel_id=1, source_target_pairs={{0,6},{2,4},{4,2},{6,0},{8,14},{10,12},{12,10},{14,8},{16,22},{18,... | collective-permute-start | bytes 24584 | tf_op jit(solution)/shard_map/ppermute | solution.py:32
  42.5 3.7 %collective-permute-start.18 = (f32[4,512]{1,0:T(4,128)S(1)}, f32[4,512]{1,0:T(4,128)S(1)}, u32[]{:S(2)}, u32[]{:S(2)}) collective-permute-start(f32[4,512]{1,0:T(4,128)S(1)} %pad_maximum_fusion.1.refs_0_), channel_id=1, source_target_pairs={{0,4},{2,6},{4,0},{6,2},{8,12},{10,14},{12,8},{14,10},{16,20},{18,... | collective-permute-start | bytes 24584 | tf_op jit(solution)/shard_map/ppermute | solution.py:32
  42.5 3.7 %collective-permute-start.17 = (f32[4,512]{1,0:T(4,128)S(1)}, f32[4,512]{1,0:T(4,128)S(1)}, u32[]{:S(2)}, u32[]{:S(2)}) collective-permute-start(f32[4,512]{1,0:T(4,128)S(1)} %pad_maximum_fusion.1.refs_0_), channel_id=1, source_target_pairs={{0,2},{2,0},{4,6},{6,4},{8,10},{10,8},{12,14},{14,12},{16,18},{18,... | collective-permute-start | bytes 24584 | tf_op jit(solution)/shard_map/ppermute | solution.py:32
  43.1 3.1 %collective-permute-start.22 = (bf16[2,1,96,256]{3,2,1,0:T(8,128)(2,1)S(1)}, bf16[2,1,96,256]{3,2,1,0:T(8,128)(2,1)S(1)}, u32[]{:S(2)}, u32[]{:S(2)}) collective-permute-start(bf16[2,1,96,256]{3,2,1,0:T(8,128)(2,1)S(1)} %get-tuple-element.51), channel_id=1, source_target_pairs={{0,1},{1,0},{2,3},{3,2},{4,5},{5,4},{6,7},{7,6},{8,9},{9,8},{10,11... | collective-permute-start | bytes 294920 | tf_op jit(solution)/shard_map/ppermute | solution.py:32
  44.1 2.1 %collective-permute-start.21 = (bf16[2,1,96,256]{3,2,1,0:T(8,128)(2,1)S(1)}, bf16[2,1,96,256]{3,2,1,0:T(8,128)(2,1)S(1)}, u32[]{:S(2)}, u32[]{:S(2)}) collective-permute-start(bf16[2,1,96,256]{3,2,1,0:T(8,128)(2,1)S(1)} %get-tuple-element.50), channel_id=1, source_target_pairs={{0,1},{1,0},{2,3},{3,2},{4,5},{5,4},{6,7},{7,6},{8,9},{9,8},{10,11... | collective-permute-start | bytes 294920 | tf_op jit(solution)/shard_map/ppermute | solution.py:32
  46.1 4.1 %collective-permute-start.20 = (bf16[2,1,96,256]{3,2,1,0:T(8,128)(2,1)S(1)}, bf16[2,1,96,256]{3,2,1,0:T(8,128)(2,1)S(1)}, u32[]{:S(2)}, u32[]{:S(2)}) collective-permute-start(bf16[2,1,96,256]{3,2,1,0:T(8,128)(2,1)S(1)} %constant_dynamic-slice_fusion), channel_id=1, source_target_pairs={{0,1},{1,0},{2,3},{3,2},{4,5},{5,4},{6,7},{7,6},{8,9},{9,8},{10,11... | collective-permute-start | bytes 294920 | tf_op jit(solution)/shard_map/ppermute | solution.py:32

commit v10 on v9

--- a/solution.py
+++ b/solution.py
@@ -53,17 +53,32 @@
     return offsets
 
 
-def slab_tables(stats, beside=None):
+def slab_tables(stats, rows):
     peers = lax.axis_size("tm")
     total = stats + traded(stats, "space", 1) if lax.axis_size("space") == 2 else lax.psum(stats, "space")
+    total, *rows = lax.optimization_barrier((total, *rows))
     held, left = [total], peers
+    marks = []
     for ways in group_sizes(peers):
         left //= ways
         block = held[0] if len(held) == 1 else jnp.concatenate(held, axis=0)
-        if left == 1 and beside is not None:
-            block, beside = lax.optimization_barrier((block, beside))
         held = [block] + [traded(block, "tm", left * way) for way in range(1, ways)]
-    return total, held, beside
+        marks += [block, held[-1]]
+    return held, rows, (total, marks[-2])
+
+
+def slab_halo(frames, marks):
+    parts = []
+    for part, mark in enumerate(marks):
+        frame, _ = lax.optimization_barrier((frames[part : part + 1], mark))
+        parts.append(shifted(frame, "tm", 1))
+    return parts
+
+
+def corner_rows(parts, after):
+    *parts, after = lax.optimization_barrier((*parts, after))
+    edges = [edges_of(part) for part in parts]
+    return parts, row_halo([jnp.concatenate(side, axis=0) for side in zip(*edges)]), after
 
 
 def row_halo(edges):
@@ -113,11 +128,14 @@
         stats[:, k * width : (k + 1) * width] = part if base is None else part + base[:, k * width : (k + 1) * width]
 
 
-def entry_kernel(feats_hbm, frames, tail, stats, *rest):
-    *edges, sems = rest
+def entry_kernel(slabs, per_slab, feats_hbm, kernel_hbm, clips_hbm, *refs):
+    params_hbm, (frames, taps, tail, stats, aux, *edges, params, clips, frame_sems, sems) = refs[:4], refs[4:]
     n_frames, n_rows, _, width = frames.shape
-    loads = [pltpu.make_async_copy(feats_hbm.at[f], frames.at[f], sems.at[f]) for f in range(n_frames)]
-    for copy in loads:
+    loads = [pltpu.make_async_copy(feats_hbm.at[f], frames.at[f], frame_sems.at[f]) for f in range(n_frames)]
+    clip_load = pltpu.make_async_copy(clips_hbm, clips, sems.at[0])
+    param_loads = [pltpu.make_async_copy(p, params.at[k], sems.at[1 + k]) for k, p in enumerate(params_hbm)]
+    taps_load = pltpu.make_async_copy(kernel_hbm, taps, sems.at[5])
+    for copy in [*loads, clip_load, *param_loads, taps_load]:
         copy.start()
     sums = no_stats(width)
     for frame in range(n_frames):
@@ -128,32 +146,6 @@
             sums = add_stats(sums, frames[frame, row].astype(F32))
         send_rows(frames, frame, edges)
     store_stats(stats, sums)
-
-
-def entry_call(feats):
-    n_frames, width = feats.shape[0], feats.shape[3]
-    outs = [shaped(feats.shape), shaped((TAIL,) + feats.shape[1:]), shaped((1, 2 * width), F32)]
-    outs += edge_shapes(feats, n_frames)
-    frames, tail, stats, *edges = pl.pallas_call(
-        entry_kernel,
-        out_shape=outs,
-        in_specs=[ANYWHERE],
-        out_specs=[VMEM] * len(outs),
-        scratch_shapes=[pltpu.SemaphoreType.DMA((n_frames,))],
-        compiler_params=vmem_params(),
-        cost_estimate=pl.CostEstimate(flops=4 * feats.size, bytes_accessed=4 * feats.size, transcendentals=0),
-    )(in_hbm(feats))
-    return frames, tail, stats, edges
-
-
-def setup_kernel(slabs, per_slab, kernel_hbm, clips_hbm, *refs):
-    params_hbm, (_, taps, aux, params, clips, sems) = refs[:4], refs[4:]
-    width = aux.shape[1]
-    clip_load = pltpu.make_async_copy(clips_hbm, clips, sems.at[0])
-    param_loads = [pltpu.make_async_copy(p, params.at[k], sems.at[1 + k]) for k, p in enumerate(params_hbm)]
-    taps_load = pltpu.make_async_copy(kernel_hbm, taps, sems.at[5])
-    for copy in [clip_load, *param_loads, taps_load]:
-        copy.start()
     clip_load.wait()
     own = lax.axis_index("tm")
     own_clip = clips[own]
@@ -172,21 +164,27 @@
     taps_load.wait()
 
 
-def setup_call(kernel, clip_ids, params, per_slab, after):
-    slabs, width = lax.axis_size("tm"), params[0].shape[0]
-    return pl.pallas_call(
-        functools.partial(setup_kernel, slabs, per_slab),
-        out_shape=[shaped(kernel.shape), shaped((slabs + 8, width), F32)],
+def entry_call(feats, kernel, clip_ids, params, per_slab):
+    slabs = lax.axis_size("tm")
+    n_frames, width = feats.shape[0], feats.shape[3]
+    outs = [shaped(feats.shape), shaped(kernel.shape), shaped((TAIL,) + feats.shape[1:])]
+    outs += [shaped((1, 2 * width), F32), shaped((slabs + 8, width), F32)]
+    outs += edge_shapes(feats, n_frames)
+    frames, taps, tail, stats, aux, *edges = pl.pallas_call(
+        functools.partial(entry_kernel, slabs, per_slab),
+        out_shape=outs,
         in_specs=[ANYWHERE] * 7,
-        out_specs=[VMEM, VMEM],
+        out_specs=[VMEM] * len(outs),
         scratch_shapes=[
             pltpu.VMEM((4, 1, width), F32),
             pltpu.SMEM(clip_ids.shape, jnp.int32),
+            pltpu.SemaphoreType.DMA((n_frames,)),
             pltpu.SemaphoreType.DMA((6,)),
         ],
         compiler_params=vmem_params(),
-        cost_estimate=pl.CostEstimate(flops=0, bytes_accessed=4 * kernel.size, transcendentals=0),
-    )(*[in_hbm(x) for x in (kernel, clip_ids, *[p[None] for p in params])], after)
+        cost_estimate=pl.CostEstimate(flops=4 * feats.size, bytes_accessed=4 * kernel.size, transcendentals=0),
+    )(*[in_hbm(x) for x in (feats, kernel, clip_ids, *[p[None] for p in params])])
+    return frames, taps, tail, stats, aux, edges
 
 
 def group_total(values):
@@ -227,14 +225,14 @@
     return (half * jnp.tanh(half) + half).astype(BF16)
 
 
-def extended_row(frames, sides, frame, row):
+def extended_row(frames, sides, frame, row, side_frame=None):
     n_rows = frames.shape[1]
     inner = frames[frame, min(max(row - 1, 0), n_rows - 1)]
     if 0 < row <= n_rows:
         return inner
     place, places = lax.axis_index("space"), lax.axis_size("space")
     side = sides[0 if row == 0 else -1]
-    return jnp.where(place == (0 if row == 0 else places - 1), inner, side[frame, 0])
+    return jnp.where(place == (0 if row == 0 else places - 1), inner, side[frame if side_frame is None else side_frame, 0])
 
 
 def conv_rows(planes, taps):
@@ -303,11 +301,9 @@
         store.wait()
 
 
-def early_kernel(n_sides, n_before, which, aux, *refs):
-    before = [(ref, f) for ref in refs[:n_before] for f in range(ref.shape[0])]
-    corners = [refs[n_before + k * n_sides : n_before + (k + 1) * n_sides] for k in range(n_before)]
-    corners = [corners[k] for k in range(n_before) for _ in range(refs[k].shape[0])]
-    act_low, affine_in, taps, *refs = refs[n_before * (n_sides + 1) :]
+def early_kernel(n_sides, which, aux, *refs):
+    before, corners = refs[:2], refs[2 : 2 + n_sides]
+    act_low, affine_in, taps, *refs = refs[2 + n_sides :]
     if which == 0:
         stats_in, hidden, stats, *edges, act_before = refs
     else:
@@ -315,9 +311,9 @@
     slabs = aux.shape[0] - 8
     starting = aux[slabs : slabs + 1] != 0.0
     affine = affine_in[0:1], affine_in[1:2]
-    for frame, (ref, index) in enumerate(before):
-        for row in range(ref.shape[1] + 2):
-            value = normed(extended_row(ref, corners[frame], index, row), affine).astype(F32)
+    for frame in range(2):
+        for row in range(act_low.shape[1]):
+            value = normed(extended_row(before[frame], corners, 0, row, frame), affine).astype(F32)
             act_before[frame, row] = jnp.where(starting, act_low[0, row].astype(F32), value).astype(BF16)
     planes = [(act_before, 0), (act_before, 1)] + [(act_low, f) for f in range(act_low.shape[0])]
     sums = no_stats(act_low.shape[3])
@@ -363,13 +359,10 @@
     act_shapes = [shaped((2,) + plane), shaped((2, width), F32)]
     stats_shape = shaped((1, 2 * width), F32)
 
-    frames, tail, stats, edges = entry_call(feats)
-    total, tables, first_part = slab_tables(stats, shifted(tail[:1], "tm", 1))
-    sides = row_halo(edges)
-    second, _ = lax.optimization_barrier((tail[1:], total))
-    before = [first_part, shifted(second, "tm", 1)]
-    corners = [corner for part in before for corner in row_halo(edges_of(part))]
-    taps, aux = setup_call(kernel_one, clip_ids, params, per_slab, total)
+    frames, taps, tail, stats, aux, edges = entry_call(feats, kernel_one, clip_ids, params, per_slab)
+    tables, sides, marks = slab_tables(stats, row_halo(edges))
+    before = slab_halo(tail, marks)
+    aux, before[0] = lax.optimization_barrier((aux, before[0]))
     n_sides = len(sides)
     act_low, affine, hidden_late, stats, *edges = call(
         functools.partial(late_kernel, len(tables), n_sides, 0),
@@ -378,32 +371,31 @@
         late,
         [aux, *tables, frames, *sides, *sides, taps],
     )
-    tail = hidden_late[late - 2 :]
-    before_two = shifted(tail, "tm", 1)
     sides_late = row_halo(edges)
+    before, corners, affine = corner_rows(before, affine)
     hidden_early, stats, *edges = call(
-        functools.partial(early_kernel, n_sides, len(before), 0),
+        functools.partial(early_kernel, n_sides, 0),
         [shaped((2, n_rows, cols, width)), stats_shape] + edge_shapes(feats, 2),
         [act],
         2,
         [aux, *before, *corners, act_low, affine, taps, stats],
     )
 
-    sides_early = row_halo(edges)
-    _, tables, _ = slab_tables(stats)
-    before_two, *tables = lax.optimization_barrier((before_two, *tables))
-    corners = row_halo(edges_of(before_two))
+    tables, sides, marks = slab_tables(stats, [*row_halo(edges), *sides_late])
+    before = slab_halo(hidden_late[late - 2 :], marks)
+    aux, before[0] = lax.optimization_barrier((aux, before[0]))
     act_low, affine, out = call(
         functools.partial(late_kernel, len(tables), n_sides, 1),
         act_shapes + [shaped(feats.shape, F32)],
         [act_late, pltpu.VMEM((late, n_rows, cols, width), F32), pltpu.SemaphoreType.DMA((late,))],
         late,
-        [aux, *tables, hidden_early, *sides_early, *sides_late, kernel_two, hidden_late, frames],
+        [aux, *tables, hidden_early, *sides, kernel_two, hidden_late, frames],
         out_specs=[VMEM, VMEM, ANYWHERE],
     )
-    operands = [aux, before_two, *corners, act_low, affine, kernel_two, frames, out]
+    before, corners, affine = corner_rows(before, affine)
+    operands = [aux, *before, *corners, act_low, affine, kernel_two, frames, out]
     return call(
-        functools.partial(early_kernel, n_sides, 1, 1),
+        functools.partial(early_kernel, n_sides, 1),
         shaped(feats.shape, F32),
         [act, pltpu.VMEM((2, n_rows, cols, width), F32), pltpu.SemaphoreType.DMA((2,))],
         2,

time: 54.2 us -> 62.5 us (1.15)
  local copies, waits for them, and re-layouts: 0.05 us -> 3.81 us
  waiting for transfers between devices: 13.2 us -> 16 us
  starting transfers between devices: 23.1 us -> 25.8 us
  Pallas kernels: 17.4 us -> 16.5 us
    ppermute x20 -> x19, waiting for transfers between devices: 7.32 us -> 13 us  [traded(): lax.ppermute(value, axis, [(i, i ^ mask) for i in range(lax.axis_size(axi...]
    unnamed x2 -> x8, local copies, waits for them, and re-layouts: 0.01 us -> 3.74 us
    ppermute x3 -> x4, waiting for transfers between devices: 5.92 us -> 2.98 us  [shifted(): lax.ppermute(value, axis, [(i, (i + step) % peers) for i in range(peers)])]
    ppermute x20 -> x19, starting transfers between devices: 18.5 us -> 20.3 us  [traded(): lax.ppermute(value, axis, [(i, i ^ mask) for i in range(lax.axis_size(axi...]
    ppermute x3 -> x4, starting transfers between devices: 4.59 us -> 5.52 us  [shifted(): lax.ppermute(value, axis, [(i, (i + step) % peers) for i in range(peers)])]
    pallas_call x2 -> x1, Pallas kernels: 3.42 us -> 2.52 us  [entry_call(): pl.pallas_call(functools.partial(entry_kernel, slabs, per_slab), out_shap...]
  transfers between devices with their start and end apart: 23 -> 23, of which waited for: 7 -> 17; matrix products, arithmetic and copies ran while one was open for 0% -> 0% of each run, Pallas kernels for 23% -> 16%
where the time goes in v10:
time: 62.5 us; the launch traced here: 62.3 us
  starting transfers between devices  25.8 us (41%)
  Pallas kernels  16.5 us (26%)
  waiting for transfers between devices  16 us (26%)
  local copies, waits for them, and re-layouts  3.81 us (6%)
    ppermute x19, starting transfers between devices, traded(): lax.ppermute(value, axis, [(i, i ^ mask) for i in range(lax.axis_size(axi...  20.3 us
    pallas_call x4, Pallas kernels, call(): pl.pallas_call(kernel, out_shape=outs, in_specs=[VMEM if aliases is None...  14 us
    ppermute x19, waiting for transfers between devices, traded(): lax.ppermute(value, axis, [(i, i ^ mask) for i in range(lax.axis_size(axi...  13 us
    ppermute x4, starting transfers between devices, shifted(): lax.ppermute(value, axis, [(i, (i + step) % peers) for i in range(peers)])  5.52 us
    unnamed x8, local copies, waits for them, and re-layouts  3.74 us
    ppermute x4, waiting for transfers between devices, shifted(): lax.ppermute(value, axis, [(i, (i + step) % peers) for i in range(peers)])  2.98 us
    pallas_call x1, Pallas kernels, entry_call(): pl.pallas_call(functools.partial(entry_kernel, slabs, per_slab), out_shap...  2.52 us
  transfers between devices with their start and end apart: 23, of which 17 were waited for; matrix products, arithmetic and copies ran while one was open for 0% of the time, Pallas kernels for 16%

profile of v10, /device:TPU:0, one launch (start us, length us, event | category | flops | bytes accessed | tf_op | source)
XLA Modules:
  0.0 62.3 jit_solution(7033729294631641775)
XLA Ops:
  0.0 2.5 %shard_map.82 = (bf16[4,4,96,256]{3,2,1,0:T(8,128)(2,1)S(1)}, bf16[3,3,3,256,256]{4,3,2,1,0:T(8,128)(2,1)S(1)}, bf16[2,4,96,256]{3,2,1,0:T(8,128)(2,1)S(1)}, f32...) custom-call(bf16[4,4,96,256]{3,2,1,0:T(8,128)(2,1)} %feats_hbm.1, ...), custom_call_target="tpu_custom_call" | custom-call | flops 1572864 | bytes 7077888 | tf_op jit(solution)/shard_map/pallas_call | solution.py:173
  2.5 0.0 copy-start.1
  2.5 1.7 %copy-done.1 = bf16[3,3,3,256,256]{4,3,2,1,0:T(8,128)(2,1)} copy-done((bf16[3,3,3,256,256]{4,3,2,1,0:T(8,128)(2,1)}, bf16[3,3,3,256,256]{4,3,2,1,0:T(8,128)(2,1)S(1)}, u32[]{:S(2)}) %copy-start.1) | copy-done | bytes 3538968
  4.3 0.5 collective-permute-start
  4.7 0.1 collective-permute-start.1
  4.8 0.7 %collective-permute-done = f32[1,512]{1,0:T(1,128)S(1)} collective-permute-done((f32[1,512]{1,0:T(1,128)S(1)}, f32[1,512]{1,0:T(1,128)S(1)}, u32[]{:S(2)}, u32[]{:S(2)}) %collective-permute-start) | collective-permute-done | bytes 2080 | tf_op jit(solution)/shard_map/ppermute | solution.py:32
  5.5 0.6 collective-permute-done.1.refs_5_.refs_6_
  6.2 2.6 %collective-permute-start.2 = (bf16[1,4,96,256]{3,2,1,0:T(8,128)(2,1)S(1)}, bf16[1,4,96,256]{3,2,1,0:T(8,128)(2,1)S(1)}, u32[]{:S(2)}, u32[]{:S(2)}) collective-permute-start(bf16[1,4,96,256]{3,2,1,0:T(8,128)(2,1)S(1)} %get-tuple-element.46), channel_id=1, source_target_pairs={{0,2},{2,4},{4,6},{6,8},{8,10},{10,12},{12,14},{14,16},{16,18},{18... | collective-permute-start | bytes 589832 | tf_op jit(solution)/shard_map/ppermute | solution.py:37
  8.8 3.6 %collective-permute-start.5 = (f32[1,512]{1,0:T(1,128)S(1)}, f32[1,512]{1,0:T(1,128)S(1)}, u32[]{:S(2)}, u32[]{:S(2)}) collective-permute-start(f32[1,512]{1,0:T(1,128)S(1)} %add.12), channel_id=1, source_target_pairs={{0,24},{2,26},{4,28},{6,30},{8,16},{10,18},{12,20},{14,22},{16,8},... | collective-permute-start | bytes 6152 | tf_op jit(solution)/shard_map/ppermute | solution.py:32
  12.4 0.0 collective-permute-start.4
  12.4 0.8 %collective-permute-start.3 = (f32[1,512]{1,0:T(1,128)S(1)}, f32[1,512]{1,0:T(1,128)S(1)}, u32[]{:S(2)}, u32[]{:S(2)}) collective-permute-start(f32[1,512]{1,0:T(1,128)S(1)} %add.12), channel_id=1, source_target_pairs={{0,8},{2,10},{4,12},{6,14},{8,0},{10,2},{12,4},{14,6},{16,24},{18,... | collective-permute-start | bytes 6152 | tf_op jit(solution)/shard_map/ppermute | solution.py:32
  13.2 1.0 %collective-permute-done.5 = f32[1,512]{1,0:T(1,128)S(1)} collective-permute-done((f32[1,512]{1,0:T(1,128)S(1)}, f32[1,512]{1,0:T(1,128)S(1)}, u32[]{:S(2)}, u32[]{:S(2)}) %collective-permute-start.5) | collective-permute-done | bytes 2080 | tf_op jit(solution)/shard_map/ppermute | solution.py:32
  14.2 2.7 %collective-permute-done.4 = f32[1,512]{1,0:T(1,128)S(1)} collective-permute-done((f32[1,512]{1,0:T(1,128)S(1)}, f32[1,512]{1,0:T(1,128)S(1)}, u32[]{:S(2)}, u32[]{:S(2)}) %collective-permute-start.4) | collective-permute-done | bytes 2080 | tf_op jit(solution)/shard_map/ppermute | solution.py:32
  16.9 0.0 collective-permute-done.3
  16.9 2.1 %collective-permute-start.8 = (f32[4,512]{1,0:T(4,128)S(1)}, f32[4,512]{1,0:T(4,128)S(1)}, u32[]{:S(2)}, u32[]{:S(2)}) collective-permute-start(f32[4,512]{1,0:T(4,128)S(1)} %pad_maximum_fusion.2.refs_0_), channel_id=1, source_target_pairs={{0,6},{2,4},{4,2},{6,0},{8,14},{10,12},{12,10},{14,8},{16,22},{18,... | collective-permute-start | bytes 24584 | tf_op jit(solution)/shard_map/ppermute | solution.py:32
  19.0 0.9 %collective-permute-start.7 = (f32[4,512]{1,0:T(4,128)S(1)}, f32[4,512]{1,0:T(4,128)S(1)}, u32[]{:S(2)}, u32[]{:S(2)}) collective-permute-start(f32[4,512]{1,0:T(4,128)S(1)} %pad_maximum_fusion.2.refs_0_), channel_id=1, source_target_pairs={{0,4},{2,6},{4,0},{6,2},{8,12},{10,14},{12,8},{14,10},{16,20},{18,... | collective-permute-start | bytes 24584 | tf_op jit(solution)/shard_map/ppermute | solution.py:32
  19.9 0.5 collective-permute-start.6
  20.5 1.5 %collective-permute-start.9 = (bf16[1,4,96,256]{3,2,1,0:T(8,128)(2,1)S(1)}, bf16[1,4,96,256]{3,2,1,0:T(8,128)(2,1)S(1)}, u32[]{:S(2)}, u32[]{:S(2)}) collective-permute-start(bf16[1,4,96,256]{3,2,1,0:T(8,128)(2,1)S(1)} %get-tuple-element.53), channel_id=1, source_target_pairs={{0,2},{2,4},{4,6},{6,8},{8,10},{10,12},{12,14},{14,16},{16,18},{18... | collective-permute-start | bytes 589832 | tf_op jit(solution)/shard_map/ppermute | solution.py:37
  22.0 0.0 collective-permute-done.2.refs_0_
  22.0 0.0 collective-permute-done.8.refs_3_
  22.0 0.7 %collective-permute-done.7.refs_2_ = f32[4,512]{1,0:T(4,128)S(1)} collective-permute-done((f32[4,512]{1,0:T(4,128)S(1)}, f32[4,512]{1,0:T(4,128)S(1)}, u32[]{:S(2)}, u32[]{:S(2)}) %collective-permute-start.7) | collective-permute-done | bytes 8224 | tf_op jit(solution)/shard_map/ppermute | solution.py:32
  22.7 1.0 %collective-permute-done.6.refs_1_ = f32[4,512]{1,0:T(4,128)S(1)} collective-permute-done((f32[4,512]{1,0:T(4,128)S(1)}, f32[4,512]{1,0:T(4,128)S(1)}, u32[]{:S(2)}, u32[]{:S(2)}) %collective-permute-start.6) | collective-permute-done | bytes 8224 | tf_op jit(solution)/shard_map/ppermute | solution.py:32
  23.7 0.0 copy-start.2
  23.7 2.0 %copy-done.2 = bf16[3,3,3,256,256]{4,3,2,1,0:T(8,128)(2,1)S(1)} copy-done((bf16[3,3,3,256,256]{4,3,2,1,0:T(8,128)(2,1)S(1)}, bf16[3,3,3,256,256]{4,3,2,1,0:T(8,128)(2,1)}, u32[]{:S(2)}) %copy-start.2) | copy-done | bytes 3538968
  25.7 0.0 copy-start.3
  25.7 3.2 %shard_map.83 = (bf16[2,6,96,256]{3,2,1,0:T(8,128)(2,1)S(1)}, f32[2,256]{1,0:T(2,128)S(1)}, bf16[2,4,96,256]{3,2,1,0:T(8,128)(2,1)S(1)}, f32[1,512]{1,0:T(1,128)S(1)}, bf16[2,1,96,256]{3,2,1,0:T(8,128)(2,1)S(1)}) custom-call(f32[24,256]{1,0:T(8,128)S(1)} %get-tuple-element.65.aux, f32[4,512]{1,0:T(4,128)S(1)} %pad_maximum_fusion.2.refs_0_, ...), custom_call_target="tpu_custom_call" | custom-call | flops 2717908992 | bytes 1048576 | tf_op jit(solution)/shard_map/pallas_call | solution.py:339
  28.9 0.8 %collective-permute-done.9.refs_1_ = bf16[1,4,96,256]{3,2,1,0:T(8,128)(2,1)S(1)} collective-permute-done((bf16[1,4,96,256]{3,2,1,0:T(8,128)(2,1)S(1)}, bf16[1,4,96,256]{3,2,1,0:T(8,128)(2,1)S(1)}, u32[]{:S(2)}, u32[]{:S(2)}) %collective-permute-start.9) | collective-permute-done | bytes 196640 | tf_op jit(solution)/shard_map/ppermute | solution.py:37
  29.8 0.1 collective-permute-start.10
  29.8 0.5 collective-permute-start.13
  30.3 0.8 %collective-permute-done.10.refs_2_ = bf16[2,1,96,256]{3,2,1,0:T(8,128)(2,1)S(1)} collective-permute-done((bf16[2,1,96,256]{3,2,1,0:T(8,128)(2,1)S(1)}, bf16[2,1,96,256]{3,2,1,0:T(8,128)(2,1)S(1)}, u32[]{:S(2)}, u32[]{:S(2)}) %collective-permute-start.10) | collective-permute-done | bytes 98336 | tf_op jit(solution)/shard_map/ppermute | solution.py:32
  31.1 0.0 copy-done.3
  31.1 0.0 copy-start
  31.1 3.0 %shard_map.84 = (bf16[2,4,96,256]{3,2,1,0:T(8,128)(2,1)S(1)}, f32[1,512]{1,0:T(1,128)S(1)}, bf16[2,1,96,256]{3,2,1,0:T(8,128)(2,1)S(1)}) custom-call(f32[24,256]{1,0:T(8,128)S(1)} %get-tuple-element.65.aux, bf16[1,4,96,256]{3,2,1,0:T(8,128)(2,1)S(1)} %collective-permute-done.2.refs_0_, bf16[1,4,96,256]{3,2,1,0:T(8,128)(2,1)S(1)} %collective-permute-done.9.refs_1_, ...), custom_call_target="tpu_custom_call" | custom-call | flops 2717908992 | bytes 1048576 | tf_op jit(solution)/shard_map/pallas_call | solution.py:339
  34.2 0.2 collective-permute-start.11
  34.4 0.4 collective-permute-start.12
  34.8 0.6 collective-permute-done.11
  35.4 0.0 collective-permute-done.13.refs_6_
  35.4 0.3 collective-permute-done.12.refs_5_
  35.7 0.0 collective-permute-start.14
  35.7 1.2 %collective-permute-start.17 = (f32[1,512]{1,0:T(1,128)S(1)}, f32[1,512]{1,0:T(1,128)S(1)}, u32[]{:S(2)}, u32[]{:S(2)}) collective-permute-start(f32[1,512]{1,0:T(1,128)S(1)} %add.14), channel_id=1, source_target_pairs={{0,24},{2,26},{4,28},{6,30},{8,16},{10,18},{12,20},{14,22},{16,8},... | collective-permute-start | bytes 6152 | tf_op jit(solution)/shard_map/ppermute | solution.py:32
  36.9 0.6 collective-permute-start.16
  37.5 2.6 %collective-permute-start.15 = (f32[1,512]{1,0:T(1,128)S(1)}, f32[1,512]{1,0:T(1,128)S(1)}, u32[]{:S(2)}, u32[]{:S(2)}) collective-permute-start(f32[1,512]{1,0:T(1,128)S(1)} %add.14), channel_id=1, source_target_pairs={{0,8},{2,10},{4,12},{6,14},{8,0},{10,2},{12,4},{14,6},{16,24},{18,... | collective-permute-start | bytes 6152 | tf_op jit(solution)/shard_map/ppermute | solution.py:32
  40.1 1.0 %collective-permute-done.17 = f32[1,512]{1,0:T(1,128)S(1)} collective-permute-done((f32[1,512]{1,0:T(1,128)S(1)}, f32[1,512]{1,0:T(1,128)S(1)}, u32[]{:S(2)}, u32[]{:S(2)}) %collective-permute-start.17) | collective-permute-done | bytes 2080 | tf_op jit(solution)/shard_map/ppermute | solution.py:32
  41.1 0.3 collective-permute-done.16
  41.4 0.3 collective-permute-done.15
  41.7 5.6 %collective-permute-start.21 = (f32[4,512]{1,0:T(4,128)S(1)}, f32[4,512]{1,0:T(4,128)S(1)}, u32[]{:S(2)}, u32[]{:S(2)}) collective-permute-start(f32[4,512]{1,0:T(4,128)S(1)} %pad_maximum_fusion.3.refs_0_), channel_id=1, source_target_pairs={{0,6},{2,4},{4,2},{6,0},{8,14},{10,12},{12,10},{14,8},{16,22},{18,... | collective-permute-start | bytes 24584 | tf_op jit(solution)/shard_map/ppermute | solution.py:32
  47.3 0.0 collective-permute-start.20
  47.3 0.6 %collective-permute-start.19 = (f32[4,512]{1,0:T(4,128)S(1)}, f32[4,512]{1,0:T(4,128)S(1)}, u32[]{:S(2)}, u32[]{:S(2)}) collective-permute-start(f32[4,512]{1,0:T(4,128)S(1)} %pad_maximum_fusion.3.refs_0_), channel_id=1, source_target_pairs={{0,2},{2,0},{4,6},{6,4},{8,10},{10,8},{12,14},{14,12},{16,18},{18,... | collective-permute-start | bytes 24584 | tf_op jit(solution)/shard_map/ppermute | solution.py:32
  47.9 1.4 %collective-permute-start.18 = (bf16[1,4,96,256]{3,2,1,0:T(8,128)(2,1)S(1)}, bf16[1,4,96,256]{3,2,1,0:T(8,128)(2,1)S(1)}, u32[]{:S(2)}, u32[]{:S(2)}) collective-permute-start(bf16[1,4,96,256]{3,2,1,0:T(8,128)(2,1)S(1)} %get-tuple-element.67), channel_id=1, source_target_pairs={{0,2},{2,4},{4,6},{6,8},{8,10},{10,12},{12,14},{14,16},{16,18},{18... | collective-permute-start | bytes 589832 | tf_op jit(solution)/shard_map/ppermute | solution.py:37
  49.3 0.0 collective-permute-done.14.refs_0_
  49.3 0.0 collective-permute-done.21.refs_3_
  49.3 1.6 %collective-permute-done.20.refs_2_ = f32[4,512]{1,0:T(4,128)S(1)} collective-permute-done((f32[4,512]{1,0:T(4,128)S(1)}, f32[4,512]{1,0:T(4,128)S(1)}, u32[]{:S(2)}, u32[]{:S(2)}) %collective-permute-start.20) | collective-permute-done | bytes 8224 | tf_op jit(solution)/shard_map/ppermute | solution.py:32
  50.9 0.1 collective-permute-done.19.refs_1_
  51.0 0.0 copy-done
  51.0 4.0 %shard_map.85 = (bf16[2,6,96,256]{3,2,1,0:T(8,128)(2,1)S(1)}, f32[2,256]{1,0:T(2,128)S(1)}, f32[4,4,96,256]{3,2,1,0:T(8,128)}) custom-call(f32[24,256]{1,0:T(8,128)S(1)} %get-tuple-element.65.aux, f32[4,512]{1,0:T(4,128)S(1)} %pad_maximum_fusion.3.refs_0_, f32[4,512]{1,0:T(4,128)S(1)} %collective-permute-done.19.refs_1_, ...), custom_call_target="tpu_custom_call" | custom-call | flops 2717908992 | bytes 1048576 | tf_op jit(solution)/shard_map/pallas_call | solution.py:339
  55.0 2.2 %collective-permute-done.18.refs_1_ = bf16[1,4,96,256]{3,2,1,0:T(8,128)(2,1)S(1)} collective-permute-done((bf16[1,4,96,256]{3,2,1,0:T(8,128)(2,1)S(1)}, bf16[1,4,96,256]{3,2,1,0:T(8,128)(2,1)S(1)}, u32[]{:S(2)}, u32[]{:S(2)}) %collective-permute-start.18) | collective-permute-done | bytes 196640 | tf_op jit(solution)/shard_map/ppermute | solution.py:37
  57.2 0.1 collective-permute-start.22
  57.3 1.3 %collective-permute-done.22.refs_2_ = bf16[2,1,96,256]{3,2,1,0:T(8,128)(2,1)S(1)} collective-permute-done((bf16[2,1,96,256]{3,2,1,0:T(8,128)(2,1)S(1)}, bf16[2,1,96,256]{3,2,1,0:T(8,128)(2,1)S(1)}, u32[]{:S(2)}, u32[]{:S(2)}) %collective-permute-start.22) | collective-permute-done | bytes 98336 | tf_op jit(solution)/shard_map/ppermute | solution.py:32
  58.6 3.7 %shard_map.86 = f32[4,4,96,256]{3,2,1,0:T(8,128)} custom-call(f32[24,256]{1,0:T(8,128)S(1)} %get-tuple-element.65.aux, bf16[1,4,96,256]{3,2,1,0:T(8,128)(2,1)S(1)} %collective-permute-done.14.refs_0_, bf16[1,4,96,256]{3,2,1,0:T(8,128)(2,1)S(1)} %collective-permute-done.18.refs_1_, ...), custom_call_target="tpu_custom_call", output_to_operand_aliasing={{}: (8, {})} | custom-call | flops 2717908992 | bytes 1048576 | tf_op jit(solution)/shard_map/pallas_call | solution.py:339
  (11 shorter events, 0.1 us)
Async XLA Ops:
  2.5 1.7 %copy-start.1 = (bf16[3,3,3,256,256]{4,3,2,1,0:T(8,128)(2,1)}, bf16[3,3,3,256,256]{4,3,2,1,0:T(8,128)(2,1)S(1)}, u32[]{:S(2)}) copy-start(bf16[3,3,3,256,256]{4,3,2,1,0:T(8,128)(2,1)S(1)} %get-tuple-element.50.refs_7_.refs_5_) | copy-start | bytes 10616836
  4.3 1.3 %collective-permute-start = (f32[1,512]{1,0:T(1,128)S(1)}, f32[1,512]{1,0:T(1,128)S(1)}, u32[]{:S(2)}, u32[]{:S(2)}) collective-permute-start(f32[1,512]{1,0:T(1,128)S(1)} %get-tuple-element.43), channel_id=1, source_target_pairs={{0,1},{1,0},{2,3},{3,2},{4,5},{5,4},{6,7},{7,6},{8,9},{9,8},{10,11... | collective-permute-start | bytes 6152 | tf_op jit(solution)/shard_map/ppermute | solution.py:32
  4.7 1.4 %collective-permute-start.1 = (bf16[4,1,96,256]{3,2,1,0:T(8,128)(2,1)S(1)}, bf16[4,1,96,256]{3,2,1,0:T(8,128)(2,1)S(1)}, u32[]{:S(2)}, u32[]{:S(2)}) collective-permute-start(bf16[4,1,96,256]{3,2,1,0:T(8,128)(2,1)S(1)} %get-tuple-element.44), channel_id=1, source_target_pairs={{0,1},{1,0},{2,3},{3,2},{4,5},{5,4},{6,7},{7,6},{8,9},{9,8},{10,11... | collective-permute-start | bytes 589832 | tf_op jit(solution)/shard_map/ppermute | solution.py:32
  6.2 15.8 %collective-permute-start.2 = (bf16[1,4,96,256]{3,2,1,0:T(8,128)(2,1)S(1)}, bf16[1,4,96,256]{3,2,1,0:T(8,128)(2,1)S(1)}, u32[]{:S(2)}, u32[]{:S(2)}) collective-permute-start(bf16[1,4,96,256]{3,2,1,0:T(8,128)(2,1)S(1)} %get-tuple-element.46), channel_id=1, source_target_pairs={{0,2},{2,4},{4,6},{6,8},{8,10},{10,12},{12,14},{14,16},{16,18},{18... | collective-permute-start | bytes 589832 | tf_op jit(solution)/shard_map/ppermute | solution.py:37
  8.8 5.4 %collective-permute-start.5 = (f32[1,512]{1,0:T(1,128)S(1)}, f32[1,512]{1,0:T(1,128)S(1)}, u32[]{:S(2)}, u32[]{:S(2)}) collective-permute-start(f32[1,512]{1,0:T(1,128)S(1)} %add.12), channel_id=1, source_target_pairs={{0,24},{2,26},{4,28},{6,30},{8,16},{10,18},{12,20},{14,22},{16,8},... | collective-permute-start | bytes 6152 | tf_op jit(solution)/shard_map/ppermute | solution.py:32
  12.4 4.5 %collective-permute-start.4 = (f32[1,512]{1,0:T(1,128)S(1)}, f32[1,512]{1,0:T(1,128)S(1)}, u32[]{:S(2)}, u32[]{:S(2)}) collective-permute-start(f32[1,512]{1,0:T(1,128)S(1)} %add.12), channel_id=1, source_target_pairs={{0,16},{2,18},{4,20},{6,22},{8,24},{10,26},{12,28},{14,30},{16,0},... | collective-permute-start | bytes 6152 | tf_op jit(solution)/shard_map/ppermute | solution.py:32
  12.4 4.5 %collective-permute-start.3 = (f32[1,512]{1,0:T(1,128)S(1)}, f32[1,512]{1,0:T(1,128)S(1)}, u32[]{:S(2)}, u32[]{:S(2)}) collective-permute-start(f32[1,512]{1,0:T(1,128)S(1)} %add.12), channel_id=1, source_target_pairs={{0,8},{2,10},{4,12},{6,14},{8,0},{10,2},{12,4},{14,6},{16,24},{18,... | collective-permute-start | bytes 6152 | tf_op jit(solution)/shard_map/ppermute | solution.py:32
  16.9 5.1 %collective-permute-start.8 = (f32[4,512]{1,0:T(4,128)S(1)}, f32[4,512]{1,0:T(4,128)S(1)}, u32[]{:S(2)}, u32[]{:S(2)}) collective-permute-start(f32[4,512]{1,0:T(4,128)S(1)} %pad_maximum_fusion.2.refs_0_), channel_id=1, source_target_pairs={{0,6},{2,4},{4,2},{6,0},{8,14},{10,12},{12,10},{14,8},{16,22},{18,... | collective-permute-start | bytes 24584 | tf_op jit(solution)/shard_map/ppermute | solution.py:32
  19.0 3.7 %collective-permute-start.7 = (f32[4,512]{1,0:T(4,128)S(1)}, f32[4,512]{1,0:T(4,128)S(1)}, u32[]{:S(2)}, u32[]{:S(2)}) collective-permute-start(f32[4,512]{1,0:T(4,128)S(1)} %pad_maximum_fusion.2.refs_0_), channel_id=1, source_target_pairs={{0,4},{2,6},{4,0},{6,2},{8,12},{10,14},{12,8},{14,10},{16,20},{18,... | collective-permute-start | bytes 24584 | tf_op jit(solution)/shard_map/ppermute | solution.py:32
  19.9 3.8 %collective-permute-start.6 = (f32[4,512]{1,0:T(4,128)S(1)}, f32[4,512]{1,0:T(4,128)S(1)}, u32[]{:S(2)}, u32[]{:S(2)}) collective-permute-start(f32[4,512]{1,0:T(4,128)S(1)} %pad_maximum_fusion.2.refs_0_), channel_id=1, source_target_pairs={{0,2},{2,0},{4,6},{6,4},{8,10},{10,8},{12,14},{14,12},{16,18},{18,... | collective-permute-start | bytes 24584 | tf_op jit(solution)/shard_map/ppermute | solution.py:32
  20.5 9.3 %collective-permute-start.9 = (bf16[1,4,96,256]{3,2,1,0:T(8,128)(2,1)S(1)}, bf16[1,4,96,256]{3,2,1,0:T(8,128)(2,1)S(1)}, u32[]{:S(2)}, u32[]{:S(2)}) collective-permute-start(bf16[1,4,96,256]{3,2,1,0:T(8,128)(2,1)S(1)} %get-tuple-element.53), channel_id=1, source_target_pairs={{0,2},{2,4},{4,6},{6,8},{8,10},{10,12},{12,14},{14,16},{16,18},{18... | collective-permute-start | bytes 589832 | tf_op jit(solution)/shard_map/ppermute | solution.py:37
  23.7 2.0 %copy-start.2 = (bf16[3,3,3,256,256]{4,3,2,1,0:T(8,128)(2,1)S(1)}, bf16[3,3,3,256,256]{4,3,2,1,0:T(8,128)(2,1)}, u32[]{:S(2)}) copy-start(bf16[3,3,3,256,256]{4,3,2,1,0:T(8,128)(2,1)} %copy-done.1) | copy-start | bytes 10616836
  25.7 5.4 %copy-start.3 = (bf16[3,3,3,256,256]{4,3,2,1,0:T(8,128)(2,1)S(1)}, bf16[3,3,3,256,256]{4,3,2,1,0:T(8,128)(2,1)}, u32[]{:S(2)}) copy-start(bf16[3,3,3,256,256]{4,3,2,1,0:T(8,128)(2,1)} %copy-done.1) | copy-start | bytes 10616836
  29.8 1.4 %collective-permute-start.10 = (bf16[2,1,96,256]{3,2,1,0:T(8,128)(2,1)S(1)}, bf16[2,1,96,256]{3,2,1,0:T(8,128)(2,1)S(1)}, u32[]{:S(2)}, u32[]{:S(2)}) collective-permute-start(bf16[2,1,96,256]{3,2,1,0:T(8,128)(2,1)S(1)} %pad_maximum_fusion), channel_id=1, source_target_pairs={{0,1},{1,0},{2,3},{3,2},{4,5},{5,4},{6,7},{7,6},{8,9},{9,8},{10,11... | collective-permute-start | bytes 294920 | tf_op jit(solution)/shard_map/ppermute | solution.py:32
  29.8 5.6 %collective-permute-start.13 = (bf16[2,1,96,256]{3,2,1,0:T(8,128)(2,1)S(1)}, bf16[2,1,96,256]{3,2,1,0:T(8,128)(2,1)S(1)}, u32[]{:S(2)}, u32[]{:S(2)}) collective-permute-start(bf16[2,1,96,256]{3,2,1,0:T(8,128)(2,1)S(1)} %get-tuple-element.62), channel_id=1, source_target_pairs={{0,1},{1,0},{2,3},{3,2},{4,5},{5,4},{6,7},{7,6},{8,9},{9,8},{10,11... | collective-permute-start | bytes 294920 | tf_op jit(solution)/shard_map/ppermute | solution.py:32
  31.1 19.8 %copy-start = (bf16[3,3,3,256,256]{4,3,2,1,0:T(8,128)(2,1)S(1)}, bf16[3,3,3,256,256]{4,3,2,1,0:T(8,128)(2,1)}, u32[]{:S(2)}) copy-start(bf16[3,3,3,256,256]{4,3,2,1,0:T(8,128)(2,1)} %refs_5_.1) | copy-start | bytes 10616836
  34.2 1.2 %collective-permute-start.11 = (f32[1,512]{1,0:T(1,128)S(1)}, f32[1,512]{1,0:T(1,128)S(1)}, u32[]{:S(2)}, u32[]{:S(2)}) collective-permute-start(f32[1,512]{1,0:T(1,128)S(1)} %get-tuple-element.60), channel_id=1, source_target_pairs={{0,1},{1,0},{2,3},{3,2},{4,5},{5,4},{6,7},{7,6},{8,9},{9,8},{10,11... | collective-permute-start | bytes 6152 | tf_op jit(solution)/shard_map/ppermute | solution.py:32
  34.4 1.3 %collective-permute-start.12 = (bf16[2,1,96,256]{3,2,1,0:T(8,128)(2,1)S(1)}, bf16[2,1,96,256]{3,2,1,0:T(8,128)(2,1)S(1)}, u32[]{:S(2)}, u32[]{:S(2)}) collective-permute-start(bf16[2,1,96,256]{3,2,1,0:T(8,128)(2,1)S(1)} %get-tuple-element.61), channel_id=1, source_target_pairs={{0,1},{1,0},{2,3},{3,2},{4,5},{5,4},{6,7},{7,6},{8,9},{9,8},{10,11... | collective-permute-start | bytes 294920 | tf_op jit(solution)/shard_map/ppermute | solution.py:32
  35.7 13.6 %collective-permute-start.14 = (bf16[1,4,96,256]{3,2,1,0:T(8,128)(2,1)S(1)}, bf16[1,4,96,256]{3,2,1,0:T(8,128)(2,1)S(1)}, u32[]{:S(2)}, u32[]{:S(2)}) collective-permute-start(bf16[1,4,96,256]{3,2,1,0:T(8,128)(2,1)S(1)} %get-tuple-element.64), channel_id=1, source_target_pairs={{0,2},{2,4},{4,6},{6,8},{8,10},{10,12},{12,14},{14,16},{16,18},{18... | collective-permute-start | bytes 589832 | tf_op jit(solution)/shard_map/ppermute | solution.py:37
  35.7 5.4 %collective-permute-start.17 = (f32[1,512]{1,0:T(1,128)S(1)}, f32[1,512]{1,0:T(1,128)S(1)}, u32[]{:S(2)}, u32[]{:S(2)}) collective-permute-start(f32[1,512]{1,0:T(1,128)S(1)} %add.14), channel_id=1, source_target_pairs={{0,24},{2,26},{4,28},{6,30},{8,16},{10,18},{12,20},{14,22},{16,8},... | collective-permute-start | bytes 6152 | tf_op jit(solution)/shard_map/ppermute | solution.py:32
  36.9 4.5 %collective-permute-start.16 = (f32[1,512]{1,0:T(1,128)S(1)}, f32[1,512]{1,0:T(1,128)S(1)}, u32[]{:S(2)}, u32[]{:S(2)}) collective-permute-start(f32[1,512]{1,0:T(1,128)S(1)} %add.14), channel_id=1, source_target_pairs={{0,16},{2,18},{4,20},{6,22},{8,24},{10,26},{12,28},{14,30},{16,0},... | collective-permute-start | bytes 6152 | tf_op jit(solution)/shard_map/ppermute | solution.py:32
  37.5 4.2 %collective-permute-start.15 = (f32[1,512]{1,0:T(1,128)S(1)}, f32[1,512]{1,0:T(1,128)S(1)}, u32[]{:S(2)}, u32[]{:S(2)}) collective-permute-start(f32[1,512]{1,0:T(1,128)S(1)} %add.14), channel_id=1, source_target_pairs={{0,8},{2,10},{4,12},{6,14},{8,0},{10,2},{12,4},{14,6},{16,24},{18,... | collective-permute-start | bytes 6152 | tf_op jit(solution)/shard_map/ppermute | solution.py:32
  41.7 7.6 %collective-permute-start.21 = (f32[4,512]{1,0:T(4,128)S(1)}, f32[4,512]{1,0:T(4,128)S(1)}, u32[]{:S(2)}, u32[]{:S(2)}) collective-permute-start(f32[4,512]{1,0:T(4,128)S(1)} %pad_maximum_fusion.3.refs_0_), channel_id=1, source_target_pairs={{0,6},{2,4},{4,2},{6,0},{8,14},{10,12},{12,10},{14,8},{16,22},{18,... | collective-permute-start | bytes 24584 | tf_op jit(solution)/shard_map/ppermute | solution.py:32
  47.3 3.7 %collective-permute-start.20 = (f32[4,512]{1,0:T(4,128)S(1)}, f32[4,512]{1,0:T(4,128)S(1)}, u32[]{:S(2)}, u32[]{:S(2)}) collective-permute-start(f32[4,512]{1,0:T(4,128)S(1)} %pad_maximum_fusion.3.refs_0_), channel_id=1, source_target_pairs={{0,4},{2,6},{4,0},{6,2},{8,12},{10,14},{12,8},{14,10},{16,20},{18,... | collective-permute-start | bytes 24584 | tf_op jit(solution)/shard_map/ppermute | solution.py:32
  47.3 3.7 %collective-permute-start.19 = (f32[4,512]{1,0:T(4,128)S(1)}, f32[4,512]{1,0:T(4,128)S(1)}, u32[]{:S(2)}, u32[]{:S(2)}) collective-permute-start(f32[4,512]{1,0:T(4,128)S(1)} %pad_maximum_fusion.3.refs_0_), channel_id=1, source_target_pairs={{0,2},{2,0},{4,6},{6,4},{8,10},{10,8},{12,14},{14,12},{16,18},{18,... | collective-permute-start | bytes 24584 | tf_op jit(solution)/shard_map/ppermute | solution.py:32
  47.9 9.3 %collective-permute-start.18 = (bf16[1,4,96,256]{3,2,1,0:T(8,128)(2,1)S(1)}, bf16[1,4,96,256]{3,2,1,0:T(8,128)(2,1)S(1)}, u32[]{:S(2)}, u32[]{:S(2)}) collective-permute-start(bf16[1,4,96,256]{3,2,1,0:T(8,128)(2,1)S(1)} %get-tuple-element.67), channel_id=1, source_target_pairs={{0,2},{2,4},{4,6},{6,8},{8,10},{10,12},{12,14},{14,16},{16,18},{18... | collective-permute-start | bytes 589832 | tf_op jit(solution)/shard_map/ppermute | solution.py:37
  57.2 1.4 %collective-permute-start.22 = (bf16[2,1,96,256]{3,2,1,0:T(8,128)(2,1)S(1)}, bf16[2,1,96,256]{3,2,1,0:T(8,128)(2,1)S(1)}, u32[]{:S(2)}, u32[]{:S(2)}) collective-permute-start(bf16[2,1,96,256]{3,2,1,0:T(8,128)(2,1)S(1)} %pad_maximum_fusion.1), channel_id=1, source_target_pairs={{0,1},{1,0},{2,3},{3,2},{4,5},{5,4},{6,7},{7,6},{8,9},{9,8},{10,11... | collective-permute-start | bytes 294920 | tf_op jit(solution)/shard_map/ppermute | solution.py:32

commit v11 on v9

v11 whole, which is shorter than its diff:
```python
import functools

import jax
import jax.numpy as jnp
from jax import lax
from jax.experimental import pallas as pl
from jax.experimental.pallas import tpu as pltpu
from jax.sharding import PartitionSpec as P

GROUPS = 32
TAIL = 2
F32, BF16 = jnp.float32, jnp.bfloat16


def vmem_params():
    return pltpu.CompilerParams(vmem_limit_bytes=32 << 20)


def shaped(shape, dtype=BF16):
    return jax.ShapeDtypeStruct(tuple(shape), dtype)


def in_hbm(value):
    return pltpu.with_memory_space_constraint(value, pltpu.HBM)


VMEM = pl.BlockSpec(memory_space=pltpu.VMEM)
ANYWHERE = pl.BlockSpec(memory_space=pl.ANY)


def traded(value, axis, mask):
    return lax.ppermute(value, axis, [(i, i ^ mask) for i in range(lax.axis_size(axis))])


def shifted(value, axis, step):
    peers = lax.axis_size(axis)
    return lax.ppermute(value, axis, [(i, (i + step) % peers) for i in range(peers)])


def stats_table(copies):
    return lax.all_to_all(copies, ("tm", "space"), 0, 0, tiled=True)


def corner_rows(before, after):
    before, after = lax.optimization_barrier((before, after))
    return before, row_halo(edges_of(before)), after


def row_halo(edges):
    if lax.axis_size("space") == 2:
        return [traded(edges, "space", 1)]
    return [shifted(edges[:, 1:], "space", 1), shifted(edges[:, :1], "space", -1)]


def edges_of(frames):
    rows = frames.shape[1]
    if lax.axis_size("space") == 2:
        return lax.dynamic_slice_in_dim(frames, (rows - 1) * (1 - lax.axis_index("space")), 1, axis=1)
    return jnp.concatenate([frames[:, :1], frames[:, rows - 1 :]], axis=1)


def edge_shape(frames, count):
    return (count, 1 if lax.axis_size("space") == 2 else 2) + frames.shape[2:]


def send_rows(source, frame, edges, at=0):
    rows = source.shape[1]
    if edges.shape[1] == 1:
        low = lax.axis_index("space") == 0
        edges[at + frame, 0] = jnp.where(low, source[frame, rows - 1], source[frame, 0])
    else:
        edges[at + frame, 0] = source[frame, 0]
        edges[at + frame, 1] = source[frame, rows - 1]


def add_stats(sums, values):
    width = values.shape[1]
    return (
        sums[0] + jnp.sum(values.reshape(-1, 8, width), axis=0),
        sums[1] + jnp.sum((values * values).reshape(-1, 8, width), axis=0),
    )


def no_stats(width):
    return jnp.zeros((8, width), F32), jnp.zeros((8, width), F32)


def store_stats(stats, sums):
    width = sums[0].shape[1]
    for k in range(2):
        stats[:, k * width : (k + 1) * width] = jnp.sum(sums[k], axis=0, keepdims=True)


def store_copies(copies, stats):
    copies[...] = jnp.broadcast_to(stats[...][None], copies.shape)


def stored_in_hbm(shape, dtype=BF16):
    return pltpu.HBM(tuple(shape), dtype)


def device_count():
    return lax.axis_size("tm") * lax.axis_size("space")


def entry_kernel(feats_hbm, copies_hbm, tail_hbm, edges_hbm, frames, edges, copies, stats, sems, out_sems):
    n_frames, n_rows, _, width = frames.shape
    loads = [pltpu.make_async_copy(feats_hbm.at[f], frames.at[f], sems.at[f]) for f in range(n_frames)]
    for copy in loads:
        copy.start()
    tail_copy = pltpu.make_async_copy(feats_hbm.at[pl.ds(n_frames - TAIL, TAIL)], tail_hbm, out_sems.at[0])
    tail_copy.start()
    sums = no_stats(width)
    for frame in range(n_frames):
        loads[frame].wait()
        for row in range(n_rows):
            sums = add_stats(sums, frames[frame, row].astype(F32))
        send_rows(frames, frame, edges)
    store_stats(stats, sums)
    store_copies(copies, stats)
    stores = [
        pltpu.make_async_copy(copies, copies_hbm, out_sems.at[1]),
        pltpu.make_async_copy(edges, edges_hbm, out_sems.at[2]),
    ]
    for copy in stores:
        copy.start()
    for copy in [tail_copy, *stores]:
        copy.wait()


def entry_call(feats):
    n_frames, width = feats.shape[0], feats.shape[3]
    copies = (device_count(), 1, 2 * width)
    return pl.pallas_call(
        entry_kernel,
        out_shape=[
            stored_in_hbm(copies, F32),
            stored_in_hbm((TAIL,) + feats.shape[1:]),
            stored_in_hbm(edge_shape(feats, n_frames)),
        ],
        in_specs=[ANYWHERE],
        out_specs=[ANYWHERE] * 3,
        scratch_shapes=[
            pltpu.VMEM(feats.shape, BF16),
            pltpu.VMEM(edge_shape(feats, n_frames), BF16),
            pltpu.VMEM(copies, F32),
            pltpu.VMEM((1, 2 * width), F32),
            pltpu.SemaphoreType.DMA((n_frames,)),
            pltpu.SemaphoreType.DMA((3,)),
        ],
        compiler_params=vmem_params(),
        cost_estimate=pl.CostEstimate(flops=4 * feats.size, bytes_accessed=4 * feats.size, transcendentals=0),
    )(in_hbm(feats))


def load_kernel(slabs, per_slab, n_big, clips_hbm, *refs):
    params_hbm, bigs_hbm, _ = refs[:4], refs[4 : 4 + n_big], refs[4 + n_big]
    bigs, (aux, params, clips, sems) = refs[5 + n_big : 5 + 2 * n_big], refs[5 + 2 * n_big :]
    width = aux.shape[1]
    clip_load = pltpu.make_async_copy(clips_hbm, clips, sems.at[0])
    param_loads = [pltpu.make_async_copy(p, params.at[k], sems.at[1 + k]) for k, p in enumerate(params_hbm)]
    loads = [pltpu.make_async_copy(src, dst, sems.at[5 + k]) for k, (src, dst) in enumerate(zip(bigs_hbm, bigs))]
    for copy in [clip_load, *param_loads, *loads]:
        copy.start()
    clip_load.wait()
    own = lax.axis_index("tm")
    own_clip = clips[own]
    slabs_in = jnp.int32(0)
    for slab in range(slabs):
        same = (clips[slab] == own_clip).astype(jnp.int32)
        slabs_in = slabs_in + same
        aux[slab : slab + 1] = jnp.full((1, width), same.astype(F32), F32)
    starting = jnp.logical_or(own == 0, clips[jnp.maximum(own - 1, 0)] != own_clip)
    aux[slabs : slabs + 1] = jnp.full((1, width), starting.astype(F32), F32)
    aux[slabs + 1 : slabs + 2] = jnp.full((1, width), slabs_in.astype(F32) * float(per_slab), F32)
    for k, copy in enumerate(param_loads):
        copy.wait()
        aux[slabs + 2 + k : slabs + 3 + k] = params[k]
    aux[slabs + 6 : slabs + 8] = jnp.zeros((2, width), F32)
    for copy in loads:
        copy.wait()


def load_call(bigs, clip_ids, params, per_slab, after):
    slabs, width = lax.axis_size("tm"), params[0].shape[0]
    return pl.pallas_call(
        functools.partial(load_kernel, slabs, per_slab, len(bigs)),
        out_shape=[*[shaped(big.shape) for big in bigs], shaped((slabs + 8, width), F32)],
        in_specs=[ANYWHERE] * (6 + len(bigs)),
        out_specs=[VMEM] * (1 + len(bigs)),
        scratch_shapes=[
            pltpu.VMEM((4, 1, width), F32),
            pltpu.SMEM(clip_ids.shape, jnp.int32),
            pltpu.SemaphoreType.DMA((5 + len(bigs),)),
        ],
        compiler_params=vmem_params(),
        cost_estimate=pl.CostEstimate(flops=0, bytes_accessed=4 * sum(b.size for b in bigs), transcendentals=0),
    )(*[in_hbm(x) for x in (clip_ids, *[p[None] for p in params], *bigs)], after)


def group_total(values):
    width = values.shape[-1]
    lane = lax.broadcasted_iota(jnp.int32, values.shape, 1)
    step = 1
    while step < width // GROUPS:
        upper = pltpu.roll(values, step, 1)
        lower = pltpu.roll(values, width - step, 1)
        values = values + jnp.where((lane & step) != 0, upper, lower)
        step *= 2
    return values


def half_affine(table, aux, which):
    width = aux.shape[1]
    slabs = aux.shape[0] - 8
    places = table.shape[0] // slabs
    sums = []
    for k in range(2):
        parts = [
            aux[slab : slab + 1] * sum(table[slab * places + p, :, k * width : (k + 1) * width] for p in range(places))
            for slab in range(slabs)
        ]
        while len(parts) > 1:
            parts = [sum(parts[i : i + 2]) for i in range(0, len(parts), 2)]
        sums += parts
    grouped = group_total(jnp.concatenate(sums, axis=0))
    count = aux[slabs + 1 : slabs + 2]
    gain = aux[slabs + 2 + 2 * which : slabs + 3 + 2 * which]
    shift = aux[slabs + 3 + 2 * which : slabs + 4 + 2 * which]
    mean = grouped[0:1] / count
    variance = grouped[1:2] / count - mean * mean
    scale = lax.rsqrt(variance + 1e-06) * gain
    return 0.5 * scale, 0.5 * (shift - mean * scale)


def normed(raw, affine):
    half = raw.astype(F32) * affine[0] + affine[1]
    return (half * jnp.tanh(half) + half).astype(BF16)


def extended_row(frames, sides, frame, row):
    n_rows = frames.shape[1]
    inner = frames[frame, min(max(row - 1, 0), n_rows - 1)]
    if 0 < row <= n_rows:
        return inner
    place, places = lax.axis_index("space"), lax.axis_size("space")
    side = sides[0 if row == 0 else -1]
    return jnp.where(place == (0 if row == 0 else places - 1), inner, side[frame, 0])


def conv_rows(planes, taps):
    ref, index = planes[0]
    n_rows, cols, width = ref.shape[1] - 2, ref.shape[2], ref.shape[3]
    lhs = jnp.concatenate(
        [ref[index, j : j + n_rows].reshape(n_rows * cols, width) for ref, index in planes for j in range(3)], axis=1
    )
    column = lax.broadcasted_iota(jnp.int32, (cols, width), 0)
    sums = []
    for l in range(3):
        rhs = jnp.concatenate([taps[i, j, l] for i in range(3) for j in range(3)], axis=0)
        sums.append(jnp.dot(lhs, rhs, preferred_element_type=F32))
    for row in range(n_rows):
        left, mid, right = (s[row * cols : (row + 1) * cols] for s in sums)
        left = jnp.where(column == 0, left, pltpu.roll(left, 1, 0))
        right = jnp.where(column == cols - 1, right, pltpu.roll(right, cols - 1, 0))
        yield row, left + mid + right


def put_hidden(hidden, frame, row, value, sums):
    rounded = value.astype(BF16)
    hidden[frame, row] = rounded
    return add_stats(sums, rounded.astype(F32))


def late_kernel(n_sides, which, aux, table, frames, *refs):
    sides, taps, refs = refs[:n_sides], refs[n_sides], refs[n_sides + 1 :]
    if which == 0:
        act_low, affine_out, hidden, stats, edges, act_high = refs
    else:
        feats, act_low, affine_out, out_hbm, act_high, out, sems = refs
    n_rows, width = frames.shape[1], frames.shape[3]
    low, high = act_low.shape[0], act_high.shape[0]
    affine = half_affine(table, aux, which)
    for k in range(2):
        affine_out[k : k + 1] = affine[k]
    planes = [(act_low, f) for f in range(low)] + [(act_high, f) for f in range(high)]
    for frame, (act, index) in enumerate(planes):
        for row in range(n_rows + 2):
            act[index, row] = normed(extended_row(frames, sides, frame, row), affine)
    sums = no_stats(width)
    stores = []
    for frame in range(high):
        for row, value in conv_rows(planes[frame : frame + 3], taps):
            if which == 0:
                sums = put_hidden(hidden, frame, row, value, sums)
            else:
                out[frame, row] = feats[low + frame, row].astype(F32) + value
        if which == 0:
            send_rows(hidden, frame, edges)
        else:
            stores.append(pltpu.make_async_copy(out.at[frame], out_hbm.at[low + frame], sems.at[frame]))
            stores[-1].start()
    if which == 0:
        for k in range(2):
            stats[k] = sums[k]
    for store in stores:
        store.wait()


def early_act(n_sides, aux, refs):
    before, corners, (act_low, affine_in), act_before = refs[0], refs[1 : 1 + n_sides], refs[1 + n_sides : 3 + n_sides], refs[-1]
    slabs = aux.shape[0] - 8
    starting = aux[slabs : slabs + 1] != 0.0
    affine = affine_in[0:1], affine_in[1:2]
    for frame in range(2):
        for row in range(act_low.shape[1]):
            value = normed(extended_row(before, corners, frame, row), affine).astype(F32)
            act_before[frame, row] = jnp.where(starting, act_low[0, row].astype(F32), value).astype(BF16)
    return [(act_before, 0), (act_before, 1)] + [(act_low, f) for f in range(act_low.shape[0])]


def early_hidden_kernel(n_sides, aux, *refs):
    refs, act_before, (hidden, edges, copies, stats, sems) = refs[:-6], refs[-6], refs[-5:]
    taps, late, late_stats, late_edges, hidden_hbm, tail_hbm, edges_hbm, copies_hbm = refs[3 + n_sides :]
    n_late = late.shape[0]
    stores = [
        pltpu.make_async_copy(late, hidden_hbm.at[pl.ds(2, n_late)], sems.at[0]),
        pltpu.make_async_copy(late.at[pl.ds(n_late - TAIL, TAIL)], tail_hbm, sems.at[1]),
        pltpu.make_async_copy(late_edges, edges_hbm.at[pl.ds(2, n_late)], sems.at[2]),
    ]
    for store in stores:
        store.start()
    planes = early_act(n_sides, aux, (*refs[: 3 + n_sides], act_before))
    sums = late_stats[0], late_stats[1]
    for frame in range(2):
        for row, value in conv_rows(planes[frame : frame + 3], taps):
            sums = put_hidden(hidden, frame, row, value, sums)
        send_rows(hidden, frame, edges)
        if frame == 1:
            store_stats(stats, sums)
            store_copies(copies, stats)
            stores.append(pltpu.make_async_copy(copies, copies_hbm, sems.at[5]))
            stores[-1].start()
            stores.append(pltpu.make_async_copy(edges, edges_hbm.at[pl.ds(0, 2)], sems.at[6]))
            stores[-1].start()
        stores.append(pltpu.make_async_copy(hidden.at[frame], hidden_hbm.at[frame], sems.at[3 + frame]))
        stores[-1].start()
    for store in stores:
        store.wait()


def early_out_kernel(n_sides, aux, *refs):
    refs, act_before, (out, sems) = refs[:-3], refs[-3], refs[-2:]
    taps, feats, _, out_hbm = refs[3 + n_sides :]
    planes = early_act(n_sides, aux, (*refs[: 3 + n_sides], act_before))
    stores = []
    for frame in range(2):
        for row, value in conv_rows(planes[frame : frame + 3], taps):
            out[frame, row] = feats[frame, row].astype(F32) + value
        stores.append(pltpu.make_async_copy(out.at[frame], out_hbm.at[frame], sems.at[frame]))
        stores[-1].start()
    for store in stores:
        store.wait()


def call(kernel, outs, scratch, frames, operands, out_specs=None, aliases=None):
    return pl.pallas_call(
        kernel,
        out_shape=outs,
        in_specs=[VMEM if aliases is None or k not in aliases else ANYWHERE for k in range(len(operands))],
        out_specs=[VMEM] * len(outs) if out_specs is None else out_specs,
        scratch_shapes=scratch,
        input_output_aliases=aliases or {},
        compiler_params=vmem_params(),
        cost_estimate=pl.CostEstimate(flops=54 * frames * 384 * 65536, bytes_accessed=1 << 20, transcendentals=1 << 20),
    )(*operands)


def on_device(feats, clip_ids, gain_one, shift_one, kernel_one, gain_two, shift_two, kernel_two):
    n_frames, n_rows, cols, width = feats.shape
    params = (gain_one, shift_one, gain_two, shift_two)
    per_slab = feats.size // GROUPS * lax.axis_size("space")
    late = n_frames - 2
    plane = (n_rows + 2, cols, width)
    act = pltpu.VMEM((2,) + plane, BF16)
    act_late = pltpu.VMEM((late,) + plane, BF16)
    act_shapes = [shaped((2,) + plane), shaped((2, width), F32)]

    copies, tail, edges = entry_call(feats)
    table = stats_table(copies)
    tail, edges, _ = lax.optimization_barrier((tail, edges, copies))
    before = shifted(tail, "tm", 1)
    sides = row_halo(edges)
    taps, frames, aux = load_call((kernel_one, feats), clip_ids, params, per_slab, copies)
    n_sides = len(sides)
    act_low, affine, hidden_late, stats, edges = call(
        functools.partial(late_kernel, n_sides, 0),
        act_shapes
        + [shaped((late, n_rows, cols, width)), shaped((2, 8, width), F32), shaped(edge_shape(feats, late))],
        [act_late],
        late,
        [aux, table, frames, *sides, taps],
    )
    before, corners, affine = corner_rows(before, affine)
    hidden, tail, edges, copies = call(
        functools.partial(early_hidden_kernel, n_sides),
        [
            stored_in_hbm(feats.shape),
            stored_in_hbm((TAIL,) + feats.shape[1:]),
            stored_in_hbm(edge_shape(feats, n_frames)),
            stored_in_hbm(copies.shape, F32),
        ],
        [
            act,
            pltpu.VMEM((2, n_rows, cols, width), BF16),
            pltpu.VMEM(edge_shape(feats, 2), BF16),
            pltpu.VMEM(copies.shape, F32),
            pltpu.VMEM((1, 2 * width), F32),
            pltpu.SemaphoreType.DMA((7,)),
        ],
        2,
        [aux, before, *corners, act_low, affine, taps, hidden_late, stats, edges],
        out_specs=[ANYWHERE] * 4,
    )

    table = stats_table(copies)
    before = shifted(tail, "tm", 1)
    sides = row_halo(edges)
    taps, frames, hidden, aux = load_call((kernel_two, feats, hidden), clip_ids, params, per_slab, copies)
    act_low, affine, out = call(
        functools.partial(late_kernel, n_sides, 1),
        act_shapes + [shaped(feats.shape, F32)],
        [act_late, pltpu.VMEM((late, n_rows, cols, width), F32), pltpu.SemaphoreType.DMA((late,))],
        late,
        [aux, table, hidden, *sides, taps, frames],
        out_specs=[VMEM, VMEM, ANYWHERE],
    )
    before, corners, affine = corner_rows(before, affine)
    operands = [aux, before, *corners, act_low, affine, taps, frames, out]
    return call(
        functools.partial(early_out_kernel, n_sides),
        shaped(feats.shape, F32),
        [act, pltpu.VMEM((2, n_rows, cols, width), F32), pltpu.SemaphoreType.DMA((2,))],
        2,
        operands,
        out_specs=ANYWHERE,
        aliases={len(operands) - 1: 0},
    )


def solution(mesh):
    return jax.shard_map(
        on_device,
        mesh=mesh,
        in_specs=(P("tm", "space", None, None), P(), P(), P(), P(), P(), P(), P()),
        out_specs=P("tm", "space", None, None),
        check_vma=False,
    )
```

time: 54.2 us -> 70 us (1.29)
  Pallas kernels: 17.4 us -> 32.6 us
  local copies, waits for them, and re-layouts: 0.05 us -> 9.29 us
  starting transfers between devices: 23.1 us -> 14.4 us
    ppermute x20 -> x4, starting transfers between devices: 18.5 us -> 0.88 us  [traded(): lax.ppermute(value, axis, [(i, i ^ mask) for i in range(lax.axis_size(axi...]
    pallas_call x2 -> x3, Pallas kernels: 3.42 us -> 18 us  [the longest x1 13.1 us: entry_call(): pl.pallas_call(entry_kernel, out_shape=[stored_in_hbm(copies, F32), store...]
    all_to_all x0 -> x2, waiting for transfers between devices: none -> 10.6 us  [stats_table(): return lax.all_to_all(copies, ('tm', 'space'), 0, 0, tiled=True)]
    all_to_all x0 -> x2, starting transfers between devices: none -> 10.5 us  [stats_table(): return lax.all_to_all(copies, ('tm', 'space'), 0, 0, tiled=True)]
    unnamed x2 -> x12, local copies, waits for them, and re-layouts: 0.01 us -> 9.26 us
    ppermute x3 -> x2, waiting for transfers between devices: 5.92 us -> 0.01 us  [shifted(): lax.ppermute(value, axis, [(i, (i + step) % peers) for i in range(peers)])]
    ppermute x20 -> x4, waiting for transfers between devices: 7.32 us -> 2.58 us  [traded(): lax.ppermute(value, axis, [(i, i ^ mask) for i in range(lax.axis_size(axi...]
    ppermute x3 -> x2, starting transfers between devices: 4.59 us -> 2.95 us  [shifted(): lax.ppermute(value, axis, [(i, (i + step) % peers) for i in range(peers)])]
  transfers between devices with their start and end apart: 23 -> 8, of which waited for: 7 -> 4; matrix products, arithmetic and copies ran while one was open for 0% -> 0% of each run, Pallas kernels for 23% -> 17%
where the time goes in v11:
time: 70 us; the launch traced here: 69.6 us
  Pallas kernels  32.6 us (47%)
  starting transfers between devices  14.4 us (21%)
  waiting for transfers between devices  13.2 us (19%)
  local copies, waits for them, and re-layouts  9.29 us (13%)
    pallas_call x4, Pallas kernels, call(): pl.pallas_call(kernel, out_shape=outs, in_specs=[VMEM if aliases is None...  14.6 us
    pallas_call x1, Pallas kernels, entry_call(): pl.pallas_call(entry_kernel, out_shape=[stored_in_hbm(copies, F32), store...  13.1 us
    all_to_all x2, waiting for transfers between devices, stats_table(): return lax.all_to_all(copies, ('tm', 'space'), 0, 0, tiled=True)  10.6 us
    all_to_all x2, starting transfers between devices, stats_table(): return lax.all_to_all(copies, ('tm', 'space'), 0, 0, tiled=True)  10.5 us
    unnamed x12, local copies, waits for them, and re-layouts  9.26 us
    pallas_call x2, Pallas kernels, load_call(): pl.pallas_call(functools.partial(load_kernel, slabs, per_slab, len(bigs))...  4.89 us
    ppermute x2, starting transfers between devices, shifted(): lax.ppermute(value, axis, [(i, (i + step) % peers) for i in range(peers)])  2.95 us
    ppermute x4, waiting for transfers between devices, traded(): lax.ppermute(value, axis, [(i, i ^ mask) for i in range(lax.axis_size(axi...  2.58 us
  transfers between devices with their start and end apart: 8, of which 4 were waited for; matrix products, arithmetic and copies ran while one was open for 0% of the time, Pallas kernels for 17%

profile of v11, /device:TPU:0, one launch (start us, length us, event | category | flops | bytes accessed | tf_op | source)
XLA Modules:
  0.0 69.6 jit_solution(6149343137467277714)
XLA Ops:
  0.0 13.1 %shard_map.82 = (f32[32,1,512]{2,1,0:T(1,128)}, bf16[2,4,96,256]{3,2,1,0:T(8,128)(2,1)}, bf16[4,1,96,256]{3,2,1,0:T(8,128)(2,1)}) custom-call(bf16[4,4,96,256]{3,2,1,0:T(8,128)(2,1)} %refs_5_.3), custom_call_target="tpu_custom_call" | custom-call | flops 1572864 | bytes 1572864 | tf_op jit(solution)/shard_map/pallas_call | solution.py:134
  13.1 0.5 collective-permute-start.1
  13.6 2.6 %collective-permute-start = (bf16[2,4,96,256]{3,2,1,0:T(8,128)(2,1)}, bf16[2,4,96,256]{3,2,1,0:T(8,128)(2,1)S(1)}, u32[]{:S(2)}, u32[]{:S(2)}) collective-permute-start(bf16[2,4,96,256]{3,2,1,0:T(8,128)(2,1)} %get-tuple-element.37), channel_id=1, source_target_pairs={{0,2},{2,4},{4,6},{6,8},{8,10},{10,12},{12,14},{14,16},{16,18},{18... | collective-permute-start | bytes 1179656 | tf_op jit(solution)/shard_map/ppermute | solution.py:37
  16.2 4.9 %all-to-all-start = ((f32[32,1,512]{2,1,0:T(1,128)}), f32[32,1,512]{2,1,0:T(1,128)S(1)}, u32[]{:S(2)}, u32[]{:S(2)}) async-start(f32[32,1,512]{2,1,0:T(1,128)} %get-tuple-element.33.refs_6_), calls=%async_computation | async-start | bytes 131072 | tf_op jit(solution)/shard_map/all_to_all | solution.py:41
  21.1 0.0 copy-start
  21.1 0.9 %copy-done = f32[32,1,512]{2,1,0:T(1,128)S(1)} copy-done((f32[32,1,512]{2,1,0:T(1,128)S(1)}, f32[32,1,512]{2,1,0:T(1,128)}, u32[]{:S(2)}) %copy-start) | copy-done | bytes 65560
  22.0 2.3 %shard_map.83 = (bf16[3,3,3,256,256]{4,3,2,1,0:T(8,128)(2,1)S(1)}, bf16[4,4,96,256]{3,2,1,0:T(8,128)(2,1)S(1)}, f32[24,256]{1,0:T(8,128)S(1)}) custom-call(s32[16]{0:T(128)} %clips_hbm.3, f32[1,256]{1,0:T(1,128)} %bitcast.4, f32[1,256]{1,0:T(1,128)} %bitcast.6, f32[1,256]{1,0:T(1,128)} %bitcast.8, f32[1,256]{1,0:T(1,128)} %bitcast.10, ...), custom_call_target="tpu_custom_call" | custom-call | bytes 8650752 | tf_op jit(solution)/shard_map/pallas_call | solution.py:186
  24.3 0.0 copy-start.2
  24.3 1.8 %copy-done.2 = bf16[3,3,3,256,256]{4,3,2,1,0:T(8,128)(2,1)} copy-done((bf16[3,3,3,256,256]{4,3,2,1,0:T(8,128)(2,1)}, bf16[3,3,3,256,256]{4,3,2,1,0:T(8,128)(2,1)S(1)}, u32[]{:S(2)}) %copy-start.2) | copy-done | bytes 3538968
  26.1 5.3 %all-to-all-done.table = f32[32,1,512]{2,1,0:T(1,128)S(1)} async-done(((f32[32,1,512]{2,1,0:T(1,128)}), f32[32,1,512]{2,1,0:T(1,128)S(1)}, u32[]{:S(2)}, u32[]{:S(2)}) %all-to-all-start) | async-done | bytes 65568 | tf_op jit(solution)/shard_map/all_to_all | solution.py:41
  31.4 0.0 collective-permute-done.1.refs_0_
  31.4 0.0 copy-start.3
  31.4 2.0 %copy-done.3 = bf16[3,3,3,256,256]{4,3,2,1,0:T(8,128)(2,1)S(1)} copy-done((bf16[3,3,3,256,256]{4,3,2,1,0:T(8,128)(2,1)S(1)}, bf16[3,3,3,256,256]{4,3,2,1,0:T(8,128)(2,1)}, u32[]{:S(2)}) %copy-start.3) | copy-done | bytes 3538968
  33.4 3.2 %shard_map.84 = (bf16[2,6,96,256]{3,2,1,0:T(8,128)(2,1)S(1)}, f32[2,256]{1,0:T(2,128)S(1)}, bf16[2,4,96,256]{3,2,1,0:T(8,128)(2,1)S(1)}, f32[2,8,256]{2,1,0:T(8,128)S(1)}, bf16[2,1,96,256]{3,2,1,0:T(8,128)(2,1)S(1)}) custom-call(f32[24,256]{1,0:T(8,128)S(1)} %get-tuple-element.34.aux, f32[32,1,512]{2,1,0:T(1,128)S(1)} %all-to-all-done.table, ...), custom_call_target="tpu_custom_call" | custom-call | flops 2717908992 | bytes 1048576 | tf_op jit(solution)/shard_map/pallas_call | solution.py:367
  36.6 0.0 collective-permute-done.refs_0_
  36.6 0.1 collective-permute-start.2
  36.7 1.3 %collective-permute-done.2.refs_1_ = bf16[2,1,96,256]{3,2,1,0:T(8,128)(2,1)S(1)} collective-permute-done((bf16[2,1,96,256]{3,2,1,0:T(8,128)(2,1)S(1)}, bf16[2,1,96,256]{3,2,1,0:T(8,128)(2,1)S(1)}, u32[]{:S(2)}, u32[]{:S(2)}) %collective-permute-start.2) | collective-permute-done | bytes 98336 | tf_op jit(solution)/shard_map/ppermute | solution.py:32
  38.0 3.8 %shard_map.85 = (bf16[4,4,96,256]{3,2,1,0:T(8,128)(2,1)}, bf16[2,4,96,256]{3,2,1,0:T(8,128)(2,1)}, bf16[4,1,96,256]{3,2,1,0:T(8,128)(2,1)}, f32[32,1,512]{2,1,0:T(1,128)}) custom-call(f32[24,256]{1,0:T(8,128)S(1)} %get-tuple-element.34.aux, bf16[2,4,96,256]{3,2,1,0:T(8,128)(2,1)S(1)} %collective-permute-done.refs_0_, ...), custom_call_target="tpu_custom_call" | custom-call | flops 2717908992 | bytes 1048576 | tf_op jit(solution)/shard_map/pallas_call | solution.py:367
  41.8 0.2 collective-permute-start.4
  42.0 0.4 collective-permute-start.3
  42.4 5.6 %all-to-all-start.1 = ((f32[32,1,512]{2,1,0:T(1,128)}), f32[32,1,512]{2,1,0:T(1,128)S(1)}, u32[]{:S(2)}, u32[]{:S(2)}) async-start(f32[32,1,512]{2,1,0:T(1,128)} %get-tuple-element.49.refs_7_), calls=%async_computation.1 | async-start | bytes 131072 | tf_op jit(solution)/shard_map/all_to_all | solution.py:41
  48.0 0.0 copy-start.1
  48.1 0.9 %copy-done.1 = f32[32,1,512]{2,1,0:T(1,128)S(1)} copy-done((f32[32,1,512]{2,1,0:T(1,128)S(1)}, f32[32,1,512]{2,1,0:T(1,128)}, u32[]{:S(2)}) %copy-start.1) | copy-done | bytes 65560
  48.9 2.6 %shard_map.86 = (bf16[3,3,3,256,256]{4,3,2,1,0:T(8,128)(2,1)S(1)}, bf16[4,4,96,256]{3,2,1,0:T(8,128)(2,1)S(1)}, bf16[4,4,96,256]{3,2,1,0:T(8,128)(2,1)S(1)}, f32[24,256]{1,0:T(8,128)S(1)}) custom-call(s32[16]{0:T(128)} %clips_hbm.3, f32[1,256]{1,0:T(1,128)} %bitcast.5, f32[1,256]{1,0:T(1,128)} %bitcast.7, f32[1,256]{1,0:T(1,128)} %bitcast.9, ...), custom_call_target="tpu_custom_call" | custom-call | bytes 10223616 | tf_op jit(solution)/shard_map/pallas_call | solution.py:186
  51.5 0.0 copy-start.4
  51.5 1.8 %copy-done.4 = bf16[3,3,3,256,256]{4,3,2,1,0:T(8,128)(2,1)} copy-done((bf16[3,3,3,256,256]{4,3,2,1,0:T(8,128)(2,1)}, bf16[3,3,3,256,256]{4,3,2,1,0:T(8,128)(2,1)S(1)}, u32[]{:S(2)}) %copy-start.4) | copy-done | bytes 3538968
  53.3 5.3 %all-to-all-done.1.table = f32[32,1,512]{2,1,0:T(1,128)S(1)} async-done(((f32[32,1,512]{2,1,0:T(1,128)}), f32[32,1,512]{2,1,0:T(1,128)S(1)}, u32[]{:S(2)}, u32[]{:S(2)}) %all-to-all-start.1) | async-done | bytes 65568 | tf_op jit(solution)/shard_map/all_to_all | solution.py:41
  58.6 0.0 collective-permute-done.4.refs_0_
  58.6 0.0 copy-start.5
  58.6 2.0 %copy-done.5 = bf16[3,3,3,256,256]{4,3,2,1,0:T(8,128)(2,1)S(1)} copy-done((bf16[3,3,3,256,256]{4,3,2,1,0:T(8,128)(2,1)S(1)}, bf16[3,3,3,256,256]{4,3,2,1,0:T(8,128)(2,1)}, u32[]{:S(2)}) %copy-start.5) | copy-done | bytes 3538968
  60.6 3.9 %shard_map.87 = (bf16[2,6,96,256]{3,2,1,0:T(8,128)(2,1)S(1)}, f32[2,256]{1,0:T(2,128)S(1)}, f32[4,4,96,256]{3,2,1,0:T(8,128)}) custom-call(f32[24,256]{1,0:T(8,128)S(1)} %get-tuple-element.50.aux, f32[32,1,512]{2,1,0:T(1,128)S(1)} %all-to-all-done.1.table, bf16[4,4,96,256]{3,2,1,0:T(8,128)(2,1)S(1)} %get-tuple-element.52.frames, ...), custom_call_target="tpu_custom_call" | custom-call | flops 2717908992 | bytes 1048576 | tf_op jit(solution)/shard_map/pallas_call | solution.py:367
  64.5 0.0 collective-permute-done.3.refs_0_
  64.5 0.1 collective-permute-start.5
  64.6 1.3 %collective-permute-done.5.refs_1_ = bf16[2,1,96,256]{3,2,1,0:T(8,128)(2,1)S(1)} collective-permute-done((bf16[2,1,96,256]{3,2,1,0:T(8,128)(2,1)S(1)}, bf16[2,1,96,256]{3,2,1,0:T(8,128)(2,1)S(1)}, u32[]{:S(2)}, u32[]{:S(2)}) %collective-permute-start.5) | collective-permute-done | bytes 98336 | tf_op jit(solution)/shard_map/ppermute | solution.py:32
  65.9 3.7 %shard_map.88 = f32[4,4,96,256]{3,2,1,0:T(8,128)} custom-call(f32[24,256]{1,0:T(8,128)S(1)} %get-tuple-element.50.aux, bf16[2,4,96,256]{3,2,1,0:T(8,128)(2,1)S(1)} %collective-permute-done.3.refs_0_, bf16[2,1,96,256]{3,2,1,0:T(8,128)(2,1)S(1)} %collective-permute-done.5.refs_1_, ...), custom_call_target="tpu_custom_call", output_to_operand_aliasing={{}: (7, {})} | custom-call | flops 2717908992 | bytes 1048576 | tf_op jit(solution)/shard_map/pallas_call | solution.py:367
  (2 shorter events, 0.0 us)
Async XLA Ops:
  13.1 18.3 %collective-permute-start.1 = (bf16[4,1,96,256]{3,2,1,0:T(8,128)(2,1)}, bf16[4,1,96,256]{3,2,1,0:T(8,128)(2,1)S(1)}, u32[]{:S(2)}, u32[]{:S(2)}) collective-permute-start(bf16[4,1,96,256]{3,2,1,0:T(8,128)(2,1)} %get-tuple-element.39), channel_id=1, source_target_pairs={{0,1},{1,0},{2,3},{3,2},{4,5},{5,4},{6,7},{7,6},{8,9},{9,8},{10,11... | collective-permute-start | bytes 589832 | tf_op jit(solution)/shard_map/ppermute | solution.py:32
  13.6 23.0 %collective-permute-start = (bf16[2,4,96,256]{3,2,1,0:T(8,128)(2,1)}, bf16[2,4,96,256]{3,2,1,0:T(8,128)(2,1)S(1)}, u32[]{:S(2)}, u32[]{:S(2)}) collective-permute-start(bf16[2,4,96,256]{3,2,1,0:T(8,128)(2,1)} %get-tuple-element.37), channel_id=1, source_target_pairs={{0,2},{2,4},{4,6},{6,8},{8,10},{10,12},{12,14},{14,16},{16,18},{18... | collective-permute-start | bytes 1179656 | tf_op jit(solution)/shard_map/ppermute | solution.py:37
  16.2 15.3 %all-to-all-start = ((f32[32,1,512]{2,1,0:T(1,128)}), f32[32,1,512]{2,1,0:T(1,128)S(1)}, u32[]{:S(2)}, u32[]{:S(2)}) async-start(f32[32,1,512]{2,1,0:T(1,128)} %get-tuple-element.33.refs_6_), calls=%async_computation | async-start | bytes 131072 | tf_op jit(solution)/shard_map/all_to_all | solution.py:41
  21.1 0.9 %copy-start = (f32[32,1,512]{2,1,0:T(1,128)S(1)}, f32[32,1,512]{2,1,0:T(1,128)}, u32[]{:S(2)}) copy-start(f32[32,1,512]{2,1,0:T(1,128)} %get-tuple-element.33.refs_6_) | copy-start | bytes 196612
  24.3 1.8 %copy-start.2 = (bf16[3,3,3,256,256]{4,3,2,1,0:T(8,128)(2,1)}, bf16[3,3,3,256,256]{4,3,2,1,0:T(8,128)(2,1)S(1)}, u32[]{:S(2)}) copy-start(bf16[3,3,3,256,256]{4,3,2,1,0:T(8,128)(2,1)S(1)} %get-tuple-element.40.refs_1_.refs_4_) | copy-start | bytes 10616836
  31.4 2.0 %copy-start.3 = (bf16[3,3,3,256,256]{4,3,2,1,0:T(8,128)(2,1)S(1)}, bf16[3,3,3,256,256]{4,3,2,1,0:T(8,128)(2,1)}, u32[]{:S(2)}) copy-start(bf16[3,3,3,256,256]{4,3,2,1,0:T(8,128)(2,1)} %copy-done.2) | copy-start | bytes 10616836
  36.6 1.4 %collective-permute-start.2 = (bf16[2,1,96,256]{3,2,1,0:T(8,128)(2,1)S(1)}, bf16[2,1,96,256]{3,2,1,0:T(8,128)(2,1)S(1)}, u32[]{:S(2)}, u32[]{:S(2)}) collective-permute-start(bf16[2,1,96,256]{3,2,1,0:T(8,128)(2,1)S(1)} %constant_dynamic-slice_fusion.1), channel_id=1, source_target_pairs={{0,1},{1,0},{2,3},{3,2},{4,5},{5,4},{6,7},{7,6},{8,9},{9,8},{10,11... | collective-permute-start | bytes 294920 | tf_op jit(solution)/shard_map/ppermute | solution.py:32
  41.8 16.7 %collective-permute-start.4 = (bf16[4,1,96,256]{3,2,1,0:T(8,128)(2,1)}, bf16[4,1,96,256]{3,2,1,0:T(8,128)(2,1)S(1)}, u32[]{:S(2)}, u32[]{:S(2)}) collective-permute-start(bf16[4,1,96,256]{3,2,1,0:T(8,128)(2,1)} %get-tuple-element.53), channel_id=1, source_target_pairs={{0,1},{1,0},{2,3},{3,2},{4,5},{5,4},{6,7},{7,6},{8,9},{9,8},{10,11... | collective-permute-start | bytes 589832 | tf_op jit(solution)/shard_map/ppermute | solution.py:32
  42.0 22.5 %collective-permute-start.3 = (bf16[2,4,96,256]{3,2,1,0:T(8,128)(2,1)}, bf16[2,4,96,256]{3,2,1,0:T(8,128)(2,1)S(1)}, u32[]{:S(2)}, u32[]{:S(2)}) collective-permute-start(bf16[2,4,96,256]{3,2,1,0:T(8,128)(2,1)} %get-tuple-element.51), channel_id=1, source_target_pairs={{0,2},{2,4},{4,6},{6,8},{8,10},{10,12},{12,14},{14,16},{16,18},{18... | collective-permute-start | bytes 1179656 | tf_op jit(solution)/shard_map/ppermute | solution.py:37
  42.4 16.1 %all-to-all-start.1 = ((f32[32,1,512]{2,1,0:T(1,128)}), f32[32,1,512]{2,1,0:T(1,128)S(1)}, u32[]{:S(2)}, u32[]{:S(2)}) async-start(f32[32,1,512]{2,1,0:T(1,128)} %get-tuple-element.49.refs_7_), calls=%async_computation.1 | async-start | bytes 131072 | tf_op jit(solution)/shard_map/all_to_all | solution.py:41
  48.0 0.9 %copy-start.1 = (f32[32,1,512]{2,1,0:T(1,128)S(1)}, f32[32,1,512]{2,1,0:T(1,128)}, u32[]{:S(2)}) copy-start(f32[32,1,512]{2,1,0:T(1,128)} %get-tuple-element.49.refs_7_) | copy-start | bytes 196612
  51.5 1.8 %copy-start.4 = (bf16[3,3,3,256,256]{4,3,2,1,0:T(8,128)(2,1)}, bf16[3,3,3,256,256]{4,3,2,1,0:T(8,128)(2,1)S(1)}, u32[]{:S(2)}) copy-start(bf16[3,3,3,256,256]{4,3,2,1,0:T(8,128)(2,1)S(1)} %get-tuple-element.54.refs_1_.refs_4_) | copy-start | bytes 10616836
  58.6 2.0 %copy-start.5 = (bf16[3,3,3,256,256]{4,3,2,1,0:T(8,128)(2,1)S(1)}, bf16[3,3,3,256,256]{4,3,2,1,0:T(8,128)(2,1)}, u32[]{:S(2)}) copy-start(bf16[3,3,3,256,256]{4,3,2,1,0:T(8,128)(2,1)} %copy-done.4) | copy-start | bytes 10616836
  64.5 1.4 %collective-permute-start.5 = (bf16[2,1,96,256]{3,2,1,0:T(8,128)(2,1)S(1)}, bf16[2,1,96,256]{3,2,1,0:T(8,128)(2,1)S(1)}, u32[]{:S(2)}, u32[]{:S(2)}) collective-permute-start(bf16[2,1,96,256]{3,2,1,0:T(8,128)(2,1)S(1)} %constant_dynamic-slice_fusion), channel_id=1, source_target_pairs={{0,1},{1,0},{2,3},{3,2},{4,5},{5,4},{6,7},{7,6},{8,9},{9,8},{10,11... | collective-permute-start | bytes 294920 | tf_op jit(solution)/shard_map/ppermute | solution.py:32

commit v12 on v7

--- a/solution.py
+++ b/solution.py
@@ -37,31 +37,8 @@
     return lax.ppermute(value, axis, [(i, (i + step) % peers) for i in range(peers)])
 
 
-def group_sizes(peers):
-    sizes = []
-    while peers > 1:
-        sizes.append(min(4, peers))
-        peers //= sizes[-1]
-    return sizes
-
-
-def slab_offsets(peers):
-    offsets, left = [0], peers
-    for ways in group_sizes(peers):
-        left //= ways
-        offsets = [(left * way) ^ offset for way in range(ways) for offset in offsets]
-    return offsets
-
-
 def slab_tables(stats):
-    peers = lax.axis_size("tm")
-    total = stats + traded(stats, "space", 1) if lax.axis_size("space") == 2 else lax.psum(stats, "space")
-    held, left = [total], peers
-    for ways in group_sizes(peers):
-        left //= ways
-        block = held[0] if len(held) == 1 else jnp.concatenate(held, axis=0)
-        held = [block] + [traded(block, "tm", left * way) for way in range(1, ways)]
-    return total, held
+    return stats, [lax.all_gather(stats, ("tm", "space"))]
 
 
 def row_halo(edges):
@@ -114,8 +91,8 @@
 def store_stats(stats, sums, base=None):
     width = sums[0].shape[1]
     for k in range(2):
-        part = jnp.sum(sums[k], axis=0, keepdims=True)
-        stats[:, k * width : (k + 1) * width] = part if base is None else part + base[:, k * width : (k + 1) * width]
+        at = slice(k * width, (k + 1) * width)
+        stats[:, at] = sums[k] if base is None else sums[k] + base[:, at]
 
 
 def entry_kernel(feats_hbm, frames, tail, stats, *rest):
@@ -137,7 +114,7 @@
 
 def entry_call(feats):
     n_frames, width = feats.shape[0], feats.shape[3]
-    outs = [shaped(feats.shape), shaped((TAIL,) + feats.shape[1:]), shaped((1, 2 * width), F32)]
+    outs = [shaped(feats.shape), shaped((TAIL,) + feats.shape[1:]), shaped((8, 2 * width), F32)]
     outs += edge_shapes(feats, n_frames)
     frames, tail, stats, *edges = pl.pallas_call(
         entry_kernel,
@@ -163,8 +140,8 @@
     own = lax.axis_index("tm")
     own_clip = clips[own]
     slabs_in = jnp.int32(0)
-    for entry, offset in enumerate(slab_offsets(slabs)):
-        same = (clips[own ^ offset] == own_clip).astype(jnp.int32)
+    for entry in range(slabs):
+        same = (clips[entry] == own_clip).astype(jnp.int32)
         slabs_in = slabs_in + same
         aux[entry : entry + 1] = jnp.full((1, width), same.astype(F32), F32)
     starting = jnp.logical_or(own == 0, clips[jnp.maximum(own - 1, 0)] != own_clip)
@@ -194,24 +171,6 @@
     )(*[in_hbm(x) for x in (kernel, clip_ids, *[p[None] for p in params])], after)
 
 
-def load_kernel(kernel_hbm, after, taps, sem):
-    copy = pltpu.make_async_copy(kernel_hbm, taps, sem)
-    copy.start()
-    copy.wait()
-
-
-def load_call(kernel, after):
-    return pl.pallas_call(
-        load_kernel,
-        out_shape=shaped(kernel.shape),
-        in_specs=[ANYWHERE, ANYWHERE],
-        out_specs=VMEM,
-        scratch_shapes=[pltpu.SemaphoreType.DMA],
-        compiler_params=vmem_params(),
-        cost_estimate=pl.CostEstimate(flops=0, bytes_accessed=4 * kernel.size, transcendentals=0),
-    )(in_hbm(kernel), after)
-
-
 def group_total(values):
     width = values.shape[-1]
     lane = lax.broadcasted_iota(jnp.int32, values.shape, 1)
@@ -227,14 +186,17 @@
 def half_affine(tables, aux, which):
     width = aux.shape[1]
     slabs = aux.shape[0] - 8
-    sums = [jnp.zeros((1, width), F32)] * 2
-    entry = 0
-    for table in tables:
-        mask = aux[entry : entry + table.shape[0]]
-        entry += table.shape[0]
-        sums = [
-            total + jnp.sum(table[:, k * width : (k + 1) * width] * mask, axis=0, keepdims=True) for k, total in enumerate(sums)
+    (table,) = tables
+    places = table.shape[0] // slabs
+    sums = []
+    for k in range(2):
+        parts = [
+            aux[slab : slab + 1] * sum(table[slab * places + p, :, k * width : (k + 1) * width] for p in range(places))
+            for slab in range(slabs)
         ]
+        while len(parts) > 1:
+            parts = [sum(parts[i : i + 2]) for i in range(0, len(parts), 2)]
+        sums.append(jnp.sum(parts[0], axis=0, keepdims=True))
     grouped = group_total(jnp.concatenate(sums, axis=0))
     count = aux[slabs + 1 : slabs + 2]
     gain = aux[slabs + 2 + 2 * which : slabs + 3 + 2 * which]
@@ -328,7 +290,8 @@
     tables, early, late, refs = refs[:n_tables], refs[n_tables], refs[n_tables + 1], refs[n_tables + 2 :]
     sides_early, sides_late = refs[:n_sides], refs[n_sides : 2 * n_sides]
     before, *corners = refs[2 * n_sides : 3 * n_sides + 1]
-    taps, feats, out, act = refs[3 * n_sides + 1 :]
+    taps, feats, out_hbm, act, out, sems = refs[3 * n_sides + 1 :]
+    stores = [pltpu.make_async_copy(out.at[f], out_hbm.at[f], sems.at[f]) for f in range(out.shape[0])]
     slabs = aux.shape[0] - 8
     starting = aux[slabs : slabs + 1] != 0.0
     affine = half_affine(tables, aux, 1)
@@ -347,12 +310,14 @@
     for frame in range(2, n_frames + 2):
         fill(frame)
     for frame in list(range(2, n_frames)) + [0, 1]:
-        if frame < 2:
-            fill(frame)
         if frame == 0:
+            fill(0)
             fill(1)
         for row, value in conv_rows([(act, frame + i) for i in range(3)], taps):
             out[frame, row] = feats[frame, row].astype(F32) + value
+        stores[frame].start()
+    for store in stores:
+        store.wait()
 
 
 def call(kernel, outs, scratch, frames, *operands):
@@ -360,7 +325,7 @@
         kernel,
         out_shape=outs,
         in_specs=[VMEM] * len(operands),
-        out_specs=[VMEM] * len(outs) if isinstance(outs, list) else VMEM,
+        out_specs=[VMEM] * len(outs) if isinstance(outs, list) else ANYWHERE,
         scratch_shapes=scratch,
         compiler_params=vmem_params(),
         cost_estimate=pl.CostEstimate(flops=54 * frames * 384 * 65536, bytes_accessed=1 << 20, transcendentals=1 << 20),
@@ -381,7 +346,7 @@
     late = n_frames - 2
     hidden_late, act_low, stats, affine, *edges = call(
         functools.partial(late_kernel, len(tables), n_sides),
-        [shaped((late, n_rows, cols, width)), shaped((2,) + plane), shaped((1, 2 * width), F32), shaped((2, width), F32)]
+        [shaped((late, n_rows, cols, width)), shaped((2,) + plane), shaped((8, 2 * width), F32), shaped((2, width), F32)]
         + edge_shapes(feats, late),
         [pltpu.VMEM((late,) + plane, BF16)],
         late, aux, *tables, frames, *sides, taps,
@@ -389,19 +354,18 @@
     sides_late = row_halo(edges)
     hidden_early, stats, *edges = call(
         functools.partial(early_kernel, n_sides),
-        [shaped((2, n_rows, cols, width)), shaped((1, 2 * width), F32)] + edge_shapes(feats, 2),
+        [shaped((2, n_rows, cols, width)), shaped((8, 2 * width), F32)] + edge_shapes(feats, 2),
         [pltpu.VMEM((2,) + plane, BF16)],
         2, aux, before, *corners, act_low, affine, stats, taps,
     )
     sides_early = row_halo(edges)
     total, tables = slab_tables(stats)
     before, corners, tables[0] = slab_halo(hidden_late[late - 2 :], tables[0])
-    taps = load_call(kernel_two, total)
     return call(
         functools.partial(last_kernel, len(tables), n_sides),
         shaped(feats.shape, F32),
-        [pltpu.VMEM((n_frames + 2,) + plane, BF16)],
-        n_frames, aux, *tables, hidden_early, hidden_late, *sides_early, *sides_late, before, *corners, taps, frames,
+        [pltpu.VMEM((n_frames + 2,) + plane, BF16), pltpu.VMEM(feats.shape, F32), pltpu.SemaphoreType.DMA((n_frames,))],
+        n_frames, aux, *tables, hidden_early, hidden_late, *sides_early, *sides_late, before, *corners, kernel_two, frames,
     )
 
 

time: 51.8 us -> 111 us (2.14)
  blocking collectives: 0 us -> 88.3 us
  starting transfers between devices: 21.5 us -> 4.67 us
  waiting for transfers between devices: 11 us -> 0.97 us
  Pallas kernels: 19 us -> 16.6 us
    all_gather x0 -> x2, blocking collectives: none -> 88.3 us  [slab_tables(): return (stats, [lax.all_gather(stats, ('tm', 'space'))])]
    ppermute x19 -> x5, starting transfers between devices: 17.9 us -> 1.4 us  [traded(): lax.ppermute(value, axis, [(i, i ^ mask) for i in range(lax.axis_size(axi...]
    ppermute x19 -> x5, waiting for transfers between devices: 9.41 us -> 0.96 us  [traded(): lax.ppermute(value, axis, [(i, i ^ mask) for i in range(lax.axis_size(axi...]
    pallas_call x1 -> x0, Pallas kernels: 2.01 us -> none  [load_call(): pl.pallas_call(load_kernel, out_shape=shaped(kernel.shape), in_specs=[ANY...]
    ppermute x2, waiting for transfers between devices: 1.54 us -> 0.01 us  [shifted(): lax.ppermute(value, axis, [(i, (i + step) % peers) for i in range(peers)])]
  transfers between devices with their start and end apart: 21 -> 7, of which waited for: 10 -> 1; matrix products, arithmetic and copies ran while one was open for 0% -> 0% of each run, Pallas kernels for 20% -> 8%
where the time goes in v12:
time: 111 us
  blocking collectives  88.3 us (80%)
  Pallas kernels  16.6 us (15%)
  starting transfers between devices  4.67 us (4%)
    all_gather x2, blocking collectives, slab_tables(): return (stats, [lax.all_gather(stats, ('tm', 'space'))])  88.3 us
    pallas_call x3, Pallas kernels, call(): pl.pallas_call(kernel, out_shape=outs, in_specs=[VMEM] * len(operands), o...  13.2 us
    ppermute x2, starting transfers between devices, shifted(): lax.ppermute(value, axis, [(i, (i + step) % peers) for i in range(peers)])  3.27 us
  transfers between devices with their start and end apart: 7, of which 1 were waited for; matrix products, arithmetic and copies ran while one was open for 0% of the time, Pallas kernels for 8%

profile of v12, /device:TPU:0, one launch (start us, length us, event | category | flops | bytes accessed | tf_op | source)
XLA Modules:
  0.0 110.6 jit_solution(3604279773836510262)
XLA Ops:
  0.0 1.3 %shard_map.82 = (bf16[4,4,96,256]{3,2,1,0:T(8,128)(2,1)S(1)}, bf16[2,4,96,256]{3,2,1,0:T(8,128)(2,1)S(1)}, f32[8,512]{1,0:T(8,128)S(1)}, bf16[4,1,96,256]{3,2,1,0:T(8,128)(2,1)S(1)}) custom-call(bf16[4,4,96,256]{3,2,1,0:T(8,128)(2,1)} %feats_hbm.1), custom_call_target="tpu_custom_call" | custom-call | flops 1572864 | bytes 1572864 | tf_op jit(solution)/shard_map/pallas_call | solution.py:119
  1.3 3.0 %collective-permute-start.2 = (bf16[2,4,96,256]{3,2,1,0:T(8,128)(2,1)S(1)}, bf16[2,4,96,256]{3,2,1,0:T(8,128)(2,1)S(1)}, u32[]{:S(2)}, u32[]{:S(2)}) collective-permute-start(bf16[2,4,96,256]{3,2,1,0:T(8,128)(2,1)S(1)} %get-tuple-element.27), channel_id=1, source_target_pairs={{0,2},{2,4},{4,6},{6,8},{8,10},{10,12},{12,14},{14,16},{16,18},{18... | collective-permute-start | bytes 1179656 | tf_op jit(solution)/shard_map/ppermute | solution.py:37
  4.3 0.0 collective-permute-start
  4.3 45.1 %all-gather = f32[256,512]{1,0:T(8,128)S(1)} all-gather(f32[8,512]{1,0:T(8,128)S(1)} %get-tuple-element.21.refs_4_), channel_id=2, replica_groups=mesh['tm'=16,'space'=2] {'tm','space'}, dimensions={0}, use_global_device_ids=true | all-gather | bytes 540672 | tf_op jit(solution)/shard_map/all_gather | solution.py:41
  49.4 2.1 %shard_map.83 = (bf16[3,3,3,256,256]{4,3,2,1,0:T(8,128)(2,1)S(1)}, f32[24,256]{1,0:T(8,128)S(1)}) custom-call(bf16[3,3,3,256,256]{4,3,2,1,0:T(8,128)(2,1)} %kernel_hbm.1, s32[16]{0:T(128)} %clips_hbm.1, f32[1,256]{1,0:T(1,128)} %bitcast.8, f32[1,256]{1,0:T(1,128)} %bitcast.9, f32[1,256]{1,0:T(1,128)} %bitcast.10, f32[1,256]{1,0:T(1,128)} %bitcast.11, ...), custom_call_target="tpu_custom_call" | custom-call | bytes 7077888 | tf_op jit(solution)/shard_map/pallas_call | solution.py:159
  51.5 0.0 collective-permute-done.2.before
  51.5 0.4 collective-permute-start.3
  52.0 0.0 collective-permute-done.refs_2_
  52.0 3.3 %shard_map.84 = (bf16[2,4,96,256]{3,2,1,0:T(8,128)(2,1)S(1)}, bf16[2,6,96,256]{3,2,1,0:T(8,128)(2,1)S(1)}, f32[8,512]{1,0:T(8,128)S(1)}, f32[2,256]{1,0:T(2,128)S(1)}, bf16[2,1,96,256]{3,2,1,0:T(8,128)(2,1)S(1)}) custom-call(f32[24,256]{1,0:T(8,128)S(1)} %get-tuple-element.22.aux, f32[32,8,512]{2,1,0:T(8,128)S(1)} %bitcast.6, ...), custom_call_target="tpu_custom_call" | custom-call | flops 2717908992 | bytes 1048576 | tf_op jit(solution)/shard_map/pallas_call | solution.py:324
  55.3 0.3 collective-permute-start.1
  55.6 0.0 collective-permute-start.5
  55.6 0.0 collective-permute-done.3.refs_0_
  55.6 0.0 copy-start
  55.6 3.0 %shard_map.85 = (bf16[2,4,96,256]{3,2,1,0:T(8,128)(2,1)S(1)}, f32[8,512]{1,0:T(8,128)S(1)}, bf16[2,1,96,256]{3,2,1,0:T(8,128)(2,1)S(1)}) custom-call(f32[24,256]{1,0:T(8,128)S(1)} %get-tuple-element.22.aux, bf16[2,4,96,256]{3,2,1,0:T(8,128)(2,1)S(1)} %collective-permute-done.2.before, bf16[2,1,96,256]{3,2,1,0:T(8,128)(2,1)S(1)} %collective-permute-done.3.refs_0_, ...), custom_call_target="tpu_custom_call" | custom-call | flops 2717908992 | bytes 1048576 | tf_op jit(solution)/shard_map/pallas_call | solution.py:324
  58.6 0.6 collective-permute-start.4
  59.2 43.2 %all-gather.1 = f32[256,512]{1,0:T(8,128)S(1)} all-gather(f32[8,512]{1,0:T(8,128)S(1)} %get-tuple-element.31), channel_id=3, replica_groups=mesh['tm'=16,'space'=2] {'tm','space'}, dimensions={0}, use_global_device_ids=true | all-gather | bytes 540672 | tf_op jit(solution)/shard_map/all_gather | solution.py:41
  102.4 0.0 collective-permute-done.1.refs_5_
  102.4 0.4 collective-permute-start.6
  102.8 0.0 collective-permute-done.5.refs_4_
  102.8 0.0 collective-permute-done.4.refs_3_
  102.8 0.9 collective-permute-done.6.refs_6_
  103.8 0.0 copy-done
  103.8 6.9 %shard_map.86 = f32[4,4,96,256]{3,2,1,0:T(8,128)} custom-call(f32[24,256]{1,0:T(8,128)S(1)} %get-tuple-element.22.aux, f32[32,8,512]{2,1,0:T(8,128)S(1)} %bitcast.7, bf16[2,4,96,256]{3,2,1,0:T(8,128)(2,1)S(1)} %get-tuple-element.33.refs_1_, bf16[2,4,96,256]{3,2,1,0:T(8,128)(2,1)S(1)} %get-tuple-element.26.refs_2_, ...), custom_call_target="tpu_custom_call" | custom-call | flops 5435817984 | bytes 1048576 | tf_op jit(solution)/shard_map/pallas_call | solution.py:324
  (2 shorter events, 0.0 us)
Async XLA Ops:
  1.3 50.2 %collective-permute-start.2 = (bf16[2,4,96,256]{3,2,1,0:T(8,128)(2,1)S(1)}, bf16[2,4,96,256]{3,2,1,0:T(8,128)(2,1)S(1)}, u32[]{:S(2)}, u32[]{:S(2)}) collective-permute-start(bf16[2,4,96,256]{3,2,1,0:T(8,128)(2,1)S(1)} %get-tuple-element.27), channel_id=1, source_target_pairs={{0,2},{2,4},{4,6},{6,8},{8,10},{10,12},{12,14},{14,16},{16,18},{18... | collective-permute-start | bytes 1179656 | tf_op jit(solution)/shard_map/ppermute | solution.py:37
  4.3 47.7 %collective-permute-start = (bf16[4,1,96,256]{3,2,1,0:T(8,128)(2,1)S(1)}, bf16[4,1,96,256]{3,2,1,0:T(8,128)(2,1)S(1)}, u32[]{:S(2)}, u32[]{:S(2)}) collective-permute-start(bf16[4,1,96,256]{3,2,1,0:T(8,128)(2,1)S(1)} %get-tuple-element.24), channel_id=1, source_target_pairs={{0,1},{1,0},{2,3},{3,2},{4,5},{5,4},{6,7},{7,6},{8,9},{9,8},{10,11... | collective-permute-start | bytes 589832 | tf_op jit(solution)/shard_map/ppermute | solution.py:32
  51.5 4.0 %collective-permute-start.3 = (bf16[2,1,96,256]{3,2,1,0:T(8,128)(2,1)S(1)}, bf16[2,1,96,256]{3,2,1,0:T(8,128)(2,1)S(1)}, u32[]{:S(2)}, u32[]{:S(2)}) collective-permute-start(bf16[2,1,96,256]{3,2,1,0:T(8,128)(2,1)S(1)} %constant_dynamic-slice_fusion.1), channel_id=1, source_target_pairs={{0,1},{1,0},{2,3},{3,2},{4,5},{5,4},{6,7},{7,6},{8,9},{9,8},{10,11... | collective-permute-start | bytes 294920 | tf_op jit(solution)/shard_map/ppermute | solution.py:32
  55.3 47.1 %collective-permute-start.1 = (bf16[2,4,96,256]{3,2,1,0:T(8,128)(2,1)S(1)}, bf16[2,4,96,256]{3,2,1,0:T(8,128)(2,1)S(1)}, u32[]{:S(2)}, u32[]{:S(2)}) collective-permute-start(bf16[2,4,96,256]{3,2,1,0:T(8,128)(2,1)S(1)} %get-tuple-element.26.refs_2_), channel_id=1, source_target_pairs={{0,2},{2,4},{4,6},{6,8},{8,10},{10,12},{12,14},{14,16},{16,18},{18... | collective-permute-start | bytes 1179656 | tf_op jit(solution)/shard_map/ppermute | solution.py:37
  55.6 47.2 %collective-permute-start.5 = (bf16[2,1,96,256]{3,2,1,0:T(8,128)(2,1)S(1)}, bf16[2,1,96,256]{3,2,1,0:T(8,128)(2,1)S(1)}, u32[]{:S(2)}, u32[]{:S(2)}) collective-permute-start(bf16[2,1,96,256]{3,2,1,0:T(8,128)(2,1)S(1)} %get-tuple-element.35), channel_id=1, source_target_pairs={{0,1},{1,0},{2,3},{3,2},{4,5},{5,4},{6,7},{7,6},{8,9},{9,8},{10,11... | collective-permute-start | bytes 294920 | tf_op jit(solution)/shard_map/ppermute | solution.py:32
  55.6 48.2 %copy-start = (bf16[3,3,3,256,256]{4,3,2,1,0:T(8,128)(2,1)S(1)}, bf16[3,3,3,256,256]{4,3,2,1,0:T(8,128)(2,1)}, u32[]{:S(2)}) copy-start(bf16[3,3,3,256,256]{4,3,2,1,0:T(8,128)(2,1)} %refs_7_.1) | copy-start | bytes 10616836
  58.6 44.2 %collective-permute-start.4 = (bf16[2,1,96,256]{3,2,1,0:T(8,128)(2,1)S(1)}, bf16[2,1,96,256]{3,2,1,0:T(8,128)(2,1)S(1)}, u32[]{:S(2)}, u32[]{:S(2)}) collective-permute-start(bf16[2,1,96,256]{3,2,1,0:T(8,128)(2,1)S(1)} %get-tuple-element.34), channel_id=1, source_target_pairs={{0,1},{1,0},{2,3},{3,2},{4,5},{5,4},{6,7},{7,6},{8,9},{9,8},{10,11... | collective-permute-start | bytes 294920 | tf_op jit(solution)/shard_map/ppermute | solution.py:32
  102.4 1.4 %collective-permute-start.6 = (bf16[2,1,96,256]{3,2,1,0:T(8,128)(2,1)S(1)}, bf16[2,1,96,256]{3,2,1,0:T(8,128)(2,1)S(1)}, u32[]{:S(2)}, u32[]{:S(2)}) collective-permute-start(bf16[2,1,96,256]{3,2,1,0:T(8,128)(2,1)S(1)} %constant_dynamic-slice_fusion), channel_id=1, source_target_pairs={{0,1},{1,0},{2,3},{3,2},{4,5},{5,4},{6,7},{7,6},{8,9},{9,8},{10,11... | collective-permute-start | bytes 294920 | tf_op jit(solution)/shard_map/ppermute | solution.py:32

commit v13 on v9

--- a/solution.py
+++ b/solution.py
@@ -8,6 +8,7 @@
 from jax.sharding import PartitionSpec as P
 
 GROUPS = 32
+AXES = ("tm", "space")
 TAIL = 2
 F32, BF16 = jnp.float32, jnp.bfloat16
 
@@ -53,17 +54,40 @@
     return offsets
 
 
-def slab_tables(stats, beside=None):
+def chip_pairs(place, target):
+    slabs = lax.axis_size("tm")
+    return [(t * 2 + s, (target(t) if s == place else t) * 2 + s) for t in range(slabs) for s in range(2)]
+
+
+def slab_tables(stats, tail, beside=None):
     peers = lax.axis_size("tm")
-    total = stats + traded(stats, "space", 1) if lax.axis_size("space") == 2 else lax.psum(stats, "space")
+    shared = lax.axis_size("space") == 2
+    total = stats + traded(stats, "space", 1) if shared else lax.psum(stats, "space")
+    first, total = lax.optimization_barrier((tail, total))
+    done = () if beside is None else beside(total)
+    arrived = [lax.ppermute(first, AXES, chip_pairs(0, lambda t: (t + 1) % peers)) if shared else shifted(first, "tm", 1)]
     held, left = [total], peers
     for ways in group_sizes(peers):
         left //= ways
         block = held[0] if len(held) == 1 else jnp.concatenate(held, axis=0)
-        if left == 1 and beside is not None:
-            block, beside = lax.optimization_barrier((block, beside))
-        held = [block] + [traded(block, "tm", left * way) for way in range(1, ways)]
-    return total, held, beside
+        held = [block]
+        for way in range(1, ways):
+            mask = left * way
+            held.append(lax.ppermute(block, AXES, chip_pairs(1, lambda t: t ^ mask)) if shared else traded(block, "tm", mask))
+    if shared:
+        second, _ = lax.optimization_barrier((tail, held[0]))
+        table, arrived[0], *done = lax.optimization_barrier((jnp.concatenate(held, axis=0), arrived[0], *done))
+        arrived.append(lax.ppermute(second, AXES, chip_pairs(1, lambda t: (t + 1) % peers)))
+        held = [jnp.where(lax.axis_index("space") == 0, traded(table, "space", 1), table)]
+    return held, arrived, done
+
+
+def corner_rows(arrived):
+    if len(arrived) == 1:
+        return row_halo(edges_of(arrived[0]))
+    upper, lower = arrived
+    edge = jnp.where(lax.axis_index("space") == 0, upper[:, upper.shape[1] - 1 :], lower[:, :1])
+    return [traded(edge, "space", 1)]
 
 
 def row_halo(edges):
@@ -228,11 +252,13 @@
 
 
 def extended_row(frames, sides, frame, row):
-    n_rows = frames.shape[1]
-    inner = frames[frame, min(max(row - 1, 0), n_rows - 1)]
+    frames = frames if isinstance(frames, (list, tuple)) else [frames]
+    n_rows = frames[0].shape[1]
+    place, places = lax.axis_index("space"), lax.axis_size("space")
+    inner = [ref[frame, min(max(row - 1, 0), n_rows - 1)] for ref in frames]
+    inner = inner[0] if len(inner) == 1 else jnp.where(place == 0, inner[0], inner[1])
     if 0 < row <= n_rows:
         return inner
-    place, places = lax.axis_index("space"), lax.axis_size("space")
     side = sides[0 if row == 0 else -1]
     return jnp.where(place == (0 if row == 0 else places - 1), inner, side[frame, 0])
 
@@ -304,10 +330,8 @@
 
 
 def early_kernel(n_sides, n_before, which, aux, *refs):
-    before = [(ref, f) for ref in refs[:n_before] for f in range(ref.shape[0])]
-    corners = [refs[n_before + k * n_sides : n_before + (k + 1) * n_sides] for k in range(n_before)]
-    corners = [corners[k] for k in range(n_before) for _ in range(refs[k].shape[0])]
-    act_low, affine_in, taps, *refs = refs[n_before * (n_sides + 1) :]
+    before, corners = refs[:n_before], refs[n_before : n_before + n_sides]
+    act_low, affine_in, taps, *refs = refs[n_before + n_sides :]
     if which == 0:
         stats_in, hidden, stats, *edges, act_before = refs
     else:
@@ -315,9 +339,9 @@
     slabs = aux.shape[0] - 8
     starting = aux[slabs : slabs + 1] != 0.0
     affine = affine_in[0:1], affine_in[1:2]
-    for frame, (ref, index) in enumerate(before):
-        for row in range(ref.shape[1] + 2):
-            value = normed(extended_row(ref, corners[frame], index, row), affine).astype(F32)
+    for frame in range(2):
+        for row in range(act_low.shape[1]):
+            value = normed(extended_row(before, corners, frame, row), affine).astype(F32)
             act_before[frame, row] = jnp.where(starting, act_low[0, row].astype(F32), value).astype(BF16)
     planes = [(act_before, 0), (act_before, 1)] + [(act_low, f) for f in range(act_low.shape[0])]
     sums = no_stats(act_low.shape[3])
@@ -364,12 +388,9 @@
     stats_shape = shaped((1, 2 * width), F32)
 
     frames, tail, stats, edges = entry_call(feats)
-    total, tables, first_part = slab_tables(stats, shifted(tail[:1], "tm", 1))
+    setup = functools.partial(setup_call, kernel_one, clip_ids, params, per_slab)
+    tables, before, (taps, aux) = slab_tables(stats, tail, setup)
     sides = row_halo(edges)
-    second, _ = lax.optimization_barrier((tail[1:], total))
-    before = [first_part, shifted(second, "tm", 1)]
-    corners = [corner for part in before for corner in row_halo(edges_of(part))]
-    taps, aux = setup_call(kernel_one, clip_ids, params, per_slab, total)
     n_sides = len(sides)
     act_low, affine, hidden_late, stats, *edges = call(
         functools.partial(late_kernel, len(tables), n_sides, 0),
@@ -378,8 +399,8 @@
         late,
         [aux, *tables, frames, *sides, *sides, taps],
     )
-    tail = hidden_late[late - 2 :]
-    before_two = shifted(tail, "tm", 1)
+    *before, affine = lax.optimization_barrier((*before, affine))
+    corners = corner_rows(before)
     sides_late = row_halo(edges)
     hidden_early, stats, *edges = call(
         functools.partial(early_kernel, n_sides, len(before), 0),
@@ -390,9 +411,7 @@
     )
 
     sides_early = row_halo(edges)
-    _, tables, _ = slab_tables(stats)
-    before_two, *tables = lax.optimization_barrier((before_two, *tables))
-    corners = row_halo(edges_of(before_two))
+    tables, before, _ = slab_tables(stats, hidden_late[late - 2 :])
     act_low, affine, out = call(
         functools.partial(late_kernel, len(tables), n_sides, 1),
         act_shapes + [shaped(feats.shape, F32)],
@@ -401,9 +420,11 @@
         [aux, *tables, hidden_early, *sides_early, *sides_late, kernel_two, hidden_late, frames],
         out_specs=[VMEM, VMEM, ANYWHERE],
     )
-    operands = [aux, before_two, *corners, act_low, affine, kernel_two, frames, out]
+    *before, affine = lax.optimization_barrier((*before, affine))
+    corners = corner_rows(before)
+    operands = [aux, *before, *corners, act_low, affine, kernel_two, frames, out]
     return call(
-        functools.partial(early_kernel, n_sides, 1, 1),
+        functools.partial(early_kernel, n_sides, len(before), 1),
         shaped(feats.shape, F32),
         [act, pltpu.VMEM((2, n_rows, cols, width), F32), pltpu.SemaphoreType.DMA((2,))],
         2,

time: 54.2 us -> 86.2 us (1.59)
  starting transfers between devices: 23.1 us -> 48.5 us
  local copies, waits for them, and re-layouts: 0.05 us -> 5.86 us
    ppermute x20 -> x9, starting transfers between devices: 18.5 us -> 32.6 us  [traded(): lax.ppermute(value, axis, [(i, i ^ mask) for i in range(lax.axis_size(axi...]
    ppermute x3 -> x16, starting transfers between devices: 4.59 us -> 15.9 us  [the longest x12 7.94 us: slab_tables(): lax.ppermute(block, AXES, chip_pairs(1, lambda t: t ^ mask))]
    unnamed x2 -> x10, local copies, waits for them, and re-layouts: 0.01 us -> 5.76 us
    ppermute x3 -> x16, waiting for transfers between devices: 5.92 us -> 9 us  [the longest x2 8.96 us: slab_tables(): lax.ppermute(first, AXES, chip_pairs(0, lambda t: (t + 1) % peers))]
    ppermute x20 -> x9, waiting for transfers between devices: 7.32 us -> 4.44 us  [traded(): lax.ppermute(value, axis, [(i, i ^ mask) for i in range(lax.axis_size(axi...]
  transfers between devices with their start and end apart: 23 -> 25, of which waited for: 7 -> 10; matrix products, arithmetic and copies ran while one was open for 0% -> 0% of each run, Pallas kernels for 23% -> 11%
where the time goes in v13:
time: 86.2 us; the launch traced here: 85.6 us
  starting transfers between devices  48.5 us (56%)
  Pallas kernels  17.4 us (20%)
  waiting for transfers between devices  13.4 us (16%)
  local copies, waits for them, and re-layouts  5.86 us (7%)
    ppermute x9, starting transfers between devices, traded(): lax.ppermute(value, axis, [(i, i ^ mask) for i in range(lax.axis_size(axi...  32.6 us
    pallas_call x4, Pallas kernels, call(): pl.pallas_call(kernel, out_shape=outs, in_specs=[VMEM if aliases is None...  14 us
    ppermute x2, waiting for transfers between devices, slab_tables(): lax.ppermute(first, AXES, chip_pairs(0, lambda t: (t + 1) % peers))  8.96 us
    ppermute x12, starting transfers between devices, slab_tables(): lax.ppermute(block, AXES, chip_pairs(1, lambda t: t ^ mask))  7.94 us
    ppermute x2, starting transfers between devices, slab_tables(): lax.ppermute(first, AXES, chip_pairs(0, lambda t: (t + 1) % peers))  6.63 us
    unnamed x10, local copies, waits for them, and re-layouts  5.76 us
    ppermute x9, waiting for transfers between devices, traded(): lax.ppermute(value, axis, [(i, i ^ mask) for i in range(lax.axis_size(axi...  4.44 us
    pallas_call x1, Pallas kernels, setup_call(): pl.pallas_call(functools.partial(setup_kernel, slabs, per_slab), out_shap...  2.12 us
  transfers between devices with their start and end apart: 25, of which 10 were waited for; matrix products, arithmetic and copies ran while one was open for 0% of the time, Pallas kernels for 11%

profile of v13, /device:TPU:0, one launch (start us, length us, event | category | flops | bytes accessed | tf_op | source)
XLA Modules:
  0.0 85.6 jit_solution(14998574496000222114)
XLA Ops:
  0.0 1.3 %shard_map.82 = (bf16[4,4,96,256]{3,2,1,0:T(8,128)(2,1)S(1)}, bf16[2,4,96,256]{3,2,1,0:T(8,128)(2,1)S(1)}, f32[1,512]{1,0:T(1,128)S(1)}, bf16[4,1,96,256]{3,2,1,0:T(8,128)(2,1)S(1)}) custom-call(bf16[4,4,96,256]{3,2,1,0:T(8,128)(2,1)} %feats_hbm.1), custom_call_target="tpu_custom_call" | custom-call | flops 1572864 | bytes 1572864 | tf_op jit(solution)/shard_map/pallas_call | solution.py:161
  1.3 0.5 collective-permute-start
  1.8 0.8 collective-permute-done
  2.7 4.7 %collective-permute-start.7 = (bf16[2,4,96,256]{3,2,1,0:T(8,128)(2,1)S(1)}, bf16[2,4,96,256]{3,2,1,0:T(8,128)(2,1)S(1)}, u32[]{:S(2)}, u32[]{:S(2)}) collective-permute-start(bf16[2,4,96,256]{3,2,1,0:T(8,128)(2,1)S(1)} %get-tuple-element.53), channel_id=1, source_target_pairs={{0,2},{1,1},{2,4},{3,3},{4,6},{5,5},{6,8},{7,7},{8,10},{9,9},{10,1... | collective-permute-start | bytes 1179656 | tf_op jit(solution)/shard_map/ppermute | solution.py:68
  7.4 0.7 collective-permute-start.3
  8.1 0.7 collective-permute-start.2
  8.7 0.7 collective-permute-start.1
  9.4 0.0 collective-permute-done.3
  9.4 0.0 collective-permute-done.2
  9.4 0.0 collective-permute-done.1
  9.4 0.7 collective-permute-start.6
  10.1 0.7 collective-permute-start.5
  10.8 0.7 collective-permute-start.4
  11.5 2.1 %shard_map.83 = (bf16[3,3,3,256,256]{4,3,2,1,0:T(8,128)(2,1)S(1)}, f32[24,256]{1,0:T(8,128)S(1)}) custom-call(bf16[3,3,3,256,256]{4,3,2,1,0:T(8,128)(2,1)} %kernel_hbm.1, s32[16]{0:T(128)} %clips_hbm.1, f32[1,256]{1,0:T(1,128)} %bitcast.4, f32[1,256]{1,0:T(1,128)} %bitcast.5, f32[1,256]{1,0:T(1,128)} %bitcast.6, f32[1,256]{1,0:T(1,128)} %bitcast.7, ...), custom_call_target="tpu_custom_call" | custom-call | bytes 7077888 | tf_op jit(solution)/shard_map/pallas_call | solution.py:201
  13.6 0.0 copy-start.2
  13.6 1.7 %copy-done.2 = bf16[3,3,3,256,256]{4,3,2,1,0:T(8,128)(2,1)} copy-done((bf16[3,3,3,256,256]{4,3,2,1,0:T(8,128)(2,1)}, bf16[3,3,3,256,256]{4,3,2,1,0:T(8,128)(2,1)S(1)}, u32[]{:S(2)}) %copy-start.2) | copy-done | bytes 3538968
  15.3 0.0 collective-permute-done.6
  15.3 0.0 collective-permute-done.5
  15.3 0.0 collective-permute-done.4
  15.4 0.1 concatenate.15
  15.4 1.8 %collective-permute-done.7.refs_0_ = bf16[2,4,96,256]{3,2,1,0:T(8,128)(2,1)S(1)} collective-permute-done((bf16[2,4,96,256]{3,2,1,0:T(8,128)(2,1)S(1)}, bf16[2,4,96,256]{3,2,1,0:T(8,128)(2,1)S(1)}, u32[]{:S(2)}, u32[]{:S(2)}) %collective-permute-start.7) | collective-permute-done | bytes 393248 | tf_op jit(solution)/shard_map/ppermute | solution.py:68
  17.2 11.9 %collective-permute-start.8 = (f32[16,512]{1,0:T(8,128)S(1)}, f32[16,512]{1,0:T(8,128)S(1)}, u32[]{:S(2)}, u32[]{:S(2)}) collective-permute-start(f32[16,512]{1,0:T(8,128)S(1)} %concatenate.15), channel_id=1, source_target_pairs={{0,1},{1,0},{2,3},{3,2},{4,5},{5,4},{6,7},{7,6},{8,9},{9,8},{10,11... | collective-permute-start | bytes 98312 | tf_op jit(solution)/shard_map/ppermute | solution.py:33
  29.1 0.1 collective-permute-start.9
  29.2 0.7 collective-permute-start.10
  29.8 0.1 collective-permute-done.8
  29.9 0.6 collective-permute-done.9.refs_2_.refs_3_
  30.5 2.0 %copy-done.3 = bf16[3,3,3,256,256]{4,3,2,1,0:T(8,128)(2,1)S(1)} copy-done((bf16[3,3,3,256,256]{4,3,2,1,0:T(8,128)(2,1)S(1)}, bf16[3,3,3,256,256]{4,3,2,1,0:T(8,128)(2,1)}, u32[]{:S(2)}) %copy-start.3) | copy-done | bytes 3538968
  32.5 3.2 %shard_map.84 = (bf16[2,6,96,256]{3,2,1,0:T(8,128)(2,1)S(1)}, f32[2,256]{1,0:T(2,128)S(1)}, bf16[2,4,96,256]{3,2,1,0:T(8,128)(2,1)S(1)}, f32[1,512]{1,0:T(1,128)S(1)}, bf16[2,1,96,256]{3,2,1,0:T(8,128)(2,1)S(1)}) custom-call(f32[24,256]{1,0:T(8,128)S(1)} %get-tuple-element.46.aux, f32[16,512]{1,0:T(8,128)S(1)} %broadcast_select_fusion.1.refs_0_, ...), custom_call_target="tpu_custom_call" | custom-call | flops 2717908992 | bytes 1048576 | tf_op jit(solution)/shard_map/pallas_call | solution.py:367
  35.7 0.0 collective-permute-done.10.refs_1_
  35.8 6.0 %collective-permute-start.11 = (bf16[2,1,96,256]{3,2,1,0:T(8,128)(2,1)S(1)}, bf16[2,1,96,256]{3,2,1,0:T(8,128)(2,1)S(1)}, u32[]{:S(2)}, u32[]{:S(2)}) collective-permute-start(bf16[2,1,96,256]{3,2,1,0:T(8,128)(2,1)S(1)} %slice_select_fusion.1), channel_id=1, source_target_pairs={{0,1},{1,0},{2,3},{3,2},{4,5},{5,4},{6,7},{7,6},{8,9},{9,8},{10,11... | collective-permute-start | bytes 294920 | tf_op jit(solution)/shard_map/ppermute | solution.py:33
  41.8 0.9 %collective-permute-done.11.refs_2_ = bf16[2,1,96,256]{3,2,1,0:T(8,128)(2,1)S(1)} collective-permute-done((bf16[2,1,96,256]{3,2,1,0:T(8,128)(2,1)S(1)}, bf16[2,1,96,256]{3,2,1,0:T(8,128)(2,1)S(1)}, u32[]{:S(2)}, u32[]{:S(2)}) %collective-permute-start.11) | collective-permute-done | bytes 98336 | tf_op jit(solution)/shard_map/ppermute | solution.py:33
  42.7 0.0 copy-done.4
  42.7 3.0 %shard_map.85 = (bf16[2,4,96,256]{3,2,1,0:T(8,128)(2,1)S(1)}, f32[1,512]{1,0:T(1,128)S(1)}, bf16[2,1,96,256]{3,2,1,0:T(8,128)(2,1)S(1)}) custom-call(f32[24,256]{1,0:T(8,128)S(1)} %get-tuple-element.46.aux, bf16[2,4,96,256]{3,2,1,0:T(8,128)(2,1)S(1)} %collective-permute-done.7.refs_0_, bf16[2,4,96,256]{3,2,1,0:T(8,128)(2,1)S(1)} %collective-permute-done.10.refs_1_, ...), custom_call_target="tpu_custom_call" | custom-call | flops 2717908992 | bytes 1048576 | tf_op jit(solution)/shard_map/pallas_call | solution.py:367
  45.7 0.4 collective-permute-start.12
  46.2 0.8 collective-permute-done.12
  47.0 1.9 %collective-permute-start.19 = (bf16[2,4,96,256]{3,2,1,0:T(8,128)(2,1)S(1)}, bf16[2,4,96,256]{3,2,1,0:T(8,128)(2,1)S(1)}, u32[]{:S(2)}, u32[]{:S(2)}) collective-permute-start(bf16[2,4,96,256]{3,2,1,0:T(8,128)(2,1)S(1)} %get-tuple-element.64.refs_5_), channel_id=1, source_target_pairs={{0,2},{1,1},{2,4},{3,3},{4,6},{5,5},{6,8},{7,7},{8,10},{9,9},{10,1... | collective-permute-start | bytes 1179656 | tf_op jit(solution)/shard_map/ppermute | solution.py:68
  48.9 0.7 collective-permute-start.15
  49.6 0.7 collective-permute-start.14
  50.3 0.7 collective-permute-start.13
  50.9 0.0 collective-permute-done.15
  50.9 0.0 collective-permute-done.14
  51.0 0.0 collective-permute-done.13
  51.0 0.7 collective-permute-start.18
  51.7 0.7 collective-permute-start.17
  52.3 0.7 collective-permute-start.16
  53.0 0.0 collective-permute-done.18
  53.0 0.0 collective-permute-done.17
  53.0 0.0 collective-permute-done.16
  53.0 0.1 concatenate.17
  53.1 7.2 %collective-permute-done.19.refs_0_ = bf16[2,4,96,256]{3,2,1,0:T(8,128)(2,1)S(1)} collective-permute-done((bf16[2,4,96,256]{3,2,1,0:T(8,128)(2,1)S(1)}, bf16[2,4,96,256]{3,2,1,0:T(8,128)(2,1)S(1)}, u32[]{:S(2)}, u32[]{:S(2)}) %collective-permute-start.19) | collective-permute-done | bytes 393248 | tf_op jit(solution)/shard_map/ppermute | solution.py:68
  60.3 7.9 %collective-permute-start.21 = (f32[16,512]{1,0:T(8,128)S(1)}, f32[16,512]{1,0:T(8,128)S(1)}, u32[]{:S(2)}, u32[]{:S(2)}) collective-permute-start(f32[16,512]{1,0:T(8,128)S(1)} %concatenate.17), channel_id=1, source_target_pairs={{0,1},{1,0},{2,3},{3,2},{4,5},{5,4},{6,7},{7,6},{8,9},{9,8},{10,11... | collective-permute-start | bytes 98312 | tf_op jit(solution)/shard_map/ppermute | solution.py:33
  68.1 0.1 collective-permute-start.23
  68.2 0.4 collective-permute-start.22
  68.7 0.7 collective-permute-start.20
  69.3 0.0 collective-permute-done.21
  69.4 0.1 collective-permute-done.23.refs_3_
  69.4 0.2 collective-permute-done.22.refs_2_
  69.6 2.0 %copy-done = bf16[3,3,3,256,256]{4,3,2,1,0:T(8,128)(2,1)S(1)} copy-done((bf16[3,3,3,256,256]{4,3,2,1,0:T(8,128)(2,1)S(1)}, bf16[3,3,3,256,256]{4,3,2,1,0:T(8,128)(2,1)}, u32[]{:S(2)}) %copy-start) | copy-done | bytes 3538968
  71.6 4.0 %shard_map.86 = (bf16[2,6,96,256]{3,2,1,0:T(8,128)(2,1)S(1)}, f32[2,256]{1,0:T(2,128)S(1)}, f32[4,4,96,256]{3,2,1,0:T(8,128)}) custom-call(f32[24,256]{1,0:T(8,128)S(1)} %get-tuple-element.46.aux, f32[16,512]{1,0:T(8,128)S(1)} %broadcast_select_fusion.refs_0_, bf16[2,4,96,256]{3,2,1,0:T(8,128)(2,1)S(1)} %get-tuple-element.66.refs_1_, ...), custom_call_target="tpu_custom_call" | custom-call | flops 2717908992 | bytes 1048576 | tf_op jit(solution)/shard_map/pallas_call | solution.py:367
  75.6 0.0 collective-permute-done.20.refs_1_
  75.6 5.3 %collective-permute-start.24 = (bf16[2,1,96,256]{3,2,1,0:T(8,128)(2,1)S(1)}, bf16[2,1,96,256]{3,2,1,0:T(8,128)(2,1)S(1)}, u32[]{:S(2)}, u32[]{:S(2)}) collective-permute-start(bf16[2,1,96,256]{3,2,1,0:T(8,128)(2,1)S(1)} %slice_select_fusion), channel_id=1, source_target_pairs={{0,1},{1,0},{2,3},{3,2},{4,5},{5,4},{6,7},{7,6},{8,9},{9,8},{10,11... | collective-permute-start | bytes 294920 | tf_op jit(solution)/shard_map/ppermute | solution.py:33
  80.9 0.9 %collective-permute-done.24.refs_2_ = bf16[2,1,96,256]{3,2,1,0:T(8,128)(2,1)S(1)} collective-permute-done((bf16[2,1,96,256]{3,2,1,0:T(8,128)(2,1)S(1)}, bf16[2,1,96,256]{3,2,1,0:T(8,128)(2,1)S(1)}, u32[]{:S(2)}, u32[]{:S(2)}) %collective-permute-start.24) | collective-permute-done | bytes 98336 | tf_op jit(solution)/shard_map/ppermute | solution.py:33
  81.9 0.0 copy-done.1
  81.9 3.8 %shard_map.87 = f32[4,4,96,256]{3,2,1,0:T(8,128)} custom-call(f32[24,256]{1,0:T(8,128)S(1)} %get-tuple-element.46.aux, bf16[2,4,96,256]{3,2,1,0:T(8,128)(2,1)S(1)} %collective-permute-done.19.refs_0_, bf16[2,4,96,256]{3,2,1,0:T(8,128)(2,1)S(1)} %collective-permute-done.20.refs_1_, ...), custom_call_target="tpu_custom_call", output_to_operand_aliasing={{}: (8, {})} | custom-call | flops 2717908992 | bytes 1048576 | tf_op jit(solution)/shard_map/pallas_call | solution.py:367
  (12 shorter events, 0.1 us)
Async XLA Ops:
  1.3 1.3 %collective-permute-start = (f32[1,512]{1,0:T(1,128)S(1)}, f32[1,512]{1,0:T(1,128)S(1)}, u32[]{:S(2)}, u32[]{:S(2)}) collective-permute-start(f32[1,512]{1,0:T(1,128)S(1)} %get-tuple-element.41), channel_id=1, source_target_pairs={{0,1},{1,0},{2,3},{3,2},{4,5},{5,4},{6,7},{7,6},{8,9},{9,8},{10,11... | collective-permute-start | bytes 6152 | tf_op jit(solution)/shard_map/ppermute | solution.py:33
  2.7 14.5 %collective-permute-start.7 = (bf16[2,4,96,256]{3,2,1,0:T(8,128)(2,1)S(1)}, bf16[2,4,96,256]{3,2,1,0:T(8,128)(2,1)S(1)}, u32[]{:S(2)}, u32[]{:S(2)}) collective-permute-start(bf16[2,4,96,256]{3,2,1,0:T(8,128)(2,1)S(1)} %get-tuple-element.53), channel_id=1, source_target_pairs={{0,2},{1,1},{2,4},{3,3},{4,6},{5,5},{6,8},{7,7},{8,10},{9,9},{10,1... | collective-permute-start | bytes 1179656 | tf_op jit(solution)/shard_map/ppermute | solution.py:68
  7.4 2.0 %collective-permute-start.3 = (f32[1,512]{1,0:T(1,128)S(1)}, f32[1,512]{1,0:T(1,128)S(1)}, u32[]{:S(2)}, u32[]{:S(2)}) collective-permute-start(f32[1,512]{1,0:T(1,128)S(1)} %add.6.refs_4_), channel_id=1, source_target_pairs={{0,0},{1,25},{2,2},{3,27},{4,4},{5,29},{6,6},{7,31},{8,8},{9,17},{... | collective-permute-start | bytes 6152 | tf_op jit(solution)/shard_map/ppermute | solution.py:76
  8.1 1.4 %collective-permute-start.2 = (f32[1,512]{1,0:T(1,128)S(1)}, f32[1,512]{1,0:T(1,128)S(1)}, u32[]{:S(2)}, u32[]{:S(2)}) collective-permute-start(f32[1,512]{1,0:T(1,128)S(1)} %add.6.refs_4_), channel_id=1, source_target_pairs={{0,0},{1,17},{2,2},{3,19},{4,4},{5,21},{6,6},{7,23},{8,8},{9,25},{... | collective-permute-start | bytes 6152 | tf_op jit(solution)/shard_map/ppermute | solution.py:76
  8.7 0.7 collective-permute-start.1
  9.4 5.9 %collective-permute-start.6 = (f32[4,512]{1,0:T(4,128)S(1)}, f32[4,512]{1,0:T(4,128)S(1)}, u32[]{:S(2)}, u32[]{:S(2)}) collective-permute-start(f32[4,512]{1,0:T(4,128)S(1)} %pad_maximum_fusion), channel_id=1, source_target_pairs={{0,0},{1,7},{2,2},{3,5},{4,4},{5,3},{6,6},{7,1},{8,8},{9,15},{10,1... | collective-permute-start | bytes 24584 | tf_op jit(solution)/shard_map/ppermute | solution.py:76
  10.1 5.2 %collective-permute-start.5 = (f32[4,512]{1,0:T(4,128)S(1)}, f32[4,512]{1,0:T(4,128)S(1)}, u32[]{:S(2)}, u32[]{:S(2)}) collective-permute-start(f32[4,512]{1,0:T(4,128)S(1)} %pad_maximum_fusion), channel_id=1, source_target_pairs={{0,0},{1,5},{2,2},{3,7},{4,4},{5,1},{6,6},{7,3},{8,8},{9,13},{10,1... | collective-permute-start | bytes 24584 | tf_op jit(solution)/shard_map/ppermute | solution.py:76
  10.8 4.6 %collective-permute-start.4 = (f32[4,512]{1,0:T(4,128)S(1)}, f32[4,512]{1,0:T(4,128)S(1)}, u32[]{:S(2)}, u32[]{:S(2)}) collective-permute-start(f32[4,512]{1,0:T(4,128)S(1)} %pad_maximum_fusion), channel_id=1, source_target_pairs={{0,0},{1,3},{2,2},{3,1},{4,4},{5,7},{6,6},{7,5},{8,8},{9,11},{10,1... | collective-permute-start | bytes 24584 | tf_op jit(solution)/shard_map/ppermute | solution.py:76
  13.6 1.8 %copy-start.2 = (bf16[3,3,3,256,256]{4,3,2,1,0:T(8,128)(2,1)}, bf16[3,3,3,256,256]{4,3,2,1,0:T(8,128)(2,1)S(1)}, u32[]{:S(2)}) copy-start(bf16[3,3,3,256,256]{4,3,2,1,0:T(8,128)(2,1)S(1)} %get-tuple-element.50.refs_4_.refs_5_) | copy-start | bytes 10616836
  17.2 12.8 %collective-permute-start.8 = (f32[16,512]{1,0:T(8,128)S(1)}, f32[16,512]{1,0:T(8,128)S(1)}, u32[]{:S(2)}, u32[]{:S(2)}) collective-permute-start(f32[16,512]{1,0:T(8,128)S(1)} %concatenate.15), channel_id=1, source_target_pairs={{0,1},{1,0},{2,3},{3,2},{4,5},{5,4},{6,7},{7,6},{8,9},{9,8},{10,11... | collective-permute-start | bytes 98312 | tf_op jit(solution)/shard_map/ppermute | solution.py:33
  29.1 1.4 %collective-permute-start.9 = (bf16[4,1,96,256]{3,2,1,0:T(8,128)(2,1)S(1)}, bf16[4,1,96,256]{3,2,1,0:T(8,128)(2,1)S(1)}, u32[]{:S(2)}, u32[]{:S(2)}) collective-permute-start(bf16[4,1,96,256]{3,2,1,0:T(8,128)(2,1)S(1)} %get-tuple-element.49), channel_id=1, source_target_pairs={{0,1},{1,0},{2,3},{3,2},{4,5},{5,4},{6,7},{7,6},{8,9},{9,8},{10,11... | collective-permute-start | bytes 589832 | tf_op jit(solution)/shard_map/ppermute | solution.py:33
  29.2 6.6 %collective-permute-start.10 = (bf16[2,4,96,256]{3,2,1,0:T(8,128)(2,1)S(1)}, bf16[2,4,96,256]{3,2,1,0:T(8,128)(2,1)S(1)}, u32[]{:S(2)}, u32[]{:S(2)}) collective-permute-start(bf16[2,4,96,256]{3,2,1,0:T(8,128)(2,1)S(1)} %get-tuple-element.53), channel_id=1, source_target_pairs={{0,0},{1,3},{2,2},{3,5},{4,4},{5,7},{6,6},{7,9},{8,8},{9,11},{10,1... | collective-permute-start | bytes 1179656 | tf_op jit(solution)/shard_map/ppermute | solution.py:80
  30.5 2.0 %copy-start.3 = (bf16[3,3,3,256,256]{4,3,2,1,0:T(8,128)(2,1)S(1)}, bf16[3,3,3,256,256]{4,3,2,1,0:T(8,128)(2,1)}, u32[]{:S(2)}) copy-start(bf16[3,3,3,256,256]{4,3,2,1,0:T(8,128)(2,1)} %copy-done.2) | copy-start | bytes 10616836
  32.5 10.2 %copy-start.4 = (bf16[3,3,3,256,256]{4,3,2,1,0:T(8,128)(2,1)S(1)}, bf16[3,3,3,256,256]{4,3,2,1,0:T(8,128)(2,1)}, u32[]{:S(2)}) copy-start(bf16[3,3,3,256,256]{4,3,2,1,0:T(8,128)(2,1)} %copy-done.2) | copy-start | bytes 10616836
  35.8 6.9 %collective-permute-start.11 = (bf16[2,1,96,256]{3,2,1,0:T(8,128)(2,1)S(1)}, bf16[2,1,96,256]{3,2,1,0:T(8,128)(2,1)S(1)}, u32[]{:S(2)}, u32[]{:S(2)}) collective-permute-start(bf16[2,1,96,256]{3,2,1,0:T(8,128)(2,1)S(1)} %slice_select_fusion.1), channel_id=1, source_target_pairs={{0,1},{1,0},{2,3},{3,2},{4,5},{5,4},{6,7},{7,6},{8,9},{9,8},{10,11... | collective-permute-start | bytes 294920 | tf_op jit(solution)/shard_map/ppermute | solution.py:33
  45.7 1.3 %collective-permute-start.12 = (f32[1,512]{1,0:T(1,128)S(1)}, f32[1,512]{1,0:T(1,128)S(1)}, u32[]{:S(2)}, u32[]{:S(2)}) collective-permute-start(f32[1,512]{1,0:T(1,128)S(1)} %get-tuple-element.60), channel_id=1, source_target_pairs={{0,1},{1,0},{2,3},{3,2},{4,5},{5,4},{6,7},{7,6},{8,9},{9,8},{10,11... | collective-permute-start | bytes 6152 | tf_op jit(solution)/shard_map/ppermute | solution.py:33
  47.0 13.3 %collective-permute-start.19 = (bf16[2,4,96,256]{3,2,1,0:T(8,128)(2,1)S(1)}, bf16[2,4,96,256]{3,2,1,0:T(8,128)(2,1)S(1)}, u32[]{:S(2)}, u32[]{:S(2)}) collective-permute-start(bf16[2,4,96,256]{3,2,1,0:T(8,128)(2,1)S(1)} %get-tuple-element.64.refs_5_), channel_id=1, source_target_pairs={{0,2},{1,1},{2,4},{3,3},{4,6},{5,5},{6,8},{7,7},{8,10},{9,9},{10,1... | collective-permute-start | bytes 1179656 | tf_op jit(solution)/shard_map/ppermute | solution.py:68
  48.9 2.0 %collective-permute-start.15 = (f32[1,512]{1,0:T(1,128)S(1)}, f32[1,512]{1,0:T(1,128)S(1)}, u32[]{:S(2)}, u32[]{:S(2)}) collective-permute-start(f32[1,512]{1,0:T(1,128)S(1)} %add.7), channel_id=1, source_target_pairs={{0,0},{1,25},{2,2},{3,27},{4,4},{5,29},{6,6},{7,31},{8,8},{9,17},{... | collective-permute-start | bytes 6152 | tf_op jit(solution)/shard_map/ppermute | solution.py:76
  49.6 1.4 %collective-permute-start.14 = (f32[1,512]{1,0:T(1,128)S(1)}, f32[1,512]{1,0:T(1,128)S(1)}, u32[]{:S(2)}, u32[]{:S(2)}) collective-permute-start(f32[1,512]{1,0:T(1,128)S(1)} %add.7), channel_id=1, source_target_pairs={{0,0},{1,17},{2,2},{3,19},{4,4},{5,21},{6,6},{7,23},{8,8},{9,25},{... | collective-permute-start | bytes 6152 | tf_op jit(solution)/shard_map/ppermute | solution.py:76
  50.3 0.7 collective-permute-start.13
  51.0 2.0 %collective-permute-start.18 = (f32[4,512]{1,0:T(4,128)S(1)}, f32[4,512]{1,0:T(4,128)S(1)}, u32[]{:S(2)}, u32[]{:S(2)}) collective-permute-start(f32[4,512]{1,0:T(4,128)S(1)} %pad_maximum_fusion.1), channel_id=1, source_target_pairs={{0,0},{1,7},{2,2},{3,5},{4,4},{5,3},{6,6},{7,1},{8,8},{9,15},{10,1... | collective-permute-start | bytes 24584 | tf_op jit(solution)/shard_map/ppermute | solution.py:76
  51.7 1.4 %collective-permute-start.17 = (f32[4,512]{1,0:T(4,128)S(1)}, f32[4,512]{1,0:T(4,128)S(1)}, u32[]{:S(2)}, u32[]{:S(2)}) collective-permute-start(f32[4,512]{1,0:T(4,128)S(1)} %pad_maximum_fusion.1), channel_id=1, source_target_pairs={{0,0},{1,5},{2,2},{3,7},{4,4},{5,1},{6,6},{7,3},{8,8},{9,13},{10,1... | collective-permute-start | bytes 24584 | tf_op jit(solution)/shard_map/ppermute | solution.py:76
  52.3 0.7 collective-permute-start.16
  60.3 9.1 %collective-permute-start.21 = (f32[16,512]{1,0:T(8,128)S(1)}, f32[16,512]{1,0:T(8,128)S(1)}, u32[]{:S(2)}, u32[]{:S(2)}) collective-permute-start(f32[16,512]{1,0:T(8,128)S(1)} %concatenate.17), channel_id=1, source_target_pairs={{0,1},{1,0},{2,3},{3,2},{4,5},{5,4},{6,7},{7,6},{8,9},{9,8},{10,11... | collective-permute-start | bytes 98312 | tf_op jit(solution)/shard_map/ppermute | solution.py:33
  68.1 1.3 %collective-permute-start.23 = (bf16[2,1,96,256]{3,2,1,0:T(8,128)(2,1)S(1)}, bf16[2,1,96,256]{3,2,1,0:T(8,128)(2,1)S(1)}, u32[]{:S(2)}, u32[]{:S(2)}) collective-permute-start(bf16[2,1,96,256]{3,2,1,0:T(8,128)(2,1)S(1)} %get-tuple-element.68), channel_id=1, source_target_pairs={{0,1},{1,0},{2,3},{3,2},{4,5},{5,4},{6,7},{7,6},{8,9},{9,8},{10,11... | collective-permute-start | bytes 294920 | tf_op jit(solution)/shard_map/ppermute | solution.py:33
  68.2 1.4 %collective-permute-start.22 = (bf16[2,1,96,256]{3,2,1,0:T(8,128)(2,1)S(1)}, bf16[2,1,96,256]{3,2,1,0:T(8,128)(2,1)S(1)}, u32[]{:S(2)}, u32[]{:S(2)}) collective-permute-start(bf16[2,1,96,256]{3,2,1,0:T(8,128)(2,1)S(1)} %get-tuple-element.67), channel_id=1, source_target_pairs={{0,1},{1,0},{2,3},{3,2},{4,5},{5,4},{6,7},{7,6},{8,9},{9,8},{10,11... | collective-permute-start | bytes 294920 | tf_op jit(solution)/shard_map/ppermute | solution.py:33
  68.7 7.0 %collective-permute-start.20 = (bf16[2,4,96,256]{3,2,1,0:T(8,128)(2,1)S(1)}, bf16[2,4,96,256]{3,2,1,0:T(8,128)(2,1)S(1)}, u32[]{:S(2)}, u32[]{:S(2)}) collective-permute-start(bf16[2,4,96,256]{3,2,1,0:T(8,128)(2,1)S(1)} %get-tuple-element.64.refs_5_), channel_id=1, source_target_pairs={{0,0},{1,3},{2,2},{3,5},{4,4},{5,7},{6,6},{7,9},{8,8},{9,11},{10,1... | collective-permute-start | bytes 1179656 | tf_op jit(solution)/shard_map/ppermute | solution.py:80
  69.6 2.0 %copy-start = (bf16[3,3,3,256,256]{4,3,2,1,0:T(8,128)(2,1)S(1)}, bf16[3,3,3,256,256]{4,3,2,1,0:T(8,128)(2,1)}, u32[]{:S(2)}) copy-start(bf16[3,3,3,256,256]{4,3,2,1,0:T(8,128)(2,1)} %refs_5_.1) | copy-start | bytes 10616836
  71.6 10.3 %copy-start.1 = (bf16[3,3,3,256,256]{4,3,2,1,0:T(8,128)(2,1)S(1)}, bf16[3,3,3,256,256]{4,3,2,1,0:T(8,128)(2,1)}, u32[]{:S(2)}) copy-start(bf16[3,3,3,256,256]{4,3,2,1,0:T(8,128)(2,1)} %refs_5_.1) | copy-start | bytes 10616836
  75.6 6.2 %collective-permute-start.24 = (bf16[2,1,96,256]{3,2,1,0:T(8,128)(2,1)S(1)}, bf16[2,1,96,256]{3,2,1,0:T(8,128)(2,1)S(1)}, u32[]{:S(2)}, u32[]{:S(2)}) collective-permute-start(bf16[2,1,96,256]{3,2,1,0:T(8,128)(2,1)S(1)} %slice_select_fusion), channel_id=1, source_target_pairs={{0,1},{1,0},{2,3},{3,2},{4,5},{5,4},{6,7},{7,6},{8,9},{9,8},{10,11... | collective-permute-start | bytes 294920 | tf_op jit(solution)/shard_map/ppermute | solution.py:33

commit v14 on v11

v14 whole, which is shorter than its diff:
```python
import functools

import jax
import jax.numpy as jnp
from jax import lax
from jax.experimental import pallas as pl
from jax.experimental.pallas import tpu as pltpu
from jax.sharding import PartitionSpec as P

GROUPS = 32
TAIL = 2
F32, BF16 = jnp.float32, jnp.bfloat16


def vmem_params():
    return pltpu.CompilerParams(vmem_limit_bytes=32 << 20)


def shaped(shape, dtype=BF16):
    return jax.ShapeDtypeStruct(tuple(shape), dtype)


def in_hbm(value):
    return pltpu.with_memory_space_constraint(value, pltpu.HBM)


VMEM = pl.BlockSpec(memory_space=pltpu.VMEM)
ANYWHERE = pl.BlockSpec(memory_space=pl.ANY)


def traded(value, axis, mask):
    return lax.ppermute(value, axis, [(i, i ^ mask) for i in range(lax.axis_size(axis))])


def shifted(value, axis, step):
    peers = lax.axis_size(axis)
    return lax.ppermute(value, axis, [(i, (i + step) % peers) for i in range(peers)])


def stats_table(copies):
    return lax.all_to_all(copies, ("tm", "space"), 0, 0, tiled=True)


def corner_rows(before, after):
    before, after = lax.optimization_barrier((before, after))
    return before, row_halo(edges_of(before)), after


def row_halo(edges):
    if lax.axis_size("space") == 2:
        return [traded(edges, "space", 1)]
    return [shifted(edges[:, 1:], "space", 1), shifted(edges[:, :1], "space", -1)]


def edges_of(frames):
    rows = frames.shape[1]
    if lax.axis_size("space") == 2:
        return lax.dynamic_slice_in_dim(frames, (rows - 1) * (1 - lax.axis_index("space")), 1, axis=1)
    return jnp.concatenate([frames[:, :1], frames[:, rows - 1 :]], axis=1)


def edge_shape(frames, count):
    return (count, 1 if lax.axis_size("space") == 2 else 2) + frames.shape[2:]


def send_rows(source, frame, edges, at=0):
    rows = source.shape[1]
    if edges.shape[1] == 1:
        low = lax.axis_index("space") == 0
        edges[at + frame, 0] = jnp.where(low, source[frame, rows - 1], source[frame, 0])
    else:
        edges[at + frame, 0] = source[frame, 0]
        edges[at + frame, 1] = source[frame, rows - 1]


def add_stats(sums, values):
    width = values.shape[1]
    return (
        sums[0] + jnp.sum(values.reshape(-1, 8, width), axis=0),
        sums[1] + jnp.sum((values * values).reshape(-1, 8, width), axis=0),
    )


def no_stats(width):
    return jnp.zeros((8, width), F32), jnp.zeros((8, width), F32)


def store_stats(stats, sums):
    width = sums[0].shape[1]
    for k in range(2):
        stats[:, k * width : (k + 1) * width] = jnp.sum(sums[k], axis=0, keepdims=True)


def store_copies(copies, stats):
    copies[...] = jnp.broadcast_to(stats[...][None], copies.shape)


def device_count():
    return lax.axis_size("tm") * lax.axis_size("space")


def entry_kernel(feats_hbm, frames, tail, edges, copies, mark, stats, sems):
    n_frames, n_rows, _, width = frames.shape
    loads = [pltpu.make_async_copy(feats_hbm.at[f], frames.at[f], sems.at[f]) for f in range(n_frames)]
    for copy in loads:
        copy.start()
    mark[...] = jnp.zeros_like(mark)
    sums = no_stats(width)
    for frame in range(n_frames):
        loads[frame].wait()
        for row in range(n_rows):
            if frame >= n_frames - TAIL:
                tail[frame - n_frames + TAIL, row] = frames[frame, row]
            sums = add_stats(sums, frames[frame, row].astype(F32))
        send_rows(frames, frame, edges)
    store_stats(stats, sums)
    store_copies(copies, stats)


def copies_shape(width):
    return shaped((device_count(), 1, 2 * width), F32)


MARK = jax.ShapeDtypeStruct((8, 128), F32)


def entry_call(feats):
    n_frames, width = feats.shape[0], feats.shape[3]
    outs = [
        shaped(feats.shape),
        shaped((TAIL,) + feats.shape[1:]),
        shaped(edge_shape(feats, n_frames)),
        copies_shape(width),
        MARK,
    ]
    return pl.pallas_call(
        entry_kernel,
        out_shape=outs,
        in_specs=[ANYWHERE],
        out_specs=[VMEM] * len(outs),
        scratch_shapes=[pltpu.VMEM((1, 2 * width), F32), pltpu.SemaphoreType.DMA((n_frames,))],
        compiler_params=vmem_params(),
        cost_estimate=pl.CostEstimate(flops=4 * feats.size, bytes_accessed=4 * feats.size, transcendentals=0),
    )(in_hbm(feats))


def passed_kernel(before, after):
    after[...] = before[...]


def passed(mark):
    return pl.pallas_call(
        passed_kernel,
        out_shape=MARK,
        in_specs=[VMEM],
        out_specs=VMEM,
        compiler_params=vmem_params(),
        cost_estimate=pl.CostEstimate(flops=1 << 32, bytes_accessed=8192, transcendentals=0),
    )(mark)


def setup_kernel(slabs, per_slab, clips_hbm, *refs):
    params_hbm, (_, aux, params, clips, sems) = refs[:4], refs[4:]
    width = aux.shape[1]
    clip_load = pltpu.make_async_copy(clips_hbm, clips, sems.at[0])
    param_loads = [pltpu.make_async_copy(p, params.at[k], sems.at[1 + k]) for k, p in enumerate(params_hbm)]
    for copy in [clip_load, *param_loads]:
        copy.start()
    clip_load.wait()
    own = lax.axis_index("tm")
    own_clip = clips[own]
    slabs_in = jnp.int32(0)
    for slab in range(slabs):
        same = (clips[slab] == own_clip).astype(jnp.int32)
        slabs_in = slabs_in + same
        aux[slab : slab + 1] = jnp.full((1, width), same.astype(F32), F32)
    starting = jnp.logical_or(own == 0, clips[jnp.maximum(own - 1, 0)] != own_clip)
    aux[slabs : slabs + 1] = jnp.full((1, width), starting.astype(F32), F32)
    aux[slabs + 1 : slabs + 2] = jnp.full((1, width), slabs_in.astype(F32) * float(per_slab), F32)
    for k, copy in enumerate(param_loads):
        copy.wait()
        aux[slabs + 2 + k : slabs + 3 + k] = params[k]
    aux[slabs + 6 : slabs + 8] = jnp.zeros((2, width), F32)


def setup_call(clip_ids, params, per_slab, mark):
    slabs, width = lax.axis_size("tm"), params[0].shape[0]
    return pl.pallas_call(
        functools.partial(setup_kernel, slabs, per_slab),
        out_shape=shaped((slabs + 8, width), F32),
        in_specs=[ANYWHERE] * 5 + [VMEM],
        out_specs=VMEM,
        scratch_shapes=[
            pltpu.VMEM((4, 1, width), F32),
            pltpu.SMEM(clip_ids.shape, jnp.int32),
            pltpu.SemaphoreType.DMA((5,)),
        ],
        compiler_params=vmem_params(),
        cost_estimate=pl.CostEstimate(flops=1 << 30, bytes_accessed=1 << 16, transcendentals=0),
    )(*[in_hbm(x) for x in (clip_ids, *[p[None] for p in params])], mark)


def group_total(values):
    width = values.shape[-1]
    lane = lax.broadcasted_iota(jnp.int32, values.shape, 1)
    step = 1
    while step < width // GROUPS:
        upper = pltpu.roll(values, step, 1)
        lower = pltpu.roll(values, width - step, 1)
        values = values + jnp.where((lane & step) != 0, upper, lower)
        step *= 2
    return values


def half_affine(table, aux, which):
    width = aux.shape[1]
    slabs = aux.shape[0] - 8
    places = table.shape[0] // slabs
    sums = []
    for k in range(2):
        parts = [
            aux[slab : slab + 1] * sum(table[slab * places + p, :, k * width : (k + 1) * width] for p in range(places))
            for slab in range(slabs)
        ]
        while len(parts) > 1:
            parts = [sum(parts[i : i + 2]) for i in range(0, len(parts), 2)]
        sums += parts
    grouped = group_total(jnp.concatenate(sums, axis=0))
    count = aux[slabs + 1 : slabs + 2]
    gain = aux[slabs + 2 + 2 * which : slabs + 3 + 2 * which]
    shift = aux[slabs + 3 + 2 * which : slabs + 4 + 2 * which]
    mean = grouped[0:1] / count
    variance = grouped[1:2] / count - mean * mean
    scale = lax.rsqrt(variance + 1e-06) * gain
    return 0.5 * scale, 0.5 * (shift - mean * scale)


def normed(raw, affine):
    half = raw.astype(F32) * affine[0] + affine[1]
    return (half * jnp.tanh(half) + half).astype(BF16)


def extended_row(frames, sides, frame, row):
    n_rows = frames.shape[1]
    inner = frames[frame, min(max(row - 1, 0), n_rows - 1)]
    if 0 < row <= n_rows:
        return inner
    place, places = lax.axis_index("space"), lax.axis_size("space")
    side = sides[0 if row == 0 else -1]
    return jnp.where(place == (0 if row == 0 else places - 1), inner, side[frame, 0])


def conv_rows(planes, taps, loads=None):
    ref, index = planes[0]
    n_rows, cols, width = ref.shape[1] - 2, ref.shape[2], ref.shape[3]
    lhs = jnp.concatenate(
        [ref[index, j : j + n_rows].reshape(n_rows * cols, width) for ref, index in planes for j in range(3)], axis=1
    )
    column = lax.broadcasted_iota(jnp.int32, (cols, width), 0)
    sums = []
    for l in range(3):
        if loads is not None:
            loads[l].wait()
        rhs = jnp.concatenate([taps[i, j, l] for i in range(3) for j in range(3)], axis=0)
        sums.append(jnp.dot(lhs, rhs, preferred_element_type=F32))
    for row in range(n_rows):
        left, mid, right = (s[row * cols : (row + 1) * cols] for s in sums)
        left = jnp.where(column == 0, left, pltpu.roll(left, 1, 0))
        right = jnp.where(column == cols - 1, right, pltpu.roll(right, cols - 1, 0))
        yield row, left + mid + right


def put_hidden(hidden, frame, row, value, sums):
    rounded = value.astype(BF16)
    hidden[frame, row] = rounded
    return add_stats(sums, rounded.astype(F32))


def late_kernel(n_sides, which, aux, table, _, frames, *refs):
    early_sides, late_sides, kernel_hbm = refs[:n_sides], refs[n_sides : 2 * n_sides], refs[2 * n_sides]
    if which == 0:
        act_low, affine_out, taps, hidden, stats, edges, act_high, taps_sems = refs[2 * n_sides + 1 :]
        early = late = frames
        late_first = 0
    else:
        late, feats, act_low, affine_out, taps, out_hbm, act_high, taps_sems, out, sems = refs[2 * n_sides + 1 :]
        early, late_first = frames, frames.shape[0]
    loads = [pltpu.make_async_copy(kernel_hbm.at[:, :, l], taps.at[:, :, l], taps_sems.at[l]) for l in range(3)]
    for copy in loads:
        copy.start()
    n_rows, width = frames.shape[1], frames.shape[3]
    low, high = act_low.shape[0], act_high.shape[0]
    affine = half_affine(table, aux, which)
    for k in range(2):
        affine_out[k : k + 1] = affine[k]
    planes = [(act_low, f) for f in range(low)] + [(act_high, f) for f in range(high)]
    for frame, (act, index) in enumerate(planes):
        for row in range(n_rows + 2):
            if which == 0 or frame < 2:
                value = extended_row(early, early_sides, frame, row)
            else:
                value = extended_row(late, late_sides, frame - late_first, row)
            act[index, row] = normed(value, affine)
    sums = no_stats(width)
    stores = []
    for frame in range(high):
        for row, value in conv_rows(planes[frame : frame + 3], taps, loads if frame == 0 else None):
            if which == 0:
                sums = put_hidden(hidden, frame, row, value, sums)
            else:
                out[frame, row] = feats[low + frame, row].astype(F32) + value
        if which == 0:
            send_rows(hidden, frame, edges)
        else:
            stores.append(pltpu.make_async_copy(out.at[frame], out_hbm.at[low + frame], sems.at[frame]))
            stores[-1].start()
    if which == 0:
        for k in range(2):
            stats[k] = sums[k]
    for store in stores:
        store.wait()


def early_kernel(n_sides, which, aux, before, *refs):
    corners, (act_low, affine_in, taps), refs = refs[:n_sides], refs[n_sides : n_sides + 3], refs[n_sides + 3 :]
    if which == 0:
        late_stats, hidden, edges, copies, mark, act_before, stats = refs
        mark[...] = jnp.zeros_like(mark)
        sums = late_stats[0], late_stats[1]
    else:
        feats, _, out_hbm, act_before, out, sems = refs
    slabs = aux.shape[0] - 8
    starting = aux[slabs : slabs + 1] != 0.0
    affine = affine_in[0:1], affine_in[1:2]
    for frame in range(2):
        for row in range(act_low.shape[1]):
            value = normed(extended_row(before, corners, frame, row), affine).astype(F32)
            act_before[frame, row] = jnp.where(starting, act_low[0, row].astype(F32), value).astype(BF16)
    planes = [(act_before, 0), (act_before, 1)] + [(act_low, f) for f in range(act_low.shape[0])]
    stores = []
    for frame in range(2):
        for row, value in conv_rows(planes[frame : frame + 3], taps):
            if which == 0:
                sums = put_hidden(hidden, frame, row, value, sums)
            else:
                out[frame, row] = feats[frame, row].astype(F32) + value
        if which == 0:
            send_rows(hidden, frame, edges)
        else:
            stores.append(pltpu.make_async_copy(out.at[frame], out_hbm.at[frame], sems.at[frame]))
            stores[-1].start()
    if which == 0:
        store_stats(stats, sums)
        store_copies(copies, stats)
    for store in stores:
        store.wait()


def call(kernel, outs, scratch, frames, operands, out_specs=None, aliases=None, outside=()):
    return pl.pallas_call(
        kernel,
        out_shape=outs,
        in_specs=[ANYWHERE if k in (aliases or {}) or k in outside else VMEM for k in range(len(operands))],
        out_specs=[VMEM] * len(outs) if out_specs is None else out_specs,
        scratch_shapes=scratch,
        input_output_aliases=aliases or {},
        compiler_params=vmem_params(),
        cost_estimate=pl.CostEstimate(flops=54 * frames * 384 * 65536, bytes_accessed=1 << 20, transcendentals=1 << 20),
    )(*operands)


def on_device(feats, clip_ids, gain_one, shift_one, kernel_one, gain_two, shift_two, kernel_two):
    n_frames, n_rows, cols, width = feats.shape
    params = (gain_one, shift_one, gain_two, shift_two)
    per_slab = feats.size // GROUPS * lax.axis_size("space")
    late = n_frames - 2
    plane = (n_rows + 2, cols, width)
    act = pltpu.VMEM((2,) + plane, BF16)
    act_late = pltpu.VMEM((late,) + plane, BF16)
    late_shapes = [shaped((2,) + plane), shaped((2, width), F32), shaped(kernel_one.shape)]
    hidden_shapes = [shaped((late, n_rows, cols, width)), shaped((2, 8, width), F32), shaped(edge_shape(feats, late))]
    taps_sems = pltpu.SemaphoreType.DMA((3,))

    frames, tail, edges, copies, mark = entry_call(feats)
    table = stats_table(copies)
    tail, edges, mark = lax.optimization_barrier((tail, edges, passed(mark)))
    before = shifted(tail, "tm", 1)
    sides = row_halo(edges)
    n_sides = len(sides)
    aux = setup_call(clip_ids, params, per_slab, mark)
    operands = [aux, table, mark, frames, *sides, *sides, in_hbm(kernel_one)]
    act_low, affine, taps, hidden_late, stats, edges_late = call(
        functools.partial(late_kernel, n_sides, 0),
        late_shapes + hidden_shapes,
        [act_late, taps_sems],
        late,
        operands,
        outside=(len(operands) - 1,),
    )
    before, corners, affine = corner_rows(before, affine)
    hidden_early, edges, copies, mark = call(
        functools.partial(early_kernel, n_sides, 0),
        [shaped((2, n_rows, cols, width)), shaped(edge_shape(feats, 2)), copies_shape(width), MARK],
        [act, pltpu.VMEM((1, 2 * width), F32)],
        2,
        [aux, before, *corners, act_low, affine, taps, stats],
    )

    table = stats_table(copies)
    tail, edges, edges_late, mark = lax.optimization_barrier((hidden_late[late - 2 :], edges, edges_late, passed(mark)))
    before = shifted(tail, "tm", 1)
    operands = [aux, table, mark, hidden_early, *row_halo(edges), *row_halo(edges_late), in_hbm(kernel_two), hidden_late, frames]
    act_low, affine, taps, out = call(
        functools.partial(late_kernel, n_sides, 1),
        late_shapes + [shaped(feats.shape, F32)],
        [act_late, taps_sems, pltpu.VMEM((late, n_rows, cols, width), F32), pltpu.SemaphoreType.DMA((late,))],
        late,
        operands,
        out_specs=[VMEM, VMEM, VMEM, ANYWHERE],
        outside=(len(operands) - 3,),
    )
    before, corners, affine = corner_rows(before, affine)
    operands = [aux, before, *corners, act_low, affine, taps, frames, out]
    return call(
        functools.partial(early_kernel, n_sides, 1),
        shaped(feats.shape, F32),
        [act, pltpu.VMEM((2, n_rows, cols, width), F32), pltpu.SemaphoreType.DMA((2,))],
        2,
        operands,
        out_specs=ANYWHERE,
        aliases={len(operands) - 1: 0},
    )


def solution(mesh):
    return jax.shard_map(
        on_device,
        mesh=mesh,
        in_specs=(P("tm", "space", None, None), P(), P(), P(), P(), P(), P(), P()),
        out_specs=P("tm", "space", None, None),
        check_vma=False,
    )
```

time: 70 us -> 58.3 us (0.83)
  Pallas kernels: 32.6 us -> 21.9 us
  local copies, waits for them, and re-layouts: 9.29 us -> 0.03 us
  waiting for transfers between devices: 13.2 us -> 21.4 us
    pallas_call x7 -> x8, Pallas kernels: 32.6 us -> 21.9 us  [the longest x4 19.2 us: call(): pl.pallas_call(kernel, out_shape=outs, in_specs=[ANYWHERE if k in (aliase...]
    unnamed x12 -> x0, local copies, waits for them, and re-layouts: 9.26 us -> none
    all_to_all x2, waiting for transfers between devices: 10.6 us -> 17.7 us  [stats_table(): return lax.all_to_all(copies, ('tm', 'space'), 0, 0, tiled=True)]
    ppermute x4 -> x5, waiting for transfers between devices: 2.58 us -> 3.62 us  [traded(): lax.ppermute(value, axis, [(i, i ^ mask) for i in range(lax.axis_size(axi...]
  transfers between devices with their start and end apart: 8 -> 9, of which waited for: 4 -> 6; matrix products, arithmetic and copies ran while one was open for 0% -> 0% of each run, Pallas kernels for 17% -> 22%
where the time goes in v14:
time: 58.3 us; the launch traced here: 58.1 us
  Pallas kernels  21.9 us (38%)
  waiting for transfers between devices  21.4 us (37%)
  starting transfers between devices  14.7 us (25%)
    pallas_call x4, Pallas kernels, call(): pl.pallas_call(kernel, out_shape=outs, in_specs=[ANYWHERE if k in (aliase...  19.2 us
    all_to_all x2, waiting for transfers between devices, stats_table(): return lax.all_to_all(copies, ('tm', 'space'), 0, 0, tiled=True)  17.7 us
    all_to_all x2, starting transfers between devices, stats_table(): return lax.all_to_all(copies, ('tm', 'space'), 0, 0, tiled=True)  10.6 us
    ppermute x5, waiting for transfers between devices, traded(): lax.ppermute(value, axis, [(i, i ^ mask) for i in range(lax.axis_size(axi...  3.62 us
    ppermute x2, starting transfers between devices, shifted(): lax.ppermute(value, axis, [(i, (i + step) % peers) for i in range(peers)])  2.9 us
    pallas_call x1, Pallas kernels, entry_call(): pl.pallas_call(entry_kernel, out_shape=outs, in_specs=[ANYWHERE], out_spe...  1.95 us
    ppermute x5, starting transfers between devices, traded(): lax.ppermute(value, axis, [(i, i ^ mask) for i in range(lax.axis_size(axi...  1.24 us
  transfers between devices with their start and end apart: 9, of which 6 were waited for; matrix products, arithmetic and copies ran while one was open for 0% of the time, Pallas kernels for 22%

profile of v14, /device:TPU:0, one launch (start us, length us, event | category | flops | bytes accessed | tf_op | source)
XLA Modules:
  0.0 58.1 jit_solution(1394880028349216493)
XLA Ops:
  0.0 1.9 %shard_map.82 = (bf16[4,4,96,256]{3,2,1,0:T(8,128)(2,1)S(1)}, bf16[2,4,96,256]{3,2,1,0:T(8,128)(2,1)S(1)}, bf16[4,1,96,256]{3,2,1,0:T(8,128)(2,1)S(1)}, f32[32,1,512]{2,1,0:T(1,128)}, f32[8,128]{1,0:T(8,128)S(1)}) custom-call(bf16[4,4,96,256]{3,2,1,0:T(8,128)(2,1)} %feats_hbm.1), custom_call_target="tpu_custom_call" | custom-call | flops 1572864 | bytes 1572864 | tf_op jit(solution)/shard_map/pallas_call | solution.py:136
  2.0 0.5 collective-permute-start
  2.5 2.6 %collective-permute-start.1 = (bf16[2,4,96,256]{3,2,1,0:T(8,128)(2,1)S(1)}, bf16[2,4,96,256]{3,2,1,0:T(8,128)(2,1)S(1)}, u32[]{:S(2)}, u32[]{:S(2)}) collective-permute-start(bf16[2,4,96,256]{3,2,1,0:T(8,128)(2,1)S(1)} %get-tuple-element.43), channel_id=1, source_target_pairs={{0,2},{2,4},{4,6},{6,8},{8,10},{10,12},{12,14},{14,16},{16,18},{18... | collective-permute-start | bytes 1179656 | tf_op jit(solution)/shard_map/ppermute | solution.py:37
  5.0 4.9 %all-to-all-start = ((f32[32,1,512]{2,1,0:T(1,128)}), f32[32,1,512]{2,1,0:T(1,128)S(1)}, u32[]{:S(2)}, u32[]{:S(2)}) async-start(f32[32,1,512]{2,1,0:T(1,128)} %get-tuple-element.39), calls=%async_computation | async-start | bytes 131072 | tf_op jit(solution)/shard_map/all_to_all | solution.py:41
  10.0 0.8 %shard_map.84.aux = f32[24,256]{1,0:T(8,128)S(1)} custom-call(s32[16]{0:T(128)} %clips_hbm.1, f32[1,256]{1,0:T(1,128)} %bitcast.4, f32[1,256]{1,0:T(1,128)} %bitcast.5, f32[1,256]{1,0:T(1,128)} %bitcast.6, f32[1,256]{1,0:T(1,128)} %bitcast.7, f32[8,128]{1,0:T(8,128)S(1)} %shard_map.83.refs_4_._), custom_call_target="tpu_custom_call" | custom-call | flops 1073741824 | bytes 65536 | tf_op jit(solution)/shard_map/pallas_call | solution.py:188
  10.8 9.3 %all-to-all-done.table = f32[32,1,512]{2,1,0:T(1,128)S(1)} async-done(((f32[32,1,512]{2,1,0:T(1,128)}), f32[32,1,512]{2,1,0:T(1,128)S(1)}, u32[]{:S(2)}, u32[]{:S(2)}) %all-to-all-start) | async-done | bytes 65568 | tf_op jit(solution)/shard_map/all_to_all | solution.py:41
  20.1 0.0 collective-permute-done.refs_0_.refs_1_
  20.1 5.5 %shard_map.85 = (bf16[2,6,96,256]{3,2,1,0:T(8,128)(2,1)S(1)}, f32[2,256]{1,0:T(2,128)S(1)}, bf16[3,3,3,256,256]{4,3,2,1,0:T(8,128)(2,1)S(1)}, bf16[2,4,96,256]{3...) custom-call(f32[24,256]{1,0:T(8,128)S(1)} %shard_map.84.aux, ...), custom_call_target="tpu_custom_call" | custom-call | flops 2717908992 | bytes 1048576 | tf_op jit(solution)/shard_map/pallas_call | solution.py:360
  25.6 0.0 collective-permute-done.1.before
  25.6 0.1 collective-permute-start.2
  25.7 1.3 %collective-permute-done.2.refs_0_ = bf16[2,1,96,256]{3,2,1,0:T(8,128)(2,1)S(1)} collective-permute-done((bf16[2,1,96,256]{3,2,1,0:T(8,128)(2,1)S(1)}, bf16[2,1,96,256]{3,2,1,0:T(8,128)(2,1)S(1)}, u32[]{:S(2)}, u32[]{:S(2)}) %collective-permute-start.2) | collective-permute-done | bytes 98336 | tf_op jit(solution)/shard_map/ppermute | solution.py:32
  27.0 3.7 %shard_map.86 = (bf16[2,4,96,256]{3,2,1,0:T(8,128)(2,1)S(1)}, bf16[2,1,96,256]{3,2,1,0:T(8,128)(2,1)S(1)}, f32[32,1,512]{2,1,0:T(1,128)}, f32[8,128]{1,0:T(8,128)S(1)}) custom-call(f32[24,256]{1,0:T(8,128)S(1)} %shard_map.84.aux, bf16[2,4,96,256]{3,2,1,0:T(8,128)(2,1)S(1)} %collective-permute-done.1.before, ...), custom_call_target="tpu_custom_call" | custom-call | flops 2717908992 | bytes 1048576 | tf_op jit(solution)/shard_map/pallas_call | solution.py:360
  30.7 0.3 collective-permute-start.3
  31.0 5.6 %all-to-all-start.1 = ((f32[32,1,512]{2,1,0:T(1,128)}), f32[32,1,512]{2,1,0:T(1,128)S(1)}, u32[]{:S(2)}, u32[]{:S(2)}) async-start(f32[32,1,512]{2,1,0:T(1,128)} %get-tuple-element.54), calls=%async_computation.1 | async-start | bytes 131072 | tf_op jit(solution)/shard_map/all_to_all | solution.py:41
  36.6 0.3 collective-permute-start.4
  37.0 0.3 collective-permute-start.5
  37.2 0.8 %collective-permute-done.4.refs_0_ = bf16[2,1,96,256]{3,2,1,0:T(8,128)(2,1)S(1)} collective-permute-done((bf16[2,1,96,256]{3,2,1,0:T(8,128)(2,1)S(1)}, bf16[2,1,96,256]{3,2,1,0:T(8,128)(2,1)S(1)}, u32[]{:S(2)}, u32[]{:S(2)}) %collective-permute-start.4) | collective-permute-done | bytes 98336 | tf_op jit(solution)/shard_map/ppermute | solution.py:32
  38.0 0.3 collective-permute-done.5.refs_1_
  38.3 8.4 %all-to-all-done.1.table = f32[32,1,512]{2,1,0:T(1,128)S(1)} async-done(((f32[32,1,512]{2,1,0:T(1,128)}), f32[32,1,512]{2,1,0:T(1,128)S(1)}, u32[]{:S(2)}, u32[]{:S(2)}) %all-to-all-start.1) | async-done | bytes 65568 | tf_op jit(solution)/shard_map/all_to_all | solution.py:41
  46.7 6.3 %shard_map.88 = (bf16[2,6,96,256]{3,2,1,0:T(8,128)(2,1)S(1)}, f32[2,256]{1,0:T(2,128)S(1)}, bf16[3,3,3,256,256]{4,3,2,1,0:T(8,128)(2,1)S(1)}, f32[4,4,96,256]{3,2,1,0:T(8,128)}) custom-call(f32[24,256]{1,0:T(8,128)S(1)} %shard_map.84.aux, f32[32,1,512]{2,1,0:T(1,128)S(1)} %all-to-all-done.1.table, f32[8,128]{1,0:T(8,128)S(1)} %shard_map.87._, ...), custom_call_target="tpu_custom_call" | custom-call | flops 2717908992 | bytes 1048576 | tf_op jit(solution)/shard_map/pallas_call | solution.py:360
  53.0 0.0 collective-permute-done.3.before
  53.0 0.1 collective-permute-start.6
  53.1 1.3 %collective-permute-done.6.refs_0_ = bf16[2,1,96,256]{3,2,1,0:T(8,128)(2,1)S(1)} collective-permute-done((bf16[2,1,96,256]{3,2,1,0:T(8,128)(2,1)S(1)}, bf16[2,1,96,256]{3,2,1,0:T(8,128)(2,1)S(1)}, u32[]{:S(2)}, u32[]{:S(2)}) %collective-permute-start.6) | collective-permute-done | bytes 98336 | tf_op jit(solution)/shard_map/ppermute | solution.py:32
  54.4 3.7 %shard_map.89 = f32[4,4,96,256]{3,2,1,0:T(8,128)} custom-call(f32[24,256]{1,0:T(8,128)S(1)} %shard_map.84.aux, bf16[2,4,96,256]{3,2,1,0:T(8,128)(2,1)S(1)} %collective-permute-done.3.before, bf16[2,1,96,256]{3,2,1,0:T(8,128)(2,1)S(1)} %collective-permute-done.6.refs_0_, ...), custom_call_target="tpu_custom_call", output_to_operand_aliasing={{}: (7, {})} | custom-call | flops 2717908992 | bytes 1048576 | tf_op jit(solution)/shard_map/pallas_call | solution.py:360
  (4 shorter events, 0.0 us)
Async XLA Ops:
  2.0 18.1 %collective-permute-start = (bf16[4,1,96,256]{3,2,1,0:T(8,128)(2,1)S(1)}, bf16[4,1,96,256]{3,2,1,0:T(8,128)(2,1)S(1)}, u32[]{:S(2)}, u32[]{:S(2)}) collective-permute-start(bf16[4,1,96,256]{3,2,1,0:T(8,128)(2,1)S(1)} %get-tuple-element.41), channel_id=1, source_target_pairs={{0,1},{1,0},{2,3},{3,2},{4,5},{5,4},{6,7},{7,6},{8,9},{9,8},{10,11... | collective-permute-start | bytes 589832 | tf_op jit(solution)/shard_map/ppermute | solution.py:32
  2.5 23.1 %collective-permute-start.1 = (bf16[2,4,96,256]{3,2,1,0:T(8,128)(2,1)S(1)}, bf16[2,4,96,256]{3,2,1,0:T(8,128)(2,1)S(1)}, u32[]{:S(2)}, u32[]{:S(2)}) collective-permute-start(bf16[2,4,96,256]{3,2,1,0:T(8,128)(2,1)S(1)} %get-tuple-element.43), channel_id=1, source_target_pairs={{0,2},{2,4},{4,6},{6,8},{8,10},{10,12},{12,14},{14,16},{16,18},{18... | collective-permute-start | bytes 1179656 | tf_op jit(solution)/shard_map/ppermute | solution.py:37
  5.0 15.0 %all-to-all-start = ((f32[32,1,512]{2,1,0:T(1,128)}), f32[32,1,512]{2,1,0:T(1,128)S(1)}, u32[]{:S(2)}, u32[]{:S(2)}) async-start(f32[32,1,512]{2,1,0:T(1,128)} %get-tuple-element.39), calls=%async_computation | async-start | bytes 131072 | tf_op jit(solution)/shard_map/all_to_all | solution.py:41
  25.6 1.4 %collective-permute-start.2 = (bf16[2,1,96,256]{3,2,1,0:T(8,128)(2,1)S(1)}, bf16[2,1,96,256]{3,2,1,0:T(8,128)(2,1)S(1)}, u32[]{:S(2)}, u32[]{:S(2)}) collective-permute-start(bf16[2,1,96,256]{3,2,1,0:T(8,128)(2,1)S(1)} %constant_dynamic-slice_fusion.1), channel_id=1, source_target_pairs={{0,1},{1,0},{2,3},{3,2},{4,5},{5,4},{6,7},{7,6},{8,9},{9,8},{10,11... | collective-permute-start | bytes 294920 | tf_op jit(solution)/shard_map/ppermute | solution.py:32
  30.7 22.3 %collective-permute-start.3 = (bf16[2,4,96,256]{3,2,1,0:T(8,128)(2,1)S(1)}, bf16[2,4,96,256]{3,2,1,0:T(8,128)(2,1)S(1)}, u32[]{:S(2)}, u32[]{:S(2)}) collective-permute-start(bf16[2,4,96,256]{3,2,1,0:T(8,128)(2,1)S(1)} %get-tuple-element.53.refs_3_), channel_id=1, source_target_pairs={{0,2},{2,4},{4,6},{6,8},{8,10},{10,12},{12,14},{14,16},{16,18},{18... | collective-permute-start | bytes 1179656 | tf_op jit(solution)/shard_map/ppermute | solution.py:37
  31.0 15.7 %all-to-all-start.1 = ((f32[32,1,512]{2,1,0:T(1,128)}), f32[32,1,512]{2,1,0:T(1,128)S(1)}, u32[]{:S(2)}, u32[]{:S(2)}) async-start(f32[32,1,512]{2,1,0:T(1,128)} %get-tuple-element.54), calls=%async_computation.1 | async-start | bytes 131072 | tf_op jit(solution)/shard_map/all_to_all | solution.py:41
  36.6 1.4 %collective-permute-start.4 = (bf16[2,1,96,256]{3,2,1,0:T(8,128)(2,1)S(1)}, bf16[2,1,96,256]{3,2,1,0:T(8,128)(2,1)S(1)}, u32[]{:S(2)}, u32[]{:S(2)}) collective-permute-start(bf16[2,1,96,256]{3,2,1,0:T(8,128)(2,1)S(1)} %get-tuple-element.57), channel_id=1, source_target_pairs={{0,1},{1,0},{2,3},{3,2},{4,5},{5,4},{6,7},{7,6},{8,9},{9,8},{10,11... | collective-permute-start | bytes 294920 | tf_op jit(solution)/shard_map/ppermute | solution.py:32
  37.0 1.3 %collective-permute-start.5 = (bf16[2,1,96,256]{3,2,1,0:T(8,128)(2,1)S(1)}, bf16[2,1,96,256]{3,2,1,0:T(8,128)(2,1)S(1)}, u32[]{:S(2)}, u32[]{:S(2)}) collective-permute-start(bf16[2,1,96,256]{3,2,1,0:T(8,128)(2,1)S(1)} %get-tuple-element.58), channel_id=1, source_target_pairs={{0,1},{1,0},{2,3},{3,2},{4,5},{5,4},{6,7},{7,6},{8,9},{9,8},{10,11... | collective-permute-start | bytes 294920 | tf_op jit(solution)/shard_map/ppermute | solution.py:32
  53.0 1.4 %collective-permute-start.6 = (bf16[2,1,96,256]{3,2,1,0:T(8,128)(2,1)S(1)}, bf16[2,1,96,256]{3,2,1,0:T(8,128)(2,1)S(1)}, u32[]{:S(2)}, u32[]{:S(2)}) collective-permute-start(bf16[2,1,96,256]{3,2,1,0:T(8,128)(2,1)S(1)} %constant_dynamic-slice_fusion), channel_id=1, source_target_pairs={{0,1},{1,0},{2,3},{3,2},{4,5},{5,4},{6,7},{7,6},{8,9},{9,8},{10,11... | collective-permute-start | bytes 294920 | tf_op jit(solution)/shard_map/ppermute | solution.py:32

commit v15 on v14

--- a/solution.py
+++ b/solution.py
@@ -142,21 +142,6 @@
         compiler_params=vmem_params(),
         cost_estimate=pl.CostEstimate(flops=4 * feats.size, bytes_accessed=4 * feats.size, transcendentals=0),
     )(in_hbm(feats))
-
-
-def passed_kernel(before, after):
-    after[...] = before[...]
-
-
-def passed(mark):
-    return pl.pallas_call(
-        passed_kernel,
-        out_shape=MARK,
-        in_specs=[VMEM],
-        out_specs=VMEM,
-        compiler_params=vmem_params(),
-        cost_estimate=pl.CostEstimate(flops=1 << 32, bytes_accessed=8192, transcendentals=0),
-    )(mark)
 
 
 def setup_kernel(slabs, per_slab, clips_hbm, *refs):
@@ -250,7 +235,7 @@
     return jnp.where(place == (0 if row == 0 else places - 1), inner, side[frame, 0])
 
 
-def conv_rows(planes, taps, loads=None):
+def conv_rows(planes, taps):
     ref, index = planes[0]
     n_rows, cols, width = ref.shape[1] - 2, ref.shape[2], ref.shape[3]
     lhs = jnp.concatenate(
@@ -259,8 +244,6 @@
     column = lax.broadcasted_iota(jnp.int32, (cols, width), 0)
     sums = []
     for l in range(3):
-        if loads is not None:
-            loads[l].wait()
         rhs = jnp.concatenate([taps[i, j, l] for i in range(3) for j in range(3)], axis=0)
         sums.append(jnp.dot(lhs, rhs, preferred_element_type=F32))
     for row in range(n_rows):
@@ -276,7 +259,7 @@
     return add_stats(sums, rounded.astype(F32))
 
 
-def late_kernel(n_sides, which, aux, table, _, frames, *refs):
+def late_kernel(n_sides, which, aux, table, frames, *refs):
     early_sides, late_sides, kernel_hbm = refs[:n_sides], refs[n_sides : 2 * n_sides], refs[2 * n_sides]
     if which == 0:
         act_low, affine_out, taps, hidden, stats, edges, act_high, taps_sems = refs[2 * n_sides + 1 :]
@@ -285,7 +268,9 @@
     else:
         late, feats, act_low, affine_out, taps, out_hbm, act_high, taps_sems, out, sems = refs[2 * n_sides + 1 :]
         early, late_first = frames, frames.shape[0]
-    loads = [pltpu.make_async_copy(kernel_hbm.at[:, :, l], taps.at[:, :, l], taps_sems.at[l]) for l in range(3)]
+    loads = [
+        pltpu.make_async_copy(kernel_hbm.at[i, j], taps.at[i, j], taps_sems.at[3 * i + j]) for i in range(3) for j in range(3)
+    ]
     for copy in loads:
         copy.start()
     n_rows, width = frames.shape[1], frames.shape[3]
@@ -303,8 +288,10 @@
             act[index, row] = normed(value, affine)
     sums = no_stats(width)
     stores = []
+    for copy in loads:
+        copy.wait()
     for frame in range(high):
-        for row, value in conv_rows(planes[frame : frame + 3], taps, loads if frame == 0 else None):
+        for row, value in conv_rows(planes[frame : frame + 3], taps):
             if which == 0:
                 sums = put_hidden(hidden, frame, row, value, sums)
             else:
@@ -324,8 +311,7 @@
 def early_kernel(n_sides, which, aux, before, *refs):
     corners, (act_low, affine_in, taps), refs = refs[:n_sides], refs[n_sides : n_sides + 3], refs[n_sides + 3 :]
     if which == 0:
-        late_stats, hidden, edges, copies, mark, act_before, stats = refs
-        mark[...] = jnp.zeros_like(mark)
+        late_stats, hidden, edges, copies, act_before, stats = refs
         sums = late_stats[0], late_stats[1]
     else:
         feats, _, out_hbm, act_before, out, sems = refs
@@ -356,7 +342,7 @@
         store.wait()
 
 
-def call(kernel, outs, scratch, frames, operands, out_specs=None, aliases=None, outside=()):
+def call(kernel, outs, scratch, weight, operands, out_specs=None, aliases=None, outside=()):
     return pl.pallas_call(
         kernel,
         out_shape=outs,
@@ -365,7 +351,7 @@
         scratch_shapes=scratch,
         input_output_aliases=aliases or {},
         compiler_params=vmem_params(),
-        cost_estimate=pl.CostEstimate(flops=54 * frames * 384 * 65536, bytes_accessed=1 << 20, transcendentals=1 << 20),
+        cost_estimate=pl.CostEstimate(flops=weight << 32, bytes_accessed=1 << 20, transcendentals=1 << 20),
     )(*operands)
 
 
@@ -379,42 +365,40 @@
     act_late = pltpu.VMEM((late,) + plane, BF16)
     late_shapes = [shaped((2,) + plane), shaped((2, width), F32), shaped(kernel_one.shape)]
     hidden_shapes = [shaped((late, n_rows, cols, width)), shaped((2, 8, width), F32), shaped(edge_shape(feats, late))]
-    taps_sems = pltpu.SemaphoreType.DMA((3,))
+    taps_sems = pltpu.SemaphoreType.DMA((9,))
 
     frames, tail, edges, copies, mark = entry_call(feats)
     table = stats_table(copies)
-    tail, edges, mark = lax.optimization_barrier((tail, edges, passed(mark)))
     before = shifted(tail, "tm", 1)
     sides = row_halo(edges)
     n_sides = len(sides)
     aux = setup_call(clip_ids, params, per_slab, mark)
-    operands = [aux, table, mark, frames, *sides, *sides, in_hbm(kernel_one)]
+    operands = [aux, table, frames, *sides, *sides, in_hbm(kernel_one)]
     act_low, affine, taps, hidden_late, stats, edges_late = call(
         functools.partial(late_kernel, n_sides, 0),
         late_shapes + hidden_shapes,
         [act_late, taps_sems],
-        late,
+        32,
         operands,
         outside=(len(operands) - 1,),
     )
     before, corners, affine = corner_rows(before, affine)
-    hidden_early, edges, copies, mark = call(
+    hidden_early, edges, copies = call(
         functools.partial(early_kernel, n_sides, 0),
-        [shaped((2, n_rows, cols, width)), shaped(edge_shape(feats, 2)), copies_shape(width), MARK],
+        [shaped((2, n_rows, cols, width)), shaped(edge_shape(feats, 2)), copies_shape(width)],
         [act, pltpu.VMEM((1, 2 * width), F32)],
         2,
         [aux, before, *corners, act_low, affine, taps, stats],
     )
 
     table = stats_table(copies)
-    tail, edges, edges_late, mark = lax.optimization_barrier((hidden_late[late - 2 :], edges, edges_late, passed(mark)))
-    before = shifted(tail, "tm", 1)
-    operands = [aux, table, mark, hidden_early, *row_halo(edges), *row_halo(edges_late), in_hbm(kernel_two), hidden_late, frames]
+    before = shifted(hidden_late[late - 2 :], "tm", 1)
+    operands = [aux, table, hidden_early, *row_halo(edges), *row_halo(edges_late), in_hbm(kernel_two), hidden_late, frames]
     act_low, affine, taps, out = call(
         functools.partial(late_kernel, n_sides, 1),
         late_shapes + [shaped(feats.shape, F32)],
         [act_late, taps_sems, pltpu.VMEM((late, n_rows, cols, width), F32), pltpu.SemaphoreType.DMA((late,))],
-        late,
+        32,
         operands,
         out_specs=[VMEM, VMEM, VMEM, ANYWHERE],
         outside=(len(operands) - 3,),

time: 58.3 us -> 54.5 us (0.935)
  waiting for transfers between devices: 21.4 us -> 19 us
  Pallas kernels: 21.9 us -> 21 us
    all_to_all x2, waiting for transfers between devices: 17.7 us -> 10.5 us  [stats_table(): return lax.all_to_all(copies, ('tm', 'space'), 0, 0, tiled=True)]
    ppermute x2, waiting for transfers between devices: 0.01 us -> 5.9 us  [shifted(): lax.ppermute(value, axis, [(i, (i + step) % peers) for i in range(peers)])]
    ppermute x5, waiting for transfers between devices: 3.62 us -> 2.58 us  [traded(): lax.ppermute(value, axis, [(i, i ^ mask) for i in range(lax.axis_size(axi...]
    all_to_all x2, starting transfers between devices: 10.6 us -> 9.53 us  [stats_table(): return lax.all_to_all(copies, ('tm', 'space'), 0, 0, tiled=True)]
    pallas_call x4, Pallas kernels: 19.2 us -> 18.3 us  [call(): pl.pallas_call(kernel, out_shape=outs, in_specs=[ANYWHERE if k in (aliase...]
  transfers between devices with their start and end apart: 9 -> 9, of which waited for: 6 -> 6; matrix products, arithmetic and copies ran while one was open for 0% -> 0% of each run, Pallas kernels for 22% -> 21%
where the time goes in v15:
time: 54.5 us; the launch traced here: 54.3 us
  Pallas kernels  21 us (39%)
  waiting for transfers between devices  19 us (35%)
  starting transfers between devices  14.2 us (26%)
    pallas_call x4, Pallas kernels, call(): pl.pallas_call(kernel, out_shape=outs, in_specs=[ANYWHERE if k in (aliase...  18.3 us
    all_to_all x2, waiting for transfers between devices, stats_table(): return lax.all_to_all(copies, ('tm', 'space'), 0, 0, tiled=True)  10.5 us
    all_to_all x2, starting transfers between devices, stats_table(): return lax.all_to_all(copies, ('tm', 'space'), 0, 0, tiled=True)  9.53 us
    ppermute x2, waiting for transfers between devices, shifted(): lax.ppermute(value, axis, [(i, (i + step) % peers) for i in range(peers)])  5.9 us
    ppermute x2, starting transfers between devices, shifted(): lax.ppermute(value, axis, [(i, (i + step) % peers) for i in range(peers)])  3.46 us
    ppermute x5, waiting for transfers between devices, traded(): lax.ppermute(value, axis, [(i, i ^ mask) for i in range(lax.axis_size(axi...  2.58 us
    pallas_call x1, Pallas kernels, entry_call(): pl.pallas_call(entry_kernel, out_shape=outs, in_specs=[ANYWHERE], out_spe...  1.95 us
    ppermute x5, starting transfers between devices, traded(): lax.ppermute(value, axis, [(i, i ^ mask) for i in range(lax.axis_size(axi...  1.24 us
  transfers between devices with their start and end apart: 9, of which 6 were waited for; matrix products, arithmetic and copies ran while one was open for 0% of the time, Pallas kernels for 21%

profile of v15, /device:TPU:0, one launch (start us, length us, event | category | flops | bytes accessed | tf_op | source)
XLA Modules:
  0.0 54.3 jit_solution(9623525202611058875)
XLA Ops:
  0.0 1.9 %shard_map.82 = (bf16[4,4,96,256]{3,2,1,0:T(8,128)(2,1)S(1)}, bf16[2,4,96,256]{3,2,1,0:T(8,128)(2,1)S(1)}, bf16[4,1,96,256]{3,2,1,0:T(8,128)(2,1)S(1)}, f32[32,1,512]{2,1,0:T(1,128)}, f32[8,128]{1,0:T(8,128)S(1)}) custom-call(bf16[4,4,96,256]{3,2,1,0:T(8,128)(2,1)} %feats_hbm.1), custom_call_target="tpu_custom_call" | custom-call | flops 1572864 | bytes 1572864 | tf_op jit(solution)/shard_map/pallas_call | solution.py:136
  2.0 0.5 collective-permute-start
  2.5 7.0 %all-to-all-start = ((f32[32,1,512]{2,1,0:T(1,128)}), f32[32,1,512]{2,1,0:T(1,128)S(1)}, u32[]{:S(2)}, u32[]{:S(2)}) async-start(f32[32,1,512]{2,1,0:T(1,128)} %get-tuple-element.28), calls=%async_computation | async-start | bytes 131072 | tf_op jit(solution)/shard_map/all_to_all | solution.py:41
  9.4 1.8 %collective-permute-start.2 = (bf16[2,4,96,256]{3,2,1,0:T(8,128)(2,1)S(1)}, bf16[2,4,96,256]{3,2,1,0:T(8,128)(2,1)S(1)}, u32[]{:S(2)}, u32[]{:S(2)}) collective-permute-start(bf16[2,4,96,256]{3,2,1,0:T(8,128)(2,1)S(1)} %get-tuple-element.32), channel_id=1, source_target_pairs={{0,2},{2,4},{4,6},{6,8},{8,10},{10,12},{12,14},{14,16},{16,18},{18... | collective-permute-start | bytes 1179656 | tf_op jit(solution)/shard_map/ppermute | solution.py:37
  11.3 0.8 %shard_map.83.aux = f32[24,256]{1,0:T(8,128)S(1)} custom-call(s32[16]{0:T(128)} %clips_hbm.1, f32[1,256]{1,0:T(1,128)} %bitcast.4, f32[1,256]{1,0:T(1,128)} %bitcast.5, f32[1,256]{1,0:T(1,128)} %bitcast.6, f32[1,256]{1,0:T(1,128)} %bitcast.7, f32[8,128]{1,0:T(8,128)S(1)} %get-tuple-element.27.refs_4_), custom_call_target="tpu_custom_call" | custom-call | flops 1073741824 | bytes 65536 | tf_op jit(solution)/shard_map/pallas_call | solution.py:173
  12.0 5.0 %all-to-all-done.table = f32[32,1,512]{2,1,0:T(1,128)S(1)} async-done(((f32[32,1,512]{2,1,0:T(1,128)}), f32[32,1,512]{2,1,0:T(1,128)S(1)}, u32[]{:S(2)}, u32[]{:S(2)}) %all-to-all-start) | async-done | bytes 65568 | tf_op jit(solution)/shard_map/all_to_all | solution.py:41
  17.1 0.0 collective-permute-done.refs_0_.refs_1_
  17.1 5.1 %shard_map.84 = (bf16[2,6,96,256]{3,2,1,0:T(8,128)(2,1)S(1)}, f32[2,256]{1,0:T(2,128)S(1)}, bf16[3,3,3,256,256]{4,3,2,1,0:T(8,128)(2,1)S(1)}, bf16[2,4,96,256]{3...) custom-call(f32[24,256]{1,0:T(8,128)S(1)} %shard_map.83.aux, ...), custom_call_target="tpu_custom_call" | custom-call | flops 137438953472 | bytes 1048576 | tf_op jit(solution)/shard_map/pallas_call | solution.py:346
  22.2 3.3 %collective-permute-done.2.before = bf16[2,4,96,256]{3,2,1,0:T(8,128)(2,1)S(1)} collective-permute-done((bf16[2,4,96,256]{3,2,1,0:T(8,128)(2,1)S(1)}, bf16[2,4,96,256]{3,2,1,0:T(8,128)(2,1)S(1)}, u32[]{:S(2)}, u32[]{:S(2)}) %collective-permute-start.2) | collective-permute-done | bytes 393248 | tf_op jit(solution)/shard_map/ppermute | solution.py:37
  25.5 0.1 collective-permute-start.3
  25.6 1.3 %collective-permute-done.3.refs_0_ = bf16[2,1,96,256]{3,2,1,0:T(8,128)(2,1)S(1)} collective-permute-done((bf16[2,1,96,256]{3,2,1,0:T(8,128)(2,1)S(1)}, bf16[2,1,96,256]{3,2,1,0:T(8,128)(2,1)S(1)}, u32[]{:S(2)}, u32[]{:S(2)}) %collective-permute-start.3) | collective-permute-done | bytes 98336 | tf_op jit(solution)/shard_map/ppermute | solution.py:32
  26.9 3.7 %shard_map.85 = (bf16[2,4,96,256]{3,2,1,0:T(8,128)(2,1)S(1)}, bf16[2,1,96,256]{3,2,1,0:T(8,128)(2,1)S(1)}, f32[32,1,512]{2,1,0:T(1,128)}) custom-call(f32[24,256]{1,0:T(8,128)S(1)} %shard_map.83.aux, bf16[2,4,96,256]{3,2,1,0:T(8,128)(2,1)S(1)} %collective-permute-done.2.before, bf16[2,1,96,256]{3,2,1,0:T(8,128)(2,1)S(1)} %collective-permute-done.3.refs_0_, ...), custom_call_target="tpu_custom_call" | custom-call | flops 8589934592 | bytes 1048576 | tf_op jit(solution)/shard_map/pallas_call | solution.py:346
  30.5 2.6 %all-to-all-start.1 = ((f32[32,1,512]{2,1,0:T(1,128)}), f32[32,1,512]{2,1,0:T(1,128)S(1)}, u32[]{:S(2)}, u32[]{:S(2)}) async-start(f32[32,1,512]{2,1,0:T(1,128)} %get-tuple-element.39), calls=%async_computation.1 | async-start | bytes 131072 | tf_op jit(solution)/shard_map/all_to_all | solution.py:41
  33.1 0.2 collective-permute-start.5
  33.3 0.4 collective-permute-start.4
  33.7 1.6 %collective-permute-start.1 = (bf16[2,4,96,256]{3,2,1,0:T(8,128)(2,1)S(1)}, bf16[2,4,96,256]{3,2,1,0:T(8,128)(2,1)S(1)}, u32[]{:S(2)}, u32[]{:S(2)}) collective-permute-start(bf16[2,4,96,256]{3,2,1,0:T(8,128)(2,1)S(1)} %get-tuple-element.31.refs_3_), channel_id=1, source_target_pairs={{0,2},{2,4},{4,6},{6,8},{8,10},{10,12},{12,14},{14,16},{16,18},{18... | collective-permute-start | bytes 1179656 | tf_op jit(solution)/shard_map/ppermute | solution.py:37
  35.3 0.0 collective-permute-done.5.refs_1_
  35.3 0.0 collective-permute-done.4.refs_0_
  35.3 5.4 %all-to-all-done.1.table = f32[32,1,512]{2,1,0:T(1,128)S(1)} async-done(((f32[32,1,512]{2,1,0:T(1,128)}), f32[32,1,512]{2,1,0:T(1,128)S(1)}, u32[]{:S(2)}, u32[]{:S(2)}) %all-to-all-start.1) | async-done | bytes 65568 | tf_op jit(solution)/shard_map/all_to_all | solution.py:41
  40.8 5.8 %shard_map.86 = (bf16[2,6,96,256]{3,2,1,0:T(8,128)(2,1)S(1)}, f32[2,256]{1,0:T(2,128)S(1)}, bf16[3,3,3,256,256]{4,3,2,1,0:T(8,128)(2,1)S(1)}, f32[4,4,96,256]{3,2,1,0:T(8,128)}) custom-call(f32[24,256]{1,0:T(8,128)S(1)} %shard_map.83.aux, f32[32,1,512]{2,1,0:T(1,128)S(1)} %all-to-all-done.1.table, bf16[2,4,96,256]{3,2,1,0:T(8,128)(2,1)S(1)} %get-tuple-element.40.frames, ...), custom_call_target="tpu_custom_call" | custom-call | flops 137438953472 | bytes 1048576 | tf_op jit(solution)/shard_map/pallas_call | solution.py:346
  46.6 2.6 %collective-permute-done.1.before = bf16[2,4,96,256]{3,2,1,0:T(8,128)(2,1)S(1)} collective-permute-done((bf16[2,4,96,256]{3,2,1,0:T(8,128)(2,1)S(1)}, bf16[2,4,96,256]{3,2,1,0:T(8,128)(2,1)S(1)}, u32[]{:S(2)}, u32[]{:S(2)}) %collective-permute-start.1) | collective-permute-done | bytes 393248 | tf_op jit(solution)/shard_map/ppermute | solution.py:37
  49.2 0.1 collective-permute-start.6
  49.3 1.3 %collective-permute-done.6.refs_0_ = bf16[2,1,96,256]{3,2,1,0:T(8,128)(2,1)S(1)} collective-permute-done((bf16[2,1,96,256]{3,2,1,0:T(8,128)(2,1)S(1)}, bf16[2,1,96,256]{3,2,1,0:T(8,128)(2,1)S(1)}, u32[]{:S(2)}, u32[]{:S(2)}) %collective-permute-start.6) | collective-permute-done | bytes 98336 | tf_op jit(solution)/shard_map/ppermute | solution.py:32
  50.5 3.7 %shard_map.87 = f32[4,4,96,256]{3,2,1,0:T(8,128)} custom-call(f32[24,256]{1,0:T(8,128)S(1)} %shard_map.83.aux, bf16[2,4,96,256]{3,2,1,0:T(8,128)(2,1)S(1)} %collective-permute-done.1.before, bf16[2,1,96,256]{3,2,1,0:T(8,128)(2,1)S(1)} %collective-permute-done.6.refs_0_, ...), custom_call_target="tpu_custom_call", output_to_operand_aliasing={{}: (7, {})} | custom-call | flops 8589934592 | bytes 1048576 | tf_op jit(solution)/shard_map/pallas_call | solution.py:346
  (2 shorter events, 0.0 us)
Async XLA Ops:
  2.0 15.1 %collective-permute-start = (bf16[4,1,96,256]{3,2,1,0:T(8,128)(2,1)S(1)}, bf16[4,1,96,256]{3,2,1,0:T(8,128)(2,1)S(1)}, u32[]{:S(2)}, u32[]{:S(2)}) collective-permute-start(bf16[4,1,96,256]{3,2,1,0:T(8,128)(2,1)S(1)} %get-tuple-element.30), channel_id=1, source_target_pairs={{0,1},{1,0},{2,3},{3,2},{4,5},{5,4},{6,7},{7,6},{8,9},{9,8},{10,11... | collective-permute-start | bytes 589832 | tf_op jit(solution)/shard_map/ppermute | solution.py:32
  2.5 14.6 %all-to-all-start = ((f32[32,1,512]{2,1,0:T(1,128)}), f32[32,1,512]{2,1,0:T(1,128)S(1)}, u32[]{:S(2)}, u32[]{:S(2)}) async-start(f32[32,1,512]{2,1,0:T(1,128)} %get-tuple-element.28), calls=%async_computation | async-start | bytes 131072 | tf_op jit(solution)/shard_map/all_to_all | solution.py:41
  9.4 16.0 %collective-permute-start.2 = (bf16[2,4,96,256]{3,2,1,0:T(8,128)(2,1)S(1)}, bf16[2,4,96,256]{3,2,1,0:T(8,128)(2,1)S(1)}, u32[]{:S(2)}, u32[]{:S(2)}) collective-permute-start(bf16[2,4,96,256]{3,2,1,0:T(8,128)(2,1)S(1)} %get-tuple-element.32), channel_id=1, source_target_pairs={{0,2},{2,4},{4,6},{6,8},{8,10},{10,12},{12,14},{14,16},{16,18},{18... | collective-permute-start | bytes 1179656 | tf_op jit(solution)/shard_map/ppermute | solution.py:37
  25.5 1.4 %collective-permute-start.3 = (bf16[2,1,96,256]{3,2,1,0:T(8,128)(2,1)S(1)}, bf16[2,1,96,256]{3,2,1,0:T(8,128)(2,1)S(1)}, u32[]{:S(2)}, u32[]{:S(2)}) collective-permute-start(bf16[2,1,96,256]{3,2,1,0:T(8,128)(2,1)S(1)} %constant_dynamic-slice_fusion.1), channel_id=1, source_target_pairs={{0,1},{1,0},{2,3},{3,2},{4,5},{5,4},{6,7},{7,6},{8,9},{9,8},{10,11... | collective-permute-start | bytes 294920 | tf_op jit(solution)/shard_map/ppermute | solution.py:32
  30.5 10.2 %all-to-all-start.1 = ((f32[32,1,512]{2,1,0:T(1,128)}), f32[32,1,512]{2,1,0:T(1,128)S(1)}, u32[]{:S(2)}, u32[]{:S(2)}) async-start(f32[32,1,512]{2,1,0:T(1,128)} %get-tuple-element.39), calls=%async_computation.1 | async-start | bytes 131072 | tf_op jit(solution)/shard_map/all_to_all | solution.py:41
  33.1 2.2 %collective-permute-start.5 = (bf16[2,1,96,256]{3,2,1,0:T(8,128)(2,1)S(1)}, bf16[2,1,96,256]{3,2,1,0:T(8,128)(2,1)S(1)}, u32[]{:S(2)}, u32[]{:S(2)}) collective-permute-start(bf16[2,1,96,256]{3,2,1,0:T(8,128)(2,1)S(1)} %get-tuple-element.42), channel_id=1, source_target_pairs={{0,1},{1,0},{2,3},{3,2},{4,5},{5,4},{6,7},{7,6},{8,9},{9,8},{10,11... | collective-permute-start | bytes 294920 | tf_op jit(solution)/shard_map/ppermute | solution.py:32
  33.3 2.0 %collective-permute-start.4 = (bf16[2,1,96,256]{3,2,1,0:T(8,128)(2,1)S(1)}, bf16[2,1,96,256]{3,2,1,0:T(8,128)(2,1)S(1)}, u32[]{:S(2)}, u32[]{:S(2)}) collective-permute-start(bf16[2,1,96,256]{3,2,1,0:T(8,128)(2,1)S(1)} %get-tuple-element.41), channel_id=1, source_target_pairs={{0,1},{1,0},{2,3},{3,2},{4,5},{5,4},{6,7},{7,6},{8,9},{9,8},{10,11... | collective-permute-start | bytes 294920 | tf_op jit(solution)/shard_map/ppermute | solution.py:32
  33.7 15.5 %collective-permute-start.1 = (bf16[2,4,96,256]{3,2,1,0:T(8,128)(2,1)S(1)}, bf16[2,4,96,256]{3,2,1,0:T(8,128)(2,1)S(1)}, u32[]{:S(2)}, u32[]{:S(2)}) collective-permute-start(bf16[2,4,96,256]{3,2,1,0:T(8,128)(2,1)S(1)} %get-tuple-element.31.refs_3_), channel_id=1, source_target_pairs={{0,2},{2,4},{4,6},{6,8},{8,10},{10,12},{12,14},{14,16},{16,18},{18... | collective-permute-start | bytes 1179656 | tf_op jit(solution)/shard_map/ppermute | solution.py:37
  49.2 1.4 %collective-permute-start.6 = (bf16[2,1,96,256]{3,2,1,0:T(8,128)(2,1)S(1)}, bf16[2,1,96,256]{3,2,1,0:T(8,128)(2,1)S(1)}, u32[]{:S(2)}, u32[]{:S(2)}) collective-permute-start(bf16[2,1,96,256]{3,2,1,0:T(8,128)(2,1)S(1)} %constant_dynamic-slice_fusion), channel_id=1, source_target_pairs={{0,1},{1,0},{2,3},{3,2},{4,5},{5,4},{6,7},{7,6},{8,9},{9,8},{10,11... | collective-permute-start | bytes 294920 | tf_op jit(solution)/shard_map/ppermute | solution.py:32

commit v16 on v15

--- a/solution.py
+++ b/solution.py
@@ -41,9 +41,9 @@
     return lax.all_to_all(copies, ("tm", "space"), 0, 0, tiled=True)
 
 
-def corner_rows(before, after):
-    before, after = lax.optimization_barrier((before, after))
-    return before, row_halo(edges_of(before)), after
+def slab_halo(tail, sides):
+    rows = [side[-1:] for side in sides]
+    return shifted(tail[:1], "tm", 1), shifted(jnp.concatenate([tail[1:], *rows], axis=1), "tm", 1)
 
 
 def row_halo(edges):
@@ -144,12 +144,13 @@
     )(in_hbm(feats))
 
 
-def setup_kernel(slabs, per_slab, clips_hbm, *refs):
-    params_hbm, (_, aux, params, clips, sems) = refs[:4], refs[4:]
+def setup_kernel(slabs, per_slab, kernel_hbm, clips_hbm, *refs):
+    params_hbm, (_, taps, aux, params, clips, sems) = refs[:4], refs[4:]
+    taps_load = pltpu.make_async_copy(kernel_hbm.at[0], taps.at[0], sems.at[5])
     width = aux.shape[1]
     clip_load = pltpu.make_async_copy(clips_hbm, clips, sems.at[0])
     param_loads = [pltpu.make_async_copy(p, params.at[k], sems.at[1 + k]) for k, p in enumerate(params_hbm)]
-    for copy in [clip_load, *param_loads]:
+    for copy in [clip_load, *param_loads, taps_load]:
         copy.start()
     clip_load.wait()
     own = lax.axis_index("tm")
@@ -166,23 +167,24 @@
         copy.wait()
         aux[slabs + 2 + k : slabs + 3 + k] = params[k]
     aux[slabs + 6 : slabs + 8] = jnp.zeros((2, width), F32)
-
-
-def setup_call(clip_ids, params, per_slab, mark):
+    taps_load.wait()
+
+
+def setup_call(kernel, clip_ids, params, per_slab, mark):
     slabs, width = lax.axis_size("tm"), params[0].shape[0]
     return pl.pallas_call(
         functools.partial(setup_kernel, slabs, per_slab),
-        out_shape=shaped((slabs + 8, width), F32),
-        in_specs=[ANYWHERE] * 5 + [VMEM],
-        out_specs=VMEM,
+        out_shape=[shaped((1,) + kernel.shape[1:]), shaped((slabs + 8, width), F32)],
+        in_specs=[ANYWHERE] * 6 + [VMEM],
+        out_specs=[VMEM, VMEM],
         scratch_shapes=[
             pltpu.VMEM((4, 1, width), F32),
             pltpu.SMEM(clip_ids.shape, jnp.int32),
-            pltpu.SemaphoreType.DMA((5,)),
+            pltpu.SemaphoreType.DMA((6,)),
         ],
         compiler_params=vmem_params(),
         cost_estimate=pl.CostEstimate(flops=1 << 30, bytes_accessed=1 << 16, transcendentals=0),
-    )(*[in_hbm(x) for x in (clip_ids, *[p[None] for p in params])], mark)
+    )(*[in_hbm(x) for x in (kernel, clip_ids, *[p[None] for p in params])], mark)
 
 
 def group_total(values):
@@ -244,7 +246,7 @@
     column = lax.broadcasted_iota(jnp.int32, (cols, width), 0)
     sums = []
     for l in range(3):
-        rhs = jnp.concatenate([taps[i, j, l] for i in range(3) for j in range(3)], axis=0)
+        rhs = jnp.concatenate([taps[0][0, j, l] for j in range(3)] + [taps[1][i, j, l] for i in range(2) for j in range(3)], axis=0)
         sums.append(jnp.dot(lhs, rhs, preferred_element_type=F32))
     for row in range(n_rows):
         left, mid, right = (s[row * cols : (row + 1) * cols] for s in sums)
@@ -260,17 +262,23 @@
 
 
 def late_kernel(n_sides, which, aux, table, frames, *refs):
-    early_sides, late_sides, kernel_hbm = refs[:n_sides], refs[n_sides : 2 * n_sides], refs[2 * n_sides]
+    early_sides, late_sides = refs[:n_sides], refs[n_sides : 2 * n_sides]
+    first_taps, kernel_hbm, *refs = refs[2 * n_sides :]
     if which == 0:
-        act_low, affine_out, taps, hidden, stats, edges, act_high, taps_sems = refs[2 * n_sides + 1 :]
+        act_low, affine_out, more_taps, hidden, stats, edges, act_high, taps_sems = refs
         early = late = frames
         late_first = 0
     else:
-        late, feats, act_low, affine_out, taps, out_hbm, act_high, taps_sems, out, sems = refs[2 * n_sides + 1 :]
+        late, feats_hbm, act_low, affine_out, more_taps, out_hbm, act_high, taps_sems, out, feats, sems = refs
         early, late_first = frames, frames.shape[0]
+    taps = (first_taps, more_taps)
     loads = [
-        pltpu.make_async_copy(kernel_hbm.at[i, j], taps.at[i, j], taps_sems.at[3 * i + j]) for i in range(3) for j in range(3)
+        pltpu.make_async_copy(kernel_hbm.at[i, j], more_taps.at[i - 1, j], taps_sems.at[3 * i + j])
+        for i in range(1, 3)
+        for j in range(3)
     ]
+    if which == 1:
+        loads.append(pltpu.make_async_copy(feats_hbm.at[pl.ds(2, feats.shape[0])], feats, taps_sems.at[0]))
     for copy in loads:
         copy.start()
     n_rows, width = frames.shape[1], frames.shape[3]
@@ -295,7 +303,7 @@
             if which == 0:
                 sums = put_hidden(hidden, frame, row, value, sums)
             else:
-                out[frame, row] = feats[low + frame, row].astype(F32) + value
+                out[frame, row] = feats[frame, row].astype(F32) + value
         if which == 0:
             send_rows(hidden, frame, edges)
         else:
@@ -308,21 +316,32 @@
         store.wait()
 
 
-def early_kernel(n_sides, which, aux, before, *refs):
-    corners, (act_low, affine_in, taps), refs = refs[:n_sides], refs[n_sides : n_sides + 3], refs[n_sides + 3 :]
+def early_kernel(n_sides, which, aux, first, second, *refs):
+    corners, (act_low, affine_in, *taps), refs = refs[:n_sides], refs[n_sides : n_sides + 4], refs[n_sides + 4 :]
     if which == 0:
-        late_stats, hidden, edges, copies, act_before, stats = refs
+        late_stats, kernel_hbm, hidden, edges, copies, next_taps, act_before, stats, sems = refs
         sums = late_stats[0], late_stats[1]
+        loads = [pltpu.make_async_copy(kernel_hbm.at[0], next_taps.at[0], sems.at[0])]
     else:
-        feats, _, out_hbm, act_before, out, sems = refs
+        feats_hbm, _, out_hbm, act_before, out, feats, sems = refs
+        loads = [pltpu.make_async_copy(feats_hbm.at[pl.ds(0, 2)], feats, sems.at[2])]
+    for load in loads:
+        load.start()
     slabs = aux.shape[0] - 8
     starting = aux[slabs : slabs + 1] != 0.0
     affine = affine_in[0:1], affine_in[1:2]
-    for frame in range(2):
-        for row in range(act_low.shape[1]):
-            value = normed(extended_row(before, corners, frame, row), affine).astype(F32)
+    n_rows = first.shape[1]
+    for row in range(n_rows + 2):
+        for frame in range(2):
+            if frame == 0:
+                raw = extended_row(first, corners, 0, row)
+            else:
+                raw = extended_row(second.at[:, :n_rows], [second.at[:, n_rows + k :] for k in range(n_sides)], 0, row)
+            value = normed(raw, affine).astype(F32)
             act_before[frame, row] = jnp.where(starting, act_low[0, row].astype(F32), value).astype(BF16)
     planes = [(act_before, 0), (act_before, 1)] + [(act_low, f) for f in range(act_low.shape[0])]
+    if which == 1:
+        loads[0].wait()
     stores = []
     for frame in range(2):
         for row, value in conv_rows(planes[frame : frame + 3], taps):
@@ -338,6 +357,7 @@
     if which == 0:
         store_stats(stats, sums)
         store_copies(copies, stats)
+        loads[0].wait()
     for store in stores:
         store.wait()
 
@@ -363,18 +383,21 @@
     plane = (n_rows + 2, cols, width)
     act = pltpu.VMEM((2,) + plane, BF16)
     act_late = pltpu.VMEM((late,) + plane, BF16)
-    late_shapes = [shaped((2,) + plane), shaped((2, width), F32), shaped(kernel_one.shape)]
+    late_shapes = [shaped((2,) + plane), shaped((2, width), F32), shaped((2,) + kernel_one.shape[1:])]
     hidden_shapes = [shaped((late, n_rows, cols, width)), shaped((2, 8, width), F32), shaped(edge_shape(feats, late))]
+    first_taps = shaped((1,) + kernel_one.shape[1:])
     taps_sems = pltpu.SemaphoreType.DMA((9,))
 
     frames, tail, edges, copies, mark = entry_call(feats)
     table = stats_table(copies)
-    before = shifted(tail, "tm", 1)
     sides = row_halo(edges)
     n_sides = len(sides)
-    aux = setup_call(clip_ids, params, per_slab, mark)
-    operands = [aux, table, frames, *sides, *sides, in_hbm(kernel_one)]
-    act_low, affine, taps, hidden_late, stats, edges_late = call(
+    first, second = slab_halo(tail, sides)
+    corners = row_halo(edges_of(first))
+    taps, aux = setup_call(kernel_one, clip_ids, params, per_slab, mark)
+    aux, *corners = lax.optimization_barrier((aux, *corners))
+    operands = [aux, table, frames, *sides, *sides, taps, in_hbm(kernel_one)]
+    act_low, affine, more_taps, hidden_late, stats, edges_late = call(
         functools.partial(late_kernel, n_sides, 0),
         late_shapes + hidden_shapes,
         [act_late, taps_sems],
@@ -382,37 +405,48 @@
         operands,
         outside=(len(operands) - 1,),
     )
-    before, corners, affine = corner_rows(before, affine)
-    hidden_early, edges, copies = call(
+    operands = [aux, first, second, *corners, act_low, affine, taps, more_taps, stats, in_hbm(kernel_two)]
+    hidden_early, edges, copies, taps = call(
         functools.partial(early_kernel, n_sides, 0),
-        [shaped((2, n_rows, cols, width)), shaped(edge_shape(feats, 2)), copies_shape(width)],
-        [act, pltpu.VMEM((1, 2 * width), F32)],
+        [shaped((2, n_rows, cols, width)), shaped(edge_shape(feats, 2)), copies_shape(width), first_taps],
+        [act, pltpu.VMEM((1, 2 * width), F32), pltpu.SemaphoreType.DMA((1,))],
         2,
-        [aux, before, *corners, act_low, affine, taps, stats],
+        operands,
+        outside=(len(operands) - 1,),
     )
 
     table = stats_table(copies)
-    before = shifted(hidden_late[late - 2 :], "tm", 1)
-    operands = [aux, table, hidden_early, *row_halo(edges), *row_halo(edges_late), in_hbm(kernel_two), hidden_late, frames]
-    act_low, affine, taps, out = call(
+    sides_late = row_halo(edges_late)
+    tail, edges = lax.optimization_barrier((hidden_late[late - 2 :], edges))
+    first, second = slab_halo(tail, sides_late)
+    corners = row_halo(edges_of(first))
+    aux, *corners = lax.optimization_barrier((aux, *corners))
+    operands = [aux, table, hidden_early, *row_halo(edges), *sides_late, taps, in_hbm(kernel_two), hidden_late, in_hbm(feats)]
+    act_low, affine, more_taps, out = call(
         functools.partial(late_kernel, n_sides, 1),
         late_shapes + [shaped(feats.shape, F32)],
-        [act_late, taps_sems, pltpu.VMEM((late, n_rows, cols, width), F32), pltpu.SemaphoreType.DMA((late,))],
+        [
+            act_late,
+            taps_sems,
+            pltpu.VMEM((late, n_rows, cols, width), F32),
+            pltpu.VMEM((late, n_rows, cols, width), BF16),
+            pltpu.SemaphoreType.DMA((late,)),
+        ],
         32,
         operands,
         out_specs=[VMEM, VMEM, VMEM, ANYWHERE],
-        outside=(len(operands) - 3,),
-    )
-    before, corners, affine = corner_rows(before, affine)
-    operands = [aux, before, *corners, act_low, affine, taps, frames, out]
+        outside=(len(operands) - 3, len(operands) - 1),
+    )
+    operands = [aux, first, second, *corners, act_low, affine, taps, more_taps, in_hbm(feats), out]
     return call(
         functools.partial(early_kernel, n_sides, 1),
         shaped(feats.shape, F32),
-        [act, pltpu.VMEM((2, n_rows, cols, width), F32), pltpu.SemaphoreType.DMA((2,))],
+        [act, pltpu.VMEM((2, n_rows, cols, width), F32), pltpu.VMEM((2, n_rows, cols, width), BF16), pltpu.SemaphoreType.DMA((3,))],
         2,
         operands,
         out_specs=ANYWHERE,
         aliases={len(operands) - 1: 0},
+        outside=(len(operands) - 2,),
     )
 
 

time: 54.5 us -> 58.9 us (1.081)
  local copies, waits for them, and re-layouts: 0.01 us -> 2.38 us
  Pallas kernels: 21 us -> 22 us
  other arithmetic: 0 us -> 0.74 us
    all_to_all x2, waiting for transfers between devices: 10.5 us -> 5.44 us  [stats_table(): return lax.all_to_all(copies, ('tm', 'space'), 0, 0, tiled=True)]
    ppermute x2 -> x4, waiting for transfers between devices: 5.9 us -> 10.3 us  [shifted(): lax.ppermute(value, axis, [(i, (i + step) % peers) for i in range(peers)])]
    unnamed x0 -> x6, local copies, waits for them, and re-layouts: none -> 2.3 us
    all_to_all x2, starting transfers between devices: 9.53 us -> 10.8 us  [stats_table(): return lax.all_to_all(copies, ('tm', 'space'), 0, 0, tiled=True)]
    concatenate x0 -> x2, other arithmetic: none -> 0.74 us  [slab_halo(): jnp.concatenate([tail[1:], *rows], axis=1)]
    pallas_call x1, Pallas kernels: 0.77 us -> 1.39 us  [setup_call(): pl.pallas_call(functools.partial(setup_kernel, slabs, per_slab), out_shap...]
    ppermute x2 -> x4, starting transfers between devices: 3.46 us -> 3.11 us  [shifted(): lax.ppermute(value, axis, [(i, (i + step) % peers) for i in range(peers)])]
  transfers between devices with their start and end apart: 9 -> 11, of which waited for: 6 -> 9; matrix products, arithmetic and copies ran while one was open for 0% -> 1% of each run, Pallas kernels for 21% -> 20%
where the time goes in v16:
time: 58.9 us; the launch traced here: 58.6 us
  Pallas kernels  22 us (37%)
  waiting for transfers between devices  18.6 us (32%)
  starting transfers between devices  14.6 us (25%)
  local copies, waits for them, and re-layouts  2.38 us (4%)
  other arithmetic  0.74 us (1%)
    pallas_call x4, Pallas kernels, call(): pl.pallas_call(kernel, out_shape=outs, in_specs=[ANYWHERE if k in (aliase...  18.7 us
    all_to_all x2, starting transfers between devices, stats_table(): return lax.all_to_all(copies, ('tm', 'space'), 0, 0, tiled=True)  10.8 us
    ppermute x4, waiting for transfers between devices, shifted(): lax.ppermute(value, axis, [(i, (i + step) % peers) for i in range(peers)])  10.3 us
    all_to_all x2, waiting for transfers between devices, stats_table(): return lax.all_to_all(copies, ('tm', 'space'), 0, 0, tiled=True)  5.44 us
    ppermute x4, starting transfers between devices, shifted(): lax.ppermute(value, axis, [(i, (i + step) % peers) for i in range(peers)])  3.11 us
    ppermute x5, waiting for transfers between devices, traded(): lax.ppermute(value, axis, [(i, i ^ mask) for i in range(lax.axis_size(axi...  2.9 us
    unnamed x6, local copies, waits for them, and re-layouts  2.3 us
    pallas_call x1, Pallas kernels, entry_call(): pl.pallas_call(entry_kernel, out_shape=outs, in_specs=[ANYWHERE], out_spe...  1.95 us
  transfers between devices with their start and end apart: 11, of which 9 were waited for; matrix products, arithmetic and copies ran while one was open for 1% of the time, Pallas kernels for 20%

profile of v16, /device:TPU:0, one launch (start us, length us, event | category | flops | bytes accessed | tf_op | source)
XLA Modules:
  0.0 58.6 jit_solution(10987756298670083645)
XLA Ops:
  0.0 1.9 %shard_map.82 = (bf16[4,4,96,256]{3,2,1,0:T(8,128)(2,1)S(1)}, bf16[2,4,96,256]{3,2,1,0:T(8,128)(2,1)S(1)}, bf16[4,1,96,256]{3,2,1,0:T(8,128)(2,1)S(1)}, f32[32,1,512]{2,1,0:T(1,128)}, f32[8,128]{1,0:T(8,128)S(1)}) custom-call(bf16[4,4,96,256]{3,2,1,0:T(8,128)(2,1)} %refs_5_.3), custom_call_target="tpu_custom_call" | custom-call | flops 1572864 | bytes 1572864 | tf_op jit(solution)/shard_map/pallas_call | solution.py:136
  2.0 3.0 %collective-permute-start = (bf16[1,4,96,256]{3,2,1,0:T(8,128)(2,1)S(1)}, bf16[1,4,96,256]{3,2,1,0:T(8,128)(2,1)S(1)}, u32[]{:S(2)}, u32[]{:S(2)}) collective-permute-start(bf16[1,4,96,256]{3,2,1,0:T(8,128)(2,1)S(1)} %get-tuple-element.62), channel_id=1, source_target_pairs={{0,2},{2,4},{4,6},{6,8},{8,10},{10,12},{12,14},{14,16},{16,18},{18... | collective-permute-start | bytes 589832 | tf_op jit(solution)/shard_map/ppermute | solution.py:37
  5.0 4.9 %all-to-all-start = ((f32[32,1,512]{2,1,0:T(1,128)}), f32[32,1,512]{2,1,0:T(1,128)S(1)}, u32[]{:S(2)}, u32[]{:S(2)}) async-start(f32[32,1,512]{2,1,0:T(1,128)} %get-tuple-element.36), calls=%async_computation | async-start | bytes 131072 | tf_op jit(solution)/shard_map/all_to_all | solution.py:41
  9.9 0.3 collective-permute-start.2
  10.2 1.4 %shard_map.83 = (bf16[1,3,3,256,256]{4,3,2,1,0:T(8,128)(2,1)S(1)}, f32[24,256]{1,0:T(8,128)S(1)}) custom-call(bf16[3,3,3,256,256]{4,3,2,1,0:T(8,128)(2,1)} %refs_3_.2, s32[16]{0:T(128)} %clips_hbm.1, f32[1,256]{1,0:T(1,128)} %bitcast.4, f32[1,256]{1,0:T(1,128)} %bitcast.5, f32[1,256]{1,0:T(1,128)} %bitcast.6, f32[1,256]{1,0:T(1,128)} %bitcast.7, ...), custom_call_target="tpu_custom_call" | custom-call | flops 1073741824 | bytes 65536 | tf_op jit(solution)/shard_map/pallas_call | solution.py:175
  11.6 2.4 %collective-permute-done.first = bf16[1,4,96,256]{3,2,1,0:T(8,128)(2,1)S(1)} collective-permute-done((bf16[1,4,96,256]{3,2,1,0:T(8,128)(2,1)S(1)}, bf16[1,4,96,256]{3,2,1,0:T(8,128)(2,1)S(1)}, u32[]{:S(2)}, u32[]{:S(2)}) %collective-permute-start) | collective-permute-done | bytes 196640 | tf_op jit(solution)/shard_map/ppermute | solution.py:37
  14.0 0.0 collective-permute-start.1
  14.0 0.0 collective-permute-done.2.refs_0_.refs_1_
  14.1 0.1 collective-permute-start.3
  14.1 1.1 %collective-permute-done.1.refs_0_ = bf16[1,1,96,256]{3,2,1,0:T(8,128)(2,1)S(1)} collective-permute-done((bf16[1,1,96,256]{3,2,1,0:T(8,128)(2,1)S(1)}, bf16[1,1,96,256]{3,2,1,0:T(8,128)(2,1)S(1)}, u32[]{:S(2)}, u32[]{:S(2)}) %collective-permute-start.1) | collective-permute-done | bytes 49184 | tf_op jit(solution)/shard_map/ppermute | solution.py:32
  15.2 2.1 %all-to-all-done.table = f32[32,1,512]{2,1,0:T(1,128)S(1)} async-done(((f32[32,1,512]{2,1,0:T(1,128)}), f32[32,1,512]{2,1,0:T(1,128)S(1)}, u32[]{:S(2)}, u32[]{:S(2)}) %all-to-all-start) | async-done | bytes 65568 | tf_op jit(solution)/shard_map/all_to_all | solution.py:41
  17.3 4.7 %shard_map.84 = (bf16[2,6,96,256]{3,2,1,0:T(8,128)(2,1)S(1)}, f32[2,256]{1,0:T(2,128)S(1)}, bf16[2,3,3,256,256]{4,3,2,1,0:T(8,128)(2,1)S(1)}, bf16[2,4,96,256]{3...) custom-call(f32[24,256]{1,0:T(8,128)S(1)} %get-tuple-element.48.aux, ...), custom_call_target="tpu_custom_call" | custom-call | flops 137438953472 | bytes 1048576 | tf_op jit(solution)/shard_map/pallas_call | solution.py:366
  22.0 4.0 %collective-permute-done.3.second = bf16[1,5,96,256]{3,2,1,0:T(8,128)(2,1)S(1)} collective-permute-done((bf16[1,5,96,256]{3,2,1,0:T(8,128)(2,1)S(1)}, bf16[1,5,96,256]{3,2,1,0:T(8,128)(2,1)S(1)}, u32[]{:S(2)}, u32[]{:S(2)}) %collective-permute-start.3) | collective-permute-done | bytes 245792 | tf_op jit(solution)/shard_map/ppermute | solution.py:37
  26.1 3.7 %shard_map.85 = (bf16[2,4,96,256]{3,2,1,0:T(8,128)(2,1)S(1)}, bf16[2,1,96,256]{3,2,1,0:T(8,128)(2,1)S(1)}, f32[32,1,512]{2,1,0:T(1,128)}, bf16[1,3,3,256,256]{4,3,2,1,0:T(8,128)(2,1)S(1)}) custom-call(f32[24,256]{1,0:T(8,128)S(1)} %get-tuple-element.48.aux, bf16[1,4,96,256]{3,2,1,0:T(8,128)(2,1)S(1)} %collective-permute-done.first, ...), custom_call_target="tpu_custom_call" | custom-call | flops 8589934592 | bytes 1048576 | tf_op jit(solution)/shard_map/pallas_call | solution.py:366
  29.7 0.0 copy-start
  29.8 1.0 %copy-done = bf16[1,3,3,256,256]{4,3,2,1,0:T(8,128)(2,1)} copy-done((bf16[1,3,3,256,256]{4,3,2,1,0:T(8,128)(2,1)}, bf16[1,3,3,256,256]{4,3,2,1,0:T(8,128)(2,1)S(1)}, u32[]{:S(2)}) %copy-start) | copy-done | bytes 1179672
  30.8 0.1 collective-permute-start.4
  30.9 0.1 collective-permute-start.6
  31.0 1.3 %collective-permute-done.6.refs_1_ = bf16[2,1,96,256]{3,2,1,0:T(8,128)(2,1)S(1)} collective-permute-done((bf16[2,1,96,256]{3,2,1,0:T(8,128)(2,1)S(1)}, bf16[2,1,96,256]{3,2,1,0:T(8,128)(2,1)S(1)}, u32[]{:S(2)}, u32[]{:S(2)}) %collective-permute-start.6) | collective-permute-done | bytes 98336 | tf_op jit(solution)/shard_map/ppermute | solution.py:32
  32.2 5.9 %all-to-all-start.1 = ((f32[32,1,512]{2,1,0:T(1,128)}), f32[32,1,512]{2,1,0:T(1,128)S(1)}, u32[]{:S(2)}, u32[]{:S(2)}) async-start(f32[32,1,512]{2,1,0:T(1,128)} %get-tuple-element.51), calls=%async_computation.1 | async-start | bytes 131072 | tf_op jit(solution)/shard_map/all_to_all | solution.py:41
  38.2 0.3 collective-permute-start.8
  38.5 2.5 %collective-permute-done.4.first = bf16[1,4,96,256]{3,2,1,0:T(8,128)(2,1)S(1)} collective-permute-done((bf16[1,4,96,256]{3,2,1,0:T(8,128)(2,1)S(1)}, bf16[1,4,96,256]{3,2,1,0:T(8,128)(2,1)S(1)}, u32[]{:S(2)}, u32[]{:S(2)}) %collective-permute-start.4) | collective-permute-done | bytes 196640 | tf_op jit(solution)/shard_map/ppermute | solution.py:37
  41.0 0.0 collective-permute-start.5
  41.0 0.7 %pad_maximum_fusion.1 = bf16[1,5,96,256]{3,2,1,0:T(8,128)(2,1)} fusion(bf16[1,1,96,256]{3,2,1,0:T(8,128)(2,1)S(1)} %slice.25, bf16[1,4,96,256]{3,2,1,0:T(8,128)(2,1)S(1)} %get-tuple-element.59), kind=kLoop, calls=%fused_computation.1 | loop fusion | flops 122880 | bytes 491520 | tf_op jit(solution)/shard_map/concatenate | solution.py:46
  41.7 0.0 collective-permute-start.7
  41.7 0.5 collective-permute-done.5.refs_0_
  42.2 0.0 collective-permute-done.8.refs_0_
  42.2 3.4 %all-to-all-done.1.table = f32[32,1,512]{2,1,0:T(1,128)S(1)} async-done(((f32[32,1,512]{2,1,0:T(1,128)}), f32[32,1,512]{2,1,0:T(1,128)S(1)}, u32[]{:S(2)}, u32[]{:S(2)}) %all-to-all-start.1) | async-done | bytes 65568 | tf_op jit(solution)/shard_map/all_to_all | solution.py:41
  45.6 0.0 copy-start.1
  45.6 1.3 %copy-done.1 = bf16[1,3,3,256,256]{4,3,2,1,0:T(8,128)(2,1)S(1)} copy-done((bf16[1,3,3,256,256]{4,3,2,1,0:T(8,128)(2,1)S(1)}, bf16[1,3,3,256,256]{4,3,2,1,0:T(8,128)(2,1)}, u32[]{:S(2)}) %copy-start.1) | copy-done | bytes 1179672
  46.8 0.0 copy-start.2
  46.8 5.6 %shard_map.86 = (bf16[2,6,96,256]{3,2,1,0:T(8,128)(2,1)S(1)}, f32[2,256]{1,0:T(2,128)S(1)}, bf16[2,3,3,256,256]{4,3,2,1,0:T(8,128)(2,1)S(1)}, f32[4,4,96,256]{3,2,1,0:T(8,128)}) custom-call(f32[24,256]{1,0:T(8,128)S(1)} %get-tuple-element.48.aux, f32[32,1,512]{2,1,0:T(1,128)S(1)} %all-to-all-done.1.table, ...), custom_call_target="tpu_custom_call" | custom-call | flops 137438953472 | bytes 1048576 | tf_op jit(solution)/shard_map/pallas_call | solution.py:366
  52.5 1.4 %collective-permute-done.7.second = bf16[1,5,96,256]{3,2,1,0:T(8,128)(2,1)S(1)} collective-permute-done((bf16[1,5,96,256]{3,2,1,0:T(8,128)(2,1)}, bf16[1,5,96,256]{3,2,1,0:T(8,128)(2,1)S(1)}, u32[]{:S(2)}, u32[]{:S(2)}) %collective-permute-start.7) | collective-permute-done | bytes 245792 | tf_op jit(solution)/shard_map/ppermute | solution.py:37
  53.9 0.0 copy-done.2
  53.9 4.7 %shard_map.87 = f32[4,4,96,256]{3,2,1,0:T(8,128)} custom-call(f32[24,256]{1,0:T(8,128)S(1)} %get-tuple-element.48.aux, bf16[1,4,96,256]{3,2,1,0:T(8,128)(2,1)S(1)} %collective-permute-done.4.first, bf16[1,5,96,256]{3,2,1,0:T(8,128)(2,1)S(1)} %collective-permute-done.7.second, ...), custom_call_target="tpu_custom_call", output_to_operand_aliasing={{}: (9, {})} | custom-call | flops 8589934592 | bytes 1048576 | tf_op jit(solution)/shard_map/pallas_call | solution.py:366
  (7 shorter events, 0.1 us)
Async XLA Ops:
  2.0 12.0 %collective-permute-start = (bf16[1,4,96,256]{3,2,1,0:T(8,128)(2,1)S(1)}, bf16[1,4,96,256]{3,2,1,0:T(8,128)(2,1)S(1)}, u32[]{:S(2)}, u32[]{:S(2)}) collective-permute-start(bf16[1,4,96,256]{3,2,1,0:T(8,128)(2,1)S(1)} %get-tuple-element.62), channel_id=1, source_target_pairs={{0,2},{2,4},{4,6},{6,8},{8,10},{10,12},{12,14},{14,16},{16,18},{18... | collective-permute-start | bytes 589832 | tf_op jit(solution)/shard_map/ppermute | solution.py:37
  5.0 12.3 %all-to-all-start = ((f32[32,1,512]{2,1,0:T(1,128)}), f32[32,1,512]{2,1,0:T(1,128)S(1)}, u32[]{:S(2)}, u32[]{:S(2)}) async-start(f32[32,1,512]{2,1,0:T(1,128)} %get-tuple-element.36), calls=%async_computation | async-start | bytes 131072 | tf_op jit(solution)/shard_map/all_to_all | solution.py:41
  9.9 4.1 %collective-permute-start.2 = (bf16[4,1,96,256]{3,2,1,0:T(8,128)(2,1)S(1)}, bf16[4,1,96,256]{3,2,1,0:T(8,128)(2,1)S(1)}, u32[]{:S(2)}, u32[]{:S(2)}) collective-permute-start(bf16[4,1,96,256]{3,2,1,0:T(8,128)(2,1)S(1)} %get-tuple-element.38), channel_id=1, source_target_pairs={{0,1},{1,0},{2,3},{3,2},{4,5},{5,4},{6,7},{7,6},{8,9},{9,8},{10,11... | collective-permute-start | bytes 589832 | tf_op jit(solution)/shard_map/ppermute | solution.py:32
  14.0 1.2 %collective-permute-start.1 = (bf16[1,1,96,256]{3,2,1,0:T(8,128)(2,1)S(1)}, bf16[1,1,96,256]{3,2,1,0:T(8,128)(2,1)S(1)}, u32[]{:S(2)}, u32[]{:S(2)}) collective-permute-start(bf16[1,1,96,256]{3,2,1,0:T(8,128)(2,1)S(1)} %constant_dynamic-slice_fusion.1), channel_id=1, source_target_pairs={{0,1},{1,0},{2,3},{3,2},{4,5},{5,4},{6,7},{7,6},{8,9},{9,8},{10,11... | collective-permute-start | bytes 147464 | tf_op jit(solution)/shard_map/ppermute | solution.py:32
  14.1 12.0 %collective-permute-start.3 = (bf16[1,5,96,256]{3,2,1,0:T(8,128)(2,1)S(1)}, bf16[1,5,96,256]{3,2,1,0:T(8,128)(2,1)S(1)}, u32[]{:S(2)}, u32[]{:S(2)}) collective-permute-start(bf16[1,5,96,256]{3,2,1,0:T(8,128)(2,1)S(1)} %pad_maximum_fusion), channel_id=1, source_target_pairs={{0,2},{2,4},{4,6},{6,8},{8,10},{10,12},{12,14},{14,16},{16,18},{18... | collective-permute-start | bytes 737288 | tf_op jit(solution)/shard_map/ppermute | solution.py:37
  29.7 1.0 %copy-start = (bf16[1,3,3,256,256]{4,3,2,1,0:T(8,128)(2,1)}, bf16[1,3,3,256,256]{4,3,2,1,0:T(8,128)(2,1)S(1)}, u32[]{:S(2)}) copy-start(bf16[1,3,3,256,256]{4,3,2,1,0:T(8,128)(2,1)S(1)} %get-tuple-element.54.refs_2_.refs_3_) | copy-start | bytes 3538948
  30.8 10.2 %collective-permute-start.4 = (bf16[1,4,96,256]{3,2,1,0:T(8,128)(2,1)S(1)}, bf16[1,4,96,256]{3,2,1,0:T(8,128)(2,1)S(1)}, u32[]{:S(2)}, u32[]{:S(2)}) collective-permute-start(bf16[1,4,96,256]{3,2,1,0:T(8,128)(2,1)S(1)} %get-tuple-element.60), channel_id=1, source_target_pairs={{0,2},{2,4},{4,6},{6,8},{8,10},{10,12},{12,14},{14,16},{16,18},{18... | collective-permute-start | bytes 589832 | tf_op jit(solution)/shard_map/ppermute | solution.py:37
  30.9 1.4 %collective-permute-start.6 = (bf16[2,1,96,256]{3,2,1,0:T(8,128)(2,1)S(1)}, bf16[2,1,96,256]{3,2,1,0:T(8,128)(2,1)S(1)}, u32[]{:S(2)}, u32[]{:S(2)}) collective-permute-start(bf16[2,1,96,256]{3,2,1,0:T(8,128)(2,1)S(1)} %get-tuple-element.49), channel_id=1, source_target_pairs={{0,1},{1,0},{2,3},{3,2},{4,5},{5,4},{6,7},{7,6},{8,9},{9,8},{10,11... | collective-permute-start | bytes 294920 | tf_op jit(solution)/shard_map/ppermute | solution.py:32
  32.2 13.3 %all-to-all-start.1 = ((f32[32,1,512]{2,1,0:T(1,128)}), f32[32,1,512]{2,1,0:T(1,128)S(1)}, u32[]{:S(2)}, u32[]{:S(2)}) async-start(f32[32,1,512]{2,1,0:T(1,128)} %get-tuple-element.51), calls=%async_computation.1 | async-start | bytes 131072 | tf_op jit(solution)/shard_map/all_to_all | solution.py:41
  38.2 4.0 %collective-permute-start.8 = (bf16[2,1,96,256]{3,2,1,0:T(8,128)(2,1)S(1)}, bf16[2,1,96,256]{3,2,1,0:T(8,128)(2,1)S(1)}, u32[]{:S(2)}, u32[]{:S(2)}) collective-permute-start(bf16[2,1,96,256]{3,2,1,0:T(8,128)(2,1)S(1)} %get-tuple-element.53), channel_id=1, source_target_pairs={{0,1},{1,0},{2,3},{3,2},{4,5},{5,4},{6,7},{7,6},{8,9},{9,8},{10,11... | collective-permute-start | bytes 294920 | tf_op jit(solution)/shard_map/ppermute | solution.py:32
  41.0 1.2 %collective-permute-start.5 = (bf16[1,1,96,256]{3,2,1,0:T(8,128)(2,1)S(1)}, bf16[1,1,96,256]{3,2,1,0:T(8,128)(2,1)S(1)}, u32[]{:S(2)}, u32[]{:S(2)}) collective-permute-start(bf16[1,1,96,256]{3,2,1,0:T(8,128)(2,1)S(1)} %constant_dynamic-slice_fusion), channel_id=1, source_target_pairs={{0,1},{1,0},{2,3},{3,2},{4,5},{5,4},{6,7},{7,6},{8,9},{9,8},{10,11... | collective-permute-start | bytes 147464 | tf_op jit(solution)/shard_map/ppermute | solution.py:32
  41.7 12.2 %collective-permute-start.7 = (bf16[1,5,96,256]{3,2,1,0:T(8,128)(2,1)}, bf16[1,5,96,256]{3,2,1,0:T(8,128)(2,1)S(1)}, u32[]{:S(2)}, u32[]{:S(2)}) collective-permute-start(bf16[1,5,96,256]{3,2,1,0:T(8,128)(2,1)} %pad_maximum_fusion.1), channel_id=1, source_target_pairs={{0,2},{2,4},{4,6},{6,8},{8,10},{10,12},{12,14},{14,16},{16,18},{18... | collective-permute-start | bytes 737288 | tf_op jit(solution)/shard_map/ppermute | solution.py:37
  45.6 1.3 %copy-start.1 = (bf16[1,3,3,256,256]{4,3,2,1,0:T(8,128)(2,1)S(1)}, bf16[1,3,3,256,256]{4,3,2,1,0:T(8,128)(2,1)}, u32[]{:S(2)}) copy-start(bf16[1,3,3,256,256]{4,3,2,1,0:T(8,128)(2,1)} %copy-done) | copy-start | bytes 3538948
  46.8 7.0 %copy-start.2 = (bf16[1,3,3,256,256]{4,3,2,1,0:T(8,128)(2,1)S(1)}, bf16[1,3,3,256,256]{4,3,2,1,0:T(8,128)(2,1)}, u32[]{:S(2)}) copy-start(bf16[1,3,3,256,256]{4,3,2,1,0:T(8,128)(2,1)} %copy-done) | copy-start | bytes 3538948

commit v17 on v16

--- a/solution.py
+++ b/solution.py
@@ -41,9 +41,54 @@
     return lax.all_to_all(copies, ("tm", "space"), 0, 0, tiled=True)
 
 
+def group_sizes(peers):
+    sizes = []
+    while peers > 1:
+        sizes.append(min(4, peers))
+        peers //= sizes[-1]
+    return sizes
+
+
+def slab_offsets(peers):
+    offsets, left = [0], peers
+    for ways in group_sizes(peers):
+        left //= ways
+        offsets = [(left * way) ^ offset for way in range(ways) for offset in offsets]
+    return offsets
+
+
+def slab_tables(stats):
+    peers = lax.axis_size("tm")
+    total = stats + traded(stats, "space", 1) if lax.axis_size("space") == 2 else lax.psum(stats, "space")
+    held, left = [total], peers
+    for ways in group_sizes(peers):
+        left //= ways
+        block = held[0] if len(held) == 1 else jnp.concatenate(held, axis=0)
+        held = [block] + [traded(block, "tm", left * way) for way in range(1, ways)]
+    return total, held
+
+
+def row_halo(edges):
+    if lax.axis_size("space") == 2:
+        return [traded(edges[0], "space", 1)]
+    top, bottom = edges
+    return [shifted(bottom, "space", 1), shifted(top, "space", -1)]
+
+
+def edges_of(frames):
+    rows = frames.shape[1]
+    if lax.axis_size("space") == 2:
+        return [lax.dynamic_slice_in_dim(frames, (rows - 1) * (1 - lax.axis_index("space")), 1, axis=1)]
+    return [frames[:, :1], frames[:, rows - 1 :]]
+
+
+def chained(value):
+    return lax.ppermute(value, "tm", [(i, i + 1) for i in range(lax.axis_size("tm") - 1)])
+
+
 def slab_halo(tail, sides):
     rows = [side[-1:] for side in sides]
-    return shifted(tail[:1], "tm", 1), shifted(jnp.concatenate([tail[1:], *rows], axis=1), "tm", 1)
+    return shifted(tail[:1], "tm", 1), chained(jnp.concatenate([tail[1:], *rows], axis=1))
 
 
 def row_halo(edges):
@@ -160,6 +205,11 @@
         same = (clips[slab] == own_clip).astype(jnp.int32)
         slabs_in = slabs_in + same
         aux[slab : slab + 1] = jnp.full((1, width), same.astype(F32), F32)
+    offsets = slab_offsets(slabs)
+    for entry, offset in enumerate(offsets):
+        same = (clips[own ^ offset] == own_clip).astype(F32)
+        aux[slabs + entry : slabs + entry + 1] = jnp.full((1, width), same, F32)
+    slabs *= 2
     starting = jnp.logical_or(own == 0, clips[jnp.maximum(own - 1, 0)] != own_clip)
     aux[slabs : slabs + 1] = jnp.full((1, width), starting.astype(F32), F32)
     aux[slabs + 1 : slabs + 2] = jnp.full((1, width), slabs_in.astype(F32) * float(per_slab), F32)
@@ -174,7 +224,7 @@
     slabs, width = lax.axis_size("tm"), params[0].shape[0]
     return pl.pallas_call(
         functools.partial(setup_kernel, slabs, per_slab),
-        out_shape=[shaped((1,) + kernel.shape[1:]), shaped((slabs + 8, width), F32)],
+        out_shape=[shaped((1,) + kernel.shape[1:]), shaped((2 * slabs + 8, width), F32)],
         in_specs=[ANYWHERE] * 6 + [VMEM],
         out_specs=[VMEM, VMEM],
         scratch_shapes=[
@@ -199,9 +249,9 @@
     return values
 
 
-def half_affine(table, aux, which):
+def gathered_sums(table, aux):
     width = aux.shape[1]
-    slabs = aux.shape[0] - 8
+    slabs = (aux.shape[0] - 8) // 2
     places = table.shape[0] // slabs
     sums = []
     for k in range(2):
@@ -212,6 +262,24 @@
         while len(parts) > 1:
             parts = [sum(parts[i : i + 2]) for i in range(0, len(parts), 2)]
         sums += parts
+    return sums
+
+
+def traded_sums(tables, aux):
+    width = aux.shape[1]
+    sums = [jnp.zeros((1, width), F32)] * 2
+    entry = (aux.shape[0] - 8) // 2
+    for table in tables:
+        mask = aux[entry : entry + table.shape[0]]
+        entry += table.shape[0]
+        sums = [
+            total + jnp.sum(table[:, k * width : (k + 1) * width] * mask, axis=0, keepdims=True) for k, total in enumerate(sums)
+        ]
+    return sums
+
+
+def half_affine(sums, aux, which):
+    slabs = aux.shape[0] - 8
     grouped = group_total(jnp.concatenate(sums, axis=0))
     count = aux[slabs + 1 : slabs + 2]
     gain = aux[slabs + 2 + 2 * which : slabs + 3 + 2 * which]
@@ -261,72 +329,41 @@
     return add_stats(sums, rounded.astype(F32))
 
 
-def late_kernel(n_sides, which, aux, table, frames, *refs):
-    early_sides, late_sides = refs[:n_sides], refs[n_sides : 2 * n_sides]
-    first_taps, kernel_hbm, *refs = refs[2 * n_sides :]
-    if which == 0:
-        act_low, affine_out, more_taps, hidden, stats, edges, act_high, taps_sems = refs
-        early = late = frames
-        late_first = 0
-    else:
-        late, feats_hbm, act_low, affine_out, more_taps, out_hbm, act_high, taps_sems, out, feats, sems = refs
-        early, late_first = frames, frames.shape[0]
+def late_kernel(n_sides, aux, table, frames, *refs):
+    sides, first_taps, kernel_hbm = refs[:n_sides], refs[n_sides], refs[n_sides + 1]
+    act_low, affine_out, more_taps, hidden, stats, edges, act_high, taps_sems = refs[n_sides + 2 :]
     taps = (first_taps, more_taps)
     loads = [
-        pltpu.make_async_copy(kernel_hbm.at[i, j], more_taps.at[i - 1, j], taps_sems.at[3 * i + j])
+        pltpu.make_async_copy(kernel_hbm.at[i, j], more_taps.at[i - 1, j], taps_sems.at[3 * (i - 1) + j])
         for i in range(1, 3)
         for j in range(3)
     ]
-    if which == 1:
-        loads.append(pltpu.make_async_copy(feats_hbm.at[pl.ds(2, feats.shape[0])], feats, taps_sems.at[0]))
     for copy in loads:
         copy.start()
     n_rows, width = frames.shape[1], frames.shape[3]
     low, high = act_low.shape[0], act_high.shape[0]
-    affine = half_affine(table, aux, which)
+    affine = half_affine(gathered_sums(table, aux), aux, 0)
     for k in range(2):
         affine_out[k : k + 1] = affine[k]
     planes = [(act_low, f) for f in range(low)] + [(act_high, f) for f in range(high)]
     for frame, (act, index) in enumerate(planes):
         for row in range(n_rows + 2):
-            if which == 0 or frame < 2:
-                value = extended_row(early, early_sides, frame, row)
-            else:
-                value = extended_row(late, late_sides, frame - late_first, row)
-            act[index, row] = normed(value, affine)
-    sums = no_stats(width)
-    stores = []
+            act[index, row] = normed(extended_row(frames, sides, frame, row), affine)
     for copy in loads:
         copy.wait()
+    sums = no_stats(width)
     for frame in range(high):
         for row, value in conv_rows(planes[frame : frame + 3], taps):
-            if which == 0:
-                sums = put_hidden(hidden, frame, row, value, sums)
-            else:
-                out[frame, row] = feats[frame, row].astype(F32) + value
-        if which == 0:
-            send_rows(hidden, frame, edges)
-        else:
-            stores.append(pltpu.make_async_copy(out.at[frame], out_hbm.at[low + frame], sems.at[frame]))
-            stores[-1].start()
-    if which == 0:
-        for k in range(2):
-            stats[k] = sums[k]
-    for store in stores:
-        store.wait()
-
-
-def early_kernel(n_sides, which, aux, first, second, *refs):
+            sums = put_hidden(hidden, frame, row, value, sums)
+        send_rows(hidden, frame, edges)
+    for k in range(2):
+        stats[k] = sums[k]
+
+
+def early_kernel(n_sides, aux, first, second, *refs):
     corners, (act_low, affine_in, *taps), refs = refs[:n_sides], refs[n_sides : n_sides + 4], refs[n_sides + 4 :]
-    if which == 0:
-        late_stats, kernel_hbm, hidden, edges, copies, next_taps, act_before, stats, sems = refs
-        sums = late_stats[0], late_stats[1]
-        loads = [pltpu.make_async_copy(kernel_hbm.at[0], next_taps.at[0], sems.at[0])]
-    else:
-        feats_hbm, _, out_hbm, act_before, out, feats, sems = refs
-        loads = [pltpu.make_async_copy(feats_hbm.at[pl.ds(0, 2)], feats, sems.at[2])]
-    for load in loads:
-        load.start()
+    late_stats, hidden, edges, stats, act_before = refs
+    sums = late_stats[0], late_stats[1]
     slabs = aux.shape[0] - 8
     starting = aux[slabs : slabs + 1] != 0.0
     affine = affine_in[0:1], affine_in[1:2]
@@ -340,24 +377,43 @@
             value = normed(raw, affine).astype(F32)
             act_before[frame, row] = jnp.where(starting, act_low[0, row].astype(F32), value).astype(BF16)
     planes = [(act_before, 0), (act_before, 1)] + [(act_low, f) for f in range(act_low.shape[0])]
-    if which == 1:
-        loads[0].wait()
-    stores = []
     for frame in range(2):
         for row, value in conv_rows(planes[frame : frame + 3], taps):
-            if which == 0:
-                sums = put_hidden(hidden, frame, row, value, sums)
+            sums = put_hidden(hidden, frame, row, value, sums)
+        send_rows(hidden, frame, edges)
+    store_stats(stats, sums)
+
+
+def last_kernel(n_tables, n_sides, aux, *refs):
+    tables, early, late, refs = refs[:n_tables], refs[n_tables], refs[n_tables + 1], refs[n_tables + 2 :]
+    sides_early, sides_late = refs[:n_sides], refs[n_sides : 2 * n_sides]
+    before, *corners = refs[2 * n_sides : 3 * n_sides + 1]
+    taps, feats, out_hbm, act, out, sems = refs[3 * n_sides + 1 :]
+    stores = [pltpu.make_async_copy(out.at[f], out_hbm.at[f], sems.at[f]) for f in range(out.shape[0])]
+    slabs = aux.shape[0] - 8
+    starting = aux[slabs : slabs + 1] != 0.0
+    affine = half_affine(traded_sums(tables, aux), aux, 1)
+    n_frames, n_rows = out.shape[:2]
+
+    def fill(frame):
+        for row in range(n_rows + 2):
+            if frame < 2:
+                value = normed(extended_row(before, corners, frame, row), affine).astype(F32)
+                act[frame, row] = jnp.where(starting, act[2, row].astype(F32), value).astype(BF16)
+            elif frame < 4:
+                act[frame, row] = normed(extended_row(early, sides_early, frame - 2, row), affine)
             else:
-                out[frame, row] = feats[frame, row].astype(F32) + value
-        if which == 0:
-            send_rows(hidden, frame, edges)
-        else:
-            stores.append(pltpu.make_async_copy(out.at[frame], out_hbm.at[frame], sems.at[frame]))
-            stores[-1].start()
-    if which == 0:
-        store_stats(stats, sums)
-        store_copies(copies, stats)
-        loads[0].wait()
+                act[frame, row] = normed(extended_row(late, sides_late, frame - 4, row), affine)
+
+    for frame in range(2, n_frames + 2):
+        fill(frame)
+    for frame in list(range(2, n_frames)) + [0, 1]:
+        if frame == 0:
+            fill(0)
+            fill(1)
+        for row, value in conv_rows([(act, frame + i) for i in range(3)], (taps.at[:1], taps.at[1:])):
+            out[frame, row] = feats[frame, row].astype(F32) + value
+        stores[frame].start()
     for store in stores:
         store.wait()
 
@@ -371,7 +427,7 @@
         scratch_shapes=scratch,
         input_output_aliases=aliases or {},
         compiler_params=vmem_params(),
-        cost_estimate=pl.CostEstimate(flops=weight << 32, bytes_accessed=1 << 20, transcendentals=1 << 20),
+        cost_estimate=pl.CostEstimate(flops=weight, bytes_accessed=1 << 20, transcendentals=1 << 20),
     )(*operands)
 
 
@@ -383,10 +439,9 @@
     plane = (n_rows + 2, cols, width)
     act = pltpu.VMEM((2,) + plane, BF16)
     act_late = pltpu.VMEM((late,) + plane, BF16)
+    work = 54 * feats.size // n_frames * width
     late_shapes = [shaped((2,) + plane), shaped((2, width), F32), shaped((2,) + kernel_one.shape[1:])]
     hidden_shapes = [shaped((late, n_rows, cols, width)), shaped((2, 8, width), F32), shaped(edge_shape(feats, late))]
-    first_taps = shaped((1,) + kernel_one.shape[1:])
-    taps_sems = pltpu.SemaphoreType.DMA((9,))
 
     frames, tail, edges, copies, mark = entry_call(feats)
     table = stats_table(copies)
@@ -396,57 +451,37 @@
     corners = row_halo(edges_of(first))
     taps, aux = setup_call(kernel_one, clip_ids, params, per_slab, mark)
     aux, *corners = lax.optimization_barrier((aux, *corners))
-    operands = [aux, table, frames, *sides, *sides, taps, in_hbm(kernel_one)]
-    act_low, affine, more_taps, hidden_late, stats, edges_late = call(
-        functools.partial(late_kernel, n_sides, 0),
+    operands = [aux, table, frames, *sides, taps, in_hbm(kernel_one)]
+    act_low, affine, more_taps, hidden_late, stats, edges = call(
+        functools.partial(late_kernel, n_sides),
         late_shapes + hidden_shapes,
-        [act_late, taps_sems],
-        32,
+        [act_late, pltpu.SemaphoreType.DMA((6,))],
+        1 << 37,
         operands,
         outside=(len(operands) - 1,),
     )
-    operands = [aux, first, second, *corners, act_low, affine, taps, more_taps, stats, in_hbm(kernel_two)]
-    hidden_early, edges, copies, taps = call(
-        functools.partial(early_kernel, n_sides, 0),
-        [shaped((2, n_rows, cols, width)), shaped(edge_shape(feats, 2)), copies_shape(width), first_taps],
-        [act, pltpu.VMEM((1, 2 * width), F32), pltpu.SemaphoreType.DMA((1,))],
-        2,
-        operands,
-        outside=(len(operands) - 1,),
-    )
-
-    table = stats_table(copies)
-    sides_late = row_halo(edges_late)
-    tail, edges = lax.optimization_barrier((hidden_late[late - 2 :], edges))
-    first, second = slab_halo(tail, sides_late)
-    corners = row_halo(edges_of(first))
-    aux, *corners = lax.optimization_barrier((aux, *corners))
-    operands = [aux, table, hidden_early, *row_halo(edges), *sides_late, taps, in_hbm(kernel_two), hidden_late, in_hbm(feats)]
-    act_low, affine, more_taps, out = call(
-        functools.partial(late_kernel, n_sides, 1),
-        late_shapes + [shaped(feats.shape, F32)],
-        [
-            act_late,
-            taps_sems,
-            pltpu.VMEM((late, n_rows, cols, width), F32),
-            pltpu.VMEM((late, n_rows, cols, width), BF16),
-            pltpu.SemaphoreType.DMA((late,)),
-        ],
-        32,
-        operands,
-        out_specs=[VMEM, VMEM, VMEM, ANYWHERE],
-        outside=(len(operands) - 3, len(operands) - 1),
-    )
-    operands = [aux, first, second, *corners, act_low, affine, taps, more_taps, in_hbm(feats), out]
+    before = shifted(hidden_late[late - 2 :], "tm", 1)
+    sides_late = row_halo(edges)
+    hidden_early, edges, stats = call(
+        functools.partial(early_kernel, n_sides),
+        [shaped((2, n_rows, cols, width)), shaped(edge_shape(feats, 2)), shaped((1, 2 * width), F32)],
+        [act],
+        2 * work,
+        [aux, first, second, *corners, act_low, affine, taps, more_taps, stats],
+    )
+
+    sides_early = row_halo(edges)
+    _, tables = slab_tables(stats)
+    before, tables[0] = lax.optimization_barrier((before, tables[0]))
+    corners = row_halo(edges_of(before))
+    operands = [aux, *tables, hidden_early, hidden_late, *sides_early, *sides_late, before, *corners, kernel_two, frames]
     return call(
-        functools.partial(early_kernel, n_sides, 1),
+        functools.partial(last_kernel, len(tables), n_sides),
         shaped(feats.shape, F32),
-        [act, pltpu.VMEM((2, n_rows, cols, width), F32), pltpu.VMEM((2, n_rows, cols, width), BF16), pltpu.SemaphoreType.DMA((3,))],
-        2,
+        [pltpu.VMEM((n_frames + 2,) + plane, BF16), pltpu.VMEM(feats.shape, F32), pltpu.SemaphoreType.DMA((n_frames,))],
+        n_frames * work,
         operands,
         out_specs=ANYWHERE,
-        aliases={len(operands) - 1: 0},
-        outside=(len(operands) - 2,),
     )
 
 

time: 58.9 us -> 49.4 us (0.84)
  waiting for transfers between devices: 18.6 us -> 11.2 us
  starting transfers between devices: 14.6 us -> 19.8 us
  Pallas kernels: 22 us -> 17.9 us
  local copies, waits for them, and re-layouts: 2.38 us -> 0.05 us
  other arithmetic: 0.74 us -> 0.04 us
    ppermute x5 -> x12, starting transfers between devices: 0.71 us -> 9.75 us  [traded(): lax.ppermute(value, axis, [(i, i ^ mask) for i in range(lax.axis_size(axi...]
    ppermute x4 -> x2, waiting for transfers between devices: 10.3 us -> 2.97 us  [shifted(): lax.ppermute(value, axis, [(i, (i + step) % peers) for i in range(peers)])]
    all_to_all x2 -> x1, starting transfers between devices: 10.8 us -> 4.92 us  [stats_table(): return lax.all_to_all(copies, ('tm', 'space'), 0, 0, tiled=True)]
    pallas_call x4 -> x3, Pallas kernels: 18.7 us -> 14.6 us  [call(): pl.pallas_call(kernel, out_shape=outs, in_specs=[ANYWHERE if k in (aliase...]
    all_to_all x2 -> x1, waiting for transfers between devices: 5.44 us -> 1.6 us  [stats_table(): return lax.all_to_all(copies, ('tm', 'space'), 0, 0, tiled=True)]
    ppermute x5 -> x12, waiting for transfers between devices: 2.9 us -> 6.63 us  [traded(): lax.ppermute(value, axis, [(i, i ^ mask) for i in range(lax.axis_size(axi...]
    unnamed x6 -> x2, local copies, waits for them, and re-layouts: 2.3 us -> 0.01 us
    ppermute x0 -> x1, starting transfers between devices: none -> 1.63 us  [chained(): lax.ppermute(value, 'tm', [(i, i + 1) for i in range(lax.axis_size('tm')...]
  transfers between devices with their start and end apart: 11 -> 16, of which waited for: 9 -> 9; matrix products, arithmetic and copies ran while one was open for 1% -> 0% of each run, Pallas kernels for 20% -> 19%
where the time goes in v17:
time: 49.4 us; the launch traced here: 49.1 us
  starting transfers between devices  19.8 us (40%)
  Pallas kernels  17.9 us (36%)
  waiting for transfers between devices  11.2 us (23%)
    pallas_call x3, Pallas kernels, call(): pl.pallas_call(kernel, out_shape=outs, in_specs=[ANYWHERE if k in (aliase...  14.6 us
    ppermute x12, starting transfers between devices, traded(): lax.ppermute(value, axis, [(i, i ^ mask) for i in range(lax.axis_size(axi...  9.75 us
    ppermute x12, waiting for transfers between devices, traded(): lax.ppermute(value, axis, [(i, i ^ mask) for i in range(lax.axis_size(axi...  6.63 us
    all_to_all x1, starting transfers between devices, stats_table(): return lax.all_to_all(copies, ('tm', 'space'), 0, 0, tiled=True)  4.92 us
    ppermute x2, starting transfers between devices, shifted(): lax.ppermute(value, axis, [(i, (i + step) % peers) for i in range(peers)])  3.47 us
    ppermute x2, waiting for transfers between devices, shifted(): lax.ppermute(value, axis, [(i, (i + step) % peers) for i in range(peers)])  2.97 us
    pallas_call x1, Pallas kernels, entry_call(): pl.pallas_call(entry_kernel, out_shape=outs, in_specs=[ANYWHERE], out_spe...  1.95 us
    ppermute x1, starting transfers between devices, chained(): lax.ppermute(value, 'tm', [(i, i + 1) for i in range(lax.axis_size('tm')...  1.63 us
  transfers between devices with their start and end apart: 16, of which 9 were waited for; matrix products, arithmetic and copies ran while one was open for 0% of the time, Pallas kernels for 19%

profile of v17, /device:TPU:0, one launch (start us, length us, event | category | flops | bytes accessed | tf_op | source)
XLA Modules:
  0.0 49.1 jit_solution(5697279414557065784)
XLA Ops:
  0.0 1.9 %shard_map.82 = (bf16[4,4,96,256]{3,2,1,0:T(8,128)(2,1)S(1)}, bf16[2,4,96,256]{3,2,1,0:T(8,128)(2,1)S(1)}, bf16[4,1,96,256]{3,2,1,0:T(8,128)(2,1)S(1)}, f32[32,1,512]{2,1,0:T(1,128)}, f32[8,128]{1,0:T(8,128)S(1)}) custom-call(bf16[4,4,96,256]{3,2,1,0:T(8,128)(2,1)} %feats_hbm.1), custom_call_target="tpu_custom_call" | custom-call | flops 1572864 | bytes 1572864 | tf_op jit(solution)/shard_map/pallas_call | solution.py:181
  2.0 3.0 %collective-permute-start = (bf16[1,4,96,256]{3,2,1,0:T(8,128)(2,1)S(1)}, bf16[1,4,96,256]{3,2,1,0:T(8,128)(2,1)S(1)}, u32[]{:S(2)}, u32[]{:S(2)}) collective-permute-start(bf16[1,4,96,256]{3,2,1,0:T(8,128)(2,1)S(1)} %get-tuple-element.46), channel_id=1, source_target_pairs={{0,2},{2,4},{4,6},{6,8},{8,10},{10,12},{12,14},{14,16},{16,18},{18... | collective-permute-start | bytes 589832 | tf_op jit(solution)/shard_map/ppermute | solution.py:37
  5.0 4.9 %all-to-all-start = ((f32[32,1,512]{2,1,0:T(1,128)}), f32[32,1,512]{2,1,0:T(1,128)S(1)}, u32[]{:S(2)}, u32[]{:S(2)}) async-start(f32[32,1,512]{2,1,0:T(1,128)} %get-tuple-element.29), calls=%async_computation | async-start | bytes 131072 | tf_op jit(solution)/shard_map/all_to_all | solution.py:41
  9.9 0.3 collective-permute-start.2
  10.2 1.4 %shard_map.83 = (bf16[1,3,3,256,256]{4,3,2,1,0:T(8,128)(2,1)S(1)}, f32[40,256]{1,0:T(8,128)S(1)}) custom-call(bf16[3,3,3,256,256]{4,3,2,1,0:T(8,128)(2,1)} %refs_2_.1, s32[16]{0:T(128)} %clips_hbm.1, f32[1,256]{1,0:T(1,128)} %bitcast.4, f32[1,256]{1,0:T(1,128)} %bitcast.5, f32[1,256]{1,0:T(1,128)} %bitcast.6, f32[1,256]{1,0:T(1,128)} %bitcast.7, ...), custom_call_target="tpu_custom_call" | custom-call | flops 1073741824 | bytes 65536 | tf_op jit(solution)/shard_map/pallas_call | solution.py:225
  11.6 2.4 %collective-permute-done.first = bf16[1,4,96,256]{3,2,1,0:T(8,128)(2,1)S(1)} collective-permute-done((bf16[1,4,96,256]{3,2,1,0:T(8,128)(2,1)S(1)}, bf16[1,4,96,256]{3,2,1,0:T(8,128)(2,1)S(1)}, u32[]{:S(2)}, u32[]{:S(2)}) %collective-permute-start) | collective-permute-done | bytes 196640 | tf_op jit(solution)/shard_map/ppermute | solution.py:37
  14.0 0.0 collective-permute-start.1
  14.0 0.0 collective-permute-done.2.refs_0_
  14.1 1.6 %collective-permute-start.4 = (bf16[1,5,96,256]{3,2,1,0:T(8,128)(2,1)S(1)}, bf16[1,5,96,256]{3,2,1,0:T(8,128)(2,1)S(1)}, u32[]{:S(2)}, u32[]{:S(2)}) collective-permute-start(bf16[1,5,96,256]{3,2,1,0:T(8,128)(2,1)S(1)} %pad_maximum_fusion), channel_id=1, source_target_pairs={{0,2},{2,4},{4,6},{6,8},{8,10},{10,12},{12,14},{14,16},{16,18},{18... | collective-permute-start | bytes 737288 | tf_op jit(solution)/shard_map/ppermute | solution.py:86
  15.7 0.0 collective-permute-done.1.refs_0_
  15.7 1.6 %all-to-all-done.table = f32[32,1,512]{2,1,0:T(1,128)S(1)} async-done(((f32[32,1,512]{2,1,0:T(1,128)}), f32[32,1,512]{2,1,0:T(1,128)S(1)}, u32[]{:S(2)}, u32[]{:S(2)}) %all-to-all-start) | async-done | bytes 65568 | tf_op jit(solution)/shard_map/all_to_all | solution.py:41
  17.3 4.7 %shard_map.84 = (bf16[2,6,96,256]{3,2,1,0:T(8,128)(2,1)S(1)}, f32[2,256]{1,0:T(2,128)S(1)}, bf16[2,3,3,256,256]{4,3,2,1,0:T(8,128)(2,1)S(1)}, bf16[2,4,96,256]{3...) custom-call(f32[40,256]{1,0:T(8,128)S(1)} %get-tuple-element.28.aux, ...), custom_call_target="tpu_custom_call" | custom-call | flops 137438953472 | bytes 1048576 | tf_op jit(solution)/shard_map/pallas_call | solution.py:422
  22.0 0.5 collective-permute-start.3
  22.5 0.0 collective-permute-done.4.second
  22.5 0.0 copy-start
  22.5 3.0 %shard_map.85 = (bf16[2,4,96,256]{3,2,1,0:T(8,128)(2,1)S(1)}, bf16[2,1,96,256]{3,2,1,0:T(8,128)(2,1)S(1)}, f32[1,512]{1,0:T(1,128)S(1)}) custom-call(f32[40,256]{1,0:T(8,128)S(1)} %get-tuple-element.28.aux, bf16[1,4,96,256]{3,2,1,0:T(8,128)(2,1)S(1)} %collective-permute-done.first, bf16[1,5,96,256]{3,2,1,0:T(8,128)(2,1)S(1)} %collective-permute-done.4.second, ...), custom_call_target="tpu_custom_call" | custom-call | flops 2717908992 | bytes 1048576 | tf_op jit(solution)/shard_map/pallas_call | solution.py:422
  25.6 0.1 collective-permute-start.5
  25.6 1.1 %collective-permute-done.5 = f32[1,512]{1,0:T(1,128)S(1)} collective-permute-done((f32[1,512]{1,0:T(1,128)S(1)}, f32[1,512]{1,0:T(1,128)S(1)}, u32[]{:S(2)}, u32[]{:S(2)}) %collective-permute-start.5) | collective-permute-done | bytes 2080 | tf_op jit(solution)/shard_map/ppermute | solution.py:32
  26.8 5.1 %collective-permute-start.8 = (f32[1,512]{1,0:T(1,128)S(1)}, f32[1,512]{1,0:T(1,128)S(1)}, u32[]{:S(2)}, u32[]{:S(2)}) collective-permute-start(f32[1,512]{1,0:T(1,128)S(1)} %add.8), channel_id=1, source_target_pairs={{0,24},{2,26},{4,28},{6,30},{8,16},{10,18},{12,20},{14,22},{16,8},... | collective-permute-start | bytes 6152 | tf_op jit(solution)/shard_map/ppermute | solution.py:32
  31.9 0.0 collective-permute-start.7
  31.9 0.6 %collective-permute-start.6 = (f32[1,512]{1,0:T(1,128)S(1)}, f32[1,512]{1,0:T(1,128)S(1)}, u32[]{:S(2)}, u32[]{:S(2)}) collective-permute-start(f32[1,512]{1,0:T(1,128)S(1)} %add.8), channel_id=1, source_target_pairs={{0,8},{2,10},{4,12},{6,14},{8,0},{10,2},{12,4},{14,6},{16,24},{18,... | collective-permute-start | bytes 6152 | tf_op jit(solution)/shard_map/ppermute | solution.py:32
  32.5 0.0 collective-permute-start.13
  32.5 0.9 %collective-permute-done.8 = f32[1,512]{1,0:T(1,128)S(1)} collective-permute-done((f32[1,512]{1,0:T(1,128)S(1)}, f32[1,512]{1,0:T(1,128)S(1)}, u32[]{:S(2)}, u32[]{:S(2)}) %collective-permute-start.8) | collective-permute-done | bytes 2080 | tf_op jit(solution)/shard_map/ppermute | solution.py:32
  33.5 0.0 collective-permute-start.12
  33.5 2.9 %collective-permute-done.7 = f32[1,512]{1,0:T(1,128)S(1)} collective-permute-done((f32[1,512]{1,0:T(1,128)S(1)}, f32[1,512]{1,0:T(1,128)S(1)}, u32[]{:S(2)}, u32[]{:S(2)}) %collective-permute-start.7) | collective-permute-done | bytes 2080 | tf_op jit(solution)/shard_map/ppermute | solution.py:32
  36.4 0.0 collective-permute-done.6
  36.4 0.6 %collective-permute-done.3.refs_8_ = bf16[2,4,96,256]{3,2,1,0:T(8,128)(2,1)S(1)} collective-permute-done((bf16[2,4,96,256]{3,2,1,0:T(8,128)(2,1)S(1)}, bf16[2,4,96,256]{3,2,1,0:T(8,128)(2,1)S(1)}, u32[]{:S(2)}, u32[]{:S(2)}) %collective-permute-start.3) | collective-permute-done | bytes 393248 | tf_op jit(solution)/shard_map/ppermute | solution.py:37
  37.0 0.1 collective-permute-start.14
  37.1 1.1 %collective-permute-start.11 = (f32[4,512]{1,0:T(4,128)S(1)}, f32[4,512]{1,0:T(4,128)S(1)}, u32[]{:S(2)}, u32[]{:S(2)}) collective-permute-start(f32[4,512]{1,0:T(4,128)S(1)} %pad_maximum_fusion.1.refs_0_), channel_id=1, source_target_pairs={{0,6},{2,4},{4,2},{6,0},{8,14},{10,12},{12,10},{14,8},{16,22},{18,... | collective-permute-start | bytes 24584 | tf_op jit(solution)/shard_map/ppermute | solution.py:32
  38.2 0.0 collective-permute-start.10
  38.2 0.0 collective-permute-done.13.refs_7_
  38.2 2.4 %collective-permute-start.9 = (f32[4,512]{1,0:T(4,128)S(1)}, f32[4,512]{1,0:T(4,128)S(1)}, u32[]{:S(2)}, u32[]{:S(2)}) collective-permute-start(f32[4,512]{1,0:T(4,128)S(1)} %pad_maximum_fusion.1.refs_0_), channel_id=1, source_target_pairs={{0,2},{2,0},{4,6},{6,4},{8,10},{10,8},{12,14},{14,12},{16,18},{18,... | collective-permute-start | bytes 24584 | tf_op jit(solution)/shard_map/ppermute | solution.py:32
  40.6 1.1 %collective-permute-done.11.refs_3_ = f32[4,512]{1,0:T(4,128)S(1)} collective-permute-done((f32[4,512]{1,0:T(4,128)S(1)}, f32[4,512]{1,0:T(4,128)S(1)}, u32[]{:S(2)}, u32[]{:S(2)}) %collective-permute-start.11) | collective-permute-done | bytes 8224 | tf_op jit(solution)/shard_map/ppermute | solution.py:32
  41.7 0.2 collective-permute-done.10.refs_2_
  41.9 0.4 collective-permute-done.9.refs_1_
  42.3 0.0 collective-permute-done.12.refs_6_
  42.3 0.0 collective-permute-done.14.refs_9_
  42.3 0.0 copy-done
  42.3 6.8 %shard_map.86 = f32[4,4,96,256]{3,2,1,0:T(8,128)} custom-call(f32[40,256]{1,0:T(8,128)S(1)} %get-tuple-element.28.aux, f32[4,512]{1,0:T(4,128)S(1)} %pad_maximum_fusion.1.refs_0_, f32[4,512]{1,0:T(4,128)S(1)} %collective-permute-done.9.refs_1_, f32[4,512]{1,0:T(4,128)S(1)} %collective-permute-done.10.refs_2_, f32[4,512]{1,0:T(4,128)S(1)} %collective-permute-done.11.refs_3_, ...), custom_call_target="tpu_custom_call" | custom-call | flops 5435817984 | bytes 1048576 | tf_op jit(solution)/shard_map/pallas_call | solution.py:422
  (7 shorter events, 0.1 us)
Async XLA Ops:
  2.0 12.0 %collective-permute-start = (bf16[1,4,96,256]{3,2,1,0:T(8,128)(2,1)S(1)}, bf16[1,4,96,256]{3,2,1,0:T(8,128)(2,1)S(1)}, u32[]{:S(2)}, u32[]{:S(2)}) collective-permute-start(bf16[1,4,96,256]{3,2,1,0:T(8,128)(2,1)S(1)} %get-tuple-element.46), channel_id=1, source_target_pairs={{0,2},{2,4},{4,6},{6,8},{8,10},{10,12},{12,14},{14,16},{16,18},{18... | collective-permute-start | bytes 589832 | tf_op jit(solution)/shard_map/ppermute | solution.py:37
  5.0 12.3 %all-to-all-start = ((f32[32,1,512]{2,1,0:T(1,128)}), f32[32,1,512]{2,1,0:T(1,128)S(1)}, u32[]{:S(2)}, u32[]{:S(2)}) async-start(f32[32,1,512]{2,1,0:T(1,128)} %get-tuple-element.29), calls=%async_computation | async-start | bytes 131072 | tf_op jit(solution)/shard_map/all_to_all | solution.py:41
  9.9 4.1 %collective-permute-start.2 = (bf16[4,1,96,256]{3,2,1,0:T(8,128)(2,1)S(1)}, bf16[4,1,96,256]{3,2,1,0:T(8,128)(2,1)S(1)}, u32[]{:S(2)}, u32[]{:S(2)}) collective-permute-start(bf16[4,1,96,256]{3,2,1,0:T(8,128)(2,1)S(1)} %get-tuple-element.31), channel_id=1, source_target_pairs={{0,1},{1,0},{2,3},{3,2},{4,5},{5,4},{6,7},{7,6},{8,9},{9,8},{10,11... | collective-permute-start | bytes 589832 | tf_op jit(solution)/shard_map/ppermute | solution.py:32
  14.0 1.7 %collective-permute-start.1 = (bf16[1,1,96,256]{3,2,1,0:T(8,128)(2,1)S(1)}, bf16[1,1,96,256]{3,2,1,0:T(8,128)(2,1)S(1)}, u32[]{:S(2)}, u32[]{:S(2)}) collective-permute-start(bf16[1,1,96,256]{3,2,1,0:T(8,128)(2,1)S(1)} %constant_dynamic-slice_fusion.1), channel_id=1, source_target_pairs={{0,1},{1,0},{2,3},{3,2},{4,5},{5,4},{6,7},{7,6},{8,9},{9,8},{10,11... | collective-permute-start | bytes 147464 | tf_op jit(solution)/shard_map/ppermute | solution.py:32
  14.1 8.5 %collective-permute-start.4 = (bf16[1,5,96,256]{3,2,1,0:T(8,128)(2,1)S(1)}, bf16[1,5,96,256]{3,2,1,0:T(8,128)(2,1)S(1)}, u32[]{:S(2)}, u32[]{:S(2)}) collective-permute-start(bf16[1,5,96,256]{3,2,1,0:T(8,128)(2,1)S(1)} %pad_maximum_fusion), channel_id=1, source_target_pairs={{0,2},{2,4},{4,6},{6,8},{8,10},{10,12},{12,14},{14,16},{16,18},{18... | collective-permute-start | bytes 737288 | tf_op jit(solution)/shard_map/ppermute | solution.py:86
  22.0 14.9 %collective-permute-start.3 = (bf16[2,4,96,256]{3,2,1,0:T(8,128)(2,1)S(1)}, bf16[2,4,96,256]{3,2,1,0:T(8,128)(2,1)S(1)}, u32[]{:S(2)}, u32[]{:S(2)}) collective-permute-start(bf16[2,4,96,256]{3,2,1,0:T(8,128)(2,1)S(1)} %get-tuple-element.33.refs_5_), channel_id=1, source_target_pairs={{0,2},{2,4},{4,6},{6,8},{8,10},{10,12},{12,14},{14,16},{16,18},{18... | collective-permute-start | bytes 1179656 | tf_op jit(solution)/shard_map/ppermute | solution.py:37
  22.5 19.7 %copy-start = (bf16[3,3,3,256,256]{4,3,2,1,0:T(8,128)(2,1)S(1)}, bf16[3,3,3,256,256]{4,3,2,1,0:T(8,128)(2,1)}, u32[]{:S(2)}) copy-start(bf16[3,3,3,256,256]{4,3,2,1,0:T(8,128)(2,1)} %refs_10_.1) | copy-start | bytes 10616836
  25.6 1.2 %collective-permute-start.5 = (f32[1,512]{1,0:T(1,128)S(1)}, f32[1,512]{1,0:T(1,128)S(1)}, u32[]{:S(2)}, u32[]{:S(2)}) collective-permute-start(f32[1,512]{1,0:T(1,128)S(1)} %get-tuple-element.39), channel_id=1, source_target_pairs={{0,1},{1,0},{2,3},{3,2},{4,5},{5,4},{6,7},{7,6},{8,9},{9,8},{10,11... | collective-permute-start | bytes 6152 | tf_op jit(solution)/shard_map/ppermute | solution.py:32
  26.8 6.7 %collective-permute-start.8 = (f32[1,512]{1,0:T(1,128)S(1)}, f32[1,512]{1,0:T(1,128)S(1)}, u32[]{:S(2)}, u32[]{:S(2)}) collective-permute-start(f32[1,512]{1,0:T(1,128)S(1)} %add.8), channel_id=1, source_target_pairs={{0,24},{2,26},{4,28},{6,30},{8,16},{10,18},{12,20},{14,22},{16,8},... | collective-permute-start | bytes 6152 | tf_op jit(solution)/shard_map/ppermute | solution.py:32
  31.9 4.5 %collective-permute-start.7 = (f32[1,512]{1,0:T(1,128)S(1)}, f32[1,512]{1,0:T(1,128)S(1)}, u32[]{:S(2)}, u32[]{:S(2)}) collective-permute-start(f32[1,512]{1,0:T(1,128)S(1)} %add.8), channel_id=1, source_target_pairs={{0,16},{2,18},{4,20},{6,22},{8,24},{10,26},{12,28},{14,30},{16,0},... | collective-permute-start | bytes 6152 | tf_op jit(solution)/shard_map/ppermute | solution.py:32
  31.9 4.5 %collective-permute-start.6 = (f32[1,512]{1,0:T(1,128)S(1)}, f32[1,512]{1,0:T(1,128)S(1)}, u32[]{:S(2)}, u32[]{:S(2)}) collective-permute-start(f32[1,512]{1,0:T(1,128)S(1)} %add.8), channel_id=1, source_target_pairs={{0,8},{2,10},{4,12},{6,14},{8,0},{10,2},{12,4},{14,6},{16,24},{18,... | collective-permute-start | bytes 6152 | tf_op jit(solution)/shard_map/ppermute | solution.py:32
  32.5 5.7 %collective-permute-start.13 = (bf16[2,1,96,256]{3,2,1,0:T(8,128)(2,1)S(1)}, bf16[2,1,96,256]{3,2,1,0:T(8,128)(2,1)S(1)}, u32[]{:S(2)}, u32[]{:S(2)}) collective-permute-start(bf16[2,1,96,256]{3,2,1,0:T(8,128)(2,1)S(1)} %get-tuple-element.43), channel_id=1, source_target_pairs={{0,1},{1,0},{2,3},{3,2},{4,5},{5,4},{6,7},{7,6},{8,9},{9,8},{10,11... | collective-permute-start | bytes 294920 | tf_op jit(solution)/shard_map/ppermute | solution.py:32
  33.5 8.8 %collective-permute-start.12 = (bf16[2,1,96,256]{3,2,1,0:T(8,128)(2,1)S(1)}, bf16[2,1,96,256]{3,2,1,0:T(8,128)(2,1)S(1)}, u32[]{:S(2)}, u32[]{:S(2)}) collective-permute-start(bf16[2,1,96,256]{3,2,1,0:T(8,128)(2,1)S(1)} %get-tuple-element.42), channel_id=1, source_target_pairs={{0,1},{1,0},{2,3},{3,2},{4,5},{5,4},{6,7},{7,6},{8,9},{9,8},{10,11... | collective-permute-start | bytes 294920 | tf_op jit(solution)/shard_map/ppermute | solution.py:32
  37.0 5.3 %collective-permute-start.14 = (bf16[2,1,96,256]{3,2,1,0:T(8,128)(2,1)S(1)}, bf16[2,1,96,256]{3,2,1,0:T(8,128)(2,1)S(1)}, u32[]{:S(2)}, u32[]{:S(2)}) collective-permute-start(bf16[2,1,96,256]{3,2,1,0:T(8,128)(2,1)S(1)} %constant_dynamic-slice_fusion), channel_id=1, source_target_pairs={{0,1},{1,0},{2,3},{3,2},{4,5},{5,4},{6,7},{7,6},{8,9},{9,8},{10,11... | collective-permute-start | bytes 294920 | tf_op jit(solution)/shard_map/ppermute | solution.py:32
  37.1 4.6 %collective-permute-start.11 = (f32[4,512]{1,0:T(4,128)S(1)}, f32[4,512]{1,0:T(4,128)S(1)}, u32[]{:S(2)}, u32[]{:S(2)}) collective-permute-start(f32[4,512]{1,0:T(4,128)S(1)} %pad_maximum_fusion.1.refs_0_), channel_id=1, source_target_pairs={{0,6},{2,4},{4,2},{6,0},{8,14},{10,12},{12,10},{14,8},{16,22},{18,... | collective-permute-start | bytes 24584 | tf_op jit(solution)/shard_map/ppermute | solution.py:32
  38.2 3.7 %collective-permute-start.10 = (f32[4,512]{1,0:T(4,128)S(1)}, f32[4,512]{1,0:T(4,128)S(1)}, u32[]{:S(2)}, u32[]{:S(2)}) collective-permute-start(f32[4,512]{1,0:T(4,128)S(1)} %pad_maximum_fusion.1.refs_0_), channel_id=1, source_target_pairs={{0,4},{2,6},{4,0},{6,2},{8,12},{10,14},{12,8},{14,10},{16,20},{18,... | collective-permute-start | bytes 24584 | tf_op jit(solution)/shard_map/ppermute | solution.py:32
  38.2 4.0 %collective-permute-start.9 = (f32[4,512]{1,0:T(4,128)S(1)}, f32[4,512]{1,0:T(4,128)S(1)}, u32[]{:S(2)}, u32[]{:S(2)}) collective-permute-start(f32[4,512]{1,0:T(4,128)S(1)} %pad_maximum_fusion.1.refs_0_), channel_id=1, source_target_pairs={{0,2},{2,0},{4,6},{6,4},{8,10},{10,8},{12,14},{14,12},{16,18},{18,... | collective-permute-start | bytes 24584 | tf_op jit(solution)/shard_map/ppermute | solution.py:32

commit v18 on v17

--- a/solution.py
+++ b/solution.py
@@ -144,12 +144,14 @@
     return lax.axis_size("tm") * lax.axis_size("space")
 
 
-def entry_kernel(feats_hbm, frames, tail, edges, copies, mark, stats, sems):
+def entry_kernel(slabs, per_slab, feats_hbm, clips_hbm, *refs):
+    params_hbm, (frames, tail, edges, copies_hbm, aux, stats, copies, params, clips, frame_sems, sems) = refs[:4], refs[4:]
     n_frames, n_rows, _, width = frames.shape
-    loads = [pltpu.make_async_copy(feats_hbm.at[f], frames.at[f], sems.at[f]) for f in range(n_frames)]
-    for copy in loads:
+    loads = [pltpu.make_async_copy(feats_hbm.at[f], frames.at[f], frame_sems.at[f]) for f in range(n_frames)]
+    clip_load = pltpu.make_async_copy(clips_hbm, clips, sems.at[0])
+    param_loads = [pltpu.make_async_copy(p, params.at[k], sems.at[1 + k]) for k, p in enumerate(params_hbm)]
+    for copy in [*loads, clip_load, *param_loads]:
         copy.start()
-    mark[...] = jnp.zeros_like(mark)
     sums = no_stats(width)
     for frame in range(n_frames):
         loads[frame].wait()
@@ -160,43 +162,8 @@
         send_rows(frames, frame, edges)
     store_stats(stats, sums)
     store_copies(copies, stats)
-
-
-def copies_shape(width):
-    return shaped((device_count(), 1, 2 * width), F32)
-
-
-MARK = jax.ShapeDtypeStruct((8, 128), F32)
-
-
-def entry_call(feats):
-    n_frames, width = feats.shape[0], feats.shape[3]
-    outs = [
-        shaped(feats.shape),
-        shaped((TAIL,) + feats.shape[1:]),
-        shaped(edge_shape(feats, n_frames)),
-        copies_shape(width),
-        MARK,
-    ]
-    return pl.pallas_call(
-        entry_kernel,
-        out_shape=outs,
-        in_specs=[ANYWHERE],
-        out_specs=[VMEM] * len(outs),
-        scratch_shapes=[pltpu.VMEM((1, 2 * width), F32), pltpu.SemaphoreType.DMA((n_frames,))],
-        compiler_params=vmem_params(),
-        cost_estimate=pl.CostEstimate(flops=4 * feats.size, bytes_accessed=4 * feats.size, transcendentals=0),
-    )(in_hbm(feats))
-
-
-def setup_kernel(slabs, per_slab, kernel_hbm, clips_hbm, *refs):
-    params_hbm, (_, taps, aux, params, clips, sems) = refs[:4], refs[4:]
-    taps_load = pltpu.make_async_copy(kernel_hbm.at[0], taps.at[0], sems.at[5])
-    width = aux.shape[1]
-    clip_load = pltpu.make_async_copy(clips_hbm, clips, sems.at[0])
-    param_loads = [pltpu.make_async_copy(p, params.at[k], sems.at[1 + k]) for k, p in enumerate(params_hbm)]
-    for copy in [clip_load, *param_loads, taps_load]:
-        copy.start()
+    copies_store = pltpu.make_async_copy(copies, copies_hbm, sems.at[5])
+    copies_store.start()
     clip_load.wait()
     own = lax.axis_index("tm")
     own_clip = clips[own]
@@ -205,36 +172,47 @@
         same = (clips[slab] == own_clip).astype(jnp.int32)
         slabs_in = slabs_in + same
         aux[slab : slab + 1] = jnp.full((1, width), same.astype(F32), F32)
-    offsets = slab_offsets(slabs)
-    for entry, offset in enumerate(offsets):
+    for entry, offset in enumerate(slab_offsets(slabs)):
         same = (clips[own ^ offset] == own_clip).astype(F32)
         aux[slabs + entry : slabs + entry + 1] = jnp.full((1, width), same, F32)
-    slabs *= 2
+    row = 2 * slabs
     starting = jnp.logical_or(own == 0, clips[jnp.maximum(own - 1, 0)] != own_clip)
-    aux[slabs : slabs + 1] = jnp.full((1, width), starting.astype(F32), F32)
-    aux[slabs + 1 : slabs + 2] = jnp.full((1, width), slabs_in.astype(F32) * float(per_slab), F32)
+    aux[row : row + 1] = jnp.full((1, width), starting.astype(F32), F32)
+    aux[row + 1 : row + 2] = jnp.full((1, width), slabs_in.astype(F32) * float(per_slab), F32)
     for k, copy in enumerate(param_loads):
         copy.wait()
-        aux[slabs + 2 + k : slabs + 3 + k] = params[k]
-    aux[slabs + 6 : slabs + 8] = jnp.zeros((2, width), F32)
-    taps_load.wait()
-
-
-def setup_call(kernel, clip_ids, params, per_slab, mark):
-    slabs, width = lax.axis_size("tm"), params[0].shape[0]
+        aux[row + 2 + k : row + 3 + k] = params[k]
+    aux[row + 6 : row + 8] = jnp.zeros((2, width), F32)
+    copies_store.wait()
+
+
+def entry_call(feats, clip_ids, params, per_slab):
+    slabs = lax.axis_size("tm")
+    n_frames, width = feats.shape[0], feats.shape[3]
+    copies = (device_count(), 1, 2 * width)
+    outs = [
+        shaped(feats.shape),
+        shaped((TAIL,) + feats.shape[1:]),
+        shaped(edge_shape(feats, n_frames)),
+        shaped(copies, F32),
+        shaped((2 * slabs + 8, width), F32),
+    ]
     return pl.pallas_call(
-        functools.partial(setup_kernel, slabs, per_slab),
-        out_shape=[shaped((1,) + kernel.shape[1:]), shaped((2 * slabs + 8, width), F32)],
-        in_specs=[ANYWHERE] * 6 + [VMEM],
-        out_specs=[VMEM, VMEM],
+        functools.partial(entry_kernel, slabs, per_slab),
+        out_shape=outs,
+        in_specs=[ANYWHERE] * 6,
+        out_specs=[VMEM, VMEM, VMEM, ANYWHERE, VMEM],
         scratch_shapes=[
+            pltpu.VMEM((1, 2 * width), F32),
+            pltpu.VMEM(copies, F32),
             pltpu.VMEM((4, 1, width), F32),
             pltpu.SMEM(clip_ids.shape, jnp.int32),
+            pltpu.SemaphoreType.DMA((n_frames,)),
             pltpu.SemaphoreType.DMA((6,)),
         ],
         compiler_params=vmem_params(),
-        cost_estimate=pl.CostEstimate(flops=1 << 30, bytes_accessed=1 << 16, transcendentals=0),
-    )(*[in_hbm(x) for x in (kernel, clip_ids, *[p[None] for p in params])], mark)
+        cost_estimate=pl.CostEstimate(flops=4 * feats.size, bytes_accessed=4 * feats.size, transcendentals=0),
+    )(*[in_hbm(x) for x in (feats, clip_ids, *[p[None] for p in params])])
 
 
 def group_total(values):
@@ -314,7 +292,7 @@
     column = lax.broadcasted_iota(jnp.int32, (cols, width), 0)
     sums = []
     for l in range(3):
-        rhs = jnp.concatenate([taps[0][0, j, l] for j in range(3)] + [taps[1][i, j, l] for i in range(2) for j in range(3)], axis=0)
+        rhs = jnp.concatenate([taps[i, j, l] for i in range(3) for j in range(3)], axis=0)
         sums.append(jnp.dot(lhs, rhs, preferred_element_type=F32))
     for row in range(n_rows):
         left, mid, right = (s[row * cols : (row + 1) * cols] for s in sums)
@@ -330,13 +308,10 @@
 
 
 def late_kernel(n_sides, aux, table, frames, *refs):
-    sides, first_taps, kernel_hbm = refs[:n_sides], refs[n_sides], refs[n_sides + 1]
-    act_low, affine_out, more_taps, hidden, stats, edges, act_high, taps_sems = refs[n_sides + 2 :]
-    taps = (first_taps, more_taps)
+    sides, kernel_hbm = refs[:n_sides], refs[n_sides]
+    act_low, affine_out, taps, hidden, stats, edges, act_high, taps_sems = refs[n_sides + 1 :]
     loads = [
-        pltpu.make_async_copy(kernel_hbm.at[i, j], more_taps.at[i - 1, j], taps_sems.at[3 * (i - 1) + j])
-        for i in range(1, 3)
-        for j in range(3)
+        pltpu.make_async_copy(kernel_hbm.at[i, j], taps.at[i, j], taps_sems.at[3 * i + j]) for i in range(3) for j in range(3)
     ]
     for copy in loads:
         copy.start()
@@ -346,22 +321,30 @@
     for k in range(2):
         affine_out[k : k + 1] = affine[k]
     planes = [(act_low, f) for f in range(low)] + [(act_high, f) for f in range(high)]
-    for frame, (act, index) in enumerate(planes):
+
+    def fill(frame):
+        act, index = planes[frame]
         for row in range(n_rows + 2):
             act[index, row] = normed(extended_row(frames, sides, frame, row), affine)
+
+    for frame in range(low):
+        fill(frame)
     for copy in loads:
         copy.wait()
+    fill(low)
     sums = no_stats(width)
     for frame in range(high):
         for row, value in conv_rows(planes[frame : frame + 3], taps):
             sums = put_hidden(hidden, frame, row, value, sums)
         send_rows(hidden, frame, edges)
+        if frame + 1 < high:
+            fill(low + frame + 1)
     for k in range(2):
         stats[k] = sums[k]
 
 
 def early_kernel(n_sides, aux, first, second, *refs):
-    corners, (act_low, affine_in, *taps), refs = refs[:n_sides], refs[n_sides : n_sides + 4], refs[n_sides + 4 :]
+    corners, (act_low, affine_in, taps), refs = refs[:n_sides], refs[n_sides : n_sides + 3], refs[n_sides + 3 :]
     late_stats, hidden, edges, stats, act_before = refs
     sums = late_stats[0], late_stats[1]
     slabs = aux.shape[0] - 8
@@ -411,7 +394,7 @@
         if frame == 0:
             fill(0)
             fill(1)
-        for row, value in conv_rows([(act, frame + i) for i in range(3)], (taps.at[:1], taps.at[1:])):
+        for row, value in conv_rows([(act, frame + i) for i in range(3)], taps):
             out[frame, row] = feats[frame, row].astype(F32) + value
         stores[frame].start()
     for store in stores:
@@ -440,22 +423,21 @@
     act = pltpu.VMEM((2,) + plane, BF16)
     act_late = pltpu.VMEM((late,) + plane, BF16)
     work = 54 * feats.size // n_frames * width
-    late_shapes = [shaped((2,) + plane), shaped((2, width), F32), shaped((2,) + kernel_one.shape[1:])]
+    late_shapes = [shaped((2,) + plane), shaped((2, width), F32), shaped(kernel_one.shape)]
     hidden_shapes = [shaped((late, n_rows, cols, width)), shaped((2, 8, width), F32), shaped(edge_shape(feats, late))]
 
-    frames, tail, edges, copies, mark = entry_call(feats)
+    frames, tail, edges, copies, aux = entry_call(feats, clip_ids, params, per_slab)
     table = stats_table(copies)
     sides = row_halo(edges)
     n_sides = len(sides)
     first, second = slab_halo(tail, sides)
     corners = row_halo(edges_of(first))
-    taps, aux = setup_call(kernel_one, clip_ids, params, per_slab, mark)
     aux, *corners = lax.optimization_barrier((aux, *corners))
-    operands = [aux, table, frames, *sides, taps, in_hbm(kernel_one)]
-    act_low, affine, more_taps, hidden_late, stats, edges = call(
+    operands = [aux, table, frames, *sides, in_hbm(kernel_one)]
+    act_low, affine, taps, hidden_late, stats, edges = call(
         functools.partial(late_kernel, n_sides),
         late_shapes + hidden_shapes,
-        [act_late, pltpu.SemaphoreType.DMA((6,))],
+        [act_late, pltpu.SemaphoreType.DMA((9,))],
         1 << 37,
         operands,
         outside=(len(operands) - 1,),
@@ -467,7 +449,7 @@
         [shaped((2, n_rows, cols, width)), shaped(edge_shape(feats, 2)), shaped((1, 2 * width), F32)],
         [act],
         2 * work,
-        [aux, first, second, *corners, act_low, affine, taps, more_taps, stats],
+        [aux, first, second, *corners, act_low, affine, taps, stats],
     )
 
     sides_early = row_halo(edges)

time: 49.4 us -> 49.9 us (1.010)
  waiting for transfers between devices: 11.2 us -> 13.7 us
  starting transfers between devices: 19.8 us -> 18.8 us
  Pallas kernels: 17.9 us -> 17 us
    ppermute x2, waiting for transfers between devices: 2.97 us -> 4.98 us  [shifted(): lax.ppermute(value, axis, [(i, (i + step) % peers) for i in range(peers)])]
    pallas_call x2 -> x1, Pallas kernels: 3.33 us -> 2.05 us  [entry_call(): pl.pallas_call(functools.partial(entry_kernel, slabs, per_slab), out_shap...]
    ppermute x12, starting transfers between devices: 9.75 us -> 8.97 us  [traded(): lax.ppermute(value, axis, [(i, i ^ mask) for i in range(lax.axis_size(axi...]
  transfers between devices with their start and end apart: 16 -> 16, of which waited for: 9 -> 9; matrix products, arithmetic and copies ran while one was open for 0% -> 0% of each run, Pallas kernels for 19% -> 16%
where the time goes in v18:
time: 49.9 us; the launch traced here: 49.7 us
  starting transfers between devices  18.8 us (38%)
  Pallas kernels  17 us (34%)
  waiting for transfers between devices  13.7 us (27%)
    pallas_call x3, Pallas kernels, call(): pl.pallas_call(kernel, out_shape=outs, in_specs=[ANYWHERE if k in (aliase...  15 us
    ppermute x12, starting transfers between devices, traded(): lax.ppermute(value, axis, [(i, i ^ mask) for i in range(lax.axis_size(axi...  8.97 us
    ppermute x12, waiting for transfers between devices, traded(): lax.ppermute(value, axis, [(i, i ^ mask) for i in range(lax.axis_size(axi...  6.63 us
    all_to_all x1, starting transfers between devices, stats_table(): return lax.all_to_all(copies, ('tm', 'space'), 0, 0, tiled=True)  5.03 us
    ppermute x2, waiting for transfers between devices, shifted(): lax.ppermute(value, axis, [(i, (i + step) % peers) for i in range(peers)])  4.98 us
    ppermute x2, starting transfers between devices, shifted(): lax.ppermute(value, axis, [(i, (i + step) % peers) for i in range(peers)])  3.47 us
    all_to_all x1, waiting for transfers between devices, stats_table(): return lax.all_to_all(copies, ('tm', 'space'), 0, 0, tiled=True)  2.06 us
    pallas_call x1, Pallas kernels, entry_call(): pl.pallas_call(functools.partial(entry_kernel, slabs, per_slab), out_shap...  2.05 us
  transfers between devices with their start and end apart: 16, of which 9 were waited for; matrix products, arithmetic and copies ran while one was open for 0% of the time, Pallas kernels for 16%

profile of v18, /device:TPU:0, one launch (start us, length us, event | category | flops | bytes accessed | tf_op | source)
XLA Modules:
  0.0 49.7 jit_solution(11698787662843318865)
XLA Ops:
  0.0 2.0 %shard_map.82 = (bf16[4,4,96,256]{3,2,1,0:T(8,128)(2,1)S(1)}, bf16[2,4,96,256]{3,2,1,0:T(8,128)(2,1)S(1)}, bf16[4,1,96,256]{3,2,1,0:T(8,128)(2,1)S(1)}, f32[32,1,512]{2,1,0:T(1,128)}, f32[40,256]{1,0:T(8,128)S(1)}) custom-call(bf16[4,4,96,256]{3,2,1,0:T(8,128)(2,1)} %feats_hbm.1, s32[16]{0:T(128)} %clips_hbm.1, f32[1,256]{1,0:T(1,128)} %bitcast.4, ...), custom_call_target="tpu_custom_call" | custom-call | flops 1572864 | bytes 1572864 | tf_op jit(solution)/shard_map/pallas_call | solution.py:200
  2.1 3.0 %collective-permute-start = (bf16[1,4,96,256]{3,2,1,0:T(8,128)(2,1)S(1)}, bf16[1,4,96,256]{3,2,1,0:T(8,128)(2,1)S(1)}, u32[]{:S(2)}, u32[]{:S(2)}) collective-permute-start(bf16[1,4,96,256]{3,2,1,0:T(8,128)(2,1)S(1)} %get-tuple-element.42), channel_id=1, source_target_pairs={{0,2},{2,4},{4,6},{6,8},{8,10},{10,12},{12,14},{14,16},{16,18},{18... | collective-permute-start | bytes 589832 | tf_op jit(solution)/shard_map/ppermute | solution.py:37
  5.1 0.0 collective-permute-start.2
  5.1 5.0 %all-to-all-start = ((f32[32,1,512]{2,1,0:T(1,128)}), f32[32,1,512]{2,1,0:T(1,128)S(1)}, u32[]{:S(2)}, u32[]{:S(2)}) async-start(f32[32,1,512]{2,1,0:T(1,128)} %get-tuple-element.26), calls=%async_computation | async-start | bytes 131072 | tf_op jit(solution)/shard_map/all_to_all | solution.py:41
  10.1 4.0 %collective-permute-done.first = bf16[1,4,96,256]{3,2,1,0:T(8,128)(2,1)S(1)} collective-permute-done((bf16[1,4,96,256]{3,2,1,0:T(8,128)(2,1)S(1)}, bf16[1,4,96,256]{3,2,1,0:T(8,128)(2,1)S(1)}, u32[]{:S(2)}, u32[]{:S(2)}) %collective-permute-start) | collective-permute-done | bytes 196640 | tf_op jit(solution)/shard_map/ppermute | solution.py:37
  14.1 0.0 collective-permute-start.1
  14.1 0.0 collective-permute-done.2.refs_0_
  14.2 1.3 %collective-permute-start.4 = (bf16[1,5,96,256]{3,2,1,0:T(8,128)(2,1)S(1)}, bf16[1,5,96,256]{3,2,1,0:T(8,128)(2,1)S(1)}, u32[]{:S(2)}, u32[]{:S(2)}) collective-permute-start(bf16[1,5,96,256]{3,2,1,0:T(8,128)(2,1)S(1)} %pad_maximum_fusion), channel_id=1, source_target_pairs={{0,2},{2,4},{4,6},{6,8},{8,10},{10,12},{12,14},{14,16},{16,18},{18... | collective-permute-start | bytes 737288 | tf_op jit(solution)/shard_map/ppermute | solution.py:86
  15.5 0.0 collective-permute-done.1.refs_0_
  15.5 2.1 %all-to-all-done.table = f32[32,1,512]{2,1,0:T(1,128)S(1)} async-done(((f32[32,1,512]{2,1,0:T(1,128)}), f32[32,1,512]{2,1,0:T(1,128)S(1)}, u32[]{:S(2)}, u32[]{:S(2)}) %all-to-all-start) | async-done | bytes 65568 | tf_op jit(solution)/shard_map/all_to_all | solution.py:41
  17.5 5.1 %shard_map.83 = (bf16[2,6,96,256]{3,2,1,0:T(8,128)(2,1)S(1)}, f32[2,256]{1,0:T(2,128)S(1)}, bf16[3,3,3,256,256]{4,3,2,1,0:T(8,128)(2,1)S(1)}, bf16[2,4,96,256]{3...) custom-call(f32[40,256]{1,0:T(8,128)S(1)} %get-tuple-element.25.aux, ...), custom_call_target="tpu_custom_call" | custom-call | flops 137438953472 | bytes 1048576 | tf_op jit(solution)/shard_map/pallas_call | solution.py:405
  22.6 0.5 collective-permute-start.3
  23.1 0.0 collective-permute-done.4.second
  23.1 0.0 copy-start
  23.1 3.1 %shard_map.84 = (bf16[2,4,96,256]{3,2,1,0:T(8,128)(2,1)S(1)}, bf16[2,1,96,256]{3,2,1,0:T(8,128)(2,1)S(1)}, f32[1,512]{1,0:T(1,128)S(1)}) custom-call(f32[40,256]{1,0:T(8,128)S(1)} %get-tuple-element.25.aux, bf16[1,4,96,256]{3,2,1,0:T(8,128)(2,1)S(1)} %collective-permute-done.first, bf16[1,5,96,256]{3,2,1,0:T(8,128)(2,1)S(1)} %collective-permute-done.4.second, ...), custom_call_target="tpu_custom_call" | custom-call | flops 2717908992 | bytes 1048576 | tf_op jit(solution)/shard_map/pallas_call | solution.py:405
  26.2 0.1 collective-permute-start.5
  26.2 1.1 %collective-permute-done.5 = f32[1,512]{1,0:T(1,128)S(1)} collective-permute-done((f32[1,512]{1,0:T(1,128)S(1)}, f32[1,512]{1,0:T(1,128)S(1)}, u32[]{:S(2)}, u32[]{:S(2)}) %collective-permute-start.5) | collective-permute-done | bytes 2080 | tf_op jit(solution)/shard_map/ppermute | solution.py:32
  27.4 4.6 %collective-permute-start.8 = (f32[1,512]{1,0:T(1,128)S(1)}, f32[1,512]{1,0:T(1,128)S(1)}, u32[]{:S(2)}, u32[]{:S(2)}) collective-permute-start(f32[1,512]{1,0:T(1,128)S(1)} %add.8), channel_id=1, source_target_pairs={{0,24},{2,26},{4,28},{6,30},{8,16},{10,18},{12,20},{14,22},{16,8},... | collective-permute-start | bytes 6152 | tf_op jit(solution)/shard_map/ppermute | solution.py:32
  32.0 0.0 collective-permute-start.7
  32.0 0.6 %collective-permute-start.6 = (f32[1,512]{1,0:T(1,128)S(1)}, f32[1,512]{1,0:T(1,128)S(1)}, u32[]{:S(2)}, u32[]{:S(2)}) collective-permute-start(f32[1,512]{1,0:T(1,128)S(1)} %add.8), channel_id=1, source_target_pairs={{0,8},{2,10},{4,12},{6,14},{8,0},{10,2},{12,4},{14,6},{16,24},{18,... | collective-permute-start | bytes 6152 | tf_op jit(solution)/shard_map/ppermute | solution.py:32
  32.7 0.0 collective-permute-start.13
  32.7 0.9 %collective-permute-done.8 = f32[1,512]{1,0:T(1,128)S(1)} collective-permute-done((f32[1,512]{1,0:T(1,128)S(1)}, f32[1,512]{1,0:T(1,128)S(1)}, u32[]{:S(2)}, u32[]{:S(2)}) %collective-permute-start.8) | collective-permute-done | bytes 2080 | tf_op jit(solution)/shard_map/ppermute | solution.py:32
  33.6 0.0 collective-permute-start.12
  33.6 2.9 %collective-permute-done.7 = f32[1,512]{1,0:T(1,128)S(1)} collective-permute-done((f32[1,512]{1,0:T(1,128)S(1)}, f32[1,512]{1,0:T(1,128)S(1)}, u32[]{:S(2)}, u32[]{:S(2)}) %collective-permute-start.7) | collective-permute-done | bytes 2080 | tf_op jit(solution)/shard_map/ppermute | solution.py:32
  36.5 0.0 collective-permute-done.6
  36.5 1.0 %collective-permute-done.3.refs_8_ = bf16[2,4,96,256]{3,2,1,0:T(8,128)(2,1)S(1)} collective-permute-done((bf16[2,4,96,256]{3,2,1,0:T(8,128)(2,1)S(1)}, bf16[2,4,96,256]{3,2,1,0:T(8,128)(2,1)S(1)}, u32[]{:S(2)}, u32[]{:S(2)}) %collective-permute-start.3) | collective-permute-done | bytes 393248 | tf_op jit(solution)/shard_map/ppermute | solution.py:37
  37.6 0.1 collective-permute-start.14
  37.6 1.1 %collective-permute-start.11 = (f32[4,512]{1,0:T(4,128)S(1)}, f32[4,512]{1,0:T(4,128)S(1)}, u32[]{:S(2)}, u32[]{:S(2)}) collective-permute-start(f32[4,512]{1,0:T(4,128)S(1)} %pad_maximum_fusion.1.refs_0_), channel_id=1, source_target_pairs={{0,6},{2,4},{4,2},{6,0},{8,14},{10,12},{12,10},{14,8},{16,22},{18,... | collective-permute-start | bytes 24584 | tf_op jit(solution)/shard_map/ppermute | solution.py:32
  38.8 0.0 collective-permute-start.10
  38.8 0.0 collective-permute-done.13.refs_7_
  38.8 2.4 %collective-permute-start.9 = (f32[4,512]{1,0:T(4,128)S(1)}, f32[4,512]{1,0:T(4,128)S(1)}, u32[]{:S(2)}, u32[]{:S(2)}) collective-permute-start(f32[4,512]{1,0:T(4,128)S(1)} %pad_maximum_fusion.1.refs_0_), channel_id=1, source_target_pairs={{0,2},{2,0},{4,6},{6,4},{8,10},{10,8},{12,14},{14,12},{16,18},{18,... | collective-permute-start | bytes 24584 | tf_op jit(solution)/shard_map/ppermute | solution.py:32
  41.2 1.1 %collective-permute-done.11.refs_3_ = f32[4,512]{1,0:T(4,128)S(1)} collective-permute-done((f32[4,512]{1,0:T(4,128)S(1)}, f32[4,512]{1,0:T(4,128)S(1)}, u32[]{:S(2)}, u32[]{:S(2)}) %collective-permute-start.11) | collective-permute-done | bytes 8224 | tf_op jit(solution)/shard_map/ppermute | solution.py:32
  42.3 0.2 collective-permute-done.10.refs_2_
  42.4 0.4 collective-permute-done.9.refs_1_
  42.8 0.0 collective-permute-done.12.refs_6_
  42.8 0.0 collective-permute-done.14.refs_9_
  42.8 0.0 copy-done
  42.8 6.8 %shard_map.85 = f32[4,4,96,256]{3,2,1,0:T(8,128)} custom-call(f32[40,256]{1,0:T(8,128)S(1)} %get-tuple-element.25.aux, f32[4,512]{1,0:T(4,128)S(1)} %pad_maximum_fusion.1.refs_0_, f32[4,512]{1,0:T(4,128)S(1)} %collective-permute-done.9.refs_1_, f32[4,512]{1,0:T(4,128)S(1)} %collective-permute-done.10.refs_2_, f32[4,512]{1,0:T(4,128)S(1)} %collective-permute-done.11.refs_3_, ...), custom_call_target="tpu_custom_call" | custom-call | flops 5435817984 | bytes 1048576 | tf_op jit(solution)/shard_map/pallas_call | solution.py:405
  (7 shorter events, 0.1 us)
Async XLA Ops:
  2.1 12.0 %collective-permute-start = (bf16[1,4,96,256]{3,2,1,0:T(8,128)(2,1)S(1)}, bf16[1,4,96,256]{3,2,1,0:T(8,128)(2,1)S(1)}, u32[]{:S(2)}, u32[]{:S(2)}) collective-permute-start(bf16[1,4,96,256]{3,2,1,0:T(8,128)(2,1)S(1)} %get-tuple-element.42), channel_id=1, source_target_pairs={{0,2},{2,4},{4,6},{6,8},{8,10},{10,12},{12,14},{14,16},{16,18},{18... | collective-permute-start | bytes 589832 | tf_op jit(solution)/shard_map/ppermute | solution.py:37
  5.1 9.0 %collective-permute-start.2 = (bf16[4,1,96,256]{3,2,1,0:T(8,128)(2,1)S(1)}, bf16[4,1,96,256]{3,2,1,0:T(8,128)(2,1)S(1)}, u32[]{:S(2)}, u32[]{:S(2)}) collective-permute-start(bf16[4,1,96,256]{3,2,1,0:T(8,128)(2,1)S(1)} %get-tuple-element.28), channel_id=1, source_target_pairs={{0,1},{1,0},{2,3},{3,2},{4,5},{5,4},{6,7},{7,6},{8,9},{9,8},{10,11... | collective-permute-start | bytes 589832 | tf_op jit(solution)/shard_map/ppermute | solution.py:32
  5.1 12.5 %all-to-all-start = ((f32[32,1,512]{2,1,0:T(1,128)}), f32[32,1,512]{2,1,0:T(1,128)S(1)}, u32[]{:S(2)}, u32[]{:S(2)}) async-start(f32[32,1,512]{2,1,0:T(1,128)} %get-tuple-element.26), calls=%async_computation | async-start | bytes 131072 | tf_op jit(solution)/shard_map/all_to_all | solution.py:41
  14.1 1.4 %collective-permute-start.1 = (bf16[1,1,96,256]{3,2,1,0:T(8,128)(2,1)S(1)}, bf16[1,1,96,256]{3,2,1,0:T(8,128)(2,1)S(1)}, u32[]{:S(2)}, u32[]{:S(2)}) collective-permute-start(bf16[1,1,96,256]{3,2,1,0:T(8,128)(2,1)S(1)} %constant_dynamic-slice_fusion.1), channel_id=1, source_target_pairs={{0,1},{1,0},{2,3},{3,2},{4,5},{5,4},{6,7},{7,6},{8,9},{9,8},{10,11... | collective-permute-start | bytes 147464 | tf_op jit(solution)/shard_map/ppermute | solution.py:32
  14.2 8.9 %collective-permute-start.4 = (bf16[1,5,96,256]{3,2,1,0:T(8,128)(2,1)S(1)}, bf16[1,5,96,256]{3,2,1,0:T(8,128)(2,1)S(1)}, u32[]{:S(2)}, u32[]{:S(2)}) collective-permute-start(bf16[1,5,96,256]{3,2,1,0:T(8,128)(2,1)S(1)} %pad_maximum_fusion), channel_id=1, source_target_pairs={{0,2},{2,4},{4,6},{6,8},{8,10},{10,12},{12,14},{14,16},{16,18},{18... | collective-permute-start | bytes 737288 | tf_op jit(solution)/shard_map/ppermute | solution.py:86
  22.6 14.9 %collective-permute-start.3 = (bf16[2,4,96,256]{3,2,1,0:T(8,128)(2,1)S(1)}, bf16[2,4,96,256]{3,2,1,0:T(8,128)(2,1)S(1)}, u32[]{:S(2)}, u32[]{:S(2)}) collective-permute-start(bf16[2,4,96,256]{3,2,1,0:T(8,128)(2,1)S(1)} %get-tuple-element.29.refs_5_), channel_id=1, source_target_pairs={{0,2},{2,4},{4,6},{6,8},{8,10},{10,12},{12,14},{14,16},{16,18},{18... | collective-permute-start | bytes 1179656 | tf_op jit(solution)/shard_map/ppermute | solution.py:37
  23.1 19.7 %copy-start = (bf16[3,3,3,256,256]{4,3,2,1,0:T(8,128)(2,1)S(1)}, bf16[3,3,3,256,256]{4,3,2,1,0:T(8,128)(2,1)}, u32[]{:S(2)}) copy-start(bf16[3,3,3,256,256]{4,3,2,1,0:T(8,128)(2,1)} %refs_10_.1) | copy-start | bytes 10616836
  26.2 1.2 %collective-permute-start.5 = (f32[1,512]{1,0:T(1,128)S(1)}, f32[1,512]{1,0:T(1,128)S(1)}, u32[]{:S(2)}, u32[]{:S(2)}) collective-permute-start(f32[1,512]{1,0:T(1,128)S(1)} %get-tuple-element.35), channel_id=1, source_target_pairs={{0,1},{1,0},{2,3},{3,2},{4,5},{5,4},{6,7},{7,6},{8,9},{9,8},{10,11... | collective-permute-start | bytes 6152 | tf_op jit(solution)/shard_map/ppermute | solution.py:32
  27.4 6.2 %collective-permute-start.8 = (f32[1,512]{1,0:T(1,128)S(1)}, f32[1,512]{1,0:T(1,128)S(1)}, u32[]{:S(2)}, u32[]{:S(2)}) collective-permute-start(f32[1,512]{1,0:T(1,128)S(1)} %add.8), channel_id=1, source_target_pairs={{0,24},{2,26},{4,28},{6,30},{8,16},{10,18},{12,20},{14,22},{16,8},... | collective-permute-start | bytes 6152 | tf_op jit(solution)/shard_map/ppermute | solution.py:32
  32.0 4.5 %collective-permute-start.7 = (f32[1,512]{1,0:T(1,128)S(1)}, f32[1,512]{1,0:T(1,128)S(1)}, u32[]{:S(2)}, u32[]{:S(2)}) collective-permute-start(f32[1,512]{1,0:T(1,128)S(1)} %add.8), channel_id=1, source_target_pairs={{0,16},{2,18},{4,20},{6,22},{8,24},{10,26},{12,28},{14,30},{16,0},... | collective-permute-start | bytes 6152 | tf_op jit(solution)/shard_map/ppermute | solution.py:32
  32.0 4.5 %collective-permute-start.6 = (f32[1,512]{1,0:T(1,128)S(1)}, f32[1,512]{1,0:T(1,128)S(1)}, u32[]{:S(2)}, u32[]{:S(2)}) collective-permute-start(f32[1,512]{1,0:T(1,128)S(1)} %add.8), channel_id=1, source_target_pairs={{0,8},{2,10},{4,12},{6,14},{8,0},{10,2},{12,4},{14,6},{16,24},{18,... | collective-permute-start | bytes 6152 | tf_op jit(solution)/shard_map/ppermute | solution.py:32
  32.7 6.1 %collective-permute-start.13 = (bf16[2,1,96,256]{3,2,1,0:T(8,128)(2,1)S(1)}, bf16[2,1,96,256]{3,2,1,0:T(8,128)(2,1)S(1)}, u32[]{:S(2)}, u32[]{:S(2)}) collective-permute-start(bf16[2,1,96,256]{3,2,1,0:T(8,128)(2,1)S(1)} %get-tuple-element.39), channel_id=1, source_target_pairs={{0,1},{1,0},{2,3},{3,2},{4,5},{5,4},{6,7},{7,6},{8,9},{9,8},{10,11... | collective-permute-start | bytes 294920 | tf_op jit(solution)/shard_map/ppermute | solution.py:32
  33.6 9.3 %collective-permute-start.12 = (bf16[2,1,96,256]{3,2,1,0:T(8,128)(2,1)S(1)}, bf16[2,1,96,256]{3,2,1,0:T(8,128)(2,1)S(1)}, u32[]{:S(2)}, u32[]{:S(2)}) collective-permute-start(bf16[2,1,96,256]{3,2,1,0:T(8,128)(2,1)S(1)} %get-tuple-element.38), channel_id=1, source_target_pairs={{0,1},{1,0},{2,3},{3,2},{4,5},{5,4},{6,7},{7,6},{8,9},{9,8},{10,11... | collective-permute-start | bytes 294920 | tf_op jit(solution)/shard_map/ppermute | solution.py:32
  37.6 5.3 %collective-permute-start.14 = (bf16[2,1,96,256]{3,2,1,0:T(8,128)(2,1)S(1)}, bf16[2,1,96,256]{3,2,1,0:T(8,128)(2,1)S(1)}, u32[]{:S(2)}, u32[]{:S(2)}) collective-permute-start(bf16[2,1,96,256]{3,2,1,0:T(8,128)(2,1)S(1)} %constant_dynamic-slice_fusion), channel_id=1, source_target_pairs={{0,1},{1,0},{2,3},{3,2},{4,5},{5,4},{6,7},{7,6},{8,9},{9,8},{10,11... | collective-permute-start | bytes 294920 | tf_op jit(solution)/shard_map/ppermute | solution.py:32
  37.6 4.6 %collective-permute-start.11 = (f32[4,512]{1,0:T(4,128)S(1)}, f32[4,512]{1,0:T(4,128)S(1)}, u32[]{:S(2)}, u32[]{:S(2)}) collective-permute-start(f32[4,512]{1,0:T(4,128)S(1)} %pad_maximum_fusion.1.refs_0_), channel_id=1, source_target_pairs={{0,6},{2,4},{4,2},{6,0},{8,14},{10,12},{12,10},{14,8},{16,22},{18,... | collective-permute-start | bytes 24584 | tf_op jit(solution)/shard_map/ppermute | solution.py:32
  38.8 3.7 %collective-permute-start.10 = (f32[4,512]{1,0:T(4,128)S(1)}, f32[4,512]{1,0:T(4,128)S(1)}, u32[]{:S(2)}, u32[]{:S(2)}) collective-permute-start(f32[4,512]{1,0:T(4,128)S(1)} %pad_maximum_fusion.1.refs_0_), channel_id=1, source_target_pairs={{0,4},{2,6},{4,0},{6,2},{8,12},{10,14},{12,8},{14,10},{16,20},{18,... | collective-permute-start | bytes 24584 | tf_op jit(solution)/shard_map/ppermute | solution.py:32
  38.8 4.0 %collective-permute-start.9 = (f32[4,512]{1,0:T(4,128)S(1)}, f32[4,512]{1,0:T(4,128)S(1)}, u32[]{:S(2)}, u32[]{:S(2)}) collective-permute-start(f32[4,512]{1,0:T(4,128)S(1)} %pad_maximum_fusion.1.refs_0_), channel_id=1, source_target_pairs={{0,2},{2,0},{4,6},{6,4},{8,10},{10,8},{12,14},{14,12},{16,18},{18,... | collective-permute-start | bytes 24584 | tf_op jit(solution)/shard_map/ppermute | solution.py:32

commit v19 on v17

--- a/solution.py
+++ b/solution.py
@@ -346,16 +346,24 @@
     for k in range(2):
         affine_out[k : k + 1] = affine[k]
     planes = [(act_low, f) for f in range(low)] + [(act_high, f) for f in range(high)]
-    for frame, (act, index) in enumerate(planes):
+
+    def fill(frame):
+        act, index = planes[frame]
         for row in range(n_rows + 2):
             act[index, row] = normed(extended_row(frames, sides, frame, row), affine)
+
+    for frame in range(low):
+        fill(frame)
     for copy in loads:
         copy.wait()
+    fill(low)
     sums = no_stats(width)
     for frame in range(high):
         for row, value in conv_rows(planes[frame : frame + 3], taps):
             sums = put_hidden(hidden, frame, row, value, sums)
         send_rows(hidden, frame, edges)
+        if frame + 1 < high:
+            fill(low + frame + 1)
     for k in range(2):
         stats[k] = sums[k]
 
@@ -405,12 +413,14 @@
             else:
                 act[frame, row] = normed(extended_row(late, sides_late, frame - 4, row), affine)
 
-    for frame in range(2, n_frames + 2):
+    for frame in range(2, 5):
         fill(frame)
     for frame in list(range(2, n_frames)) + [0, 1]:
         if frame == 0:
             fill(0)
             fill(1)
+        elif 2 < frame:
+            fill(frame + 2)
         for row, value in conv_rows([(act, frame + i) for i in range(3)], (taps.at[:1], taps.at[1:])):
             out[frame, row] = feats[frame, row].astype(F32) + value
         stores[frame].start()
@@ -456,7 +466,7 @@
         functools.partial(late_kernel, n_sides),
         late_shapes + hidden_shapes,
         [act_late, pltpu.SemaphoreType.DMA((6,))],
-        1 << 37,
+        2 * work,
         operands,
         outside=(len(operands) - 1,),
     )

time: 49.4 us -> 49.4 us (level)
  no operation moved by 1% of the time
where the time goes in v19:
time: 49.4 us; the launch traced here: 49.1 us
  starting transfers between devices  19.8 us (40%)
  Pallas kernels  17.9 us (36%)
  waiting for transfers between devices  11.2 us (23%)
    pallas_call x3, Pallas kernels, call(): pl.pallas_call(kernel, out_shape=outs, in_specs=[ANYWHERE if k in (aliase...  14.6 us
    ppermute x12, starting transfers between devices, traded(): lax.ppermute(value, axis, [(i, i ^ mask) for i in range(lax.axis_size(axi...  9.77 us
    ppermute x12, waiting for transfers between devices, traded(): lax.ppermute(value, axis, [(i, i ^ mask) for i in range(lax.axis_size(axi...  6.63 us
    all_to_all x1, starting transfers between devices, stats_table(): return lax.all_to_all(copies, ('tm', 'space'), 0, 0, tiled=True)  4.92 us
    ppermute x2, starting transfers between devices, shifted(): lax.ppermute(value, axis, [(i, (i + step) % peers) for i in range(peers)])  3.47 us
    ppermute x2, waiting for transfers between devices, shifted(): lax.ppermute(value, axis, [(i, (i + step) % peers) for i in range(peers)])  2.96 us
    pallas_call x1, Pallas kernels, entry_call(): pl.pallas_call(entry_kernel, out_shape=outs, in_specs=[ANYWHERE], out_spe...  1.95 us
    ppermute x1, starting transfers between devices, chained(): lax.ppermute(value, 'tm', [(i, i + 1) for i in range(lax.axis_size('tm')...  1.63 us
  transfers between devices with their start and end apart: 16, of which 9 were waited for; matrix products, arithmetic and copies ran while one was open for 0% of the time, Pallas kernels for 19%

profile of v19, /device:TPU:0, one launch (start us, length us, event | category | flops | bytes accessed | tf_op | source)
XLA Modules:
  0.0 49.1 jit_solution(5169345255787642220)
XLA Ops:
  0.0 1.9 %shard_map.82 = (bf16[4,4,96,256]{3,2,1,0:T(8,128)(2,1)S(1)}, bf16[2,4,96,256]{3,2,1,0:T(8,128)(2,1)S(1)}, bf16[4,1,96,256]{3,2,1,0:T(8,128)(2,1)S(1)}, f32[32,1,512]{2,1,0:T(1,128)}, f32[8,128]{1,0:T(8,128)S(1)}) custom-call(bf16[4,4,96,256]{3,2,1,0:T(8,128)(2,1)} %feats_hbm.1), custom_call_target="tpu_custom_call" | custom-call | flops 1572864 | bytes 1572864 | tf_op jit(solution)/shard_map/pallas_call | solution.py:181
  2.0 3.0 %collective-permute-start = (bf16[1,4,96,256]{3,2,1,0:T(8,128)(2,1)S(1)}, bf16[1,4,96,256]{3,2,1,0:T(8,128)(2,1)S(1)}, u32[]{:S(2)}, u32[]{:S(2)}) collective-permute-start(bf16[1,4,96,256]{3,2,1,0:T(8,128)(2,1)S(1)} %get-tuple-element.46), channel_id=1, source_target_pairs={{0,2},{2,4},{4,6},{6,8},{8,10},{10,12},{12,14},{14,16},{16,18},{18... | collective-permute-start | bytes 589832 | tf_op jit(solution)/shard_map/ppermute | solution.py:37
  5.0 4.9 %all-to-all-start = ((f32[32,1,512]{2,1,0:T(1,128)}), f32[32,1,512]{2,1,0:T(1,128)S(1)}, u32[]{:S(2)}, u32[]{:S(2)}) async-start(f32[32,1,512]{2,1,0:T(1,128)} %get-tuple-element.29), calls=%async_computation | async-start | bytes 131072 | tf_op jit(solution)/shard_map/all_to_all | solution.py:41
  9.9 0.3 collective-permute-start.2
  10.2 1.4 %shard_map.83 = (bf16[1,3,3,256,256]{4,3,2,1,0:T(8,128)(2,1)S(1)}, f32[40,256]{1,0:T(8,128)S(1)}) custom-call(bf16[3,3,3,256,256]{4,3,2,1,0:T(8,128)(2,1)} %refs_2_.1, s32[16]{0:T(128)} %clips_hbm.1, f32[1,256]{1,0:T(1,128)} %bitcast.4, f32[1,256]{1,0:T(1,128)} %bitcast.5, f32[1,256]{1,0:T(1,128)} %bitcast.6, f32[1,256]{1,0:T(1,128)} %bitcast.7, ...), custom_call_target="tpu_custom_call" | custom-call | flops 1073741824 | bytes 65536 | tf_op jit(solution)/shard_map/pallas_call | solution.py:225
  11.6 2.4 %collective-permute-done.first = bf16[1,4,96,256]{3,2,1,0:T(8,128)(2,1)S(1)} collective-permute-done((bf16[1,4,96,256]{3,2,1,0:T(8,128)(2,1)S(1)}, bf16[1,4,96,256]{3,2,1,0:T(8,128)(2,1)S(1)}, u32[]{:S(2)}, u32[]{:S(2)}) %collective-permute-start) | collective-permute-done | bytes 196640 | tf_op jit(solution)/shard_map/ppermute | solution.py:37
  14.0 0.0 collective-permute-start.1
  14.0 0.0 collective-permute-done.2.refs_0_
  14.1 1.6 %collective-permute-start.4 = (bf16[1,5,96,256]{3,2,1,0:T(8,128)(2,1)S(1)}, bf16[1,5,96,256]{3,2,1,0:T(8,128)(2,1)S(1)}, u32[]{:S(2)}, u32[]{:S(2)}) collective-permute-start(bf16[1,5,96,256]{3,2,1,0:T(8,128)(2,1)S(1)} %pad_maximum_fusion), channel_id=1, source_target_pairs={{0,2},{2,4},{4,6},{6,8},{8,10},{10,12},{12,14},{14,16},{16,18},{18... | collective-permute-start | bytes 737288 | tf_op jit(solution)/shard_map/ppermute | solution.py:86
  15.7 0.0 collective-permute-done.1.refs_0_
  15.7 1.6 %all-to-all-done.table = f32[32,1,512]{2,1,0:T(1,128)S(1)} async-done(((f32[32,1,512]{2,1,0:T(1,128)}), f32[32,1,512]{2,1,0:T(1,128)S(1)}, u32[]{:S(2)}, u32[]{:S(2)}) %all-to-all-start) | async-done | bytes 65568 | tf_op jit(solution)/shard_map/all_to_all | solution.py:41
  17.3 4.7 %shard_map.84 = (bf16[2,6,96,256]{3,2,1,0:T(8,128)(2,1)S(1)}, f32[2,256]{1,0:T(2,128)S(1)}, bf16[2,3,3,256,256]{4,3,2,1,0:T(8,128)(2,1)S(1)}, bf16[2,4,96,256]{3...) custom-call(f32[40,256]{1,0:T(8,128)S(1)} %get-tuple-element.28.aux, ...), custom_call_target="tpu_custom_call" | custom-call | flops 2717908992 | bytes 1048576 | tf_op jit(solution)/shard_map/pallas_call | solution.py:432
  22.0 0.5 collective-permute-start.3
  22.5 0.0 collective-permute-done.4.second
  22.5 0.0 copy-start
  22.5 3.0 %shard_map.85 = (bf16[2,4,96,256]{3,2,1,0:T(8,128)(2,1)S(1)}, bf16[2,1,96,256]{3,2,1,0:T(8,128)(2,1)S(1)}, f32[1,512]{1,0:T(1,128)S(1)}) custom-call(f32[40,256]{1,0:T(8,128)S(1)} %get-tuple-element.28.aux, bf16[1,4,96,256]{3,2,1,0:T(8,128)(2,1)S(1)} %collective-permute-done.first, bf16[1,5,96,256]{3,2,1,0:T(8,128)(2,1)S(1)} %collective-permute-done.4.second, ...), custom_call_target="tpu_custom_call" | custom-call | flops 2717908992 | bytes 1048576 | tf_op jit(solution)/shard_map/pallas_call | solution.py:432
  25.5 0.1 collective-permute-start.5
  25.6 1.1 %collective-permute-done.5 = f32[1,512]{1,0:T(1,128)S(1)} collective-permute-done((f32[1,512]{1,0:T(1,128)S(1)}, f32[1,512]{1,0:T(1,128)S(1)}, u32[]{:S(2)}, u32[]{:S(2)}) %collective-permute-start.5) | collective-permute-done | bytes 2080 | tf_op jit(solution)/shard_map/ppermute | solution.py:32
  26.8 5.1 %collective-permute-start.8 = (f32[1,512]{1,0:T(1,128)S(1)}, f32[1,512]{1,0:T(1,128)S(1)}, u32[]{:S(2)}, u32[]{:S(2)}) collective-permute-start(f32[1,512]{1,0:T(1,128)S(1)} %add.8), channel_id=1, source_target_pairs={{0,24},{2,26},{4,28},{6,30},{8,16},{10,18},{12,20},{14,22},{16,8},... | collective-permute-start | bytes 6152 | tf_op jit(solution)/shard_map/ppermute | solution.py:32
  31.9 0.0 collective-permute-start.7
  31.9 0.6 %collective-permute-start.6 = (f32[1,512]{1,0:T(1,128)S(1)}, f32[1,512]{1,0:T(1,128)S(1)}, u32[]{:S(2)}, u32[]{:S(2)}) collective-permute-start(f32[1,512]{1,0:T(1,128)S(1)} %add.8), channel_id=1, source_target_pairs={{0,8},{2,10},{4,12},{6,14},{8,0},{10,2},{12,4},{14,6},{16,24},{18,... | collective-permute-start | bytes 6152 | tf_op jit(solution)/shard_map/ppermute | solution.py:32
  32.5 0.0 collective-permute-start.13
  32.5 0.9 %collective-permute-done.8 = f32[1,512]{1,0:T(1,128)S(1)} collective-permute-done((f32[1,512]{1,0:T(1,128)S(1)}, f32[1,512]{1,0:T(1,128)S(1)}, u32[]{:S(2)}, u32[]{:S(2)}) %collective-permute-start.8) | collective-permute-done | bytes 2080 | tf_op jit(solution)/shard_map/ppermute | solution.py:32
  33.5 0.0 collective-permute-start.12
  33.5 2.9 %collective-permute-done.7 = f32[1,512]{1,0:T(1,128)S(1)} collective-permute-done((f32[1,512]{1,0:T(1,128)S(1)}, f32[1,512]{1,0:T(1,128)S(1)}, u32[]{:S(2)}, u32[]{:S(2)}) %collective-permute-start.7) | collective-permute-done | bytes 2080 | tf_op jit(solution)/shard_map/ppermute | solution.py:32
  36.4 0.0 collective-permute-done.6
  36.4 0.6 %collective-permute-done.3.refs_8_ = bf16[2,4,96,256]{3,2,1,0:T(8,128)(2,1)S(1)} collective-permute-done((bf16[2,4,96,256]{3,2,1,0:T(8,128)(2,1)S(1)}, bf16[2,4,96,256]{3,2,1,0:T(8,128)(2,1)S(1)}, u32[]{:S(2)}, u32[]{:S(2)}) %collective-permute-start.3) | collective-permute-done | bytes 393248 | tf_op jit(solution)/shard_map/ppermute | solution.py:37
  37.0 0.1 collective-permute-start.14
  37.1 1.1 %collective-permute-start.11 = (f32[4,512]{1,0:T(4,128)S(1)}, f32[4,512]{1,0:T(4,128)S(1)}, u32[]{:S(2)}, u32[]{:S(2)}) collective-permute-start(f32[4,512]{1,0:T(4,128)S(1)} %pad_maximum_fusion.1.refs_0_), channel_id=1, source_target_pairs={{0,6},{2,4},{4,2},{6,0},{8,14},{10,12},{12,10},{14,8},{16,22},{18,... | collective-permute-start | bytes 24584 | tf_op jit(solution)/shard_map/ppermute | solution.py:32
  38.2 0.0 collective-permute-start.10
  38.2 0.0 collective-permute-done.13.refs_7_
  38.2 2.4 %collective-permute-start.9 = (f32[4,512]{1,0:T(4,128)S(1)}, f32[4,512]{1,0:T(4,128)S(1)}, u32[]{:S(2)}, u32[]{:S(2)}) collective-permute-start(f32[4,512]{1,0:T(4,128)S(1)} %pad_maximum_fusion.1.refs_0_), channel_id=1, source_target_pairs={{0,2},{2,0},{4,6},{6,4},{8,10},{10,8},{12,14},{14,12},{16,18},{18,... | collective-permute-start | bytes 24584 | tf_op jit(solution)/shard_map/ppermute | solution.py:32
  40.6 1.1 %collective-permute-done.11.refs_3_ = f32[4,512]{1,0:T(4,128)S(1)} collective-permute-done((f32[4,512]{1,0:T(4,128)S(1)}, f32[4,512]{1,0:T(4,128)S(1)}, u32[]{:S(2)}, u32[]{:S(2)}) %collective-permute-start.11) | collective-permute-done | bytes 8224 | tf_op jit(solution)/shard_map/ppermute | solution.py:32
  41.7 0.2 collective-permute-done.10.refs_2_
  41.8 0.4 collective-permute-done.9.refs_1_
  42.2 0.0 collective-permute-done.12.refs_6_
  42.3 0.0 collective-permute-done.14.refs_9_
  42.3 0.0 copy-done
  42.3 6.8 %shard_map.86 = f32[4,4,96,256]{3,2,1,0:T(8,128)} custom-call(f32[40,256]{1,0:T(8,128)S(1)} %get-tuple-element.28.aux, f32[4,512]{1,0:T(4,128)S(1)} %pad_maximum_fusion.1.refs_0_, f32[4,512]{1,0:T(4,128)S(1)} %collective-permute-done.9.refs_1_, f32[4,512]{1,0:T(4,128)S(1)} %collective-permute-done.10.refs_2_, f32[4,512]{1,0:T(4,128)S(1)} %collective-permute-done.11.refs_3_, ...), custom_call_target="tpu_custom_call" | custom-call | flops 5435817984 | bytes 1048576 | tf_op jit(solution)/shard_map/pallas_call | solution.py:432
  (7 shorter events, 0.1 us)
Async XLA Ops:
  2.0 12.0 %collective-permute-start = (bf16[1,4,96,256]{3,2,1,0:T(8,128)(2,1)S(1)}, bf16[1,4,96,256]{3,2,1,0:T(8,128)(2,1)S(1)}, u32[]{:S(2)}, u32[]{:S(2)}) collective-permute-start(bf16[1,4,96,256]{3,2,1,0:T(8,128)(2,1)S(1)} %get-tuple-element.46), channel_id=1, source_target_pairs={{0,2},{2,4},{4,6},{6,8},{8,10},{10,12},{12,14},{14,16},{16,18},{18... | collective-permute-start | bytes 589832 | tf_op jit(solution)/shard_map/ppermute | solution.py:37
  5.0 12.3 %all-to-all-start = ((f32[32,1,512]{2,1,0:T(1,128)}), f32[32,1,512]{2,1,0:T(1,128)S(1)}, u32[]{:S(2)}, u32[]{:S(2)}) async-start(f32[32,1,512]{2,1,0:T(1,128)} %get-tuple-element.29), calls=%async_computation | async-start | bytes 131072 | tf_op jit(solution)/shard_map/all_to_all | solution.py:41
  9.9 4.1 %collective-permute-start.2 = (bf16[4,1,96,256]{3,2,1,0:T(8,128)(2,1)S(1)}, bf16[4,1,96,256]{3,2,1,0:T(8,128)(2,1)S(1)}, u32[]{:S(2)}, u32[]{:S(2)}) collective-permute-start(bf16[4,1,96,256]{3,2,1,0:T(8,128)(2,1)S(1)} %get-tuple-element.31), channel_id=1, source_target_pairs={{0,1},{1,0},{2,3},{3,2},{4,5},{5,4},{6,7},{7,6},{8,9},{9,8},{10,11... | collective-permute-start | bytes 589832 | tf_op jit(solution)/shard_map/ppermute | solution.py:32
  14.0 1.7 %collective-permute-start.1 = (bf16[1,1,96,256]{3,2,1,0:T(8,128)(2,1)S(1)}, bf16[1,1,96,256]{3,2,1,0:T(8,128)(2,1)S(1)}, u32[]{:S(2)}, u32[]{:S(2)}) collective-permute-start(bf16[1,1,96,256]{3,2,1,0:T(8,128)(2,1)S(1)} %constant_dynamic-slice_fusion.1), channel_id=1, source_target_pairs={{0,1},{1,0},{2,3},{3,2},{4,5},{5,4},{6,7},{7,6},{8,9},{9,8},{10,11... | collective-permute-start | bytes 147464 | tf_op jit(solution)/shard_map/ppermute | solution.py:32
  14.1 8.4 %collective-permute-start.4 = (bf16[1,5,96,256]{3,2,1,0:T(8,128)(2,1)S(1)}, bf16[1,5,96,256]{3,2,1,0:T(8,128)(2,1)S(1)}, u32[]{:S(2)}, u32[]{:S(2)}) collective-permute-start(bf16[1,5,96,256]{3,2,1,0:T(8,128)(2,1)S(1)} %pad_maximum_fusion), channel_id=1, source_target_pairs={{0,2},{2,4},{4,6},{6,8},{8,10},{10,12},{12,14},{14,16},{16,18},{18... | collective-permute-start | bytes 737288 | tf_op jit(solution)/shard_map/ppermute | solution.py:86
  22.0 14.9 %collective-permute-start.3 = (bf16[2,4,96,256]{3,2,1,0:T(8,128)(2,1)S(1)}, bf16[2,4,96,256]{3,2,1,0:T(8,128)(2,1)S(1)}, u32[]{:S(2)}, u32[]{:S(2)}) collective-permute-start(bf16[2,4,96,256]{3,2,1,0:T(8,128)(2,1)S(1)} %get-tuple-element.33.refs_5_), channel_id=1, source_target_pairs={{0,2},{2,4},{4,6},{6,8},{8,10},{10,12},{12,14},{14,16},{16,18},{18... | collective-permute-start | bytes 1179656 | tf_op jit(solution)/shard_map/ppermute | solution.py:37
  22.5 19.7 %copy-start = (bf16[3,3,3,256,256]{4,3,2,1,0:T(8,128)(2,1)S(1)}, bf16[3,3,3,256,256]{4,3,2,1,0:T(8,128)(2,1)}, u32[]{:S(2)}) copy-start(bf16[3,3,3,256,256]{4,3,2,1,0:T(8,128)(2,1)} %refs_10_.1) | copy-start | bytes 10616836
  25.5 1.2 %collective-permute-start.5 = (f32[1,512]{1,0:T(1,128)S(1)}, f32[1,512]{1,0:T(1,128)S(1)}, u32[]{:S(2)}, u32[]{:S(2)}) collective-permute-start(f32[1,512]{1,0:T(1,128)S(1)} %get-tuple-element.39), channel_id=1, source_target_pairs={{0,1},{1,0},{2,3},{3,2},{4,5},{5,4},{6,7},{7,6},{8,9},{9,8},{10,11... | collective-permute-start | bytes 6152 | tf_op jit(solution)/shard_map/ppermute | solution.py:32
  26.8 6.7 %collective-permute-start.8 = (f32[1,512]{1,0:T(1,128)S(1)}, f32[1,512]{1,0:T(1,128)S(1)}, u32[]{:S(2)}, u32[]{:S(2)}) collective-permute-start(f32[1,512]{1,0:T(1,128)S(1)} %add.8), channel_id=1, source_target_pairs={{0,24},{2,26},{4,28},{6,30},{8,16},{10,18},{12,20},{14,22},{16,8},... | collective-permute-start | bytes 6152 | tf_op jit(solution)/shard_map/ppermute | solution.py:32
  31.9 4.5 %collective-permute-start.7 = (f32[1,512]{1,0:T(1,128)S(1)}, f32[1,512]{1,0:T(1,128)S(1)}, u32[]{:S(2)}, u32[]{:S(2)}) collective-permute-start(f32[1,512]{1,0:T(1,128)S(1)} %add.8), channel_id=1, source_target_pairs={{0,16},{2,18},{4,20},{6,22},{8,24},{10,26},{12,28},{14,30},{16,0},... | collective-permute-start | bytes 6152 | tf_op jit(solution)/shard_map/ppermute | solution.py:32
  31.9 4.5 %collective-permute-start.6 = (f32[1,512]{1,0:T(1,128)S(1)}, f32[1,512]{1,0:T(1,128)S(1)}, u32[]{:S(2)}, u32[]{:S(2)}) collective-permute-start(f32[1,512]{1,0:T(1,128)S(1)} %add.8), channel_id=1, source_target_pairs={{0,8},{2,10},{4,12},{6,14},{8,0},{10,2},{12,4},{14,6},{16,24},{18,... | collective-permute-start | bytes 6152 | tf_op jit(solution)/shard_map/ppermute | solution.py:32
  32.5 5.7 %collective-permute-start.13 = (bf16[2,1,96,256]{3,2,1,0:T(8,128)(2,1)S(1)}, bf16[2,1,96,256]{3,2,1,0:T(8,128)(2,1)S(1)}, u32[]{:S(2)}, u32[]{:S(2)}) collective-permute-start(bf16[2,1,96,256]{3,2,1,0:T(8,128)(2,1)S(1)} %get-tuple-element.43), channel_id=1, source_target_pairs={{0,1},{1,0},{2,3},{3,2},{4,5},{5,4},{6,7},{7,6},{8,9},{9,8},{10,11... | collective-permute-start | bytes 294920 | tf_op jit(solution)/shard_map/ppermute | solution.py:32
  33.5 8.8 %collective-permute-start.12 = (bf16[2,1,96,256]{3,2,1,0:T(8,128)(2,1)S(1)}, bf16[2,1,96,256]{3,2,1,0:T(8,128)(2,1)S(1)}, u32[]{:S(2)}, u32[]{:S(2)}) collective-permute-start(bf16[2,1,96,256]{3,2,1,0:T(8,128)(2,1)S(1)} %get-tuple-element.42), channel_id=1, source_target_pairs={{0,1},{1,0},{2,3},{3,2},{4,5},{5,4},{6,7},{7,6},{8,9},{9,8},{10,11... | collective-permute-start | bytes 294920 | tf_op jit(solution)/shard_map/ppermute | solution.py:32
  37.0 5.3 %collective-permute-start.14 = (bf16[2,1,96,256]{3,2,1,0:T(8,128)(2,1)S(1)}, bf16[2,1,96,256]{3,2,1,0:T(8,128)(2,1)S(1)}, u32[]{:S(2)}, u32[]{:S(2)}) collective-permute-start(bf16[2,1,96,256]{3,2,1,0:T(8,128)(2,1)S(1)} %constant_dynamic-slice_fusion), channel_id=1, source_target_pairs={{0,1},{1,0},{2,3},{3,2},{4,5},{5,4},{6,7},{7,6},{8,9},{9,8},{10,11... | collective-permute-start | bytes 294920 | tf_op jit(solution)/shard_map/ppermute | solution.py:32
  37.1 4.6 %collective-permute-start.11 = (f32[4,512]{1,0:T(4,128)S(1)}, f32[4,512]{1,0:T(4,128)S(1)}, u32[]{:S(2)}, u32[]{:S(2)}) collective-permute-start(f32[4,512]{1,0:T(4,128)S(1)} %pad_maximum_fusion.1.refs_0_), channel_id=1, source_target_pairs={{0,6},{2,4},{4,2},{6,0},{8,14},{10,12},{12,10},{14,8},{16,22},{18,... | collective-permute-start | bytes 24584 | tf_op jit(solution)/shard_map/ppermute | solution.py:32
  38.2 3.7 %collective-permute-start.10 = (f32[4,512]{1,0:T(4,128)S(1)}, f32[4,512]{1,0:T(4,128)S(1)}, u32[]{:S(2)}, u32[]{:S(2)}) collective-permute-start(f32[4,512]{1,0:T(4,128)S(1)} %pad_maximum_fusion.1.refs_0_), channel_id=1, source_target_pairs={{0,4},{2,6},{4,0},{6,2},{8,12},{10,14},{12,8},{14,10},{16,20},{18,... | collective-permute-start | bytes 24584 | tf_op jit(solution)/shard_map/ppermute | solution.py:32
  38.2 4.0 %collective-permute-start.9 = (f32[4,512]{1,0:T(4,128)S(1)}, f32[4,512]{1,0:T(4,128)S(1)}, u32[]{:S(2)}, u32[]{:S(2)}) collective-permute-start(f32[4,512]{1,0:T(4,128)S(1)} %pad_maximum_fusion.1.refs_0_), channel_id=1, source_target_pairs={{0,2},{2,0},{4,6},{6,4},{8,10},{10,8},{12,14},{14,12},{16,18},{18,... | collective-permute-start | bytes 24584 | tf_op jit(solution)/shard_map/ppermute | solution.py:32

commit v20 on v19

--- a/solution.py
+++ b/solution.py
@@ -466,7 +466,7 @@
         functools.partial(late_kernel, n_sides),
         late_shapes + hidden_shapes,
         [act_late, pltpu.SemaphoreType.DMA((6,))],
-        2 * work,
+        work * 3 // 4,
         operands,
         outside=(len(operands) - 1,),
     )

time: 49.4 us -> 49.3 us (level)
  starting transfers between devices: 19.8 us -> 20.3 us
    ppermute x1, starting transfers between devices: 1.63 us -> 3.69 us  [chained(): lax.ppermute(value, 'tm', [(i, i + 1) for i in range(lax.axis_size('tm')...]
    ppermute x12, starting transfers between devices: 9.77 us -> 8.61 us  [traded(): lax.ppermute(value, axis, [(i, i ^ mask) for i in range(lax.axis_size(axi...]
    ppermute x2, waiting for transfers between devices: 2.96 us -> 4.02 us  [shifted(): lax.ppermute(value, axis, [(i, (i + step) % peers) for i in range(peers)])]
    ppermute x12, waiting for transfers between devices: 6.63 us -> 5.67 us  [traded(): lax.ppermute(value, axis, [(i, i ^ mask) for i in range(lax.axis_size(axi...]
  transfers between devices with their start and end apart: 16 -> 16, of which waited for: 9 -> 9; matrix products, arithmetic and copies ran while one was open for 0% -> 0% of each run, Pallas kernels for 19% -> 18%
where the time goes in v20:
time: 49.3 us; the launch traced here: 49.1 us
  starting transfers between devices  20.3 us (41%)
  Pallas kernels  17.8 us (36%)
  waiting for transfers between devices  10.8 us (22%)
    pallas_call x3, Pallas kernels, call(): pl.pallas_call(kernel, out_shape=outs, in_specs=[ANYWHERE if k in (aliase...  14.4 us
    ppermute x12, starting transfers between devices, traded(): lax.ppermute(value, axis, [(i, i ^ mask) for i in range(lax.axis_size(axi...  8.61 us
    ppermute x12, waiting for transfers between devices, traded(): lax.ppermute(value, axis, [(i, i ^ mask) for i in range(lax.axis_size(axi...  5.67 us
    all_to_all x1, starting transfers between devices, stats_table(): return lax.all_to_all(copies, ('tm', 'space'), 0, 0, tiled=True)  4.92 us
    ppermute x2, waiting for transfers between devices, shifted(): lax.ppermute(value, axis, [(i, (i + step) % peers) for i in range(peers)])  4.02 us
    ppermute x1, starting transfers between devices, chained(): lax.ppermute(value, 'tm', [(i, i + 1) for i in range(lax.axis_size('tm')...  3.69 us
    ppermute x2, starting transfers between devices, shifted(): lax.ppermute(value, axis, [(i, (i + step) % peers) for i in range(peers)])  3.05 us
    pallas_call x1, Pallas kernels, entry_call(): pl.pallas_call(entry_kernel, out_shape=outs, in_specs=[ANYWHERE], out_spe...  1.95 us
  transfers between devices with their start and end apart: 16, of which 9 were waited for; matrix products, arithmetic and copies ran while one was open for 0% of the time, Pallas kernels for 18%

profile of v20, /device:TPU:0, one launch (start us, length us, event | category | flops | bytes accessed | tf_op | source)
XLA Modules:
  0.0 49.1 jit_solution(10646673324229170644)
XLA Ops:
  0.0 1.9 %shard_map.82 = (bf16[4,4,96,256]{3,2,1,0:T(8,128)(2,1)S(1)}, bf16[2,4,96,256]{3,2,1,0:T(8,128)(2,1)S(1)}, bf16[4,1,96,256]{3,2,1,0:T(8,128)(2,1)S(1)}, f32[32,1,512]{2,1,0:T(1,128)}, f32[8,128]{1,0:T(8,128)S(1)}) custom-call(bf16[4,4,96,256]{3,2,1,0:T(8,128)(2,1)} %feats_hbm.1), custom_call_target="tpu_custom_call" | custom-call | flops 1572864 | bytes 1572864 | tf_op jit(solution)/shard_map/pallas_call | solution.py:181
  2.0 0.5 %collective-permute-start.2 = (bf16[4,1,96,256]{3,2,1,0:T(8,128)(2,1)S(1)}, bf16[4,1,96,256]{3,2,1,0:T(8,128)(2,1)S(1)}, u32[]{:S(2)}, u32[]{:S(2)}) collective-permute-start(bf16[4,1,96,256]{3,2,1,0:T(8,128)(2,1)S(1)} %get-tuple-element.31), channel_id=1, source_target_pairs={{0,1},{1,0},{2,3},{3,2},{4,5},{5,4},{6,7},{7,6},{8,9},{9,8},{10,11... | collective-permute-start | bytes 589832 | tf_op jit(solution)/shard_map/ppermute | solution.py:32
  2.5 2.6 %collective-permute-start = (bf16[1,4,96,256]{3,2,1,0:T(8,128)(2,1)S(1)}, bf16[1,4,96,256]{3,2,1,0:T(8,128)(2,1)S(1)}, u32[]{:S(2)}, u32[]{:S(2)}) collective-permute-start(bf16[1,4,96,256]{3,2,1,0:T(8,128)(2,1)S(1)} %get-tuple-element.46), channel_id=1, source_target_pairs={{0,2},{2,4},{4,6},{6,8},{8,10},{10,12},{12,14},{14,16},{16,18},{18... | collective-permute-start | bytes 589832 | tf_op jit(solution)/shard_map/ppermute | solution.py:37
  5.1 4.9 %all-to-all-start = ((f32[32,1,512]{2,1,0:T(1,128)}), f32[32,1,512]{2,1,0:T(1,128)S(1)}, u32[]{:S(2)}, u32[]{:S(2)}) async-start(f32[32,1,512]{2,1,0:T(1,128)} %get-tuple-element.29), calls=%async_computation | async-start | bytes 131072 | tf_op jit(solution)/shard_map/all_to_all | solution.py:41
  10.0 0.0 collective-permute-done.2.refs_0_
  10.1 3.7 %collective-permute-start.4 = (bf16[1,5,96,256]{3,2,1,0:T(8,128)(2,1)S(1)}, bf16[1,5,96,256]{3,2,1,0:T(8,128)(2,1)S(1)}, u32[]{:S(2)}, u32[]{:S(2)}) collective-permute-start(bf16[1,5,96,256]{3,2,1,0:T(8,128)(2,1)S(1)} %pad_maximum_fusion), channel_id=1, source_target_pairs={{0,2},{2,4},{4,6},{6,8},{8,10},{10,12},{12,14},{14,16},{16,18},{18... | collective-permute-start | bytes 737288 | tf_op jit(solution)/shard_map/ppermute | solution.py:86
  13.7 1.1 %collective-permute-done.first = bf16[1,4,96,256]{3,2,1,0:T(8,128)(2,1)S(1)} collective-permute-done((bf16[1,4,96,256]{3,2,1,0:T(8,128)(2,1)S(1)}, bf16[1,4,96,256]{3,2,1,0:T(8,128)(2,1)S(1)}, u32[]{:S(2)}, u32[]{:S(2)}) %collective-permute-start) | collective-permute-done | bytes 196640 | tf_op jit(solution)/shard_map/ppermute | solution.py:37
  14.9 0.0 collective-permute-start.1
  14.9 1.4 %shard_map.83 = (bf16[1,3,3,256,256]{4,3,2,1,0:T(8,128)(2,1)S(1)}, f32[40,256]{1,0:T(8,128)S(1)}) custom-call(bf16[3,3,3,256,256]{4,3,2,1,0:T(8,128)(2,1)} %refs_2_.1, s32[16]{0:T(128)} %clips_hbm.1, f32[1,256]{1,0:T(1,128)} %bitcast.4, f32[1,256]{1,0:T(1,128)} %bitcast.5, f32[1,256]{1,0:T(1,128)} %bitcast.6, f32[1,256]{1,0:T(1,128)} %bitcast.7, ...), custom_call_target="tpu_custom_call" | custom-call | flops 1073741824 | bytes 65536 | tf_op jit(solution)/shard_map/pallas_call | solution.py:225
  16.3 0.0 collective-permute-done.1.refs_0_
  16.3 1.1 %all-to-all-done.table = f32[32,1,512]{2,1,0:T(1,128)S(1)} async-done(((f32[32,1,512]{2,1,0:T(1,128)}), f32[32,1,512]{2,1,0:T(1,128)S(1)}, u32[]{:S(2)}, u32[]{:S(2)}) %all-to-all-start) | async-done | bytes 65568 | tf_op jit(solution)/shard_map/all_to_all | solution.py:41
  17.4 4.7 %shard_map.84 = (bf16[2,6,96,256]{3,2,1,0:T(8,128)(2,1)S(1)}, f32[2,256]{1,0:T(2,128)S(1)}, bf16[2,3,3,256,256]{4,3,2,1,0:T(8,128)(2,1)S(1)}, bf16[2,4,96,256]{3...) custom-call(f32[40,256]{1,0:T(8,128)S(1)} %get-tuple-element.28.aux, ...), custom_call_target="tpu_custom_call" | custom-call | flops 1019215872 | bytes 1048576 | tf_op jit(solution)/shard_map/pallas_call | solution.py:432
  22.1 0.5 collective-permute-start.3
  22.6 0.0 collective-permute-done.4.second
  22.6 0.0 copy-start
  22.6 3.0 %shard_map.85 = (bf16[2,4,96,256]{3,2,1,0:T(8,128)(2,1)S(1)}, bf16[2,1,96,256]{3,2,1,0:T(8,128)(2,1)S(1)}, f32[1,512]{1,0:T(1,128)S(1)}) custom-call(f32[40,256]{1,0:T(8,128)S(1)} %get-tuple-element.28.aux, bf16[1,4,96,256]{3,2,1,0:T(8,128)(2,1)S(1)} %collective-permute-done.first, bf16[1,5,96,256]{3,2,1,0:T(8,128)(2,1)S(1)} %collective-permute-done.4.second, ...), custom_call_target="tpu_custom_call" | custom-call | flops 2717908992 | bytes 1048576 | tf_op jit(solution)/shard_map/pallas_call | solution.py:432
  25.6 0.1 collective-permute-start.5
  25.7 1.1 %collective-permute-done.5 = f32[1,512]{1,0:T(1,128)S(1)} collective-permute-done((f32[1,512]{1,0:T(1,128)S(1)}, f32[1,512]{1,0:T(1,128)S(1)}, u32[]{:S(2)}, u32[]{:S(2)}) %collective-permute-start.5) | collective-permute-done | bytes 2080 | tf_op jit(solution)/shard_map/ppermute | solution.py:32
  26.8 2.8 %collective-permute-start.8 = (f32[1,512]{1,0:T(1,128)S(1)}, f32[1,512]{1,0:T(1,128)S(1)}, u32[]{:S(2)}, u32[]{:S(2)}) collective-permute-start(f32[1,512]{1,0:T(1,128)S(1)} %add.8), channel_id=1, source_target_pairs={{0,24},{2,26},{4,28},{6,30},{8,16},{10,18},{12,20},{14,22},{16,8},... | collective-permute-start | bytes 6152 | tf_op jit(solution)/shard_map/ppermute | solution.py:32
  29.6 0.0 collective-permute-start.7
  29.6 1.6 %collective-permute-start.6 = (f32[1,512]{1,0:T(1,128)S(1)}, f32[1,512]{1,0:T(1,128)S(1)}, u32[]{:S(2)}, u32[]{:S(2)}) collective-permute-start(f32[1,512]{1,0:T(1,128)S(1)} %add.8), channel_id=1, source_target_pairs={{0,8},{2,10},{4,12},{6,14},{8,0},{10,2},{12,4},{14,6},{16,24},{18,... | collective-permute-start | bytes 6152 | tf_op jit(solution)/shard_map/ppermute | solution.py:32
  31.2 0.0 collective-permute-start.13
  31.2 1.0 %collective-permute-done.8 = f32[1,512]{1,0:T(1,128)S(1)} collective-permute-done((f32[1,512]{1,0:T(1,128)S(1)}, f32[1,512]{1,0:T(1,128)S(1)}, u32[]{:S(2)}, u32[]{:S(2)}) %collective-permute-start.8) | collective-permute-done | bytes 2080 | tf_op jit(solution)/shard_map/ppermute | solution.py:32
  32.2 0.0 collective-permute-start.12
  32.2 1.9 %collective-permute-done.7 = f32[1,512]{1,0:T(1,128)S(1)} collective-permute-done((f32[1,512]{1,0:T(1,128)S(1)}, f32[1,512]{1,0:T(1,128)S(1)}, u32[]{:S(2)}, u32[]{:S(2)}) %collective-permute-start.7) | collective-permute-done | bytes 2080 | tf_op jit(solution)/shard_map/ppermute | solution.py:32
  34.1 0.0 collective-permute-done.6
  34.1 2.9 %collective-permute-done.3.refs_8_ = bf16[2,4,96,256]{3,2,1,0:T(8,128)(2,1)S(1)} collective-permute-done((bf16[2,4,96,256]{3,2,1,0:T(8,128)(2,1)S(1)}, bf16[2,4,96,256]{3,2,1,0:T(8,128)(2,1)S(1)}, u32[]{:S(2)}, u32[]{:S(2)}) %collective-permute-start.3) | collective-permute-done | bytes 393248 | tf_op jit(solution)/shard_map/ppermute | solution.py:37
  37.0 0.1 collective-permute-start.14
  37.1 1.1 %collective-permute-start.11 = (f32[4,512]{1,0:T(4,128)S(1)}, f32[4,512]{1,0:T(4,128)S(1)}, u32[]{:S(2)}, u32[]{:S(2)}) collective-permute-start(f32[4,512]{1,0:T(4,128)S(1)} %pad_maximum_fusion.1.refs_0_), channel_id=1, source_target_pairs={{0,6},{2,4},{4,2},{6,0},{8,14},{10,12},{12,10},{14,8},{16,22},{18,... | collective-permute-start | bytes 24584 | tf_op jit(solution)/shard_map/ppermute | solution.py:32
  38.2 0.0 collective-permute-start.10
  38.2 0.0 collective-permute-done.13.refs_7_
  38.2 2.4 %collective-permute-start.9 = (f32[4,512]{1,0:T(4,128)S(1)}, f32[4,512]{1,0:T(4,128)S(1)}, u32[]{:S(2)}, u32[]{:S(2)}) collective-permute-start(f32[4,512]{1,0:T(4,128)S(1)} %pad_maximum_fusion.1.refs_0_), channel_id=1, source_target_pairs={{0,2},{2,0},{4,6},{6,4},{8,10},{10,8},{12,14},{14,12},{16,18},{18,... | collective-permute-start | bytes 24584 | tf_op jit(solution)/shard_map/ppermute | solution.py:32
  40.7 1.1 %collective-permute-done.11.refs_3_ = f32[4,512]{1,0:T(4,128)S(1)} collective-permute-done((f32[4,512]{1,0:T(4,128)S(1)}, f32[4,512]{1,0:T(4,128)S(1)}, u32[]{:S(2)}, u32[]{:S(2)}) %collective-permute-start.11) | collective-permute-done | bytes 8224 | tf_op jit(solution)/shard_map/ppermute | solution.py:32
  41.7 0.2 collective-permute-done.10.refs_2_
  41.9 0.4 collective-permute-done.9.refs_1_
  42.3 0.0 collective-permute-done.12.refs_6_
  42.3 0.0 collective-permute-done.14.refs_9_
  42.3 0.0 copy-done
  42.3 6.8 %shard_map.86 = f32[4,4,96,256]{3,2,1,0:T(8,128)} custom-call(f32[40,256]{1,0:T(8,128)S(1)} %get-tuple-element.28.aux, f32[4,512]{1,0:T(4,128)S(1)} %pad_maximum_fusion.1.refs_0_, f32[4,512]{1,0:T(4,128)S(1)} %collective-permute-done.9.refs_1_, f32[4,512]{1,0:T(4,128)S(1)} %collective-permute-done.10.refs_2_, f32[4,512]{1,0:T(4,128)S(1)} %collective-permute-done.11.refs_3_, ...), custom_call_target="tpu_custom_call" | custom-call | flops 5435817984 | bytes 1048576 | tf_op jit(solution)/shard_map/pallas_call | solution.py:432
  (7 shorter events, 0.1 us)
Async XLA Ops:
  2.0 8.0 %collective-permute-start.2 = (bf16[4,1,96,256]{3,2,1,0:T(8,128)(2,1)S(1)}, bf16[4,1,96,256]{3,2,1,0:T(8,128)(2,1)S(1)}, u32[]{:S(2)}, u32[]{:S(2)}) collective-permute-start(bf16[4,1,96,256]{3,2,1,0:T(8,128)(2,1)S(1)} %get-tuple-element.31), channel_id=1, source_target_pairs={{0,1},{1,0},{2,3},{3,2},{4,5},{5,4},{6,7},{7,6},{8,9},{9,8},{10,11... | collective-permute-start | bytes 589832 | tf_op jit(solution)/shard_map/ppermute | solution.py:32
  2.5 12.4 %collective-permute-start = (bf16[1,4,96,256]{3,2,1,0:T(8,128)(2,1)S(1)}, bf16[1,4,96,256]{3,2,1,0:T(8,128)(2,1)S(1)}, u32[]{:S(2)}, u32[]{:S(2)}) collective-permute-start(bf16[1,4,96,256]{3,2,1,0:T(8,128)(2,1)S(1)} %get-tuple-element.46), channel_id=1, source_target_pairs={{0,2},{2,4},{4,6},{6,8},{8,10},{10,12},{12,14},{14,16},{16,18},{18... | collective-permute-start | bytes 589832 | tf_op jit(solution)/shard_map/ppermute | solution.py:37
  5.1 12.3 %all-to-all-start = ((f32[32,1,512]{2,1,0:T(1,128)}), f32[32,1,512]{2,1,0:T(1,128)S(1)}, u32[]{:S(2)}, u32[]{:S(2)}) async-start(f32[32,1,512]{2,1,0:T(1,128)} %get-tuple-element.29), calls=%async_computation | async-start | bytes 131072 | tf_op jit(solution)/shard_map/all_to_all | solution.py:41
  10.1 12.5 %collective-permute-start.4 = (bf16[1,5,96,256]{3,2,1,0:T(8,128)(2,1)S(1)}, bf16[1,5,96,256]{3,2,1,0:T(8,128)(2,1)S(1)}, u32[]{:S(2)}, u32[]{:S(2)}) collective-permute-start(bf16[1,5,96,256]{3,2,1,0:T(8,128)(2,1)S(1)} %pad_maximum_fusion), channel_id=1, source_target_pairs={{0,2},{2,4},{4,6},{6,8},{8,10},{10,12},{12,14},{14,16},{16,18},{18... | collective-permute-start | bytes 737288 | tf_op jit(solution)/shard_map/ppermute | solution.py:86
  14.9 1.4 %collective-permute-start.1 = (bf16[1,1,96,256]{3,2,1,0:T(8,128)(2,1)S(1)}, bf16[1,1,96,256]{3,2,1,0:T(8,128)(2,1)S(1)}, u32[]{:S(2)}, u32[]{:S(2)}) collective-permute-start(bf16[1,1,96,256]{3,2,1,0:T(8,128)(2,1)S(1)} %constant_dynamic-slice_fusion.1), channel_id=1, source_target_pairs={{0,1},{1,0},{2,3},{3,2},{4,5},{5,4},{6,7},{7,6},{8,9},{9,8},{10,11... | collective-permute-start | bytes 147464 | tf_op jit(solution)/shard_map/ppermute | solution.py:32
  22.1 14.9 %collective-permute-start.3 = (bf16[2,4,96,256]{3,2,1,0:T(8,128)(2,1)S(1)}, bf16[2,4,96,256]{3,2,1,0:T(8,128)(2,1)S(1)}, u32[]{:S(2)}, u32[]{:S(2)}) collective-permute-start(bf16[2,4,96,256]{3,2,1,0:T(8,128)(2,1)S(1)} %get-tuple-element.33.refs_5_), channel_id=1, source_target_pairs={{0,2},{2,4},{4,6},{6,8},{8,10},{10,12},{12,14},{14,16},{16,18},{18... | collective-permute-start | bytes 1179656 | tf_op jit(solution)/shard_map/ppermute | solution.py:37
  22.6 19.7 %copy-start = (bf16[3,3,3,256,256]{4,3,2,1,0:T(8,128)(2,1)S(1)}, bf16[3,3,3,256,256]{4,3,2,1,0:T(8,128)(2,1)}, u32[]{:S(2)}) copy-start(bf16[3,3,3,256,256]{4,3,2,1,0:T(8,128)(2,1)} %refs_10_.1) | copy-start | bytes 10616836
  25.6 1.2 %collective-permute-start.5 = (f32[1,512]{1,0:T(1,128)S(1)}, f32[1,512]{1,0:T(1,128)S(1)}, u32[]{:S(2)}, u32[]{:S(2)}) collective-permute-start(f32[1,512]{1,0:T(1,128)S(1)} %get-tuple-element.39), channel_id=1, source_target_pairs={{0,1},{1,0},{2,3},{3,2},{4,5},{5,4},{6,7},{7,6},{8,9},{9,8},{10,11... | collective-permute-start | bytes 6152 | tf_op jit(solution)/shard_map/ppermute | solution.py:32
  26.8 5.4 %collective-permute-start.8 = (f32[1,512]{1,0:T(1,128)S(1)}, f32[1,512]{1,0:T(1,128)S(1)}, u32[]{:S(2)}, u32[]{:S(2)}) collective-permute-start(f32[1,512]{1,0:T(1,128)S(1)} %add.8), channel_id=1, source_target_pairs={{0,24},{2,26},{4,28},{6,30},{8,16},{10,18},{12,20},{14,22},{16,8},... | collective-permute-start | bytes 6152 | tf_op jit(solution)/shard_map/ppermute | solution.py:32
  29.6 4.5 %collective-permute-start.7 = (f32[1,512]{1,0:T(1,128)S(1)}, f32[1,512]{1,0:T(1,128)S(1)}, u32[]{:S(2)}, u32[]{:S(2)}) collective-permute-start(f32[1,512]{1,0:T(1,128)S(1)} %add.8), channel_id=1, source_target_pairs={{0,16},{2,18},{4,20},{6,22},{8,24},{10,26},{12,28},{14,30},{16,0},... | collective-permute-start | bytes 6152 | tf_op jit(solution)/shard_map/ppermute | solution.py:32
  29.6 4.5 %collective-permute-start.6 = (f32[1,512]{1,0:T(1,128)S(1)}, f32[1,512]{1,0:T(1,128)S(1)}, u32[]{:S(2)}, u32[]{:S(2)}) collective-permute-start(f32[1,512]{1,0:T(1,128)S(1)} %add.8), channel_id=1, source_target_pairs={{0,8},{2,10},{4,12},{6,14},{8,0},{10,2},{12,4},{14,6},{16,24},{18,... | collective-permute-start | bytes 6152 | tf_op jit(solution)/shard_map/ppermute | solution.py:32
  31.2 7.0 %collective-permute-start.13 = (bf16[2,1,96,256]{3,2,1,0:T(8,128)(2,1)S(1)}, bf16[2,1,96,256]{3,2,1,0:T(8,128)(2,1)S(1)}, u32[]{:S(2)}, u32[]{:S(2)}) collective-permute-start(bf16[2,1,96,256]{3,2,1,0:T(8,128)(2,1)S(1)} %get-tuple-element.43), channel_id=1, source_target_pairs={{0,1},{1,0},{2,3},{3,2},{4,5},{5,4},{6,7},{7,6},{8,9},{9,8},{10,11... | collective-permute-start | bytes 294920 | tf_op jit(solution)/shard_map/ppermute | solution.py:32
  32.2 10.1 %collective-permute-start.12 = (bf16[2,1,96,256]{3,2,1,0:T(8,128)(2,1)S(1)}, bf16[2,1,96,256]{3,2,1,0:T(8,128)(2,1)S(1)}, u32[]{:S(2)}, u32[]{:S(2)}) collective-permute-start(bf16[2,1,96,256]{3,2,1,0:T(8,128)(2,1)S(1)} %get-tuple-element.42), channel_id=1, source_target_pairs={{0,1},{1,0},{2,3},{3,2},{4,5},{5,4},{6,7},{7,6},{8,9},{9,8},{10,11... | collective-permute-start | bytes 294920 | tf_op jit(solution)/shard_map/ppermute | solution.py:32
  37.0 5.3 %collective-permute-start.14 = (bf16[2,1,96,256]{3,2,1,0:T(8,128)(2,1)S(1)}, bf16[2,1,96,256]{3,2,1,0:T(8,128)(2,1)S(1)}, u32[]{:S(2)}, u32[]{:S(2)}) collective-permute-start(bf16[2,1,96,256]{3,2,1,0:T(8,128)(2,1)S(1)} %constant_dynamic-slice_fusion), channel_id=1, source_target_pairs={{0,1},{1,0},{2,3},{3,2},{4,5},{5,4},{6,7},{7,6},{8,9},{9,8},{10,11... | collective-permute-start | bytes 294920 | tf_op jit(solution)/shard_map/ppermute | solution.py:32
  37.1 4.6 %collective-permute-start.11 = (f32[4,512]{1,0:T(4,128)S(1)}, f32[4,512]{1,0:T(4,128)S(1)}, u32[]{:S(2)}, u32[]{:S(2)}) collective-permute-start(f32[4,512]{1,0:T(4,128)S(1)} %pad_maximum_fusion.1.refs_0_), channel_id=1, source_target_pairs={{0,6},{2,4},{4,2},{6,0},{8,14},{10,12},{12,10},{14,8},{16,22},{18,... | collective-permute-start | bytes 24584 | tf_op jit(solution)/shard_map/ppermute | solution.py:32
  38.2 3.7 %collective-permute-start.10 = (f32[4,512]{1,0:T(4,128)S(1)}, f32[4,512]{1,0:T(4,128)S(1)}, u32[]{:S(2)}, u32[]{:S(2)}) collective-permute-start(f32[4,512]{1,0:T(4,128)S(1)} %pad_maximum_fusion.1.refs_0_), channel_id=1, source_target_pairs={{0,4},{2,6},{4,0},{6,2},{8,12},{10,14},{12,8},{14,10},{16,20},{18,... | collective-permute-start | bytes 24584 | tf_op jit(solution)/shard_map/ppermute | solution.py:32
  38.2 4.0 %collective-permute-start.9 = (f32[4,512]{1,0:T(4,128)S(1)}, f32[4,512]{1,0:T(4,128)S(1)}, u32[]{:S(2)}, u32[]{:S(2)}) collective-permute-start(f32[4,512]{1,0:T(4,128)S(1)} %pad_maximum_fusion.1.refs_0_), channel_id=1, source_target_pairs={{0,2},{2,0},{4,6},{6,4},{8,10},{10,8},{12,14},{14,12},{16,18},{18,... | collective-permute-start | bytes 24584 | tf_op jit(solution)/shard_map/ppermute | solution.py:32

commit v21 on v20

--- a/solution.py
+++ b/solution.py
@@ -470,7 +470,7 @@
         operands,
         outside=(len(operands) - 1,),
     )
-    before = shifted(hidden_late[late - 2 :], "tm", 1)
+    before = chained(hidden_late[late - 2 :])
     sides_late = row_halo(edges)
     hidden_early, edges, stats = call(
         functools.partial(early_kernel, n_sides),

time: 49.3 us -> 49.3 us (level)
  waiting for transfers between devices: 10.8 us -> 8.81 us
  starting transfers between devices: 20.3 us -> 22.1 us
    ppermute x2 -> x1, waiting for transfers between devices: 4.02 us -> 1.11 us  [shifted(): lax.ppermute(value, axis, [(i, (i + step) % peers) for i in range(peers)])]
    ppermute x1 -> x2, starting transfers between devices: 3.69 us -> 6.05 us  [chained(): lax.ppermute(value, 'tm', [(i, i + 1) for i in range(lax.axis_size('tm')...]
    ppermute x12, waiting for transfers between devices: 5.67 us -> 6.58 us  [traded(): lax.ppermute(value, axis, [(i, i ^ mask) for i in range(lax.axis_size(axi...]
    ppermute x2 -> x1, starting transfers between devices: 3.05 us -> 2.56 us  [shifted(): lax.ppermute(value, axis, [(i, (i + step) % peers) for i in range(peers)])]
  transfers between devices with their start and end apart: 16 -> 16, of which waited for: 9 -> 8; matrix products, arithmetic and copies ran while one was open for 0% -> 0% of each run, Pallas kernels for 18% -> 19%
where the time goes in v21:
time: 49.3 us; the launch traced here: 49 us
  starting transfers between devices  22.1 us (45%)
  Pallas kernels  17.8 us (36%)
  waiting for transfers between devices  8.81 us (18%)
    pallas_call x3, Pallas kernels, call(): pl.pallas_call(kernel, out_shape=outs, in_specs=[ANYWHERE if k in (aliase...  14.4 us
    ppermute x12, starting transfers between devices, traded(): lax.ppermute(value, axis, [(i, i ^ mask) for i in range(lax.axis_size(axi...  8.61 us
    ppermute x12, waiting for transfers between devices, traded(): lax.ppermute(value, axis, [(i, i ^ mask) for i in range(lax.axis_size(axi...  6.58 us
    ppermute x2, starting transfers between devices, chained(): lax.ppermute(value, 'tm', [(i, i + 1) for i in range(lax.axis_size('tm')...  6.05 us
    all_to_all x1, starting transfers between devices, stats_table(): return lax.all_to_all(copies, ('tm', 'space'), 0, 0, tiled=True)  4.92 us
    ppermute x1, starting transfers between devices, shifted(): lax.ppermute(value, axis, [(i, (i + step) % peers) for i in range(peers)])  2.56 us
    pallas_call x1, Pallas kernels, entry_call(): pl.pallas_call(entry_kernel, out_shape=outs, in_specs=[ANYWHERE], out_spe...  1.95 us
    pallas_call x1, Pallas kernels, setup_call(): pl.pallas_call(functools.partial(setup_kernel, slabs, per_slab), out_shap...  1.39 us
  transfers between devices with their start and end apart: 16, of which 8 were waited for; matrix products, arithmetic and copies ran while one was open for 0% of the time, Pallas kernels for 19%

profile of v21, /device:TPU:0, one launch (start us, length us, event | category | flops | bytes accessed | tf_op | source)
XLA Modules:
  0.0 49.0 jit_solution(7499738327201654062)
XLA Ops:
  0.0 1.9 %shard_map.82 = (bf16[4,4,96,256]{3,2,1,0:T(8,128)(2,1)S(1)}, bf16[2,4,96,256]{3,2,1,0:T(8,128)(2,1)S(1)}, bf16[4,1,96,256]{3,2,1,0:T(8,128)(2,1)S(1)}, f32[32,1,512]{2,1,0:T(1,128)}, f32[8,128]{1,0:T(8,128)S(1)}) custom-call(bf16[4,4,96,256]{3,2,1,0:T(8,128)(2,1)} %feats_hbm.1), custom_call_target="tpu_custom_call" | custom-call | flops 1572864 | bytes 1572864 | tf_op jit(solution)/shard_map/pallas_call | solution.py:181
  2.0 0.5 %collective-permute-start.2 = (bf16[4,1,96,256]{3,2,1,0:T(8,128)(2,1)S(1)}, bf16[4,1,96,256]{3,2,1,0:T(8,128)(2,1)S(1)}, u32[]{:S(2)}, u32[]{:S(2)}) collective-permute-start(bf16[4,1,96,256]{3,2,1,0:T(8,128)(2,1)S(1)} %get-tuple-element.31), channel_id=1, source_target_pairs={{0,1},{1,0},{2,3},{3,2},{4,5},{5,4},{6,7},{7,6},{8,9},{9,8},{10,11... | collective-permute-start | bytes 589832 | tf_op jit(solution)/shard_map/ppermute | solution.py:32
  2.5 2.6 %collective-permute-start = (bf16[1,4,96,256]{3,2,1,0:T(8,128)(2,1)S(1)}, bf16[1,4,96,256]{3,2,1,0:T(8,128)(2,1)S(1)}, u32[]{:S(2)}, u32[]{:S(2)}) collective-permute-start(bf16[1,4,96,256]{3,2,1,0:T(8,128)(2,1)S(1)} %get-tuple-element.46), channel_id=1, source_target_pairs={{0,2},{2,4},{4,6},{6,8},{8,10},{10,12},{12,14},{14,16},{16,18},{18... | collective-permute-start | bytes 589832 | tf_op jit(solution)/shard_map/ppermute | solution.py:37
  5.1 4.9 %all-to-all-start = ((f32[32,1,512]{2,1,0:T(1,128)}), f32[32,1,512]{2,1,0:T(1,128)S(1)}, u32[]{:S(2)}, u32[]{:S(2)}) async-start(f32[32,1,512]{2,1,0:T(1,128)} %get-tuple-element.29), calls=%async_computation | async-start | bytes 131072 | tf_op jit(solution)/shard_map/all_to_all | solution.py:41
  10.0 0.0 collective-permute-done.2.refs_0_
  10.1 3.7 %collective-permute-start.4 = (bf16[1,5,96,256]{3,2,1,0:T(8,128)(2,1)S(1)}, bf16[1,5,96,256]{3,2,1,0:T(8,128)(2,1)S(1)}, u32[]{:S(2)}, u32[]{:S(2)}) collective-permute-start(bf16[1,5,96,256]{3,2,1,0:T(8,128)(2,1)S(1)} %pad_maximum_fusion), channel_id=1, source_target_pairs={{0,2},{2,4},{4,6},{6,8},{8,10},{10,12},{12,14},{14,16},{16,18},{18... | collective-permute-start | bytes 737288 | tf_op jit(solution)/shard_map/ppermute | solution.py:86
  13.7 1.1 %collective-permute-done.first = bf16[1,4,96,256]{3,2,1,0:T(8,128)(2,1)S(1)} collective-permute-done((bf16[1,4,96,256]{3,2,1,0:T(8,128)(2,1)S(1)}, bf16[1,4,96,256]{3,2,1,0:T(8,128)(2,1)S(1)}, u32[]{:S(2)}, u32[]{:S(2)}) %collective-permute-start) | collective-permute-done | bytes 196640 | tf_op jit(solution)/shard_map/ppermute | solution.py:37
  14.9 0.0 collective-permute-start.1
  14.9 1.4 %shard_map.83 = (bf16[1,3,3,256,256]{4,3,2,1,0:T(8,128)(2,1)S(1)}, f32[40,256]{1,0:T(8,128)S(1)}) custom-call(bf16[3,3,3,256,256]{4,3,2,1,0:T(8,128)(2,1)} %refs_2_.1, s32[16]{0:T(128)} %clips_hbm.1, f32[1,256]{1,0:T(1,128)} %bitcast.4, f32[1,256]{1,0:T(1,128)} %bitcast.5, f32[1,256]{1,0:T(1,128)} %bitcast.6, f32[1,256]{1,0:T(1,128)} %bitcast.7, ...), custom_call_target="tpu_custom_call" | custom-call | flops 1073741824 | bytes 65536 | tf_op jit(solution)/shard_map/pallas_call | solution.py:225
  16.3 0.0 collective-permute-done.1.refs_0_
  16.3 1.1 %all-to-all-done.table = f32[32,1,512]{2,1,0:T(1,128)S(1)} async-done(((f32[32,1,512]{2,1,0:T(1,128)}), f32[32,1,512]{2,1,0:T(1,128)S(1)}, u32[]{:S(2)}, u32[]{:S(2)}) %all-to-all-start) | async-done | bytes 65568 | tf_op jit(solution)/shard_map/all_to_all | solution.py:41
  17.4 4.7 %shard_map.84 = (bf16[2,6,96,256]{3,2,1,0:T(8,128)(2,1)S(1)}, f32[2,256]{1,0:T(2,128)S(1)}, bf16[2,3,3,256,256]{4,3,2,1,0:T(8,128)(2,1)S(1)}, bf16[2,4,96,256]{3...) custom-call(f32[40,256]{1,0:T(8,128)S(1)} %get-tuple-element.28.aux, ...), custom_call_target="tpu_custom_call" | custom-call | flops 1019215872 | bytes 1048576 | tf_op jit(solution)/shard_map/pallas_call | solution.py:432
  22.1 2.4 %collective-permute-start.3 = (bf16[2,4,96,256]{3,2,1,0:T(8,128)(2,1)S(1)}, bf16[2,4,96,256]{3,2,1,0:T(8,128)(2,1)S(1)}, u32[]{:S(2)}, u32[]{:S(2)}) collective-permute-start(bf16[2,4,96,256]{3,2,1,0:T(8,128)(2,1)S(1)} %get-tuple-element.33.refs_5_), channel_id=1, source_target_pairs={{0,2},{2,4},{4,6},{6,8},{8,10},{10,12},{12,14},{14,16},{16,18},{18... | collective-permute-start | bytes 1179656 | tf_op jit(solution)/shard_map/ppermute | solution.py:86
  24.5 0.0 collective-permute-done.4.second
  24.5 0.0 copy-start
  24.5 3.0 %shard_map.85 = (bf16[2,4,96,256]{3,2,1,0:T(8,128)(2,1)S(1)}, bf16[2,1,96,256]{3,2,1,0:T(8,128)(2,1)S(1)}, f32[1,512]{1,0:T(1,128)S(1)}) custom-call(f32[40,256]{1,0:T(8,128)S(1)} %get-tuple-element.28.aux, bf16[1,4,96,256]{3,2,1,0:T(8,128)(2,1)S(1)} %collective-permute-done.first, bf16[1,5,96,256]{3,2,1,0:T(8,128)(2,1)S(1)} %collective-permute-done.4.second, ...), custom_call_target="tpu_custom_call" | custom-call | flops 2717908992 | bytes 1048576 | tf_op jit(solution)/shard_map/pallas_call | solution.py:432
  27.5 0.1 collective-permute-start.5
  27.6 1.1 %collective-permute-done.5 = f32[1,512]{1,0:T(1,128)S(1)} collective-permute-done((f32[1,512]{1,0:T(1,128)S(1)}, f32[1,512]{1,0:T(1,128)S(1)}, u32[]{:S(2)}, u32[]{:S(2)}) %collective-permute-start.5) | collective-permute-done | bytes 2080 | tf_op jit(solution)/shard_map/ppermute | solution.py:32
  28.7 2.2 %collective-permute-start.8 = (f32[1,512]{1,0:T(1,128)S(1)}, f32[1,512]{1,0:T(1,128)S(1)}, u32[]{:S(2)}, u32[]{:S(2)}) collective-permute-start(f32[1,512]{1,0:T(1,128)S(1)} %add.8), channel_id=1, source_target_pairs={{0,24},{2,26},{4,28},{6,30},{8,16},{10,18},{12,20},{14,22},{16,8},... | collective-permute-start | bytes 6152 | tf_op jit(solution)/shard_map/ppermute | solution.py:32
  30.9 0.0 collective-permute-start.7
  30.9 2.2 %collective-permute-start.6 = (f32[1,512]{1,0:T(1,128)S(1)}, f32[1,512]{1,0:T(1,128)S(1)}, u32[]{:S(2)}, u32[]{:S(2)}) collective-permute-start(f32[1,512]{1,0:T(1,128)S(1)} %add.8), channel_id=1, source_target_pairs={{0,8},{2,10},{4,12},{6,14},{8,0},{10,2},{12,4},{14,6},{16,24},{18,... | collective-permute-start | bytes 6152 | tf_op jit(solution)/shard_map/ppermute | solution.py:32
  33.1 0.0 collective-permute-start.13
  33.1 1.0 %collective-permute-done.8 = f32[1,512]{1,0:T(1,128)S(1)} collective-permute-done((f32[1,512]{1,0:T(1,128)S(1)}, f32[1,512]{1,0:T(1,128)S(1)}, u32[]{:S(2)}, u32[]{:S(2)}) %collective-permute-start.8) | collective-permute-done | bytes 2080 | tf_op jit(solution)/shard_map/ppermute | solution.py:32
  34.1 0.0 collective-permute-start.12
  34.1 1.3 %collective-permute-done.7 = f32[1,512]{1,0:T(1,128)S(1)} collective-permute-done((f32[1,512]{1,0:T(1,128)S(1)}, f32[1,512]{1,0:T(1,128)S(1)}, u32[]{:S(2)}, u32[]{:S(2)}) %collective-permute-start.7) | collective-permute-done | bytes 2080 | tf_op jit(solution)/shard_map/ppermute | solution.py:32
  35.4 0.0 collective-permute-done.6
  35.5 0.0 collective-permute-done.3.refs_8_
  35.5 0.1 collective-permute-start.14
  35.6 1.8 %collective-permute-start.11 = (f32[4,512]{1,0:T(4,128)S(1)}, f32[4,512]{1,0:T(4,128)S(1)}, u32[]{:S(2)}, u32[]{:S(2)}) collective-permute-start(f32[4,512]{1,0:T(4,128)S(1)} %pad_maximum_fusion.1.refs_0_), channel_id=1, source_target_pairs={{0,6},{2,4},{4,2},{6,0},{8,14},{10,12},{12,10},{14,8},{16,22},{18,... | collective-permute-start | bytes 24584 | tf_op jit(solution)/shard_map/ppermute | solution.py:32
  37.4 1.2 %collective-permute-start.10 = (f32[4,512]{1,0:T(4,128)S(1)}, f32[4,512]{1,0:T(4,128)S(1)}, u32[]{:S(2)}, u32[]{:S(2)}) collective-permute-start(f32[4,512]{1,0:T(4,128)S(1)} %pad_maximum_fusion.1.refs_0_), channel_id=1, source_target_pairs={{0,4},{2,6},{4,0},{6,2},{8,12},{10,14},{12,8},{14,10},{16,20},{18,... | collective-permute-start | bytes 24584 | tf_op jit(solution)/shard_map/ppermute | solution.py:32
  38.6 0.0 collective-permute-done.13.refs_7_
  38.6 0.5 %collective-permute-start.9 = (f32[4,512]{1,0:T(4,128)S(1)}, f32[4,512]{1,0:T(4,128)S(1)}, u32[]{:S(2)}, u32[]{:S(2)}) collective-permute-start(f32[4,512]{1,0:T(4,128)S(1)} %pad_maximum_fusion.1.refs_0_), channel_id=1, source_target_pairs={{0,2},{2,0},{4,6},{6,4},{8,10},{10,8},{12,14},{14,12},{16,18},{18,... | collective-permute-start | bytes 24584 | tf_op jit(solution)/shard_map/ppermute | solution.py:32
  39.1 1.1 %collective-permute-done.11.refs_3_ = f32[4,512]{1,0:T(4,128)S(1)} collective-permute-done((f32[4,512]{1,0:T(4,128)S(1)}, f32[4,512]{1,0:T(4,128)S(1)}, u32[]{:S(2)}, u32[]{:S(2)}) %collective-permute-start.11) | collective-permute-done | bytes 8224 | tf_op jit(solution)/shard_map/ppermute | solution.py:32
  40.2 0.8 %collective-permute-done.10.refs_2_ = f32[4,512]{1,0:T(4,128)S(1)} collective-permute-done((f32[4,512]{1,0:T(4,128)S(1)}, f32[4,512]{1,0:T(4,128)S(1)}, u32[]{:S(2)}, u32[]{:S(2)}) %collective-permute-start.10) | collective-permute-done | bytes 8224 | tf_op jit(solution)/shard_map/ppermute | solution.py:32
  41.0 1.2 %collective-permute-done.9.refs_1_ = f32[4,512]{1,0:T(4,128)S(1)} collective-permute-done((f32[4,512]{1,0:T(4,128)S(1)}, f32[4,512]{1,0:T(4,128)S(1)}, u32[]{:S(2)}, u32[]{:S(2)}) %collective-permute-start.9) | collective-permute-done | bytes 8224 | tf_op jit(solution)/shard_map/ppermute | solution.py:32
  42.2 0.0 collective-permute-done.12.refs_6_
  42.2 0.0 collective-permute-done.14.refs_9_
  42.2 0.0 copy-done
  42.2 6.8 %shard_map.86 = f32[4,4,96,256]{3,2,1,0:T(8,128)} custom-call(f32[40,256]{1,0:T(8,128)S(1)} %get-tuple-element.28.aux, f32[4,512]{1,0:T(4,128)S(1)} %pad_maximum_fusion.1.refs_0_, f32[4,512]{1,0:T(4,128)S(1)} %collective-permute-done.9.refs_1_, f32[4,512]{1,0:T(4,128)S(1)} %collective-permute-done.10.refs_2_, f32[4,512]{1,0:T(4,128)S(1)} %collective-permute-done.11.refs_3_, ...), custom_call_target="tpu_custom_call" | custom-call | flops 5435817984 | bytes 1048576 | tf_op jit(solution)/shard_map/pallas_call | solution.py:432
  (7 shorter events, 0.1 us)
Async XLA Ops:
  2.0 8.0 %collective-permute-start.2 = (bf16[4,1,96,256]{3,2,1,0:T(8,128)(2,1)S(1)}, bf16[4,1,96,256]{3,2,1,0:T(8,128)(2,1)S(1)}, u32[]{:S(2)}, u32[]{:S(2)}) collective-permute-start(bf16[4,1,96,256]{3,2,1,0:T(8,128)(2,1)S(1)} %get-tuple-element.31), channel_id=1, source_target_pairs={{0,1},{1,0},{2,3},{3,2},{4,5},{5,4},{6,7},{7,6},{8,9},{9,8},{10,11... | collective-permute-start | bytes 589832 | tf_op jit(solution)/shard_map/ppermute | solution.py:32
  2.5 12.4 %collective-permute-start = (bf16[1,4,96,256]{3,2,1,0:T(8,128)(2,1)S(1)}, bf16[1,4,96,256]{3,2,1,0:T(8,128)(2,1)S(1)}, u32[]{:S(2)}, u32[]{:S(2)}) collective-permute-start(bf16[1,4,96,256]{3,2,1,0:T(8,128)(2,1)S(1)} %get-tuple-element.46), channel_id=1, source_target_pairs={{0,2},{2,4},{4,6},{6,8},{8,10},{10,12},{12,14},{14,16},{16,18},{18... | collective-permute-start | bytes 589832 | tf_op jit(solution)/shard_map/ppermute | solution.py:37
  5.1 12.3 %all-to-all-start = ((f32[32,1,512]{2,1,0:T(1,128)}), f32[32,1,512]{2,1,0:T(1,128)S(1)}, u32[]{:S(2)}, u32[]{:S(2)}) async-start(f32[32,1,512]{2,1,0:T(1,128)} %get-tuple-element.29), calls=%async_computation | async-start | bytes 131072 | tf_op jit(solution)/shard_map/all_to_all | solution.py:41
  10.1 14.4 %collective-permute-start.4 = (bf16[1,5,96,256]{3,2,1,0:T(8,128)(2,1)S(1)}, bf16[1,5,96,256]{3,2,1,0:T(8,128)(2,1)S(1)}, u32[]{:S(2)}, u32[]{:S(2)}) collective-permute-start(bf16[1,5,96,256]{3,2,1,0:T(8,128)(2,1)S(1)} %pad_maximum_fusion), channel_id=1, source_target_pairs={{0,2},{2,4},{4,6},{6,8},{8,10},{10,12},{12,14},{14,16},{16,18},{18... | collective-permute-start | bytes 737288 | tf_op jit(solution)/shard_map/ppermute | solution.py:86
  14.9 1.4 %collective-permute-start.1 = (bf16[1,1,96,256]{3,2,1,0:T(8,128)(2,1)S(1)}, bf16[1,1,96,256]{3,2,1,0:T(8,128)(2,1)S(1)}, u32[]{:S(2)}, u32[]{:S(2)}) collective-permute-start(bf16[1,1,96,256]{3,2,1,0:T(8,128)(2,1)S(1)} %constant_dynamic-slice_fusion.1), channel_id=1, source_target_pairs={{0,1},{1,0},{2,3},{3,2},{4,5},{5,4},{6,7},{7,6},{8,9},{9,8},{10,11... | collective-permute-start | bytes 147464 | tf_op jit(solution)/shard_map/ppermute | solution.py:32
  22.1 13.4 %collective-permute-start.3 = (bf16[2,4,96,256]{3,2,1,0:T(8,128)(2,1)S(1)}, bf16[2,4,96,256]{3,2,1,0:T(8,128)(2,1)S(1)}, u32[]{:S(2)}, u32[]{:S(2)}) collective-permute-start(bf16[2,4,96,256]{3,2,1,0:T(8,128)(2,1)S(1)} %get-tuple-element.33.refs_5_), channel_id=1, source_target_pairs={{0,2},{2,4},{4,6},{6,8},{8,10},{10,12},{12,14},{14,16},{16,18},{18... | collective-permute-start | bytes 1179656 | tf_op jit(solution)/shard_map/ppermute | solution.py:86
  24.5 17.8 %copy-start = (bf16[3,3,3,256,256]{4,3,2,1,0:T(8,128)(2,1)S(1)}, bf16[3,3,3,256,256]{4,3,2,1,0:T(8,128)(2,1)}, u32[]{:S(2)}) copy-start(bf16[3,3,3,256,256]{4,3,2,1,0:T(8,128)(2,1)} %refs_10_.1) | copy-start | bytes 10616836
  27.5 1.2 %collective-permute-start.5 = (f32[1,512]{1,0:T(1,128)S(1)}, f32[1,512]{1,0:T(1,128)S(1)}, u32[]{:S(2)}, u32[]{:S(2)}) collective-permute-start(f32[1,512]{1,0:T(1,128)S(1)} %get-tuple-element.39), channel_id=1, source_target_pairs={{0,1},{1,0},{2,3},{3,2},{4,5},{5,4},{6,7},{7,6},{8,9},{9,8},{10,11... | collective-permute-start | bytes 6152 | tf_op jit(solution)/shard_map/ppermute | solution.py:32
  28.7 5.4 %collective-permute-start.8 = (f32[1,512]{1,0:T(1,128)S(1)}, f32[1,512]{1,0:T(1,128)S(1)}, u32[]{:S(2)}, u32[]{:S(2)}) collective-permute-start(f32[1,512]{1,0:T(1,128)S(1)} %add.8), channel_id=1, source_target_pairs={{0,24},{2,26},{4,28},{6,30},{8,16},{10,18},{12,20},{14,22},{16,8},... | collective-permute-start | bytes 6152 | tf_op jit(solution)/shard_map/ppermute | solution.py:32
  30.9 4.5 %collective-permute-start.7 = (f32[1,512]{1,0:T(1,128)S(1)}, f32[1,512]{1,0:T(1,128)S(1)}, u32[]{:S(2)}, u32[]{:S(2)}) collective-permute-start(f32[1,512]{1,0:T(1,128)S(1)} %add.8), channel_id=1, source_target_pairs={{0,16},{2,18},{4,20},{6,22},{8,24},{10,26},{12,28},{14,30},{16,0},... | collective-permute-start | bytes 6152 | tf_op jit(solution)/shard_map/ppermute | solution.py:32
  30.9 4.5 %collective-permute-start.6 = (f32[1,512]{1,0:T(1,128)S(1)}, f32[1,512]{1,0:T(1,128)S(1)}, u32[]{:S(2)}, u32[]{:S(2)}) collective-permute-start(f32[1,512]{1,0:T(1,128)S(1)} %add.8), channel_id=1, source_target_pairs={{0,8},{2,10},{4,12},{6,14},{8,0},{10,2},{12,4},{14,6},{16,24},{18,... | collective-permute-start | bytes 6152 | tf_op jit(solution)/shard_map/ppermute | solution.py:32
  33.1 5.5 %collective-permute-start.13 = (bf16[2,1,96,256]{3,2,1,0:T(8,128)(2,1)S(1)}, bf16[2,1,96,256]{3,2,1,0:T(8,128)(2,1)S(1)}, u32[]{:S(2)}, u32[]{:S(2)}) collective-permute-start(bf16[2,1,96,256]{3,2,1,0:T(8,128)(2,1)S(1)} %get-tuple-element.43), channel_id=1, source_target_pairs={{0,1},{1,0},{2,3},{3,2},{4,5},{5,4},{6,7},{7,6},{8,9},{9,8},{10,11... | collective-permute-start | bytes 294920 | tf_op jit(solution)/shard_map/ppermute | solution.py:32
  34.1 8.1 %collective-permute-start.12 = (bf16[2,1,96,256]{3,2,1,0:T(8,128)(2,1)S(1)}, bf16[2,1,96,256]{3,2,1,0:T(8,128)(2,1)S(1)}, u32[]{:S(2)}, u32[]{:S(2)}) collective-permute-start(bf16[2,1,96,256]{3,2,1,0:T(8,128)(2,1)S(1)} %get-tuple-element.42), channel_id=1, source_target_pairs={{0,1},{1,0},{2,3},{3,2},{4,5},{5,4},{6,7},{7,6},{8,9},{9,8},{10,11... | collective-permute-start | bytes 294920 | tf_op jit(solution)/shard_map/ppermute | solution.py:32
  35.5 6.7 %collective-permute-start.14 = (bf16[2,1,96,256]{3,2,1,0:T(8,128)(2,1)S(1)}, bf16[2,1,96,256]{3,2,1,0:T(8,128)(2,1)S(1)}, u32[]{:S(2)}, u32[]{:S(2)}) collective-permute-start(bf16[2,1,96,256]{3,2,1,0:T(8,128)(2,1)S(1)} %constant_dynamic-slice_fusion), channel_id=1, source_target_pairs={{0,1},{1,0},{2,3},{3,2},{4,5},{5,4},{6,7},{7,6},{8,9},{9,8},{10,11... | collective-permute-start | bytes 294920 | tf_op jit(solution)/shard_map/ppermute | solution.py:32
  35.6 4.6 %collective-permute-start.11 = (f32[4,512]{1,0:T(4,128)S(1)}, f32[4,512]{1,0:T(4,128)S(1)}, u32[]{:S(2)}, u32[]{:S(2)}) collective-permute-start(f32[4,512]{1,0:T(4,128)S(1)} %pad_maximum_fusion.1.refs_0_), channel_id=1, source_target_pairs={{0,6},{2,4},{4,2},{6,0},{8,14},{10,12},{12,10},{14,8},{16,22},{18,... | collective-permute-start | bytes 24584 | tf_op jit(solution)/shard_map/ppermute | solution.py:32
  37.4 3.7 %collective-permute-start.10 = (f32[4,512]{1,0:T(4,128)S(1)}, f32[4,512]{1,0:T(4,128)S(1)}, u32[]{:S(2)}, u32[]{:S(2)}) collective-permute-start(f32[4,512]{1,0:T(4,128)S(1)} %pad_maximum_fusion.1.refs_0_), channel_id=1, source_target_pairs={{0,4},{2,6},{4,0},{6,2},{8,12},{10,14},{12,8},{14,10},{16,20},{18,... | collective-permute-start | bytes 24584 | tf_op jit(solution)/shard_map/ppermute | solution.py:32
  38.6 3.7 %collective-permute-start.9 = (f32[4,512]{1,0:T(4,128)S(1)}, f32[4,512]{1,0:T(4,128)S(1)}, u32[]{:S(2)}, u32[]{:S(2)}) collective-permute-start(f32[4,512]{1,0:T(4,128)S(1)} %pad_maximum_fusion.1.refs_0_), channel_id=1, source_target_pairs={{0,2},{2,0},{4,6},{6,4},{8,10},{10,8},{12,14},{14,12},{16,18},{18,... | collective-permute-start | bytes 24584 | tf_op jit(solution)/shard_map/ppermute | solution.py:32

commit v22 on v20

--- a/solution.py
+++ b/solution.py
@@ -416,11 +416,11 @@
     for frame in range(2, 5):
         fill(frame)
     for frame in list(range(2, n_frames)) + [0, 1]:
-        if frame == 0:
+        if 2 <= frame < n_frames - 1:
+            fill(frame + 3)
+        elif frame == n_frames - 1:
             fill(0)
             fill(1)
-        elif 2 < frame:
-            fill(frame + 2)
         for row, value in conv_rows([(act, frame + i) for i in range(3)], (taps.at[:1], taps.at[1:])):
             out[frame, row] = feats[frame, row].astype(F32) + value
         stores[frame].start()
@@ -472,6 +472,7 @@
     )
     before = shifted(hidden_late[late - 2 :], "tm", 1)
     sides_late = row_halo(edges)
+    affine, *sides_late = lax.optimization_barrier((affine, *sides_late))
     hidden_early, edges, stats = call(
         functools.partial(early_kernel, n_sides),
         [shaped((2, n_rows, cols, width)), shaped(edge_shape(feats, 2)), shaped((1, 2 * width), F32)],

time: 49.3 us -> 49.8 us (1.010)
  waiting for transfers between devices: 10.8 us -> 12.9 us
  starting transfers between devices: 20.3 us -> 18.6 us
    ppermute x1, starting transfers between devices: 3.69 us -> 1.3 us  [chained(): lax.ppermute(value, 'tm', [(i, i + 1) for i in range(lax.axis_size('tm')...]
    ppermute x12, waiting for transfers between devices: 5.67 us -> 7.23 us  [traded(): lax.ppermute(value, axis, [(i, i ^ mask) for i in range(lax.axis_size(axi...]
    ppermute x2, waiting for transfers between devices: 4.02 us -> 5.04 us  [shifted(): lax.ppermute(value, axis, [(i, (i + step) % peers) for i in range(peers)])]
where the time goes in v22:
time: 49.8 us; the launch traced here: 49.5 us
  starting transfers between devices  18.6 us (37%)
  Pallas kernels  17.8 us (36%)
  waiting for transfers between devices  12.9 us (26%)
    pallas_call x3, Pallas kernels, call(): pl.pallas_call(kernel, out_shape=outs, in_specs=[ANYWHERE if k in (aliase...  14.4 us
    ppermute x12, starting transfers between devices, traded(): lax.ppermute(value, axis, [(i, i ^ mask) for i in range(lax.axis_size(axi...  8.82 us
    ppermute x12, waiting for transfers between devices, traded(): lax.ppermute(value, axis, [(i, i ^ mask) for i in range(lax.axis_size(axi...  7.23 us
    ppermute x2, waiting for transfers between devices, shifted(): lax.ppermute(value, axis, [(i, (i + step) % peers) for i in range(peers)])  5.04 us
    all_to_all x1, starting transfers between devices, stats_table(): return lax.all_to_all(copies, ('tm', 'space'), 0, 0, tiled=True)  5.03 us
    ppermute x2, starting transfers between devices, shifted(): lax.ppermute(value, axis, [(i, (i + step) % peers) for i in range(peers)])  3.42 us
    pallas_call x1, Pallas kernels, entry_call(): pl.pallas_call(entry_kernel, out_shape=outs, in_specs=[ANYWHERE], out_spe...  1.95 us
    pallas_call x1, Pallas kernels, setup_call(): pl.pallas_call(functools.partial(setup_kernel, slabs, per_slab), out_shap...  1.39 us
  transfers between devices with their start and end apart: 16, of which 9 were waited for; matrix products, arithmetic and copies ran while one was open for 0% of the time, Pallas kernels for 18%

profile of v22, /device:TPU:0, one launch (start us, length us, event | category | flops | bytes accessed | tf_op | source)
XLA Modules:
  0.0 49.5 jit_solution(8570436447742614317)
XLA Ops:
  0.0 1.9 %shard_map.82 = (bf16[4,4,96,256]{3,2,1,0:T(8,128)(2,1)S(1)}, bf16[2,4,96,256]{3,2,1,0:T(8,128)(2,1)S(1)}, bf16[4,1,96,256]{3,2,1,0:T(8,128)(2,1)S(1)}, f32[32,1,512]{2,1,0:T(1,128)}, f32[8,128]{1,0:T(8,128)S(1)}) custom-call(bf16[4,4,96,256]{3,2,1,0:T(8,128)(2,1)} %feats_hbm.1), custom_call_target="tpu_custom_call" | custom-call | flops 1572864 | bytes 1572864 | tf_op jit(solution)/shard_map/pallas_call | solution.py:181
  2.0 3.0 %collective-permute-start = (bf16[1,4,96,256]{3,2,1,0:T(8,128)(2,1)S(1)}, bf16[1,4,96,256]{3,2,1,0:T(8,128)(2,1)S(1)}, u32[]{:S(2)}, u32[]{:S(2)}) collective-permute-start(bf16[1,4,96,256]{3,2,1,0:T(8,128)(2,1)S(1)} %get-tuple-element.50), channel_id=1, source_target_pairs={{0,2},{2,4},{4,6},{6,8},{8,10},{10,12},{12,14},{14,16},{16,18},{18... | collective-permute-start | bytes 589832 | tf_op jit(solution)/shard_map/ppermute | solution.py:37
  5.0 0.0 collective-permute-start.2
  5.0 5.0 %all-to-all-start = ((f32[32,1,512]{2,1,0:T(1,128)}), f32[32,1,512]{2,1,0:T(1,128)S(1)}, u32[]{:S(2)}, u32[]{:S(2)}) async-start(f32[32,1,512]{2,1,0:T(1,128)} %get-tuple-element.31), calls=%async_computation | async-start | bytes 131072 | tf_op jit(solution)/shard_map/all_to_all | solution.py:41
  10.0 4.0 %collective-permute-done.first = bf16[1,4,96,256]{3,2,1,0:T(8,128)(2,1)S(1)} collective-permute-done((bf16[1,4,96,256]{3,2,1,0:T(8,128)(2,1)S(1)}, bf16[1,4,96,256]{3,2,1,0:T(8,128)(2,1)S(1)}, u32[]{:S(2)}, u32[]{:S(2)}) %collective-permute-start) | collective-permute-done | bytes 196640 | tf_op jit(solution)/shard_map/ppermute | solution.py:37
  14.0 0.0 collective-permute-start.1
  14.0 0.0 collective-permute-done.2.refs_0_
  14.1 1.3 %collective-permute-start.4 = (bf16[1,5,96,256]{3,2,1,0:T(8,128)(2,1)S(1)}, bf16[1,5,96,256]{3,2,1,0:T(8,128)(2,1)S(1)}, u32[]{:S(2)}, u32[]{:S(2)}) collective-permute-start(bf16[1,5,96,256]{3,2,1,0:T(8,128)(2,1)S(1)} %pad_maximum_fusion), channel_id=1, source_target_pairs={{0,2},{2,4},{4,6},{6,8},{8,10},{10,12},{12,14},{14,16},{16,18},{18... | collective-permute-start | bytes 737288 | tf_op jit(solution)/shard_map/ppermute | solution.py:86
  15.4 1.4 %shard_map.83 = (bf16[1,3,3,256,256]{4,3,2,1,0:T(8,128)(2,1)S(1)}, f32[40,256]{1,0:T(8,128)S(1)}) custom-call(bf16[3,3,3,256,256]{4,3,2,1,0:T(8,128)(2,1)} %refs_2_.1, s32[16]{0:T(128)} %clips_hbm.1, f32[1,256]{1,0:T(1,128)} %bitcast.4, f32[1,256]{1,0:T(1,128)} %bitcast.5, f32[1,256]{1,0:T(1,128)} %bitcast.6, f32[1,256]{1,0:T(1,128)} %bitcast.7, ...), custom_call_target="tpu_custom_call" | custom-call | flops 1073741824 | bytes 65536 | tf_op jit(solution)/shard_map/pallas_call | solution.py:225
  16.8 0.0 collective-permute-done.1.refs_0_
  16.8 0.7 %all-to-all-done.table = f32[32,1,512]{2,1,0:T(1,128)S(1)} async-done(((f32[32,1,512]{2,1,0:T(1,128)}), f32[32,1,512]{2,1,0:T(1,128)S(1)}, u32[]{:S(2)}, u32[]{:S(2)}) %all-to-all-start) | async-done | bytes 65568 | tf_op jit(solution)/shard_map/all_to_all | solution.py:41
  17.4 4.7 %shard_map.84 = (bf16[2,6,96,256]{3,2,1,0:T(8,128)(2,1)S(1)}, f32[2,256]{1,0:T(2,128)S(1)}, bf16[2,3,3,256,256]{4,3,2,1,0:T(8,128)(2,1)S(1)}, bf16[2,4,96,256]{3...) custom-call(f32[40,256]{1,0:T(8,128)S(1)} %get-tuple-element.30.aux, ...), custom_call_target="tpu_custom_call" | custom-call | flops 1019215872 | bytes 1048576 | tf_op jit(solution)/shard_map/pallas_call | solution.py:432
  22.1 0.2 collective-permute-start.5
  22.3 0.4 collective-permute-start.3
  22.7 0.8 %collective-permute-done.5.refs_7_ = bf16[2,1,96,256]{3,2,1,0:T(8,128)(2,1)S(1)} collective-permute-done((bf16[2,1,96,256]{3,2,1,0:T(8,128)(2,1)S(1)}, bf16[2,1,96,256]{3,2,1,0:T(8,128)(2,1)S(1)}, u32[]{:S(2)}, u32[]{:S(2)}) %collective-permute-start.5) | collective-permute-done | bytes 98336 | tf_op jit(solution)/shard_map/ppermute | solution.py:32
  23.5 0.0 collective-permute-done.4.second
  23.5 0.0 copy-start
  23.5 3.0 %shard_map.85 = (bf16[2,4,96,256]{3,2,1,0:T(8,128)(2,1)S(1)}, bf16[2,1,96,256]{3,2,1,0:T(8,128)(2,1)S(1)}, f32[1,512]{1,0:T(1,128)S(1)}) custom-call(f32[40,256]{1,0:T(8,128)S(1)} %get-tuple-element.30.aux, bf16[1,4,96,256]{3,2,1,0:T(8,128)(2,1)S(1)} %collective-permute-done.first, bf16[1,5,96,256]{3,2,1,0:T(8,128)(2,1)S(1)} %collective-permute-done.4.second, ...), custom_call_target="tpu_custom_call" | custom-call | flops 2717908992 | bytes 1048576 | tf_op jit(solution)/shard_map/pallas_call | solution.py:432
  26.5 0.2 collective-permute-start.6
  26.7 1.0 %collective-permute-done.6 = f32[1,512]{1,0:T(1,128)S(1)} collective-permute-done((f32[1,512]{1,0:T(1,128)S(1)}, f32[1,512]{1,0:T(1,128)S(1)}, u32[]{:S(2)}, u32[]{:S(2)}) %collective-permute-start.6) | collective-permute-done | bytes 2080 | tf_op jit(solution)/shard_map/ppermute | solution.py:32
  27.7 4.1 %collective-permute-start.9 = (f32[1,512]{1,0:T(1,128)S(1)}, f32[1,512]{1,0:T(1,128)S(1)}, u32[]{:S(2)}, u32[]{:S(2)}) collective-permute-start(f32[1,512]{1,0:T(1,128)S(1)} %add.8), channel_id=1, source_target_pairs={{0,24},{2,26},{4,28},{6,30},{8,16},{10,18},{12,20},{14,22},{16,8},... | collective-permute-start | bytes 6152 | tf_op jit(solution)/shard_map/ppermute | solution.py:32
  31.9 0.0 collective-permute-start.8
  31.9 0.6 %collective-permute-start.7 = (f32[1,512]{1,0:T(1,128)S(1)}, f32[1,512]{1,0:T(1,128)S(1)}, u32[]{:S(2)}, u32[]{:S(2)}) collective-permute-start(f32[1,512]{1,0:T(1,128)S(1)} %add.8), channel_id=1, source_target_pairs={{0,8},{2,10},{4,12},{6,14},{8,0},{10,2},{12,4},{14,6},{16,24},{18,... | collective-permute-start | bytes 6152 | tf_op jit(solution)/shard_map/ppermute | solution.py:32
  32.5 0.0 collective-permute-start.13
  32.5 0.9 %collective-permute-done.9 = f32[1,512]{1,0:T(1,128)S(1)} collective-permute-done((f32[1,512]{1,0:T(1,128)S(1)}, f32[1,512]{1,0:T(1,128)S(1)}, u32[]{:S(2)}, u32[]{:S(2)}) %collective-permute-start.9) | collective-permute-done | bytes 2080 | tf_op jit(solution)/shard_map/ppermute | solution.py:32
  33.4 2.9 %collective-permute-done.8 = f32[1,512]{1,0:T(1,128)S(1)} collective-permute-done((f32[1,512]{1,0:T(1,128)S(1)}, f32[1,512]{1,0:T(1,128)S(1)}, u32[]{:S(2)}, u32[]{:S(2)}) %collective-permute-start.8) | collective-permute-done | bytes 2080 | tf_op jit(solution)/shard_map/ppermute | solution.py:32
  36.4 0.0 collective-permute-done.7
  36.4 1.1 %collective-permute-done.3.refs_8_ = bf16[2,4,96,256]{3,2,1,0:T(8,128)(2,1)S(1)} collective-permute-done((bf16[2,4,96,256]{3,2,1,0:T(8,128)(2,1)S(1)}, bf16[2,4,96,256]{3,2,1,0:T(8,128)(2,1)S(1)}, u32[]{:S(2)}, u32[]{:S(2)}) %collective-permute-start.3) | collective-permute-done | bytes 393248 | tf_op jit(solution)/shard_map/ppermute | solution.py:37
  37.5 0.1 collective-permute-start.14
  37.6 0.7 %collective-permute-start.12 = (f32[4,512]{1,0:T(4,128)S(1)}, f32[4,512]{1,0:T(4,128)S(1)}, u32[]{:S(2)}, u32[]{:S(2)}) collective-permute-start(f32[4,512]{1,0:T(4,128)S(1)} %pad_maximum_fusion.1.refs_0_), channel_id=1, source_target_pairs={{0,6},{2,4},{4,2},{6,0},{8,14},{10,12},{12,10},{14,8},{16,22},{18,... | collective-permute-start | bytes 24584 | tf_op jit(solution)/shard_map/ppermute | solution.py:32
  38.3 0.0 collective-permute-start.11
  38.3 2.9 %collective-permute-start.10 = (f32[4,512]{1,0:T(4,128)S(1)}, f32[4,512]{1,0:T(4,128)S(1)}, u32[]{:S(2)}, u32[]{:S(2)}) collective-permute-start(f32[4,512]{1,0:T(4,128)S(1)} %pad_maximum_fusion.1.refs_0_), channel_id=1, source_target_pairs={{0,2},{2,0},{4,6},{6,4},{8,10},{10,8},{12,14},{14,12},{16,18},{18,... | collective-permute-start | bytes 24584 | tf_op jit(solution)/shard_map/ppermute | solution.py:32
  41.1 1.1 %collective-permute-done.12.refs_3_ = f32[4,512]{1,0:T(4,128)S(1)} collective-permute-done((f32[4,512]{1,0:T(4,128)S(1)}, f32[4,512]{1,0:T(4,128)S(1)}, u32[]{:S(2)}, u32[]{:S(2)}) %collective-permute-start.12) | collective-permute-done | bytes 8224 | tf_op jit(solution)/shard_map/ppermute | solution.py:32
  42.2 0.0 collective-permute-done.11.refs_2_
  42.2 0.6 %collective-permute-done.10.refs_1_ = f32[4,512]{1,0:T(4,128)S(1)} collective-permute-done((f32[4,512]{1,0:T(4,128)S(1)}, f32[4,512]{1,0:T(4,128)S(1)}, u32[]{:S(2)}, u32[]{:S(2)}) %collective-permute-start.10) | collective-permute-done | bytes 8224 | tf_op jit(solution)/shard_map/ppermute | solution.py:32
  42.7 0.0 collective-permute-done.13.refs_6_
  42.7 0.0 collective-permute-done.14.refs_9_
  42.7 0.0 copy-done
  42.8 6.8 %shard_map.86 = f32[4,4,96,256]{3,2,1,0:T(8,128)} custom-call(f32[40,256]{1,0:T(8,128)S(1)} %get-tuple-element.30.aux, f32[4,512]{1,0:T(4,128)S(1)} %pad_maximum_fusion.1.refs_0_, f32[4,512]{1,0:T(4,128)S(1)} %collective-permute-done.10.refs_1_, f32[4,512]{1,0:T(4,128)S(1)} %collective-permute-done.11.refs_2_, f32[4,512]{1,0:T(4,128)S(1)} %collective-permute-done.12.refs_3_, ...), custom_call_target="tpu_custom_call" | custom-call | flops 5435817984 | bytes 1048576 | tf_op jit(solution)/shard_map/pallas_call | solution.py:432
  (7 shorter events, 0.1 us)
Async XLA Ops:
  2.0 12.0 %collective-permute-start = (bf16[1,4,96,256]{3,2,1,0:T(8,128)(2,1)S(1)}, bf16[1,4,96,256]{3,2,1,0:T(8,128)(2,1)S(1)}, u32[]{:S(2)}, u32[]{:S(2)}) collective-permute-start(bf16[1,4,96,256]{3,2,1,0:T(8,128)(2,1)S(1)} %get-tuple-element.50), channel_id=1, source_target_pairs={{0,2},{2,4},{4,6},{6,8},{8,10},{10,12},{12,14},{14,16},{16,18},{18... | collective-permute-start | bytes 589832 | tf_op jit(solution)/shard_map/ppermute | solution.py:37
  5.0 9.0 %collective-permute-start.2 = (bf16[4,1,96,256]{3,2,1,0:T(8,128)(2,1)S(1)}, bf16[4,1,96,256]{3,2,1,0:T(8,128)(2,1)S(1)}, u32[]{:S(2)}, u32[]{:S(2)}) collective-permute-start(bf16[4,1,96,256]{3,2,1,0:T(8,128)(2,1)S(1)} %get-tuple-element.33), channel_id=1, source_target_pairs={{0,1},{1,0},{2,3},{3,2},{4,5},{5,4},{6,7},{7,6},{8,9},{9,8},{10,11... | collective-permute-start | bytes 589832 | tf_op jit(solution)/shard_map/ppermute | solution.py:32
  5.0 12.5 %all-to-all-start = ((f32[32,1,512]{2,1,0:T(1,128)}), f32[32,1,512]{2,1,0:T(1,128)S(1)}, u32[]{:S(2)}, u32[]{:S(2)}) async-start(f32[32,1,512]{2,1,0:T(1,128)} %get-tuple-element.31), calls=%async_computation | async-start | bytes 131072 | tf_op jit(solution)/shard_map/all_to_all | solution.py:41
  14.0 2.8 %collective-permute-start.1 = (bf16[1,1,96,256]{3,2,1,0:T(8,128)(2,1)S(1)}, bf16[1,1,96,256]{3,2,1,0:T(8,128)(2,1)S(1)}, u32[]{:S(2)}, u32[]{:S(2)}) collective-permute-start(bf16[1,1,96,256]{3,2,1,0:T(8,128)(2,1)S(1)} %constant_dynamic-slice_fusion.1), channel_id=1, source_target_pairs={{0,1},{1,0},{2,3},{3,2},{4,5},{5,4},{6,7},{7,6},{8,9},{9,8},{10,11... | collective-permute-start | bytes 147464 | tf_op jit(solution)/shard_map/ppermute | solution.py:32
  14.1 9.4 %collective-permute-start.4 = (bf16[1,5,96,256]{3,2,1,0:T(8,128)(2,1)S(1)}, bf16[1,5,96,256]{3,2,1,0:T(8,128)(2,1)S(1)}, u32[]{:S(2)}, u32[]{:S(2)}) collective-permute-start(bf16[1,5,96,256]{3,2,1,0:T(8,128)(2,1)S(1)} %pad_maximum_fusion), channel_id=1, source_target_pairs={{0,2},{2,4},{4,6},{6,8},{8,10},{10,12},{12,14},{14,16},{16,18},{18... | collective-permute-start | bytes 737288 | tf_op jit(solution)/shard_map/ppermute | solution.py:86
  22.1 1.4 %collective-permute-start.5 = (bf16[2,1,96,256]{3,2,1,0:T(8,128)(2,1)S(1)}, bf16[2,1,96,256]{3,2,1,0:T(8,128)(2,1)S(1)}, u32[]{:S(2)}, u32[]{:S(2)}) collective-permute-start(bf16[2,1,96,256]{3,2,1,0:T(8,128)(2,1)S(1)} %get-tuple-element.39), channel_id=1, source_target_pairs={{0,1},{1,0},{2,3},{3,2},{4,5},{5,4},{6,7},{7,6},{8,9},{9,8},{10,11... | collective-permute-start | bytes 294920 | tf_op jit(solution)/shard_map/ppermute | solution.py:32
  22.3 15.2 %collective-permute-start.3 = (bf16[2,4,96,256]{3,2,1,0:T(8,128)(2,1)S(1)}, bf16[2,4,96,256]{3,2,1,0:T(8,128)(2,1)S(1)}, u32[]{:S(2)}, u32[]{:S(2)}) collective-permute-start(bf16[2,4,96,256]{3,2,1,0:T(8,128)(2,1)S(1)} %get-tuple-element.35.refs_5_), channel_id=1, source_target_pairs={{0,2},{2,4},{4,6},{6,8},{8,10},{10,12},{12,14},{14,16},{16,18},{18... | collective-permute-start | bytes 1179656 | tf_op jit(solution)/shard_map/ppermute | solution.py:37
  23.5 19.3 %copy-start = (bf16[3,3,3,256,256]{4,3,2,1,0:T(8,128)(2,1)S(1)}, bf16[3,3,3,256,256]{4,3,2,1,0:T(8,128)(2,1)}, u32[]{:S(2)}) copy-start(bf16[3,3,3,256,256]{4,3,2,1,0:T(8,128)(2,1)} %refs_10_.1) | copy-start | bytes 10616836
  26.5 1.2 %collective-permute-start.6 = (f32[1,512]{1,0:T(1,128)S(1)}, f32[1,512]{1,0:T(1,128)S(1)}, u32[]{:S(2)}, u32[]{:S(2)}) collective-permute-start(f32[1,512]{1,0:T(1,128)S(1)} %get-tuple-element.43), channel_id=1, source_target_pairs={{0,1},{1,0},{2,3},{3,2},{4,5},{5,4},{6,7},{7,6},{8,9},{9,8},{10,11... | collective-permute-start | bytes 6152 | tf_op jit(solution)/shard_map/ppermute | solution.py:32
  27.7 5.7 %collective-permute-start.9 = (f32[1,512]{1,0:T(1,128)S(1)}, f32[1,512]{1,0:T(1,128)S(1)}, u32[]{:S(2)}, u32[]{:S(2)}) collective-permute-start(f32[1,512]{1,0:T(1,128)S(1)} %add.8), channel_id=1, source_target_pairs={{0,24},{2,26},{4,28},{6,30},{8,16},{10,18},{12,20},{14,22},{16,8},... | collective-permute-start | bytes 6152 | tf_op jit(solution)/shard_map/ppermute | solution.py:32
  31.9 4.5 %collective-permute-start.8 = (f32[1,512]{1,0:T(1,128)S(1)}, f32[1,512]{1,0:T(1,128)S(1)}, u32[]{:S(2)}, u32[]{:S(2)}) collective-permute-start(f32[1,512]{1,0:T(1,128)S(1)} %add.8), channel_id=1, source_target_pairs={{0,16},{2,18},{4,20},{6,22},{8,24},{10,26},{12,28},{14,30},{16,0},... | collective-permute-start | bytes 6152 | tf_op jit(solution)/shard_map/ppermute | solution.py:32
  31.9 4.5 %collective-permute-start.7 = (f32[1,512]{1,0:T(1,128)S(1)}, f32[1,512]{1,0:T(1,128)S(1)}, u32[]{:S(2)}, u32[]{:S(2)}) collective-permute-start(f32[1,512]{1,0:T(1,128)S(1)} %add.8), channel_id=1, source_target_pairs={{0,8},{2,10},{4,12},{6,14},{8,0},{10,2},{12,4},{14,6},{16,24},{18,... | collective-permute-start | bytes 6152 | tf_op jit(solution)/shard_map/ppermute | solution.py:32
  32.5 10.2 %collective-permute-start.13 = (bf16[2,1,96,256]{3,2,1,0:T(8,128)(2,1)S(1)}, bf16[2,1,96,256]{3,2,1,0:T(8,128)(2,1)S(1)}, u32[]{:S(2)}, u32[]{:S(2)}) collective-permute-start(bf16[2,1,96,256]{3,2,1,0:T(8,128)(2,1)S(1)} %get-tuple-element.46), channel_id=1, source_target_pairs={{0,1},{1,0},{2,3},{3,2},{4,5},{5,4},{6,7},{7,6},{8,9},{9,8},{10,11... | collective-permute-start | bytes 294920 | tf_op jit(solution)/shard_map/ppermute | solution.py:32
  37.5 5.3 %collective-permute-start.14 = (bf16[2,1,96,256]{3,2,1,0:T(8,128)(2,1)S(1)}, bf16[2,1,96,256]{3,2,1,0:T(8,128)(2,1)S(1)}, u32[]{:S(2)}, u32[]{:S(2)}) collective-permute-start(bf16[2,1,96,256]{3,2,1,0:T(8,128)(2,1)S(1)} %constant_dynamic-slice_fusion), channel_id=1, source_target_pairs={{0,1},{1,0},{2,3},{3,2},{4,5},{5,4},{6,7},{7,6},{8,9},{9,8},{10,11... | collective-permute-start | bytes 294920 | tf_op jit(solution)/shard_map/ppermute | solution.py:32
  37.6 4.6 %collective-permute-start.12 = (f32[4,512]{1,0:T(4,128)S(1)}, f32[4,512]{1,0:T(4,128)S(1)}, u32[]{:S(2)}, u32[]{:S(2)}) collective-permute-start(f32[4,512]{1,0:T(4,128)S(1)} %pad_maximum_fusion.1.refs_0_), channel_id=1, source_target_pairs={{0,6},{2,4},{4,2},{6,0},{8,14},{10,12},{12,10},{14,8},{16,22},{18,... | collective-permute-start | bytes 24584 | tf_op jit(solution)/shard_map/ppermute | solution.py:32
  38.3 3.9 %collective-permute-start.11 = (f32[4,512]{1,0:T(4,128)S(1)}, f32[4,512]{1,0:T(4,128)S(1)}, u32[]{:S(2)}, u32[]{:S(2)}) collective-permute-start(f32[4,512]{1,0:T(4,128)S(1)} %pad_maximum_fusion.1.refs_0_), channel_id=1, source_target_pairs={{0,4},{2,6},{4,0},{6,2},{8,12},{10,14},{12,8},{14,10},{16,20},{18,... | collective-permute-start | bytes 24584 | tf_op jit(solution)/shard_map/ppermute | solution.py:32
  38.3 4.5 %collective-permute-start.10 = (f32[4,512]{1,0:T(4,128)S(1)}, f32[4,512]{1,0:T(4,128)S(1)}, u32[]{:S(2)}, u32[]{:S(2)}) collective-permute-start(f32[4,512]{1,0:T(4,128)S(1)} %pad_maximum_fusion.1.refs_0_), channel_id=1, source_target_pairs={{0,2},{2,0},{4,6},{6,4},{8,10},{10,8},{12,14},{14,12},{16,18},{18,... | collective-permute-start | bytes 24584 | tf_op jit(solution)/shard_map/ppermute | solution.py:32

commit v23 on v20

--- a/solution.py
+++ b/solution.py
@@ -82,13 +82,9 @@
     return [frames[:, :1], frames[:, rows - 1 :]]
 
 
-def chained(value):
-    return lax.ppermute(value, "tm", [(i, i + 1) for i in range(lax.axis_size("tm") - 1)])
-
-
 def slab_halo(tail, sides):
     rows = [side[-1:] for side in sides]
-    return shifted(tail[:1], "tm", 1), chained(jnp.concatenate([tail[1:], *rows], axis=1))
+    return shifted(tail[:1], "tm", 1), shifted(jnp.concatenate([tail[1:], *rows], axis=1), "tm", 1)
 
 
 def row_halo(edges):

time: 49.3 us -> 49.6 us (level)
  waiting for transfers between devices: 10.8 us -> 13.1 us
  starting transfers between devices: 20.3 us -> 18.3 us
    ppermute x1 -> x0, starting transfers between devices: 3.69 us -> none  [chained(): lax.ppermute(value, 'tm', [(i, i + 1) for i in range(lax.axis_size('tm')...]
    ppermute x2 -> x3, waiting for transfers between devices: 4.02 us -> 7.45 us  [shifted(): lax.ppermute(value, axis, [(i, (i + step) % peers) for i in range(peers)])]
    ppermute x2 -> x3, starting transfers between devices: 3.05 us -> 4.74 us  [shifted(): lax.ppermute(value, axis, [(i, (i + step) % peers) for i in range(peers)])]
    ppermute x12, waiting for transfers between devices: 5.67 us -> 4.34 us  [traded(): lax.ppermute(value, axis, [(i, i ^ mask) for i in range(lax.axis_size(axi...]
  transfers between devices with their start and end apart: 16 -> 16, of which waited for: 9 -> 10; matrix products, arithmetic and copies ran while one was open for 0% -> 0% of each run, Pallas kernels for 18% -> 18%
where the time goes in v23:
time: 49.6 us; the launch traced here: 49.4 us
  starting transfers between devices  18.3 us (37%)
  Pallas kernels  17.8 us (36%)
  waiting for transfers between devices  13.1 us (26%)
    pallas_call x3, Pallas kernels, call(): pl.pallas_call(kernel, out_shape=outs, in_specs=[ANYWHERE if k in (aliase...  14.4 us
    ppermute x12, starting transfers between devices, traded(): lax.ppermute(value, axis, [(i, i ^ mask) for i in range(lax.axis_size(axi...  8.61 us
    ppermute x3, waiting for transfers between devices, shifted(): lax.ppermute(value, axis, [(i, (i + step) % peers) for i in range(peers)])  7.45 us
    all_to_all x1, starting transfers between devices, stats_table(): return lax.all_to_all(copies, ('tm', 'space'), 0, 0, tiled=True)  4.92 us
    ppermute x3, starting transfers between devices, shifted(): lax.ppermute(value, axis, [(i, (i + step) % peers) for i in range(peers)])  4.74 us
    ppermute x12, waiting for transfers between devices, traded(): lax.ppermute(value, axis, [(i, i ^ mask) for i in range(lax.axis_size(axi...  4.34 us
    pallas_call x1, Pallas kernels, entry_call(): pl.pallas_call(entry_kernel, out_shape=outs, in_specs=[ANYWHERE], out_spe...  1.95 us
    pallas_call x1, Pallas kernels, setup_call(): pl.pallas_call(functools.partial(setup_kernel, slabs, per_slab), out_shap...  1.39 us
  transfers between devices with their start and end apart: 16, of which 10 were waited for; matrix products, arithmetic and copies ran while one was open for 0% of the time, Pallas kernels for 18%

profile of v23, /device:TPU:0, one launch (start us, length us, event | category | flops | bytes accessed | tf_op | source)
XLA Modules:
  0.0 49.4 jit_solution(1809956243060898147)
XLA Ops:
  0.0 1.9 %shard_map.82 = (bf16[4,4,96,256]{3,2,1,0:T(8,128)(2,1)S(1)}, bf16[2,4,96,256]{3,2,1,0:T(8,128)(2,1)S(1)}, bf16[4,1,96,256]{3,2,1,0:T(8,128)(2,1)S(1)}, f32[32,1,512]{2,1,0:T(1,128)}, f32[8,128]{1,0:T(8,128)S(1)}) custom-call(bf16[4,4,96,256]{3,2,1,0:T(8,128)(2,1)} %feats_hbm.1), custom_call_target="tpu_custom_call" | custom-call | flops 1572864 | bytes 1572864 | tf_op jit(solution)/shard_map/pallas_call | solution.py:177
  2.0 0.5 %collective-permute-start.2 = (bf16[4,1,96,256]{3,2,1,0:T(8,128)(2,1)S(1)}, bf16[4,1,96,256]{3,2,1,0:T(8,128)(2,1)S(1)}, u32[]{:S(2)}, u32[]{:S(2)}) collective-permute-start(bf16[4,1,96,256]{3,2,1,0:T(8,128)(2,1)S(1)} %get-tuple-element.31), channel_id=1, source_target_pairs={{0,1},{1,0},{2,3},{3,2},{4,5},{5,4},{6,7},{7,6},{8,9},{9,8},{10,11... | collective-permute-start | bytes 589832 | tf_op jit(solution)/shard_map/ppermute | solution.py:32
  2.5 2.6 %collective-permute-start = (bf16[1,4,96,256]{3,2,1,0:T(8,128)(2,1)S(1)}, bf16[1,4,96,256]{3,2,1,0:T(8,128)(2,1)S(1)}, u32[]{:S(2)}, u32[]{:S(2)}) collective-permute-start(bf16[1,4,96,256]{3,2,1,0:T(8,128)(2,1)S(1)} %get-tuple-element.46), channel_id=1, source_target_pairs={{0,2},{2,4},{4,6},{6,8},{8,10},{10,12},{12,14},{14,16},{16,18},{18... | collective-permute-start | bytes 589832 | tf_op jit(solution)/shard_map/ppermute | solution.py:37
  5.1 4.9 %all-to-all-start = ((f32[32,1,512]{2,1,0:T(1,128)}), f32[32,1,512]{2,1,0:T(1,128)S(1)}, u32[]{:S(2)}, u32[]{:S(2)}) async-start(f32[32,1,512]{2,1,0:T(1,128)} %get-tuple-element.29), calls=%async_computation | async-start | bytes 131072 | tf_op jit(solution)/shard_map/all_to_all | solution.py:41
  10.0 0.0 collective-permute-done.2.refs_0_
  10.1 1.8 %collective-permute-start.4 = (bf16[1,5,96,256]{3,2,1,0:T(8,128)(2,1)S(1)}, bf16[1,5,96,256]{3,2,1,0:T(8,128)(2,1)S(1)}, u32[]{:S(2)}, u32[]{:S(2)}) collective-permute-start(bf16[1,5,96,256]{3,2,1,0:T(8,128)(2,1)S(1)} %pad_maximum_fusion), channel_id=1, source_target_pairs={{0,2},{2,4},{4,6},{6,8},{8,10},{10,12},{12,14},{14,16},{16,18},{18... | collective-permute-start | bytes 737288 | tf_op jit(solution)/shard_map/ppermute | solution.py:37
  11.9 3.0 %collective-permute-done.first = bf16[1,4,96,256]{3,2,1,0:T(8,128)(2,1)S(1)} collective-permute-done((bf16[1,4,96,256]{3,2,1,0:T(8,128)(2,1)S(1)}, bf16[1,4,96,256]{3,2,1,0:T(8,128)(2,1)S(1)}, u32[]{:S(2)}, u32[]{:S(2)}) %collective-permute-start) | collective-permute-done | bytes 196640 | tf_op jit(solution)/shard_map/ppermute | solution.py:37
  14.9 0.0 collective-permute-start.1
  14.9 1.4 %shard_map.83 = (bf16[1,3,3,256,256]{4,3,2,1,0:T(8,128)(2,1)S(1)}, f32[40,256]{1,0:T(8,128)S(1)}) custom-call(bf16[3,3,3,256,256]{4,3,2,1,0:T(8,128)(2,1)} %refs_2_.1, s32[16]{0:T(128)} %clips_hbm.1, f32[1,256]{1,0:T(1,128)} %bitcast.4, f32[1,256]{1,0:T(1,128)} %bitcast.5, f32[1,256]{1,0:T(1,128)} %bitcast.6, f32[1,256]{1,0:T(1,128)} %bitcast.7, ...), custom_call_target="tpu_custom_call" | custom-call | flops 1073741824 | bytes 65536 | tf_op jit(solution)/shard_map/pallas_call | solution.py:221
  16.3 0.0 collective-permute-done.1.refs_0_
  16.3 1.4 %all-to-all-done.table = f32[32,1,512]{2,1,0:T(1,128)S(1)} async-done(((f32[32,1,512]{2,1,0:T(1,128)}), f32[32,1,512]{2,1,0:T(1,128)S(1)}, u32[]{:S(2)}, u32[]{:S(2)}) %all-to-all-start) | async-done | bytes 65568 | tf_op jit(solution)/shard_map/all_to_all | solution.py:41
  17.6 4.7 %shard_map.84 = (bf16[2,6,96,256]{3,2,1,0:T(8,128)(2,1)S(1)}, f32[2,256]{1,0:T(2,128)S(1)}, bf16[2,3,3,256,256]{4,3,2,1,0:T(8,128)(2,1)S(1)}, bf16[2,4,96,256]{3...) custom-call(f32[40,256]{1,0:T(8,128)S(1)} %get-tuple-element.28.aux, ...), custom_call_target="tpu_custom_call" | custom-call | flops 1019215872 | bytes 1048576 | tf_op jit(solution)/shard_map/pallas_call | solution.py:428
  22.3 0.4 collective-permute-start.3
  22.7 0.2 collective-permute-done.4.second
  22.9 0.0 copy-start
  22.9 3.0 %shard_map.85 = (bf16[2,4,96,256]{3,2,1,0:T(8,128)(2,1)S(1)}, bf16[2,1,96,256]{3,2,1,0:T(8,128)(2,1)S(1)}, f32[1,512]{1,0:T(1,128)S(1)}) custom-call(f32[40,256]{1,0:T(8,128)S(1)} %get-tuple-element.28.aux, bf16[1,4,96,256]{3,2,1,0:T(8,128)(2,1)S(1)} %collective-permute-done.first, bf16[1,5,96,256]{3,2,1,0:T(8,128)(2,1)S(1)} %collective-permute-done.4.second, ...), custom_call_target="tpu_custom_call" | custom-call | flops 2717908992 | bytes 1048576 | tf_op jit(solution)/shard_map/pallas_call | solution.py:428
  25.9 0.1 collective-permute-start.5
  26.0 1.1 %collective-permute-done.5 = f32[1,512]{1,0:T(1,128)S(1)} collective-permute-done((f32[1,512]{1,0:T(1,128)S(1)}, f32[1,512]{1,0:T(1,128)S(1)}, u32[]{:S(2)}, u32[]{:S(2)}) %collective-permute-start.5) | collective-permute-done | bytes 2080 | tf_op jit(solution)/shard_map/ppermute | solution.py:32
  27.1 0.7 %collective-permute-start.8 = (f32[1,512]{1,0:T(1,128)S(1)}, f32[1,512]{1,0:T(1,128)S(1)}, u32[]{:S(2)}, u32[]{:S(2)}) collective-permute-start(f32[1,512]{1,0:T(1,128)S(1)} %add.8), channel_id=1, source_target_pairs={{0,24},{2,26},{4,28},{6,30},{8,16},{10,18},{12,20},{14,22},{16,8},... | collective-permute-start | bytes 6152 | tf_op jit(solution)/shard_map/ppermute | solution.py:32
  27.9 1.2 %collective-permute-start.7 = (f32[1,512]{1,0:T(1,128)S(1)}, f32[1,512]{1,0:T(1,128)S(1)}, u32[]{:S(2)}, u32[]{:S(2)}) collective-permute-start(f32[1,512]{1,0:T(1,128)S(1)} %add.8), channel_id=1, source_target_pairs={{0,16},{2,18},{4,20},{6,22},{8,24},{10,26},{12,28},{14,30},{16,0},... | collective-permute-start | bytes 6152 | tf_op jit(solution)/shard_map/ppermute | solution.py:32
  29.0 2.5 %collective-permute-start.6 = (f32[1,512]{1,0:T(1,128)S(1)}, f32[1,512]{1,0:T(1,128)S(1)}, u32[]{:S(2)}, u32[]{:S(2)}) collective-permute-start(f32[1,512]{1,0:T(1,128)S(1)} %add.8), channel_id=1, source_target_pairs={{0,8},{2,10},{4,12},{6,14},{8,0},{10,2},{12,4},{14,6},{16,24},{18,... | collective-permute-start | bytes 6152 | tf_op jit(solution)/shard_map/ppermute | solution.py:32
  31.5 0.0 collective-permute-start.13
  31.5 1.0 %collective-permute-done.8 = f32[1,512]{1,0:T(1,128)S(1)} collective-permute-done((f32[1,512]{1,0:T(1,128)S(1)}, f32[1,512]{1,0:T(1,128)S(1)}, u32[]{:S(2)}, u32[]{:S(2)}) %collective-permute-start.8) | collective-permute-done | bytes 2080 | tf_op jit(solution)/shard_map/ppermute | solution.py:32
  32.5 0.0 collective-permute-start.12
  32.5 0.0 collective-permute-done.7
  32.5 0.6 %collective-permute-done.6 = f32[1,512]{1,0:T(1,128)S(1)} collective-permute-done((f32[1,512]{1,0:T(1,128)S(1)}, f32[1,512]{1,0:T(1,128)S(1)}, u32[]{:S(2)}, u32[]{:S(2)}) %collective-permute-start.6) | collective-permute-done | bytes 2080 | tf_op jit(solution)/shard_map/ppermute | solution.py:32
  33.1 4.3 %collective-permute-done.3.refs_8_ = bf16[2,4,96,256]{3,2,1,0:T(8,128)(2,1)S(1)} collective-permute-done((bf16[2,4,96,256]{3,2,1,0:T(8,128)(2,1)S(1)}, bf16[2,4,96,256]{3,2,1,0:T(8,128)(2,1)S(1)}, u32[]{:S(2)}, u32[]{:S(2)}) %collective-permute-start.3) | collective-permute-done | bytes 393248 | tf_op jit(solution)/shard_map/ppermute | solution.py:37
  37.4 0.1 collective-permute-start.14
  37.5 1.1 %collective-permute-start.11 = (f32[4,512]{1,0:T(4,128)S(1)}, f32[4,512]{1,0:T(4,128)S(1)}, u32[]{:S(2)}, u32[]{:S(2)}) collective-permute-start(f32[4,512]{1,0:T(4,128)S(1)} %pad_maximum_fusion.1.refs_0_), channel_id=1, source_target_pairs={{0,6},{2,4},{4,2},{6,0},{8,14},{10,12},{12,10},{14,8},{16,22},{18,... | collective-permute-start | bytes 24584 | tf_op jit(solution)/shard_map/ppermute | solution.py:32
  38.6 0.0 collective-permute-start.10
  38.6 0.0 collective-permute-done.13.refs_7_
  38.6 2.4 %collective-permute-start.9 = (f32[4,512]{1,0:T(4,128)S(1)}, f32[4,512]{1,0:T(4,128)S(1)}, u32[]{:S(2)}, u32[]{:S(2)}) collective-permute-start(f32[4,512]{1,0:T(4,128)S(1)} %pad_maximum_fusion.1.refs_0_), channel_id=1, source_target_pairs={{0,2},{2,0},{4,6},{6,4},{8,10},{10,8},{12,14},{14,12},{16,18},{18,... | collective-permute-start | bytes 24584 | tf_op jit(solution)/shard_map/ppermute | solution.py:32
  41.0 1.1 %collective-permute-done.11.refs_3_ = f32[4,512]{1,0:T(4,128)S(1)} collective-permute-done((f32[4,512]{1,0:T(4,128)S(1)}, f32[4,512]{1,0:T(4,128)S(1)}, u32[]{:S(2)}, u32[]{:S(2)}) %collective-permute-start.11) | collective-permute-done | bytes 8224 | tf_op jit(solution)/shard_map/ppermute | solution.py:32
  42.1 0.2 collective-permute-done.10.refs_2_
  42.2 0.4 collective-permute-done.9.refs_1_
  42.6 0.0 collective-permute-done.12.refs_6_
  42.6 0.0 collective-permute-done.14.refs_9_
  42.6 0.0 copy-done
  42.6 6.8 %shard_map.86 = f32[4,4,96,256]{3,2,1,0:T(8,128)} custom-call(f32[40,256]{1,0:T(8,128)S(1)} %get-tuple-element.28.aux, f32[4,512]{1,0:T(4,128)S(1)} %pad_maximum_fusion.1.refs_0_, f32[4,512]{1,0:T(4,128)S(1)} %collective-permute-done.9.refs_1_, f32[4,512]{1,0:T(4,128)S(1)} %collective-permute-done.10.refs_2_, f32[4,512]{1,0:T(4,128)S(1)} %collective-permute-done.11.refs_3_, ...), custom_call_target="tpu_custom_call" | custom-call | flops 5435817984 | bytes 1048576 | tf_op jit(solution)/shard_map/pallas_call | solution.py:428
  (7 shorter events, 0.1 us)
Async XLA Ops:
  2.0 8.0 %collective-permute-start.2 = (bf16[4,1,96,256]{3,2,1,0:T(8,128)(2,1)S(1)}, bf16[4,1,96,256]{3,2,1,0:T(8,128)(2,1)S(1)}, u32[]{:S(2)}, u32[]{:S(2)}) collective-permute-start(bf16[4,1,96,256]{3,2,1,0:T(8,128)(2,1)S(1)} %get-tuple-element.31), channel_id=1, source_target_pairs={{0,1},{1,0},{2,3},{3,2},{4,5},{5,4},{6,7},{7,6},{8,9},{9,8},{10,11... | collective-permute-start | bytes 589832 | tf_op jit(solution)/shard_map/ppermute | solution.py:32
  2.5 12.4 %collective-permute-start = (bf16[1,4,96,256]{3,2,1,0:T(8,128)(2,1)S(1)}, bf16[1,4,96,256]{3,2,1,0:T(8,128)(2,1)S(1)}, u32[]{:S(2)}, u32[]{:S(2)}) collective-permute-start(bf16[1,4,96,256]{3,2,1,0:T(8,128)(2,1)S(1)} %get-tuple-element.46), channel_id=1, source_target_pairs={{0,2},{2,4},{4,6},{6,8},{8,10},{10,12},{12,14},{14,16},{16,18},{18... | collective-permute-start | bytes 589832 | tf_op jit(solution)/shard_map/ppermute | solution.py:37
  5.1 12.6 %all-to-all-start = ((f32[32,1,512]{2,1,0:T(1,128)}), f32[32,1,512]{2,1,0:T(1,128)S(1)}, u32[]{:S(2)}, u32[]{:S(2)}) async-start(f32[32,1,512]{2,1,0:T(1,128)} %get-tuple-element.29), calls=%async_computation | async-start | bytes 131072 | tf_op jit(solution)/shard_map/all_to_all | solution.py:41
  10.1 12.8 %collective-permute-start.4 = (bf16[1,5,96,256]{3,2,1,0:T(8,128)(2,1)S(1)}, bf16[1,5,96,256]{3,2,1,0:T(8,128)(2,1)S(1)}, u32[]{:S(2)}, u32[]{:S(2)}) collective-permute-start(bf16[1,5,96,256]{3,2,1,0:T(8,128)(2,1)S(1)} %pad_maximum_fusion), channel_id=1, source_target_pairs={{0,2},{2,4},{4,6},{6,8},{8,10},{10,12},{12,14},{14,16},{16,18},{18... | collective-permute-start | bytes 737288 | tf_op jit(solution)/shard_map/ppermute | solution.py:37
  14.9 1.4 %collective-permute-start.1 = (bf16[1,1,96,256]{3,2,1,0:T(8,128)(2,1)S(1)}, bf16[1,1,96,256]{3,2,1,0:T(8,128)(2,1)S(1)}, u32[]{:S(2)}, u32[]{:S(2)}) collective-permute-start(bf16[1,1,96,256]{3,2,1,0:T(8,128)(2,1)S(1)} %constant_dynamic-slice_fusion.1), channel_id=1, source_target_pairs={{0,1},{1,0},{2,3},{3,2},{4,5},{5,4},{6,7},{7,6},{8,9},{9,8},{10,11... | collective-permute-start | bytes 147464 | tf_op jit(solution)/shard_map/ppermute | solution.py:32
  22.3 15.0 %collective-permute-start.3 = (bf16[2,4,96,256]{3,2,1,0:T(8,128)(2,1)S(1)}, bf16[2,4,96,256]{3,2,1,0:T(8,128)(2,1)S(1)}, u32[]{:S(2)}, u32[]{:S(2)}) collective-permute-start(bf16[2,4,96,256]{3,2,1,0:T(8,128)(2,1)S(1)} %get-tuple-element.33.refs_5_), channel_id=1, source_target_pairs={{0,2},{2,4},{4,6},{6,8},{8,10},{10,12},{12,14},{14,16},{16,18},{18... | collective-permute-start | bytes 1179656 | tf_op jit(solution)/shard_map/ppermute | solution.py:37
  22.9 19.8 %copy-start = (bf16[3,3,3,256,256]{4,3,2,1,0:T(8,128)(2,1)S(1)}, bf16[3,3,3,256,256]{4,3,2,1,0:T(8,128)(2,1)}, u32[]{:S(2)}) copy-start(bf16[3,3,3,256,256]{4,3,2,1,0:T(8,128)(2,1)} %refs_10_.1) | copy-start | bytes 10616836
  25.9 1.2 %collective-permute-start.5 = (f32[1,512]{1,0:T(1,128)S(1)}, f32[1,512]{1,0:T(1,128)S(1)}, u32[]{:S(2)}, u32[]{:S(2)}) collective-permute-start(f32[1,512]{1,0:T(1,128)S(1)} %get-tuple-element.39), channel_id=1, source_target_pairs={{0,1},{1,0},{2,3},{3,2},{4,5},{5,4},{6,7},{7,6},{8,9},{9,8},{10,11... | collective-permute-start | bytes 6152 | tf_op jit(solution)/shard_map/ppermute | solution.py:32
  27.1 5.4 %collective-permute-start.8 = (f32[1,512]{1,0:T(1,128)S(1)}, f32[1,512]{1,0:T(1,128)S(1)}, u32[]{:S(2)}, u32[]{:S(2)}) collective-permute-start(f32[1,512]{1,0:T(1,128)S(1)} %add.8), channel_id=1, source_target_pairs={{0,24},{2,26},{4,28},{6,30},{8,16},{10,18},{12,20},{14,22},{16,8},... | collective-permute-start | bytes 6152 | tf_op jit(solution)/shard_map/ppermute | solution.py:32
  27.9 4.6 %collective-permute-start.7 = (f32[1,512]{1,0:T(1,128)S(1)}, f32[1,512]{1,0:T(1,128)S(1)}, u32[]{:S(2)}, u32[]{:S(2)}) collective-permute-start(f32[1,512]{1,0:T(1,128)S(1)} %add.8), channel_id=1, source_target_pairs={{0,16},{2,18},{4,20},{6,22},{8,24},{10,26},{12,28},{14,30},{16,0},... | collective-permute-start | bytes 6152 | tf_op jit(solution)/shard_map/ppermute | solution.py:32
  29.0 4.0 %collective-permute-start.6 = (f32[1,512]{1,0:T(1,128)S(1)}, f32[1,512]{1,0:T(1,128)S(1)}, u32[]{:S(2)}, u32[]{:S(2)}) collective-permute-start(f32[1,512]{1,0:T(1,128)S(1)} %add.8), channel_id=1, source_target_pairs={{0,8},{2,10},{4,12},{6,14},{8,0},{10,2},{12,4},{14,6},{16,24},{18,... | collective-permute-start | bytes 6152 | tf_op jit(solution)/shard_map/ppermute | solution.py:32
  31.5 7.1 %collective-permute-start.13 = (bf16[2,1,96,256]{3,2,1,0:T(8,128)(2,1)S(1)}, bf16[2,1,96,256]{3,2,1,0:T(8,128)(2,1)S(1)}, u32[]{:S(2)}, u32[]{:S(2)}) collective-permute-start(bf16[2,1,96,256]{3,2,1,0:T(8,128)(2,1)S(1)} %get-tuple-element.43), channel_id=1, source_target_pairs={{0,1},{1,0},{2,3},{3,2},{4,5},{5,4},{6,7},{7,6},{8,9},{9,8},{10,11... | collective-permute-start | bytes 294920 | tf_op jit(solution)/shard_map/ppermute | solution.py:32
  32.5 10.1 %collective-permute-start.12 = (bf16[2,1,96,256]{3,2,1,0:T(8,128)(2,1)S(1)}, bf16[2,1,96,256]{3,2,1,0:T(8,128)(2,1)S(1)}, u32[]{:S(2)}, u32[]{:S(2)}) collective-permute-start(bf16[2,1,96,256]{3,2,1,0:T(8,128)(2,1)S(1)} %get-tuple-element.42), channel_id=1, source_target_pairs={{0,1},{1,0},{2,3},{3,2},{4,5},{5,4},{6,7},{7,6},{8,9},{9,8},{10,11... | collective-permute-start | bytes 294920 | tf_op jit(solution)/shard_map/ppermute | solution.py:32
  37.4 5.3 %collective-permute-start.14 = (bf16[2,1,96,256]{3,2,1,0:T(8,128)(2,1)S(1)}, bf16[2,1,96,256]{3,2,1,0:T(8,128)(2,1)S(1)}, u32[]{:S(2)}, u32[]{:S(2)}) collective-permute-start(bf16[2,1,96,256]{3,2,1,0:T(8,128)(2,1)S(1)} %constant_dynamic-slice_fusion), channel_id=1, source_target_pairs={{0,1},{1,0},{2,3},{3,2},{4,5},{5,4},{6,7},{7,6},{8,9},{9,8},{10,11... | collective-permute-start | bytes 294920 | tf_op jit(solution)/shard_map/ppermute | solution.py:32
  37.5 4.6 %collective-permute-start.11 = (f32[4,512]{1,0:T(4,128)S(1)}, f32[4,512]{1,0:T(4,128)S(1)}, u32[]{:S(2)}, u32[]{:S(2)}) collective-permute-start(f32[4,512]{1,0:T(4,128)S(1)} %pad_maximum_fusion.1.refs_0_), channel_id=1, source_target_pairs={{0,6},{2,4},{4,2},{6,0},{8,14},{10,12},{12,10},{14,8},{16,22},{18,... | collective-permute-start | bytes 24584 | tf_op jit(solution)/shard_map/ppermute | solution.py:32
  38.6 3.7 %collective-permute-start.10 = (f32[4,512]{1,0:T(4,128)S(1)}, f32[4,512]{1,0:T(4,128)S(1)}, u32[]{:S(2)}, u32[]{:S(2)}) collective-permute-start(f32[4,512]{1,0:T(4,128)S(1)} %pad_maximum_fusion.1.refs_0_), channel_id=1, source_target_pairs={{0,4},{2,6},{4,0},{6,2},{8,12},{10,14},{12,8},{14,10},{16,20},{18,... | collective-permute-start | bytes 24584 | tf_op jit(solution)/shard_map/ppermute | solution.py:32
  38.6 4.0 %collective-permute-start.9 = (f32[4,512]{1,0:T(4,128)S(1)}, f32[4,512]{1,0:T(4,128)S(1)}, u32[]{:S(2)}, u32[]{:S(2)}) collective-permute-start(f32[4,512]{1,0:T(4,128)S(1)} %pad_maximum_fusion.1.refs_0_), channel_id=1, source_target_pairs={{0,2},{2,0},{4,6},{6,4},{8,10},{10,8},{12,14},{14,12},{16,18},{18,... | collective-permute-start | bytes 24584 | tf_op jit(solution)/shard_map/ppermute | solution.py:32

commit v24 on v21

--- a/solution.py
+++ b/solution.py
@@ -88,7 +88,7 @@
 
 def slab_halo(tail, sides):
     rows = [side[-1:] for side in sides]
-    return shifted(tail[:1], "tm", 1), chained(jnp.concatenate([tail[1:], *rows], axis=1))
+    return shifted(tail[:1], "tm", 1), shifted(jnp.concatenate([tail[1:], *rows], axis=1), "tm", 1)
 
 
 def row_halo(edges):

time: 49.3 us -> 48.6 us (0.986)
  starting transfers between devices: 22.1 us -> 20.2 us
  waiting for transfers between devices: 8.81 us -> 10.1 us
    ppermute x2 -> x1, starting transfers between devices: 6.05 us -> 2.24 us  [chained(): lax.ppermute(value, 'tm', [(i, i + 1) for i in range(lax.axis_size('tm')...]
    ppermute x1 -> x2, waiting for transfers between devices: 1.11 us -> 2.99 us  [shifted(): lax.ppermute(value, axis, [(i, (i + step) % peers) for i in range(peers)])]
    ppermute x1 -> x2, starting transfers between devices: 2.56 us -> 4.38 us  [shifted(): lax.ppermute(value, axis, [(i, (i + step) % peers) for i in range(peers)])]
    ppermute x12, waiting for transfers between devices: 6.58 us -> 5.77 us  [traded(): lax.ppermute(value, axis, [(i, i ^ mask) for i in range(lax.axis_size(axi...]
where the time goes in v24:
time: 48.6 us; the launch traced here: 48.4 us
  starting transfers between devices  20.2 us (42%)
  Pallas kernels  17.8 us (37%)
  waiting for transfers between devices  10.1 us (21%)
    pallas_call x3, Pallas kernels, call(): pl.pallas_call(kernel, out_shape=outs, in_specs=[ANYWHERE if k in (aliase...  14.4 us
    ppermute x12, starting transfers between devices, traded(): lax.ppermute(value, axis, [(i, i ^ mask) for i in range(lax.axis_size(axi...  8.67 us
    ppermute x12, waiting for transfers between devices, traded(): lax.ppermute(value, axis, [(i, i ^ mask) for i in range(lax.axis_size(axi...  5.77 us
    all_to_all x1, starting transfers between devices, stats_table(): return lax.all_to_all(copies, ('tm', 'space'), 0, 0, tiled=True)  4.92 us
    ppermute x2, starting transfers between devices, shifted(): lax.ppermute(value, axis, [(i, (i + step) % peers) for i in range(peers)])  4.38 us
    ppermute x2, waiting for transfers between devices, shifted(): lax.ppermute(value, axis, [(i, (i + step) % peers) for i in range(peers)])  2.99 us
    ppermute x1, starting transfers between devices, chained(): lax.ppermute(value, 'tm', [(i, i + 1) for i in range(lax.axis_size('tm')...  2.24 us
    pallas_call x1, Pallas kernels, entry_call(): pl.pallas_call(entry_kernel, out_shape=outs, in_specs=[ANYWHERE], out_spe...  1.95 us
  transfers between devices with their start and end apart: 16, of which 8 were waited for; matrix products, arithmetic and copies ran while one was open for 0% of the time, Pallas kernels for 19%

profile of v24, /device:TPU:0, one launch (start us, length us, event | category | flops | bytes accessed | tf_op | source)
XLA Modules:
  0.0 48.4 jit_solution(4091381474933080022)
XLA Ops:
  0.0 1.9 %shard_map.82 = (bf16[4,4,96,256]{3,2,1,0:T(8,128)(2,1)S(1)}, bf16[2,4,96,256]{3,2,1,0:T(8,128)(2,1)S(1)}, bf16[4,1,96,256]{3,2,1,0:T(8,128)(2,1)S(1)}, f32[32,1,512]{2,1,0:T(1,128)}, f32[8,128]{1,0:T(8,128)S(1)}) custom-call(bf16[4,4,96,256]{3,2,1,0:T(8,128)(2,1)} %feats_hbm.1), custom_call_target="tpu_custom_call" | custom-call | flops 1572864 | bytes 1572864 | tf_op jit(solution)/shard_map/pallas_call | solution.py:181
  2.0 0.5 %collective-permute-start.2 = (bf16[4,1,96,256]{3,2,1,0:T(8,128)(2,1)S(1)}, bf16[4,1,96,256]{3,2,1,0:T(8,128)(2,1)S(1)}, u32[]{:S(2)}, u32[]{:S(2)}) collective-permute-start(bf16[4,1,96,256]{3,2,1,0:T(8,128)(2,1)S(1)} %get-tuple-element.31), channel_id=1, source_target_pairs={{0,1},{1,0},{2,3},{3,2},{4,5},{5,4},{6,7},{7,6},{8,9},{9,8},{10,11... | collective-permute-start | bytes 589832 | tf_op jit(solution)/shard_map/ppermute | solution.py:32
  2.5 2.6 %collective-permute-start = (bf16[1,4,96,256]{3,2,1,0:T(8,128)(2,1)S(1)}, bf16[1,4,96,256]{3,2,1,0:T(8,128)(2,1)S(1)}, u32[]{:S(2)}, u32[]{:S(2)}) collective-permute-start(bf16[1,4,96,256]{3,2,1,0:T(8,128)(2,1)S(1)} %get-tuple-element.46), channel_id=1, source_target_pairs={{0,2},{2,4},{4,6},{6,8},{8,10},{10,12},{12,14},{14,16},{16,18},{18... | collective-permute-start | bytes 589832 | tf_op jit(solution)/shard_map/ppermute | solution.py:37
  5.1 4.9 %all-to-all-start = ((f32[32,1,512]{2,1,0:T(1,128)}), f32[32,1,512]{2,1,0:T(1,128)S(1)}, u32[]{:S(2)}, u32[]{:S(2)}) async-start(f32[32,1,512]{2,1,0:T(1,128)} %get-tuple-element.29), calls=%async_computation | async-start | bytes 131072 | tf_op jit(solution)/shard_map/all_to_all | solution.py:41
  10.0 0.0 collective-permute-done.2.refs_0_
  10.1 1.8 %collective-permute-start.4 = (bf16[1,5,96,256]{3,2,1,0:T(8,128)(2,1)S(1)}, bf16[1,5,96,256]{3,2,1,0:T(8,128)(2,1)S(1)}, u32[]{:S(2)}, u32[]{:S(2)}) collective-permute-start(bf16[1,5,96,256]{3,2,1,0:T(8,128)(2,1)S(1)} %pad_maximum_fusion), channel_id=1, source_target_pairs={{0,2},{2,4},{4,6},{6,8},{8,10},{10,12},{12,14},{14,16},{16,18},{18... | collective-permute-start | bytes 737288 | tf_op jit(solution)/shard_map/ppermute | solution.py:37
  11.9 3.0 %collective-permute-done.first = bf16[1,4,96,256]{3,2,1,0:T(8,128)(2,1)S(1)} collective-permute-done((bf16[1,4,96,256]{3,2,1,0:T(8,128)(2,1)S(1)}, bf16[1,4,96,256]{3,2,1,0:T(8,128)(2,1)S(1)}, u32[]{:S(2)}, u32[]{:S(2)}) %collective-permute-start) | collective-permute-done | bytes 196640 | tf_op jit(solution)/shard_map/ppermute | solution.py:37
  14.9 0.0 collective-permute-start.1
  14.9 1.4 %shard_map.83 = (bf16[1,3,3,256,256]{4,3,2,1,0:T(8,128)(2,1)S(1)}, f32[40,256]{1,0:T(8,128)S(1)}) custom-call(bf16[3,3,3,256,256]{4,3,2,1,0:T(8,128)(2,1)} %refs_2_.1, s32[16]{0:T(128)} %clips_hbm.1, f32[1,256]{1,0:T(1,128)} %bitcast.4, f32[1,256]{1,0:T(1,128)} %bitcast.5, f32[1,256]{1,0:T(1,128)} %bitcast.6, f32[1,256]{1,0:T(1,128)} %bitcast.7, ...), custom_call_target="tpu_custom_call" | custom-call | flops 1073741824 | bytes 65536 | tf_op jit(solution)/shard_map/pallas_call | solution.py:225
  16.3 0.0 collective-permute-done.1.refs_0_
  16.3 1.4 %all-to-all-done.table = f32[32,1,512]{2,1,0:T(1,128)S(1)} async-done(((f32[32,1,512]{2,1,0:T(1,128)}), f32[32,1,512]{2,1,0:T(1,128)S(1)}, u32[]{:S(2)}, u32[]{:S(2)}) %all-to-all-start) | async-done | bytes 65568 | tf_op jit(solution)/shard_map/all_to_all | solution.py:41
  17.6 4.7 %shard_map.84 = (bf16[2,6,96,256]{3,2,1,0:T(8,128)(2,1)S(1)}, f32[2,256]{1,0:T(2,128)S(1)}, bf16[2,3,3,256,256]{4,3,2,1,0:T(8,128)(2,1)S(1)}, bf16[2,4,96,256]{3...) custom-call(f32[40,256]{1,0:T(8,128)S(1)} %get-tuple-element.28.aux, ...), custom_call_target="tpu_custom_call" | custom-call | flops 1019215872 | bytes 1048576 | tf_op jit(solution)/shard_map/pallas_call | solution.py:432
  22.3 2.2 %collective-permute-start.3 = (bf16[2,4,96,256]{3,2,1,0:T(8,128)(2,1)S(1)}, bf16[2,4,96,256]{3,2,1,0:T(8,128)(2,1)S(1)}, u32[]{:S(2)}, u32[]{:S(2)}) collective-permute-start(bf16[2,4,96,256]{3,2,1,0:T(8,128)(2,1)S(1)} %get-tuple-element.33.refs_5_), channel_id=1, source_target_pairs={{0,2},{2,4},{4,6},{6,8},{8,10},{10,12},{12,14},{14,16},{16,18},{18... | collective-permute-start | bytes 1179656 | tf_op jit(solution)/shard_map/ppermute | solution.py:86
  24.6 0.0 collective-permute-done.4.second
  24.6 0.0 copy-start
  24.6 3.0 %shard_map.85 = (bf16[2,4,96,256]{3,2,1,0:T(8,128)(2,1)S(1)}, bf16[2,1,96,256]{3,2,1,0:T(8,128)(2,1)S(1)}, f32[1,512]{1,0:T(1,128)S(1)}) custom-call(f32[40,256]{1,0:T(8,128)S(1)} %get-tuple-element.28.aux, bf16[1,4,96,256]{3,2,1,0:T(8,128)(2,1)S(1)} %collective-permute-done.first, bf16[1,5,96,256]{3,2,1,0:T(8,128)(2,1)S(1)} %collective-permute-done.4.second, ...), custom_call_target="tpu_custom_call" | custom-call | flops 2717908992 | bytes 1048576 | tf_op jit(solution)/shard_map/pallas_call | solution.py:432
  27.6 0.1 collective-permute-start.5
  27.7 1.1 %collective-permute-done.5 = f32[1,512]{1,0:T(1,128)S(1)} collective-permute-done((f32[1,512]{1,0:T(1,128)S(1)}, f32[1,512]{1,0:T(1,128)S(1)}, u32[]{:S(2)}, u32[]{:S(2)}) %collective-permute-start.5) | collective-permute-done | bytes 2080 | tf_op jit(solution)/shard_map/ppermute | solution.py:32
  28.8 0.8 %collective-permute-start.8 = (f32[1,512]{1,0:T(1,128)S(1)}, f32[1,512]{1,0:T(1,128)S(1)}, u32[]{:S(2)}, u32[]{:S(2)}) collective-permute-start(f32[1,512]{1,0:T(1,128)S(1)} %add.8), channel_id=1, source_target_pairs={{0,24},{2,26},{4,28},{6,30},{8,16},{10,18},{12,20},{14,22},{16,8},... | collective-permute-start | bytes 6152 | tf_op jit(solution)/shard_map/ppermute | solution.py:32
  29.6 1.3 %collective-permute-start.7 = (f32[1,512]{1,0:T(1,128)S(1)}, f32[1,512]{1,0:T(1,128)S(1)}, u32[]{:S(2)}, u32[]{:S(2)}) collective-permute-start(f32[1,512]{1,0:T(1,128)S(1)} %add.8), channel_id=1, source_target_pairs={{0,16},{2,18},{4,20},{6,22},{8,24},{10,26},{12,28},{14,30},{16,0},... | collective-permute-start | bytes 6152 | tf_op jit(solution)/shard_map/ppermute | solution.py:32
  30.9 2.3 %collective-permute-start.6 = (f32[1,512]{1,0:T(1,128)S(1)}, f32[1,512]{1,0:T(1,128)S(1)}, u32[]{:S(2)}, u32[]{:S(2)}) collective-permute-start(f32[1,512]{1,0:T(1,128)S(1)} %add.8), channel_id=1, source_target_pairs={{0,8},{2,10},{4,12},{6,14},{8,0},{10,2},{12,4},{14,6},{16,24},{18,... | collective-permute-start | bytes 6152 | tf_op jit(solution)/shard_map/ppermute | solution.py:32
  33.2 0.0 collective-permute-start.13
  33.2 1.0 %collective-permute-done.8 = f32[1,512]{1,0:T(1,128)S(1)} collective-permute-done((f32[1,512]{1,0:T(1,128)S(1)}, f32[1,512]{1,0:T(1,128)S(1)}, u32[]{:S(2)}, u32[]{:S(2)}) %collective-permute-start.8) | collective-permute-done | bytes 2080 | tf_op jit(solution)/shard_map/ppermute | solution.py:32
  34.2 0.0 collective-permute-start.12
  34.2 0.0 collective-permute-done.7
  34.2 0.6 %collective-permute-done.6 = f32[1,512]{1,0:T(1,128)S(1)} collective-permute-done((f32[1,512]{1,0:T(1,128)S(1)}, f32[1,512]{1,0:T(1,128)S(1)}, u32[]{:S(2)}, u32[]{:S(2)}) %collective-permute-start.6) | collective-permute-done | bytes 2080 | tf_op jit(solution)/shard_map/ppermute | solution.py:32
  34.8 0.0 collective-permute-done.3.refs_8_
  34.8 0.1 collective-permute-start.14
  34.9 3.0 %collective-permute-start.11 = (f32[4,512]{1,0:T(4,128)S(1)}, f32[4,512]{1,0:T(4,128)S(1)}, u32[]{:S(2)}, u32[]{:S(2)}) collective-permute-start(f32[4,512]{1,0:T(4,128)S(1)} %pad_maximum_fusion.1.refs_0_), channel_id=1, source_target_pairs={{0,6},{2,4},{4,2},{6,0},{8,14},{10,12},{12,10},{14,8},{16,22},{18,... | collective-permute-start | bytes 24584 | tf_op jit(solution)/shard_map/ppermute | solution.py:32
  37.9 0.1 collective-permute-start.10
  37.9 0.0 collective-permute-done.13.refs_7_
  37.9 0.6 %collective-permute-start.9 = (f32[4,512]{1,0:T(4,128)S(1)}, f32[4,512]{1,0:T(4,128)S(1)}, u32[]{:S(2)}, u32[]{:S(2)}) collective-permute-start(f32[4,512]{1,0:T(4,128)S(1)} %pad_maximum_fusion.1.refs_0_), channel_id=1, source_target_pairs={{0,2},{2,0},{4,6},{6,4},{8,10},{10,8},{12,14},{14,12},{16,18},{18,... | collective-permute-start | bytes 24584 | tf_op jit(solution)/shard_map/ppermute | solution.py:32
  38.5 1.0 %collective-permute-done.11.refs_3_ = f32[4,512]{1,0:T(4,128)S(1)} collective-permute-done((f32[4,512]{1,0:T(4,128)S(1)}, f32[4,512]{1,0:T(4,128)S(1)}, u32[]{:S(2)}, u32[]{:S(2)}) %collective-permute-start.11) | collective-permute-done | bytes 8224 | tf_op jit(solution)/shard_map/ppermute | solution.py:32
  39.5 2.0 %collective-permute-done.10.refs_2_ = f32[4,512]{1,0:T(4,128)S(1)} collective-permute-done((f32[4,512]{1,0:T(4,128)S(1)}, f32[4,512]{1,0:T(4,128)S(1)}, u32[]{:S(2)}, u32[]{:S(2)}) %collective-permute-start.10) | collective-permute-done | bytes 8224 | tf_op jit(solution)/shard_map/ppermute | solution.py:32
  41.5 0.1 collective-permute-done.9.refs_1_
  41.6 0.0 collective-permute-done.12.refs_6_
  41.6 0.0 collective-permute-done.14.refs_9_
  41.6 0.0 copy-done
  41.6 6.8 %shard_map.86 = f32[4,4,96,256]{3,2,1,0:T(8,128)} custom-call(f32[40,256]{1,0:T(8,128)S(1)} %get-tuple-element.28.aux, f32[4,512]{1,0:T(4,128)S(1)} %pad_maximum_fusion.1.refs_0_, f32[4,512]{1,0:T(4,128)S(1)} %collective-permute-done.9.refs_1_, f32[4,512]{1,0:T(4,128)S(1)} %collective-permute-done.10.refs_2_, f32[4,512]{1,0:T(4,128)S(1)} %collective-permute-done.11.refs_3_, ...), custom_call_target="tpu_custom_call" | custom-call | flops 5435817984 | bytes 1048576 | tf_op jit(solution)/shard_map/pallas_call | solution.py:432
  (7 shorter events, 0.1 us)
Async XLA Ops:
  2.0 8.0 %collective-permute-start.2 = (bf16[4,1,96,256]{3,2,1,0:T(8,128)(2,1)S(1)}, bf16[4,1,96,256]{3,2,1,0:T(8,128)(2,1)S(1)}, u32[]{:S(2)}, u32[]{:S(2)}) collective-permute-start(bf16[4,1,96,256]{3,2,1,0:T(8,128)(2,1)S(1)} %get-tuple-element.31), channel_id=1, source_target_pairs={{0,1},{1,0},{2,3},{3,2},{4,5},{5,4},{6,7},{7,6},{8,9},{9,8},{10,11... | collective-permute-start | bytes 589832 | tf_op jit(solution)/shard_map/ppermute | solution.py:32
  2.5 12.4 %collective-permute-start = (bf16[1,4,96,256]{3,2,1,0:T(8,128)(2,1)S(1)}, bf16[1,4,96,256]{3,2,1,0:T(8,128)(2,1)S(1)}, u32[]{:S(2)}, u32[]{:S(2)}) collective-permute-start(bf16[1,4,96,256]{3,2,1,0:T(8,128)(2,1)S(1)} %get-tuple-element.46), channel_id=1, source_target_pairs={{0,2},{2,4},{4,6},{6,8},{8,10},{10,12},{12,14},{14,16},{16,18},{18... | collective-permute-start | bytes 589832 | tf_op jit(solution)/shard_map/ppermute | solution.py:37
  5.1 12.6 %all-to-all-start = ((f32[32,1,512]{2,1,0:T(1,128)}), f32[32,1,512]{2,1,0:T(1,128)S(1)}, u32[]{:S(2)}, u32[]{:S(2)}) async-start(f32[32,1,512]{2,1,0:T(1,128)} %get-tuple-element.29), calls=%async_computation | async-start | bytes 131072 | tf_op jit(solution)/shard_map/all_to_all | solution.py:41
  10.1 14.5 %collective-permute-start.4 = (bf16[1,5,96,256]{3,2,1,0:T(8,128)(2,1)S(1)}, bf16[1,5,96,256]{3,2,1,0:T(8,128)(2,1)S(1)}, u32[]{:S(2)}, u32[]{:S(2)}) collective-permute-start(bf16[1,5,96,256]{3,2,1,0:T(8,128)(2,1)S(1)} %pad_maximum_fusion), channel_id=1, source_target_pairs={{0,2},{2,4},{4,6},{6,8},{8,10},{10,12},{12,14},{14,16},{16,18},{18... | collective-permute-start | bytes 737288 | tf_op jit(solution)/shard_map/ppermute | solution.py:37
  14.9 1.4 %collective-permute-start.1 = (bf16[1,1,96,256]{3,2,1,0:T(8,128)(2,1)S(1)}, bf16[1,1,96,256]{3,2,1,0:T(8,128)(2,1)S(1)}, u32[]{:S(2)}, u32[]{:S(2)}) collective-permute-start(bf16[1,1,96,256]{3,2,1,0:T(8,128)(2,1)S(1)} %constant_dynamic-slice_fusion.1), channel_id=1, source_target_pairs={{0,1},{1,0},{2,3},{3,2},{4,5},{5,4},{6,7},{7,6},{8,9},{9,8},{10,11... | collective-permute-start | bytes 147464 | tf_op jit(solution)/shard_map/ppermute | solution.py:32
  22.3 12.5 %collective-permute-start.3 = (bf16[2,4,96,256]{3,2,1,0:T(8,128)(2,1)S(1)}, bf16[2,4,96,256]{3,2,1,0:T(8,128)(2,1)S(1)}, u32[]{:S(2)}, u32[]{:S(2)}) collective-permute-start(bf16[2,4,96,256]{3,2,1,0:T(8,128)(2,1)S(1)} %get-tuple-element.33.refs_5_), channel_id=1, source_target_pairs={{0,2},{2,4},{4,6},{6,8},{8,10},{10,12},{12,14},{14,16},{16,18},{18... | collective-permute-start | bytes 1179656 | tf_op jit(solution)/shard_map/ppermute | solution.py:86
  24.6 17.0 %copy-start = (bf16[3,3,3,256,256]{4,3,2,1,0:T(8,128)(2,1)S(1)}, bf16[3,3,3,256,256]{4,3,2,1,0:T(8,128)(2,1)}, u32[]{:S(2)}) copy-start(bf16[3,3,3,256,256]{4,3,2,1,0:T(8,128)(2,1)} %refs_10_.1) | copy-start | bytes 10616836
  27.6 1.2 %collective-permute-start.5 = (f32[1,512]{1,0:T(1,128)S(1)}, f32[1,512]{1,0:T(1,128)S(1)}, u32[]{:S(2)}, u32[]{:S(2)}) collective-permute-start(f32[1,512]{1,0:T(1,128)S(1)} %get-tuple-element.39), channel_id=1, source_target_pairs={{0,1},{1,0},{2,3},{3,2},{4,5},{5,4},{6,7},{7,6},{8,9},{9,8},{10,11... | collective-permute-start | bytes 6152 | tf_op jit(solution)/shard_map/ppermute | solution.py:32
  28.8 5.4 %collective-permute-start.8 = (f32[1,512]{1,0:T(1,128)S(1)}, f32[1,512]{1,0:T(1,128)S(1)}, u32[]{:S(2)}, u32[]{:S(2)}) collective-permute-start(f32[1,512]{1,0:T(1,128)S(1)} %add.8), channel_id=1, source_target_pairs={{0,24},{2,26},{4,28},{6,30},{8,16},{10,18},{12,20},{14,22},{16,8},... | collective-permute-start | bytes 6152 | tf_op jit(solution)/shard_map/ppermute | solution.py:32
  29.6 4.6 %collective-permute-start.7 = (f32[1,512]{1,0:T(1,128)S(1)}, f32[1,512]{1,0:T(1,128)S(1)}, u32[]{:S(2)}, u32[]{:S(2)}) collective-permute-start(f32[1,512]{1,0:T(1,128)S(1)} %add.8), channel_id=1, source_target_pairs={{0,16},{2,18},{4,20},{6,22},{8,24},{10,26},{12,28},{14,30},{16,0},... | collective-permute-start | bytes 6152 | tf_op jit(solution)/shard_map/ppermute | solution.py:32
  30.9 3.9 %collective-permute-start.6 = (f32[1,512]{1,0:T(1,128)S(1)}, f32[1,512]{1,0:T(1,128)S(1)}, u32[]{:S(2)}, u32[]{:S(2)}) collective-permute-start(f32[1,512]{1,0:T(1,128)S(1)} %add.8), channel_id=1, source_target_pairs={{0,8},{2,10},{4,12},{6,14},{8,0},{10,2},{12,4},{14,6},{16,24},{18,... | collective-permute-start | bytes 6152 | tf_op jit(solution)/shard_map/ppermute | solution.py:32
  33.2 4.7 %collective-permute-start.13 = (bf16[2,1,96,256]{3,2,1,0:T(8,128)(2,1)S(1)}, bf16[2,1,96,256]{3,2,1,0:T(8,128)(2,1)S(1)}, u32[]{:S(2)}, u32[]{:S(2)}) collective-permute-start(bf16[2,1,96,256]{3,2,1,0:T(8,128)(2,1)S(1)} %get-tuple-element.43), channel_id=1, source_target_pairs={{0,1},{1,0},{2,3},{3,2},{4,5},{5,4},{6,7},{7,6},{8,9},{9,8},{10,11... | collective-permute-start | bytes 294920 | tf_op jit(solution)/shard_map/ppermute | solution.py:32
  34.2 7.4 %collective-permute-start.12 = (bf16[2,1,96,256]{3,2,1,0:T(8,128)(2,1)S(1)}, bf16[2,1,96,256]{3,2,1,0:T(8,128)(2,1)S(1)}, u32[]{:S(2)}, u32[]{:S(2)}) collective-permute-start(bf16[2,1,96,256]{3,2,1,0:T(8,128)(2,1)S(1)} %get-tuple-element.42), channel_id=1, source_target_pairs={{0,1},{1,0},{2,3},{3,2},{4,5},{5,4},{6,7},{7,6},{8,9},{9,8},{10,11... | collective-permute-start | bytes 294920 | tf_op jit(solution)/shard_map/ppermute | solution.py:32
  34.8 6.8 %collective-permute-start.14 = (bf16[2,1,96,256]{3,2,1,0:T(8,128)(2,1)S(1)}, bf16[2,1,96,256]{3,2,1,0:T(8,128)(2,1)S(1)}, u32[]{:S(2)}, u32[]{:S(2)}) collective-permute-start(bf16[2,1,96,256]{3,2,1,0:T(8,128)(2,1)S(1)} %constant_dynamic-slice_fusion), channel_id=1, source_target_pairs={{0,1},{1,0},{2,3},{3,2},{4,5},{5,4},{6,7},{7,6},{8,9},{9,8},{10,11... | collective-permute-start | bytes 294920 | tf_op jit(solution)/shard_map/ppermute | solution.py:32
  34.9 4.6 %collective-permute-start.11 = (f32[4,512]{1,0:T(4,128)S(1)}, f32[4,512]{1,0:T(4,128)S(1)}, u32[]{:S(2)}, u32[]{:S(2)}) collective-permute-start(f32[4,512]{1,0:T(4,128)S(1)} %pad_maximum_fusion.1.refs_0_), channel_id=1, source_target_pairs={{0,6},{2,4},{4,2},{6,0},{8,14},{10,12},{12,10},{14,8},{16,22},{18,... | collective-permute-start | bytes 24584 | tf_op jit(solution)/shard_map/ppermute | solution.py:32
  37.9 3.7 %collective-permute-start.10 = (f32[4,512]{1,0:T(4,128)S(1)}, f32[4,512]{1,0:T(4,128)S(1)}, u32[]{:S(2)}, u32[]{:S(2)}) collective-permute-start(f32[4,512]{1,0:T(4,128)S(1)} %pad_maximum_fusion.1.refs_0_), channel_id=1, source_target_pairs={{0,4},{2,6},{4,0},{6,2},{8,12},{10,14},{12,8},{14,10},{16,20},{18,... | collective-permute-start | bytes 24584 | tf_op jit(solution)/shard_map/ppermute | solution.py:32
  37.9 3.7 %collective-permute-start.9 = (f32[4,512]{1,0:T(4,128)S(1)}, f32[4,512]{1,0:T(4,128)S(1)}, u32[]{:S(2)}, u32[]{:S(2)}) collective-permute-start(f32[4,512]{1,0:T(4,128)S(1)} %pad_maximum_fusion.1.refs_0_), channel_id=1, source_target_pairs={{0,2},{2,0},{4,6},{6,4},{8,10},{10,8},{12,14},{14,12},{16,18},{18,... | collective-permute-start | bytes 24584 | tf_op jit(solution)/shard_map/ppermute | solution.py:32
